TPU v7x, 128 devices: a whole 4x4x4 slice. The times are simulated.
128 devices in a mesh: rep: 16 (over y, z_hi, core), shard: 8 (over z_lo, x).
Axes of the slice: x: 4, y: 4, z: 4 (z_hi: 2, z_lo: 2; z = z_hi * 2 + z_lo), core: 2. Of those that a mesh axis runs over, the one named last changes fastest.
Arguments:
- tokens: bfloat16 [16384, 2048], P(('rep', 'shard')), may hold values from -6 to 6
- doc_lengths: int32 [128, 3], P(('rep', 'shard')), may hold values from 1 to 64, 128 in all within a row
- cotangent: bfloat16 [16384, 2048], P(('rep', 'shard')), may hold values from -6 to 6
- ln1_gain: bfloat16 [2048], P('shard'), may hold values from 0.5 to 1.5
- ln1_bias: bfloat16 [2048], P('shard'), may hold values from -1.5 to 1.5
- ln2_gain: bfloat16 [2048], P('shard'), may hold values from 0.5 to 1.5
- ln2_bias: bfloat16 [2048], P('shard'), may hold values from -1.5 to 1.5
- qkv_weight: bfloat16 [2048, 6144], P('shard'), may hold values from -0.125 to 0.125
- qkv_bias: bfloat16 [6144], P('shard'), may hold values from -3 to 3
- out_weight: bfloat16 [2048, 2048], P('shard'), may hold values from -0.5 to 0.5
- out_bias: bfloat16 [2048], P('shard'), may hold values from -3 to 3
- up_weight: bfloat16 [2048, 8192], P('shard'), may hold values from -0.125 to 0.125
- up_bias: bfloat16 [8192], P('shard'), may hold values from -3 to 3
- down_weight: bfloat16 [8192, 2048], P('shard'), may hold values from -0.09375 to 0.09375
- down_bias: bfloat16 [2048], P('shard'), may hold values from -3 to 3
Outputs:
- mixed: bfloat16 [16384, 2048], P(('rep', 'shard'))
- tokens_grad: float32 [16384, 2048], P(('rep', 'shard'))
- ln1_gain_grad: float32 [2048], P('shard')
- ln1_bias_grad: float32 [2048], P('shard')
- ln2_gain_grad: float32 [2048], P('shard')
- ln2_bias_grad: float32 [2048], P('shard')
- qkv_weight_grad: float32 [2048, 6144], P('shard')
- qkv_bias_grad: float32 [6144], P('shard')
- out_weight_grad: float32 [2048, 2048], P('shard')
- out_bias_grad: float32 [2048], P('shard')
- up_weight_grad: float32 [2048, 8192], P('shard')
- up_bias_grad: float32 [8192], P('shard')
- down_weight_grad: float32 [8192, 2048], P('shard')
- down_bias_grad: float32 [2048], P('shard')
Inputs may be any that keep to these rules, and one draw needn't show every extreme that they name: `doc_lengths`: each row sums to 128; some document has exactly 64 tokens.
All inputs are finite; a program needn't handle non-finite values.
Results may differ from a plain program's by a relative error of at most 0.02.
Values may be sent and summed in bfloat16 or wider, within the bound.
No kernel may reach another device: no remote copies, remote signals or barrier semaphores. Data moves between devices by JAX's collectives and lax.ppermute only.
A program may use at most 448 MiB of HBM per device.

v0:
```python
import math

import jax
import jax.numpy as jnp
from jax import lax
from jax.experimental import pallas as pl
from jax.experimental.pallas import tpu as pltpu
from jax.sharding import PartitionSpec as P

HEADS = 8
ROT = 64
EPS = 1e-05
f32 = jnp.float32
bf16 = jnp.bfloat16
COST = pl.CostEstimate(flops=1000, bytes_accessed=1000, transcendentals=0)
BOTH = ("rep", "shard")
SIZES = (4, 2, 2, 2, 4)


def coords():
    for y in range(4):
        for h in range(2):
            for c in range(2):
                for l in range(2):
                    for x in range(4):
                        yield (y, h, c, l, x)


def linear(t):
    y, h, c, l, x = (v % m for v, m in zip(t, SIZES))
    return ((y * 2 + h) * 2 + c) * 8 + l * 4 + x


def move(value, y=0, h=0, c=0, l=0, x=0):
    step = (y, h, c, l, x)
    pairs = [(linear(t), linear(tuple(a + b for a, b in zip(t, step)))) for t in coords()]
    return lax.ppermute(value, BOTH, pairs)


def swap(value, axis, bit):
    at = "yhclx".index(axis)
    pairs = [(linear(t), linear(t[:at] + (t[at] ^ bit,) + t[at + 1 :])) for t in coords()]
    return lax.ppermute(value, BOTH, pairs)


def pick(value, index, axis):
    return lax.dynamic_index_in_dim(value, index, axis, keepdims=False)


def ring_gather(own, axis, cut):
    below = move(own, **{axis: 1})
    above = move(own, **{axis: -1})
    far_low = move(below[:cut], **{axis: 1})
    far_high = move(above[cut:], **{axis: -1})
    return [own, above, jnp.concatenate([far_low, far_high], 0), below]


def ring_reduce(pieces, axis, cut):
    own, above, far, below = pieces
    low = move(far[:cut].astype(bf16), **{axis: 1})
    high = move(far[cut:].astype(bf16), **{axis: -1})
    up = jnp.concatenate([above[:cut].astype(f32) + low.astype(f32), above[cut:].astype(f32)], 0)
    down = jnp.concatenate([below[:cut].astype(f32), below[cut:].astype(f32) + high.astype(f32)], 0)
    from_below = move(up.astype(bf16), **{axis: 1})
    from_above = move(down.astype(bf16), **{axis: -1})
    return own.astype(f32) + from_below.astype(f32) + from_above.astype(f32)


def group_gather(own, cut):
    other = move(own, l=1)
    return ring_gather(own, "x", cut) + ring_gather(other, "x", cut)


def group_reduce(pieces, cut):
    other = ring_reduce(pieces[4:], "x", cut)
    crossed = move(other.astype(bf16), l=1)
    return ring_reduce(pieces[:4], "x", cut) + crossed.astype(f32)


def place(pieces, start, count, axis):
    full = jnp.stack(pieces + pieces[:-1], axis)
    return lax.dynamic_slice_in_dim(full, (count - start) % count, count, axis)


def normalize(value):
    xf = value.astype(f32)
    centre = xf - jnp.mean(xf, -1, keepdims=True)
    inverse = lax.rsqrt(jnp.mean(centre * centre, -1, keepdims=True) + EPS)
    return centre * inverse, inverse


def kernel_params():
    return pltpu.CompilerParams(vmem_limit_bytes=56 * 1024 * 1024)


def dot(a, b, ca=1, cb=0):
    return lax.dot_general(a, b, (((ca,), (cb,)), ((), ())), preferred_element_type=f32)


def hidden_part(h2, weight, first, bias):
    rows, width = h2.shape
    ff = bias.shape[1]

    def body(h_ref, w_ref, b_ref, act_ref, slope_ref):
        u = dot(h_ref[...], w_ref[...]) + b_ref[...]
        cdf = 0.5 * (1.0 + lax.erf(u * math.sqrt(0.5)))
        pdf = jnp.exp(-0.5 * u * u) * (1.0 / math.sqrt(2.0 * math.pi))
        act_ref[...] = (u * cdf).astype(bf16)
        slope_ref[...] = cdf + u * pdf

    return pl.pallas_call(
        body,
        out_shape=(
            jax.ShapeDtypeStruct((rows, ff), bf16),
            jax.ShapeDtypeStruct((rows, ff), f32),
        ),
        grid=(ff // 256,),
        in_specs=[
            pl.BlockSpec((rows, width), lambda i: (0, 0)),
            pl.BlockSpec((width, 256), lambda i: (0, i + first)),
            pl.BlockSpec((1, 256), lambda i: (0, i)),
        ],
        out_specs=(
            pl.BlockSpec((rows, 256), lambda i: (0, i)),
            pl.BlockSpec((rows, 256), lambda i: (0, i)),
        ),
        compiler_params=kernel_params(),
        cost_estimate=COST,
        name="hidden_part",
    )(h2, weight, bias)


def swap_halves(value):
    lane = lax.broadcasted_iota(jnp.int32, value.shape, 1)
    return jnp.where(lane < 32, pltpu.roll(value, 96, 1), pltpu.roll(value, 32, 1))


def allowed_mask(lengths_ref, block, rows):
    e0 = lengths_ref[block, 0]
    e1 = e0 + lengths_ref[block, 1]
    t = lax.broadcasted_iota(jnp.int32, (rows, rows), 0)
    s = lax.broadcasted_iota(jnp.int32, (rows, rows), 1)
    seg_t = (t >= e0).astype(jnp.int32) + (t >= e1).astype(jnp.int32)
    seg_s = (s >= e0).astype(jnp.int32) + (s >= e1).astype(jnp.int32)
    return (seg_t == seg_s) & (s <= t)


def attention(h1, weight, bias, cosine, sine, lengths, rows=128, head=256):
    total, width = h1.shape
    blocks = total // rows
    scale = head ** (-0.5)

    def body(len_ref, h_ref, w_ref, b_ref, cos_ref, sin_ref, qkv_ref, p_ref, o_ref, work):
        step = pl.program_id(0)

        @pl.when(step < 3)
        def _():
            work[step] = dot(h_ref[...], w_ref[...]) + b_ref[0]

        @pl.when(step >= 3)
        def _():
            block = step - 3
            at = pl.ds(block * rows, rows)
            cos, sin = cos_ref[...], sin_ref[...]

            def turned(value):
                left = value[:, :128]
                left = left * cos + swap_halves(left) * sin
                return jnp.concatenate([left, value[:, 128:]], 1).astype(bf16)

            q, k = turned(work[0, at, :]), turned(work[1, at, :])
            v = work[2, at, :].astype(bf16)
            qkv_ref[:, 0:head] = q
            qkv_ref[:, head : 2 * head] = k
            qkv_ref[:, 2 * head :] = v
            scores = dot(q, k, 1, 1) * scale
            masked = jnp.where(allowed_mask(len_ref, block, rows), scores, -1e30)
            shifted = jnp.exp(masked - jnp.max(masked, 1, keepdims=True))
            probs = shifted / jnp.sum(shifted, 1, keepdims=True)
            p_ref[...] = probs
            o_ref[...] = dot(probs.astype(bf16), v).astype(bf16)

    def at_block(i, lens):
        return (jnp.maximum(i - 3, 0), 0)

    return pl.pallas_call(
        body,
        out_shape=(
            jax.ShapeDtypeStruct((total, 3 * head), bf16),
            jax.ShapeDtypeStruct((total, rows), f32),
            jax.ShapeDtypeStruct((total, head), bf16),
        ),
        grid_spec=pltpu.PrefetchScalarGridSpec(
            num_scalar_prefetch=1,
            grid=(3 + blocks,),
            in_specs=[
                pl.BlockSpec((total, width), lambda i, lens: (0, 0)),
                pl.BlockSpec((width, head), lambda i, lens: (0, jnp.minimum(i, 2))),
                pl.BlockSpec((1, 1, head), lambda i, lens: (jnp.minimum(i, 2), 0, 0)),
                pl.BlockSpec((rows, 128), at_block),
                pl.BlockSpec((rows, 128), at_block),
            ],
            out_specs=(
                pl.BlockSpec((rows, 3 * head), at_block),
                pl.BlockSpec((rows, rows), at_block),
                pl.BlockSpec((rows, head), at_block),
            ),
            scratch_shapes=[pltpu.VMEM((3, total, head), f32)],
        ),
        compiler_params=kernel_params(),
        cost_estimate=COST,
        name="attention",
    )(lengths, h1, weight, bias, cosine, sine)


def mixed_part(active, attended, down, out, bias):
    rows, ff = active.shape
    head, width = out.shape

    def body(act_ref, ol_ref, wd_ref, wo_ref, b_ref, mix_ref):
        total = dot(act_ref[...], wd_ref[...]) + dot(ol_ref[...], wo_ref[...]) + b_ref[...]
        mix_ref[...] = total.astype(bf16)

    return pl.pallas_call(
        body,
        out_shape=jax.ShapeDtypeStruct((rows, width), bf16),
        grid=(width // 256,),
        in_specs=[
            pl.BlockSpec((rows, ff), lambda i: (0, 0)),
            pl.BlockSpec((rows, head), lambda i: (0, 0)),
            pl.BlockSpec((ff, 256), lambda i: (0, i)),
            pl.BlockSpec((head, 256), lambda i: (0, i)),
            pl.BlockSpec((1, 256), lambda i: (0, i)),
        ],
        out_specs=pl.BlockSpec((rows, 256), lambda i: (0, i)),
        compiler_params=kernel_params(),
        cost_estimate=COST,
        name="mixed_part",
    )(active, attended, down, out, bias)


def back_inner(dy, down, out, slope, qkv, probs, cosine, sine, rows=128):
    total, width = dy.shape
    ff, head = down.shape[0], out.shape[0]
    steps = ff // 256
    blocks = total // rows
    scale = head ** (-0.5)

    def body(dy_ref, wd_ref, wo_ref, s_ref, qkv_ref, p_ref, cos_ref, sin_ref, du_ref, db_ref, dq_ref, dqb_ref, work):
        step = pl.program_id(0)

        @pl.when(step < steps)
        def _():
            du = (dot(dy_ref[...], wd_ref[...], 1, 1) * s_ref[...]).astype(bf16)
            du_ref[...] = du
            db_ref[...] = jnp.sum(du.astype(f32), 0, keepdims=True)

        @pl.when(step == steps)
        def _():
            work[...] = dot(dy_ref[...], wo_ref[...], 1, 1).astype(bf16)
            dqb_ref[...] = jnp.zeros_like(dqb_ref)

        @pl.when(step > steps)
        def _():
            block = step - steps - 1
            cos, sin = cos_ref[...], sin_ref[...]
            q, k, v = (qkv_ref[:, n * head : (n + 1) * head] for n in range(3))
            probs = p_ref[...]
            d_out = work[pl.ds(block * rows, rows), :]
            d_value = dot(probs.astype(bf16), d_out, 0, 0)
            d_probs = dot(d_out, v, 1, 1)
            centred = d_probs - jnp.sum(d_probs * probs, 1, keepdims=True)
            d_scores = (probs * centred).astype(bf16)

            def back(value):
                value = value * scale
                left = value[:, :128]
                left = left * cos - swap_halves(left) * sin
                return jnp.concatenate([left, value[:, 128:]], 1).astype(bf16)

            for n, grad in enumerate(
                (back(dot(d_scores, k)), back(dot(d_scores, q, 0, 0)), d_value.astype(bf16))
            ):
                dq_ref[:, n * head : (n + 1) * head] = grad
                dqb_ref[:, n * head : (n + 1) * head] += jnp.sum(grad.astype(f32), 0, keepdims=True)

    def part(i):
        return jnp.minimum(i, steps - 1)

    def at_block(i):
        return (jnp.maximum(i - steps - 1, 0), 0)

    return pl.pallas_call(
        body,
        out_shape=(
            jax.ShapeDtypeStruct((total, ff), bf16),
            jax.ShapeDtypeStruct((1, ff), f32),
            jax.ShapeDtypeStruct((total, 3 * head), bf16),
            jax.ShapeDtypeStruct((1, 3 * head), f32),
        ),
        grid=(steps + 1 + blocks,),
        in_specs=[
            pl.BlockSpec((total, width), lambda i: (0, 0)),
            pl.BlockSpec((256, width), lambda i: (part(i), 0)),
            pl.BlockSpec((head, width), lambda i: (0, 0)),
            pl.BlockSpec((total, 256), lambda i: (0, part(i))),
            pl.BlockSpec((rows, 3 * head), at_block),
            pl.BlockSpec((rows, rows), at_block),
            pl.BlockSpec((rows, 128), at_block),
            pl.BlockSpec((rows, 128), at_block),
        ],
        out_specs=(
            pl.BlockSpec((total, 256), lambda i: (0, part(i))),
            pl.BlockSpec((1, 256), lambda i: (0, part(i))),
            pl.BlockSpec((rows, 3 * head), at_block),
            pl.BlockSpec((1, 3 * head), lambda i: (0, 0)),
        ),
        scratch_shapes=[pltpu.VMEM((total, head), bf16)],
        compiler_params=kernel_params(),
        cost_estimate=COST,
        name="back_inner",
    )(dy, down, out, slope, qkv, probs, cosine, sine)


def back_norms(d_qkv, d_hidden, weight, tokens, mean, inverse, gains):
    total, n1 = d_qkv.shape
    n2 = d_hidden.shape[1]
    width = tokens.shape[1]

    def body(dq_ref, du_ref, w_ref, x_ref, m_ref, i_ref, g_ref, s_ref, sums_ref):
        d1 = dot(dq_ref[...], w_ref[:, :n1], 1, 1)
        d2 = dot(du_ref[...], w_ref[:, n1:], 1, 1)
        normed = (x_ref[...].astype(f32) - m_ref[...]) * i_ref[...]
        s_ref[...] = (d1 * g_ref[0:1] + d2 * g_ref[1:2]).astype(bf16)
        sums_ref[0:1] = jnp.sum(d1 * normed, 0, keepdims=True)
        sums_ref[1:2] = jnp.sum(d1, 0, keepdims=True)
        sums_ref[2:3] = jnp.sum(d2 * normed, 0, keepdims=True)
        sums_ref[3:4] = jnp.sum(d2, 0, keepdims=True)

    return pl.pallas_call(
        body,
        out_shape=(
            jax.ShapeDtypeStruct((total, width), bf16),
            jax.ShapeDtypeStruct((4, width), f32),
        ),
        grid=(width // 256,),
        in_specs=[
            pl.BlockSpec((total, n1), lambda i: (0, 0)),
            pl.BlockSpec((total, n2), lambda i: (0, 0)),
            pl.BlockSpec((256, n1 + n2), lambda i: (i, 0)),
            pl.BlockSpec((total, 256), lambda i: (0, i)),
            pl.BlockSpec((total, 1), lambda i: (0, 0)),
            pl.BlockSpec((total, 1), lambda i: (0, 0)),
            pl.BlockSpec((2, 256), lambda i: (0, i)),
        ],
        out_specs=(
            pl.BlockSpec((total, 256), lambda i: (0, i)),
            pl.BlockSpec((4, 256), lambda i: (0, i)),
        ),
        compiler_params=kernel_params(),
        cost_estimate=COST,
        name="back_norms",
    )(d_qkv, d_hidden, weight, tokens, mean, inverse, gains)


def norms(tokens, gains):
    total, width = tokens.shape
    rows = 128

    def body(x_ref, g_ref, h1_ref, h2_ref, m_ref, i_ref):
        x = x_ref[...].astype(f32)
        mean = jnp.mean(x, 1, keepdims=True)
        centre = x - mean
        inverse = lax.rsqrt(jnp.mean(centre * centre, 1, keepdims=True) + 1e-5)
        normed = centre * inverse
        m_ref[...] = mean
        i_ref[...] = inverse
        h1_ref[...] = (normed * g_ref[0:1] + g_ref[1:2]).astype(bf16)
        h2_ref[...] = (normed * g_ref[2:3] + g_ref[3:4]).astype(bf16)

    column = jax.ShapeDtypeStruct((total, 1), f32)
    wide = jax.ShapeDtypeStruct((total, width), bf16)
    block = pl.BlockSpec((rows, width), lambda i: (i, 0))
    thin = pl.BlockSpec((rows, 1), lambda i: (i, 0))
    return pl.pallas_call(
        body,
        out_shape=(wide, wide, column, column),
        grid=(total // rows,),
        in_specs=[block, pl.BlockSpec((4, width), lambda i: (0, 0))],
        out_specs=(block, block, thin, thin),
        compiler_params=kernel_params(),
        cost_estimate=COST,
        name="norms",
    )(tokens, gains)


def dot_rows(a, b):
    return lax.dot_general(a, b, (((0,), (0,)), ((), ())), preferred_element_type=f32)


def sorted_weight(mine, yours, spots):
    sources, rows, cols = mine.shape[1:]

    def body(spot_ref, mine_ref, yours_ref, out_ref):
        step = pl.program_id(0)

        @pl.when(step < 4)
        def _():
            out_ref[:, 0] = mine_ref[0]

        @pl.when(step >= 4)
        def _():
            out_ref[:, 0] = yours_ref[0]

    block = (1, sources, rows, cols)
    return pl.pallas_call(
        body,
        out_shape=jax.ShapeDtypeStruct((sources, 8, rows, cols), bf16),
        grid_spec=pltpu.PrefetchScalarGridSpec(
            num_scalar_prefetch=1,
            grid=(8,),
            in_specs=[
                pl.BlockSpec(block, lambda i, spot: (jnp.minimum(i, 3), 0, 0, 0)),
                pl.BlockSpec(block, lambda i, spot: (jnp.maximum(i - 4, 0), 0, 0, 0)),
            ],
            out_specs=pl.BlockSpec(
                (sources, 1, rows, cols), lambda i, spot: (0, spot[i], 0, 0)
            ),
        ),
        compiler_params=kernel_params(),
        cost_estimate=COST,
        name="sorted_weight",
    )(spots, mine, yours).reshape(sources * 8 * rows, cols)


def late_grads(active, attended, dy, core):
    width = dy.shape[1]

    def body(core_ref, act_ref, ol_ref, dy_ref, keep_ref, send_ref):
        step = pl.program_id(0)
        first = core_ref[0] == 0

        @pl.when(step < 4)
        def _():
            part = dot_rows(act_ref[...], dy_ref[...]).astype(bf16).reshape(2, 2, 64, width)
            at = pl.ds(step * 2, 2)

            @pl.when(first)
            def _():
                keep_ref[at, 0:64] = part[:, 0]
                send_ref[at, 0:64] = part[:, 1]

            @pl.when(jnp.logical_not(first))
            def _():
                keep_ref[at, 0:64] = part[:, 1]
                send_ref[at, 0:64] = part[:, 0]

        @pl.when(step == 4)
        def _():
            part = dot_rows(ol_ref[...], dy_ref[...]).astype(bf16).reshape(8, 2, 16, width)

            @pl.when(first)
            def _():
                keep_ref[:, 64:80] = part[:, 0]
                send_ref[:, 64:80] = part[:, 1]

            @pl.when(jnp.logical_not(first))
            def _():
                keep_ref[:, 64:80] = part[:, 1]
                send_ref[:, 64:80] = part[:, 0]

    rows = dy.shape[0]
    out = jax.ShapeDtypeStruct((8, 80, width), bf16)
    whole = pl.BlockSpec((8, 80, width), lambda i, core: (0, 0, 0))
    keep, send = pl.pallas_call(
        body,
        out_shape=(out, out),
        grid_spec=pltpu.PrefetchScalarGridSpec(
            num_scalar_prefetch=1,
            grid=(5,),
            in_specs=[
                pl.BlockSpec((rows, 256), lambda i, core: (0, jnp.minimum(i, 3))),
                pl.BlockSpec((rows, 256), lambda i, core: (0, 0)),
                pl.BlockSpec((rows, width), lambda i, core: (0, 0)),
            ],
            out_specs=(whole, whole),
        ),
        compiler_params=kernel_params(),
        cost_estimate=COST,
        name="late_grads",
    )(core, active, attended, dy)
    return keep.reshape(4, 2, 80, width), send.reshape(4, 2, 80, width)


def early_grads(h1, h2, d_qkv, d_hidden, core):
    rows, width = h1.shape
    n1, n2 = d_qkv.shape[1], d_hidden.shape[1]

    def body(core_ref, h1_ref, h2_ref, dq_ref, du_ref, keep_ref, send_ref):
        first = core_ref[0] == 0
        left = dot_rows(h1_ref[...], dq_ref[...]).astype(bf16).reshape(4, 2, 2, 16, n1)
        right = dot_rows(h2_ref[...], du_ref[...]).astype(bf16).reshape(4, 2, 2, 16, n2)

        @pl.when(first)
        def _():
            keep_ref[:, 0, :, :, 0:n1] = left[:, :, 0]
            keep_ref[:, 0, :, :, n1:] = right[:, :, 0]
            send_ref[:, 0, :, :, 0:n1] = left[:, :, 1]
            send_ref[:, 0, :, :, n1:] = right[:, :, 1]

        @pl.when(jnp.logical_not(first))
        def _():
            keep_ref[:, 0, :, :, 0:n1] = left[:, :, 1]
            keep_ref[:, 0, :, :, n1:] = right[:, :, 1]
            send_ref[:, 0, :, :, 0:n1] = left[:, :, 0]
            send_ref[:, 0, :, :, n1:] = right[:, :, 0]

    out = jax.ShapeDtypeStruct((4, 8, 2, 16, n1 + n2), bf16)
    block = pl.BlockSpec((4, 1, 2, 16, n1 + n2), lambda i, core: (0, i, 0, 0, 0))
    return pl.pallas_call(
        body,
        out_shape=(out, out),
        grid_spec=pltpu.PrefetchScalarGridSpec(
            num_scalar_prefetch=1,
            grid=(8,),
            in_specs=[
                pl.BlockSpec((rows, width // 8), lambda i, core: (0, i)),
                pl.BlockSpec((rows, width // 8), lambda i, core: (0, i)),
                pl.BlockSpec((rows, n1), lambda i, core: (0, 0)),
                pl.BlockSpec((rows, n2), lambda i, core: (0, 0)),
            ],
            out_specs=(block, block),
        ),
        compiler_params=kernel_params(),
        cost_estimate=COST,
        name="early_grads",
    )(core, h1, h2, d_qkv, d_hidden)


def late_outputs(groups, spots):
    width = groups[0].shape[-1]

    def body(spot_ref, *refs):
        ins, down_ref, out_ref = refs[:4], refs[4], refs[5]
        step = pl.program_id(0)
        for at, ref in enumerate(ins):

            @pl.when(step // 4 == at)
            def _(ref=ref):
                down_ref[...] = ref[0, 0:64].astype(f32)
                out_ref[...] = ref[0, 64:80].astype(f32)

    def chosen(at):
        return pl.BlockSpec(
            (1, 80, width), lambda i, spot: (jnp.clip(i - 4 * at, 0, 3), 0, 0)
        )

    return pl.pallas_call(
        body,
        out_shape=(
            jax.ShapeDtypeStruct((1024, width), f32),
            jax.ShapeDtypeStruct((256, width), f32),
        ),
        grid_spec=pltpu.PrefetchScalarGridSpec(
            num_scalar_prefetch=1,
            grid=(16,),
            in_specs=[chosen(at) for at in range(4)],
            out_specs=(
                pl.BlockSpec((64, width), lambda i, spot: (spot[i], 0)),
                pl.BlockSpec((16, width), lambda i, spot: (spot[i], 0)),
            ),
        ),
        compiler_params=kernel_params(),
        cost_estimate=COST,
        name="late_outputs",
    )(spots, *groups)


def early_outputs(mine, yours, spots, n1):
    cols = mine.shape[-1]
    n2 = cols - n1
    head = n1 // 3

    def body(spot_ref, mine_ref, yours_ref, qkv_ref, up_ref):
        step = pl.program_id(0)

        def put(ref):
            for source in range(8):
                for third in range(3):
                    at = (third * 8 + source) * head
                    qkv_ref[:, at : at + head] = ref[
                        0, source, :, third * head : (third + 1) * head
                    ].astype(f32)
                up_ref[:, source * n2 : (source + 1) * n2] = ref[0, source, :, n1:].astype(f32)

        @pl.when(step < 8)
        def _():
            put(mine_ref)

        @pl.when(step >= 8)
        def _():
            put(yours_ref)

    block = (1, 8, 16, cols)
    return pl.pallas_call(
        body,
        out_shape=(
            jax.ShapeDtypeStruct((256, 8 * n1), f32),
            jax.ShapeDtypeStruct((256, 8 * n2), f32),
        ),
        grid_spec=pltpu.PrefetchScalarGridSpec(
            num_scalar_prefetch=1,
            grid=(16,),
            in_specs=[
                pl.BlockSpec(block, lambda i, spot: (jnp.minimum(i, 7), 0, 0, 0)),
                pl.BlockSpec(block, lambda i, spot: (jnp.maximum(i - 8, 0), 0, 0, 0)),
            ],
            out_specs=(
                pl.BlockSpec((16, 8 * n1), lambda i, spot: (spot[i], 0)),
                pl.BlockSpec((16, 8 * n2), lambda i, spot: (spot[i], 0)),
            ),
        ),
        compiler_params=kernel_params(),
        cost_estimate=COST,
        name="early_outputs",
    )(spots, mine, yours)


def local(
    tokens,
    doc_lengths,
    cotangent,
    ln1_gain,
    ln1_bias,
    ln2_gain,
    ln2_bias,
    qkv_weight,
    qkv_bias,
    out_weight,
    out_bias,
    up_weight,
    up_bias,
    down_weight,
    down_bias,
):
    rows, width = tokens.shape
    head = width // HEADS
    group = 8
    rep = lax.axis_index("rep")
    shard = lax.axis_index("shard")
    y, h, c = rep // 4, (rep // 2) % 2, rep % 2
    l, x = shard // 4, shard % 4
    ff = up_bias.shape[0]

    cols = 3 * head + ff
    part = lax.dynamic_slice_in_dim(qkv_weight, y * 64 + c * 32, 32, 0).reshape(32, 3, 8, head)
    part_up = lax.dynamic_slice_in_dim(up_weight, y * 64 + c * 32, 32, 0).reshape(32, 8, ff)
    small = jnp.concatenate([ln1_gain, ln1_bias, ln2_gain, ln2_bias, qkv_bias])
    size = jnp.pad(doc_lengths[0].astype(bf16), (0, cols - doc_lengths.shape[1]))
    small = jnp.pad(jnp.stack([small, size]), ((0, 6), (0, 0)))
    part = jnp.concatenate(
        [part.transpose(2, 0, 1, 3).reshape(8, 32, 3 * head), part_up.transpose(1, 0, 2)], -1
    )
    part = jnp.concatenate([part, jnp.broadcast_to(small[None], (8, 8, cols))], 1)
    part = lax.all_to_all(part, "shard", 0, 0)
    infos = part[:, 32:34]
    mine = jnp.stack(ring_gather(part[:, :32], "y", 4))
    yours = move(mine, c=1)
    steps4 = (y + jnp.arange(4)) % 4
    spots = jnp.concatenate([steps4 * 2 + c, steps4 * 2 + 1 - c]).astype(jnp.int32)
    w_mixed = sorted_weight(mine, yours, spots)

    places = [((l ^ (k // 4)) * 4 + (x + k % 4) % 4) for k in range(8)]
    x_all = jnp.zeros((group * rows, width), bf16)
    for place_of, piece in zip(places, group_gather(tokens, 64)):
        x_all = lax.dynamic_update_slice(x_all, piece, (place_of * rows, 0))
    dy_all = lax.all_gather(cotangent, "shard", axis=0, tiled=True)

    gains = infos[:, 0, :1024].reshape(8, 4, 256).transpose(1, 0, 2).reshape(4, width).astype(f32)
    qkv_b = infos[:, 0, 1024:].astype(f32).reshape(8 * 3, 1, head)
    qkv_b = jnp.stack(
        [lax.dynamic_index_in_dim(qkv_b, third * 8 + shard, 0, False) for third in range(3)]
    )
    lengths = infos[:, 1, :3].astype(jnp.int32)
    ends = jnp.cumsum(lengths, 1)
    starts = ends - lengths
    steps_t = jnp.arange(rows, dtype=jnp.int32)
    segment = jnp.sum((steps_t[None, :, None] >= ends[:, None, :]).astype(jnp.int32), -1)
    slots = jnp.arange(lengths.shape[1], dtype=jnp.int32)
    begin = jnp.sum(
        jnp.where(segment[:, :, None] == slots[None, None, :], starts[:, None, :], 0), -1
    )
    position = (steps_t[None, :] - begin).astype(f32).reshape(group * rows, 1)
    lane = jnp.arange(128)
    freq = 10000.0 ** (-2.0 * (lane % (ROT // 2)).astype(f32) / ROT)
    angle = position * freq[None, :]
    cosine = jnp.where(lane < ROT, jnp.cos(angle), 1.0)
    sine = jnp.sin(angle)
    sine = jnp.where(lane < ROT // 2, -sine, jnp.where(lane < ROT, sine, 0.0))

    h1, h2, mean, inverse = norms(x_all, gains)
    active, slope = hidden_part(h2, w_mixed, 3 * head // 256, up_bias.astype(f32)[None])
    qkv, probs, attended = attention(h1, w_mixed, qkv_b, cosine, sine, lengths)
    both_bias = (out_bias.astype(f32) + down_bias.astype(f32))[None, :]
    wide_bias = lax.dynamic_update_slice(jnp.zeros((1, width), f32), both_bias, (0, shard * 256))
    mix = mixed_part(active, attended, down_weight, out_weight, wide_bias)
    mixed = lax.psum_scatter(mix, "shard", scatter_dimension=0, tiled=True)
    mixed = (tokens.astype(f32) + mixed.astype(f32)).astype(bf16)

    core = c.astype(jnp.int32).reshape(1)
    late_keep, late_send = late_grads(active, attended, dy_all, core)
    d_hidden, up_b, d_qkv, qkv_bg = back_inner(
        dy_all, down_weight, out_weight, slope, qkv, probs, cosine, sine
    )
    early_keep, early_send = early_grads(h1, h2, d_qkv, d_hidden, core)
    sums, norm_sums = back_norms(
        d_qkv, d_hidden, w_mixed, x_all, mean, inverse, jnp.stack([gains[0], gains[2]])
    )
    sums = sums.reshape(group, rows, width)
    own_sum = group_reduce([pick(sums, place_of, 0) for place_of in places], 64)
    own_normed, own_inverse = normalize(tokens)
    tokens_grad = cotangent.astype(f32) + own_inverse * (
        own_sum
        - jnp.mean(own_sum, -1, keepdims=True)
        - own_normed * jnp.mean(own_sum * own_normed, -1, keepdims=True)
    )

    dy_sum = jnp.sum(dy_all.astype(f32), 0)
    dy_own = lax.dynamic_slice_in_dim(dy_sum, shard * 256, 256)
    wide_qkv = lax.dynamic_update_slice(
        jnp.zeros((3, 8, head), f32), qkv_bg.reshape(3, 1, head), (0, shard, 0)
    )
    wide_up = lax.dynamic_update_slice(jnp.zeros((8 * ff,), f32), up_b.reshape(-1), (shard * ff,))
    wide_dy = lax.dynamic_update_slice(jnp.zeros((width,), f32), dy_own, (shard * 256,))
    smalls = jnp.concatenate([norm_sums.reshape(-1), wide_dy, wide_qkv.reshape(-1), wide_up])
    smalls = smalls.reshape(-1, 1024)
    for axis, bit in (("c", 1), ("l", 1), ("h", 1), ("x", 1), ("y", 1), ("x", 2), ("y", 2)):
        smalls = smalls + swap(smalls, axis, bit)
    smalls = smalls.reshape(-1)

    def small_at(start, size):
        return lax.dynamic_slice_in_dim(smalls, start + shard * size, size)

    got = move(late_send, c=1)

    def late_part(high, index):
        both = [pick(pick(v, high, 1), index, 0).astype(f32) for v in (late_keep, got)]
        return both[0] + both[1]

    away = (pick(late_keep, 1 - h, 1).astype(f32) + pick(got, 1 - h, 1).astype(f32)).astype(bf16)
    crossed = move(away, h=1)
    parts = [late_part(h, (y + k) % 4) + pick(crossed, (y + k) % 4, 0).astype(f32) for k in range(4)]
    late = ring_reduce(parts, "y", 40).astype(bf16)
    late = jnp.stack(ring_gather(late, "y", 40))
    late_h = move(late, h=1)
    late_c = move(late, c=1)
    late_hc = move(late_h, c=1)
    spots = [
        (steps4 * 2 + high) * 2 + low for high, low in ((h, c), (1 - h, c), (h, 1 - c), (1 - h, 1 - c))
    ]
    down_grad, out_grad = late_outputs(
        (late, late_h, late_c, late_hc), jnp.concatenate(spots).astype(jnp.int32)
    )

    got_early = move(early_send, c=1)
    parts = [
        pick(early_keep, (y + k) % 4, 0).astype(f32) + pick(got_early, (y + k) % 4, 0).astype(f32)
        for k in range(4)
    ]
    early = ring_reduce(parts, "y", 4)
    crossed = move(pick(early, 1 - h, 1).astype(bf16), h=1)
    early = (pick(early, h, 1) + crossed.astype(f32)).astype(bf16)
    early = lax.all_to_all(early, "shard", 0, 0)
    early = jnp.stack([early, move(early, h=1)])
    early = jnp.concatenate(ring_gather(early, "y", 1), 0)
    early_c = move(early, c=1)
    spots = [
        ((steps4[:, None] * 2 + jnp.stack([h, 1 - h])[None, :]) * 2 + low).reshape(8)
        for low in (c, 1 - c)
    ]
    qkv_grad, up_grad = early_outputs(
        early, early_c, jnp.concatenate(spots).astype(jnp.int32), 3 * head
    )

    dy_total = small_at(4 * width, 256)
    return (
        mixed,
        tokens_grad,
        small_at(0, 256),
        small_at(width, 256),
        small_at(2 * width, 256),
        small_at(3 * width, 256),
        qkv_grad,
        small_at(5 * width, 768),
        out_grad,
        dy_total,
        up_grad,
        small_at(8 * width, ff),
        down_grad,
        dy_total,
    )


def solution(mesh):
    rows = P(BOTH, None)
    vector, matrix = P("shard"), P("shard", None)
    return jax.shard_map(
        local,
        mesh=mesh,
        in_specs=(rows, rows, rows, vector, vector, vector, vector)
        + (matrix, vector, matrix, vector, matrix, vector, matrix, vector),
        out_specs=(rows, rows, vector, vector, vector, vector)
        + (matrix, vector, matrix, vector, matrix, vector, matrix, vector),
        check_vma=False,
    )
```

profile of v0, /device:TPU:1, one launch (start us, length us, event | category | flops | bytes accessed | tf_op | source)
XLA Modules:
  0.0 545.4 jit_solution(5131743738901134254)
XLA Ops:
  16.8 34.3 %all_to_all.10 = bf16[8,40,1792]{2,1,0:T(8,128)(2,1)S(1)} all-to-all(bf16[8,40,1792]{2,1,0:T(8,128)(2,1)S(1)} %pad_maximum_fusion.2), channel_id=1, replica_groups=mesh['rep'=16,'shard'=8] {'shard'}, dimensions={0} | all-to-all | bytes 2293760 | tf_op jit(solution)/shard_map/all_to_all | solution.py:665
  54.0 17.4 %collective-permute-done.9 = bf16[8,32,1792]{2,1,0:T(8,128)(2,1)S(1)} collective-permute-done((bf16[8,32,1792]{2,1,0:T(8,128)(2,1)S(1)}, bf16[8,32,1792]{2,1,0:T(8,128)(2,1)S(1)}, u32[]{:S(2)}, u32[]{:S(2)}) %collective-permute-start.9) | collective-permute-done | bytes 917536 | tf_op jit(solution)/shard_map/ppermute | solution.py:37
  71.4 3.6 collective-permute-start.12
  87.2 4.3 collective-permute-start.13
  128.9 9.2 %norms.1 = (bf16[1024,2048]{1,0:T(8,128)(2,1)}, bf16[1024,2048]{1,0:T(8,128)(2,1)}, f32[1024,1]{1,0:T(8,128)}, f32[1024,1]{1,0:T(8,128)}) custom-call(bf16[1024,2048]{1,0:T(8,128)(2,1)} %constant_dynamic-update-slice_fusion.1.x_ref, f32[4,2048]{1,0:T(4,128)} %bitcast.183), custom_call_target="tpu_custom_call" | custom-call | flops 1000 | bytes 1000 | tf_op jit(solution)/shard_map/norms/pallas_call | solution.py:385
  138.1 9.6 %sorted_weight.1 = bf16[8,8,32,1792]{3,2,1,0:T(8,128)(2,1)} custom-call(s32[8]{0:T(128)} %pad_add_fusion.spot_ref, bf16[4,8,32,1792]{3,2,1,0:T(8,128)(2,1)} %pad_maximum_fusion.mine_ref, bf16[4,8,32,1792]{3,2,1,0:T(8,128)(2,1)} %collective-permute-done.13.yours_ref), custom_call_target="tpu_custom_call" | custom-call | flops 1000 | bytes 1000 | tf_op jit(solution)/shard_map/sorted_weight/pallas_call | solution.py:416
  147.7 10.2 %hidden_part.1 = (bf16[1024,1024]{1,0:T(8,128)(2,1)}, f32[1024,1024]{1,0:T(8,128)}) custom-call(bf16[1024,2048]{1,0:T(8,128)(2,1)} %get-tuple-element.37.h_ref.h2_ref, bf16[2048,1792]{1,0:T(8,128)(2,1)} %bitcast.160, f32[1,1024]{1,0:T(1,128)} %bitcast.197), custom_call_target="tpu_custom_call" | custom-call | flops 1000 | bytes 1000 | tf_op jit(solution)/shard_map/hidden_part/pallas_call | solution.py:111
  157.9 14.4 %attention.1 = (bf16[1024,768]{1,0:T(8,128)(2,1)}, f32[1024,128]{1,0:T(8,128)}, bf16[1024,256]{1,0:T(8,128)(2,1)}) custom-call(s32[8,3]{1,0:T(8,128)} %copy.75.len_ref, bf16[1024,2048]{1,0:T(8,128)(2,1)} %get-tuple-element.39.h_ref.h1_ref, bf16[2048,1792]{1,0:T(8,128)(2,1)} %bitcast.161, f32[3,1,256]{2,1,0:T(1,128)} %pad_maximum_fusion.14.b_ref, ...), custom_call_target="tpu_custom_call" | custom-call | flops 1000 | bytes 1000 | tf_op jit(solution)/shard_map/attention/pallas_call | solution.py:186
  172.3 18.6 %back_inner.1 = (bf16[1024,1024]{1,0:T(8,128)(2,1)}, f32[1,1024]{1,0:T(1,128)}, bf16[1024,768]{1,0:T(8,128)(2,1)}, f32[1,768]{1,0:T(1,128)}) custom-call(bf16[1024,2048]{1,0:T(8,128)(2,1)} %all-gather.2.cloned.1.call-done.dy_ref, bf16[1024,2048]{1,0:T(8,128)(2,1)} %wd_ref.3, bf16[256,2048]{1,0:T(8,128)(2,1)} %wo_ref.3, ...), custom_call_target="tpu_custom_call" | custom-call | flops 1000 | bytes 1000 | tf_op jit(solution)/shard_map/back_inner/pallas_call | solution.py:293
  190.9 14.5 %early_grads.1 = (bf16[4,8,2,16,1792]{4,3,2,1,0:T(8,128)(2,1)}, bf16[4,8,2,16,1792]{4,3,2,1,0:T(8,128)(2,1)}) custom-call(s32[1]{0:T(128)} %bitcast.36.core_ref, bf16[1024,2048]{1,0:T(8,128)(2,1)} %get-tuple-element.39.h_ref.h1_ref, bf16[1024,2048]{1,0:T(8,128)(2,1)} %get-tuple-element.37.h_ref.h2_ref, bf16[1024,768]{1,0:T(8,128)(2,1)} %get-tuple-element.44.dq_ref, ...), custom_call_target="tpu_custom_call" | custom-call | flops 1000 | bytes 1000 | tf_op jit(solution)/shard_map/early_grads/pallas_call | solution.py:520
  205.4 4.2 copy.78
  212.0 11.9 %late_grads.1 = (bf16[8,80,2048]{2,1,0:T(8,128)(2,1)}, bf16[8,80,2048]{2,1,0:T(8,128)(2,1)}) custom-call(s32[1]{0:T(128)} %bitcast.36.core_ref, bf16[1024,1024]{1,0:T(8,128)(2,1)} %get-tuple-element.38.act_ref, bf16[1024,256]{1,0:T(8,128)(2,1)} %get-tuple-element.40.ol_ref, bf16[1024,2048]{1,0:T(8,128)(2,1)} %all-gather.2.cloned.1.call-done.dy_ref), custom_call_target="tpu_custom_call" | custom-call | flops 1000 | bytes 1000 | tf_op jit(solution)/shard_map/late_grads/pallas_call | solution.py:475
  225.7 14.7 %back_norms.1 = (bf16[1024,2048]{1,0:T(8,128)(2,1)}, f32[4,2048]{1,0:T(4,128)}) custom-call(bf16[1024,768]{1,0:T(8,128)(2,1)} %get-tuple-element.44.dq_ref, bf16[1024,1024]{1,0:T(8,128)(2,1)} %get-tuple-element.45.du_ref, bf16[2048,1792]{1,0:T(8,128)(2,1)} %bitcast.162, bf16[1024,2048]{1,0:T(8,128)(2,1)} %constant_dynamic-update-slice_fusion.1.x_ref, ...), custom_call_target="tpu_custom_call" | custom-call | flops 1000 | bytes 1000 | tf_op jit(solution)/shard_map/back_norms/pallas_call | solution.py:340
  246.1 11.1 %mixed_part.1 = bf16[1024,2048]{1,0:T(8,128)(2,1)} custom-call(bf16[1024,1024]{1,0:T(8,128)(2,1)} %get-tuple-element.38.act_ref, bf16[1024,256]{1,0:T(8,128)(2,1)} %get-tuple-element.40.ol_ref, bf16[1024,2048]{1,0:T(8,128)(2,1)} %wd_ref.3, bf16[256,2048]{1,0:T(8,128)(2,1)} %wo_ref.3, f32[1,2048]{1,0:T(1,128)} %copy-done.14), custom_call_target="tpu_custom_call" | custom-call | flops 1000 | bytes 1000 | tf_op jit(solution)/shard_map/mixed_part/pallas_call | solution.py:224
  268.3 64.3 %collective-permute-done.43 = bf16[4,80,2048]{2,1,0:T(8,128)(2,1)S(1)} collective-permute-done((bf16[4,80,2048]{2,1,0:T(8,128)(2,1)S(1)}, bf16[4,80,2048]{2,1,0:T(8,128)(2,1)S(1)}, u32[]{:S(2)}, u32[]{:S(2)}) %collective-permute-start.43) | collective-permute-done | bytes 1310752 | tf_op jit(solution)/shard_map/ppermute | solution.py:37
  341.1 19.0 %collective-permute-done.46 = bf16[40,2048]{1,0:T(8,128)(2,1)S(1)} collective-permute-done((bf16[40,2048]{1,0:T(8,128)(2,1)S(1)}, bf16[40,2048]{1,0:T(8,128)(2,1)S(1)}, u32[]{:S(2)}, u32[]{:S(2)}) %collective-permute-start.46) | collective-permute-done | bytes 163872 | tf_op jit(solution)/shard_map/ppermute | solution.py:37
  362.7 3.6 collective-permute-done.44
  369.2 8.0 %collective-permute-done.35 = bf16[8,16,1792]{2,1,0:T(8,128)(2,1)S(1)} collective-permute-done((bf16[8,16,1792]{2,1,0:T(8,128)(2,1)S(1)}, bf16[8,16,1792]{2,1,0:T(8,128)(2,1)S(1)}, u32[]{:S(2)}, u32[]{:S(2)}) %collective-permute-start.35) | collective-permute-done | bytes 458784 | tf_op jit(solution)/shard_map/ppermute | solution.py:37
  380.9 3.9 all-to-all-start.1
  387.2 4.8 all-to-all-done.1
  394.7 6.9 %collective-permute-done.36 = bf16[8,16,1792]{2,1,0:T(8,128)(2,1)S(1)} collective-permute-done((bf16[8,16,1792]{2,1,0:T(8,128)(2,1)S(1)}, bf16[8,16,1792]{2,1,0:T(8,128)(2,1)S(1)}, u32[]{:S(2)}, u32[]{:S(2)}) %collective-permute-start.36) | collective-permute-done | bytes 458784 | tf_op jit(solution)/shard_map/ppermute | solution.py:37
  408.6 10.1 %collective-permute-done.38 = bf16[2,8,16,1792]{3,2,1,0:T(8,128)(2,1)S(1)} collective-permute-done((bf16[2,8,16,1792]{3,2,1,0:T(8,128)(2,1)S(1)}, bf16[2,8,16,1792]{3,2,1,0:T(8,128)(2,1)S(1)}, u32[]{:S(2)}, u32[]{:S(2)}) %collective-permute-start.38) | collective-permute-done | bytes 917536 | tf_op jit(solution)/shard_map/ppermute | solution.py:37
  419.6 6.8 %collective-permute-done.37 = bf16[2,8,16,1792]{3,2,1,0:T(8,128)(2,1)S(1)} collective-permute-done((bf16[2,8,16,1792]{3,2,1,0:T(8,128)(2,1)S(1)}, bf16[2,8,16,1792]{3,2,1,0:T(8,128)(2,1)S(1)}, u32[]{:S(2)}, u32[]{:S(2)}) %collective-permute-start.37) | collective-permute-done | bytes 917536 | tf_op jit(solution)/shard_map/ppermute | solution.py:37
  430.9 4.7 collective-permute-done.39
  440.3 8.4 %collective-permute-start.41 = (bf16[8,8,16,1792]{3,2,1,0:T(8,128)(2,1)}, bf16[8,8,16,1792]{3,2,1,0:T(8,128)(2,1)}, u32[]{:S(2)}, u32[]{:S(2)}) collective-permute-start(bf16[8,8,16,1792]{3,2,1,0:T(8,128)(2,1)} %constant_dynamic-update-slice_fusion.7.mine_ref), channel_id=1, source_target_pairs={{0,8},{1,9},{2,10},{3,11},{4,12},{5,13},{6,14},{7,15},{8,0},{9,1},... | collective-permute-start | bytes 11010056 | tf_op jit(solution)/shard_map/ppermute | solution.py:37
  455.0 9.5 %collective-permute-done.26 = f32[24,1024]{1,0:T(8,128)S(1)} collective-permute-done((f32[24,1024]{1,0:T(8,128)S(1)}, f32[24,1024]{1,0:T(8,128)S(1)}, u32[]{:S(2)}, u32[]{:S(2)}) %collective-permute-start.26) | collective-permute-done | bytes 98336 | tf_op jit(solution)/shard_map/ppermute | solution.py:43
  469.4 10.0 %collective-permute-done.28 = f32[24,1024]{1,0:T(8,128)S(1)} collective-permute-done((f32[24,1024]{1,0:T(8,128)S(1)}, f32[24,1024]{1,0:T(8,128)S(1)}, u32[]{:S(2)}, u32[]{:S(2)}) %collective-permute-start.28) | collective-permute-done | bytes 98336 | tf_op jit(solution)/shard_map/ppermute | solution.py:43
  486.8 4.8 collective-permute-done.17
  497.2 3.6 collective-permute-start.54
  502.7 3.6 collective-permute-done.22
  510.8 12.9 %late_outputs.1 = (f32[1024,2048]{1,0:T(8,128)}, f32[256,2048]{1,0:T(8,128)}) custom-call(s32[16]{0:T(128)} %pad_add_fusion.3.spot_ref, bf16[4,80,2048]{2,1,0:T(8,128)(2,1)} %copy-done.3, bf16[4,80,2048]{2,1,0:T(8,128)(2,1)} %collective-permute-done.52.refs_1_, bf16[4,80,2048]{2,1,0:T(8,128)(2,1)} %collective-permute-done.53.refs_2_, ...), custom_call_target="tpu_custom_call" | custom-call | flops 1000 | bytes 1000 | tf_op jit(solution)/shard_map/late_outputs/pallas_call | solution.py:558
  523.8 13.8 %early_outputs.1 = (f32[256,6144]{1,0:T(8,128)}, f32[256,8192]{1,0:T(8,128)}) custom-call(s32[16]{0:T(128)} %pad_add_fusion.2.spot_ref, bf16[8,8,16,1792]{3,2,1,0:T(8,128)(2,1)} %constant_dynamic-update-slice_fusion.7.mine_ref, bf16[8,8,16,1792]{3,2,1,0:T(8,128)(2,1)} %collective-permute-done.41.yours_ref), custom_call_target="tpu_custom_call" | custom-call | flops 1000 | bytes 1000 | tf_op jit(solution)/shard_map/early_outputs/pallas_call | solution.py:605
  (289 shorter events, 153.3 us)
Async XLA Ops:
  7.2 165.1 %all-gather.2.cloned.1.call-start = ((), (), s32[]{:S(2)}) async-start(), calls=%async_computation.4 | async-start | bytes 4718592 | tf_op jit(solution)/shard_map/all_gather | solution.py:677
  7.9 500.0 %reduce-scatter.2.cloned.1.call-start = ((), (), s32[]{:S(2)}) async-start(), calls=%async_computation.3 | async-start | bytes 4718592 | tf_op jit(solution)/shard_map/reduce_scatter | solution.py:707
  51.2 20.2 %collective-permute-start.9 = (bf16[8,32,1792]{2,1,0:T(8,128)(2,1)S(1)}, bf16[8,32,1792]{2,1,0:T(8,128)(2,1)S(1)}, u32[]{:S(2)}, u32[]{:S(2)}) collective-permute-start(bf16[8,32,1792]{2,1,0:T(8,128)(2,1)S(1)} %get-tuple-element.82), channel_id=1, source_target_pairs={{0,96},{1,97},{2,98},{3,99},{4,100},{5,101},{6,102},{7,103},{8,104... | collective-permute-start | bytes 2752520 | tf_op jit(solution)/shard_map/ppermute | solution.py:37
  54.0 21.0 %collective-permute-start.10 = (bf16[8,32,1792]{2,1,0:T(8,128)(2,1)S(1)}, bf16[8,32,1792]{2,1,0:T(8,128)(2,1)S(1)}, u32[]{:S(2)}, u32[]{:S(2)}) collective-permute-start(bf16[8,32,1792]{2,1,0:T(8,128)(2,1)S(1)} %get-tuple-element.82), channel_id=1, source_target_pairs={{0,32},{1,33},{2,34},{3,35},{4,36},{5,37},{6,38},{7,39},{8,40},{9,... | collective-permute-start | bytes 2752520 | tf_op jit(solution)/shard_map/ppermute | solution.py:37
  75.1 19.8 %collective-permute-start = (bf16[128,2048]{1,0:T(8,128)(2,1)S(1)}, bf16[128,2048]{1,0:T(8,128)(2,1)}, u32[]{:S(2)}, u32[]{:S(2)}) collective-permute-start(bf16[128,2048]{1,0:T(8,128)(2,1)S(1)} %copy-done.2), channel_id=1, source_target_pairs={{0,3},{1,0},{2,1},{3,2},{4,7},{5,4},{6,5},{7,6},{8,11},{9,8},{10,9... | collective-permute-start | bytes 1572872 | tf_op jit(solution)/shard_map/ppermute | solution.py:37
  76.8 20.7 %collective-permute-start.1 = (bf16[128,2048]{1,0:T(8,128)(2,1)S(1)}, bf16[128,2048]{1,0:T(8,128)(2,1)S(1)}, u32[]{:S(2)}, u32[]{:S(2)}) collective-permute-start(bf16[128,2048]{1,0:T(8,128)(2,1)S(1)} %copy-done.2), channel_id=1, source_target_pairs={{0,1},{1,2},{2,3},{3,0},{4,5},{5,6},{6,7},{7,4},{8,9},{9,10},{10,1... | collective-permute-start | bytes 1572872 | tf_op jit(solution)/shard_map/ppermute | solution.py:37
  76.8 22.0 %collective-permute-start.4 = (bf16[128,2048]{1,0:T(8,128)(2,1)S(1)}, bf16[128,2048]{1,0:T(8,128)(2,1)}, u32[]{:S(2)}, u32[]{:S(2)}) collective-permute-start(bf16[128,2048]{1,0:T(8,128)(2,1)S(1)} %copy-done.2), channel_id=1, source_target_pairs={{0,4},{1,5},{2,6},{3,7},{4,0},{5,1},{6,2},{7,3},{8,12},{9,13},{10,... | collective-permute-start | bytes 1572872 | tf_op jit(solution)/shard_map/ppermute | solution.py:37
  87.2 50.9 %collective-permute-start.13 = (bf16[4,8,32,1792]{3,2,1,0:T(8,128)(2,1)}, bf16[4,8,32,1792]{3,2,1,0:T(8,128)(2,1)}, u32[]{:S(2)}, u32[]{:S(2)}) collective-permute-start(bf16[4,8,32,1792]{3,2,1,0:T(8,128)(2,1)} %pad_maximum_fusion.mine_ref), channel_id=1, source_target_pairs={{0,8},{1,9},{2,10},{3,11},{4,12},{5,13},{6,14},{7,15},{8,0},{9,1},... | collective-permute-start | bytes 11010056 | tf_op jit(solution)/shard_map/ppermute | solution.py:37
  101.5 17.5 %collective-permute-start.6 = (bf16[128,2048]{1,0:T(8,128)(2,1)}, bf16[128,2048]{1,0:T(8,128)(2,1)S(1)}, u32[]{:S(2)}, u32[]{:S(2)}) collective-permute-start(bf16[128,2048]{1,0:T(8,128)(2,1)} %collective-permute-done.4), channel_id=1, source_target_pairs={{0,1},{1,2},{2,3},{3,0},{4,5},{5,6},{6,7},{7,4},{8,9},{9,10},{10,1... | collective-permute-start | bytes 1572872 | tf_op jit(solution)/shard_map/ppermute | solution.py:37
  209.6 54.6 %collective-permute-start.30 = (bf16[4,8,2,16,1792]{4,3,1,2,0:T(8,128)(2,1)}, bf16[4,8,2,16,1792]{4,3,1,2,0:T(8,128)(2,1)}, u32[]{:S(2)}, u32[]{:S(2)}) collective-permute-start(bf16[4,8,2,16,1792]{4,3,1,2,0:T(8,128)(2,1)} %copy.78), channel_id=1, source_target_pairs={{0,8},{1,9},{2,10},{3,11},{4,12},{5,13},{6,14},{7,15},{8,0},{9,1},... | collective-permute-start | bytes 11010056 | tf_op jit(solution)/shard_map/ppermute | solution.py:37
  223.9 34.8 %collective-permute-start.42 = (bf16[4,2,80,2048]{3,2,1,0:T(8,128)(2,1)}, bf16[4,2,80,2048]{3,2,1,0:T(8,128)(2,1)}, u32[]{:S(2)}, u32[]{:S(2)}) collective-permute-start(bf16[4,2,80,2048]{3,2,1,0:T(8,128)(2,1)} %bitcast.202), channel_id=1, source_target_pairs={{0,8},{1,9},{2,10},{3,11},{4,12},{5,13},{6,14},{7,15},{8,0},{9,1},... | collective-permute-start | bytes 7864328 | tf_op jit(solution)/shard_map/ppermute | solution.py:37
  257.2 82.4 %collective-permute-start.24 = (f32[24,1024]{1,0:T(8,128)S(1)}, f32[24,1024]{1,0:T(8,128)S(1)}, u32[]{:S(2)}, u32[]{:S(2)}) collective-permute-start(f32[24,1024]{1,0:T(8,128)S(1)} %add.645), channel_id=1, source_target_pairs={{0,4},{1,5},{2,6},{3,7},{4,0},{5,1},{6,2},{7,3},{8,12},{9,13},{10,... | collective-permute-start | bytes 294920 | tf_op jit(solution)/shard_map/ppermute | solution.py:43
  260.8 71.8 %collective-permute-start.43 = (bf16[4,80,2048]{2,1,0:T(8,128)(2,1)S(1)}, bf16[4,80,2048]{2,1,0:T(8,128)(2,1)S(1)}, u32[]{:S(2)}, u32[]{:S(2)}) collective-permute-start(bf16[4,80,2048]{2,1,0:T(8,128)(2,1)S(1)} %fusion.1), channel_id=1, source_target_pairs={{0,16},{1,17},{2,18},{3,19},{4,20},{5,21},{6,22},{7,23},{8,24},{9,... | collective-permute-start | bytes 3932168 | tf_op jit(solution)/shard_map/ppermute | solution.py:37
  266.6 68.5 %collective-permute-start.33 = (bf16[4,2,16,1792]{3,2,0,1:T(8,128)(2,1)S(1)}, bf16[4,2,16,1792]{3,2,0,1:T(8,128)(2,1)S(1)}, u32[]{:S(2)}, u32[]{:S(2)}) collective-permute-start(bf16[4,2,16,1792]{3,2,0,1:T(8,128)(2,1)S(1)} %get-tuple-element.84), channel_id=1, source_target_pairs={{0,96},{1,97},{2,98},{3,99},{4,100},{5,101},{6,102},{7,103},{8,104... | collective-permute-start | bytes 1376264 | tf_op jit(solution)/shard_map/ppermute | solution.py:37
  266.9 68.5 %collective-permute-start.31 = (bf16[4,2,16,1792]{3,2,0,1:T(8,128)(2,1)S(1)}, bf16[4,2,16,1792]{3,2,0,1:T(8,128)(2,1)S(1)}, u32[]{:S(2)}, u32[]{:S(2)}) collective-permute-start(bf16[4,2,16,1792]{3,2,0,1:T(8,128)(2,1)S(1)} %get-tuple-element.83), channel_id=1, source_target_pairs={{0,32},{1,33},{2,34},{3,35},{4,36},{5,37},{6,38},{7,39},{8,40},{9,... | collective-permute-start | bytes 1376264 | tf_op jit(solution)/shard_map/ppermute | solution.py:37
  335.3 25.6 %collective-permute-start.34 = (bf16[8,2,16,1792]{3,2,0,1:T(8,128)(2,1)S(1)}, bf16[8,2,16,1792]{3,2,0,1:T(8,128)(2,1)S(1)}, u32[]{:S(2)}, u32[]{:S(2)}) collective-permute-start(bf16[8,2,16,1792]{3,2,0,1:T(8,128)(2,1)S(1)} %pad_maximum_fusion.4), channel_id=1, source_target_pairs={{0,96},{1,97},{2,98},{3,99},{4,100},{5,101},{6,102},{7,103},{8,104... | collective-permute-start | bytes 2752520 | tf_op jit(solution)/shard_map/ppermute | solution.py:37
  335.6 25.3 %collective-permute-start.32 = (bf16[8,2,16,1792]{3,2,0,1:T(8,128)(2,1)S(1)}, bf16[8,2,16,1792]{3,2,0,1:T(8,128)(2,1)S(1)}, u32[]{:S(2)}, u32[]{:S(2)}) collective-permute-start(bf16[8,2,16,1792]{3,2,0,1:T(8,128)(2,1)S(1)} %pad_maximum_fusion.3), channel_id=1, source_target_pairs={{0,32},{1,33},{2,34},{3,35},{4,36},{5,37},{6,38},{7,39},{8,40},{9,... | collective-permute-start | bytes 2752520 | tf_op jit(solution)/shard_map/ppermute | solution.py:37
  337.1 23.1 %collective-permute-start.46 = (bf16[40,2048]{1,0:T(8,128)(2,1)S(1)}, bf16[40,2048]{1,0:T(8,128)(2,1)S(1)}, u32[]{:S(2)}, u32[]{:S(2)}) collective-permute-start(bf16[40,2048]{1,0:T(8,128)(2,1)S(1)} %get-tuple-element.88), channel_id=1, source_target_pairs={{0,96},{1,97},{2,98},{3,99},{4,100},{5,101},{6,102},{7,103},{8,104... | collective-permute-start | bytes 491528 | tf_op jit(solution)/shard_map/ppermute | solution.py:37
  339.6 46.0 %collective-permute-start.14 = (bf16[64,2048]{1,0:T(8,128)(2,1)}, bf16[64,2048]{1,0:T(8,128)(2,1)}, u32[]{:S(2)}, u32[]{:S(2)}) collective-permute-start(bf16[64,2048]{1,0:T(8,128)(2,1)} %get-tuple-element.73), channel_id=1, source_target_pairs={{0,1},{1,2},{2,3},{3,0},{4,5},{5,6},{6,7},{7,4},{8,9},{9,10},{10,1... | collective-permute-start | bytes 786440 | tf_op jit(solution)/shard_map/ppermute | solution.py:37
  339.7 47.1 %collective-permute-start.18 = (bf16[64,2048]{1,0:T(8,128)(2,1)}, bf16[64,2048]{1,0:T(8,128)(2,1)}, u32[]{:S(2)}, u32[]{:S(2)}) collective-permute-start(bf16[64,2048]{1,0:T(8,128)(2,1)} %get-tuple-element.75), channel_id=1, source_target_pairs={{0,1},{1,2},{2,3},{3,0},{4,5},{5,6},{6,7},{7,4},{8,9},{9,10},{10,1... | collective-permute-start | bytes 786440 | tf_op jit(solution)/shard_map/ppermute | solution.py:37
  360.1 27.0 %collective-permute-start.20 = (bf16[64,2048]{1,0:T(8,128)(2,1)}, bf16[64,2048]{1,0:T(8,128)(2,1)}, u32[]{:S(2)}, u32[]{:S(2)}) collective-permute-start(bf16[64,2048]{1,0:T(8,128)(2,1)} %get-tuple-element.77), channel_id=1, source_target_pairs={{0,3},{1,0},{2,1},{3,2},{4,7},{5,4},{6,5},{7,6},{8,11},{9,8},{10,9... | collective-permute-start | bytes 786440 | tf_op jit(solution)/shard_map/ppermute | solution.py:37
  360.9 31.9 %collective-permute-start.16 = (bf16[64,2048]{1,0:T(8,128)(2,1)}, bf16[64,2048]{1,0:T(8,128)(2,1)}, u32[]{:S(2)}, u32[]{:S(2)}) collective-permute-start(bf16[64,2048]{1,0:T(8,128)(2,1)} %get-tuple-element.79), channel_id=1, source_target_pairs={{0,3},{1,0},{2,1},{3,2},{4,7},{5,4},{6,5},{7,6},{8,11},{9,8},{10,9... | collective-permute-start | bytes 786440 | tf_op jit(solution)/shard_map/ppermute | solution.py:37
  377.2 72.4 %collective-permute-start.25 = (f32[24,1024]{1,0:T(8,128)S(1)}, f32[24,1024]{1,0:T(8,128)}, u32[]{:S(2)}, u32[]{:S(2)}) collective-permute-start(f32[24,1024]{1,0:T(8,128)S(1)} %add.646), channel_id=1, source_target_pairs={{0,16},{1,17},{2,18},{3,19},{4,20},{5,21},{6,22},{7,23},{8,24},{9,... | collective-permute-start | bytes 294920 | tf_op jit(solution)/shard_map/ppermute | solution.py:43
  403.6 51.2 %collective-permute-start.49 = (bf16[80,2048]{1,0:T(8,128)(2,1)S(1)}, bf16[80,2048]{1,0:T(8,128)(2,1)S(1)}, u32[]{:S(2)}, u32[]{:S(2)}) collective-permute-start(bf16[80,2048]{1,0:T(8,128)(2,1)S(1)} %fusion.26), channel_id=1, source_target_pairs={{0,32},{1,33},{2,34},{3,35},{4,36},{5,37},{6,38},{7,39},{8,40},{9,... | collective-permute-start | bytes 983048 | tf_op jit(solution)/shard_map/ppermute | solution.py:37
  403.7 47.6 %collective-permute-start.48 = (bf16[80,2048]{1,0:T(8,128)(2,1)S(1)}, bf16[80,2048]{1,0:T(8,128)(2,1)S(1)}, u32[]{:S(2)}, u32[]{:S(2)}) collective-permute-start(bf16[80,2048]{1,0:T(8,128)(2,1)S(1)} %fusion.26), channel_id=1, source_target_pairs={{0,96},{1,97},{2,98},{3,99},{4,100},{5,101},{6,102},{7,103},{8,104... | collective-permute-start | bytes 983048 | tf_op jit(solution)/shard_map/ppermute | solution.py:37
  406.4 20.0 %collective-permute-start.37 = (bf16[2,8,16,1792]{3,2,1,0:T(8,128)(2,1)S(1)}, bf16[2,8,16,1792]{3,2,1,0:T(8,128)(2,1)S(1)}, u32[]{:S(2)}, u32[]{:S(2)}) collective-permute-start(bf16[2,8,16,1792]{3,2,1,0:T(8,128)(2,1)S(1)} %pad_maximum_fusion.5), channel_id=1, source_target_pairs={{0,96},{1,97},{2,98},{3,99},{4,100},{5,101},{6,102},{7,103},{8,104... | collective-permute-start | bytes 2752520 | tf_op jit(solution)/shard_map/ppermute | solution.py:37
  440.3 83.4 %collective-permute-start.41 = (bf16[8,8,16,1792]{3,2,1,0:T(8,128)(2,1)}, bf16[8,8,16,1792]{3,2,1,0:T(8,128)(2,1)}, u32[]{:S(2)}, u32[]{:S(2)}) collective-permute-start(bf16[8,8,16,1792]{3,2,1,0:T(8,128)(2,1)} %constant_dynamic-update-slice_fusion.7.mine_ref), channel_id=1, source_target_pairs={{0,8},{1,9},{2,10},{3,11},{4,12},{5,13},{6,14},{7,15},{8,0},{9,1},... | collective-permute-start | bytes 11010056 | tf_op jit(solution)/shard_map/ppermute | solution.py:37
  448.8 30.7 %collective-permute-start.21 = (bf16[128,2048]{1,0:T(8,128)(2,1)S(1)}, bf16[128,2048]{1,0:T(8,128)(2,1)S(1)}, u32[]{:S(2)}, u32[]{:S(2)}) collective-permute-start(bf16[128,2048]{1,0:T(8,128)(2,1)S(1)} %pad_maximum_fusion.9), channel_id=1, source_target_pairs={{0,3},{1,0},{2,1},{3,2},{4,7},{5,4},{6,5},{7,6},{8,11},{9,8},{10,9... | collective-permute-start | bytes 1572872 | tf_op jit(solution)/shard_map/ppermute | solution.py:37
  466.3 30.9 %collective-permute-start.52 = (bf16[4,80,2048]{2,1,0:T(8,128)(2,1)S(1)}, bf16[4,80,2048]{2,1,0:T(8,128)(2,1)}, u32[]{:S(2)}, u32[]{:S(2)}) collective-permute-start(bf16[4,80,2048]{2,1,0:T(8,128)(2,1)S(1)} %pad_maximum_fusion.1.refs_0_), channel_id=1, source_target_pairs={{0,16},{1,17},{2,18},{3,19},{4,20},{5,21},{6,22},{7,23},{8,24},{9,... | collective-permute-start | bytes 3932168 | tf_op jit(solution)/shard_map/ppermute | solution.py:37
  479.5 23.2 %collective-permute-start.15 = (bf16[128,2048]{1,0:T(8,128)(2,1)S(1)}, bf16[128,2048]{1,0:T(8,128)(2,1)S(1)}, u32[]{:S(2)}, u32[]{:S(2)}) collective-permute-start(bf16[128,2048]{1,0:T(8,128)(2,1)S(1)} %pad_maximum_fusion.6), channel_id=1, source_target_pairs={{0,1},{1,2},{2,3},{3,0},{4,5},{5,6},{6,7},{7,4},{8,9},{9,10},{10,1... | collective-permute-start | bytes 1572872 | tf_op jit(solution)/shard_map/ppermute | solution.py:37
  486.5 19.8 %collective-permute-start.22 = (bf16[128,2048]{1,0:T(8,128)(2,1)S(1)}, bf16[128,2048]{1,0:T(8,128)(2,1)S(1)}, u32[]{:S(2)}, u32[]{:S(2)}) collective-permute-start(bf16[128,2048]{1,0:T(8,128)(2,1)S(1)} %fusion.13), channel_id=1, source_target_pairs={{0,4},{1,5},{2,6},{3,7},{4,0},{5,1},{6,2},{7,3},{8,12},{9,13},{10,... | collective-permute-start | bytes 1572872 | tf_op jit(solution)/shard_map/ppermute | solution.py:37
  491.6 19.2 %collective-permute-start.53 = (bf16[4,80,2048]{2,1,0:T(8,128)(2,1)S(1)}, bf16[4,80,2048]{2,1,0:T(8,128)(2,1)}, u32[]{:S(2)}, u32[]{:S(2)}) collective-permute-start(bf16[4,80,2048]{2,1,0:T(8,128)(2,1)S(1)} %pad_maximum_fusion.1.refs_0_), channel_id=1, source_target_pairs={{0,8},{1,9},{2,10},{3,11},{4,12},{5,13},{6,14},{7,15},{8,0},{9,1},... | collective-permute-start | bytes 3932168 | tf_op jit(solution)/shard_map/ppermute | solution.py:37
  (47 other events, 726.6 us)
Sparse Core Ops, SparseCore 0:
  9.7 68.1 all-gather.1
  257.3 49.7 reduce-scatter.1
where the time goes:
time: 556 us; the launch traced here: 545 us
  waiting for transfers between devices  196 us (35%)
  Pallas kernels  141 us (25%)
  starting transfers between devices  81.6 us (15%)
  other arithmetic  39 us (7%)
  local copies, waits for them, and re-layouts  38.2 us (7%)
  blocking collectives  34.3 us (6%)
  between operations  15.4 us (3%)
    ppermute x48, waiting for transfers between devices, move(): return lax.ppermute(value, BOTH, pairs)  169 us
    ppermute x48, starting transfers between devices, move(): return lax.ppermute(value, BOTH, pairs)  66.2 us
    all_to_all x1, blocking collectives, local(): part = lax.all_to_all(part, 'shard', 0, 0)  34.3 us
    ppermute x7, waiting for transfers between devices, swap(): return lax.ppermute(value, BOTH, pairs)  21.6 us
    pallas_call x1, Pallas kernels, back_inner(): pl.pallas_call(body, out_shape=(jax.ShapeDtypeStruct((total, ff), bf16),...  18.6 us
    pallas_call x1, Pallas kernels, back_norms(): pl.pallas_call(body, out_shape=(jax.ShapeDtypeStruct((total, width), bf16...  14.7 us
    pallas_call x1, Pallas kernels, early_grads(): pl.pallas_call(body, out_shape=(out, out), grid_spec=pltpu.PrefetchScalar...  14.5 us
    pallas_call x1, Pallas kernels, attention(): pl.pallas_call(body, out_shape=(jax.ShapeDtypeStruct((total, 3 * head), b...  14.4 us
  transfers between devices with their start and end apart: 58, of which 25 were waited for; matrix products, arithmetic and copies ran while one was open for 13% of the time, Pallas kernels for 17%

commit v1 on v0

--- a/solution.py
+++ b/solution.py
@@ -15,6 +15,8 @@
 COST = pl.CostEstimate(flops=1000, bytes_accessed=1000, transcendentals=0)
 BOTH = ("rep", "shard")
 SIZES = (4, 2, 2, 2, 4)
+SAME_CORE = [[2 * n + c for n in range(8)] for c in range(2)]
+SAME_CORE_ALL = [[(2 * n + c) * 8 + s for n in range(8) for s in range(8)] for c in range(2)]
 
 
 def coords():
@@ -55,33 +57,6 @@
     return [own, above, jnp.concatenate([far_low, far_high], 0), below]
 
 
-def ring_reduce(pieces, axis, cut):
-    own, above, far, below = pieces
-    low = move(far[:cut].astype(bf16), **{axis: 1})
-    high = move(far[cut:].astype(bf16), **{axis: -1})
-    up = jnp.concatenate([above[:cut].astype(f32) + low.astype(f32), above[cut:].astype(f32)], 0)
-    down = jnp.concatenate([below[:cut].astype(f32), below[cut:].astype(f32) + high.astype(f32)], 0)
-    from_below = move(up.astype(bf16), **{axis: 1})
-    from_above = move(down.astype(bf16), **{axis: -1})
-    return own.astype(f32) + from_below.astype(f32) + from_above.astype(f32)
-
-
-def group_gather(own, cut):
-    other = move(own, l=1)
-    return ring_gather(own, "x", cut) + ring_gather(other, "x", cut)
-
-
-def group_reduce(pieces, cut):
-    other = ring_reduce(pieces[4:], "x", cut)
-    crossed = move(other.astype(bf16), l=1)
-    return ring_reduce(pieces[:4], "x", cut) + crossed.astype(f32)
-
-
-def place(pieces, start, count, axis):
-    full = jnp.stack(pieces + pieces[:-1], axis)
-    return lax.dynamic_slice_in_dim(full, (count - start) % count, count, axis)
-
-
 def normalize(value):
     xf = value.astype(f32)
     centre = xf - jnp.mean(xf, -1, keepdims=True)
@@ -91,6 +66,14 @@
 
 def kernel_params():
     return pltpu.CompilerParams(vmem_limit_bytes=56 * 1024 * 1024)
+
+
+def after_inputs(body, count, extra):
+    return lambda *refs: body(*refs[:count], *refs[count + extra :])
+
+
+def anywhere(count):
+    return [pl.BlockSpec(memory_space=pl.ANY)] * count
 
 
 def dot(a, b, ca=1, cb=0):
@@ -213,17 +196,19 @@
     )(lengths, h1, weight, bias, cosine, sine)
 
 
-def mixed_part(active, attended, down, out, bias):
+def mixed_part(active, attended, down, out, bias, after):
     rows, ff = active.shape
     head, width = out.shape
-
-    def body(act_ref, ol_ref, wd_ref, wo_ref, b_ref, mix_ref):
+    count = rows // 128
+
+    def body(act_ref, ol_ref, wd_ref, wo_ref, b_ref, *refs):
         total = dot(act_ref[...], wd_ref[...]) + dot(ol_ref[...], wo_ref[...]) + b_ref[...]
-        mix_ref[...] = total.astype(bf16)
-
-    return pl.pallas_call(
-        body,
-        out_shape=jax.ShapeDtypeStruct((rows, width), bf16),
+        for at in range(count):
+            refs[at][...] = total[at * 128 : (at + 1) * 128].astype(bf16)
+
+    return pl.pallas_call(
+        after_inputs(body, 5, len(after)),
+        out_shape=(jax.ShapeDtypeStruct((128, width), bf16),) * count,
         grid=(width // 256,),
         in_specs=[
             pl.BlockSpec((rows, ff), lambda i: (0, 0)),
@@ -231,23 +216,32 @@
             pl.BlockSpec((ff, 256), lambda i: (0, i)),
             pl.BlockSpec((head, 256), lambda i: (0, i)),
             pl.BlockSpec((1, 256), lambda i: (0, i)),
-        ],
-        out_specs=pl.BlockSpec((rows, 256), lambda i: (0, i)),
+        ]
+        + anywhere(len(after)),
+        out_specs=(pl.BlockSpec((128, 256), lambda i: (0, i)),) * count,
         compiler_params=kernel_params(),
         cost_estimate=COST,
         name="mixed_part",
-    )(active, attended, down, out, bias)
-
-
-def back_inner(dy, down, out, slope, qkv, probs, cosine, sine, rows=128):
-    total, width = dy.shape
+    )(active, attended, down, out, bias, *after)
+
+
+def back_inner(dy, down, out, slope, qkv, probs, cosine, sine, after, rows=128):
+    width = dy[0].shape[1]
+    count = len(dy)
+    total = count * rows
     ff, head = down.shape[0], out.shape[0]
     steps = ff // 256
     blocks = total // rows
     scale = head ** (-0.5)
 
-    def body(dy_ref, wd_ref, wo_ref, s_ref, qkv_ref, p_ref, cos_ref, sin_ref, du_ref, db_ref, dq_ref, dqb_ref, work):
+    def body(*refs):
+        wd_ref, wo_ref, s_ref, qkv_ref, p_ref, cos_ref, sin_ref = refs[count : count + 7]
+        du_ref, db_ref, dq_ref, dqb_ref, work, dy_ref, sems = refs[count + 7 :]
         step = pl.program_id(0)
+
+        @pl.when(step == 0)
+        def _():
+            fetch(refs[:count], dy_ref, sems, rows)
 
         @pl.when(step < steps)
         def _():
@@ -291,7 +285,7 @@
         return (jnp.maximum(i - steps - 1, 0), 0)
 
     return pl.pallas_call(
-        body,
+        after_inputs(body, count + 7, len(after)),
         out_shape=(
             jax.ShapeDtypeStruct((total, ff), bf16),
             jax.ShapeDtypeStruct((1, ff), f32),
@@ -299,8 +293,8 @@
             jax.ShapeDtypeStruct((1, 3 * head), f32),
         ),
         grid=(steps + 1 + blocks,),
-        in_specs=[
-            pl.BlockSpec((total, width), lambda i: (0, 0)),
+        in_specs=anywhere(count)
+        + [
             pl.BlockSpec((256, width), lambda i: (part(i), 0)),
             pl.BlockSpec((head, width), lambda i: (0, 0)),
             pl.BlockSpec((total, 256), lambda i: (0, part(i))),
@@ -308,41 +302,47 @@
             pl.BlockSpec((rows, rows), at_block),
             pl.BlockSpec((rows, 128), at_block),
             pl.BlockSpec((rows, 128), at_block),
-        ],
+        ]
+        + anywhere(len(after)),
         out_specs=(
             pl.BlockSpec((total, 256), lambda i: (0, part(i))),
             pl.BlockSpec((1, 256), lambda i: (0, part(i))),
             pl.BlockSpec((rows, 3 * head), at_block),
             pl.BlockSpec((1, 3 * head), lambda i: (0, 0)),
         ),
-        scratch_shapes=[pltpu.VMEM((total, head), bf16)],
+        scratch_shapes=[
+            pltpu.VMEM((total, head), bf16),
+            pltpu.VMEM((total, width), bf16),
+            pltpu.SemaphoreType.DMA((count,)),
+        ],
         compiler_params=kernel_params(),
         cost_estimate=COST,
         name="back_inner",
-    )(dy, down, out, slope, qkv, probs, cosine, sine)
-
-
-def back_norms(d_qkv, d_hidden, weight, tokens, mean, inverse, gains):
+    )(*dy, down, out, slope, qkv, probs, cosine, sine, *after)
+
+
+def back_norms(d_qkv, d_hidden, weight, tokens, mean, inverse, gains, after):
     total, n1 = d_qkv.shape
     n2 = d_hidden.shape[1]
     width = tokens.shape[1]
-
-    def body(dq_ref, du_ref, w_ref, x_ref, m_ref, i_ref, g_ref, s_ref, sums_ref):
+    count = total // 128
+
+    def body(dq_ref, du_ref, w_ref, x_ref, m_ref, i_ref, g_ref, sums_ref, *refs):
         d1 = dot(dq_ref[...], w_ref[:, :n1], 1, 1)
         d2 = dot(du_ref[...], w_ref[:, n1:], 1, 1)
         normed = (x_ref[...].astype(f32) - m_ref[...]) * i_ref[...]
-        s_ref[...] = (d1 * g_ref[0:1] + d2 * g_ref[1:2]).astype(bf16)
+        both = (d1 * g_ref[0:1] + d2 * g_ref[1:2]).astype(bf16)
+        for at in range(count):
+            refs[at][...] = both[at * 128 : (at + 1) * 128]
         sums_ref[0:1] = jnp.sum(d1 * normed, 0, keepdims=True)
         sums_ref[1:2] = jnp.sum(d1, 0, keepdims=True)
         sums_ref[2:3] = jnp.sum(d2 * normed, 0, keepdims=True)
         sums_ref[3:4] = jnp.sum(d2, 0, keepdims=True)
 
     return pl.pallas_call(
-        body,
-        out_shape=(
-            jax.ShapeDtypeStruct((total, width), bf16),
-            jax.ShapeDtypeStruct((4, width), f32),
-        ),
+        after_inputs(body, 7, len(after)),
+        out_shape=(jax.ShapeDtypeStruct((4, width), f32),)
+        + (jax.ShapeDtypeStruct((128, width), bf16),) * count,
         grid=(width // 256,),
         in_specs=[
             pl.BlockSpec((total, n1), lambda i: (0, 0)),
@@ -352,26 +352,33 @@
             pl.BlockSpec((total, 1), lambda i: (0, 0)),
             pl.BlockSpec((total, 1), lambda i: (0, 0)),
             pl.BlockSpec((2, 256), lambda i: (0, i)),
-        ],
-        out_specs=(
-            pl.BlockSpec((total, 256), lambda i: (0, i)),
-            pl.BlockSpec((4, 256), lambda i: (0, i)),
-        ),
+        ]
+        + anywhere(len(after)),
+        out_specs=(pl.BlockSpec((4, 256), lambda i: (0, i)),)
+        + (pl.BlockSpec((128, 256), lambda i: (0, i)),) * count,
         compiler_params=kernel_params(),
         cost_estimate=COST,
         name="back_norms",
-    )(d_qkv, d_hidden, weight, tokens, mean, inverse, gains)
-
-
-def norms(tokens, gains):
-    total, width = tokens.shape
-    rows = 128
-
-    def body(x_ref, g_ref, h1_ref, h2_ref, m_ref, i_ref):
+    )(d_qkv, d_hidden, weight, tokens, mean, inverse, gains, *after)
+
+
+def norms(pieces, gains):
+    rows, width = pieces[0].shape
+    count = len(pieces)
+    total = rows * count
+
+    def body(*refs):
+        g_ref, x_ref, h1_ref, h2_ref, m_ref, i_ref = refs[count:]
+        for at in range(count):
+
+            @pl.when(pl.program_id(0) == at)
+            def _(at=at):
+                x_ref[...] = refs[at][...]
+
         x = x_ref[...].astype(f32)
         mean = jnp.mean(x, 1, keepdims=True)
         centre = x - mean
-        inverse = lax.rsqrt(jnp.mean(centre * centre, 1, keepdims=True) + 1e-5)
+        inverse = lax.rsqrt(jnp.mean(centre * centre, 1, keepdims=True) + EPS)
         normed = centre * inverse
         m_ref[...] = mean
         i_ref[...] = inverse
@@ -384,61 +391,180 @@
     thin = pl.BlockSpec((rows, 1), lambda i: (i, 0))
     return pl.pallas_call(
         body,
-        out_shape=(wide, wide, column, column),
-        grid=(total // rows,),
-        in_specs=[block, pl.BlockSpec((4, width), lambda i: (0, 0))],
-        out_specs=(block, block, thin, thin),
+        out_shape=(wide, wide, wide, column, column),
+        grid=(count,),
+        in_specs=[pl.BlockSpec((rows, width), lambda i: (0, 0))] * count
+        + [pl.BlockSpec((4, width), lambda i: (0, 0))],
+        out_specs=(block, block, block, thin, thin),
         compiler_params=kernel_params(),
         cost_estimate=COST,
         name="norms",
-    )(tokens, gains)
+    )(*pieces, gains)
+
+
+def fetch(pieces, target, sems, rows):
+    copies = [
+        pltpu.make_async_copy(piece, target.at[pl.ds(at * rows, rows)], sems.at[at])
+        for at, piece in enumerate(pieces)
+    ]
+    for copy in copies:
+        copy.start()
+    for copy in copies:
+        copy.wait()
 
 
 def dot_rows(a, b):
     return lax.dot_general(a, b, (((0,), (0,)), ((), ())), preferred_element_type=f32)
 
 
-def sorted_weight(mine, yours, spots):
-    sources, rows, cols = mine.shape[1:]
-
-    def body(spot_ref, mine_ref, yours_ref, out_ref):
-        step = pl.program_id(0)
-
-        @pl.when(step < 4)
-        def _():
-            out_ref[:, 0] = mine_ref[0]
-
-        @pl.when(step >= 4)
-        def _():
-            out_ref[:, 0] = yours_ref[0]
-
-    block = (1, sources, rows, cols)
+def packed(qkv_weight, up_weight, vectors, lengths, place, head):
+    wide, up_wide = qkv_weight.shape[1], up_weight.shape[1]
+    part, up_part = 3 * head, up_wide // 8
+    cols = part + up_part
+
+    def body(place_ref, len_ref, q_ref, u_ref, v_ref, out_ref):
+        lane = lax.broadcasted_iota(jnp.int32, (8, cols), 1)
+        row = lax.broadcasted_iota(jnp.int32, (8, cols), 0)
+        sizes = jnp.zeros((8, cols), f32)
+        for at in range(3):
+            sizes = jnp.where(lane == at, len_ref[0, at].astype(f32), sizes)
+        vector = jnp.broadcast_to(v_ref[...].astype(f32), (8, cols))
+        tail = jnp.where(row == 0, vector, jnp.where(row == 1, sizes, 0.0)).astype(bf16)
+        for owner in range(8):
+            pieces = [
+                q_ref[:, (third * 8 + owner) * head : (third * 8 + owner + 1) * head]
+                for third in range(3)
+            ]
+            pieces.append(u_ref[:, owner * up_part : (owner + 1) * up_part])
+            out_ref[owner] = jnp.concatenate([jnp.concatenate(pieces, 1), tail], 0)
+
     return pl.pallas_call(
         body,
-        out_shape=jax.ShapeDtypeStruct((sources, 8, rows, cols), bf16),
+        out_shape=jax.ShapeDtypeStruct((8, 40, cols), bf16),
+        grid_spec=pltpu.PrefetchScalarGridSpec(
+            num_scalar_prefetch=2,
+            grid=(1,),
+            in_specs=[
+                pl.BlockSpec((32, wide), lambda i, place, lens: (place[0], 0)),
+                pl.BlockSpec((32, up_wide), lambda i, place, lens: (place[0], 0)),
+                pl.BlockSpec((1, cols), lambda i, place, lens: (0, 0)),
+            ],
+            out_specs=pl.BlockSpec((8, 40, cols), lambda i, place, lens: (0, 0, 0)),
+        ),
+        compiler_params=kernel_params(),
+        cost_estimate=COST,
+        name="packed",
+    )(place, lengths, qkv_weight, up_weight, vectors)
+
+
+def unpacked(part, after):
+    owners, _, cols = part.shape
+
+    def body(part_ref, rows_ref, info_ref):
+        rows_ref[0] = part_ref[0, 0:32]
+        info_ref[0] = part_ref[0, 32:40].astype(f32)
+
+    def block(rows):
+        return pl.BlockSpec((1, rows, cols), lambda i: (i, 0, 0))
+
+    return pl.pallas_call(
+        after_inputs(body, 1, len(after)),
+        out_shape=(
+            jax.ShapeDtypeStruct((owners, 32, cols), bf16),
+            jax.ShapeDtypeStruct((owners, 8, cols), f32),
+        ),
+        grid=(owners,),
+        in_specs=[block(40)] + anywhere(len(after)),
+        out_specs=(block(32), block(8)),
+        compiler_params=kernel_params(),
+        cost_estimate=COST,
+        name="unpacked",
+    )(part, *after)
+
+
+def added(left, right, after):
+    count, rows, cols = left.shape
+
+    def body(left_ref, right_ref, out_ref):
+        out_ref[...] = (left_ref[...].astype(f32) + right_ref[...].astype(f32)).astype(bf16)
+
+    block = pl.BlockSpec((1, rows, cols), lambda i: (i, 0, 0))
+    return pl.pallas_call(
+        after_inputs(body, 2, len(after)),
+        out_shape=jax.ShapeDtypeStruct(left.shape, bf16),
+        grid=(count,),
+        in_specs=[block, block] + anywhere(len(after)),
+        out_specs=block,
+        compiler_params=kernel_params(),
+        cost_estimate=COST,
+        name="added",
+    )(left, right, *after)
+
+
+def summed(parts, after):
+    count, blocks, rows, cols = parts.shape
+
+    def body(parts_ref, out_ref):
+        out_ref[0] = jnp.sum(parts_ref[:, 0].astype(f32), 0).astype(bf16)
+
+    return pl.pallas_call(
+        after_inputs(body, 1, len(after)),
+        out_shape=jax.ShapeDtypeStruct((blocks, rows, cols), bf16),
+        grid=(blocks,),
+        in_specs=[pl.BlockSpec((count, 1, rows, cols), lambda i: (0, i, 0, 0))]
+        + anywhere(len(after)),
+        out_specs=pl.BlockSpec((1, rows, cols), lambda i: (i, 0, 0)),
+        compiler_params=kernel_params(),
+        cost_estimate=COST,
+        name="summed",
+    )(parts, *after)
+
+
+def sorted_weight(pieces, spots):
+    rows, cols = pieces[0][0].shape[1:]
+    count = len(pieces)
+
+    def body(spot_ref, *refs):
+        out_ref, sems = refs[count], refs[count + 1]
+        copies = []
+        for at, (array, first, spot) in enumerate(pieces):
+            target = out_ref.at[pl.ds(first, array.shape[0]), spot_ref[spot]]
+            copies.append(pltpu.make_async_copy(refs[at], target, sems.at[at]))
+        for copy in copies:
+            copy.start()
+        for copy in copies:
+            copy.wait()
+
+    return pl.pallas_call(
+        body,
+        out_shape=jax.ShapeDtypeStruct((8, 8, rows, cols), bf16),
         grid_spec=pltpu.PrefetchScalarGridSpec(
             num_scalar_prefetch=1,
-            grid=(8,),
-            in_specs=[
-                pl.BlockSpec(block, lambda i, spot: (jnp.minimum(i, 3), 0, 0, 0)),
-                pl.BlockSpec(block, lambda i, spot: (jnp.maximum(i - 4, 0), 0, 0, 0)),
-            ],
-            out_specs=pl.BlockSpec(
-                (sources, 1, rows, cols), lambda i, spot: (0, spot[i], 0, 0)
-            ),
+            grid=(1,),
+            in_specs=anywhere(count),
+            out_specs=pl.BlockSpec(memory_space=pl.ANY),
+            scratch_shapes=[pltpu.SemaphoreType.DMA((count,))],
         ),
         compiler_params=kernel_params(),
         cost_estimate=COST,
         name="sorted_weight",
-    )(spots, mine, yours).reshape(sources * 8 * rows, cols)
-
-
-def late_grads(active, attended, dy, core):
-    width = dy.shape[1]
-
-    def body(core_ref, act_ref, ol_ref, dy_ref, keep_ref, send_ref):
+    )(spots, *[piece[0] for piece in pieces]).reshape(64 * rows, cols)
+
+
+def late_grads(active, attended, dy, numbers):
+    piece_rows, width = dy[0].shape
+    count = len(dy)
+
+    def body(number_ref, act_ref, ol_ref, *refs):
+        keep_ref, send_ref, sum_ref, dy_ref, sems = refs[count:]
         step = pl.program_id(0)
-        first = core_ref[0] == 0
+        first = number_ref[0] == 0
+
+        @pl.when(step == 0)
+        def _():
+            fetch(refs[:count], dy_ref, sems, piece_rows)
+            own = dy_ref[:, pl.ds(pl.multiple_of(number_ref[1] * 256, 256), 256)]
+            sum_ref[...] = jnp.sum(own.astype(f32), 0, keepdims=True)
 
         @pl.when(step < 4)
         def _():
@@ -469,30 +595,34 @@
                 keep_ref[:, 64:80] = part[:, 1]
                 send_ref[:, 64:80] = part[:, 0]
 
-    rows = dy.shape[0]
+    rows = active.shape[0]
     out = jax.ShapeDtypeStruct((8, 80, width), bf16)
     whole = pl.BlockSpec((8, 80, width), lambda i, core: (0, 0, 0))
-    keep, send = pl.pallas_call(
+    keep, send, sums = pl.pallas_call(
         body,
-        out_shape=(out, out),
+        out_shape=(out, out, jax.ShapeDtypeStruct((1, 256), f32)),
         grid_spec=pltpu.PrefetchScalarGridSpec(
             num_scalar_prefetch=1,
             grid=(5,),
             in_specs=[
                 pl.BlockSpec((rows, 256), lambda i, core: (0, jnp.minimum(i, 3))),
                 pl.BlockSpec((rows, 256), lambda i, core: (0, 0)),
-                pl.BlockSpec((rows, width), lambda i, core: (0, 0)),
+            ]
+            + anywhere(count),
+            out_specs=(whole, whole, pl.BlockSpec((1, 256), lambda i, core: (0, 0))),
+            scratch_shapes=[
+                pltpu.VMEM((rows, width), bf16),
+                pltpu.SemaphoreType.DMA((count,)),
             ],
-            out_specs=(whole, whole),
         ),
         compiler_params=kernel_params(),
         cost_estimate=COST,
         name="late_grads",
-    )(core, active, attended, dy)
-    return keep.reshape(4, 2, 80, width), send.reshape(4, 2, 80, width)
-
-
-def early_grads(h1, h2, d_qkv, d_hidden, core):
+    )(numbers, active, attended, *dy)
+    return keep, send, sums
+
+
+def early_grads(h1, h2, d_qkv, d_hidden, numbers, after):
     rows, width = h1.shape
     n1, n2 = d_qkv.shape[1], d_hidden.shape[1]
 
@@ -503,22 +633,22 @@
 
         @pl.when(first)
         def _():
-            keep_ref[:, 0, :, :, 0:n1] = left[:, :, 0]
-            keep_ref[:, 0, :, :, n1:] = right[:, :, 0]
-            send_ref[:, 0, :, :, 0:n1] = left[:, :, 1]
-            send_ref[:, 0, :, :, n1:] = right[:, :, 1]
+            keep_ref[:, :, 0, :, 0:n1] = left[:, :, 0]
+            keep_ref[:, :, 0, :, n1:] = right[:, :, 0]
+            send_ref[:, :, 0, :, 0:n1] = left[:, :, 1]
+            send_ref[:, :, 0, :, n1:] = right[:, :, 1]
 
         @pl.when(jnp.logical_not(first))
         def _():
-            keep_ref[:, 0, :, :, 0:n1] = left[:, :, 1]
-            keep_ref[:, 0, :, :, n1:] = right[:, :, 1]
-            send_ref[:, 0, :, :, 0:n1] = left[:, :, 0]
-            send_ref[:, 0, :, :, n1:] = right[:, :, 0]
-
-    out = jax.ShapeDtypeStruct((4, 8, 2, 16, n1 + n2), bf16)
-    block = pl.BlockSpec((4, 1, 2, 16, n1 + n2), lambda i, core: (0, i, 0, 0, 0))
-    return pl.pallas_call(
-        body,
+            keep_ref[:, :, 0, :, 0:n1] = left[:, :, 1]
+            keep_ref[:, :, 0, :, n1:] = right[:, :, 1]
+            send_ref[:, :, 0, :, 0:n1] = left[:, :, 0]
+            send_ref[:, :, 0, :, n1:] = right[:, :, 0]
+
+    out = jax.ShapeDtypeStruct((4, 2, 8, 16, n1 + n2), bf16)
+    block = pl.BlockSpec((4, 2, 1, 16, n1 + n2), lambda i, core: (0, 0, i, 0, 0))
+    return pl.pallas_call(
+        after_inputs(body, 5, len(after)),
         out_shape=(out, out),
         grid_spec=pltpu.PrefetchScalarGridSpec(
             num_scalar_prefetch=1,
@@ -528,13 +658,14 @@
                 pl.BlockSpec((rows, width // 8), lambda i, core: (0, i)),
                 pl.BlockSpec((rows, n1), lambda i, core: (0, 0)),
                 pl.BlockSpec((rows, n2), lambda i, core: (0, 0)),
-            ],
+            ]
+            + anywhere(len(after)),
             out_specs=(block, block),
         ),
         compiler_params=kernel_params(),
         cost_estimate=COST,
         name="early_grads",
-    )(core, h1, h2, d_qkv, d_hidden)
+    )(numbers, h1, h2, d_qkv, d_hidden, *after)
 
 
 def late_outputs(groups, spots):
@@ -652,36 +783,51 @@
     l, x = shard // 4, shard % 4
     ff = up_bias.shape[0]
 
-    cols = 3 * head + ff
-    part = lax.dynamic_slice_in_dim(qkv_weight, y * 64 + c * 32, 32, 0).reshape(32, 3, 8, head)
-    part_up = lax.dynamic_slice_in_dim(up_weight, y * 64 + c * 32, 32, 0).reshape(32, 8, ff)
-    small = jnp.concatenate([ln1_gain, ln1_bias, ln2_gain, ln2_bias, qkv_bias])
-    size = jnp.pad(doc_lengths[0].astype(bf16), (0, cols - doc_lengths.shape[1]))
-    small = jnp.pad(jnp.stack([small, size]), ((0, 6), (0, 0)))
-    part = jnp.concatenate(
-        [part.transpose(2, 0, 1, 3).reshape(8, 32, 3 * head), part_up.transpose(1, 0, 2)], -1
-    )
-    part = jnp.concatenate([part, jnp.broadcast_to(small[None], (8, 8, cols))], 1)
+    x_below, x_above = move(tokens, x=1), move(tokens, x=-1)
+    x_other = move(tokens, l=1)
+    x_other_below, x_other_above = move(x_other, x=1), move(x_other, x=-1)
+    x_far, x_other_far = move(x_below, x=1), move(x_other_below, x=1)
+    dy_other = move(cotangent, l=1)
+    dy_below, dy_above = move(cotangent, x=1), move(cotangent, x=-1)
+    dy_other_below, dy_other_above = move(dy_other, x=1), move(dy_other, x=-1)
+    dy_far, dy_other_far = move(dy_above, x=-1), move(dy_other_above, x=-1)
+    x_all = (tokens, x_above, x_far, x_below, x_other, x_other_above, x_other_far, x_other_below)
+    dy_all = (
+        cotangent,
+        dy_above,
+        dy_far,
+        dy_below,
+        dy_other,
+        dy_other_above,
+        dy_other_far,
+        dy_other_below,
+    )
+
+    vectors = jnp.concatenate([ln1_gain, ln1_bias, ln2_gain, ln2_bias, qkv_bias])[None]
+    place = (y * 2 + c).astype(jnp.int32).reshape(1)
+    part = packed(qkv_weight, up_weight, vectors, doc_lengths, place, head)
     part = lax.all_to_all(part, "shard", 0, 0)
-    infos = part[:, 32:34]
-    mine = jnp.stack(ring_gather(part[:, :32], "y", 4))
-    yours = move(mine, c=1)
+    cols = part.shape[-1]
+    own, infos = unpacked(part, (x_other, x_below, x_above))
+    below, above = move(own, y=1), move(own, y=-1)
+    far_low, far_high = move(below[:4], y=1), move(above[4:], y=-1)
+    mine = ((own, 0, 0), (above, 0, 1), (far_low, 0, 2), (far_high, 4, 2), (below, 0, 3))
+    yours = tuple((move(array, c=1), first, spot + 4) for array, first, spot in mine)
     steps4 = (y + jnp.arange(4)) % 4
     spots = jnp.concatenate([steps4 * 2 + c, steps4 * 2 + 1 - c]).astype(jnp.int32)
-    w_mixed = sorted_weight(mine, yours, spots)
-
-    places = [((l ^ (k // 4)) * 4 + (x + k % 4) % 4) for k in range(8)]
-    x_all = jnp.zeros((group * rows, width), bf16)
-    for place_of, piece in zip(places, group_gather(tokens, 64)):
-        x_all = lax.dynamic_update_slice(x_all, piece, (place_of * rows, 0))
-    dy_all = lax.all_gather(cotangent, "shard", axis=0, tiled=True)
-
-    gains = infos[:, 0, :1024].reshape(8, 4, 256).transpose(1, 0, 2).reshape(4, width).astype(f32)
-    qkv_b = infos[:, 0, 1024:].astype(f32).reshape(8 * 3, 1, head)
+    w_mixed = sorted_weight(mine + yours, spots)
+
+    gains = infos[:, 0, :1024].reshape(8, 4, 256).transpose(1, 0, 2).reshape(4, width)
+    qkv_b = infos[:, 0, 1024:].reshape(8 * 3, 1, head)
     qkv_b = jnp.stack(
         [lax.dynamic_index_in_dim(qkv_b, third * 8 + shard, 0, False) for third in range(3)]
     )
-    lengths = infos[:, 1, :3].astype(jnp.int32)
+    steps8 = jnp.arange(8)
+    sources = ((steps8 // 4) ^ l) * 4 + (x + steps8 % 4) % 4
+    lengths = infos[:, 1, :3]
+    lengths = jnp.sum(
+        jnp.where(sources[:, None, None] == steps8[None, :, None], lengths[None], 0.0), 1
+    ).astype(jnp.int32)
     ends = jnp.cumsum(lengths, 1)
     starts = ends - lengths
     steps_t = jnp.arange(rows, dtype=jnp.int32)
@@ -698,26 +844,59 @@
     sine = jnp.sin(angle)
     sine = jnp.where(lane < ROT // 2, -sine, jnp.where(lane < ROT, sine, 0.0))
 
-    h1, h2, mean, inverse = norms(x_all, gains)
+    x_rows, h1, h2, mean, inverse = norms(x_all, gains)
     active, slope = hidden_part(h2, w_mixed, 3 * head // 256, up_bias.astype(f32)[None])
     qkv, probs, attended = attention(h1, w_mixed, qkv_b, cosine, sine, lengths)
     both_bias = (out_bias.astype(f32) + down_bias.astype(f32))[None, :]
     wide_bias = lax.dynamic_update_slice(jnp.zeros((1, width), f32), both_bias, (0, shard * 256))
-    mix = mixed_part(active, attended, down_weight, out_weight, wide_bias)
-    mixed = lax.psum_scatter(mix, "shard", scatter_dimension=0, tiled=True)
-    mixed = (tokens.astype(f32) + mixed.astype(f32)).astype(bf16)
-
-    core = c.astype(jnp.int32).reshape(1)
-    late_keep, late_send = late_grads(active, attended, dy_all, core)
+    numbers = jnp.stack([c, shard]).astype(jnp.int32)
+
+    late_keep, late_send, dy_sums = late_grads(active, attended, dy_all, numbers)
+    late_got = move(late_send, c=1)
     d_hidden, up_b, d_qkv, qkv_bg = back_inner(
-        dy_all, down_weight, out_weight, slope, qkv, probs, cosine, sine
-    )
-    early_keep, early_send = early_grads(h1, h2, d_qkv, d_hidden, core)
-    sums, norm_sums = back_norms(
-        d_qkv, d_hidden, w_mixed, x_all, mean, inverse, jnp.stack([gains[0], gains[2]])
-    )
-    sums = sums.reshape(group, rows, width)
-    own_sum = group_reduce([pick(sums, place_of, 0) for place_of in places], 64)
+        dy_all, down_weight, out_weight, slope, qkv, probs, cosine, sine, (late_send,)
+    )
+    late = (late_keep.astype(f32) + late_got.astype(f32)).astype(bf16)
+    early_keep, early_send = early_grads(h1, h2, d_qkv, d_hidden, numbers, (late,))
+    early_got = move(early_send, c=1)
+    late = lax.all_to_all(late, "rep", 0, 0, axis_index_groups=SAME_CORE)
+    norm_sums, *sums = back_norms(
+        d_qkv,
+        d_hidden,
+        w_mixed,
+        x_rows,
+        mean,
+        inverse,
+        jnp.stack([gains[0], gains[2]]),
+        (early_send,),
+    )
+    late = summed(late[:, None], (sums[0],))[0]
+    early = added(early_keep.reshape(8, 128, cols), early_got.reshape(8, 128, cols), (late,))
+    early = early.reshape(64, 16, cols)
+    mix = mixed_part(active, attended, down_weight, out_weight, wide_bias, (early, sums[0]))
+    early = lax.all_to_all(early, BOTH, 0, 0, axis_index_groups=SAME_CORE_ALL)
+
+    def ring(at):
+        mix_low = move(mix[at + 2], x=1)
+        sum_high = move(sums[at + 2], x=-1)
+        mix_above = (mix[at + 1].astype(f32) + mix_low.astype(f32)).astype(bf16)
+        sum_below = (sums[at + 3].astype(f32) + sum_high.astype(f32)).astype(bf16)
+        mix_total = (
+            mix[at].astype(f32)
+            + move(mix_above, x=1).astype(f32)
+            + move(mix[at + 3], x=-1).astype(f32)
+        )
+        sum_total = (
+            sums[at].astype(f32)
+            + move(sums[at + 1], x=1).astype(f32)
+            + move(sum_below, x=-1).astype(f32)
+        )
+        return mix_total, sum_total
+
+    mix_other, sum_other = (move(v.astype(bf16), l=1).astype(f32) for v in ring(4))
+    mix_own, sum_own = ring(0)
+    mixed = (tokens.astype(f32) + mix_own + mix_other).astype(bf16)
+    own_sum = sum_own + sum_other
     own_normed, own_inverse = normalize(tokens)
     tokens_grad = cotangent.astype(f32) + own_inverse * (
         own_sum
@@ -725,8 +904,7 @@
         - own_normed * jnp.mean(own_sum * own_normed, -1, keepdims=True)
     )
 
-    dy_sum = jnp.sum(dy_all.astype(f32), 0)
-    dy_own = lax.dynamic_slice_in_dim(dy_sum, shard * 256, 256)
+    dy_own = dy_sums.reshape(256)
     wide_qkv = lax.dynamic_update_slice(
         jnp.zeros((3, 8, head), f32), qkv_bg.reshape(3, 1, head), (0, shard, 0)
     )
@@ -741,16 +919,6 @@
     def small_at(start, size):
         return lax.dynamic_slice_in_dim(smalls, start + shard * size, size)
 
-    got = move(late_send, c=1)
-
-    def late_part(high, index):
-        both = [pick(pick(v, high, 1), index, 0).astype(f32) for v in (late_keep, got)]
-        return both[0] + both[1]
-
-    away = (pick(late_keep, 1 - h, 1).astype(f32) + pick(got, 1 - h, 1).astype(f32)).astype(bf16)
-    crossed = move(away, h=1)
-    parts = [late_part(h, (y + k) % 4) + pick(crossed, (y + k) % 4, 0).astype(f32) for k in range(4)]
-    late = ring_reduce(parts, "y", 40).astype(bf16)
     late = jnp.stack(ring_gather(late, "y", 40))
     late_h = move(late, h=1)
     late_c = move(late, c=1)
@@ -762,15 +930,7 @@
         (late, late_h, late_c, late_hc), jnp.concatenate(spots).astype(jnp.int32)
     )
 
-    got_early = move(early_send, c=1)
-    parts = [
-        pick(early_keep, (y + k) % 4, 0).astype(f32) + pick(got_early, (y + k) % 4, 0).astype(f32)
-        for k in range(4)
-    ]
-    early = ring_reduce(parts, "y", 4)
-    crossed = move(pick(early, 1 - h, 1).astype(bf16), h=1)
-    early = (pick(early, h, 1) + crossed.astype(f32)).astype(bf16)
-    early = lax.all_to_all(early, "shard", 0, 0)
+    early = summed(early.reshape(8, 8, 16, cols), (mix[0],))
     early = jnp.stack([early, move(early, h=1)])
     early = jnp.concatenate(ring_gather(early, "y", 1), 0)
     early_c = move(early, c=1)

time: 556 us -> 751 us (1.35)
  the two profiles are of different devices: /device:TPU:1 before, /device:TPU:32 now
where the time goes in v1:
time: 751 us; the launch traced here: 741 us
  Pallas kernels  382 us (51%)
  waiting for transfers between devices  224 us (30%)
  starting transfers between devices  84.6 us (11%)
  local copies, waits for them, and re-layouts  30.2 us (4%)
  other arithmetic  18.9 us (3%)
    pallas_call x1, Pallas kernels, sorted_weight(): pl.pallas_call(body, out_shape=jax.ShapeDtypeStruct((8, 8, rows, cols), b...  224 us
    ppermute x52, waiting for transfers between devices, move(): return lax.ppermute(value, BOTH, pairs)  158 us
    ppermute x52, starting transfers between devices, move(): return lax.ppermute(value, BOTH, pairs)  51.7 us
    ppermute x7, waiting for transfers between devices, swap(): return lax.ppermute(value, BOTH, pairs)  42.4 us
    all_to_all x1, waiting for transfers between devices, local(): late = lax.all_to_all(late, 'rep', 0, 0, axis_index_groups=SAME_CORE)  23.5 us
    pallas_call x1, Pallas kernels, back_inner(): pl.pallas_call(after_inputs(body, count + 7, len(after)), out_shape=(jax....  19.7 us
    unnamed x119, local copies, waits for them, and re-layouts  17.6 us
    ppermute x7, starting transfers between devices, swap(): return lax.ppermute(value, BOTH, pairs)  15.3 us
  transfers between devices with their start and end apart: 62, of which 27 were waited for; matrix products, arithmetic and copies ran while one was open for 4% of the time, Pallas kernels for 44%

profile of v1, /device:TPU:32, one launch (start us, length us, event | category | flops | bytes accessed | tf_op | source)
XLA Modules:
  0.0 741.4 jit_solution(14071847889678237059)
XLA Ops:
  8.4 5.9 all-to-all-start
  17.5 22.1 %collective-permute-done.refs_3_.refs_1_ = bf16[128,2048]{1,0:T(8,128)(2,1)S(1)} collective-permute-done((bf16[128,2048]{1,0:T(8,128)(2,1)S(1)}, bf16[128,2048]{1,0:T(8,128)(2,1)S(1)}, u32[]{:S(2)}, u32[]{:S(2)}) %collective-permute-start) | collective-permute-done | bytes 524320 | tf_op jit(solution)/shard_map/ppermute | solution.py:39
  42.7 5.2 unpacked.1
  53.6 10.5 %collective-permute-done.19.refs_4_ = bf16[128,2048]{1,0:T(8,128)(2,1)S(1)} collective-permute-done((bf16[128,2048]{1,0:T(8,128)(2,1)S(1)}, bf16[128,2048]{1,0:T(8,128)(2,1)S(1)}, u32[]{:S(2)}, u32[]{:S(2)}) %collective-permute-start.19) | collective-permute-done | bytes 524320 | tf_op jit(solution)/shard_map/ppermute | solution.py:39
  64.2 6.5 collective-permute-done.7.refs_1_
  77.3 10.6 %collective-permute-done.20.refs_5_ = bf16[128,2048]{1,0:T(8,128)(2,1)S(1)} collective-permute-done((bf16[128,2048]{1,0:T(8,128)(2,1)S(1)}, bf16[128,2048]{1,0:T(8,128)(2,1)S(1)}, u32[]{:S(2)}, u32[]{:S(2)}) %collective-permute-start.20) | collective-permute-done | bytes 524320 | tf_op jit(solution)/shard_map/ppermute | solution.py:39
  101.0 7.3 collective-permute-done.6.refs_6_
  120.6 9.1 %norms.1 = (bf16[1024,2048]{1,0:T(8,128)(2,1)}, bf16[1024,2048]{1,0:T(8,128)(2,1)}, bf16[1024,2048]{1,0:T(8,128)(2,1)}, f32[1024,1]{1,0:T(8,128)}, f32[1024,1]{1,0:T(8,128)}) custom-call(bf16[128,2048]{1,0:T(8,128)(2,1)} %refs_0_.3, bf16[128,2048]{1,0:T(8,128)(2,1)} %copy-done.20, bf16[128,2048]{1,0:T(8,128)(2,1)} %copy-done.32, ...), custom_call_target="tpu_custom_call" | custom-call | flops 1000 | bytes 1000 | tf_op jit(solution)/shard_map/norms/pallas_call | solution.py:392
  130.8 224.2 %sorted_weight.1 = bf16[8,8,32,1792]{3,2,1,0:T(8,128)(2,1)} custom-call(s32[8]{0:T(128)} %pad_add_fusion.spot_ref, bf16[8,32,1792]{2,1,0:T(8,128)(2,1)} %get-tuple-element.58.refs_0_, bf16[8,32,1792]{2,1,0:T(8,128)(2,1)} %copy-done.22, bf16[4,32,1792]{2,1,0:T(8,128)(2,1)} %collective-permute-done.9.refs_2_, ...), custom_call_target="tpu_custom_call" | custom-call | flops 1000 | bytes 1000 | tf_op jit(solution)/shard_map/sorted_weight/pallas_call | solution.py:538
  355.0 10.2 %hidden_part.1 = (bf16[1024,1024]{1,0:T(8,128)(2,1)}, f32[1024,1024]{1,0:T(8,128)}) custom-call(bf16[1024,2048]{1,0:T(8,128)(2,1)} %get-tuple-element.57.h_ref.refs_2_, bf16[2048,1792]{1,0:T(8,128)(2,1)} %bitcast.47, f32[1,1024]{1,0:T(1,128)} %bitcast.74), custom_call_target="tpu_custom_call" | custom-call | flops 1000 | bytes 1000 | tf_op jit(solution)/shard_map/hidden_part/pallas_call | solution.py:94
  365.2 14.4 %attention.1 = (bf16[1024,768]{1,0:T(8,128)(2,1)}, f32[1024,128]{1,0:T(8,128)}, bf16[1024,256]{1,0:T(8,128)(2,1)}) custom-call(s32[8,3]{1,0:T(8,128)} %copy-done.37, bf16[1024,2048]{1,0:T(8,128)(2,1)} %get-tuple-element.60.h_ref.refs_1_, bf16[2048,1792]{1,0:T(8,128)(2,1)} %bitcast.48, f32[3,1,256]{2,1,0:T(1,128)} %pad_maximum_fusion.4.b_ref, ...), custom_call_target="tpu_custom_call" | custom-call | flops 1000 | bytes 1000 | tf_op jit(solution)/shard_map/attention/pallas_call | solution.py:169
  381.0 13.6 %late_grads.1 = (bf16[8,80,2048]{2,1,0:T(8,128)(2,1)}, bf16[8,80,2048]{2,1,0:T(8,128)(2,1)}, f32[1,256]{1,0:T(1,128)}) custom-call(s32[2]{0:T(128)} %pad_add_fusion.1.number_ref.refs_0_, bf16[1024,1024]{1,0:T(8,128)(2,1)} %get-tuple-element.59.act_ref.refs_0_, bf16[1024,256]{1,0:T(8,128)(2,1)} %get-tuple-element.61.ol_ref.refs_1_, ...), custom_call_target="tpu_custom_call" | custom-call | flops 1000 | bytes 1000 | tf_op jit(solution)/shard_map/late_grads/pallas_call | solution.py:601
  394.7 19.7 %back_inner.1 = (bf16[1024,1024]{1,0:T(8,128)(2,1)}, f32[1,1024]{1,0:T(1,128)}, bf16[1024,768]{1,0:T(8,128)(2,1)}, f32[1,768]{1,0:T(1,128)}) custom-call(bf16[128,2048]{1,0:T(8,128)(2,1)} %refs_0_.5, bf16[128,2048]{1,0:T(8,128)(2,1)} %copy-done.14, bf16[128,2048]{1,0:T(8,128)(2,1)} %copy-done.18, bf16[128,2048]{1,0:T(8,128)(2,1)} %copy-done.16, ...), custom_call_target="tpu_custom_call" | custom-call | flops 1000 | bytes 1000 | tf_op jit(solution)/shard_map/back_inner/pallas_call | solution.py:287
  417.2 15.1 %early_grads.1 = (bf16[4,2,8,16,1792]{4,3,2,1,0:T(8,128)(2,1)}, bf16[4,2,8,16,1792]{4,3,2,1,0:T(8,128)(2,1)}) custom-call(s32[2]{0:T(128)} %pad_add_fusion.1.number_ref.refs_0_, bf16[1024,2048]{1,0:T(8,128)(2,1)} %get-tuple-element.60.h_ref.refs_1_, bf16[1024,2048]{1,0:T(8,128)(2,1)} %get-tuple-element.57.h_ref.refs_2_, ...), custom_call_target="tpu_custom_call" | custom-call | flops 1000 | bytes 1000 | tf_op jit(solution)/shard_map/early_grads/pallas_call | solution.py:650
  432.7 5.4 all-to-all-start.1
  438.8 14.4 %back_norms.1 = (f32[4,2048]{1,0:T(4,128)}, bf16[128,2048]{1,0:T(8,128)(2,1)}, bf16[128,2048]{1,0:T(8,128)(2,1)}, bf16[128,2048]{1,0:T(8,128)(2,1)}, bf16[128,20...) custom-call(bf16[1024,768]{1,0:T(8,128)(2,1)} %get-tuple-element.66., ...), custom_call_target="tpu_custom_call" | custom-call | flops 1000 | bytes 1000 | tf_op jit(solution)/shard_map/back_norms/pallas_call | solution.py:342
  453.2 23.5 %all-to-all-done.1 = bf16[8,80,2048]{2,1,0:T(8,128)(2,1)S(1)} async-done(((bf16[8,80,2048]{2,1,0:T(8,128)(2,1)}), bf16[8,80,2048]{2,1,0:T(8,128)(2,1)S(1)}, u32[]{:S(2)}, u32[]{:S(2)}) %all-to-all-start.1) | async-done | bytes 2621472 | tf_op jit(solution)/shard_map/all_to_all | solution.py:862
  481.0 7.3 added.1
  488.4 6.4 all-to-all-start.2
  501.2 30.2 %collective-permute-done.40 = f32[24,1024]{1,0:T(8,128)S(1)} collective-permute-done((f32[24,1024]{1,0:T(8,128)S(1)}, f32[24,1024]{1,0:T(8,128)S(1)}, u32[]{:S(2)}, u32[]{:S(2)}) %collective-permute-start.40) | collective-permute-done | bytes 98336 | tf_op jit(solution)/shard_map/ppermute | solution.py:45
  556.2 10.6 %mixed_part.1 = (bf16[128,2048]{1,0:T(8,128)(2,1)}, bf16[128,2048]{1,0:T(8,128)(2,1)}, bf16[128,2048]{1,0:T(8,128)(2,1)}, bf16[128,2048]{1,0:T(8,128)(2,1)}, bf1...) custom-call(bf16[1024,1024]{1,0:T(8,128)(2,1)} %get-tuple-element.59., ...), custom_call_target="tpu_custom_call" | custom-call | flops 1000 | bytes 1000 | tf_op jit(solution)/shard_map/mixed_part/pallas_call | solution.py:209
  566.8 5.8 summed.3
  592.1 6.5 collective-permute-done.52
  600.3 12.1 %collective-permute-done.53 = bf16[80,2048]{1,0:T(8,128)(2,1)S(1)} collective-permute-done((bf16[80,2048]{1,0:T(8,128)(2,1)S(1)}, bf16[80,2048]{1,0:T(8,128)(2,1)S(1)}, u32[]{:S(2)}, u32[]{:S(2)}) %collective-permute-start.53) | collective-permute-done | bytes 327712 | tf_op jit(solution)/shard_map/ppermute | solution.py:39
  616.2 16.4 %collective-permute-done.47 = bf16[2,8,16,1792]{3,2,1,0:T(8,128)(2,1)S(1)} collective-permute-done((bf16[2,8,16,1792]{3,2,1,0:T(8,128)(2,1)S(1)}, bf16[2,8,16,1792]{3,2,1,0:T(8,128)(2,1)S(1)}, u32[]{:S(2)}, u32[]{:S(2)}) %collective-permute-start.47) | collective-permute-done | bytes 917536 | tf_op jit(solution)/shard_map/ppermute | solution.py:39
  646.5 5.6 collective-permute-done.28
  661.6 6.2 collective-permute-done.30
  675.3 7.3 collective-permute-done.34
  687.5 10.7 %collective-permute-done.38 = bf16[128,2048]{1,0:T(8,128)(2,1)S(1)} collective-permute-done((bf16[128,2048]{1,0:T(8,128)(2,1)S(1)}, bf16[128,2048]{1,0:T(8,128)(2,1)S(1)}, u32[]{:S(2)}, u32[]{:S(2)}) %collective-permute-start.38) | collective-permute-done | bytes 524320 | tf_op jit(solution)/shard_map/ppermute | solution.py:39
  698.8 9.8 %collective-permute-done.26 = bf16[128,2048]{1,0:T(8,128)(2,1)S(1)} collective-permute-done((bf16[128,2048]{1,0:T(8,128)(2,1)S(1)}, bf16[128,2048]{1,0:T(8,128)(2,1)S(1)}, u32[]{:S(2)}, u32[]{:S(2)}) %collective-permute-start.26) | collective-permute-done | bytes 524320 | tf_op jit(solution)/shard_map/ppermute | solution.py:39
  712.0 12.7 %late_outputs.1 = (f32[1024,2048]{1,0:T(8,128)}, f32[256,2048]{1,0:T(8,128)}) custom-call(s32[16]{0:T(128)} %pad_add_fusion.4.spot_ref, bf16[4,80,2048]{2,1,0:T(8,128)(2,1)} %copy-done.4, bf16[4,80,2048]{2,1,0:T(8,128)(2,1)} %copy-done.23, bf16[4,80,2048]{2,1,0:T(8,128)(2,1)} %copy-done.24, bf16[4,80,2048]{2,1,0:T(8,128)(2,1)} %collective-permute-done.58.refs_3_), custom_call_target="tpu_custom_call" | custom-call | flops 1000 | bytes 1000 | tf_op jit(solution)/shard_map/late_outputs/pallas_call | solution.py:689
  726.6 13.8 %early_outputs.1 = (f32[256,6144]{1,0:T(8,128)}, f32[256,8192]{1,0:T(8,128)}) custom-call(s32[16]{0:T(128)} %pad_add_fusion.3.spot_ref, bf16[8,8,16,1792]{3,2,1,0:T(8,128)(2,1)} %constant_dynamic-update-slice_fusion.mine_ref, bf16[8,8,16,1792]{3,2,1,0:T(8,128)(2,1)} %copy-done.9), custom_call_target="tpu_custom_call" | custom-call | flops 1000 | bytes 1000 | tf_op jit(solution)/shard_map/early_outputs/pallas_call | solution.py:736
  (311 shorter events, 160.2 us)
Async XLA Ops:
  8.4 32.5 %all-to-all-start = ((bf16[8,40,1792]{2,1,0:T(8,128)(2,1)}), bf16[8,40,1792]{2,1,0:T(8,128)(2,1)S(1)}, u32[]{:S(2)}, u32[]{:S(2)}) async-start(bf16[8,40,1792]{2,1,0:T(8,128)(2,1)} %packed.1), calls=%async_computation | async-start | bytes 2293760 | tf_op jit(solution)/shard_map/all_to_all | solution.py:809
  14.3 25.4 %collective-permute-start = (bf16[128,2048]{1,0:T(8,128)(2,1)S(1)}, bf16[128,2048]{1,0:T(8,128)(2,1)S(1)}, u32[]{:S(2)}, u32[]{:S(2)}) collective-permute-start(bf16[128,2048]{1,0:T(8,128)(2,1)S(1)} %copy-done), channel_id=1, source_target_pairs={{0,3},{1,0},{2,1},{3,2},{4,7},{5,4},{6,5},{7,6},{8,11},{9,8},{10,9... | collective-permute-start | bytes 1572872 | tf_op jit(solution)/shard_map/ppermute | solution.py:39
  16.9 23.9 %collective-permute-start.1 = (bf16[128,2048]{1,0:T(8,128)(2,1)S(1)}, bf16[128,2048]{1,0:T(8,128)(2,1)S(1)}, u32[]{:S(2)}, u32[]{:S(2)}) collective-permute-start(bf16[128,2048]{1,0:T(8,128)(2,1)S(1)} %copy-done), channel_id=1, source_target_pairs={{0,1},{1,2},{2,3},{3,0},{4,5},{5,6},{6,7},{7,4},{8,9},{9,10},{10,1... | collective-permute-start | bytes 1572872 | tf_op jit(solution)/shard_map/ppermute | solution.py:39
  16.9 23.9 %collective-permute-start.3 = (bf16[128,2048]{1,0:T(8,128)(2,1)S(1)}, bf16[128,2048]{1,0:T(8,128)(2,1)}, u32[]{:S(2)}, u32[]{:S(2)}) collective-permute-start(bf16[128,2048]{1,0:T(8,128)(2,1)S(1)} %copy-done), channel_id=1, source_target_pairs={{0,4},{1,5},{2,6},{3,7},{4,0},{5,1},{6,2},{7,3},{8,12},{9,13},{10,... | collective-permute-start | bytes 1572872 | tf_op jit(solution)/shard_map/ppermute | solution.py:39
  47.9 22.8 %collective-permute-start.7 = (bf16[8,32,1792]{2,1,0:T(8,128)(2,1)}, bf16[8,32,1792]{2,1,0:T(8,128)(2,1)S(1)}, u32[]{:S(2)}, u32[]{:S(2)}) collective-permute-start(bf16[8,32,1792]{2,1,0:T(8,128)(2,1)} %get-tuple-element.58.refs_0_), channel_id=1, source_target_pairs={{0,96},{1,97},{2,98},{3,99},{4,100},{5,101},{6,102},{7,103},{8,104... | collective-permute-start | bytes 2752520 | tf_op jit(solution)/shard_map/ppermute | solution.py:39
  50.9 23.2 %collective-permute-start.8 = (bf16[8,32,1792]{2,1,0:T(8,128)(2,1)}, bf16[8,32,1792]{2,1,0:T(8,128)(2,1)}, u32[]{:S(2)}, u32[]{:S(2)}) collective-permute-start(bf16[8,32,1792]{2,1,0:T(8,128)(2,1)} %get-tuple-element.58.refs_0_), channel_id=1, source_target_pairs={{0,32},{1,33},{2,34},{3,35},{4,36},{5,37},{6,38},{7,39},{8,40},{9,... | collective-permute-start | bytes 2752520 | tf_op jit(solution)/shard_map/ppermute | solution.py:39
  51.5 25.8 %collective-permute-start.16 = (bf16[128,2048]{1,0:T(8,128)(2,1)S(1)}, bf16[128,2048]{1,0:T(8,128)(2,1)S(1)}, u32[]{:S(2)}, u32[]{:S(2)}) collective-permute-start(bf16[128,2048]{1,0:T(8,128)(2,1)S(1)} %copy-done.5), channel_id=1, source_target_pairs={{0,3},{1,0},{2,1},{3,2},{4,7},{5,4},{6,5},{7,6},{8,11},{9,8},{10,9... | collective-permute-start | bytes 1572872 | tf_op jit(solution)/shard_map/ppermute | solution.py:39
  52.4 35.7 %collective-permute-start.2 = (bf16[128,2048]{1,0:T(8,128)(2,1)}, bf16[128,2048]{1,0:T(8,128)(2,1)S(1)}, u32[]{:S(2)}, u32[]{:S(2)}) collective-permute-start(bf16[128,2048]{1,0:T(8,128)(2,1)} %copy-done.21), channel_id=1, source_target_pairs={{0,1},{1,2},{2,3},{3,0},{4,5},{5,6},{6,7},{7,4},{8,9},{9,10},{10,1... | collective-permute-start | bytes 1572872 | tf_op jit(solution)/shard_map/ppermute | solution.py:39
  64.1 27.1 %collective-permute-start.4 = (bf16[128,2048]{1,0:T(8,128)(2,1)}, bf16[128,2048]{1,0:T(8,128)(2,1)}, u32[]{:S(2)}, u32[]{:S(2)}) collective-permute-start(bf16[128,2048]{1,0:T(8,128)(2,1)} %collective-permute-done.3.refs_1_.refs_4_), channel_id=1, source_target_pairs={{0,3},{1,0},{2,1},{3,2},{4,7},{5,4},{6,5},{7,6},{8,11},{9,8},{10,9... | collective-permute-start | bytes 1572872 | tf_op jit(solution)/shard_map/ppermute | solution.py:39
  77.3 32.8 %collective-permute-start.11 = (bf16[8,32,1792]{2,1,0:T(8,128)(2,1)}, bf16[8,32,1792]{2,1,0:T(8,128)(2,1)}, u32[]{:S(2)}, u32[]{:S(2)}) collective-permute-start(bf16[8,32,1792]{2,1,0:T(8,128)(2,1)} %get-tuple-element.58.refs_0_), channel_id=1, source_target_pairs={{0,8},{1,9},{2,10},{3,11},{4,12},{5,13},{6,14},{7,15},{8,0},{9,1},... | collective-permute-start | bytes 2752520 | tf_op jit(solution)/shard_map/ppermute | solution.py:39
  110.1 269.6 %collective-permute-start.18 = (bf16[128,2048]{1,0:T(8,128)(2,1)S(1)}, bf16[128,2048]{1,0:T(8,128)(2,1)S(1)}, u32[]{:S(2)}, u32[]{:S(2)}) collective-permute-start(bf16[128,2048]{1,0:T(8,128)(2,1)S(1)} %copy-done.5), channel_id=1, source_target_pairs={{0,1},{1,2},{2,3},{3,0},{4,5},{5,6},{6,7},{7,4},{8,9},{9,10},{10,1... | collective-permute-start | bytes 1572872 | tf_op jit(solution)/shard_map/ppermute | solution.py:39
  110.2 269.5 %collective-permute-start.22 = (bf16[128,2048]{1,0:T(8,128)(2,1)S(1)}, bf16[128,2048]{1,0:T(8,128)(2,1)S(1)}, u32[]{:S(2)}, u32[]{:S(2)}) collective-permute-start(bf16[128,2048]{1,0:T(8,128)(2,1)S(1)} %collective-permute-done.19.refs_4_), channel_id=1, source_target_pairs={{0,1},{1,2},{2,3},{3,0},{4,5},{5,6},{6,7},{7,4},{8,9},{9,10},{10,1... | collective-permute-start | bytes 1572872 | tf_op jit(solution)/shard_map/ppermute | solution.py:39
  110.3 269.4 %collective-permute-start.17 = (bf16[128,2048]{1,0:T(8,128)(2,1)S(1)}, bf16[128,2048]{1,0:T(8,128)(2,1)S(1)}, u32[]{:S(2)}, u32[]{:S(2)}) collective-permute-start(bf16[128,2048]{1,0:T(8,128)(2,1)S(1)} %collective-permute-done.16.refs_1_), channel_id=1, source_target_pairs={{0,3},{1,0},{2,1},{3,2},{4,7},{5,4},{6,5},{7,6},{8,11},{9,8},{10,9... | collective-permute-start | bytes 1572872 | tf_op jit(solution)/shard_map/ppermute | solution.py:39
  113.5 266.2 %collective-permute-start.21 = (bf16[128,2048]{1,0:T(8,128)(2,1)S(1)}, bf16[128,2048]{1,0:T(8,128)(2,1)S(1)}, u32[]{:S(2)}, u32[]{:S(2)}) collective-permute-start(bf16[128,2048]{1,0:T(8,128)(2,1)S(1)} %collective-permute-done.20.refs_5_), channel_id=1, source_target_pairs={{0,3},{1,0},{2,1},{3,2},{4,7},{5,4},{6,5},{7,6},{8,11},{9,8},{10,9... | collective-permute-start | bytes 1572872 | tf_op jit(solution)/shard_map/ppermute | solution.py:39
  432.3 48.8 %collective-permute-start.24 = (bf16[4,2,8,16,1792]{4,3,2,1,0:T(8,128)(2,1)}, bf16[4,2,8,16,1792]{4,3,2,1,0:T(8,128)(2,1)}, u32[]{:S(2)}, u32[]{:S(2)}) collective-permute-start(bf16[4,2,8,16,1792]{4,3,2,1,0:T(8,128)(2,1)} %get-tuple-element.70.refs_7_), channel_id=1, source_target_pairs={{0,8},{1,9},{2,10},{3,11},{4,12},{5,13},{6,14},{7,15},{8,0},{9,1},... | collective-permute-start | bytes 11010056 | tf_op jit(solution)/shard_map/ppermute | solution.py:39
  432.7 44.0 %all-to-all-start.1 = ((bf16[8,80,2048]{2,1,0:T(8,128)(2,1)}), bf16[8,80,2048]{2,1,0:T(8,128)(2,1)S(1)}, u32[]{:S(2)}, u32[]{:S(2)}) async-start(bf16[8,80,2048]{2,1,0:T(8,128)(2,1)} %add_convert_fusion.refs_5_), calls=%async_computation.1 | async-start | bytes 5242880 | tf_op jit(solution)/shard_map/all_to_all | solution.py:862
  488.4 78.4 %all-to-all-start.2 = ((bf16[64,16,1792]{2,1,0:T(8,128)(2,1)}), bf16[64,16,1792]{2,1,0:T(8,128)(2,1)}, u32[]{:S(2)}, u32[]{:S(2)}) async-start(bf16[64,16,1792]{2,1,0:T(8,128)(2,1)} %bitcast.50), calls=%async_computation.2 | async-start | bytes 7340032 | tf_op jit(solution)/shard_map/all_to_all | solution.py:877
  496.3 76.3 %collective-permute-start.36 = (bf16[128,2048]{1,0:T(8,128)(2,1)}, bf16[128,2048]{1,0:T(8,128)(2,1)S(1)}, u32[]{:S(2)}, u32[]{:S(2)}) collective-permute-start(bf16[128,2048]{1,0:T(8,128)(2,1)} %get-tuple-element.89), channel_id=1, source_target_pairs={{0,3},{1,0},{2,1},{3,2},{4,7},{5,4},{6,5},{7,6},{8,11},{9,8},{10,9... | collective-permute-start | bytes 1572872 | tf_op jit(solution)/shard_map/ppermute | solution.py:39
  500.4 30.9 %collective-permute-start.40 = (f32[24,1024]{1,0:T(8,128)S(1)}, f32[24,1024]{1,0:T(8,128)S(1)}, u32[]{:S(2)}, u32[]{:S(2)}) collective-permute-start(f32[24,1024]{1,0:T(8,128)S(1)} %add.361), channel_id=1, source_target_pairs={{0,4},{1,5},{2,6},{3,7},{4,0},{5,1},{6,2},{7,3},{8,12},{9,13},{10,... | collective-permute-start | bytes 294920 | tf_op jit(solution)/shard_map/ppermute | solution.py:45
  551.4 102.2 %collective-permute-start.35 = (bf16[128,2048]{1,0:T(8,128)(2,1)}, bf16[128,2048]{1,0:T(8,128)(2,1)S(1)}, u32[]{:S(2)}, u32[]{:S(2)}) collective-permute-start(bf16[128,2048]{1,0:T(8,128)(2,1)} %get-tuple-element.87), channel_id=1, source_target_pairs={{0,1},{1,2},{2,3},{3,0},{4,5},{5,6},{6,7},{7,4},{8,9},{9,10},{10,1... | collective-permute-start | bytes 1572872 | tf_op jit(solution)/shard_map/ppermute | solution.py:39
  551.4 35.3 %collective-permute-start.33 = (bf16[128,2048]{1,0:T(8,128)(2,1)}, bf16[128,2048]{1,0:T(8,128)(2,1)S(1)}, u32[]{:S(2)}, u32[]{:S(2)}) collective-permute-start(bf16[128,2048]{1,0:T(8,128)(2,1)} %get-tuple-element.85), channel_id=1, source_target_pairs={{0,3},{1,0},{2,1},{3,2},{4,7},{5,4},{6,5},{7,6},{8,11},{9,8},{10,9... | collective-permute-start | bytes 1572872 | tf_op jit(solution)/shard_map/ppermute | solution.py:39
  554.6 99.8 %collective-permute-start.32 = (bf16[128,2048]{1,0:T(8,128)(2,1)}, bf16[128,2048]{1,0:T(8,128)(2,1)S(1)}, u32[]{:S(2)}, u32[]{:S(2)}) collective-permute-start(bf16[128,2048]{1,0:T(8,128)(2,1)} %get-tuple-element.83), channel_id=1, source_target_pairs={{0,1},{1,2},{2,3},{3,0},{4,5},{5,6},{6,7},{7,4},{8,9},{9,10},{10,1... | collective-permute-start | bytes 1572872 | tf_op jit(solution)/shard_map/ppermute | solution.py:39
  554.6 23.0 %collective-permute-start.44 = (f32[24,1024]{1,0:T(8,128)S(1)}, f32[24,1024]{1,0:T(8,128)S(1)}, u32[]{:S(2)}, u32[]{:S(2)}) collective-permute-start(f32[24,1024]{1,0:T(8,128)S(1)} %add.365), channel_id=1, source_target_pairs={{0,2},{1,3},{2,0},{3,1},{4,6},{5,7},{6,4},{7,5},{8,10},{9,11},{10,... | collective-permute-start | bytes 294920 | tf_op jit(solution)/shard_map/ppermute | solution.py:45
  585.0 30.0 %collective-permute-start.48 = (bf16[2,8,16,1792]{3,2,1,0:T(8,128)(2,1)S(1)}, bf16[2,8,16,1792]{3,2,1,0:T(8,128)(2,1)S(1)}, u32[]{:S(2)}, u32[]{:S(2)}) collective-permute-start(bf16[2,8,16,1792]{3,2,1,0:T(8,128)(2,1)S(1)} %pad_maximum_fusion.1), channel_id=1, source_target_pairs={{0,32},{1,33},{2,34},{3,35},{4,36},{5,37},{6,38},{7,39},{8,40},{9,... | collective-permute-start | bytes 2752520 | tf_op jit(solution)/shard_map/ppermute | solution.py:39
  586.9 25.5 %collective-permute-start.53 = (bf16[80,2048]{1,0:T(8,128)(2,1)S(1)}, bf16[80,2048]{1,0:T(8,128)(2,1)S(1)}, u32[]{:S(2)}, u32[]{:S(2)}) collective-permute-start(bf16[80,2048]{1,0:T(8,128)(2,1)S(1)} %bitcast.56), channel_id=1, source_target_pairs={{0,32},{1,33},{2,34},{3,35},{4,36},{5,37},{6,38},{7,39},{8,40},{9,... | collective-permute-start | bytes 983048 | tf_op jit(solution)/shard_map/ppermute | solution.py:39
  598.6 46.7 %collective-permute-start.55 = (bf16[40,2048]{1,0:T(8,128)(2,1)S(1)}, bf16[40,2048]{1,0:T(8,128)(2,1)S(1)}, u32[]{:S(2)}, u32[]{:S(2)}) collective-permute-start(bf16[40,2048]{1,0:T(8,128)(2,1)S(1)} %slice.59), channel_id=1, source_target_pairs={{0,96},{1,97},{2,98},{3,99},{4,100},{5,101},{6,102},{7,103},{8,104... | collective-permute-start | bytes 491528 | tf_op jit(solution)/shard_map/ppermute | solution.py:39
  646.5 78.2 %collective-permute-start.51 = (bf16[8,8,16,1792]{3,2,1,0:T(8,128)(2,1)}, bf16[8,8,16,1792]{3,2,1,0:T(8,128)(2,1)S(1)}, u32[]{:S(2)}, u32[]{:S(2)}) collective-permute-start(bf16[8,8,16,1792]{3,2,1,0:T(8,128)(2,1)} %constant_dynamic-update-slice_fusion.mine_ref), channel_id=1, source_target_pairs={{0,8},{1,9},{2,10},{3,11},{4,12},{5,13},{6,14},{7,15},{8,0},{9,1},... | collective-permute-start | bytes 11010056 | tf_op jit(solution)/shard_map/ppermute | solution.py:39
  659.3 28.2 %collective-permute-start.56 = (bf16[4,80,2048]{2,1,0:T(8,128)(2,1)S(1)}, bf16[4,80,2048]{2,1,0:T(8,128)(2,1)S(1)}, u32[]{:S(2)}, u32[]{:S(2)}) collective-permute-start(bf16[4,80,2048]{2,1,0:T(8,128)(2,1)S(1)} %pad_maximum_fusion.refs_0_), channel_id=1, source_target_pairs={{0,16},{1,17},{2,18},{3,19},{4,20},{5,21},{6,22},{7,23},{8,24},{9,... | collective-permute-start | bytes 3932168 | tf_op jit(solution)/shard_map/ppermute | solution.py:39
  669.5 28.7 %collective-permute-start.38 = (bf16[128,2048]{1,0:T(8,128)(2,1)S(1)}, bf16[128,2048]{1,0:T(8,128)(2,1)S(1)}, u32[]{:S(2)}, u32[]{:S(2)}) collective-permute-start(bf16[128,2048]{1,0:T(8,128)(2,1)S(1)} %add_convert_fusion.1), channel_id=1, source_target_pairs={{0,4},{1,5},{2,6},{3,7},{4,0},{5,1},{6,2},{7,3},{8,12},{9,13},{10,... | collective-permute-start | bytes 1572872 | tf_op jit(solution)/shard_map/ppermute | solution.py:39
  674.3 23.8 %collective-permute-start.27 = (bf16[128,2048]{1,0:T(8,128)(2,1)S(1)}, bf16[128,2048]{1,0:T(8,128)(2,1)S(1)}, u32[]{:S(2)}, u32[]{:S(2)}) collective-permute-start(bf16[128,2048]{1,0:T(8,128)(2,1)S(1)} %copy-done.47), channel_id=1, source_target_pairs={{0,3},{1,0},{2,1},{3,2},{4,7},{5,4},{6,5},{7,6},{8,11},{9,8},{10,9... | collective-permute-start | bytes 1572872 | tf_op jit(solution)/shard_map/ppermute | solution.py:39
  682.6 28.3 %collective-permute-start.57 = (bf16[4,80,2048]{2,1,0:T(8,128)(2,1)S(1)}, bf16[4,80,2048]{2,1,0:T(8,128)(2,1)S(1)}, u32[]{:S(2)}, u32[]{:S(2)}) collective-permute-start(bf16[4,80,2048]{2,1,0:T(8,128)(2,1)S(1)} %pad_maximum_fusion.refs_0_), channel_id=1, source_target_pairs={{0,8},{1,9},{2,10},{3,11},{4,12},{5,13},{6,14},{7,15},{8,0},{9,1},... | collective-permute-start | bytes 3932168 | tf_op jit(solution)/shard_map/ppermute | solution.py:39
  687.5 24.5 %collective-permute-start.58 = (bf16[4,80,2048]{2,1,0:T(8,128)(2,1)S(1)}, bf16[4,80,2048]{2,1,0:T(8,128)(2,1)}, u32[]{:S(2)}, u32[]{:S(2)}) collective-permute-start(bf16[4,80,2048]{2,1,0:T(8,128)(2,1)S(1)} %collective-permute-done.56.refs_1_), channel_id=1, source_target_pairs={{0,8},{1,9},{2,10},{3,11},{4,12},{5,13},{6,14},{7,15},{8,0},{9,1},... | collective-permute-start | bytes 3932168 | tf_op jit(solution)/shard_map/ppermute | solution.py:39
  (81 other events, 2571.7 us)

commit v2 on v1

v2 whole, which is shorter than its diff:
```python
import functools
import math

import jax
import jax.numpy as jnp
from jax import lax
from jax.experimental import pallas as pl
from jax.experimental.pallas import tpu as pltpu
from jax.sharding import PartitionSpec as P

HEADS = 8
ROT = 64
EPS = 1e-05
f32 = jnp.float32
bf16 = jnp.bfloat16


def cost(time):
    return pl.CostEstimate(flops=int(time * 1.15e9), bytes_accessed=1000, transcendentals=0)


BOTH = ("rep", "shard")
SIZES = (4, 2, 2, 2, 4)
SAME_CORE = [[2 * n + c for n in range(8)] for c in range(2)]
SAME_CORE_ALL = [[(2 * n + c) * 8 + s for n in range(8) for s in range(8)] for c in range(2)]


def coords():
    for y in range(4):
        for h in range(2):
            for c in range(2):
                for l in range(2):
                    for x in range(4):
                        yield (y, h, c, l, x)


def linear(t):
    y, h, c, l, x = (v % m for v, m in zip(t, SIZES))
    return ((y * 2 + h) * 2 + c) * 8 + l * 4 + x


def move(value, y=0, h=0, c=0, l=0, x=0):
    step = (y, h, c, l, x)
    pairs = [(linear(t), linear(tuple(a + b for a, b in zip(t, step)))) for t in coords()]
    return lax.ppermute(value, BOTH, pairs)


def swap(value, axis, bit):
    at = "yhclx".index(axis)
    pairs = [(linear(t), linear(t[:at] + (t[at] ^ bit,) + t[at + 1 :])) for t in coords()]
    return lax.ppermute(value, BOTH, pairs)


def pick(value, index, axis):
    return lax.dynamic_index_in_dim(value, index, axis, keepdims=False)


def ring_gather(own, axis, cut):
    below = move(own, **{axis: 1})
    above = move(own, **{axis: -1})
    far_low = move(below[:cut], **{axis: 1})
    far_high = move(above[cut:], **{axis: -1})
    return [own, above, jnp.concatenate([far_low, far_high], 0), below]


def ring_reduce(pieces, axis, cut):
    own, above, far, below = pieces
    low = move(far[:cut].astype(bf16), **{axis: 1})
    high = move(far[cut:].astype(bf16), **{axis: -1})
    up = jnp.concatenate([above[:cut].astype(f32) + low.astype(f32), above[cut:].astype(f32)], 0)
    down = jnp.concatenate([below[:cut].astype(f32), below[cut:].astype(f32) + high.astype(f32)], 0)
    from_below = move(up.astype(bf16), **{axis: 1})
    from_above = move(down.astype(bf16), **{axis: -1})
    return own.astype(f32) + from_below.astype(f32) + from_above.astype(f32)


def normalize(value):
    xf = value.astype(f32)
    centre = xf - jnp.mean(xf, -1, keepdims=True)
    inverse = lax.rsqrt(jnp.mean(centre * centre, -1, keepdims=True) + EPS)
    return centre * inverse, inverse


def kernel_params():
    return pltpu.CompilerParams(vmem_limit_bytes=56 * 1024 * 1024)


def after_inputs(body, count, extra):
    return lambda *refs: body(*refs[:count], *refs[count + extra :])


def anywhere(count):
    return [pl.BlockSpec(memory_space=pl.ANY)] * count


def dot(a, b, ca=1, cb=0):
    return lax.dot_general(a, b, (((ca,), (cb,)), ((), ())), preferred_element_type=f32)


def hidden_part(h2, weight, first, bias):
    rows, width = h2.shape
    ff = bias.shape[1]

    def body(h_ref, w_ref, b_ref, act_ref, slope_ref):
        u = dot(h_ref[...], w_ref[...]) + b_ref[...]
        cdf = 0.5 * (1.0 + lax.erf(u * math.sqrt(0.5)))
        pdf = jnp.exp(-0.5 * u * u) * (1.0 / math.sqrt(2.0 * math.pi))
        act_ref[...] = (u * cdf).astype(bf16)
        slope_ref[...] = cdf + u * pdf

    return pl.pallas_call(
        body,
        out_shape=(
            jax.ShapeDtypeStruct((rows, ff), bf16),
            jax.ShapeDtypeStruct((rows, ff), f32),
        ),
        grid=(ff // 256,),
        in_specs=[
            pl.BlockSpec((rows, width), lambda i: (0, 0)),
            pl.BlockSpec((width, 256), lambda i: (0, i + first)),
            pl.BlockSpec((1, 256), lambda i: (0, i)),
        ],
        out_specs=(
            pl.BlockSpec((rows, 256), lambda i: (0, i)),
            pl.BlockSpec((rows, 256), lambda i: (0, i)),
        ),
        compiler_params=kernel_params(),
        cost_estimate=cost(10),
        name="hidden_part",
    )(h2, weight, bias)


def swap_halves(value):
    lane = lax.broadcasted_iota(jnp.int32, value.shape, 1)
    return jnp.where(lane < 32, pltpu.roll(value, 96, 1), pltpu.roll(value, 32, 1))


def allowed_mask(lengths_ref, block, rows):
    e0 = lengths_ref[block, 0]
    e1 = e0 + lengths_ref[block, 1]
    t = lax.broadcasted_iota(jnp.int32, (rows, rows), 0)
    s = lax.broadcasted_iota(jnp.int32, (rows, rows), 1)
    seg_t = (t >= e0).astype(jnp.int32) + (t >= e1).astype(jnp.int32)
    seg_s = (s >= e0).astype(jnp.int32) + (s >= e1).astype(jnp.int32)
    return (seg_t == seg_s) & (s <= t)


def attention(h1, weight, bias, cosine, sine, lengths, after, rows=128, head=256):
    total, width = h1.shape
    blocks = total // rows
    scale = head ** (-0.5)

    def body(len_ref, h_ref, w_ref, b_ref, cos_ref, sin_ref, qkv_ref, p_ref, o_ref, work):
        step = pl.program_id(0)

        @pl.when(step < 3)
        def _():
            work[step] = dot(h_ref[...], w_ref[...]) + b_ref[0]

        @pl.when(step >= 3)
        def _():
            block = step - 3
            at = pl.ds(block * rows, rows)
            cos, sin = cos_ref[...], sin_ref[...]

            def turned(value):
                left = value[:, :128]
                left = left * cos + swap_halves(left) * sin
                return jnp.concatenate([left, value[:, 128:]], 1).astype(bf16)

            q, k = turned(work[0, at, :]), turned(work[1, at, :])
            v = work[2, at, :].astype(bf16)
            qkv_ref[:, 0:head] = q
            qkv_ref[:, head : 2 * head] = k
            qkv_ref[:, 2 * head :] = v
            scores = dot(q, k, 1, 1) * scale
            masked = jnp.where(allowed_mask(len_ref, block, rows), scores, -1e30)
            shifted = jnp.exp(masked - jnp.max(masked, 1, keepdims=True))
            probs = shifted / jnp.sum(shifted, 1, keepdims=True)
            p_ref[...] = probs
            o_ref[...] = dot(probs.astype(bf16), v).astype(bf16)

    def at_block(i, lens):
        return (jnp.maximum(i - 3, 0), 0)

    return pl.pallas_call(
        after_inputs(body, 6, len(after)),
        out_shape=(
            jax.ShapeDtypeStruct((total, 3 * head), bf16),
            jax.ShapeDtypeStruct((total, rows), f32),
            jax.ShapeDtypeStruct((total, head), bf16),
        ),
        grid_spec=pltpu.PrefetchScalarGridSpec(
            num_scalar_prefetch=1,
            grid=(3 + blocks,),
            in_specs=[
                pl.BlockSpec((total, width), lambda i, lens: (0, 0)),
                pl.BlockSpec((width, head), lambda i, lens: (0, jnp.minimum(i, 2))),
                pl.BlockSpec((1, 1, head), lambda i, lens: (jnp.minimum(i, 2), 0, 0)),
                pl.BlockSpec((rows, 128), at_block),
                pl.BlockSpec((rows, 128), at_block),
            ]
            + anywhere(len(after)),
            out_specs=(
                pl.BlockSpec((rows, 3 * head), at_block),
                pl.BlockSpec((rows, rows), at_block),
                pl.BlockSpec((rows, head), at_block),
            ),
            scratch_shapes=[pltpu.VMEM((3, total, head), f32)],
        ),
        compiler_params=kernel_params(),
        cost_estimate=cost(14),
        name="attention",
    )(lengths, h1, weight, bias, cosine, sine, *after)


def mixed_part(active, attended, down, out, bias, sources, after):
    rows, ff = active.shape
    head, width = out.shape

    def body(source_ref, act_ref, ol_ref, wd_ref, wo_ref, b_ref, mix_ref):
        total = dot(act_ref[...], wd_ref[...]) + dot(ol_ref[...], wo_ref[...]) + b_ref[...]
        total = total.astype(bf16)
        for at in range(rows // 128):
            to = pl.ds(pl.multiple_of(source_ref[at] * 128, 128), 128)
            mix_ref[to, :] = total[at * 128 : (at + 1) * 128]

    return pl.pallas_call(
        after_inputs(body, 6, len(after)),
        out_shape=jax.ShapeDtypeStruct((rows, width), bf16),
        grid_spec=pltpu.PrefetchScalarGridSpec(
            num_scalar_prefetch=1,
            grid=(width // 256,),
            in_specs=[
                pl.BlockSpec((rows, ff), lambda i, n: (0, 0)),
                pl.BlockSpec((rows, head), lambda i, n: (0, 0)),
                pl.BlockSpec((ff, 256), lambda i, n: (0, i)),
                pl.BlockSpec((head, 256), lambda i, n: (0, i)),
                pl.BlockSpec((1, 256), lambda i, n: (0, i)),
            ]
            + anywhere(len(after)),
            out_specs=pl.BlockSpec((rows, 256), lambda i, n: (0, i)),
        ),
        compiler_params=kernel_params(),
        cost_estimate=cost(11),
        name="mixed_part",
    )(sources, active, attended, down, out, bias, *after)


def inner_grad(dy, down, slope, after):
    rows, width = dy[0].shape[1:]
    count = len(dy)
    total = count * rows
    ff = down.shape[0]

    def body(*refs):
        wd_ref, s_ref, du_ref, db_ref, dy_ref, sems = refs[count:]

        @pl.when(pl.program_id(0) == 0)
        def _():
            fetch(refs[:count], dy_ref, sems, rows)

        du = (dot(dy_ref[...], wd_ref[...], 1, 1) * s_ref[...]).astype(bf16)
        du_ref[...] = du
        db_ref[...] = jnp.sum(du.astype(f32), 0, keepdims=True)

    return pl.pallas_call(
        after_inputs(body, count + 2, len(after)),
        out_shape=(
            jax.ShapeDtypeStruct((total, ff), bf16),
            jax.ShapeDtypeStruct((1, ff), f32),
        ),
        grid=(ff // 256,),
        in_specs=anywhere(count)
        + [
            pl.BlockSpec((256, width), lambda i: (i, 0)),
            pl.BlockSpec((total, 256), lambda i: (0, i)),
        ]
        + anywhere(len(after)),
        out_specs=(
            pl.BlockSpec((total, 256), lambda i: (0, i)),
            pl.BlockSpec((1, 256), lambda i: (0, i)),
        ),
        scratch_shapes=[
            pltpu.VMEM((total, width), bf16),
            pltpu.SemaphoreType.DMA((count,)),
        ],
        compiler_params=kernel_params(),
        cost_estimate=cost(8),
        name="inner_grad",
    )(*dy, down, slope, *after)


def back_norms(d_qkv, d_hidden, weight, tokens, mean, inverse, gains, after):
    total, n1 = d_qkv.shape
    n2 = d_hidden.shape[1]
    width = tokens.shape[1]
    count = total // 128

    def body(dq_ref, du_ref, w_ref, x_ref, m_ref, i_ref, g_ref, sums_ref, *refs):
        d1 = dot(dq_ref[...], w_ref[:, :n1], 1, 1)
        d2 = dot(du_ref[...], w_ref[:, n1:], 1, 1)
        normed = (x_ref[...].astype(f32) - m_ref[...]) * i_ref[...]
        both = (d1 * g_ref[0:1] + d2 * g_ref[1:2]).astype(bf16)
        for at in range(count):
            refs[at][...] = both[at * 128 : (at + 1) * 128]
        sums_ref[0:1] = jnp.sum(d1 * normed, 0, keepdims=True)
        sums_ref[1:2] = jnp.sum(d1, 0, keepdims=True)
        sums_ref[2:3] = jnp.sum(d2 * normed, 0, keepdims=True)
        sums_ref[3:4] = jnp.sum(d2, 0, keepdims=True)

    return pl.pallas_call(
        after_inputs(body, 7, len(after)),
        out_shape=(jax.ShapeDtypeStruct((4, width), f32),)
        + (jax.ShapeDtypeStruct((128, width), bf16),) * count,
        grid=(width // 256,),
        in_specs=[
            pl.BlockSpec((total, n1), lambda i: (0, 0)),
            pl.BlockSpec((total, n2), lambda i: (0, 0)),
            pl.BlockSpec((256, n1 + n2), lambda i: (i, 0)),
            pl.BlockSpec((total, 256), lambda i: (0, i)),
            pl.BlockSpec((total, 1), lambda i: (0, 0)),
            pl.BlockSpec((total, 1), lambda i: (0, 0)),
            pl.BlockSpec((2, 256), lambda i: (0, i)),
        ]
        + anywhere(len(after)),
        out_specs=(pl.BlockSpec((4, 256), lambda i: (0, i)),)
        + (pl.BlockSpec((128, 256), lambda i: (0, i)),) * count,
        compiler_params=kernel_params(),
        cost_estimate=cost(15),
        name="back_norms",
    )(d_qkv, d_hidden, weight, tokens, mean, inverse, gains, *after)


def norms(pieces, gains):
    rows, width = pieces[0].shape[1:]
    count = len(pieces)
    total = rows * count

    def body(*refs):
        g_ref, x_ref, h1_ref, h2_ref, m_ref, i_ref = refs[count:]
        for at in range(count):

            @pl.when(pl.program_id(0) == at)
            def _(at=at):
                x_ref[...] = refs[at][0]

        x = x_ref[...].astype(f32)
        mean = jnp.mean(x, 1, keepdims=True)
        centre = x - mean
        inverse = lax.rsqrt(jnp.mean(centre * centre, 1, keepdims=True) + EPS)
        normed = centre * inverse
        m_ref[...] = mean
        i_ref[...] = inverse
        h1_ref[...] = (normed * g_ref[0:1] + g_ref[1:2]).astype(bf16)
        h2_ref[...] = (normed * g_ref[2:3] + g_ref[3:4]).astype(bf16)

    column = jax.ShapeDtypeStruct((total, 1), f32)
    wide = jax.ShapeDtypeStruct((total, width), bf16)
    block = pl.BlockSpec((rows, width), lambda i: (i, 0))
    thin = pl.BlockSpec((rows, 1), lambda i: (i, 0))
    return pl.pallas_call(
        body,
        out_shape=(wide, wide, wide, column, column),
        grid=(count,),
        in_specs=[pl.BlockSpec((1, rows, width), lambda i: (0, 0, 0))] * count
        + [pl.BlockSpec((4, width), lambda i: (0, 0))],
        out_specs=(block, block, block, thin, thin),
        compiler_params=kernel_params(),
        cost_estimate=cost(9),
        name="norms",
    )(*pieces, gains)


def fetch(pieces, target, sems, rows):
    copies = [
        pltpu.make_async_copy(
            piece.at[1] if len(piece.shape) == 3 else piece,
            target.at[pl.ds(at * rows, rows)],
            sems.at[at],
        )
        for at, piece in enumerate(pieces)
    ]
    for copy in copies:
        copy.start()
    for copy in copies:
        copy.wait()


def dot_rows(a, b):
    return lax.dot_general(a, b, (((0,), (0,)), ((), ())), preferred_element_type=f32)


def packed(qkv_weight, up_weight, vectors, lengths, place, head):
    wide, up_wide = qkv_weight.shape[1], up_weight.shape[1]
    part, up_part = 3 * head, up_wide // 8
    cols = part + up_part

    def body(place_ref, len_ref, q_ref, u_ref, v_ref, out_ref):
        lane = lax.broadcasted_iota(jnp.int32, (8, cols), 1)
        row = lax.broadcasted_iota(jnp.int32, (8, cols), 0)
        sizes = jnp.zeros((8, cols), f32)
        for at in range(3):
            sizes = jnp.where(lane == at, len_ref[0, at].astype(f32), sizes)
        vector = jnp.broadcast_to(v_ref[...].astype(f32), (8, cols))
        tail = jnp.where(row == 0, vector, jnp.where(row == 1, sizes, 0.0)).astype(bf16)
        for owner in range(8):
            pieces = [
                q_ref[:, (third * 8 + owner) * head : (third * 8 + owner + 1) * head]
                for third in range(3)
            ]
            pieces.append(u_ref[:, owner * up_part : (owner + 1) * up_part])
            out_ref[owner] = jnp.concatenate([jnp.concatenate(pieces, 1), tail], 0)

    return pl.pallas_call(
        body,
        out_shape=jax.ShapeDtypeStruct((8, 40, cols), bf16),
        grid_spec=pltpu.PrefetchScalarGridSpec(
            num_scalar_prefetch=2,
            grid=(1,),
            in_specs=[
                pl.BlockSpec((32, wide), lambda i, place, lens: (place[0], 0)),
                pl.BlockSpec((32, up_wide), lambda i, place, lens: (place[0], 0)),
                pl.BlockSpec((1, cols), lambda i, place, lens: (0, 0)),
            ],
            out_specs=pl.BlockSpec((8, 40, cols), lambda i, place, lens: (0, 0, 0)),
        ),
        compiler_params=kernel_params(),
        cost_estimate=cost(3),
        name="packed",
    )(place, lengths, qkv_weight, up_weight, vectors)


def sorted_weight(pieces, spots):
    rows, cols = pieces[0][0].shape[1:]
    count = len(pieces)

    def body(spot_ref, *refs):
        step = pl.program_id(0)
        for ref, (array, first, at) in zip(refs, pieces):

            @pl.when(step == at)
            def _(ref=ref, first=first, size=array.shape[0]):
                refs[count][first : first + size, 0] = ref[...]

    return pl.pallas_call(
        body,
        out_shape=jax.ShapeDtypeStruct((8, 8, rows, cols), bf16),
        grid_spec=pltpu.PrefetchScalarGridSpec(
            num_scalar_prefetch=1,
            grid=(8,),
            in_specs=[
                pl.BlockSpec(array.shape, lambda i, spot: (0, 0, 0)) for array, _, _ in pieces
            ],
            out_specs=pl.BlockSpec((8, 1, rows, cols), lambda i, spot: (0, spot[i], 0, 0)),
        ),
        compiler_params=kernel_params(),
        cost_estimate=cost(6),
        name="sorted_weight",
    )(spots, *[piece[0] for piece in pieces]).reshape(64 * rows, cols)


def split(part, first, keep_ref, send_ref, index):
    @pl.when(first)
    def _():
        keep_ref[index] = part[:, 0]
        send_ref[index] = part[:, 1]

    @pl.when(jnp.logical_not(first))
    def _():
        keep_ref[index] = part[:, 1]
        send_ref[index] = part[:, 0]


def inner_weight_grads(active, h2, dy, d_hidden, numbers):
    piece_rows, width = dy[0].shape[1:]
    count = len(dy)
    rows, ff = active.shape
    downs = ff // 256

    def body(number_ref, act_ref, h2_ref, du_ref, *refs):
        keep_ref, send_ref, sum_ref, dy_ref, sems = refs[count:]
        step = pl.program_id(0)
        first = number_ref[0] == 0

        @pl.when(step == 0)
        def _():
            fetch(refs[:count], dy_ref, sems, piece_rows)
            own = dy_ref[:, pl.ds(pl.multiple_of(number_ref[1] * 256, 256), 256)]
            sum_ref[...] = jnp.sum(own.astype(f32), 0, keepdims=True)

        @pl.when(step < downs)
        def _():
            part = dot_rows(act_ref[...], dy_ref[...]).astype(bf16).reshape(2, 2, 64, width)
            split(part, first, keep_ref, send_ref, (pl.ds(step * 2, 2), pl.ds(0, 64)))

        for owner in range(8):

            @pl.when(step == downs + owner)
            def _(owner=owner):
                part = dot_rows(h2_ref[...], du_ref[...]).astype(bf16).reshape(8, 2, 16, ff)
                at = (slice(None), pl.ds(64 + 16 * (owner % 4), 16), pl.ds(owner // 4 * ff, ff))
                split(part, first, keep_ref, send_ref, at)

    out = jax.ShapeDtypeStruct((8, 128, width), bf16)
    whole = pl.BlockSpec((8, 128, width), lambda i, n: (0, 0, 0))
    return pl.pallas_call(
        body,
        out_shape=(out, out, jax.ShapeDtypeStruct((1, 256), f32)),
        grid_spec=pltpu.PrefetchScalarGridSpec(
            num_scalar_prefetch=1,
            grid=(downs + 8,),
            in_specs=[
                pl.BlockSpec((rows, 256), lambda i, n: (0, jnp.minimum(i, downs - 1))),
                pl.BlockSpec((rows, 256), lambda i, n: (0, jnp.maximum(i - downs, 0))),
                pl.BlockSpec((rows, ff), lambda i, n: (0, 0)),
            ]
            + anywhere(count),
            out_specs=(whole, whole, pl.BlockSpec((1, 256), lambda i, n: (0, 0))),
            scratch_shapes=[
                pltpu.VMEM((rows, width), bf16),
                pltpu.SemaphoreType.DMA((count,)),
            ],
        ),
        compiler_params=kernel_params(),
        cost_estimate=cost(16),
        name="inner_weight_grads",
    )(numbers, active, h2, d_hidden, *dy)


def attention_grads(dy, out, qkv, probs, cosine, sine, h1, attended, numbers, after, rows=128):
    width = dy[0].shape[2]
    count = len(dy)
    total = count * rows
    head = out.shape[0]
    blocks = total // rows
    scale = head ** (-0.5)

    def body(number_ref, *refs):
        wo_ref, qkv_ref, p_ref, cos_ref, sin_ref, h1_ref, ol_ref = refs[count : count + 7]
        dq_ref, dqb_ref, keep_ref, send_ref, d_att, dy_ref, sems = refs[count + 7 :]
        step = pl.program_id(0)
        first = number_ref[0] == 0

        @pl.when(step == 0)
        def _():
            fetch(refs[:count], dy_ref, sems, rows)
            d_att[...] = dot(dy_ref[...], wo_ref[...], 1, 1).astype(bf16)
            dqb_ref[...] = jnp.zeros_like(dqb_ref)
            part = dot_rows(ol_ref[...], dy_ref[...]).astype(bf16).reshape(8, 2, 16, width)
            split(part, first, keep_ref, send_ref, (slice(None), pl.ds(48, 16)))

        @pl.when((step > 0) & (step <= blocks))
        def _():
            at = pl.ds(pl.multiple_of((step - 1) * rows, rows), rows)
            cos, sin = cos_ref[...], sin_ref[...]
            q, k, v = (qkv_ref[:, n * head : (n + 1) * head] for n in range(3))
            probs = p_ref[...]
            d_out = d_att[at, :]
            d_value = dot(probs.astype(bf16), d_out, 0, 0)
            d_probs = dot(d_out, v, 1, 1)
            centred = d_probs - jnp.sum(d_probs * probs, 1, keepdims=True)
            d_scores = (probs * centred).astype(bf16)

            def back(value):
                value = value * scale
                left = value[:, :128]
                left = left * cos - swap_halves(left) * sin
                return jnp.concatenate([left, value[:, 128:]], 1).astype(bf16)

            for n, grad in enumerate(
                (back(dot(d_scores, k)), back(dot(d_scores, q, 0, 0)), d_value.astype(bf16))
            ):
                dq_ref[at, n * head : (n + 1) * head] = grad
                dqb_ref[:, n * head : (n + 1) * head] += jnp.sum(grad.astype(f32), 0, keepdims=True)

        for owner in range(8):

            @pl.when(step == blocks + 1 + owner)
            def _(owner=owner):
                part = dot_rows(h1_ref[...], dq_ref[...]).astype(bf16).reshape(8, 2, 16, 3 * head)
                for third in range(3):
                    at = (slice(None), pl.ds(16 * third, 16), pl.ds(owner * head, head))
                    split(
                        part[..., third * head : (third + 1) * head],
                        first,
                        keep_ref,
                        send_ref,
                        at,
                    )

    def at_block(i, n):
        return (jnp.clip(i - 1, 0, blocks - 1), 0)

    grads = jax.ShapeDtypeStruct((8, 64, width), bf16)

    def whole(*shape):
        return pl.BlockSpec(shape, lambda i, n: (0,) * len(shape))

    return pl.pallas_call(
        after_inputs(body, 8 + count, len(after)),
        out_shape=(
            jax.ShapeDtypeStruct((total, 3 * head), bf16),
            jax.ShapeDtypeStruct((1, 3 * head), f32),
            grads,
            grads,
        ),
        grid_spec=pltpu.PrefetchScalarGridSpec(
            num_scalar_prefetch=1,
            grid=(1 + blocks + 8,),
            in_specs=anywhere(count)
            + [
                whole(head, width),
                pl.BlockSpec((rows, 3 * head), at_block),
                pl.BlockSpec((rows, rows), at_block),
                pl.BlockSpec((rows, 128), at_block),
                pl.BlockSpec((rows, 128), at_block),
                pl.BlockSpec((total, 256), lambda i, n: (0, jnp.maximum(i - 1 - blocks, 0))),
                whole(total, head),
            ]
            + anywhere(len(after)),
            out_specs=(
                whole(total, 3 * head),
                whole(1, 3 * head),
                whole(8, 64, width),
                whole(8, 64, width),
            ),
            scratch_shapes=[
                pltpu.VMEM((total, head), bf16),
                pltpu.VMEM((total, width), bf16),
                pltpu.SemaphoreType.DMA((count,)),
            ],
        ),
        compiler_params=kernel_params(),
        cost_estimate=cost(20),
        name="attention_grads",
    )(numbers, *dy, out, qkv, probs, cosine, sine, h1, attended, *after)


def added(terms, groups, numbers, after):
    rows, cols = terms[0][0].shape[1:]
    firsts = [sum(groups[:n]) for n in range(len(groups))]

    def body(number_ref, *refs):
        step = pl.program_id(0)
        total = None
        for ref, (_, _, steps) in zip(refs, terms):
            value = ref[0].astype(f32)
            if steps is not None:
                counts = functools.reduce(jnp.logical_or, [step == at for at in steps])
                value = jnp.where(counts, value, 0.0)
            total = value if total is None else total + value
        total = total.astype(bf16)
        for ref, first, size in zip(refs[len(terms) :], firsts, groups):

            @pl.when((step >= first) & (step < first + size))
            def _(ref=ref):
                ref[0] = total

    def came(place):
        return pl.BlockSpec((1, rows, cols), lambda i, n: (place(i, n), 0, 0))

    def goes(first, size):
        return pl.BlockSpec((1, rows, cols), lambda i, n: (jnp.clip(i - first, 0, size - 1), 0, 0))

    return pl.pallas_call(
        after_inputs(body, 1 + len(terms), len(after)),
        out_shape=tuple(jax.ShapeDtypeStruct((size, rows, cols), bf16) for size in groups),
        grid_spec=pltpu.PrefetchScalarGridSpec(
            num_scalar_prefetch=1,
            grid=(sum(groups),),
            in_specs=[came(place) for _, place, _ in terms] + anywhere(len(after)),
            out_specs=tuple(goes(first, size) for first, size in zip(firsts, groups)),
        ),
        compiler_params=kernel_params(),
        cost_estimate=cost(4),
        name="added",
    )(numbers, *[term[0] for term in terms], *after)


def spread(pieces, spots, targets):
    rows, cols = pieces[0].shape[1:]
    firsts, total = [], 0
    for piece in pieces:
        firsts.append(total)
        total += piece.shape[0]

    def body(spot_ref, *refs):
        step = pl.program_id(0)
        for ref, first, piece in zip(refs, firsts, pieces):

            @pl.when((step >= first) & (step < first + piece.shape[0]))
            def _(ref=ref):
                for out_ref, (_, high, parts) in zip(refs[len(pieces) :], targets):
                    for to, row, col, size in parts:
                        out_ref[:, to : to + size] = ref[0, row : row + high, col : col + size].astype(
                            f32
                        )

    def chosen(first, size):
        return pl.BlockSpec(
            (1, rows, cols), lambda i, spot: (jnp.clip(i - first, 0, size - 1), 0, 0)
        )

    return pl.pallas_call(
        body,
        out_shape=tuple(
            jax.ShapeDtypeStruct((total * high, wide), f32) for wide, high, _ in targets
        ),
        grid_spec=pltpu.PrefetchScalarGridSpec(
            num_scalar_prefetch=1,
            grid=(total,),
            in_specs=[chosen(first, piece.shape[0]) for first, piece in zip(firsts, pieces)],
            out_specs=tuple(
                pl.BlockSpec((high, wide), lambda i, spot: (spot[i], 0))
                for wide, high, _ in targets
            ),
        ),
        compiler_params=kernel_params(),
        cost_estimate=cost(10),
        name="spread",
    )(spots, *pieces)


def small_sums(norm_sums, qkv_sums, up_sums, dy_sums, numbers):
    def body(number_ref, norm_ref, q_ref, u_ref, y_ref, out_ref, work):
        shard = number_ref[1]
        for owner in range(8):
            mine = shard == owner
            for n in range(4):
                for half in range(2):
                    at = owner * 256 + half * 128
                    work[owner, n * 2 + half : n * 2 + half + 1] = norm_ref[n : n + 1, at : at + 128]
            for n in range(3):
                third, source = divmod(owner * 3 + n, 8)
                for half in range(2):
                    at = third * 256 + half * 128
                    work[owner, 8 + n * 2 + half : 9 + n * 2 + half] = jnp.where(
                        shard == source, q_ref[:, at : at + 128], 0.0
                    )
            for n in range(8):
                work[owner, 14 + n : 15 + n] = jnp.where(
                    mine, u_ref[:, n * 128 : (n + 1) * 128], 0.0
                )
            for n in range(2):
                work[owner, 22 + n : 23 + n] = jnp.where(
                    mine, y_ref[:, n * 128 : (n + 1) * 128], 0.0
                )
        out_ref[0] = work[...].astype(bf16)

    def whole(*shape):
        return pl.BlockSpec(shape, lambda i, n: (0,) * len(shape))

    return pl.pallas_call(
        body,
        out_shape=jax.ShapeDtypeStruct((16, 8, 24, 128), bf16),
        grid_spec=pltpu.PrefetchScalarGridSpec(
            num_scalar_prefetch=1,
            grid=(16,),
            in_specs=[whole(4, 2048), whole(1, 768), whole(1, 1024), whole(1, 256)],
            out_specs=pl.BlockSpec((1, 8, 24, 128), lambda i, n: (i, 0, 0, 0)),
            scratch_shapes=[pltpu.VMEM((8, 24, 128), f32)],
        ),
        compiler_params=kernel_params(),
        cost_estimate=cost(3),
        name="small_sums",
    )(numbers, norm_sums, qkv_sums, up_sums, dy_sums)


def local(
    tokens,
    doc_lengths,
    cotangent,
    ln1_gain,
    ln1_bias,
    ln2_gain,
    ln2_bias,
    qkv_weight,
    qkv_bias,
    out_weight,
    out_bias,
    up_weight,
    up_bias,
    down_weight,
    down_bias,
):
    rows, width = tokens.shape
    head = width // HEADS
    group = 8
    rep = lax.axis_index("rep")
    shard = lax.axis_index("shard")
    y, h, c = rep // 4, (rep // 2) % 2, rep % 2
    l, x = shard // 4, shard % 4
    ff = up_bias.shape[0]

    pair = jnp.stack([tokens, cotangent])
    below, above, other = move(pair, x=1), move(pair, x=-1), move(pair, l=1)
    far, other_above, other_below = move(below, x=1), move(other, x=-1), move(below, l=1)
    x_other_far, dy_other_far = move(other_below[0], x=1), move(other_above[1], x=-1)
    pairs = (pair, above, far, below, other, other_above, None, other_below)
    x_all = tuple(x_other_far[None] if p is None else p for p in pairs)
    dy_all = tuple(dy_other_far if p is None else p for p in pairs)

    vectors = jnp.concatenate([ln1_gain, ln1_bias, ln2_gain, ln2_bias, qkv_bias])[None]
    place = (y * 2 + c).astype(jnp.int32).reshape(1)
    part = packed(qkv_weight, up_weight, vectors, doc_lengths, place, head)
    part = lax.all_to_all(part, "shard", 0, 0)
    cols = part.shape[-1]
    own, infos = part[:, :32], part[:, 32:].astype(f32)
    below, above = move(own, y=1), move(own, y=-1)
    far_low, far_high = move(below[:4], y=1), move(above[4:], y=-1)
    mine = ((own, 0, 0), (above, 0, 1), (far_low, 0, 2), (far_high, 4, 2), (below, 0, 3))
    yours = tuple((move(array, c=1), first, spot + 4) for array, first, spot in mine)
    steps4 = (y + jnp.arange(4)) % 4
    spots = jnp.concatenate([steps4 * 2 + c, steps4 * 2 + 1 - c]).astype(jnp.int32)
    w_mixed = sorted_weight(mine + yours, spots)

    gains = infos[:, 0, :1024].reshape(8, 4, 256).transpose(1, 0, 2).reshape(4, width)
    qkv_b = infos[:, 0, 1024:].reshape(8 * 3, 1, head)
    qkv_b = jnp.stack(
        [lax.dynamic_index_in_dim(qkv_b, third * 8 + shard, 0, False) for third in range(3)]
    )
    steps8 = jnp.arange(8)
    sources = ((steps8 // 4) ^ l) * 4 + (x + steps8 % 4) % 4
    sources = sources.astype(jnp.int32)
    lengths = infos[:, 1, :3]
    lengths = jnp.sum(
        jnp.where(sources[:, None, None] == steps8[None, :, None], lengths[None], 0.0), 1
    ).astype(jnp.int32)
    ends = jnp.cumsum(lengths, 1)
    starts = ends - lengths
    steps_t = jnp.arange(rows, dtype=jnp.int32)
    segment = jnp.sum((steps_t[None, :, None] >= ends[:, None, :]).astype(jnp.int32), -1)
    slots = jnp.arange(lengths.shape[1], dtype=jnp.int32)
    begin = jnp.sum(
        jnp.where(segment[:, :, None] == slots[None, None, :], starts[:, None, :], 0), -1
    )
    position = (steps_t[None, :] - begin).astype(f32).reshape(group * rows, 1)
    lane = jnp.arange(128)
    freq = 10000.0 ** (-2.0 * (lane % (ROT // 2)).astype(f32) / ROT)
    angle = position * freq[None, :]
    cosine = jnp.where(lane < ROT, jnp.cos(angle), 1.0)
    sine = jnp.sin(angle)
    sine = jnp.where(lane < ROT // 2, -sine, jnp.where(lane < ROT, sine, 0.0))

    x_rows, h1, h2, mean, inverse = norms(x_all, gains)
    active, slope = hidden_part(h2, w_mixed, 3 * head // 256, up_bias.astype(f32)[None])
    both_bias = (out_bias.astype(f32) + down_bias.astype(f32))[None, :]
    wide_bias = lax.dynamic_update_slice(jnp.zeros((1, width), f32), both_bias, (0, shard * 256))
    numbers = jnp.stack([c, shard, y, h]).astype(jnp.int32)

    d_hidden, up_sums = inner_grad(dy_all, down_weight, slope, ())
    keep, send, dy_sums = inner_weight_grads(active, h2, dy_all, d_hidden, numbers)
    got = move(send, c=1)
    qkv, probs, attended = attention(h1, w_mixed, qkv_b, cosine, sine, lengths, (send,))

    def turn(k):
        return lambda i, n: (n[2] + k) % 4 * 2 + i % 2

    low, high = added([(keep, turn(2), None), (got, turn(2), None)], (1, 1), numbers, (attended,))
    from_low, from_high = move(low, y=1), move(high, y=-1)
    mix = mixed_part(
        active, attended, down_weight, out_weight, wide_bias, sources, (low, high)
    )
    def sides(i, n):
        return (n[2] + 1 + i // 2 * 2) % 4 * 2 + i % 2

    above, below = added(
        [
            (keep, sides, None),
            (got, sides, None),
            (from_low, lambda i, n: 0, (0,)),
            (from_high, lambda i, n: 0, (3,)),
        ],
        (2, 2),
        numbers,
        (mix,),
    )
    from_below, from_above = move(above, y=1), move(below, y=-1)
    d_qkv, qkv_sums, a_keep, a_send = attention_grads(
        dy_all, out_weight, qkv, probs, cosine, sine, h1, attended, numbers, (above, below)
    )
    a_got = move(a_send, c=1)

    def ends_at(i, n):
        return n[2] * 2 + jnp.where(i == 0, 1 - n[3], n[3])

    def crosses(i, n):
        return jnp.where(i == 0, 1 - n[3], n[3])

    leaves, inner = added(
        [
            (keep, ends_at, None),
            (got, ends_at, None),
            (from_below, crosses, None),
            (from_above, crosses, None),
        ],
        (1, 1),
        numbers,
        (a_send,),
    )
    crossed = move(leaves, h=1)

    def away(i, n):
        return i * 2 + 1 - n[3]

    (a_away,) = added([(a_keep, away, None), (a_got, away, None)], (4,), numbers, (leaves,))
    a_crossed = move(a_away, h=1)

    def around(i, n):
        return (n[2] + 2 - i) % 4

    def around_here(i, n):
        return around(i, n) * 2 + n[3]

    a_far, a_above, a_own, a_below = added(
        [
            (a_keep, around_here, None),
            (a_got, around_here, None),
            (a_crossed, around, None),
        ],
        (1, 1, 1, 1),
        numbers,
        (),
    )
    norm_sums, *sums = back_norms(
        d_qkv,
        d_hidden,
        w_mixed,
        x_rows,
        mean,
        inverse,
        jnp.stack([gains[0], gains[2]]),
        (a_away,),
    )
    ((inner,),) = added(
        [(inner, lambda i, n: 0, None), (crossed, lambda i, n: 0, None)], (1,), numbers, (sums[0],)
    )
    up = inner[64:].reshape(4, 16, 2, ff).transpose(2, 0, 1, 3).reshape(8, 16, ff)
    up = lax.all_to_all(up, "shard", 0, 0)
    up = up.reshape(2, 4, 16, ff).transpose(1, 2, 0, 3).reshape(64, width)
    inner = jnp.concatenate([inner[:64], up], 0)
    inner = jnp.stack([inner, move(inner, h=1)])

    a_sum = ring_reduce([a_own[0], a_above[0], a_far[0], a_below[0]], "y", 32).astype(bf16)
    third = a_sum[:48].reshape(48, 8, head).transpose(1, 0, 2)
    third = lax.all_to_all(third, "shard", 0, 0).transpose(1, 0, 2).reshape(48, width)
    a_sum = jnp.concatenate([third, a_sum[48:]], 0)

    def ring(pieces, way):
        own, above, far, below = pieces if way == 1 else (pieces[n] for n in (0, 3, 2, 1))
        passed = move(far, x=way)
        above = (above.astype(f32) + passed.astype(f32)).astype(bf16)
        return (
            own.astype(f32) + move(above, x=way).astype(f32) + move(below, x=-way).astype(f32)
        )

    sum_other = move(ring(sums[4:], 1).astype(bf16), l=1)
    own_sum = ring(sums[:4], -1) + sum_other.astype(f32)
    mixed = lax.psum_scatter(mix, "shard", scatter_dimension=0, tiled=True)
    mixed = (tokens.astype(f32) + mixed.astype(f32)).astype(bf16)
    own_normed, own_inverse = normalize(tokens)
    tokens_grad = cotangent.astype(f32) + own_inverse * (
        own_sum
        - jnp.mean(own_sum, -1, keepdims=True)
        - own_normed * jnp.mean(own_sum * own_normed, -1, keepdims=True)
    )

    smalls = small_sums(norm_sums, qkv_sums, up_sums, dy_sums, numbers)
    smalls = lax.all_to_all(smalls.reshape(128, 24, 128), BOTH, 0, 0)
    smalls = jnp.sum(smalls.astype(f32), 0)
    norm_grads = smalls[:8].reshape(4, 256)
    dy_total = smalls[22:].reshape(256)

    below, above = move(inner, y=1), move(inner, y=-1)
    far_low, far_high = move(below[:1], y=1), move(above[1:], y=-1)
    pieces = [inner, above, far_low, far_high, below]
    pieces += [move(piece, c=1) for piece in pieces]
    spots = []
    for low in (c, 1 - c):
        for k, highs in ((0, (h, 1 - h)), (1, (h, 1 - h)), (2, (h,)), (2, (1 - h,)), (3, (h, 1 - h))):
            spots += [(((y + k) % 4) * 2 + high) * 2 + low for high in highs]
    up_parts = [
        (source * ff, 64 + 16 * (source % 4), source // 4 * ff, ff) for source in range(8)
    ]
    down_grad, up_grad = spread(
        pieces,
        jnp.stack(spots).astype(jnp.int32),
        [(width, 64, [(0, 0, 0, width)]), (8 * ff, 16, up_parts)],
    )

    a_sum = jnp.stack(ring_gather(a_sum, "y", 32))
    a_other = move(a_sum, h=1)
    pieces = [a_sum, a_other, move(a_sum, c=1), move(a_other, c=1)]
    spots = [
        (steps4 * 2 + high) * 2 + low for low in (c, 1 - c) for high in (h, 1 - h)
    ]
    out_grad, qkv_grad = spread(
        pieces,
        jnp.concatenate(spots).astype(jnp.int32),
        [
            (width, 16, [(0, 48, 0, width)]),
            (3 * width, 16, [(n * width, 16 * n, 0, width) for n in range(3)]),
        ],
    )
    return (
        mixed,
        tokens_grad,
        norm_grads[0],
        norm_grads[1],
        norm_grads[2],
        norm_grads[3],
        qkv_grad,
        smalls[8:14].reshape(768),
        out_grad,
        dy_total,
        up_grad,
        smalls[14:22].reshape(ff),
        down_grad,
        dy_total,
    )


def solution(mesh):
    rows = P(BOTH, None)
    vector, matrix = P("shard"), P("shard", None)
    return jax.shard_map(
        local,
        mesh=mesh,
        in_specs=(rows, rows, rows, vector, vector, vector, vector)
        + (matrix, vector, matrix, vector, matrix, vector, matrix, vector),
        out_specs=(rows, rows, vector, vector, vector, vector)
        + (matrix, vector, matrix, vector, matrix, vector, matrix, vector),
        check_vma=False,
    )
```

time: 751 us -> 513 us (0.68)
  the two profiles are of different devices: /device:TPU:32 before, /device:TPU:1 now
where the time goes in v2:
time: 513 us; the launch traced here: 504 us
  Pallas kernels  188 us (37%)
  waiting for transfers between devices  148 us (29%)
  starting transfers between devices  101 us (20%)
  local copies, waits for them, and re-layouts  29.6 us (6%)
  other arithmetic  22.9 us (4%)
  between operations  15.2 us (3%)
    ppermute x53, waiting for transfers between devices, move(): return lax.ppermute(value, BOTH, pairs)  134 us
    ppermute x53, starting transfers between devices, move(): return lax.ppermute(value, BOTH, pairs)  82.3 us
    pallas_call x2, Pallas kernels, spread(): pl.pallas_call(body, out_shape=tuple((jax.ShapeDtypeStruct((total * high,...  27.3 us
    pallas_call x6, Pallas kernels, added(): pl.pallas_call(after_inputs(body, 1 + len(terms), len(after)), out_shape=...  26.3 us
    pallas_call x1, Pallas kernels, attention_grads(): pl.pallas_call(after_inputs(body, 8 + count, len(after)), out_shape=(jax....  23.6 us
    pallas_call x1, Pallas kernels, inner_weight_grads(): pl.pallas_call(body, out_shape=(out, out, jax.ShapeDtypeStruct((1, 256),...  21.6 us
    pallas_call x1, Pallas kernels, back_norms(): pl.pallas_call(after_inputs(body, 7, len(after)), out_shape=(jax.ShapeDty...  14.7 us
    pallas_call x1, Pallas kernels, attention(): pl.pallas_call(after_inputs(body, 6, len(after)), out_shape=(jax.ShapeDty...  14.5 us
  transfers between devices with their start and end apart: 58, of which 18 were waited for; matrix products, arithmetic and copies ran while one was open for 8% of the time, Pallas kernels for 24%

profile of v2, /device:TPU:1, one launch (start us, length us, event | category | flops | bytes accessed | tf_op | source)
XLA Modules:
  0.0 504.0 jit_solution(408420496997566087)
XLA Ops:
  23.7 10.8 %collective-permute-done.1.refs_3_.refs_4_ = bf16[2,128,2048]{2,1,0:T(8,128)(2,1)} collective-permute-done((bf16[2,128,2048]{2,1,0:T(8,128)(2,1)S(1)}, bf16[2,128,2048]{2,1,0:T(8,128)(2,1)}, u32[]{:S(2)}, u32[]{:S(2)}) %collective-permute-start.1) | collective-permute-done | bytes 1048608 | tf_op jit(solution)/shard_map/ppermute | solution.py:45
  39.4 8.8 %all-to-all-done = bf16[8,40,1792]{2,1,0:T(8,128)(2,1)S(1)} async-done(((bf16[8,40,1792]{2,1,0:T(8,128)(2,1)}), bf16[8,40,1792]{2,1,0:T(8,128)(2,1)S(1)}, u32[]{:S(2)}, u32[]{:S(2)}) %all-to-all-start) | async-done | bytes 1146912 | tf_op jit(solution)/shard_map/all_to_all | solution.py:807
  51.3 18.3 %collective-permute-done.5.refs_7_.refs_8_ = bf16[2,128,2048]{2,1,0:T(8,128)(2,1)} collective-permute-done((bf16[2,128,2048]{2,1,0:T(8,128)(2,1)}, bf16[2,128,2048]{2,1,0:T(8,128)(2,1)}, u32[]{:S(2)}, u32[]{:S(2)}) %collective-permute-start.5) | collective-permute-done | bytes 1048608 | tf_op jit(solution)/shard_map/ppermute | solution.py:45
  78.9 8.6 %collective-permute-start.11 = (bf16[8,32,1792]{2,1,0:T(8,128)(2,1)S(1)}, bf16[8,32,1792]{2,1,0:T(8,128)(2,1)S(1)}, u32[]{:S(2)}, u32[]{:S(2)}) collective-permute-start(bf16[8,32,1792]{2,1,0:T(8,128)(2,1)S(1)} %slice.165.refs_0_), channel_id=1, source_target_pairs={{0,8},{1,9},{2,10},{3,11},{4,12},{5,13},{6,14},{7,15},{8,0},{9,1},... | collective-permute-start | bytes 2752520 | tf_op jit(solution)/shard_map/ppermute | solution.py:45
  87.6 6.4 %collective-permute-done.2.refs_2_.refs_3_ = bf16[2,128,2048]{2,1,0:T(8,128)(2,1)S(1)} collective-permute-done((bf16[2,128,2048]{2,1,0:T(8,128)(2,1)}, bf16[2,128,2048]{2,1,0:T(8,128)(2,1)S(1)}, u32[]{:S(2)}, u32[]{:S(2)}) %collective-permute-start.2) | collective-permute-done | bytes 1048608 | tf_op jit(solution)/shard_map/ppermute | solution.py:45
  93.9 4.8 collective-permute-start.15
  99.3 5.9 %collective-permute-done.6 = bf16[128,2048]{1,0:T(8,128)(2,1)S(1)} collective-permute-done((bf16[128,2048]{1,0:T(8,128)(2,1)S(1)}, bf16[128,2048]{1,0:T(8,128)(2,1)S(1)}, u32[]{:S(2)}, u32[]{:S(2)}) %collective-permute-start.6) | collective-permute-done | bytes 524320 | tf_op jit(solution)/shard_map/ppermute | solution.py:45
  107.8 9.0 %norms.1 = (bf16[1024,2048]{1,0:T(8,128)(2,1)}, bf16[1024,2048]{1,0:T(8,128)(2,1)}, bf16[1024,2048]{1,0:T(8,128)(2,1)}, f32[1024,1]{1,0:T(8,128)}, f32[1024,1]{1,0:T(8,128)}) custom-call(bf16[2,128,2048]{2,1,0:T(8,128)(2,1)} %copy-done.3, bf16[2,128,2048]{2,1,0:T(8,128)(2,1)} %collective-permute-done.refs_1_.refs_2_, bf16[2,128,2048]{2,1,0:T(8,128)(2,1)} %copy-done.15, ...), custom_call_target="tpu_custom_call" | custom-call | flops 10350000128 | bytes 1000 | tf_op jit(solution)/shard_map/norms/pallas_call | solution.py:362
  119.0 8.1 %sorted_weight.1 = bf16[8,8,32,1792]{3,2,1,0:T(8,128)(2,1)} custom-call(s32[8]{0:T(128)} %pad_add_fusion.spot_ref, bf16[8,32,1792]{2,1,0:T(8,128)(2,1)} %copy-done.5, bf16[8,32,1792]{2,1,0:T(8,128)(2,1)} %collective-permute-done.7.refs_1_, bf16[4,32,1792]{2,1,0:T(8,128)(2,1)} %collective-permute-done.9.refs_2_, ...), custom_call_target="tpu_custom_call" | custom-call | flops 6899999744 | bytes 1000 | tf_op jit(solution)/shard_map/sorted_weight/pallas_call | solution.py:446
  127.1 10.2 %hidden_part.1 = (bf16[1024,1024]{1,0:T(8,128)(2,1)}, f32[1024,1024]{1,0:T(8,128)}) custom-call(bf16[1024,2048]{1,0:T(8,128)(2,1)} %get-tuple-element.56.h_ref.h2_ref, bf16[2048,1792]{1,0:T(8,128)(2,1)} %bitcast.128, f32[1,1024]{1,0:T(1,128)} %bitcast.125), custom_call_target="tpu_custom_call" | custom-call | flops 11500000256 | bytes 1000 | tf_op jit(solution)/shard_map/hidden_part/pallas_call | solution.py:111
  138.1 10.5 %inner_grad.1 = (bf16[1024,1024]{1,0:T(8,128)(2,1)}, f32[1,1024]{1,0:T(1,128)}) custom-call(bf16[2,128,2048]{2,1,0:T(8,128)(2,1)} %copy-done.3, bf16[2,128,2048]{2,1,0:T(8,128)(2,1)} %collective-permute-done.refs_1_.refs_2_, bf16[2,128,2048]{2,1,0:T(8,128)(2,1)} %copy-done.15, bf16[2,128,2048]{2,1,0:T(8,128)(2,1)} %collective-permute-done.1.refs_3_.refs_4_, ...), custom_call_target="tpu_custom_call" | custom-call | flops 9200000000 | bytes 1000 | tf_op jit(solution)/shard_map/inner_grad/pallas_call | solution.py:267
  148.7 21.6 %inner_weight_grads.1 = (bf16[8,128,2048]{2,1,0:T(8,128)(2,1)}, bf16[8,128,2048]{2,1,0:T(8,128)(2,1)}, f32[1,256]{1,0:T(1,128)}) custom-call(s32[4]{0:T(128)} %pad_add_fusion.1.number_ref.refs_0_, bf16[1024,1024]{1,0:T(8,128)(2,1)} %get-tuple-element.57.act_ref.refs_1_, bf16[1024,2048]{1,0:T(8,128)(2,1)} %get-tuple-element.56.h_ref.h2_ref, ...), custom_call_target="tpu_custom_call" | custom-call | flops 18400000000 | bytes 1000 | tf_op jit(solution)/shard_map/inner_weight_grads/pallas_call | solution.py:507
  176.2 14.5 %attention.1 = (bf16[1024,768]{1,0:T(8,128)(2,1)}, f32[1024,128]{1,0:T(8,128)}, bf16[1024,256]{1,0:T(8,128)(2,1)}) custom-call(s32[8,3]{1,0:T(8,128)} %copy-done.8, bf16[1024,2048]{1,0:T(8,128)(2,1)} %get-tuple-element.58.refs_1_.refs_14_, bf16[2048,1792]{1,0:T(8,128)(2,1)} %bitcast.129, f32[3,1,256]{2,1,0:T(1,128)} %pad_maximum_fusion.8.refs_3_, ...), custom_call_target="tpu_custom_call" | custom-call | flops 16099999744 | bytes 1000 | tf_op jit(solution)/shard_map/attention/pallas_call | solution.py:186
  196.9 11.8 %mixed_part.1.refs_5_ = bf16[1024,2048]{1,0:T(8,128)(2,1)} custom-call(s32[8]{0:T(128)} %copy-done.33, bf16[1024,1024]{1,0:T(8,128)(2,1)} %get-tuple-element.57.act_ref.refs_1_, bf16[1024,256]{1,0:T(8,128)(2,1)} %get-tuple-element.62.refs_3_.refs_2_.refs_15_, bf16[1024,2048]{1,0:T(8,128)(2,1)} %refs_3_.1, bf16[256,2048]{1,0:T(8,128)(2,1)} %refs_9_.1, ...), custom_call_target="tpu_custom_call" | custom-call | flops 12650000384 | bytes 1000 | tf_op jit(solution)/shard_map/mixed_part/pallas_call | solution.py:228
  210.6 6.7 %added.7 = (bf16[2,128,2048]{2,1,0:T(8,128)(2,1)}, bf16[2,128,2048]{2,1,0:T(8,128)(2,1)}) custom-call(s32[4]{0:T(128)} %pad_add_fusion.1.number_ref.refs_0_, bf16[8,128,2048]{2,1,0:T(8,128)(2,1)} %get-tuple-element.63.refs_1_, bf16[8,128,2048]{2,1,0:T(8,128)(2,1)} %collective-permute-done.17.refs_2_, bf16[1,128,2048]{2,1,0:T(8,128)(2,1)} %copy-done.29, ...), custom_call_target="tpu_custom_call" | custom-call | flops 4600000000 | bytes 1000 | tf_op jit(solution)/shard_map/added/pallas_call | solution.py:666
  217.4 23.6 %attention_grads.1 = (bf16[1024,768]{1,0:T(8,128)(2,1)}, f32[1,768]{1,0:T(1,128)}, bf16[8,64,2048]{2,1,0:T(8,128)(2,1)}, bf16[8,64,2048]{2,1,0:T(8,128)(2,1)}) custom-call(s32[4]{0:T(128)} %pad_add_fusion.1.number_ref.refs_0_, bf16[2,128,2048]{2,1,0:T(8,128)(2,1)} %copy-done.3, bf16[2,128,2048]{2,1,0:T(8,128)(2,1)} %collective-permute-done.refs_1_.refs_2_, ...), custom_call_target="tpu_custom_call" | custom-call | flops 23000000512 | bytes 1000 | tf_op jit(solution)/shard_map/attention_grads/pallas_call | solution.py:600
  247.0 22.4 %collective-permute-done.21.refs_3_ = bf16[2,128,2048]{2,1,0:T(8,128)(2,1)} collective-permute-done((bf16[2,128,2048]{2,1,0:T(8,128)(2,1)}, bf16[2,128,2048]{2,1,0:T(8,128)(2,1)}, u32[]{:S(2)}, u32[]{:S(2)}) %collective-permute-start.21) | collective-permute-done | bytes 1048608 | tf_op jit(solution)/shard_map/ppermute | solution.py:45
  269.5 4.4 added.8
  278.4 4.4 added.9.refs_7_
  283.0 14.7 %back_norms.1 = (f32[4,2048]{1,0:T(4,128)}, bf16[128,2048]{1,0:T(8,128)(2,1)}, bf16[128,2048]{1,0:T(8,128)(2,1)}, bf16[128,2048]{1,0:T(8,128)(2,1)}, bf16[128,20...) custom-call(bf16[1024,768]{1,0:T(8,128)(2,1)} %get-tuple-element.70., ...), custom_call_target="tpu_custom_call" | custom-call | flops 17250000896 | bytes 1000 | tf_op jit(solution)/shard_map/back_norms/pallas_call | solution.py:312
  297.7 13.3 %collective-permute-done.42.refs_2_ = bf16[1,128,2048]{2,1,0:T(8,128)(2,1)S(1)} collective-permute-done((bf16[1,128,2048]{2,1,0:T(8,128)(2,1)}, bf16[1,128,2048]{2,1,0:T(8,128)(2,1)S(1)}, u32[]{:S(2)}, u32[]{:S(2)}) %collective-permute-start.42) | collective-permute-done | bytes 524320 | tf_op jit(solution)/shard_map/ppermute | solution.py:45
  325.3 10.3 %collective-permute-done.30.refs_3_ = bf16[4,64,2048]{2,1,0:T(8,128)(2,1)S(1)} collective-permute-done((bf16[4,64,2048]{2,1,0:T(8,128)(2,1)}, bf16[4,64,2048]{2,1,0:T(8,128)(2,1)S(1)}, u32[]{:S(2)}, u32[]{:S(2)}) %collective-permute-start.30) | collective-permute-done | bytes 1048608 | tf_op jit(solution)/shard_map/ppermute | solution.py:45
  336.6 4.6 added.10
  353.3 7.2 %small_sums.1 = bf16[16,8,24,128]{3,2,1,0:T(8,128)(2,1)} custom-call(s32[4]{0:T(128)} %pad_add_fusion.1.number_ref.refs_0_, f32[4,2048]{1,0:T(4,128)} %get-tuple-element.85.norm_ref, f32[1,768]{1,0:T(1,128)} %get-tuple-element.86.q_ref, f32[1,1024]{1,0:T(1,128)} %get-tuple-element.87.u_ref, f32[1,256]{1,0:T(1,128)} %get-tuple-element.88.y_ref), custom_call_target="tpu_custom_call" | custom-call | flops 3449999872 | bytes 1000 | tf_op jit(solution)/shard_map/small_sums/pallas_call | solution.py:754
  366.4 4.5 all-to-all-done.2
  370.8 7.8 %all-to-all-start.1 = ((bf16[128,24,128]{2,1,0:T(8,128)(2,1)}), bf16[128,24,128]{2,1,0:T(8,128)(2,1)S(1)}, u32[]{:S(2)}, u32[]{:S(2)}) async-start(bf16[128,24,128]{2,1,0:T(8,128)(2,1)} %bitcast.17), calls=%async_computation.2 | async-start | bytes 1572864 | tf_op jit(solution)/shard_map/all_to_all | solution.py:970
  388.9 5.5 %collective-permute-done.35 = bf16[64,2048]{1,0:T(8,128)(2,1)S(1)} collective-permute-done((bf16[64,2048]{1,0:T(8,128)(2,1)S(1)}, bf16[64,2048]{1,0:T(8,128)(2,1)S(1)}, u32[]{:S(2)}, u32[]{:S(2)}) %collective-permute-start.35) | collective-permute-done | bytes 262176 | tf_op jit(solution)/shard_map/ppermute | solution.py:45
  402.0 17.3 %collective-permute-done.36 = bf16[64,2048]{1,0:T(8,128)(2,1)S(1)} collective-permute-done((bf16[64,2048]{1,0:T(8,128)(2,1)S(1)}, bf16[64,2048]{1,0:T(8,128)(2,1)S(1)}, u32[]{:S(2)}, u32[]{:S(2)}) %collective-permute-start.36) | collective-permute-done | bytes 262176 | tf_op jit(solution)/shard_map/ppermute | solution.py:45
  439.9 4.0 collective-permute-start.50
  445.1 16.7 %collective-permute-done.39.refs_1_ = bf16[4,64,2048]{2,1,0:T(8,128)(2,1)} collective-permute-done((bf16[4,64,2048]{2,1,0:T(8,128)(2,1)S(1)}, bf16[4,64,2048]{2,1,0:T(8,128)(2,1)}, u32[]{:S(2)}, u32[]{:S(2)}) %collective-permute-start.39) | collective-permute-done | bytes 1048608 | tf_op jit(solution)/shard_map/ppermute | solution.py:45
  463.8 15.3 %spread.3 = (f32[1024,2048]{1,0:T(8,128)}, f32[256,8192]{1,0:T(8,128)}) custom-call(s32[16]{0:T(128)} %stack.139.spot_ref, bf16[2,128,2048]{2,1,0:T(8,128)(2,1)} %pad_maximum_fusion.2.refs_0_, bf16[2,128,2048]{2,1,0:T(8,128)(2,1)} %collective-permute-done.44.refs_1_, bf16[1,128,2048]{2,1,0:T(8,128)(2,1)} %copy-done.24, bf16[1,128,2048]{2,1,0:T(8,128)(2,1)} %copy-done.25, ...), custom_call_target="tpu_custom_call" | custom-call | flops 11500000256 | bytes 1000 | tf_op jit(solution)/shard_map/spread/pallas_call | solution.py:705
  481.2 12.0 %spread.2 = (f32[256,2048]{1,0:T(8,128)}, f32[256,6144]{1,0:T(8,128)}) custom-call(s32[16]{0:T(128)} %pad_add_fusion.2.spot_ref, bf16[4,64,2048]{2,1,0:T(8,128)(2,1)} %copy-done.4, bf16[4,64,2048]{2,1,0:T(8,128)(2,1)} %collective-permute-done.39.refs_1_, bf16[4,64,2048]{2,1,0:T(8,128)(2,1)} %copy-done.19, bf16[4,64,2048]{2,1,0:T(8,128)(2,1)} %copy-done.20), custom_call_target="tpu_custom_call" | custom-call | flops 11500000256 | bytes 1000 | tf_op jit(solution)/shard_map/spread/pallas_call | solution.py:705
  (265 shorter events, 144.7 us)
Async XLA Ops:
  8.5 25.9 %collective-permute-start.1 = (bf16[2,128,2048]{2,1,0:T(8,128)(2,1)S(1)}, bf16[2,128,2048]{2,1,0:T(8,128)(2,1)}, u32[]{:S(2)}, u32[]{:S(2)}) collective-permute-start(bf16[2,128,2048]{2,1,0:T(8,128)(2,1)S(1)} %pad_maximum_fusion.refs_0_.refs_1_), channel_id=1, source_target_pairs={{0,1},{1,2},{2,3},{3,0},{4,5},{5,6},{6,7},{7,4},{8,9},{9,10},{10,1... | collective-permute-start | bytes 3145736 | tf_op jit(solution)/shard_map/ppermute | solution.py:45
  10.6 40.6 %collective-permute-start.3 = (bf16[2,128,2048]{2,1,0:T(8,128)(2,1)S(1)}, bf16[2,128,2048]{2,1,0:T(8,128)(2,1)}, u32[]{:S(2)}, u32[]{:S(2)}) collective-permute-start(bf16[2,128,2048]{2,1,0:T(8,128)(2,1)S(1)} %pad_maximum_fusion.refs_0_.refs_1_), channel_id=1, source_target_pairs={{0,4},{1,5},{2,6},{3,7},{4,0},{5,1},{6,2},{7,3},{8,12},{9,13},{10,... | collective-permute-start | bytes 3145736 | tf_op jit(solution)/shard_map/ppermute | solution.py:45
  19.9 28.4 %all-to-all-start = ((bf16[8,40,1792]{2,1,0:T(8,128)(2,1)}), bf16[8,40,1792]{2,1,0:T(8,128)(2,1)S(1)}, u32[]{:S(2)}, u32[]{:S(2)}) async-start(bf16[8,40,1792]{2,1,0:T(8,128)(2,1)} %packed.1), calls=%async_computation | async-start | bytes 2293760 | tf_op jit(solution)/shard_map/all_to_all | solution.py:807
  23.6 469.6 %reduce-scatter.2.cloned.1.call-start = ((), (), s32[]{:S(2)}) async-start(), calls=%async_computation.5 | async-start | bytes 4718592 | tf_op jit(solution)/shard_map/reduce_scatter | solution.py:960
  34.4 35.1 %collective-permute-start.5 = (bf16[2,128,2048]{2,1,0:T(8,128)(2,1)}, bf16[2,128,2048]{2,1,0:T(8,128)(2,1)}, u32[]{:S(2)}, u32[]{:S(2)}) collective-permute-start(bf16[2,128,2048]{2,1,0:T(8,128)(2,1)} %collective-permute-done.1.refs_3_.refs_4_), channel_id=1, source_target_pairs={{0,4},{1,5},{2,6},{3,7},{4,0},{5,1},{6,2},{7,3},{8,12},{9,13},{10,... | collective-permute-start | bytes 3145736 | tf_op jit(solution)/shard_map/ppermute | solution.py:45
  36.4 42.5 %collective-permute-start = (bf16[2,128,2048]{2,1,0:T(8,128)(2,1)S(1)}, bf16[2,128,2048]{2,1,0:T(8,128)(2,1)}, u32[]{:S(2)}, u32[]{:S(2)}) collective-permute-start(bf16[2,128,2048]{2,1,0:T(8,128)(2,1)S(1)} %pad_maximum_fusion.refs_0_.refs_1_), channel_id=1, source_target_pairs={{0,3},{1,0},{2,1},{3,2},{4,7},{5,4},{6,5},{7,6},{8,11},{9,8},{10,9... | collective-permute-start | bytes 3145736 | tf_op jit(solution)/shard_map/ppermute | solution.py:45
  48.4 23.5 %collective-permute-start.8 = (bf16[8,32,1792]{2,1,0:T(8,128)(2,1)S(1)}, bf16[8,32,1792]{2,1,0:T(8,128)(2,1)}, u32[]{:S(2)}, u32[]{:S(2)}) collective-permute-start(bf16[8,32,1792]{2,1,0:T(8,128)(2,1)S(1)} %slice.165.refs_0_), channel_id=1, source_target_pairs={{0,32},{1,33},{2,34},{3,35},{4,36},{5,37},{6,38},{7,39},{8,40},{9,... | collective-permute-start | bytes 2752520 | tf_op jit(solution)/shard_map/ppermute | solution.py:45
  49.7 24.9 %collective-permute-start.7 = (bf16[8,32,1792]{2,1,0:T(8,128)(2,1)S(1)}, bf16[8,32,1792]{2,1,0:T(8,128)(2,1)}, u32[]{:S(2)}, u32[]{:S(2)}) collective-permute-start(bf16[8,32,1792]{2,1,0:T(8,128)(2,1)S(1)} %slice.165.refs_0_), channel_id=1, source_target_pairs={{0,96},{1,97},{2,98},{3,99},{4,100},{5,101},{6,102},{7,103},{8,104... | collective-permute-start | bytes 2752520 | tf_op jit(solution)/shard_map/ppermute | solution.py:45
  51.2 25.8 %collective-permute-start.4 = (bf16[2,128,2048]{2,1,0:T(8,128)(2,1)}, bf16[2,128,2048]{2,1,0:T(8,128)(2,1)S(1)}, u32[]{:S(2)}, u32[]{:S(2)}) collective-permute-start(bf16[2,128,2048]{2,1,0:T(8,128)(2,1)} %collective-permute-done.3.refs_4_.refs_5_), channel_id=1, source_target_pairs={{0,3},{1,0},{2,1},{3,2},{4,7},{5,4},{6,5},{7,6},{8,11},{9,8},{10,9... | collective-permute-start | bytes 3145736 | tf_op jit(solution)/shard_map/ppermute | solution.py:45
  69.5 24.4 %collective-permute-start.2 = (bf16[2,128,2048]{2,1,0:T(8,128)(2,1)}, bf16[2,128,2048]{2,1,0:T(8,128)(2,1)S(1)}, u32[]{:S(2)}, u32[]{:S(2)}) collective-permute-start(bf16[2,128,2048]{2,1,0:T(8,128)(2,1)} %collective-permute-done.1.refs_3_.refs_4_), channel_id=1, source_target_pairs={{0,1},{1,2},{2,3},{3,0},{4,5},{5,6},{6,7},{7,4},{8,9},{9,10},{10,1... | collective-permute-start | bytes 3145736 | tf_op jit(solution)/shard_map/ppermute | solution.py:45
  71.9 33.3 %collective-permute-start.6 = (bf16[128,2048]{1,0:T(8,128)(2,1)S(1)}, bf16[128,2048]{1,0:T(8,128)(2,1)S(1)}, u32[]{:S(2)}, u32[]{:S(2)}) collective-permute-start(bf16[128,2048]{1,0:T(8,128)(2,1)S(1)} %slice_bitcast_fusion.1), channel_id=1, source_target_pairs={{0,1},{1,2},{2,3},{3,0},{4,5},{5,6},{6,7},{7,4},{8,9},{9,10},{10,1... | collective-permute-start | bytes 1572872 | tf_op jit(solution)/shard_map/ppermute | solution.py:45
  74.6 24.1 %collective-permute-start.9 = (bf16[4,32,1792]{2,1,0:T(8,128)(2,1)S(1)}, bf16[4,32,1792]{2,1,0:T(8,128)(2,1)}, u32[]{:S(2)}, u32[]{:S(2)}) collective-permute-start(bf16[4,32,1792]{2,1,0:T(8,128)(2,1)S(1)} %slice.166), channel_id=1, source_target_pairs={{0,32},{1,33},{2,34},{3,35},{4,36},{5,37},{6,38},{7,39},{8,40},{9,... | collective-permute-start | bytes 1376264 | tf_op jit(solution)/shard_map/ppermute | solution.py:45
  78.9 37.9 %collective-permute-start.11 = (bf16[8,32,1792]{2,1,0:T(8,128)(2,1)S(1)}, bf16[8,32,1792]{2,1,0:T(8,128)(2,1)S(1)}, u32[]{:S(2)}, u32[]{:S(2)}) collective-permute-start(bf16[8,32,1792]{2,1,0:T(8,128)(2,1)S(1)} %slice.165.refs_0_), channel_id=1, source_target_pairs={{0,8},{1,9},{2,10},{3,11},{4,12},{5,13},{6,14},{7,15},{8,0},{9,1},... | collective-permute-start | bytes 2752520 | tf_op jit(solution)/shard_map/ppermute | solution.py:45
  93.9 23.8 %collective-permute-start.15 = (bf16[8,32,1792]{2,1,0:T(8,128)(2,1)}, bf16[8,32,1792]{2,1,0:T(8,128)(2,1)S(1)}, u32[]{:S(2)}, u32[]{:S(2)}) collective-permute-start(bf16[8,32,1792]{2,1,0:T(8,128)(2,1)} %collective-permute-done.8.refs_4_), channel_id=1, source_target_pairs={{0,8},{1,9},{2,10},{3,11},{4,12},{5,13},{6,14},{7,15},{8,0},{9,1},... | collective-permute-start | bytes 2752520 | tf_op jit(solution)/shard_map/ppermute | solution.py:45
  241.0 36.1 %collective-permute-start.20 = (bf16[8,64,2048]{2,1,0:T(8,128)(2,1)}, bf16[8,64,2048]{2,1,0:T(8,128)(2,1)S(1)}, u32[]{:S(2)}, u32[]{:S(2)}) collective-permute-start(bf16[8,64,2048]{2,1,0:T(8,128)(2,1)} %get-tuple-element.75.refs_5_), channel_id=1, source_target_pairs={{0,8},{1,9},{2,10},{3,11},{4,12},{5,13},{6,14},{7,15},{8,0},{9,1},... | collective-permute-start | bytes 6291464 | tf_op jit(solution)/shard_map/ppermute | solution.py:45
  243.3 26.2 %collective-permute-start.21 = (bf16[2,128,2048]{2,1,0:T(8,128)(2,1)}, bf16[2,128,2048]{2,1,0:T(8,128)(2,1)}, u32[]{:S(2)}, u32[]{:S(2)}) collective-permute-start(bf16[2,128,2048]{2,1,0:T(8,128)(2,1)} %get-tuple-element.68.refs_16_), channel_id=1, source_target_pairs={{0,32},{1,33},{2,34},{3,35},{4,36},{5,37},{6,38},{7,39},{8,40},{9,... | collective-permute-start | bytes 3145736 | tf_op jit(solution)/shard_map/ppermute | solution.py:45
  244.0 25.4 %collective-permute-start.22 = (bf16[2,128,2048]{2,1,0:T(8,128)(2,1)}, bf16[2,128,2048]{2,1,0:T(8,128)(2,1)}, u32[]{:S(2)}, u32[]{:S(2)}) collective-permute-start(bf16[2,128,2048]{2,1,0:T(8,128)(2,1)} %get-tuple-element.69.refs_17_), channel_id=1, source_target_pairs={{0,96},{1,97},{2,98},{3,99},{4,100},{5,101},{6,102},{7,103},{8,104... | collective-permute-start | bytes 3145736 | tf_op jit(solution)/shard_map/ppermute | solution.py:45
  273.9 37.2 %collective-permute-start.42 = (bf16[1,128,2048]{2,1,0:T(8,128)(2,1)}, bf16[1,128,2048]{2,1,0:T(8,128)(2,1)S(1)}, u32[]{:S(2)}, u32[]{:S(2)}) collective-permute-start(bf16[1,128,2048]{2,1,0:T(8,128)(2,1)} %get-tuple-element.76.refs_3_), channel_id=1, source_target_pairs={{0,16},{1,17},{2,18},{3,19},{4,20},{5,21},{6,22},{7,23},{8,24},{9,... | collective-permute-start | bytes 1572872 | tf_op jit(solution)/shard_map/ppermute | solution.py:45
  282.8 52.8 %collective-permute-start.30 = (bf16[4,64,2048]{2,1,0:T(8,128)(2,1)}, bf16[4,64,2048]{2,1,0:T(8,128)(2,1)S(1)}, u32[]{:S(2)}, u32[]{:S(2)}) collective-permute-start(bf16[4,64,2048]{2,1,0:T(8,128)(2,1)} %added.9.refs_7_), channel_id=1, source_target_pairs={{0,16},{1,17},{2,18},{3,19},{4,20},{5,21},{6,22},{7,23},{8,24},{9,... | collective-permute-start | bytes 3145736 | tf_op jit(solution)/shard_map/ppermute | solution.py:45
  316.6 43.9 %all-to-all-start.3 = ((bf16[8,16,1024]{2,1,0:T(8,128)(2,1)}), bf16[8,16,1024]{2,1,0:T(8,128)(2,1)S(1)}, u32[]{:S(2)}, u32[]{:S(2)}) async-start(bf16[8,16,1024]{2,1,0:T(8,128)(2,1)} %bitcast.55), calls=%async_computation.4 | async-start | bytes 524288 | tf_op jit(solution)/shard_map/all_to_all | solution.py:940
  320.0 66.2 %collective-permute-start.23 = (bf16[128,2048]{1,0:T(8,128)(2,1)}, bf16[128,2048]{1,0:T(8,128)(2,1)}, u32[]{:S(2)}, u32[]{:S(2)}) collective-permute-start(bf16[128,2048]{1,0:T(8,128)(2,1)} %get-tuple-element.79), channel_id=1, source_target_pairs={{0,3},{1,0},{2,1},{3,2},{4,7},{5,4},{6,5},{7,6},{8,11},{9,8},{10,9... | collective-permute-start | bytes 1572872 | tf_op jit(solution)/shard_map/ppermute | solution.py:45
  322.6 58.9 %collective-permute-start.26 = (bf16[128,2048]{1,0:T(8,128)(2,1)}, bf16[128,2048]{1,0:T(8,128)(2,1)}, u32[]{:S(2)}, u32[]{:S(2)}) collective-permute-start(bf16[128,2048]{1,0:T(8,128)(2,1)} %get-tuple-element.83), channel_id=1, source_target_pairs={{0,1},{1,2},{2,3},{3,0},{4,5},{5,6},{6,7},{7,4},{8,9},{9,10},{10,1... | collective-permute-start | bytes 1572872 | tf_op jit(solution)/shard_map/ppermute | solution.py:45
  322.6 75.7 %collective-permute-start.28 = (bf16[128,2048]{1,0:T(8,128)(2,1)}, bf16[128,2048]{1,0:T(8,128)(2,1)}, u32[]{:S(2)}, u32[]{:S(2)}) collective-permute-start(bf16[128,2048]{1,0:T(8,128)(2,1)} %get-tuple-element.84), channel_id=1, source_target_pairs={{0,3},{1,0},{2,1},{3,2},{4,7},{5,4},{6,5},{7,6},{8,11},{9,8},{10,9... | collective-permute-start | bytes 1572872 | tf_op jit(solution)/shard_map/ppermute | solution.py:45
  370.8 27.3 %all-to-all-start.1 = ((bf16[128,24,128]{2,1,0:T(8,128)(2,1)}), bf16[128,24,128]{2,1,0:T(8,128)(2,1)S(1)}, u32[]{:S(2)}, u32[]{:S(2)}) async-start(bf16[128,24,128]{2,1,0:T(8,128)(2,1)} %bitcast.17), calls=%async_computation.2 | async-start | bytes 1572864 | tf_op jit(solution)/shard_map/all_to_all | solution.py:970
  386.2 34.7 %collective-permute-start.45 = (bf16[2,128,2048]{2,1,0:T(8,128)(2,1)}, bf16[2,128,2048]{2,1,0:T(8,128)(2,1)}, u32[]{:S(2)}, u32[]{:S(2)}) collective-permute-start(bf16[2,128,2048]{2,1,0:T(8,128)(2,1)} %pad_maximum_fusion.2.refs_0_), channel_id=1, source_target_pairs={{0,32},{1,33},{2,34},{3,35},{4,36},{5,37},{6,38},{7,39},{8,40},{9,... | collective-permute-start | bytes 3145736 | tf_op jit(solution)/shard_map/ppermute | solution.py:45
  386.2 34.8 %collective-permute-start.44 = (bf16[2,128,2048]{2,1,0:T(8,128)(2,1)}, bf16[2,128,2048]{2,1,0:T(8,128)(2,1)}, u32[]{:S(2)}, u32[]{:S(2)}) collective-permute-start(bf16[2,128,2048]{2,1,0:T(8,128)(2,1)} %pad_maximum_fusion.2.refs_0_), channel_id=1, source_target_pairs={{0,96},{1,97},{2,98},{3,99},{4,100},{5,101},{6,102},{7,103},{8,104... | collective-permute-start | bytes 3145736 | tf_op jit(solution)/shard_map/ppermute | solution.py:45
  394.3 25.0 %collective-permute-start.36 = (bf16[64,2048]{1,0:T(8,128)(2,1)S(1)}, bf16[64,2048]{1,0:T(8,128)(2,1)S(1)}, u32[]{:S(2)}, u32[]{:S(2)}) collective-permute-start(bf16[64,2048]{1,0:T(8,128)(2,1)S(1)} %get-tuple-element.107), channel_id=1, source_target_pairs={{0,32},{1,33},{2,34},{3,35},{4,36},{5,37},{6,38},{7,39},{8,40},{9,... | collective-permute-start | bytes 786440 | tf_op jit(solution)/shard_map/ppermute | solution.py:45
  398.3 30.1 %collective-permute-start.25 = (bf16[128,2048]{1,0:T(8,128)(2,1)}, bf16[128,2048]{1,0:T(8,128)(2,1)S(1)}, u32[]{:S(2)}, u32[]{:S(2)}) collective-permute-start(bf16[128,2048]{1,0:T(8,128)(2,1)} %get-tuple-element.80), channel_id=1, source_target_pairs={{0,1},{1,2},{2,3},{3,0},{4,5},{5,6},{6,7},{7,4},{8,9},{9,10},{10,1... | collective-permute-start | bytes 1572872 | tf_op jit(solution)/shard_map/ppermute | solution.py:45
  401.2 34.6 %collective-permute-start.48 = (bf16[2,128,2048]{2,1,0:T(8,128)(2,1)}, bf16[2,128,2048]{2,1,0:T(8,128)(2,1)S(1)}, u32[]{:S(2)}, u32[]{:S(2)}) collective-permute-start(bf16[2,128,2048]{2,1,0:T(8,128)(2,1)} %pad_maximum_fusion.2.refs_0_), channel_id=1, source_target_pairs={{0,8},{1,9},{2,10},{3,11},{4,12},{5,13},{6,14},{7,15},{8,0},{9,1},... | collective-permute-start | bytes 3145736 | tf_op jit(solution)/shard_map/ppermute | solution.py:45
  435.7 27.3 %collective-permute-start.49 = (bf16[2,128,2048]{2,1,0:T(8,128)(2,1)}, bf16[2,128,2048]{2,1,0:T(8,128)(2,1)}, u32[]{:S(2)}, u32[]{:S(2)}) collective-permute-start(bf16[2,128,2048]{2,1,0:T(8,128)(2,1)} %collective-permute-done.44.refs_1_), channel_id=1, source_target_pairs={{0,8},{1,9},{2,10},{3,11},{4,12},{5,13},{6,14},{7,15},{8,0},{9,1},... | collective-permute-start | bytes 3145736 | tf_op jit(solution)/shard_map/ppermute | solution.py:45
  435.8 25.9 %collective-permute-start.39 = (bf16[4,64,2048]{2,1,0:T(8,128)(2,1)S(1)}, bf16[4,64,2048]{2,1,0:T(8,128)(2,1)}, u32[]{:S(2)}, u32[]{:S(2)}) collective-permute-start(bf16[4,64,2048]{2,1,0:T(8,128)(2,1)S(1)} %pad_maximum_fusion.1.refs_0_), channel_id=1, source_target_pairs={{0,16},{1,17},{2,18},{3,19},{4,20},{5,21},{6,22},{7,23},{8,24},{9,... | collective-permute-start | bytes 3145736 | tf_op jit(solution)/shard_map/ppermute | solution.py:45
  444.6 34.5 %collective-permute-start.40 = (bf16[4,64,2048]{2,1,0:T(8,128)(2,1)S(1)}, bf16[4,64,2048]{2,1,0:T(8,128)(2,1)S(1)}, u32[]{:S(2)}, u32[]{:S(2)}) collective-permute-start(bf16[4,64,2048]{2,1,0:T(8,128)(2,1)S(1)} %pad_maximum_fusion.1.refs_0_), channel_id=1, source_target_pairs={{0,8},{1,9},{2,10},{3,11},{4,12},{5,13},{6,14},{7,15},{8,0},{9,1},... | collective-permute-start | bytes 3145736 | tf_op jit(solution)/shard_map/ppermute | solution.py:45
  (60 other events, 931.5 us)
Sparse Core Ops, SparseCore 0:
  247.2 51.9 reduce-scatter.1

commit v3 on v2

v3 whole, which is shorter than its diff:
```python
import functools
import math

import jax
import jax.numpy as jnp
from jax import lax
from jax.experimental import pallas as pl
from jax.experimental.pallas import tpu as pltpu
from jax.sharding import PartitionSpec as P

HEADS = 8
ROT = 64
EPS = 1e-05
f32 = jnp.float32
bf16 = jnp.bfloat16


def cost(time):
    return pl.CostEstimate(flops=int(time * 1.15e9), bytes_accessed=1000, transcendentals=0)


BOTH = ("rep", "shard")
SIZES = (4, 2, 2, 2, 4)
SAME_CORE = [[2 * n + c for n in range(8)] for c in range(2)]
SAME_CORE_ALL = [[(2 * n + c) * 8 + s for n in range(8) for s in range(8)] for c in range(2)]


def coords():
    for y in range(4):
        for h in range(2):
            for c in range(2):
                for l in range(2):
                    for x in range(4):
                        yield (y, h, c, l, x)


def linear(t):
    y, h, c, l, x = (v % m for v, m in zip(t, SIZES))
    return ((y * 2 + h) * 2 + c) * 8 + l * 4 + x


def move(value, y=0, h=0, c=0, l=0, x=0):
    step = (y, h, c, l, x)
    pairs = [(linear(t), linear(tuple(a + b for a, b in zip(t, step)))) for t in coords()]
    return lax.ppermute(value, BOTH, pairs)


def pick(value, index, axis):
    return lax.dynamic_index_in_dim(value, index, axis, keepdims=False)


def ring_gather(own, axis, cut):
    below = move(own, **{axis: 1})
    above = move(own, **{axis: -1})
    far_low = move(below[:cut], **{axis: 1})
    far_high = move(above[cut:], **{axis: -1})
    return [own, above, jnp.concatenate([far_low, far_high], 0), below]


def normalize(value):
    xf = value.astype(f32)
    centre = xf - jnp.mean(xf, -1, keepdims=True)
    inverse = lax.rsqrt(jnp.mean(centre * centre, -1, keepdims=True) + EPS)
    return centre * inverse, inverse


def kernel_params():
    return pltpu.CompilerParams(vmem_limit_bytes=56 * 1024 * 1024)


def after_inputs(body, count, extra):
    return lambda *refs: body(*refs[:count], *refs[count + extra :])


def anywhere(count):
    return [pl.BlockSpec(memory_space=pl.ANY)] * count


def dot(a, b, ca=1, cb=0):
    return lax.dot_general(a, b, (((ca,), (cb,)), ((), ())), preferred_element_type=f32)


def swap_halves(value):
    lane = lax.broadcasted_iota(jnp.int32, value.shape, 1)
    return jnp.where(lane < 32, pltpu.roll(value, 96, 1), pltpu.roll(value, 32, 1))


def allowed_mask(lengths_ref, block, rows):
    e0 = lengths_ref[block, 0]
    e1 = e0 + lengths_ref[block, 1]
    t = lax.broadcasted_iota(jnp.int32, (rows, rows), 0)
    s = lax.broadcasted_iota(jnp.int32, (rows, rows), 1)
    seg_t = (t >= e0).astype(jnp.int32) + (t >= e1).astype(jnp.int32)
    seg_s = (s >= e0).astype(jnp.int32) + (s >= e1).astype(jnp.int32)
    return (seg_t == seg_s) & (s <= t)


def dot_rows(a, b):
    return lax.dot_general(a, b, (((0,), (0,)), ((), ())), preferred_element_type=f32)


def loads(copies):
    for copy in copies:
        copy.start()
    return copies


def piece_copies(pieces, half, target, sems, rows):
    return [
        pltpu.make_async_copy(
            piece.at[half] if len(piece.shape) == 3 else piece,
            target.at[pl.ds(at * rows, rows)],
            sems.at[at],
        )
        for at, piece in enumerate(pieces)
    ]


def feed_forward(x, dy, gains, weight, down, bias, numbers, first, after):
    rows, width = x[0].shape[1:]
    count = len(x)
    total = rows * count
    ff = bias.shape[1]

    def body(number_ref, g_ref, b_ref, *refs):
        x_refs, dy_refs = refs[:count], refs[count : 2 * count]
        w_hbm, d_hbm = refs[2 * count : 2 * count + 2]
        (h1_hbm, act_hbm, du_hbm, keep_hbm, send_hbm, m_ref, i_ref, db_ref, sum_ref) = refs[
            2 * count + 2 : 2 * count + 11
        ]
        (x_v, dy_v, h1_v, h2_v, w_v, d_v, act_v, du_v, keep_v, send_v, x_sem, dy_sem, sems) = refs[
            2 * count + 11 :
        ]
        own = number_ref[0] == 0
        x_copies = loads(piece_copies(x_refs, 0, x_v, x_sem, rows))
        w_copy = pltpu.make_async_copy(w_hbm.at[:, pl.ds(first, ff)], w_v, sems.at[0])
        w_copy.start()
        dy_copies = loads(piece_copies(dy_refs, 1, dy_v, dy_sem, rows))
        d_copy = pltpu.make_async_copy(d_hbm, d_v, sems.at[1])
        d_copy.start()
        for copy in x_copies:
            copy.wait()

        @pl.loop(0, count)
        def _(n):
            at = pl.ds(pl.multiple_of(n * rows, rows), rows)
            value = x_v[at, :].astype(f32)
            mean = jnp.mean(value, 1, keepdims=True)
            centre = value - mean
            inverse = lax.rsqrt(jnp.mean(centre * centre, 1, keepdims=True) + EPS)
            normed = centre * inverse
            m_ref[at, :] = mean
            i_ref[at, :] = inverse
            h1_v[at, :] = (normed * g_ref[0:1] + g_ref[1:2]).astype(bf16)
            h2_v[at, :] = (normed * g_ref[2:3] + g_ref[3:4]).astype(bf16)

        h1_copy = pltpu.make_async_copy(h1_v, h1_hbm, sems.at[2])
        h1_copy.start()
        w_copy.wait()
        for copy in dy_copies:
            copy.wait()
        d_copy.wait()
        mine = dy_v[:, pl.ds(pl.multiple_of(number_ref[1] * 256, 256), 256)]
        sum_ref[...] = jnp.sum(mine.astype(f32), 0, keepdims=True)

        def split(part, places, high, wide):
            at = (places, high, wide)

            @pl.when(own)
            def _():
                keep_v[at] = part[:, 0]
                send_v[at] = part[:, 1]

            @pl.when(jnp.logical_not(own))
            def _():
                keep_v[at] = part[:, 1]
                send_v[at] = part[:, 0]

        def leaving(n):
            at = (pl.ds(n * 2, 2), pl.ds(0, 64))
            return (
                pltpu.make_async_copy(keep_v.at[at], keep_hbm.at[at], sems.at[3]),
                pltpu.make_async_copy(send_v.at[at], send_hbm.at[at], sems.at[4]),
            )

        @pl.loop(0, ff // 256)
        def _(n):
            at = pl.ds(pl.multiple_of(n * 256, 256), 256)
            u = dot(h2_v[...], w_v[:, at]) + b_ref[:, at]
            cdf = 0.5 * (1.0 + lax.erf(u * math.sqrt(0.5)))
            pdf = jnp.exp(-0.5 * u * u) * (1.0 / math.sqrt(2.0 * math.pi))
            act = (u * cdf).astype(bf16)
            act_v[:, at] = act
            du = (dot(dy_v[...], d_v[at, :], 1, 1) * (cdf + u * pdf)).astype(bf16)
            du_v[:, at] = du
            db_ref[:, at] = jnp.sum(du.astype(f32), 0, keepdims=True)
            part = dot_rows(act, dy_v[...]).astype(bf16).reshape(2, 2, 64, width)
            split(part, pl.ds(n * 2, 2), pl.ds(0, 64), slice(None))
            for copy in leaving(n):
                copy.start()

        act_copy = pltpu.make_async_copy(act_v, act_hbm, sems.at[0])
        act_copy.start()
        du_copy = pltpu.make_async_copy(du_v, du_hbm, sems.at[1])
        du_copy.start()
        for n in range(ff // 256):
            for copy in leaving(n):
                copy.wait()

        def block(n):
            at = (
                slice(None),
                pl.ds(pl.multiple_of(64 + 16 * (n % 4), 16), 16),
                pl.ds(pl.multiple_of(n // 4 * ff, ff), ff),
            )
            return at

        def away(n):
            at = block(n)
            return (
                pltpu.make_async_copy(keep_v.at[at], keep_hbm.at[at], sems.at[3]),
                pltpu.make_async_copy(send_v.at[at], send_hbm.at[at], sems.at[4]),
            )

        @pl.loop(0, 8)
        def _(n):
            lanes = pl.ds(pl.multiple_of(n * 256, 256), 256)
            part = dot_rows(h2_v[:, lanes], du_v[...]).astype(bf16).reshape(8, 2, 16, ff)
            split(part, *block(n))
            for copy in away(n):
                copy.start()

        for n in range(8):
            for copy in away(n):
                copy.wait()
        h1_copy.wait()
        act_copy.wait()
        du_copy.wait()

    wide = jax.ShapeDtypeStruct((total, width), bf16)
    thin = jax.ShapeDtypeStruct((total, ff), bf16)
    column = jax.ShapeDtypeStruct((total, 1), f32)
    grads = jax.ShapeDtypeStruct((8, 128, width), bf16)
    vmem = pl.BlockSpec(memory_space=pltpu.VMEM)
    return pl.pallas_call(
        after_inputs(body, 5 + 2 * count, len(after)),
        out_shape=(
            wide,
            thin,
            thin,
            grads,
            grads,
            column,
            column,
            jax.ShapeDtypeStruct((1, ff), f32),
            jax.ShapeDtypeStruct((1, 256), f32),
        ),
        in_specs=[pl.BlockSpec(memory_space=pltpu.SMEM), vmem, vmem]
        + anywhere(2 * count + 2 + len(after)),
        out_specs=tuple(anywhere(5)) + (vmem,) * 4,
        scratch_shapes=[
            pltpu.VMEM((total, width), bf16),
            pltpu.VMEM((total, width), bf16),
            pltpu.VMEM((total, width), bf16),
            pltpu.VMEM((total, width), bf16),
            pltpu.VMEM((width, ff), bf16),
            pltpu.VMEM((ff, width), bf16),
            pltpu.VMEM((total, ff), bf16),
            pltpu.VMEM((total, ff), bf16),
            pltpu.VMEM((8, 128, width), bf16),
            pltpu.VMEM((8, 128, width), bf16),
            pltpu.SemaphoreType.DMA((count,)),
            pltpu.SemaphoreType.DMA((count,)),
            pltpu.SemaphoreType.DMA((5,)),
        ],
        compiler_params=kernel_params(),
        cost_estimate=cost(32),
        name="feed_forward",
    )(numbers, gains, bias, *x, *dy, weight, down, *after)


def attend(h1, dy, weight, out, bias, cosine, sine, lengths, numbers, after, rows=128):
    total, width = h1.shape
    count = len(dy)
    head = out.shape[0]
    scale = head ** (-0.5)

    def body(number_ref, len_ref, b_ref, *refs):
        dy_refs = refs[:count]
        h1_hbm, w_hbm, out_hbm, cos_hbm, sin_hbm = refs[count : count + 5]
        ol_hbm, dq_hbm, keep_hbm, send_hbm, sum_ref = refs[count + 5 : count + 10]
        (dy_v, h1_v, w_v, wo_v, cos_v, sin_v, qkv_v, do_v, ol_v, dq_v, keep_v, send_v, dy_sem, sems) = (
            refs[count + 10 :]
        )
        own = number_ref[0] == 0
        pairs = (
            (h1_hbm, h1_v),
            (w_hbm.at[:, pl.ds(0, 3 * head)], w_v),
            (out_hbm, wo_v),
            (cos_hbm, cos_v),
            (sin_hbm, sin_v),
        )
        copies = loads(
            [pltpu.make_async_copy(*pair, sems.at[n]) for n, pair in enumerate(pairs)]
        )
        dy_copies = loads(piece_copies(dy_refs, 1, dy_v, dy_sem, rows))
        copies[0].wait()
        copies[1].wait()

        @pl.loop(0, 3)
        def _(n):
            at = pl.ds(pl.multiple_of(n * head, head), head)
            qkv_v[:, at] = dot(h1_v[...], w_v[:, at]) + b_ref[n]

        for copy in copies[2:] + dy_copies:
            copy.wait()
        do_v[...] = dot(dy_v[...], wo_v[...], 1, 1).astype(bf16)
        sum_ref[...] = jnp.zeros_like(sum_ref)

        @pl.loop(0, total // rows)
        def _(block):
            at = pl.ds(pl.multiple_of(block * rows, rows), rows)
            cos, sin = cos_v[at, :], sin_v[at, :]

            def turned(value, sign):
                left = value[:, :128]
                left = left * cos + swap_halves(left) * (sin * sign)
                return jnp.concatenate([left, value[:, 128:]], 1).astype(bf16)

            q, k = turned(qkv_v[at, 0:head], 1.0), turned(qkv_v[at, head : 2 * head], 1.0)
            v = qkv_v[at, 2 * head :].astype(bf16)
            scores = dot(q, k, 1, 1) * scale
            masked = jnp.where(allowed_mask(len_ref, block, rows), scores, -1e30)
            shifted = jnp.exp(masked - jnp.max(masked, 1, keepdims=True))
            probs = shifted / jnp.sum(shifted, 1, keepdims=True)
            low = probs.astype(bf16)
            ol_v[at, :] = dot(low, v).astype(bf16)
            d_out = do_v[at, :]
            d_value = dot(low, d_out, 0, 0)
            d_probs = dot(d_out, v, 1, 1)
            centred = d_probs - jnp.sum(d_probs * probs, 1, keepdims=True)
            d_scores = (probs * centred).astype(bf16)
            d_query = turned(dot(d_scores, k) * scale, -1.0)
            d_key = turned(dot(d_scores, q, 0, 0) * scale, -1.0)
            for n, grad in enumerate((d_query, d_key, d_value.astype(bf16))):
                lanes = slice(n * head, (n + 1) * head)
                dq_v[at, lanes] = grad
                sum_ref[:, lanes] += jnp.sum(grad.astype(f32), 0, keepdims=True)

        ol_copy = pltpu.make_async_copy(ol_v, ol_hbm, sems.at[0])
        ol_copy.start()
        dq_copy = pltpu.make_async_copy(dq_v, dq_hbm, sems.at[1])
        dq_copy.start()

        def split(part, high, wide):
            at = (slice(None), high, wide)

            @pl.when(own)
            def _():
                keep_v[at] = part[:, 0]
                send_v[at] = part[:, 1]

            @pl.when(jnp.logical_not(own))
            def _():
                keep_v[at] = part[:, 1]
                send_v[at] = part[:, 0]

        part = dot_rows(ol_v[...], dy_v[...]).astype(bf16).reshape(8, 2, 16, width)
        split(part, pl.ds(48, 16), slice(None))

        @pl.loop(0, 8)
        def _(n):
            lanes = pl.ds(pl.multiple_of(n * 256, 256), 256)
            part = dot_rows(h1_v[:, lanes], dq_v[...]).astype(bf16).reshape(8, 2, 16, 3 * head)
            for third in range(3):
                split(
                    part[..., third * head : (third + 1) * head],
                    pl.ds(16 * third, 16),
                    pl.ds(pl.multiple_of(n * head, head), head),
                )

        keep_copy = pltpu.make_async_copy(keep_v, keep_hbm, sems.at[2])
        keep_copy.start()
        send_copy = pltpu.make_async_copy(send_v, send_hbm, sems.at[3])
        send_copy.start()
        for copy in (ol_copy, dq_copy, keep_copy, send_copy):
            copy.wait()

    grads = jax.ShapeDtypeStruct((8, 64, width), bf16)
    vmem = pl.BlockSpec(memory_space=pltpu.VMEM)
    smem = pl.BlockSpec(memory_space=pltpu.SMEM)
    return pl.pallas_call(
        after_inputs(body, 8 + count, len(after)),
        out_shape=(
            jax.ShapeDtypeStruct((total, head), bf16),
            jax.ShapeDtypeStruct((total, 3 * head), bf16),
            grads,
            grads,
            jax.ShapeDtypeStruct((1, 3 * head), f32),
        ),
        in_specs=[smem, smem, vmem] + anywhere(count + 5 + len(after)),
        out_specs=tuple(anywhere(4)) + (vmem,),
        scratch_shapes=[
            pltpu.VMEM((total, width), bf16),
            pltpu.VMEM((total, width), bf16),
            pltpu.VMEM((width, 3 * head), bf16),
            pltpu.VMEM((head, width), bf16),
            pltpu.VMEM((total, 128), f32),
            pltpu.VMEM((total, 128), f32),
            pltpu.VMEM((total, 3 * head), f32),
            pltpu.VMEM((total, head), bf16),
            pltpu.VMEM((total, head), bf16),
            pltpu.VMEM((total, 3 * head), bf16),
            pltpu.VMEM((8, 64, width), bf16),
            pltpu.VMEM((8, 64, width), bf16),
            pltpu.SemaphoreType.DMA((count,)),
            pltpu.SemaphoreType.DMA((5,)),
        ],
        compiler_params=kernel_params(),
        cost_estimate=cost(22),
        name="attend",
    )(numbers, lengths, bias, *dy, h1, weight, out, cosine, sine, *after)


def mixed_part(active, attended, down, out, bias, sources, after):
    rows, ff = active.shape
    head, width = out.shape
    step = 512

    def body(source_ref, act_ref, ol_ref, wd_ref, wo_ref, b_ref, mix_ref):
        total = dot(act_ref[...], wd_ref[...]) + dot(ol_ref[...], wo_ref[...]) + b_ref[...]
        total = total.astype(bf16)
        for at in range(rows // 128):
            to = pl.ds(pl.multiple_of(source_ref[at] * 128, 128), 128)
            mix_ref[to, :] = total[at * 128 : (at + 1) * 128]

    return pl.pallas_call(
        after_inputs(body, 6, len(after)),
        out_shape=jax.ShapeDtypeStruct((rows, width), bf16),
        grid_spec=pltpu.PrefetchScalarGridSpec(
            num_scalar_prefetch=1,
            grid=(width // step,),
            in_specs=[
                pl.BlockSpec((rows, ff), lambda i, n: (0, 0)),
                pl.BlockSpec((rows, head), lambda i, n: (0, 0)),
                pl.BlockSpec((ff, step), lambda i, n: (0, i)),
                pl.BlockSpec((head, step), lambda i, n: (0, i)),
                pl.BlockSpec((1, step), lambda i, n: (0, i)),
            ]
            + anywhere(len(after)),
            out_specs=pl.BlockSpec((rows, step), lambda i, n: (0, i)),
        ),
        compiler_params=kernel_params(),
        cost_estimate=cost(10),
        name="mixed_part",
    )(sources, active, attended, down, out, bias, *after)


def back_norms(d_qkv, d_hidden, weight, tokens, mean, inverse, gains, after):
    total, n1 = d_qkv.shape
    n2 = d_hidden.shape[1]
    count = len(tokens)
    width = tokens[0].shape[2]
    step = 512

    def body(dq_ref, du_ref, w_ref, m_ref, i_ref, g_ref, *refs):
        x_refs, sums_ref, outs = refs[:count], refs[count], refs[count + 1 :]
        d1 = dot(dq_ref[...], w_ref[:, :n1], 1, 1)
        d2 = dot(du_ref[...], w_ref[:, n1:], 1, 1)
        both = (d1 * g_ref[0:1] + d2 * g_ref[1:2]).astype(bf16)
        for at in range(count):
            outs[at][...] = both[at * 128 : (at + 1) * 128]
        x = jnp.concatenate([ref[0] for ref in x_refs], 0)
        normed = (x.astype(f32) - m_ref[...]) * i_ref[...]
        sums_ref[0:1] = jnp.sum(d1 * normed, 0, keepdims=True)
        sums_ref[1:2] = jnp.sum(d1, 0, keepdims=True)
        sums_ref[2:3] = jnp.sum(d2 * normed, 0, keepdims=True)
        sums_ref[3:4] = jnp.sum(d2, 0, keepdims=True)

    return pl.pallas_call(
        after_inputs(body, 6 + count, len(after)),
        out_shape=(jax.ShapeDtypeStruct((4, width), f32),)
        + (jax.ShapeDtypeStruct((128, width), bf16),) * count,
        grid=(width // step,),
        in_specs=[
            pl.BlockSpec((total, n1), lambda i: (0, 0)),
            pl.BlockSpec((total, n2), lambda i: (0, 0)),
            pl.BlockSpec((step, n1 + n2), lambda i: (i, 0)),
            pl.BlockSpec((total, 1), lambda i: (0, 0)),
            pl.BlockSpec((total, 1), lambda i: (0, 0)),
            pl.BlockSpec((2, step), lambda i: (0, i)),
        ]
        + [pl.BlockSpec((1, 128, step), lambda i: (0, 0, i))] * count
        + anywhere(len(after)),
        out_specs=(pl.BlockSpec((4, step), lambda i: (0, i)),)
        + (pl.BlockSpec((128, step), lambda i: (0, i)),) * count,
        compiler_params=kernel_params(),
        cost_estimate=cost(14),
        name="back_norms",
    )(d_qkv, d_hidden, weight, mean, inverse, gains, *tokens, *after)


def unpacked(part, after):
    owners, _, cols = part.shape

    def body(part_ref, rows_ref, info_ref):
        for owner in range(owners):
            rows_ref[owner] = part_ref[owner, 0:32]
            info_ref[owner] = part_ref[owner, 32:40].astype(f32)

    return pl.pallas_call(
        after_inputs(body, 1, len(after)),
        out_shape=(
            jax.ShapeDtypeStruct((owners, 32, cols), bf16),
            jax.ShapeDtypeStruct((owners, 8, cols), f32),
        ),
        in_specs=[pl.BlockSpec(memory_space=pltpu.VMEM)] + anywhere(len(after)),
        out_specs=(pl.BlockSpec(memory_space=pltpu.VMEM),) * 2,
        compiler_params=kernel_params(),
        cost_estimate=cost(3),
        name="unpacked",
    )(part, *after)


def halves(below, above, after):
    _, rows, cols = below.shape

    def body(below_ref, above_ref, low_ref, high_ref):
        low_ref[...] = below_ref[...]
        high_ref[...] = above_ref[...]

    out = jax.ShapeDtypeStruct((4, rows, cols), bf16)
    return pl.pallas_call(
        after_inputs(body, 2, len(after)),
        out_shape=(out, out),
        grid=(1,),
        in_specs=[
            pl.BlockSpec((4, rows, cols), lambda i: (0, 0, 0)),
            pl.BlockSpec((4, rows, cols), lambda i: (1, 0, 0)),
        ]
        + anywhere(len(after)),
        out_specs=(pl.BlockSpec((4, rows, cols), lambda i: (0, 0, 0)),) * 2,
        compiler_params=kernel_params(),
        cost_estimate=cost(3),
        name="halves",
    )(below, above, *after)


def packed_sums(inner, own, below, above, ff, head, after):
    width = inner.shape[1]

    def body(inner_ref, own_ref, below_ref, above_ref, out_ref, down_ref, stay_ref):
        total = own_ref[...].astype(f32) + below_ref[...].astype(f32) + above_ref[...].astype(f32)
        total = total.astype(bf16)
        for owner in range(8):
            pieces = [
                total[16 * third : 16 * third + 16, owner * head : (owner + 1) * head]
                for third in range(3)
            ]
            row, col = 64 + 16 * (owner % 4), owner // 4 * ff
            pieces.append(inner_ref[row : row + 16, col : col + ff])
            out_ref[owner] = jnp.concatenate(pieces, 1)
        down_ref[...] = inner_ref[0:64, :]
        stay_ref[...] = total[48:64]

    vmem = pl.BlockSpec(memory_space=pltpu.VMEM)
    return pl.pallas_call(
        after_inputs(body, 4, len(after)),
        out_shape=(
            jax.ShapeDtypeStruct((8, 16, 3 * head + ff), bf16),
            jax.ShapeDtypeStruct((64, width), bf16),
            jax.ShapeDtypeStruct((16, width), bf16),
        ),
        in_specs=[vmem] * 4 + anywhere(len(after)),
        out_specs=(vmem,) * 3,
        compiler_params=kernel_params(),
        cost_estimate=cost(3),
        name="packed_sums",
    )(inner, own, below, above, *after)


def unpacked_sums(part, down, stay, ff, head, after):
    width = down.shape[1]

    def body(part_ref, down_ref, stay_ref, inner_ref, out_ref):
        inner_ref[0:64] = down_ref[...]
        out_ref[48:64] = stay_ref[...]
        for source in range(8):
            for third in range(3):
                out_ref[16 * third : 16 * third + 16, source * head : (source + 1) * head] = part_ref[
                    source, :, third * head : (third + 1) * head
                ]
            row, col = 64 + 16 * (source % 4), source // 4 * ff
            inner_ref[row : row + 16, col : col + ff] = part_ref[source, :, 3 * head :]

    vmem = pl.BlockSpec(memory_space=pltpu.VMEM)
    return pl.pallas_call(
        after_inputs(body, 3, len(after)),
        out_shape=(
            jax.ShapeDtypeStruct((128, width), bf16),
            jax.ShapeDtypeStruct((64, width), bf16),
        ),
        in_specs=[vmem] * 3 + anywhere(len(after)),
        out_specs=(vmem,) * 2,
        compiler_params=kernel_params(),
        cost_estimate=cost(3),
        name="unpacked_sums",
    )(part, down, stay, *after)


def spread(pieces, places, core, targets):
    rows, cols = pieces[0][0].shape[1:]
    firsts, total = [], 0
    for mine, _ in pieces:
        firsts.append(total)
        total += mine.shape[0]

    def body(place_ref, core_ref, *refs):
        step = pl.program_id(0)
        outs = refs[2 * len(pieces) :]
        first_core = core_ref[0] == 0

        def fill(ref, low):
            for out_ref, (_, high, parts) in zip(outs, targets):
                for to, row, col, size in parts:
                    out_ref[low * high : (low + 1) * high, to : to + size] = ref[
                        0, row : row + high, col : col + size
                    ].astype(f32)

        for n, (first, (mine, _)) in enumerate(zip(firsts, pieces)):
            here = (step >= first) & (step < first + mine.shape[0])

            @pl.when(here & first_core)
            def _(n=n):
                fill(refs[2 * n], 0)
                fill(refs[2 * n + 1], 1)

            @pl.when(here & jnp.logical_not(first_core))
            def _(n=n):
                fill(refs[2 * n], 1)
                fill(refs[2 * n + 1], 0)

    def chosen(first, size):
        return pl.BlockSpec(
            (1, rows, cols), lambda i, place, core: (jnp.clip(i - first, 0, size - 1), 0, 0)
        )

    specs, arrays = [], []
    for first, (mine, yours) in zip(firsts, pieces):
        specs += [chosen(first, mine.shape[0])] * 2
        arrays += [mine, yours]
    return pl.pallas_call(
        body,
        out_shape=tuple(
            jax.ShapeDtypeStruct((2 * total * high, wide), f32) for wide, high, _ in targets
        ),
        grid_spec=pltpu.PrefetchScalarGridSpec(
            num_scalar_prefetch=2,
            grid=(total,),
            in_specs=specs,
            out_specs=tuple(
                pl.BlockSpec((2 * high, wide), lambda i, place, core: (place[i], 0))
                for wide, high, _ in targets
            ),
        ),
        compiler_params=kernel_params(),
        cost_estimate=cost(10),
        name="spread",
    )(places, core, *arrays)


def small_sums(norm_sums, qkv_sums, up_sums, dy_sums, numbers):
    def body(number_ref, norm_ref, q_ref, u_ref, y_ref, out_ref, work):
        shard = number_ref[1]
        for owner in range(8):
            mine = shard == owner
            for n in range(4):
                for half in range(2):
                    at = owner * 256 + half * 128
                    work[owner, n * 2 + half : n * 2 + half + 1] = norm_ref[n : n + 1, at : at + 128]
            for n in range(3):
                third, source = divmod(owner * 3 + n, 8)
                for half in range(2):
                    at = third * 256 + half * 128
                    work[owner, 8 + n * 2 + half : 9 + n * 2 + half] = jnp.where(
                        shard == source, q_ref[:, at : at + 128], 0.0
                    )
            for n in range(8):
                work[owner, 14 + n : 15 + n] = jnp.where(
                    mine, u_ref[:, n * 128 : (n + 1) * 128], 0.0
                )
            for n in range(2):
                work[owner, 22 + n : 23 + n] = jnp.where(
                    mine, y_ref[:, n * 128 : (n + 1) * 128], 0.0
                )
        out_ref[...] = work[...].astype(bf16)

    vmem = pl.BlockSpec(memory_space=pltpu.VMEM)
    return pl.pallas_call(
        body,
        out_shape=jax.ShapeDtypeStruct((8, 24, 128), bf16),
        in_specs=[pl.BlockSpec(memory_space=pltpu.SMEM)] + [vmem] * 4,
        out_specs=vmem,
        scratch_shapes=[pltpu.VMEM((8, 24, 128), f32)],
        compiler_params=kernel_params(),
        cost_estimate=cost(3),
        name="small_sums",
    )(numbers, norm_sums, qkv_sums, up_sums, dy_sums)


def packed(qkv_weight, up_weight, vectors, lengths, place, head):
    wide, up_wide = qkv_weight.shape[1], up_weight.shape[1]
    part, up_part = 3 * head, up_wide // 8
    cols = part + up_part

    def body(place_ref, len_ref, q_ref, u_ref, v_ref, out_ref):
        lane = lax.broadcasted_iota(jnp.int32, (8, cols), 1)
        row = lax.broadcasted_iota(jnp.int32, (8, cols), 0)
        sizes = jnp.zeros((8, cols), f32)
        for at in range(3):
            sizes = jnp.where(lane == at, len_ref[0, at].astype(f32), sizes)
        vector = jnp.broadcast_to(v_ref[...].astype(f32), (8, cols))
        tail = jnp.where(row == 0, vector, jnp.where(row == 1, sizes, 0.0)).astype(bf16)
        for owner in range(8):
            pieces = [
                q_ref[:, (third * 8 + owner) * head : (third * 8 + owner + 1) * head]
                for third in range(3)
            ]
            pieces.append(u_ref[:, owner * up_part : (owner + 1) * up_part])
            out_ref[owner] = jnp.concatenate([jnp.concatenate(pieces, 1), tail], 0)

    return pl.pallas_call(
        body,
        out_shape=jax.ShapeDtypeStruct((8, 40, cols), bf16),
        grid_spec=pltpu.PrefetchScalarGridSpec(
            num_scalar_prefetch=2,
            grid=(1,),
            in_specs=[
                pl.BlockSpec((32, wide), lambda i, place, lens: (place[0], 0)),
                pl.BlockSpec((32, up_wide), lambda i, place, lens: (place[0], 0)),
                pl.BlockSpec((1, cols), lambda i, place, lens: (0, 0)),
            ],
            out_specs=pl.BlockSpec((8, 40, cols), lambda i, place, lens: (0, 0, 0)),
        ),
        compiler_params=kernel_params(),
        cost_estimate=cost(3),
        name="packed",
    )(place, lengths, qkv_weight, up_weight, vectors)


def sorted_weight(pieces, spots):
    rows, cols = pieces[0][0].shape[1:]
    count = len(pieces)

    def body(spot_ref, *refs):
        step = pl.program_id(0)
        for ref, (array, first, at) in zip(refs, pieces):

            @pl.when(step == at)
            def _(ref=ref, first=first, size=array.shape[0]):
                refs[count][first : first + size, 0] = ref[...]

    return pl.pallas_call(
        body,
        out_shape=jax.ShapeDtypeStruct((8, 8, rows, cols), bf16),
        grid_spec=pltpu.PrefetchScalarGridSpec(
            num_scalar_prefetch=1,
            grid=(8,),
            in_specs=[
                pl.BlockSpec(array.shape, lambda i, spot: (0, 0, 0)) for array, _, _ in pieces
            ],
            out_specs=pl.BlockSpec((8, 1, rows, cols), lambda i, spot: (0, spot[i], 0, 0)),
        ),
        compiler_params=kernel_params(),
        cost_estimate=cost(6),
        name="sorted_weight",
    )(spots, *[piece[0] for piece in pieces]).reshape(64 * rows, cols)


def added(terms, groups, numbers, after):
    rows, cols = terms[0][0].shape[1:]
    firsts = [sum(groups[:n]) for n in range(len(groups))]

    def body(number_ref, *refs):
        step = pl.program_id(0)
        total = None
        for ref, (_, _, steps) in zip(refs, terms):
            value = ref[0].astype(f32)
            if steps is not None:
                counts = functools.reduce(jnp.logical_or, [step == at for at in steps])
                value = jnp.where(counts, value, 0.0)
            total = value if total is None else total + value
        total = total.astype(bf16)
        for ref, first, size in zip(refs[len(terms) :], firsts, groups):

            @pl.when((step >= first) & (step < first + size))
            def _(ref=ref):
                ref[0] = total

    def came(place):
        return pl.BlockSpec((1, rows, cols), lambda i, n: (place(i, n), 0, 0))

    def goes(first, size):
        return pl.BlockSpec((1, rows, cols), lambda i, n: (jnp.clip(i - first, 0, size - 1), 0, 0))

    return pl.pallas_call(
        after_inputs(body, 1 + len(terms), len(after)),
        out_shape=tuple(jax.ShapeDtypeStruct((size, rows, cols), bf16) for size in groups),
        grid_spec=pltpu.PrefetchScalarGridSpec(
            num_scalar_prefetch=1,
            grid=(sum(groups),),
            in_specs=[came(place) for _, place, _ in terms] + anywhere(len(after)),
            out_specs=tuple(goes(first, size) for first, size in zip(firsts, groups)),
        ),
        compiler_params=kernel_params(),
        cost_estimate=cost(4),
        name="added",
    )(numbers, *[term[0] for term in terms], *after)


def local(
    tokens,
    doc_lengths,
    cotangent,
    ln1_gain,
    ln1_bias,
    ln2_gain,
    ln2_bias,
    qkv_weight,
    qkv_bias,
    out_weight,
    out_bias,
    up_weight,
    up_bias,
    down_weight,
    down_bias,
):
    rows, width = tokens.shape
    head = width // HEADS
    group = 8
    rep = lax.axis_index("rep")
    shard = lax.axis_index("shard")
    y, h, c = rep // 4, (rep // 2) % 2, rep % 2
    l, x = shard // 4, shard % 4
    ff = up_bias.shape[0]

    pair = jnp.stack([tokens, cotangent])
    below, above, other = move(pair, x=1), move(pair, x=-1), move(pair, l=1)
    far, other_above, other_below = move(below, x=1), move(other, x=-1), move(below, l=1)
    x_other_far, dy_other_far = move(other_below[0], x=1), move(other_above[1], x=-1)
    pairs = (pair, above, far, below, other, other_above, None, other_below)
    x_all = tuple(x_other_far[None] if p is None else p for p in pairs)
    dy_all = tuple(dy_other_far if p is None else p for p in pairs)

    vectors = jnp.concatenate([ln1_gain, ln1_bias, ln2_gain, ln2_bias, qkv_bias])[None]
    place = (y * 2 + c).astype(jnp.int32).reshape(1)
    part = packed(qkv_weight, up_weight, vectors, doc_lengths, place, head)
    part = lax.all_to_all(part, "shard", 0, 0)
    cols = part.shape[-1]
    own, infos = unpacked(part, (pairs[1], pairs[3], pairs[4]))
    below, above = move(own, y=1), move(own, y=-1)
    low, high = halves(below, above, (pairs[2], pairs[5], pairs[7]))
    far_low, far_high = move(low, y=1), move(high, y=-1)
    mine = ((own, 0, 0), (above, 0, 1), (far_low, 0, 2), (far_high, 4, 2), (below, 0, 3))
    yours = tuple((move(array, c=1), first, spot + 4) for array, first, spot in mine)
    steps4 = (y + jnp.arange(4)) % 4
    spots = jnp.concatenate([steps4 * 2 + c, steps4 * 2 + 1 - c]).astype(jnp.int32)
    w_mixed = sorted_weight(mine + yours, spots)

    gains = infos[:, 0, :1024].reshape(8, 4, 256).transpose(1, 0, 2).reshape(4, width)
    qkv_b = infos[:, 0, 1024:].reshape(8 * 3, 1, head)
    qkv_b = jnp.stack(
        [lax.dynamic_index_in_dim(qkv_b, third * 8 + shard, 0, False) for third in range(3)]
    )
    steps8 = jnp.arange(8)
    sources = ((steps8 // 4) ^ l) * 4 + (x + steps8 % 4) % 4
    sources = sources.astype(jnp.int32)
    lengths = infos[:, 1, :3]
    lengths = jnp.sum(
        jnp.where(sources[:, None, None] == steps8[None, :, None], lengths[None], 0.0), 1
    ).astype(jnp.int32)
    ends = jnp.cumsum(lengths, 1)
    starts = ends - lengths
    steps_t = jnp.arange(rows, dtype=jnp.int32)
    segment = jnp.sum((steps_t[None, :, None] >= ends[:, None, :]).astype(jnp.int32), -1)
    slots = jnp.arange(lengths.shape[1], dtype=jnp.int32)
    begin = jnp.sum(
        jnp.where(segment[:, :, None] == slots[None, None, :], starts[:, None, :], 0), -1
    )
    position = (steps_t[None, :] - begin).astype(f32).reshape(group * rows, 1)
    lane = jnp.arange(128)
    freq = 10000.0 ** (-2.0 * (lane % (ROT // 2)).astype(f32) / ROT)
    angle = position * freq[None, :]
    cosine = jnp.where(lane < ROT, jnp.cos(angle), 1.0)
    sine = jnp.sin(angle)
    sine = jnp.where(lane < ROT // 2, -sine, jnp.where(lane < ROT, sine, 0.0))

    both_bias = (out_bias.astype(f32) + down_bias.astype(f32))[None, :]
    wide_bias = lax.dynamic_update_slice(jnp.zeros((1, width), f32), both_bias, (0, shard * 256))
    numbers = jnp.stack([c, shard, y, h]).astype(jnp.int32)

    h1, active, d_hidden, keep, send, mean, inverse, up_sums, dy_sums = feed_forward(
        x_all,
        dy_all,
        gains,
        w_mixed,
        down_weight,
        up_bias.astype(f32)[None],
        numbers,
        3 * head,
        (cosine, sine),
    )
    got = move(send, c=1)
    attended, d_qkv, a_keep, a_send, qkv_sums = attend(
        h1, dy_all, w_mixed, out_weight, qkv_b, cosine, sine, lengths, numbers, (send,)
    )

    def turn(k):
        return lambda i, n: (n[2] + k) % 4 * 2 + i % 2

    low, high = added([(keep, turn(2), None), (got, turn(2), None)], (1, 1), numbers, (attended,))
    from_low, from_high = move(low, y=1), move(high, y=-1)
    a_got = move(a_send, c=1)
    mix = mixed_part(
        active, attended, down_weight, out_weight, wide_bias, sources, (low, high)
    )

    def sides(i, n):
        return (n[2] + 1 + i // 2 * 2) % 4 * 2 + i % 2

    above, below = added(
        [
            (keep, sides, None),
            (got, sides, None),
            (from_low, lambda i, n: 0, (0,)),
            (from_high, lambda i, n: 0, (3,)),
        ],
        (2, 2),
        numbers,
        (mix,),
    )
    from_below, from_above = move(above, y=1), move(below, y=-1)
    def away(i, n):
        return i * 2 + 1 - n[3]

    (a_away,) = added([(a_keep, away, None), (a_got, away, None)], (4,), numbers, (above,))
    a_crossed = move(a_away, h=1)
    norm_sums, *sums = back_norms(
        d_qkv,
        d_hidden,
        w_mixed,
        x_all,
        mean,
        inverse,
        jnp.stack([gains[0], gains[2]]),
        (a_away,),
    )

    def ends_at(i, n):
        return n[2] * 2 + jnp.where(i == 0, 1 - n[3], n[3])

    def crosses(i, n):
        return jnp.where(i == 0, 1 - n[3], n[3])

    leaves, inner = added(
        [
            (keep, ends_at, None),
            (got, ends_at, None),
            (from_below, crosses, None),
            (from_above, crosses, None),
        ],
        (1, 1),
        numbers,
        (sums[0],),
    )
    crossed = move(leaves, h=1)

    def around(i, n):
        return (n[2] + 2 - i) % 4

    def around_here(i, n):
        return around(i, n) * 2 + n[3]

    a_far, a_above, a_own, a_below = added(
        [
            (a_keep, around_here, None),
            (a_got, around_here, None),
            (a_crossed, around, None),
        ],
        (1, 1, 1, 1),
        numbers,
        (),
    )
    a_low, a_high = move(a_far[0, :32], y=1), move(a_far[0, 32:], y=-1)
    ((inner,),) = added(
        [(inner, lambda i, n: 0, None), (crossed, lambda i, n: 0, None)],
        (1,),
        numbers,
        (a_low, a_high),
    )
    a_above = jnp.concatenate(
        [a_above[0, :32].astype(f32) + a_low.astype(f32), a_above[0, 32:].astype(f32)], 0
    )
    a_below = jnp.concatenate(
        [a_below[0, :32].astype(f32), a_below[0, 32:].astype(f32) + a_high.astype(f32)], 0
    )
    a_from_below, a_from_above = move(a_above.astype(bf16), y=1), move(a_below.astype(bf16), y=-1)

    part, down_stays, out_stays = packed_sums(
        inner, a_own[0], a_from_below, a_from_above, ff, head, ()
    )
    part = lax.all_to_all(part, "shard", 0, 0)
    inner, a_sum = unpacked_sums(part, down_stays, out_stays, ff, head, ())
    inner = jnp.stack([inner, move(inner, h=1)])

    def ring(pieces, way):
        own, above, far, below = pieces if way == 1 else (pieces[n] for n in (0, 3, 2, 1))
        passed = move(far, x=way)
        above = (above.astype(f32) + passed.astype(f32)).astype(bf16)
        return (
            own.astype(f32) + move(above, x=way).astype(f32) + move(below, x=-way).astype(f32)
        )

    sum_other = move(ring(sums[4:], 1).astype(bf16), l=1)
    own_sum = ring(sums[:4], -1) + sum_other.astype(f32)
    mixed = lax.psum_scatter(mix, "shard", scatter_dimension=0, tiled=True)
    mixed = (tokens.astype(f32) + mixed.astype(f32)).astype(bf16)
    own_normed, own_inverse = normalize(tokens)
    tokens_grad = cotangent.astype(f32) + own_inverse * (
        own_sum
        - jnp.mean(own_sum, -1, keepdims=True)
        - own_normed * jnp.mean(own_sum * own_normed, -1, keepdims=True)
    )

    smalls = small_sums(norm_sums, qkv_sums, up_sums, dy_sums, numbers)
    smalls = jnp.broadcast_to(smalls[None], (16, 8, 24, 128)).reshape(128, 24, 128)
    smalls = lax.all_to_all(smalls, BOTH, 0, 0)
    smalls = jnp.sum(smalls.astype(f32), 0)
    norm_grads = smalls[:8].reshape(4, 256)
    dy_total = smalls[22:].reshape(256)

    below, above = move(inner, y=1), move(inner, y=-1)
    far_low, far_high = move(below[:1], y=1), move(above[1:], y=-1)
    pieces = [(v, move(v, c=1)) for v in (inner, above, far_low, far_high, below)]
    order = ((0, h), (0, 1 - h), (1, h), (1, 1 - h), (2, h), (2, 1 - h), (3, h), (3, 1 - h))
    places = jnp.stack([(y + k) % 4 * 2 + high for k, high in order]).astype(jnp.int32)
    up_parts = [
        (source * ff, 64 + 16 * (source % 4), source // 4 * ff, ff) for source in range(8)
    ]
    down_grad, up_grad = spread(
        pieces,
        places,
        numbers[:1],
        [(width, 64, [(0, 0, 0, width)]), (8 * ff, 16, up_parts)],
    )

    a_sum = jnp.stack(ring_gather(a_sum, "y", 32))
    a_other = move(a_sum, h=1)
    places = jnp.concatenate([steps4 * 2 + h, steps4 * 2 + 1 - h]).astype(jnp.int32)
    out_grad, qkv_grad = spread(
        [(a_sum, move(a_sum, c=1)), (a_other, move(a_other, c=1))],
        places,
        numbers[:1],
        [
            (width, 16, [(0, 48, 0, width)]),
            (3 * width, 16, [(n * width, 16 * n, 0, width) for n in range(3)]),
        ],
    )
    return (
        mixed,
        tokens_grad,
        norm_grads[0],
        norm_grads[1],
        norm_grads[2],
        norm_grads[3],
        qkv_grad,
        smalls[8:14].reshape(768),
        out_grad,
        dy_total,
        up_grad,
        smalls[14:22].reshape(ff),
        down_grad,
        dy_total,
    )


def solution(mesh):
    rows = P(BOTH, None)
    vector, matrix = P("shard"), P("shard", None)
    return jax.shard_map(
        local,
        mesh=mesh,
        in_specs=(rows, rows, rows, vector, vector, vector, vector)
        + (matrix, vector, matrix, vector, matrix, vector, matrix, vector),
        out_specs=(rows, rows, vector, vector, vector, vector)
        + (matrix, vector, matrix, vector, matrix, vector, matrix, vector),
        check_vma=False,
    )
```

time: 513 us -> 454 us (0.88)
  Pallas kernels: 188 us -> 152 us
  starting transfers between devices: 101 us -> 89.4 us
  waiting for transfers between devices: 148 us -> 137 us
    pallas_call x10, Pallas kernels: 139 us -> 104 us  [the longest x1 34.5 us: feed_forward(): pl.pallas_call(after_inputs(body, 5 + 2 * count, len(after)), out_shape=(...]
    ppermute x53, waiting for transfers between devices: 134 us -> 111 us  [move(): return lax.ppermute(value, BOTH, pairs)]
    all_to_all x1 -> x2, waiting for transfers between devices: 8.84 us -> 26.1 us  [local(): part = lax.all_to_all(part, 'shard', 0, 0)]
    ppermute x53, starting transfers between devices: 82.3 us -> 74.2 us  [move(): return lax.ppermute(value, BOTH, pairs)]
    all_to_all x3 -> x1, starting transfers between devices: 14.6 us -> 8.17 us  [local(): smalls = lax.all_to_all(smalls, BOTH, 0, 0)]
    unnamed x78 -> x101, local copies, waits for them, and re-layouts: 14.2 us -> 18 us
  transfers between devices with their start and end apart: 58 -> 57, of which waited for: 18 -> 15; matrix products, arithmetic and copies ran while one was open for 8% -> 8% of each run, Pallas kernels for 24% -> 26%
where the time goes in v3:
time: 454 us; the launch traced here: 446 us
  Pallas kernels  152 us (33%)
  waiting for transfers between devices  137 us (30%)
  starting transfers between devices  89.4 us (20%)
  local copies, waits for them, and re-layouts  33.9 us (7%)
  other arithmetic  18.5 us (4%)
  between operations  15.2 us (3%)
    ppermute x53, waiting for transfers between devices, move(): return lax.ppermute(value, BOTH, pairs)  111 us
    ppermute x53, starting transfers between devices, move(): return lax.ppermute(value, BOTH, pairs)  74.2 us
    pallas_call x1, Pallas kernels, feed_forward(): pl.pallas_call(after_inputs(body, 5 + 2 * count, len(after)), out_shape=(...  34.5 us
    pallas_call x6, Pallas kernels, added(): pl.pallas_call(after_inputs(body, 1 + len(terms), len(after)), out_shape=...  26.4 us
    all_to_all x2, waiting for transfers between devices, local(): part = lax.all_to_all(part, 'shard', 0, 0)  26.1 us
    pallas_call x1, Pallas kernels, attend(): pl.pallas_call(after_inputs(body, 8 + count, len(after)), out_shape=(jax....  25.6 us
    pallas_call x2, Pallas kernels, spread(): pl.pallas_call(body, out_shape=tuple((jax.ShapeDtypeStruct((2 * total * h...  20.3 us
    unnamed x101, local copies, waits for them, and re-layouts  18 us
  transfers between devices with their start and end apart: 57, of which 15 were waited for; matrix products, arithmetic and copies ran while one was open for 8% of the time, Pallas kernels for 26%

profile of v3, /device:TPU:1, one launch (start us, length us, event | category | flops | bytes accessed | tf_op | source)
XLA Modules:
  0.0 446.2 jit_solution(4519581851033411354)
XLA Ops:
  18.3 3.0 packed.1
  21.4 3.6 all-to-all-start
  26.9 21.3 %all-to-all-done.refs_0_ = bf16[8,40,1792]{2,1,0:T(8,128)(2,1)S(1)} async-done(((bf16[8,40,1792]{2,1,0:T(8,128)(2,1)}), bf16[8,40,1792]{2,1,0:T(8,128)(2,1)S(1)}, u32[]{:S(2)}, u32[]{:S(2)}) %all-to-all-start) | async-done | bytes 1146912 | tf_op jit(solution)/shard_map/all_to_all | solution.py:858
  60.4 3.1 fusion.12
  63.5 9.4 %collective-permute-done.8.refs_1_ = bf16[8,32,1792]{2,1,0:T(8,128)(2,1)} collective-permute-done((bf16[8,32,1792]{2,1,0:T(8,128)(2,1)}, bf16[8,32,1792]{2,1,0:T(8,128)(2,1)}, u32[]{:S(2)}, u32[]{:S(2)}) %collective-permute-start.8) | collective-permute-done | bytes 917536 | tf_op jit(solution)/shard_map/ppermute | solution.py:45
  88.4 7.3 %collective-permute-done.10.refs_2_ = bf16[4,32,1792]{2,1,0:T(8,128)(2,1)S(1)} collective-permute-done((bf16[4,32,1792]{2,1,0:T(8,128)(2,1)}, bf16[4,32,1792]{2,1,0:T(8,128)(2,1)S(1)}, u32[]{:S(2)}, u32[]{:S(2)}) %collective-permute-start.10) | collective-permute-done | bytes 458784 | tf_op jit(solution)/shard_map/ppermute | solution.py:45
  95.6 3.3 collective-permute-start.14
  105.1 8.1 %sorted_weight.1 = bf16[8,8,32,1792]{3,2,1,0:T(8,128)(2,1)} custom-call(s32[8]{0:T(128)} %pad_add_fusion.1.spot_ref, bf16[8,32,1792]{2,1,0:T(8,128)(2,1)} %get-tuple-element.61.refs_0_, bf16[8,32,1792]{2,1,0:T(8,128)(2,1)} %collective-permute-done.8.refs_1_, bf16[4,32,1792]{2,1,0:T(8,128)(2,1)} %copy-done.39, bf16[4,32,1792]{2,1,0:T(8,128)(2,1)} %copy-done.40, ...), custom_call_target="tpu_custom_call" | custom-call | flops 6899999744 | bytes 1000 | tf_op jit(solution)/shard_map/sorted_weight/pallas_call | solution.py:763
  115.7 34.5 %feed_forward.1 = (bf16[1024,2048]{1,0:T(8,128)(2,1)}, bf16[1024,1024]{1,0:T(8,128)(2,1)}, bf16[1024,1024]{1,0:T(8,128)(2,1)}, bf16[8,128,2048]{2,1,0:T(8,128)(2...) custom-call(s32[4]{0:T(128)} %pad_add_fusion.refs_0_.number_ref, ...), custom_call_target="tpu_custom_call" | custom-call | flops 36800000000 | bytes 1000 | tf_op jit(solution)/shard_map/feed_forward/pallas_call | solution.py:245
  153.3 25.6 %attend.1 = (bf16[1024,256]{1,0:T(8,128)(2,1)}, bf16[1024,768]{1,0:T(8,128)(2,1)}, bf16[8,64,2048]{2,1,0:T(8,128)(2,1)}, bf16[8,64,2048]{2,1,0:T(8,128)(2,1)}, f32[1,768]{1,0:T(1,128)}) custom-call(s32[4]{0:T(128)} %pad_add_fusion.refs_0_.number_ref, s32[8,3]{1,0:T(8,128)} %copy-done.16, f32[3,1,256]{2,1,0:T(1,128)} %pad_maximum_fusion.6.refs_2_, ...), custom_call_target="tpu_custom_call" | custom-call | flops 25300000768 | bytes 1000 | tf_op jit(solution)/shard_map/attend/pallas_call | solution.py:392
  179.6 3.4 added.6
  185.9 10.3 %mixed_part.1.refs_5_ = bf16[1024,2048]{1,0:T(8,128)(2,1)} custom-call(s32[8]{0:T(128)} %copy-done.45, bf16[1024,1024]{1,0:T(8,128)(2,1)} %get-tuple-element.64.refs_1_, bf16[1024,256]{1,0:T(8,128)(2,1)} %get-tuple-element.67.refs_3_.refs_2_, bf16[1024,2048]{1,0:T(8,128)(2,1)} %refs_3_.1, bf16[256,2048]{1,0:T(8,128)(2,1)} %refs_4_.1, f32[1,2048]{1,0:T(1,128)} %copy-done.17, ...), custom_call_target="tpu_custom_call" | custom-call | flops 11500000256 | bytes 1000 | tf_op jit(solution)/shard_map/mixed_part/pallas_call | solution.py:437
  198.2 6.7 %added.7 = (bf16[2,128,2048]{2,1,0:T(8,128)(2,1)}, bf16[2,128,2048]{2,1,0:T(8,128)(2,1)}) custom-call(s32[4]{0:T(128)} %pad_add_fusion.refs_0_.number_ref, bf16[8,128,2048]{2,1,0:T(8,128)(2,1)} %get-tuple-element.68.refs_1_, bf16[8,128,2048]{2,1,0:T(8,128)(2,1)} %collective-permute-done.17.refs_2_, bf16[1,128,2048]{2,1,0:T(8,128)(2,1)} %copy-done.38, ...), custom_call_target="tpu_custom_call" | custom-call | flops 4600000000 | bytes 1000 | tf_op jit(solution)/shard_map/added/pallas_call | solution.py:806
  206.3 4.5 %added.8.refs_14_ = bf16[4,64,2048]{2,1,0:T(8,128)(2,1)} custom-call(s32[4]{0:T(128)} %pad_add_fusion.refs_0_.number_ref, bf16[8,64,2048]{2,1,0:T(8,128)(2,1)} %get-tuple-element.75.refs_1_, bf16[8,64,2048]{2,1,0:T(8,128)(2,1)} %copy-done.22, bf16[2,128,2048]{2,1,0:T(8,128)(2,1)} %get-tuple-element.77.refs_3_), custom_call_target="tpu_custom_call" | custom-call | flops 4600000000 | bytes 1000 | tf_op jit(solution)/shard_map/added/pallas_call | solution.py:806
  210.9 3.3 collective-permute-start.31
  216.8 13.8 %back_norms.1 = (f32[4,2048]{1,0:T(4,128)}, bf16[128,2048]{1,0:T(8,128)(2,1)}, bf16[128,2048]{1,0:T(8,128)(2,1)}, bf16[128,2048]{1,0:T(8,128)(2,1)}, bf16[128,20...) custom-call(bf16[1024,768]{1,0:T(8,128)(2,1)} %get-tuple-element.71., ...), custom_call_target="tpu_custom_call" | custom-call | flops 16099999744 | bytes 1000 | tf_op jit(solution)/shard_map/back_norms/pallas_call | solution.py:480
  230.5 42.7 %collective-permute-done.31.refs_3_ = bf16[4,64,2048]{2,1,0:T(8,128)(2,1)S(1)} collective-permute-done((bf16[4,64,2048]{2,1,0:T(8,128)(2,1)}, bf16[4,64,2048]{2,1,0:T(8,128)(2,1)S(1)}, u32[]{:S(2)}, u32[]{:S(2)}) %collective-permute-start.31) | collective-permute-done | bytes 1048608 | tf_op jit(solution)/shard_map/ppermute | solution.py:45
  274.2 4.6 %added.10 = (bf16[1,64,2048]{2,1,0:T(8,128)(2,1)}, bf16[1,64,2048]{2,1,0:T(8,128)(2,1)}, bf16[1,64,2048]{2,1,0:T(8,128)(2,1)}, bf16[1,64,2048]{2,1,0:T(8,128)(2,1)}) custom-call(s32[4]{0:T(128)} %pad_add_fusion.refs_0_.number_ref, bf16[8,64,2048]{2,1,0:T(8,128)(2,1)} %get-tuple-element.75.refs_1_, bf16[8,64,2048]{2,1,0:T(8,128)(2,1)} %copy-done.22, ...), custom_call_target="tpu_custom_call" | custom-call | flops 4600000000 | bytes 1000 | tf_op jit(solution)/shard_map/added/pallas_call | solution.py:806
  285.4 4.4 added.9
  292.9 11.3 %collective-permute-done.30.refs_2_ = bf16[1,128,2048]{2,1,0:T(8,128)(2,1)S(1)} collective-permute-done((bf16[1,128,2048]{2,1,0:T(8,128)(2,1)}, bf16[1,128,2048]{2,1,0:T(8,128)(2,1)S(1)}, u32[]{:S(2)}, u32[]{:S(2)}) %collective-permute-start.30) | collective-permute-done | bytes 524320 | tf_op jit(solution)/shard_map/ppermute | solution.py:45
  310.8 3.5 all-to-all-start.2
  317.2 4.8 %all-to-all-done.2.refs_0_ = bf16[8,16,1792]{2,1,0:T(8,128)(2,1)S(1)} async-done(((bf16[8,16,1792]{2,1,0:T(8,128)(2,1)}), bf16[8,16,1792]{2,1,0:T(8,128)(2,1)S(1)}, u32[]{:S(2)}, u32[]{:S(2)}) %all-to-all-start.2) | async-done | bytes 458784 | tf_op jit(solution)/shard_map/all_to_all | solution.py:1012
  330.9 8.2 %all-to-all-start.1 = ((bf16[128,24,128]{2,1,0:T(8,128)(2,1)}), bf16[128,24,128]{2,1,0:T(8,128)(2,1)S(1)}, u32[]{:S(2)}, u32[]{:S(2)}) async-start(bf16[128,24,128]{2,1,0:T(8,128)(2,1)} %bitcast.17), calls=%async_computation.2 | async-start | bytes 1572864 | tf_op jit(solution)/shard_map/all_to_all | solution.py:1037
  342.3 3.1 collective-permute-start.43
  349.4 4.6 %collective-permute-done.38 = bf16[32,2048]{1,0:T(8,128)(2,1)S(1)} collective-permute-done((bf16[32,2048]{1,0:T(8,128)(2,1)S(1)}, bf16[32,2048]{1,0:T(8,128)(2,1)S(1)}, u32[]{:S(2)}, u32[]{:S(2)}) %collective-permute-start.38) | collective-permute-done | bytes 131104 | tf_op jit(solution)/shard_map/ppermute | solution.py:45
  354.4 3.6 collective-permute-start.41
  358.0 6.3 %collective-permute-done.43 = bf16[128,2048]{1,0:T(8,128)(2,1)S(1)} collective-permute-done((bf16[128,2048]{1,0:T(8,128)(2,1)}, bf16[128,2048]{1,0:T(8,128)(2,1)S(1)}, u32[]{:S(2)}, u32[]{:S(2)}) %collective-permute-start.43) | collective-permute-done | bytes 524320 | tf_op jit(solution)/shard_map/ppermute | solution.py:45
  375.8 11.0 %collective-permute-done.41.refs_2_ = bf16[4,64,2048]{2,1,0:T(8,128)(2,1)} collective-permute-done((bf16[4,64,2048]{2,1,0:T(8,128)(2,1)S(1)}, bf16[4,64,2048]{2,1,0:T(8,128)(2,1)}, u32[]{:S(2)}, u32[]{:S(2)}) %collective-permute-start.41) | collective-permute-done | bytes 1048608 | tf_op jit(solution)/shard_map/ppermute | solution.py:45
  388.0 4.0 collective-permute-done.47.refs_8_
  402.0 9.3 %collective-permute-done.48.refs_4_ = bf16[1,128,2048]{2,1,0:T(8,128)(2,1)S(1)} collective-permute-done((bf16[1,128,2048]{2,1,0:T(8,128)(2,1)S(1)}, bf16[1,128,2048]{2,1,0:T(8,128)(2,1)S(1)}, u32[]{:S(2)}, u32[]{:S(2)}) %collective-permute-start.48) | collective-permute-done | bytes 524320 | tf_op jit(solution)/shard_map/ppermute | solution.py:45
  413.7 8.3 %spread.2 = (f32[256,2048]{1,0:T(8,128)}, f32[256,6144]{1,0:T(8,128)}) custom-call(s32[8]{0:T(128)} %pad_add_fusion.2.place_ref, s32[1]{0:T(128)} %bitcast.core_ref, bf16[4,64,2048]{2,1,0:T(8,128)(2,1)} %copy-done.5, bf16[4,64,2048]{2,1,0:T(8,128)(2,1)} %copy-done.23, bf16[4,64,2048]{2,1,0:T(8,128)(2,1)} %collective-permute-done.41.refs_2_, ...), custom_call_target="tpu_custom_call" | custom-call | flops 11500000256 | bytes 1000 | tf_op jit(solution)/shard_map/spread/pallas_call | solution.py:652
  423.4 12.0 %spread.3 = (f32[1024,2048]{1,0:T(8,128)}, f32[256,8192]{1,0:T(8,128)}) custom-call(s32[8]{0:T(128)} %stack.107.place_ref, s32[1]{0:T(128)} %bitcast.core_ref, bf16[2,128,2048]{2,1,0:T(8,128)(2,1)} %pad_maximum_fusion.2.refs_0_, bf16[2,128,2048]{2,1,0:T(8,128)(2,1)} %copy-done.28, bf16[2,128,2048]{2,1,0:T(8,128)(2,1)} %collective-permute-done.45.refs_2_, ...), custom_call_target="tpu_custom_call" | custom-call | flops 11500000256 | bytes 1000 | tf_op jit(solution)/shard_map/spread/pallas_call | solution.py:652
  (271 shorter events, 128.1 us)
Async XLA Ops:
  8.5 39.8 %collective-permute-start.1 = (bf16[2,128,2048]{2,1,0:T(8,128)(2,1)S(1)}, bf16[2,128,2048]{2,1,0:T(8,128)(2,1)}, u32[]{:S(2)}, u32[]{:S(2)}) collective-permute-start(bf16[2,128,2048]{2,1,0:T(8,128)(2,1)S(1)} %pad_maximum_fusion.refs_3_.refs_11_.refs_6_), channel_id=1, source_target_pairs={{0,1},{1,2},{2,3},{3,0},{4,5},{5,6},{6,7},{7,4},{8,9},{9,10},{10,1... | collective-permute-start | bytes 3145736 | tf_op jit(solution)/shard_map/ppermute | solution.py:45
  10.6 37.7 %collective-permute-start.2 = (bf16[2,128,2048]{2,1,0:T(8,128)(2,1)S(1)}, bf16[2,128,2048]{2,1,0:T(8,128)(2,1)}, u32[]{:S(2)}, u32[]{:S(2)}) collective-permute-start(bf16[2,128,2048]{2,1,0:T(8,128)(2,1)S(1)} %pad_maximum_fusion.refs_3_.refs_11_.refs_6_), channel_id=1, source_target_pairs={{0,4},{1,5},{2,6},{3,7},{4,0},{5,1},{6,2},{7,3},{8,12},{9,13},{10,... | collective-permute-start | bytes 3145736 | tf_op jit(solution)/shard_map/ppermute | solution.py:45
  12.2 36.0 %collective-permute-start = (bf16[2,128,2048]{2,1,0:T(8,128)(2,1)S(1)}, bf16[2,128,2048]{2,1,0:T(8,128)(2,1)}, u32[]{:S(2)}, u32[]{:S(2)}) collective-permute-start(bf16[2,128,2048]{2,1,0:T(8,128)(2,1)S(1)} %pad_maximum_fusion.refs_3_.refs_11_.refs_6_), channel_id=1, source_target_pairs={{0,3},{1,0},{2,1},{3,2},{4,7},{5,4},{6,5},{7,6},{8,11},{9,8},{10,9... | collective-permute-start | bytes 3145736 | tf_op jit(solution)/shard_map/ppermute | solution.py:45
  21.4 26.9 %all-to-all-start = ((bf16[8,40,1792]{2,1,0:T(8,128)(2,1)}), bf16[8,40,1792]{2,1,0:T(8,128)(2,1)S(1)}, u32[]{:S(2)}, u32[]{:S(2)}) async-start(bf16[8,40,1792]{2,1,0:T(8,128)(2,1)} %packed.1), calls=%async_computation | async-start | bytes 2293760 | tf_op jit(solution)/shard_map/all_to_all | solution.py:858
  24.9 410.5 %reduce-scatter.2.cloned.1.call-start = ((), (), s32[]{:S(2)}) async-start(), calls=%async_computation.4 | async-start | bytes 4718592 | tf_op jit(solution)/shard_map/reduce_scatter | solution.py:1026
  51.8 21.1 %collective-permute-start.8 = (bf16[8,32,1792]{2,1,0:T(8,128)(2,1)}, bf16[8,32,1792]{2,1,0:T(8,128)(2,1)}, u32[]{:S(2)}, u32[]{:S(2)}) collective-permute-start(bf16[8,32,1792]{2,1,0:T(8,128)(2,1)} %get-tuple-element.61.refs_0_), channel_id=1, source_target_pairs={{0,96},{1,97},{2,98},{3,99},{4,100},{5,101},{6,102},{7,103},{8,104... | collective-permute-start | bytes 2752520 | tf_op jit(solution)/shard_map/ppermute | solution.py:45
  54.5 21.5 %collective-permute-start.9 = (bf16[8,32,1792]{2,1,0:T(8,128)(2,1)}, bf16[8,32,1792]{2,1,0:T(8,128)(2,1)}, u32[]{:S(2)}, u32[]{:S(2)}) collective-permute-start(bf16[8,32,1792]{2,1,0:T(8,128)(2,1)} %get-tuple-element.61.refs_0_), channel_id=1, source_target_pairs={{0,32},{1,33},{2,34},{3,35},{4,36},{5,37},{6,38},{7,39},{8,40},{9,... | collective-permute-start | bytes 2752520 | tf_op jit(solution)/shard_map/ppermute | solution.py:45
  55.7 23.1 %collective-permute-start.5 = (bf16[2,128,2048]{2,1,0:T(8,128)(2,1)}, bf16[2,128,2048]{2,1,0:T(8,128)(2,1)S(1)}, u32[]{:S(2)}, u32[]{:S(2)}) collective-permute-start(bf16[2,128,2048]{2,1,0:T(8,128)(2,1)} %collective-permute-done.1.refs_2_.refs_6_.refs_14_.refs_9_), channel_id=1, source_target_pairs={{0,4},{1,5},{2,6},{3,7},{4,0},{5,1},{6,2},{7,3},{8,12},{9,13},{10,... | collective-permute-start | bytes 3145736 | tf_op jit(solution)/shard_map/ppermute | solution.py:45
  55.7 25.8 %collective-permute-start.3 = (bf16[2,128,2048]{2,1,0:T(8,128)(2,1)}, bf16[2,128,2048]{2,1,0:T(8,128)(2,1)}, u32[]{:S(2)}, u32[]{:S(2)}) collective-permute-start(bf16[2,128,2048]{2,1,0:T(8,128)(2,1)} %collective-permute-done.1.refs_2_.refs_6_.refs_14_.refs_9_), channel_id=1, source_target_pairs={{0,1},{1,2},{2,3},{3,0},{4,5},{5,6},{6,7},{7,4},{8,9},{9,10},{10,1... | collective-permute-start | bytes 3145736 | tf_op jit(solution)/shard_map/ppermute | solution.py:45
  58.1 23.4 %collective-permute-start.4 = (bf16[2,128,2048]{2,1,0:T(8,128)(2,1)}, bf16[2,128,2048]{2,1,0:T(8,128)(2,1)S(1)}, u32[]{:S(2)}, u32[]{:S(2)}) collective-permute-start(bf16[2,128,2048]{2,1,0:T(8,128)(2,1)} %collective-permute-done.2.refs_3_.refs_7_.refs_15_.refs_10_), channel_id=1, source_target_pairs={{0,3},{1,0},{2,1},{3,2},{4,7},{5,4},{6,5},{7,6},{8,11},{9,8},{10,9... | collective-permute-start | bytes 3145736 | tf_op jit(solution)/shard_map/ppermute | solution.py:45
  72.9 27.3 %collective-permute-start.12 = (bf16[8,32,1792]{2,1,0:T(8,128)(2,1)}, bf16[8,32,1792]{2,1,0:T(8,128)(2,1)S(1)}, u32[]{:S(2)}, u32[]{:S(2)}) collective-permute-start(bf16[8,32,1792]{2,1,0:T(8,128)(2,1)} %get-tuple-element.61.refs_0_), channel_id=1, source_target_pairs={{0,8},{1,9},{2,10},{3,11},{4,12},{5,13},{6,14},{7,15},{8,0},{9,1},... | collective-permute-start | bytes 2752520 | tf_op jit(solution)/shard_map/ppermute | solution.py:45
  76.0 25.4 %collective-permute-start.13 = (bf16[8,32,1792]{2,1,0:T(8,128)(2,1)}, bf16[8,32,1792]{2,1,0:T(8,128)(2,1)S(1)}, u32[]{:S(2)}, u32[]{:S(2)}) collective-permute-start(bf16[8,32,1792]{2,1,0:T(8,128)(2,1)} %collective-permute-done.8.refs_1_), channel_id=1, source_target_pairs={{0,8},{1,9},{2,10},{3,11},{4,12},{5,13},{6,14},{7,15},{8,0},{9,1},... | collective-permute-start | bytes 2752520 | tf_op jit(solution)/shard_map/ppermute | solution.py:45
  78.8 24.3 %collective-permute-start.16 = (bf16[8,32,1792]{2,1,0:T(8,128)(2,1)}, bf16[8,32,1792]{2,1,0:T(8,128)(2,1)S(1)}, u32[]{:S(2)}, u32[]{:S(2)}) collective-permute-start(bf16[8,32,1792]{2,1,0:T(8,128)(2,1)} %collective-permute-done.9.refs_0_.refs_4_), channel_id=1, source_target_pairs={{0,8},{1,9},{2,10},{3,11},{4,12},{5,13},{6,14},{7,15},{8,0},{9,1},... | collective-permute-start | bytes 2752520 | tf_op jit(solution)/shard_map/ppermute | solution.py:45
  150.2 29.4 %collective-permute-start.17 = (bf16[8,128,2048]{2,1,0:T(8,128)(2,1)}, bf16[8,128,2048]{2,1,0:T(8,128)(2,1)}, u32[]{:S(2)}, u32[]{:S(2)}) collective-permute-start(bf16[8,128,2048]{2,1,0:T(8,128)(2,1)} %get-tuple-element.66.refs_16_), channel_id=1, source_target_pairs={{0,8},{1,9},{2,10},{3,11},{4,12},{5,13},{6,14},{7,15},{8,0},{9,1},... | collective-permute-start | bytes 12582920 | tf_op jit(solution)/shard_map/ppermute | solution.py:45
  178.9 26.2 %collective-permute-start.18 = (bf16[8,64,2048]{2,1,0:T(8,128)(2,1)}, bf16[8,64,2048]{2,1,0:T(8,128)(2,1)S(1)}, u32[]{:S(2)}, u32[]{:S(2)}) collective-permute-start(bf16[8,64,2048]{2,1,0:T(8,128)(2,1)} %get-tuple-element.76), channel_id=1, source_target_pairs={{0,8},{1,9},{2,10},{3,11},{4,12},{5,13},{6,14},{7,15},{8,0},{9,1},... | collective-permute-start | bytes 6291464 | tf_op jit(solution)/shard_map/ppermute | solution.py:45
  204.9 79.2 %collective-permute-start.28 = (bf16[2,128,2048]{2,1,0:T(8,128)(2,1)}, bf16[2,128,2048]{2,1,0:T(8,128)(2,1)S(1)}, u32[]{:S(2)}, u32[]{:S(2)}) collective-permute-start(bf16[2,128,2048]{2,1,0:T(8,128)(2,1)} %get-tuple-element.77.refs_3_), channel_id=1, source_target_pairs={{0,32},{1,33},{2,34},{3,35},{4,36},{5,37},{6,38},{7,39},{8,40},{9,... | collective-permute-start | bytes 3145736 | tf_op jit(solution)/shard_map/ppermute | solution.py:45
  210.9 62.3 %collective-permute-start.31 = (bf16[4,64,2048]{2,1,0:T(8,128)(2,1)}, bf16[4,64,2048]{2,1,0:T(8,128)(2,1)S(1)}, u32[]{:S(2)}, u32[]{:S(2)}) collective-permute-start(bf16[4,64,2048]{2,1,0:T(8,128)(2,1)} %added.8.refs_14_), channel_id=1, source_target_pairs={{0,16},{1,17},{2,18},{3,19},{4,20},{5,21},{6,22},{7,23},{8,24},{9,... | collective-permute-start | bytes 3145736 | tf_op jit(solution)/shard_map/ppermute | solution.py:45
  214.2 69.9 %collective-permute-start.29 = (bf16[2,128,2048]{2,1,0:T(8,128)(2,1)S(1)}, bf16[2,128,2048]{2,1,0:T(8,128)(2,1)S(1)}, u32[]{:S(2)}, u32[]{:S(2)}) collective-permute-start(bf16[2,128,2048]{2,1,0:T(8,128)(2,1)S(1)} %copy-done.25), channel_id=1, source_target_pairs={{0,96},{1,97},{2,98},{3,99},{4,100},{5,101},{6,102},{7,103},{8,104... | collective-permute-start | bytes 3145736 | tf_op jit(solution)/shard_map/ppermute | solution.py:45
  315.7 31.3 %collective-permute-start.24 = (bf16[128,2048]{1,0:T(8,128)(2,1)}, bf16[128,2048]{1,0:T(8,128)(2,1)S(1)}, u32[]{:S(2)}, u32[]{:S(2)}) collective-permute-start(bf16[128,2048]{1,0:T(8,128)(2,1)} %get-tuple-element.84), channel_id=1, source_target_pairs={{0,1},{1,2},{2,3},{3,0},{4,5},{5,6},{6,7},{7,4},{8,9},{9,10},{10,1... | collective-permute-start | bytes 1572872 | tf_op jit(solution)/shard_map/ppermute | solution.py:45
  324.8 20.6 %collective-permute-start.36 = (bf16[64,2048]{1,0:T(8,128)(2,1)}, bf16[64,2048]{1,0:T(8,128)(2,1)S(1)}, u32[]{:S(2)}, u32[]{:S(2)}) collective-permute-start(bf16[64,2048]{1,0:T(8,128)(2,1)} %get-tuple-element.100), channel_id=1, source_target_pairs={{0,96},{1,97},{2,98},{3,99},{4,100},{5,101},{6,102},{7,103},{8,104... | collective-permute-start | bytes 786440 | tf_op jit(solution)/shard_map/ppermute | solution.py:45
  330.9 39.2 %all-to-all-start.1 = ((bf16[128,24,128]{2,1,0:T(8,128)(2,1)}), bf16[128,24,128]{2,1,0:T(8,128)(2,1)S(1)}, u32[]{:S(2)}, u32[]{:S(2)}) async-start(bf16[128,24,128]{2,1,0:T(8,128)(2,1)} %bitcast.17), calls=%async_computation.2 | async-start | bytes 1572864 | tf_op jit(solution)/shard_map/all_to_all | solution.py:1037
  339.0 27.8 %collective-permute-start.21 = (bf16[128,2048]{1,0:T(8,128)(2,1)}, bf16[128,2048]{1,0:T(8,128)(2,1)S(1)}, u32[]{:S(2)}, u32[]{:S(2)}) collective-permute-start(bf16[128,2048]{1,0:T(8,128)(2,1)} %get-tuple-element.80), channel_id=1, source_target_pairs={{0,3},{1,0},{2,1},{3,2},{4,7},{5,4},{6,5},{7,6},{8,11},{9,8},{10,9... | collective-permute-start | bytes 1572872 | tf_op jit(solution)/shard_map/ppermute | solution.py:45
  341.7 29.8 %collective-permute-start.26 = (bf16[128,2048]{1,0:T(8,128)(2,1)}, bf16[128,2048]{1,0:T(8,128)(2,1)}, u32[]{:S(2)}, u32[]{:S(2)}) collective-permute-start(bf16[128,2048]{1,0:T(8,128)(2,1)} %get-tuple-element.85), channel_id=1, source_target_pairs={{0,3},{1,0},{2,1},{3,2},{4,7},{5,4},{6,5},{7,6},{8,11},{9,8},{10,9... | collective-permute-start | bytes 1572872 | tf_op jit(solution)/shard_map/ppermute | solution.py:45
  342.3 22.0 %collective-permute-start.43 = (bf16[128,2048]{1,0:T(8,128)(2,1)}, bf16[128,2048]{1,0:T(8,128)(2,1)S(1)}, u32[]{:S(2)}, u32[]{:S(2)}) collective-permute-start(bf16[128,2048]{1,0:T(8,128)(2,1)} %get-tuple-element.103), channel_id=1, source_target_pairs={{0,16},{1,17},{2,18},{3,19},{4,20},{5,21},{6,22},{7,23},{8,24},{9,... | collective-permute-start | bytes 1572872 | tf_op jit(solution)/shard_map/ppermute | solution.py:45
  354.4 32.5 %collective-permute-start.41 = (bf16[4,64,2048]{2,1,0:T(8,128)(2,1)S(1)}, bf16[4,64,2048]{2,1,0:T(8,128)(2,1)}, u32[]{:S(2)}, u32[]{:S(2)}) collective-permute-start(bf16[4,64,2048]{2,1,0:T(8,128)(2,1)S(1)} %pad_maximum_fusion.1.refs_0_), channel_id=1, source_target_pairs={{0,16},{1,17},{2,18},{3,19},{4,20},{5,21},{6,22},{7,23},{8,24},{9,... | collective-permute-start | bytes 3145736 | tf_op jit(solution)/shard_map/ppermute | solution.py:45
  366.5 25.5 %collective-permute-start.47 = (bf16[2,128,2048]{2,1,0:T(8,128)(2,1)}, bf16[2,128,2048]{2,1,0:T(8,128)(2,1)}, u32[]{:S(2)}, u32[]{:S(2)}) collective-permute-start(bf16[2,128,2048]{2,1,0:T(8,128)(2,1)} %pad_maximum_fusion.2.refs_0_), channel_id=1, source_target_pairs={{0,32},{1,33},{2,34},{3,35},{4,36},{5,37},{6,38},{7,39},{8,40},{9,... | collective-permute-start | bytes 3145736 | tf_op jit(solution)/shard_map/ppermute | solution.py:45
  366.8 26.8 %collective-permute-start.45 = (bf16[2,128,2048]{2,1,0:T(8,128)(2,1)}, bf16[2,128,2048]{2,1,0:T(8,128)(2,1)}, u32[]{:S(2)}, u32[]{:S(2)}) collective-permute-start(bf16[2,128,2048]{2,1,0:T(8,128)(2,1)} %pad_maximum_fusion.2.refs_0_), channel_id=1, source_target_pairs={{0,96},{1,97},{2,98},{3,99},{4,100},{5,101},{6,102},{7,103},{8,104... | collective-permute-start | bytes 3145736 | tf_op jit(solution)/shard_map/ppermute | solution.py:45
  371.5 25.4 %collective-permute-start.23 = (bf16[128,2048]{1,0:T(8,128)(2,1)}, bf16[128,2048]{1,0:T(8,128)(2,1)S(1)}, u32[]{:S(2)}, u32[]{:S(2)}) collective-permute-start(bf16[128,2048]{1,0:T(8,128)(2,1)} %get-tuple-element.81), channel_id=1, source_target_pairs={{0,1},{1,2},{2,3},{3,0},{4,5},{5,6},{6,7},{7,4},{8,9},{9,10},{10,1... | collective-permute-start | bytes 1572872 | tf_op jit(solution)/shard_map/ppermute | solution.py:45
  372.7 24.3 %collective-permute-start.22 = (bf16[128,2048]{1,0:T(8,128)(2,1)}, bf16[128,2048]{1,0:T(8,128)(2,1)S(1)}, u32[]{:S(2)}, u32[]{:S(2)}) collective-permute-start(bf16[128,2048]{1,0:T(8,128)(2,1)} %add_convert_fusion.2), channel_id=1, source_target_pairs={{0,3},{1,0},{2,1},{3,2},{4,7},{5,4},{6,5},{7,6},{8,11},{9,8},{10,9... | collective-permute-start | bytes 1572872 | tf_op jit(solution)/shard_map/ppermute | solution.py:45
  393.6 19.1 %collective-permute-start.42 = (bf16[4,64,2048]{2,1,0:T(8,128)(2,1)}, bf16[4,64,2048]{2,1,0:T(8,128)(2,1)S(1)}, u32[]{:S(2)}, u32[]{:S(2)}) collective-permute-start(bf16[4,64,2048]{2,1,0:T(8,128)(2,1)} %collective-permute-done.41.refs_2_), channel_id=1, source_target_pairs={{0,8},{1,9},{2,10},{3,11},{4,12},{5,13},{6,14},{7,15},{8,0},{9,1},... | collective-permute-start | bytes 3145736 | tf_op jit(solution)/shard_map/ppermute | solution.py:45
  400.4 21.6 %collective-permute-start.44 = (bf16[2,128,2048]{2,1,0:T(8,128)(2,1)}, bf16[2,128,2048]{2,1,0:T(8,128)(2,1)S(1)}, u32[]{:S(2)}, u32[]{:S(2)}) collective-permute-start(bf16[2,128,2048]{2,1,0:T(8,128)(2,1)} %pad_maximum_fusion.2.refs_0_), channel_id=1, source_target_pairs={{0,8},{1,9},{2,10},{3,11},{4,12},{5,13},{6,14},{7,15},{8,0},{9,1},... | collective-permute-start | bytes 3145736 | tf_op jit(solution)/shard_map/ppermute | solution.py:45
  401.8 20.2 %collective-permute-start.46 = (bf16[2,128,2048]{2,1,0:T(8,128)(2,1)}, bf16[2,128,2048]{2,1,0:T(8,128)(2,1)S(1)}, u32[]{:S(2)}, u32[]{:S(2)}) collective-permute-start(bf16[2,128,2048]{2,1,0:T(8,128)(2,1)} %collective-permute-done.45.refs_2_), channel_id=1, source_target_pairs={{0,8},{1,9},{2,10},{3,11},{4,12},{5,13},{6,14},{7,15},{8,0},{9,1},... | collective-permute-start | bytes 3145736 | tf_op jit(solution)/shard_map/ppermute | solution.py:45
  (71 other events, 817.3 us)
Sparse Core Ops, SparseCore 0:
  196.3 53.8 reduce-scatter.1

commit v4 on v3

--- a/solution.py
+++ b/solution.py
@@ -47,14 +47,6 @@
 
 def pick(value, index, axis):
     return lax.dynamic_index_in_dim(value, index, axis, keepdims=False)
-
-
-def ring_gather(own, axis, cut):
-    below = move(own, **{axis: 1})
-    above = move(own, **{axis: -1})
-    far_low = move(below[:cut], **{axis: 1})
-    far_high = move(above[cut:], **{axis: -1})
-    return [own, above, jnp.concatenate([far_low, far_high], 0), below]
 
 
 def normalize(value):
@@ -116,25 +108,39 @@
     ]
 
 
-def feed_forward(x, dy, gains, weight, down, bias, numbers, first, after):
+def weight_copies(pieces, refs, spot_ref, target, lanes, sems):
+    return [
+        pltpu.make_async_copy(
+            ref.at[:, :, lanes],
+            target.at[pl.ds(first, array.shape[0]), spot_ref[spot]],
+            sems.at[at],
+        )
+        for at, (ref, (array, first, spot)) in enumerate(zip(refs, pieces))
+    ]
+
+
+def feed_forward(x, dy, gains, weight, spots, down, bias, numbers, first, after):
     rows, width = x[0].shape[1:]
     count = len(x)
     total = rows * count
     ff = bias.shape[1]
 
-    def body(number_ref, g_ref, b_ref, *refs):
-        x_refs, dy_refs = refs[:count], refs[count : 2 * count]
-        w_hbm, d_hbm = refs[2 * count : 2 * count + 2]
+    parts = len(weight)
+
+    def body(number_ref, spot_ref, g_ref, b_ref, *refs):
+        w_refs, refs = refs[:parts], refs[parts:]
+        x_refs, dy_refs, d_hbm = refs[:count], refs[count : 2 * count], refs[2 * count]
         (h1_hbm, act_hbm, du_hbm, keep_hbm, send_hbm, m_ref, i_ref, db_ref, sum_ref) = refs[
-            2 * count + 2 : 2 * count + 11
+            2 * count + 1 : 2 * count + 10
         ]
-        (x_v, dy_v, h1_v, h2_v, w_v, d_v, act_v, du_v, keep_v, send_v, x_sem, dy_sem, sems) = refs[
-            2 * count + 11 :
+        (x_v, dy_v, h1_v, h2_v, w_v, d_v, act_v, du_v, keep_v, send_v, x_sem, dy_sem, w_sem, sems) = refs[
+            2 * count + 10 :
         ]
         own = number_ref[0] == 0
         x_copies = loads(piece_copies(x_refs, 0, x_v, x_sem, rows))
-        w_copy = pltpu.make_async_copy(w_hbm.at[:, pl.ds(first, ff)], w_v, sems.at[0])
-        w_copy.start()
+        w_copies = loads(
+            weight_copies(weight, w_refs, spot_ref, w_v, pl.ds(first, ff), w_sem)
+        )
         dy_copies = loads(piece_copies(dy_refs, 1, dy_v, dy_sem, rows))
         d_copy = pltpu.make_async_copy(d_hbm, d_v, sems.at[1])
         d_copy.start()
@@ -156,8 +162,7 @@
 
         h1_copy = pltpu.make_async_copy(h1_v, h1_hbm, sems.at[2])
         h1_copy.start()
-        w_copy.wait()
-        for copy in dy_copies:
+        for copy in w_copies + dy_copies:
             copy.wait()
         d_copy.wait()
         mine = dy_v[:, pl.ds(pl.multiple_of(number_ref[1] * 256, 256), 256)]
@@ -186,7 +191,7 @@
         @pl.loop(0, ff // 256)
         def _(n):
             at = pl.ds(pl.multiple_of(n * 256, 256), 256)
-            u = dot(h2_v[...], w_v[:, at]) + b_ref[:, at]
+            u = dot(h2_v[...], w_v[:, :, :, at].reshape(width, 256)) + b_ref[:, at]
             cdf = 0.5 * (1.0 + lax.erf(u * math.sqrt(0.5)))
             pdf = jnp.exp(-0.5 * u * u) * (1.0 / math.sqrt(2.0 * math.pi))
             act = (u * cdf).astype(bf16)
@@ -243,7 +248,7 @@
     grads = jax.ShapeDtypeStruct((8, 128, width), bf16)
     vmem = pl.BlockSpec(memory_space=pltpu.VMEM)
     return pl.pallas_call(
-        after_inputs(body, 5 + 2 * count, len(after)),
+        after_inputs(body, 5 + parts + 2 * count, len(after)),
         out_shape=(
             wide,
             thin,
@@ -255,15 +260,16 @@
             jax.ShapeDtypeStruct((1, ff), f32),
             jax.ShapeDtypeStruct((1, 256), f32),
         ),
-        in_specs=[pl.BlockSpec(memory_space=pltpu.SMEM), vmem, vmem]
-        + anywhere(2 * count + 2 + len(after)),
+        in_specs=[pl.BlockSpec(memory_space=pltpu.SMEM)] * 2
+        + [vmem, vmem]
+        + anywhere(parts + 2 * count + 1 + len(after)),
         out_specs=tuple(anywhere(5)) + (vmem,) * 4,
         scratch_shapes=[
             pltpu.VMEM((total, width), bf16),
             pltpu.VMEM((total, width), bf16),
             pltpu.VMEM((total, width), bf16),
             pltpu.VMEM((total, width), bf16),
-            pltpu.VMEM((width, ff), bf16),
+            pltpu.VMEM((8, 8, width // 64, ff), bf16),
             pltpu.VMEM((ff, width), bf16),
             pltpu.VMEM((total, ff), bf16),
             pltpu.VMEM((total, ff), bf16),
@@ -271,31 +277,34 @@
             pltpu.VMEM((8, 128, width), bf16),
             pltpu.SemaphoreType.DMA((count,)),
             pltpu.SemaphoreType.DMA((count,)),
+            pltpu.SemaphoreType.DMA((parts,)),
             pltpu.SemaphoreType.DMA((5,)),
         ],
         compiler_params=kernel_params(),
         cost_estimate=cost(32),
         name="feed_forward",
-    )(numbers, gains, bias, *x, *dy, weight, down, *after)
-
-
-def attend(h1, dy, weight, out, bias, cosine, sine, lengths, numbers, after, rows=128):
+    )(numbers, spots, gains, bias, *[p[0] for p in weight], *x, *dy, down, *after)
+
+
+def attend(h1, dy, weight, spots, out, bias, cosine, sine, lengths, numbers, after, rows=128):
     total, width = h1.shape
     count = len(dy)
     head = out.shape[0]
     scale = head ** (-0.5)
 
-    def body(number_ref, len_ref, b_ref, *refs):
+    parts = len(weight)
+
+    def body(number_ref, len_ref, spot_ref, b_ref, *refs):
+        w_refs, refs = refs[:parts], refs[parts:]
         dy_refs = refs[:count]
-        h1_hbm, w_hbm, out_hbm, cos_hbm, sin_hbm = refs[count : count + 5]
-        ol_hbm, dq_hbm, keep_hbm, send_hbm, sum_ref = refs[count + 5 : count + 10]
-        (dy_v, h1_v, w_v, wo_v, cos_v, sin_v, qkv_v, do_v, ol_v, dq_v, keep_v, send_v, dy_sem, sems) = (
-            refs[count + 10 :]
+        h1_hbm, out_hbm, cos_hbm, sin_hbm = refs[count : count + 4]
+        ol_hbm, dq_hbm, keep_hbm, send_hbm, sum_ref = refs[count + 4 : count + 9]
+        (dy_v, h1_v, w_v, wo_v, cos_v, sin_v, qkv_v, do_v, ol_v, dq_v, keep_v, send_v, dy_sem, w_sem, sems) = (
+            refs[count + 9 :]
         )
         own = number_ref[0] == 0
         pairs = (
             (h1_hbm, h1_v),
-            (w_hbm.at[:, pl.ds(0, 3 * head)], w_v),
             (out_hbm, wo_v),
             (cos_hbm, cos_v),
             (sin_hbm, sin_v),
@@ -303,16 +312,19 @@
         copies = loads(
             [pltpu.make_async_copy(*pair, sems.at[n]) for n, pair in enumerate(pairs)]
         )
+        w_copies = loads(
+            weight_copies(weight, w_refs, spot_ref, w_v, pl.ds(0, 3 * head), w_sem)
+        )
         dy_copies = loads(piece_copies(dy_refs, 1, dy_v, dy_sem, rows))
-        copies[0].wait()
-        copies[1].wait()
+        for copy in copies[:1] + w_copies:
+            copy.wait()
 
         @pl.loop(0, 3)
         def _(n):
             at = pl.ds(pl.multiple_of(n * head, head), head)
-            qkv_v[:, at] = dot(h1_v[...], w_v[:, at]) + b_ref[n]
-
-        for copy in copies[2:] + dy_copies:
+            qkv_v[:, at] = dot(h1_v[...], w_v[:, :, :, at].reshape(width, head)) + b_ref[n]
+
+        for copy in copies[1:] + dy_copies:
             copy.wait()
         do_v[...] = dot(dy_v[...], wo_v[...], 1, 1).astype(bf16)
         sum_ref[...] = jnp.zeros_like(sum_ref)
@@ -390,7 +402,7 @@
     vmem = pl.BlockSpec(memory_space=pltpu.VMEM)
     smem = pl.BlockSpec(memory_space=pltpu.SMEM)
     return pl.pallas_call(
-        after_inputs(body, 8 + count, len(after)),
+        after_inputs(body, 8 + parts + count, len(after)),
         out_shape=(
             jax.ShapeDtypeStruct((total, head), bf16),
             jax.ShapeDtypeStruct((total, 3 * head), bf16),
@@ -398,12 +410,12 @@
             grads,
             jax.ShapeDtypeStruct((1, 3 * head), f32),
         ),
-        in_specs=[smem, smem, vmem] + anywhere(count + 5 + len(after)),
+        in_specs=[smem, smem, smem, vmem] + anywhere(parts + count + 4 + len(after)),
         out_specs=tuple(anywhere(4)) + (vmem,),
         scratch_shapes=[
             pltpu.VMEM((total, width), bf16),
             pltpu.VMEM((total, width), bf16),
-            pltpu.VMEM((width, 3 * head), bf16),
+            pltpu.VMEM((8, 8, width // 64, 3 * head), bf16),
             pltpu.VMEM((head, width), bf16),
             pltpu.VMEM((total, 128), f32),
             pltpu.VMEM((total, 128), f32),
@@ -414,12 +426,25 @@
             pltpu.VMEM((8, 64, width), bf16),
             pltpu.VMEM((8, 64, width), bf16),
             pltpu.SemaphoreType.DMA((count,)),
-            pltpu.SemaphoreType.DMA((5,)),
+            pltpu.SemaphoreType.DMA((parts,)),
+            pltpu.SemaphoreType.DMA((4,)),
         ],
         compiler_params=kernel_params(),
         cost_estimate=cost(22),
         name="attend",
-    )(numbers, lengths, bias, *dy, h1, weight, out, cosine, sine, *after)
+    )(
+        numbers,
+        lengths,
+        spots,
+        bias,
+        *[p[0] for p in weight],
+        *dy,
+        h1,
+        out,
+        cosine,
+        sine,
+        *after,
+    )
 
 
 def mixed_part(active, attended, down, out, bias, sources, after):
@@ -456,48 +481,133 @@
     )(sources, active, attended, down, out, bias, *after)
 
 
-def back_norms(d_qkv, d_hidden, weight, tokens, mean, inverse, gains, after):
+def packed(qkv_weight, up_weight, vectors, lengths, place, head, tokens, cotangent):
+    wide, up_wide = qkv_weight.shape[1], up_weight.shape[1]
+    part, up_part = 3 * head, up_wide // 8
+    cols = part + up_part
+
+    def body(place_ref, len_ref, q_ref, u_ref, x_ref, dy_ref, *refs):
+        v_refs, out_ref, pair_ref = refs[: len(vectors)], refs[-2], refs[-1]
+        pair_ref[0] = x_ref[...]
+        pair_ref[1] = dy_ref[...]
+        lane = lax.broadcasted_iota(jnp.int32, (8, cols), 1)
+        row = lax.broadcasted_iota(jnp.int32, (8, cols), 0)
+        sizes = jnp.zeros((8, cols), f32)
+        for at in range(3):
+            sizes = jnp.where(lane == at, len_ref[0, at].astype(f32), sizes)
+        vector = jnp.concatenate([ref[...].astype(f32) for ref in v_refs], 1)
+        vector = jnp.broadcast_to(vector, (8, cols))
+        tail = jnp.where(row == 0, vector, jnp.where(row == 1, sizes, 0.0)).astype(bf16)
+        for owner in range(8):
+            pieces = [
+                q_ref[:, (third * 8 + owner) * head : (third * 8 + owner + 1) * head]
+                for third in range(3)
+            ]
+            pieces.append(u_ref[:, owner * up_part : (owner + 1) * up_part])
+            out_ref[owner] = jnp.concatenate([jnp.concatenate(pieces, 1), tail], 0)
+
+    return pl.pallas_call(
+        body,
+        out_shape=(
+            jax.ShapeDtypeStruct((8, 40, cols), bf16),
+            jax.ShapeDtypeStruct((2,) + tokens.shape, bf16),
+        ),
+        grid_spec=pltpu.PrefetchScalarGridSpec(
+            num_scalar_prefetch=2,
+            grid=(1,),
+            in_specs=[
+                pl.BlockSpec((32, wide), lambda i, place, lens: (place[0], 0)),
+                pl.BlockSpec((32, up_wide), lambda i, place, lens: (place[0], 0)),
+                pl.BlockSpec(tokens.shape, lambda i, place, lens: (0, 0)),
+                pl.BlockSpec(tokens.shape, lambda i, place, lens: (0, 0)),
+            ]
+            + [pl.BlockSpec(v.shape, lambda i, place, lens: (0, 0)) for v in vectors],
+            out_specs=(
+                pl.BlockSpec((8, 40, cols), lambda i, place, lens: (0, 0, 0)),
+                pl.BlockSpec((2,) + tokens.shape, lambda i, place, lens: (0, 0, 0)),
+            ),
+        ),
+        compiler_params=kernel_params(),
+        cost_estimate=cost(3),
+        name="packed",
+    )(place, lengths, qkv_weight, up_weight, tokens, cotangent, *vectors)
+
+
+def back_norms(d_qkv, d_hidden, weight, spots, tokens, mean, inverse, gains, after):
     total, n1 = d_qkv.shape
     n2 = d_hidden.shape[1]
     count = len(tokens)
-    width = tokens[0].shape[2]
+    parts = len(weight)
+    width = tokens[0].shape[-1]
     step = 512
 
-    def body(dq_ref, du_ref, w_ref, m_ref, i_ref, g_ref, *refs):
-        x_refs, sums_ref, outs = refs[:count], refs[count], refs[count + 1 :]
-        d1 = dot(dq_ref[...], w_ref[:, :n1], 1, 1)
-        d2 = dot(du_ref[...], w_ref[:, n1:], 1, 1)
-        both = (d1 * g_ref[0:1] + d2 * g_ref[1:2]).astype(bf16)
-        for at in range(count):
-            outs[at][...] = both[at * 128 : (at + 1) * 128]
-        x = jnp.concatenate([ref[0] for ref in x_refs], 0)
-        normed = (x.astype(f32) - m_ref[...]) * i_ref[...]
-        sums_ref[0:1] = jnp.sum(d1 * normed, 0, keepdims=True)
-        sums_ref[1:2] = jnp.sum(d1, 0, keepdims=True)
-        sums_ref[2:3] = jnp.sum(d2 * normed, 0, keepdims=True)
-        sums_ref[3:4] = jnp.sum(d2, 0, keepdims=True)
-
+    def body(spot_ref, m_ref, i_ref, g_ref, *refs):
+        w_refs, x_refs = refs[:parts], refs[parts : parts + count]
+        dq_hbm, du_hbm = refs[parts + count : parts + count + 2]
+        sums_ref = refs[parts + count + 2]
+        outs = refs[parts + count + 3 : parts + 2 * count + 3]
+        dq_v, du_v, w_v, x_v, s_v, w_sem, x_sem, sems = refs[parts + 2 * count + 3 :]
+        copies = loads(
+            [
+                pltpu.make_async_copy(dq_hbm, dq_v, sems.at[0]),
+                pltpu.make_async_copy(du_hbm, du_v, sems.at[1]),
+            ]
+            + weight_copies(weight, w_refs, spot_ref, w_v, slice(None), w_sem)
+            + piece_copies(x_refs, 0, x_v, x_sem, 128)
+        )
+        for copy in copies:
+            copy.wait()
+
+        def leaving(n):
+            lanes = pl.ds(pl.multiple_of(n * step, step), step)
+            return [
+                pltpu.make_async_copy(
+                    s_v.at[pl.ds(at * 128, 128), lanes], outs[at].at[:, lanes], x_sem.at[at]
+                )
+                for at in range(count)
+            ]
+
+        @pl.loop(0, width // step)
+        def _(n):
+            lanes = pl.ds(pl.multiple_of(n * step, step), step)
+            sources = pl.ds(n * (step // 256), step // 256)
+            d1 = dot(dq_v[...], w_v[sources, :, :, 0:n1].reshape(step, n1), 1, 1)
+            d2 = dot(du_v[...], w_v[sources, :, :, n1:].reshape(step, n2), 1, 1)
+            s_v[:, lanes] = (d1 * g_ref[0:1, lanes] + d2 * g_ref[1:2, lanes]).astype(bf16)
+            for copy in leaving(n):
+                copy.start()
+            normed = (x_v[:, lanes].astype(f32) - m_ref[...]) * i_ref[...]
+            sums_ref[0:1, lanes] = jnp.sum(d1 * normed, 0, keepdims=True)
+            sums_ref[1:2, lanes] = jnp.sum(d1, 0, keepdims=True)
+            sums_ref[2:3, lanes] = jnp.sum(d2 * normed, 0, keepdims=True)
+            sums_ref[3:4, lanes] = jnp.sum(d2, 0, keepdims=True)
+
+        for n in range(width // step):
+            for copy in leaving(n):
+                copy.wait()
+
+    vmem = pl.BlockSpec(memory_space=pltpu.VMEM)
     return pl.pallas_call(
-        after_inputs(body, 6 + count, len(after)),
+        after_inputs(body, 6 + parts + count, len(after)),
         out_shape=(jax.ShapeDtypeStruct((4, width), f32),)
         + (jax.ShapeDtypeStruct((128, width), bf16),) * count,
-        grid=(width // step,),
-        in_specs=[
-            pl.BlockSpec((total, n1), lambda i: (0, 0)),
-            pl.BlockSpec((total, n2), lambda i: (0, 0)),
-            pl.BlockSpec((step, n1 + n2), lambda i: (i, 0)),
-            pl.BlockSpec((total, 1), lambda i: (0, 0)),
-            pl.BlockSpec((total, 1), lambda i: (0, 0)),
-            pl.BlockSpec((2, step), lambda i: (0, i)),
-        ]
-        + [pl.BlockSpec((1, 128, step), lambda i: (0, 0, i))] * count
-        + anywhere(len(after)),
-        out_specs=(pl.BlockSpec((4, step), lambda i: (0, i)),)
-        + (pl.BlockSpec((128, step), lambda i: (0, i)),) * count,
+        in_specs=[pl.BlockSpec(memory_space=pltpu.SMEM), vmem, vmem, vmem]
+        + anywhere(parts + count + 2 + len(after)),
+        out_specs=(vmem,) + tuple(anywhere(count)),
+        scratch_shapes=[
+            pltpu.VMEM((total, n1), bf16),
+            pltpu.VMEM((total, n2), bf16),
+            pltpu.VMEM((8, 8, width // 64, n1 + n2), bf16),
+            pltpu.VMEM((total, width), bf16),
+            pltpu.VMEM((total, width), bf16),
+            pltpu.SemaphoreType.DMA((parts,)),
+            pltpu.SemaphoreType.DMA((count,)),
+            pltpu.SemaphoreType.DMA((2,)),
+        ],
         compiler_params=kernel_params(),
         cost_estimate=cost(14),
         name="back_norms",
-    )(d_qkv, d_hidden, weight, mean, inverse, gains, *tokens, *after)
+    )(spots, mean, inverse, gains, *[p[0] for p in weight], *tokens, d_qkv, d_hidden, *after)
 
 
 def unpacked(part, after):
@@ -523,23 +633,25 @@
 
 
 def halves(below, above, after):
-    _, rows, cols = below.shape
+    count, rows, cols = below.shape
+    half = (count // 2, rows, cols) if count > 1 else (1, rows // 2, cols)
+    at = (1, 0, 0) if count > 1 else (0, 1, 0)
 
     def body(below_ref, above_ref, low_ref, high_ref):
         low_ref[...] = below_ref[...]
         high_ref[...] = above_ref[...]
 
-    out = jax.ShapeDtypeStruct((4, rows, cols), bf16)
+    out = jax.ShapeDtypeStruct(half, bf16)
     return pl.pallas_call(
         after_inputs(body, 2, len(after)),
         out_shape=(out, out),
         grid=(1,),
         in_specs=[
-            pl.BlockSpec((4, rows, cols), lambda i: (0, 0, 0)),
-            pl.BlockSpec((4, rows, cols), lambda i: (1, 0, 0)),
+            pl.BlockSpec(half, lambda i: (0, 0, 0)),
+            pl.BlockSpec(half, lambda i: at),
         ]
         + anywhere(len(after)),
-        out_specs=(pl.BlockSpec((4, rows, cols), lambda i: (0, 0, 0)),) * 2,
+        out_specs=(pl.BlockSpec(half, lambda i: (0, 0, 0)),) * 2,
         compiler_params=kernel_params(),
         cost_estimate=cost(3),
         name="halves",
@@ -608,7 +720,7 @@
     )(part, down, stay, *after)
 
 
-def spread(pieces, places, core, targets):
+def spread(pieces, places, core, targets, count, before, after):
     rows, cols = pieces[0][0].shape[1:]
     firsts, total = [], 0
     for mine, _ in pieces:
@@ -617,7 +729,7 @@
 
     def body(place_ref, core_ref, *refs):
         step = pl.program_id(0)
-        outs = refs[2 * len(pieces) :]
+        outs = refs[2 * len(pieces) + len(before) :]
         first_core = core_ref[0] == 0
 
         def fill(ref, low):
@@ -650,23 +762,24 @@
         specs += [chosen(first, mine.shape[0])] * 2
         arrays += [mine, yours]
     return pl.pallas_call(
-        body,
+        after_inputs(body, 2 + 2 * len(pieces) + len(before), len(after)),
         out_shape=tuple(
-            jax.ShapeDtypeStruct((2 * total * high, wide), f32) for wide, high, _ in targets
+            jax.ShapeDtypeStruct((2 * count * high, wide), f32) for wide, high, _ in targets
         ),
         grid_spec=pltpu.PrefetchScalarGridSpec(
             num_scalar_prefetch=2,
             grid=(total,),
-            in_specs=specs,
+            in_specs=specs + anywhere(len(before) + len(after)),
             out_specs=tuple(
                 pl.BlockSpec((2 * high, wide), lambda i, place, core: (place[i], 0))
                 for wide, high, _ in targets
             ),
         ),
+        input_output_aliases={2 + len(arrays) + n: n for n in range(len(before))},
         compiler_params=kernel_params(),
-        cost_estimate=cost(10),
+        cost_estimate=cost(1.2 * total),
         name="spread",
-    )(places, core, *arrays)
+    )(places, core, *arrays, *before, *after)
 
 
 def small_sums(norm_sums, qkv_sums, up_sums, dy_sums, numbers):
@@ -708,75 +821,6 @@
     )(numbers, norm_sums, qkv_sums, up_sums, dy_sums)
 
 
-def packed(qkv_weight, up_weight, vectors, lengths, place, head):
-    wide, up_wide = qkv_weight.shape[1], up_weight.shape[1]
-    part, up_part = 3 * head, up_wide // 8
-    cols = part + up_part
-
-    def body(place_ref, len_ref, q_ref, u_ref, v_ref, out_ref):
-        lane = lax.broadcasted_iota(jnp.int32, (8, cols), 1)
-        row = lax.broadcasted_iota(jnp.int32, (8, cols), 0)
-        sizes = jnp.zeros((8, cols), f32)
-        for at in range(3):
-            sizes = jnp.where(lane == at, len_ref[0, at].astype(f32), sizes)
-        vector = jnp.broadcast_to(v_ref[...].astype(f32), (8, cols))
-        tail = jnp.where(row == 0, vector, jnp.where(row == 1, sizes, 0.0)).astype(bf16)
-        for owner in range(8):
-            pieces = [
-                q_ref[:, (third * 8 + owner) * head : (third * 8 + owner + 1) * head]
-                for third in range(3)
-            ]
-            pieces.append(u_ref[:, owner * up_part : (owner + 1) * up_part])
-            out_ref[owner] = jnp.concatenate([jnp.concatenate(pieces, 1), tail], 0)
-
-    return pl.pallas_call(
-        body,
-        out_shape=jax.ShapeDtypeStruct((8, 40, cols), bf16),
-        grid_spec=pltpu.PrefetchScalarGridSpec(
-            num_scalar_prefetch=2,
-            grid=(1,),
-            in_specs=[
-                pl.BlockSpec((32, wide), lambda i, place, lens: (place[0], 0)),
-                pl.BlockSpec((32, up_wide), lambda i, place, lens: (place[0], 0)),
-                pl.BlockSpec((1, cols), lambda i, place, lens: (0, 0)),
-            ],
-            out_specs=pl.BlockSpec((8, 40, cols), lambda i, place, lens: (0, 0, 0)),
-        ),
-        compiler_params=kernel_params(),
-        cost_estimate=cost(3),
-        name="packed",
-    )(place, lengths, qkv_weight, up_weight, vectors)
-
-
-def sorted_weight(pieces, spots):
-    rows, cols = pieces[0][0].shape[1:]
-    count = len(pieces)
-
-    def body(spot_ref, *refs):
-        step = pl.program_id(0)
-        for ref, (array, first, at) in zip(refs, pieces):
-
-            @pl.when(step == at)
-            def _(ref=ref, first=first, size=array.shape[0]):
-                refs[count][first : first + size, 0] = ref[...]
-
-    return pl.pallas_call(
-        body,
-        out_shape=jax.ShapeDtypeStruct((8, 8, rows, cols), bf16),
-        grid_spec=pltpu.PrefetchScalarGridSpec(
-            num_scalar_prefetch=1,
-            grid=(8,),
-            in_specs=[
-                pl.BlockSpec(array.shape, lambda i, spot: (0, 0, 0)) for array, _, _ in pieces
-            ],
-            out_specs=pl.BlockSpec((8, 1, rows, cols), lambda i, spot: (0, spot[i], 0, 0)),
-        ),
-        compiler_params=kernel_params(),
-        cost_estimate=cost(6),
-        name="sorted_weight",
-    )(spots, *[piece[0] for piece in pieces]).reshape(64 * rows, cols)
-
-
 def added(terms, groups, numbers, after):
     rows, cols = terms[0][0].shape[1:]
     firsts = [sum(groups[:n]) for n in range(len(groups))]
@@ -844,19 +888,20 @@
     l, x = shard // 4, shard % 4
     ff = up_bias.shape[0]
 
-    pair = jnp.stack([tokens, cotangent])
+    cols = 3 * head + ff
+    vectors = [v[None] for v in (ln1_gain, ln1_bias, ln2_gain, ln2_bias, qkv_bias)]
+    place = (y * 2 + c).astype(jnp.int32).reshape(1)
+    part, pair = packed(
+        qkv_weight, up_weight, vectors, doc_lengths, place, head, tokens, cotangent
+    )
     below, above, other = move(pair, x=1), move(pair, x=-1), move(pair, l=1)
     far, other_above, other_below = move(below, x=1), move(other, x=-1), move(below, l=1)
     x_other_far, dy_other_far = move(other_below[0], x=1), move(other_above[1], x=-1)
     pairs = (pair, above, far, below, other, other_above, None, other_below)
-    x_all = tuple(x_other_far[None] if p is None else p for p in pairs)
+    x_all = tuple(x_other_far if p is None else p for p in pairs)
     dy_all = tuple(dy_other_far if p is None else p for p in pairs)
 
-    vectors = jnp.concatenate([ln1_gain, ln1_bias, ln2_gain, ln2_bias, qkv_bias])[None]
-    place = (y * 2 + c).astype(jnp.int32).reshape(1)
-    part = packed(qkv_weight, up_weight, vectors, doc_lengths, place, head)
     part = lax.all_to_all(part, "shard", 0, 0)
-    cols = part.shape[-1]
     own, infos = unpacked(part, (pairs[1], pairs[3], pairs[4]))
     below, above = move(own, y=1), move(own, y=-1)
     low, high = halves(below, above, (pairs[2], pairs[5], pairs[7]))
@@ -865,7 +910,7 @@
     yours = tuple((move(array, c=1), first, spot + 4) for array, first, spot in mine)
     steps4 = (y + jnp.arange(4)) % 4
     spots = jnp.concatenate([steps4 * 2 + c, steps4 * 2 + 1 - c]).astype(jnp.int32)
-    w_mixed = sorted_weight(mine + yours, spots)
+    weight = mine + yours
 
     gains = infos[:, 0, :1024].reshape(8, 4, 256).transpose(1, 0, 2).reshape(4, width)
     qkv_b = infos[:, 0, 1024:].reshape(8 * 3, 1, head)
@@ -903,7 +948,8 @@
         x_all,
         dy_all,
         gains,
-        w_mixed,
+        weight,
+        spots,
         down_weight,
         up_bias.astype(f32)[None],
         numbers,
@@ -912,7 +958,7 @@
     )
     got = move(send, c=1)
     attended, d_qkv, a_keep, a_send, qkv_sums = attend(
-        h1, dy_all, w_mixed, out_weight, qkv_b, cosine, sine, lengths, numbers, (send,)
+        h1, dy_all, weight, spots, out_weight, qkv_b, cosine, sine, lengths, numbers, (send,)
     )
 
     def turn(k):
@@ -921,8 +967,16 @@
     low, high = added([(keep, turn(2), None), (got, turn(2), None)], (1, 1), numbers, (attended,))
     from_low, from_high = move(low, y=1), move(high, y=-1)
     a_got = move(a_send, c=1)
-    mix = mixed_part(
-        active, attended, down_weight, out_weight, wide_bias, sources, (low, high)
+    norm_sums, *sums = back_norms(
+        d_qkv,
+        d_hidden,
+        weight,
+        spots,
+        x_all,
+        mean,
+        inverse,
+        jnp.stack([gains[0], gains[2]]),
+        (low, high),
     )
 
     def sides(i, n):
@@ -937,7 +991,7 @@
         ],
         (2, 2),
         numbers,
-        (mix,),
+        (sums[0],),
     )
     from_below, from_above = move(above, y=1), move(below, y=-1)
     def away(i, n):
@@ -945,16 +999,14 @@
 
     (a_away,) = added([(a_keep, away, None), (a_got, away, None)], (4,), numbers, (above,))
     a_crossed = move(a_away, h=1)
-    norm_sums, *sums = back_norms(
-        d_qkv,
-        d_hidden,
-        w_mixed,
-        x_all,
-        mean,
-        inverse,
-        jnp.stack([gains[0], gains[2]]),
-        (a_away,),
-    )
+    mix = mixed_part(
+        active, attended, down_weight, out_weight, wide_bias, sources, (above, below, a_away)
+    )
+
+    smalls = small_sums(norm_sums, qkv_sums, up_sums, dy_sums, numbers)
+    smalls = jnp.broadcast_to(smalls[None], (16, 8, 24, 128)).reshape(128, 24, 128)
+    smalls = lax.all_to_all(smalls, BOTH, 0, 0)
+    smalls = jnp.sum(smalls.astype(f32), 0)
 
     def ends_at(i, n):
         return n[2] * 2 + jnp.where(i == 0, 1 - n[3], n[3])
@@ -971,7 +1023,7 @@
         ],
         (1, 1),
         numbers,
-        (sums[0],),
+        (mix,),
     )
     crossed = move(leaves, h=1)
 
@@ -1007,11 +1059,12 @@
     a_from_below, a_from_above = move(a_above.astype(bf16), y=1), move(a_below.astype(bf16), y=-1)
 
     part, down_stays, out_stays = packed_sums(
-        inner, a_own[0], a_from_below, a_from_above, ff, head, ()
+        inner, a_own[0], a_from_below, a_from_above, ff, head, (smalls,)
     )
     part = lax.all_to_all(part, "shard", 0, 0)
     inner, a_sum = unpacked_sums(part, down_stays, out_stays, ff, head, ())
-    inner = jnp.stack([inner, move(inner, h=1)])
+    inner_other = move(inner, h=1)
+    inner = jnp.stack([inner, inner_other])
 
     def ring(pieces, way):
         own, above, far, below = pieces if way == 1 else (pieces[n] for n in (0, 3, 2, 1))
@@ -1032,10 +1085,6 @@
         - own_normed * jnp.mean(own_sum * own_normed, -1, keepdims=True)
     )
 
-    smalls = small_sums(norm_sums, qkv_sums, up_sums, dy_sums, numbers)
-    smalls = jnp.broadcast_to(smalls[None], (16, 8, 24, 128)).reshape(128, 24, 128)
-    smalls = lax.all_to_all(smalls, BOTH, 0, 0)
-    smalls = jnp.sum(smalls.astype(f32), 0)
     norm_grads = smalls[:8].reshape(4, 256)
     dy_total = smalls[22:].reshape(256)
 
@@ -1047,14 +1096,18 @@
     up_parts = [
         (source * ff, 64 + 16 * (source % 4), source // 4 * ff, ff) for source in range(8)
     ]
+    targets = [(width, 64, [(0, 0, 0, width)]), (8 * ff, 16, up_parts)]
+    near = pieces[:2] + pieces[4:]
+    near_places = jnp.concatenate([places[:4], places[6:]])
+    grads = spread(near, near_places, numbers[:1], targets, 8, (), ())
     down_grad, up_grad = spread(
-        pieces,
-        places,
-        numbers[:1],
-        [(width, 64, [(0, 0, 0, width)]), (8 * ff, 16, up_parts)],
-    )
-
-    a_sum = jnp.stack(ring_gather(a_sum, "y", 32))
+        pieces[2:4], places[4:6], numbers[:1], targets, 8, grads, (tokens_grad, mixed)
+    )
+
+    a_below, a_above = move(a_sum, y=1), move(a_sum, y=-1)
+    a_low, a_high = halves(a_below[None], a_above[None], (inner_other,))
+    a_far = jnp.concatenate([move(a_low, y=1), move(a_high, y=-1)], 1)
+    a_sum = jnp.concatenate([a_sum[None], a_above[None], a_far, a_below[None]])
     a_other = move(a_sum, h=1)
     places = jnp.concatenate([steps4 * 2 + h, steps4 * 2 + 1 - h]).astype(jnp.int32)
     out_grad, qkv_grad = spread(
@@ -1065,6 +1118,9 @@
             (width, 16, [(0, 48, 0, width)]),
             (3 * width, 16, [(n * width, 16 * n, 0, width) for n in range(3)]),
         ],
+        8,
+        (),
+        (),
     )
     return (
         mixed,

time: 454 us -> 473 us (1.042)
  starting transfers between devices: 89.4 us -> 116 us
    ppermute x53, starting transfers between devices: 74.2 us -> 101 us  [move(): return lax.ppermute(value, BOTH, pairs)]
    ppermute x53, waiting for transfers between devices: 111 us -> 103 us  [move(): return lax.ppermute(value, BOTH, pairs)]
    broadcast_in_dim x1 -> x5, local copies, waits for them, and re-layouts: 0.6 us -> 6.14 us  [local(): v[None]]
    all_to_all x2, waiting for transfers between devices: 26.1 us -> 31.5 us  [local(): part = lax.all_to_all(part, 'shard', 0, 0)]
  transfers between devices with their start and end apart: 57 -> 57, of which waited for: 15 -> 15; matrix products, arithmetic and copies ran while one was open for 8% -> 7% of each run, Pallas kernels for 26% -> 23%
where the time goes in v4:
time: 473 us; the launch traced here: 466 us
  Pallas kernels  150 us (32%)
  waiting for transfers between devices  135 us (29%)
  starting transfers between devices  116 us (25%)
  local copies, waits for them, and re-layouts  35 us (7%)
  other arithmetic  15.9 us (3%)
  between operations  15.2 us (3%)
    ppermute x53, waiting for transfers between devices, move(): return lax.ppermute(value, BOTH, pairs)  103 us
    ppermute x53, starting transfers between devices, move(): return lax.ppermute(value, BOTH, pairs)  101 us
    pallas_call x1, Pallas kernels, feed_forward(): pl.pallas_call(after_inputs(body, 5 + parts + 2 * count, len(after)), out...  32.2 us
    all_to_all x2, waiting for transfers between devices, local(): part = lax.all_to_all(part, 'shard', 0, 0)  31.5 us
    pallas_call x6, Pallas kernels, added(): pl.pallas_call(after_inputs(body, 1 + len(terms), len(after)), out_shape=...  26.1 us
    pallas_call x1, Pallas kernels, attend(): pl.pallas_call(after_inputs(body, 8 + parts + count, len(after)), out_sha...  25.6 us
    pallas_call x3, Pallas kernels, spread(): pl.pallas_call(after_inputs(body, 2 + 2 * len(pieces) + len(before), len(...  22.2 us
    pallas_call x1, Pallas kernels, back_norms(): pl.pallas_call(after_inputs(body, 6 + parts + count, len(after)), out_sha...  17.7 us
  transfers between devices with their start and end apart: 57, of which 15 were waited for; matrix products, arithmetic and copies ran while one was open for 7% of the time, Pallas kernels for 23%

profile of v4, /device:TPU:1, one launch (start us, length us, event | category | flops | bytes accessed | tf_op | source)
XLA Modules:
  0.0 466.2 jit_solution(9948989830527085883)
XLA Ops:
  13.3 3.6 packed.1
  22.1 3.6 all-to-all-start
  26.3 30.5 %all-to-all-done.refs_0_ = bf16[8,40,1792]{2,1,0:T(8,128)(2,1)S(1)} async-done(((bf16[8,40,1792]{2,1,0:T(8,128)(2,1)}), bf16[8,40,1792]{2,1,0:T(8,128)(2,1)S(1)}, u32[]{:S(2)}, u32[]{:S(2)}) %all-to-all-start) | async-done | bytes 1146912 | tf_op jit(solution)/shard_map/all_to_all | solution.py:904
  68.5 12.9 %collective-permute-done.3.refs_1_.refs_5_ = bf16[8,32,1792]{2,1,0:T(8,128)(2,1)} collective-permute-done((bf16[8,32,1792]{2,1,0:T(8,128)(2,1)}, bf16[8,32,1792]{2,1,0:T(8,128)(2,1)}, u32[]{:S(2)}, u32[]{:S(2)}) %collective-permute-start.3) | collective-permute-done | bytes 917536 | tf_op jit(solution)/shard_map/ppermute | solution.py:45
  86.2 3.9 collective-permute-start.11
  100.3 7.3 %collective-permute-done.8.refs_6_ = bf16[4,32,1792]{2,1,0:T(8,128)(2,1)S(1)} collective-permute-done((bf16[4,32,1792]{2,1,0:T(8,128)(2,1)}, bf16[4,32,1792]{2,1,0:T(8,128)(2,1)S(1)}, u32[]{:S(2)}, u32[]{:S(2)}) %collective-permute-start.8) | collective-permute-done | bytes 458784 | tf_op jit(solution)/shard_map/ppermute | solution.py:45
  113.7 3.1 fusion.12
  116.8 3.2 collective-permute-done.16.refs_28_.refs_20_
  121.8 32.2 %feed_forward.1 = (bf16[1024,2048]{1,0:T(8,128)(2,1)}, bf16[1024,1024]{1,0:T(8,128)(2,1)}, bf16[1024,1024]{1,0:T(8,128)(2,1)}, bf16[8,128,2048]{2,1,0:T(8,128)(2...) custom-call(s32[4]{0:T(128)} %get-tuple-element.136.refs_0_.number_r, ...), custom_call_target="tpu_custom_call" | custom-call | flops 36800000000 | bytes 1000 | tf_op jit(solution)/shard_map/feed_forward/pallas_call | solution.py:250
  158.4 25.6 %attend.1 = (bf16[1024,256]{1,0:T(8,128)(2,1)}, bf16[1024,768]{1,0:T(8,128)(2,1)}, bf16[8,64,2048]{2,1,0:T(8,128)(2,1)}, bf16[8,64,2048]{2,1,0:T(8,128)(2,1)}, f32[1,768]{1,0:T(1,128)}) custom-call(s32[4]{0:T(128)} %get-tuple-element.136.refs_0_.number_ref, s32[8,3]{1,0:T(8,128)} %copy-done.22, s32[8]{0:T(128)} %pad_add_fusion.1.refs_1_.refs_2_.refs_0_, ...), custom_call_target="tpu_custom_call" | custom-call | flops 25300000768 | bytes 1000 | tf_op jit(solution)/shard_map/attend/pallas_call | solution.py:404
  184.2 3.4 added.6
  190.5 17.7 %back_norms.1 = (f32[4,2048]{1,0:T(4,128)}, bf16[128,2048]{1,0:T(8,128)(2,1)}, bf16[128,2048]{1,0:T(8,128)(2,1)}, bf16[128,2048]{1,0:T(8,128)(2,1)}, bf16[128,20...) custom-call(s32[8]{0:T(128)} %pad_add_fusion.1.refs_1_.refs_2_.refs_, ...), custom_call_target="tpu_custom_call" | custom-call | flops 16099999744 | bytes 1000 | tf_op jit(solution)/shard_map/back_norms/pallas_call | solution.py:590
  211.5 6.9 %all-to-all-start.1 = ((bf16[128,24,128]{2,1,0:T(8,128)(2,1)}), bf16[128,24,128]{2,1,0:T(8,128)(2,1)S(1)}, u32[]{:S(2)}, u32[]{:S(2)}) async-start(bf16[128,24,128]{2,1,0:T(8,128)(2,1)} %bitcast.13), calls=%async_computation.2 | async-start | bytes 1572864 | tf_op jit(solution)/shard_map/all_to_all | solution.py:1008
  219.5 6.6 %added.7 = (bf16[2,128,2048]{2,1,0:T(8,128)(2,1)}, bf16[2,128,2048]{2,1,0:T(8,128)(2,1)}) custom-call(s32[4]{0:T(128)} %get-tuple-element.136.refs_0_.number_ref, bf16[8,128,2048]{2,1,0:T(8,128)(2,1)} %get-tuple-element.76.refs_1_, bf16[8,128,2048]{2,1,0:T(8,128)(2,1)} %collective-permute-done.17.refs_2_, bf16[1,128,2048]{2,1,0:T(8,128)(2,1)} %copy-done.38, ...), custom_call_target="tpu_custom_call" | custom-call | flops 4600000000 | bytes 1000 | tf_op jit(solution)/shard_map/added/pallas_call | solution.py:850
  227.5 4.4 added.8.refs_8_
  231.9 3.1 collective-permute-start.31
  236.5 10.3 %mixed_part.1.refs_5_ = bf16[1024,2048]{1,0:T(8,128)(2,1)} custom-call(s32[8]{0:T(128)} %copy-done.47, bf16[1024,1024]{1,0:T(8,128)(2,1)} %get-tuple-element.72.refs_1_, bf16[1024,256]{1,0:T(8,128)(2,1)} %get-tuple-element.75.refs_3_.refs_2_, bf16[1024,2048]{1,0:T(8,128)(2,1)} %refs_3_.1, bf16[256,2048]{1,0:T(8,128)(2,1)} %refs_4_.1, f32[1,2048]{1,0:T(1,128)} %copy-done.23, ...), custom_call_target="tpu_custom_call" | custom-call | flops 11500000256 | bytes 1000 | tf_op jit(solution)/shard_map/mixed_part/pallas_call | solution.py:462
  247.6 48.9 %collective-permute-done.31.refs_3_ = bf16[4,64,2048]{2,1,0:T(8,128)(2,1)} collective-permute-done((bf16[4,64,2048]{2,1,0:T(8,128)(2,1)}, bf16[4,64,2048]{2,1,0:T(8,128)(2,1)}, u32[]{:S(2)}, u32[]{:S(2)}) %collective-permute-start.31) | collective-permute-done | bytes 1048608 | tf_op jit(solution)/shard_map/ppermute | solution.py:45
  296.4 4.6 added.10
  306.4 4.3 added.9
  310.7 3.8 collective-permute-start.30
  316.3 8.6 %collective-permute-done.30.refs_2_ = bf16[1,128,2048]{2,1,0:T(8,128)(2,1)S(1)} collective-permute-done((bf16[1,128,2048]{2,1,0:T(8,128)(2,1)}, bf16[1,128,2048]{2,1,0:T(8,128)(2,1)S(1)}, u32[]{:S(2)}, u32[]{:S(2)}) %collective-permute-start.30) | collective-permute-done | bytes 524320 | tf_op jit(solution)/shard_map/ppermute | solution.py:45
  331.4 4.3 all-to-all-start.2
  364.7 10.2 %collective-permute-start.50 = (bf16[2,128,2048]{2,1,0:T(8,128)(2,1)}, bf16[2,128,2048]{2,1,0:T(8,128)(2,1)}, u32[]{:S(2)}, u32[]{:S(2)}) collective-permute-start(bf16[2,128,2048]{2,1,0:T(8,128)(2,1)} %pad_maximum_fusion.1.refs_2_), channel_id=1, source_target_pairs={{0,8},{1,9},{2,10},{3,11},{4,12},{5,13},{6,14},{7,15},{8,0},{9,1},... | collective-permute-start | bytes 3145736 | tf_op jit(solution)/shard_map/ppermute | solution.py:45
  380.9 5.7 %collective-permute-done.39 = bf16[1,32,2048]{2,1,0:T(8,128)(2,1)S(1)} collective-permute-done((bf16[1,32,2048]{2,1,0:T(8,128)(2,1)}, bf16[1,32,2048]{2,1,0:T(8,128)(2,1)S(1)}, u32[]{:S(2)}, u32[]{:S(2)}) %collective-permute-start.39) | collective-permute-done | bytes 131104 | tf_op jit(solution)/shard_map/ppermute | solution.py:45
  390.5 3.5 collective-permute-start.42
  397.0 14.5 %collective-permute-start.52 = (bf16[2,128,2048]{2,1,0:T(8,128)(2,1)}, bf16[2,128,2048]{2,1,0:T(8,128)(2,1)S(1)}, u32[]{:S(2)}, u32[]{:S(2)}) collective-permute-start(bf16[2,128,2048]{2,1,0:T(8,128)(2,1)} %collective-permute-done.44.refs_6_), channel_id=1, source_target_pairs={{0,8},{1,9},{2,10},{3,11},{4,12},{5,13},{6,14},{7,15},{8,0},{9,1},... | collective-permute-start | bytes 3145736 | tf_op jit(solution)/shard_map/ppermute | solution.py:45
  414.4 5.1 %collective-permute-done.42.refs_4_ = bf16[4,64,2048]{2,1,0:T(8,128)(2,1)} collective-permute-done((bf16[4,64,2048]{2,1,0:T(8,128)(2,1)}, bf16[4,64,2048]{2,1,0:T(8,128)(2,1)}, u32[]{:S(2)}, u32[]{:S(2)}) %collective-permute-start.42) | collective-permute-done | bytes 1048608 | tf_op jit(solution)/shard_map/ppermute | solution.py:45
  419.5 9.1 %collective-permute-start.41 = (bf16[4,64,2048]{2,1,0:T(8,128)(2,1)}, bf16[4,64,2048]{2,1,0:T(8,128)(2,1)S(1)}, u32[]{:S(2)}, u32[]{:S(2)}) collective-permute-start(bf16[4,64,2048]{2,1,0:T(8,128)(2,1)} %pad_maximum_fusion.refs_2_), channel_id=1, source_target_pairs={{0,8},{1,9},{2,10},{3,11},{4,12},{5,13},{6,14},{7,15},{8,0},{9,1},... | collective-permute-start | bytes 3145736 | tf_op jit(solution)/shard_map/ppermute | solution.py:45
  431.2 9.5 %spread.4 = (f32[1024,2048]{1,0:T(8,128)}, f32[256,8192]{1,0:T(8,128)}) custom-call(s32[6]{0:T(128)} %concatenate.33.refs_0_, s32[1]{0:T(128)} %bitcast.refs_1_, bf16[2,128,2048]{2,1,0:T(8,128)(2,1)} %pad_maximum_fusion.1.refs_2_, bf16[2,128,2048]{2,1,0:T(8,128)(2,1)} %collective-permute-done.50.refs_3_, ...), custom_call_target="tpu_custom_call" | custom-call | flops 8280000000 | bytes 1000 | tf_op jit(solution)/shard_map/spread/pallas_call | solution.py:764
  442.8 8.3 %spread.3 = (f32[256,2048]{1,0:T(8,128)}, f32[256,6144]{1,0:T(8,128)}) custom-call(s32[8]{0:T(128)} %pad_add_fusion.2.refs_0_, s32[1]{0:T(128)} %bitcast.refs_1_, bf16[4,64,2048]{2,1,0:T(8,128)(2,1)} %pad_maximum_fusion.refs_2_, bf16[4,64,2048]{2,1,0:T(8,128)(2,1)} %copy-done.31, bf16[4,64,2048]{2,1,0:T(8,128)(2,1)} %collective-permute-done.42.refs_4_, ...), custom_call_target="tpu_custom_call" | custom-call | flops 11040000000 | bytes 1000 | tf_op jit(solution)/shard_map/spread/pallas_call | solution.py:764
  454.0 4.4 spread.5
  (271 shorter events, 127.5 us)
Async XLA Ops:
  16.9 39.9 %collective-permute-start.1 = (bf16[2,128,2048]{2,1,0:T(8,128)(2,1)}, bf16[2,128,2048]{2,1,0:T(8,128)(2,1)}, u32[]{:S(2)}, u32[]{:S(2)}) collective-permute-start(bf16[2,128,2048]{2,1,0:T(8,128)(2,1)} %get-tuple-element.67.refs_14_.refs_22_), channel_id=1, source_target_pairs={{0,1},{1,2},{2,3},{3,0},{4,5},{5,6},{6,7},{7,4},{8,9},{9,10},{10,1... | collective-permute-start | bytes 3145736 | tf_op jit(solution)/shard_map/ppermute | solution.py:45
  19.0 37.9 %collective-permute-start.2 = (bf16[2,128,2048]{2,1,0:T(8,128)(2,1)}, bf16[2,128,2048]{2,1,0:T(8,128)(2,1)}, u32[]{:S(2)}, u32[]{:S(2)}) collective-permute-start(bf16[2,128,2048]{2,1,0:T(8,128)(2,1)} %get-tuple-element.67.refs_14_.refs_22_), channel_id=1, source_target_pairs={{0,4},{1,5},{2,6},{3,7},{4,0},{5,1},{6,2},{7,3},{8,12},{9,13},{10,... | collective-permute-start | bytes 3145736 | tf_op jit(solution)/shard_map/ppermute | solution.py:45
  20.6 36.3 %collective-permute-start = (bf16[2,128,2048]{2,1,0:T(8,128)(2,1)}, bf16[2,128,2048]{2,1,0:T(8,128)(2,1)}, u32[]{:S(2)}, u32[]{:S(2)}) collective-permute-start(bf16[2,128,2048]{2,1,0:T(8,128)(2,1)} %get-tuple-element.67.refs_14_.refs_22_), channel_id=1, source_target_pairs={{0,3},{1,0},{2,1},{3,2},{4,7},{5,4},{6,5},{7,6},{8,11},{9,8},{10,9... | collective-permute-start | bytes 3145736 | tf_op jit(solution)/shard_map/ppermute | solution.py:45
  22.1 34.8 %all-to-all-start = ((bf16[8,40,1792]{2,1,0:T(8,128)(2,1)}), bf16[8,40,1792]{2,1,0:T(8,128)(2,1)S(1)}, u32[]{:S(2)}, u32[]{:S(2)}) async-start(bf16[8,40,1792]{2,1,0:T(8,128)(2,1)} %get-tuple-element.66), calls=%async_computation | async-start | bytes 2293760 | tf_op jit(solution)/shard_map/all_to_all | solution.py:904
  60.3 21.1 %collective-permute-start.3 = (bf16[8,32,1792]{2,1,0:T(8,128)(2,1)}, bf16[8,32,1792]{2,1,0:T(8,128)(2,1)}, u32[]{:S(2)}, u32[]{:S(2)}) collective-permute-start(bf16[8,32,1792]{2,1,0:T(8,128)(2,1)} %get-tuple-element.69.refs_4_), channel_id=1, source_target_pairs={{0,96},{1,97},{2,98},{3,99},{4,100},{5,101},{6,102},{7,103},{8,104... | collective-permute-start | bytes 2752520 | tf_op jit(solution)/shard_map/ppermute | solution.py:45
  63.1 27.1 %collective-permute-start.7 = (bf16[2,128,2048]{2,1,0:T(8,128)(2,1)}, bf16[2,128,2048]{2,1,0:T(8,128)(2,1)S(1)}, u32[]{:S(2)}, u32[]{:S(2)}) collective-permute-start(bf16[2,128,2048]{2,1,0:T(8,128)(2,1)} %collective-permute-done.1.refs_2_.refs_17_.refs_25_), channel_id=1, source_target_pairs={{0,4},{1,5},{2,6},{3,7},{4,0},{5,1},{6,2},{7,3},{8,12},{9,13},{10,... | collective-permute-start | bytes 3145736 | tf_op jit(solution)/shard_map/ppermute | solution.py:45
  63.1 27.2 %collective-permute-start.5 = (bf16[2,128,2048]{2,1,0:T(8,128)(2,1)}, bf16[2,128,2048]{2,1,0:T(8,128)(2,1)}, u32[]{:S(2)}, u32[]{:S(2)}) collective-permute-start(bf16[2,128,2048]{2,1,0:T(8,128)(2,1)} %collective-permute-done.1.refs_2_.refs_17_.refs_25_), channel_id=1, source_target_pairs={{0,1},{1,2},{2,3},{3,0},{4,5},{5,6},{6,7},{7,4},{8,9},{9,10},{10,1... | collective-permute-start | bytes 3145736 | tf_op jit(solution)/shard_map/ppermute | solution.py:45
  65.5 24.8 %collective-permute-start.6 = (bf16[2,128,2048]{2,1,0:T(8,128)(2,1)}, bf16[2,128,2048]{2,1,0:T(8,128)(2,1)S(1)}, u32[]{:S(2)}, u32[]{:S(2)}) collective-permute-start(bf16[2,128,2048]{2,1,0:T(8,128)(2,1)} %collective-permute-done.2.refs_3_.refs_18_.refs_26_), channel_id=1, source_target_pairs={{0,3},{1,0},{2,1},{3,2},{4,7},{5,4},{6,5},{7,6},{8,11},{9,8},{10,9... | collective-permute-start | bytes 3145736 | tf_op jit(solution)/shard_map/ppermute | solution.py:45
  65.8 20.4 %collective-permute-start.4 = (bf16[8,32,1792]{2,1,0:T(8,128)(2,1)}, bf16[8,32,1792]{2,1,0:T(8,128)(2,1)}, u32[]{:S(2)}, u32[]{:S(2)}) collective-permute-start(bf16[8,32,1792]{2,1,0:T(8,128)(2,1)} %get-tuple-element.69.refs_4_), channel_id=1, source_target_pairs={{0,32},{1,33},{2,34},{3,35},{4,36},{5,37},{6,38},{7,39},{8,40},{9,... | collective-permute-start | bytes 2752520 | tf_op jit(solution)/shard_map/ppermute | solution.py:45
  86.2 33.9 %collective-permute-start.11 = (bf16[8,32,1792]{2,1,0:T(8,128)(2,1)}, bf16[8,32,1792]{2,1,0:T(8,128)(2,1)S(1)}, u32[]{:S(2)}, u32[]{:S(2)}) collective-permute-start(bf16[8,32,1792]{2,1,0:T(8,128)(2,1)} %collective-permute-done.3.refs_1_.refs_5_), channel_id=1, source_target_pairs={{0,8},{1,9},{2,10},{3,11},{4,12},{5,13},{6,14},{7,15},{8,0},{9,1},... | collective-permute-start | bytes 2752520 | tf_op jit(solution)/shard_map/ppermute | solution.py:45
  90.1 29.9 %collective-permute-start.14 = (bf16[8,32,1792]{2,1,0:T(8,128)(2,1)}, bf16[8,32,1792]{2,1,0:T(8,128)(2,1)S(1)}, u32[]{:S(2)}, u32[]{:S(2)}) collective-permute-start(bf16[8,32,1792]{2,1,0:T(8,128)(2,1)} %collective-permute-done.4.refs_0_.refs_8_), channel_id=1, source_target_pairs={{0,8},{1,9},{2,10},{3,11},{4,12},{5,13},{6,14},{7,15},{8,0},{9,1},... | collective-permute-start | bytes 2752520 | tf_op jit(solution)/shard_map/ppermute | solution.py:45
  154.0 30.2 %collective-permute-start.17 = (bf16[8,128,2048]{2,1,0:T(8,128)(2,1)}, bf16[8,128,2048]{2,1,0:T(8,128)(2,1)}, u32[]{:S(2)}, u32[]{:S(2)}) collective-permute-start(bf16[8,128,2048]{2,1,0:T(8,128)(2,1)} %get-tuple-element.74.refs_26_), channel_id=1, source_target_pairs={{0,8},{1,9},{2,10},{3,11},{4,12},{5,13},{6,14},{7,15},{8,0},{9,1},... | collective-permute-start | bytes 12582920 | tf_op jit(solution)/shard_map/ppermute | solution.py:45
  184.1 43.4 %collective-permute-start.20 = (bf16[8,64,2048]{2,1,0:T(8,128)(2,1)}, bf16[8,64,2048]{2,1,0:T(8,128)(2,1)}, u32[]{:S(2)}, u32[]{:S(2)}) collective-permute-start(bf16[8,64,2048]{2,1,0:T(8,128)(2,1)} %get-tuple-element.87), channel_id=1, source_target_pairs={{0,8},{1,9},{2,10},{3,11},{4,12},{5,13},{6,14},{7,15},{8,0},{9,1},... | collective-permute-start | bytes 6291464 | tf_op jit(solution)/shard_map/ppermute | solution.py:45
  187.6 30.9 %collective-permute-start.18 = (bf16[1,128,2048]{2,1,0:T(8,128)(2,1)}, bf16[1,128,2048]{2,1,0:T(8,128)(2,1)S(1)}, u32[]{:S(2)}, u32[]{:S(2)}) collective-permute-start(bf16[1,128,2048]{2,1,0:T(8,128)(2,1)} %get-tuple-element.77.refs_24_), channel_id=1, source_target_pairs={{0,32},{1,33},{2,34},{3,35},{4,36},{5,37},{6,38},{7,39},{8,40},{9,... | collective-permute-start | bytes 1572872 | tf_op jit(solution)/shard_map/ppermute | solution.py:45
  187.6 30.9 %collective-permute-start.19 = (bf16[1,128,2048]{2,1,0:T(8,128)(2,1)}, bf16[1,128,2048]{2,1,0:T(8,128)(2,1)S(1)}, u32[]{:S(2)}, u32[]{:S(2)}) collective-permute-start(bf16[1,128,2048]{2,1,0:T(8,128)(2,1)} %get-tuple-element.78.refs_25_), channel_id=1, source_target_pairs={{0,96},{1,97},{2,98},{3,99},{4,100},{5,101},{6,102},{7,103},{8,104... | collective-permute-start | bytes 1572872 | tf_op jit(solution)/shard_map/ppermute | solution.py:45
  211.5 35.3 %all-to-all-start.1 = ((bf16[128,24,128]{2,1,0:T(8,128)(2,1)}), bf16[128,24,128]{2,1,0:T(8,128)(2,1)S(1)}, u32[]{:S(2)}, u32[]{:S(2)}) async-start(bf16[128,24,128]{2,1,0:T(8,128)(2,1)} %bitcast.13), calls=%async_computation.2 | async-start | bytes 1572864 | tf_op jit(solution)/shard_map/all_to_all | solution.py:1008
  218.4 232.6 %reduce-scatter.2.cloned.1.call-start = ((), (), s32[]{:S(2)}) async-start(), calls=%async_computation.4 | async-start | bytes 4718592 | tf_op jit(solution)/shard_map/reduce_scatter | solution.py:1079
  226.1 79.3 %collective-permute-start.28 = (bf16[2,128,2048]{2,1,0:T(8,128)(2,1)}, bf16[2,128,2048]{2,1,0:T(8,128)(2,1)S(1)}, u32[]{:S(2)}, u32[]{:S(2)}) collective-permute-start(bf16[2,128,2048]{2,1,0:T(8,128)(2,1)} %get-tuple-element.84.refs_3_.refs_6_), channel_id=1, source_target_pairs={{0,32},{1,33},{2,34},{3,35},{4,36},{5,37},{6,38},{7,39},{8,40},{9,... | collective-permute-start | bytes 3145736 | tf_op jit(solution)/shard_map/ppermute | solution.py:45
  231.9 64.5 %collective-permute-start.31 = (bf16[4,64,2048]{2,1,0:T(8,128)(2,1)}, bf16[4,64,2048]{2,1,0:T(8,128)(2,1)}, u32[]{:S(2)}, u32[]{:S(2)}) collective-permute-start(bf16[4,64,2048]{2,1,0:T(8,128)(2,1)} %added.8.refs_8_), channel_id=1, source_target_pairs={{0,16},{1,17},{2,18},{3,19},{4,20},{5,21},{6,22},{7,23},{8,24},{9,... | collective-permute-start | bytes 3145736 | tf_op jit(solution)/shard_map/ppermute | solution.py:45
  235.1 70.3 %collective-permute-start.29 = (bf16[2,128,2048]{2,1,0:T(8,128)(2,1)}, bf16[2,128,2048]{2,1,0:T(8,128)(2,1)}, u32[]{:S(2)}, u32[]{:S(2)}) collective-permute-start(bf16[2,128,2048]{2,1,0:T(8,128)(2,1)} %get-tuple-element.85.refs_7_), channel_id=1, source_target_pairs={{0,96},{1,97},{2,98},{3,99},{4,100},{5,101},{6,102},{7,103},{8,104... | collective-permute-start | bytes 3145736 | tf_op jit(solution)/shard_map/ppermute | solution.py:45
  339.4 25.3 %collective-permute-start.26 = (bf16[128,2048]{1,0:T(8,128)(2,1)}, bf16[128,2048]{1,0:T(8,128)(2,1)S(1)}, u32[]{:S(2)}, u32[]{:S(2)}) collective-permute-start(bf16[128,2048]{1,0:T(8,128)(2,1)} %get-tuple-element.94), channel_id=1, source_target_pairs={{0,3},{1,0},{2,1},{3,2},{4,7},{5,4},{6,5},{7,6},{8,11},{9,8},{10,9... | collective-permute-start | bytes 1572872 | tf_op jit(solution)/shard_map/ppermute | solution.py:45
  342.0 32.9 %collective-permute-start.23 = (bf16[128,2048]{1,0:T(8,128)(2,1)}, bf16[128,2048]{1,0:T(8,128)(2,1)S(1)}, u32[]{:S(2)}, u32[]{:S(2)}) collective-permute-start(bf16[128,2048]{1,0:T(8,128)(2,1)} %get-tuple-element.90), channel_id=1, source_target_pairs={{0,1},{1,2},{2,3},{3,0},{4,5},{5,6},{6,7},{7,4},{8,9},{9,10},{10,1... | collective-permute-start | bytes 1572872 | tf_op jit(solution)/shard_map/ppermute | solution.py:45
  356.7 21.2 %collective-permute-start.25 = (bf16[128,2048]{1,0:T(8,128)(2,1)S(1)}, bf16[128,2048]{1,0:T(8,128)(2,1)S(1)}, u32[]{:S(2)}, u32[]{:S(2)}) collective-permute-start(bf16[128,2048]{1,0:T(8,128)(2,1)S(1)} %add_convert_fusion.1), channel_id=1, source_target_pairs={{0,1},{1,2},{2,3},{3,0},{4,5},{5,6},{6,7},{7,4},{8,9},{9,10},{10,1... | collective-permute-start | bytes 1572872 | tf_op jit(solution)/shard_map/ppermute | solution.py:45
  357.9 53.6 %collective-permute-start.47 = (bf16[2,128,2048]{2,1,0:T(8,128)(2,1)}, bf16[2,128,2048]{2,1,0:T(8,128)(2,1)}, u32[]{:S(2)}, u32[]{:S(2)}) collective-permute-start(bf16[2,128,2048]{2,1,0:T(8,128)(2,1)} %pad_maximum_fusion.1.refs_2_), channel_id=1, source_target_pairs={{0,96},{1,97},{2,98},{3,99},{4,100},{5,101},{6,102},{7,103},{8,104... | collective-permute-start | bytes 3145736 | tf_op jit(solution)/shard_map/ppermute | solution.py:45
  362.2 28.3 %collective-permute-start.44 = (bf16[2,128,2048]{2,1,0:T(8,128)(2,1)}, bf16[2,128,2048]{2,1,0:T(8,128)(2,1)}, u32[]{:S(2)}, u32[]{:S(2)}) collective-permute-start(bf16[2,128,2048]{2,1,0:T(8,128)(2,1)} %pad_maximum_fusion.1.refs_2_), channel_id=1, source_target_pairs={{0,32},{1,33},{2,34},{3,35},{4,36},{5,37},{6,38},{7,39},{8,40},{9,... | collective-permute-start | bytes 3145736 | tf_op jit(solution)/shard_map/ppermute | solution.py:45
  364.7 49.1 %collective-permute-start.50 = (bf16[2,128,2048]{2,1,0:T(8,128)(2,1)}, bf16[2,128,2048]{2,1,0:T(8,128)(2,1)}, u32[]{:S(2)}, u32[]{:S(2)}) collective-permute-start(bf16[2,128,2048]{2,1,0:T(8,128)(2,1)} %pad_maximum_fusion.1.refs_2_), channel_id=1, source_target_pairs={{0,8},{1,9},{2,10},{3,11},{4,12},{5,13},{6,14},{7,15},{8,0},{9,1},... | collective-permute-start | bytes 3145736 | tf_op jit(solution)/shard_map/ppermute | solution.py:45
  390.5 29.0 %collective-permute-start.42 = (bf16[4,64,2048]{2,1,0:T(8,128)(2,1)}, bf16[4,64,2048]{2,1,0:T(8,128)(2,1)}, u32[]{:S(2)}, u32[]{:S(2)}) collective-permute-start(bf16[4,64,2048]{2,1,0:T(8,128)(2,1)} %pad_maximum_fusion.refs_2_), channel_id=1, source_target_pairs={{0,16},{1,17},{2,18},{3,19},{4,20},{5,21},{6,22},{7,23},{8,24},{9,... | collective-permute-start | bytes 3145736 | tf_op jit(solution)/shard_map/ppermute | solution.py:45
  396.9 31.7 %collective-permute-start.45 = (bf16[1,128,2048]{2,1,0:T(8,128)(2,1)S(1)}, bf16[1,128,2048]{2,1,0:T(8,128)(2,1)}, u32[]{:S(2)}, u32[]{:S(2)}) collective-permute-start(bf16[1,128,2048]{2,1,0:T(8,128)(2,1)S(1)} %slice.121), channel_id=1, source_target_pairs={{0,32},{1,33},{2,34},{3,35},{4,36},{5,37},{6,38},{7,39},{8,40},{9,... | collective-permute-start | bytes 1572872 | tf_op jit(solution)/shard_map/ppermute | solution.py:45
  397.0 32.4 %collective-permute-start.52 = (bf16[2,128,2048]{2,1,0:T(8,128)(2,1)}, bf16[2,128,2048]{2,1,0:T(8,128)(2,1)S(1)}, u32[]{:S(2)}, u32[]{:S(2)}) collective-permute-start(bf16[2,128,2048]{2,1,0:T(8,128)(2,1)} %collective-permute-done.44.refs_6_), channel_id=1, source_target_pairs={{0,8},{1,9},{2,10},{3,11},{4,12},{5,13},{6,14},{7,15},{8,0},{9,1},... | collective-permute-start | bytes 3145736 | tf_op jit(solution)/shard_map/ppermute | solution.py:45
  419.5 21.2 %collective-permute-start.41 = (bf16[4,64,2048]{2,1,0:T(8,128)(2,1)}, bf16[4,64,2048]{2,1,0:T(8,128)(2,1)S(1)}, u32[]{:S(2)}, u32[]{:S(2)}) collective-permute-start(bf16[4,64,2048]{2,1,0:T(8,128)(2,1)} %pad_maximum_fusion.refs_2_), channel_id=1, source_target_pairs={{0,8},{1,9},{2,10},{3,11},{4,12},{5,13},{6,14},{7,15},{8,0},{9,1},... | collective-permute-start | bytes 3145736 | tf_op jit(solution)/shard_map/ppermute | solution.py:45
  428.7 25.3 %collective-permute-start.46 = (bf16[1,128,2048]{2,1,0:T(8,128)(2,1)}, bf16[1,128,2048]{2,1,0:T(8,128)(2,1)}, u32[]{:S(2)}, u32[]{:S(2)}) collective-permute-start(bf16[1,128,2048]{2,1,0:T(8,128)(2,1)} %collective-permute-done.45.refs_2_), channel_id=1, source_target_pairs={{0,8},{1,9},{2,10},{3,11},{4,12},{5,13},{6,14},{7,15},{8,0},{9,1},... | collective-permute-start | bytes 1572872 | tf_op jit(solution)/shard_map/ppermute | solution.py:45
  429.3 24.7 %collective-permute-start.49 = (bf16[1,128,2048]{2,1,0:T(8,128)(2,1)}, bf16[1,128,2048]{2,1,0:T(8,128)(2,1)}, u32[]{:S(2)}, u32[]{:S(2)}) collective-permute-start(bf16[1,128,2048]{2,1,0:T(8,128)(2,1)} %collective-permute-done.48.refs_4_), channel_id=1, source_target_pairs={{0,8},{1,9},{2,10},{3,11},{4,12},{5,13},{6,14},{7,15},{8,0},{9,1},... | collective-permute-start | bytes 1572872 | tf_op jit(solution)/shard_map/ppermute | solution.py:45
  (73 other events, 893.0 us)
Sparse Core Ops, SparseCore 0:
  246.9 51.6 reduce-scatter.1

commit v5 on v4

--- a/solution.py
+++ b/solution.py
@@ -111,11 +111,11 @@
 def weight_copies(pieces, refs, spot_ref, target, lanes, sems):
     return [
         pltpu.make_async_copy(
-            ref.at[:, :, lanes],
-            target.at[pl.ds(first, array.shape[0]), spot_ref[spot]],
+            ref.at[pl.ds(begin, size), :, lanes],
+            target.at[pl.ds(first, size), spot_ref[spot]],
             sems.at[at],
         )
-        for at, (ref, (array, first, spot)) in enumerate(zip(refs, pieces))
+        for at, (ref, (_, begin, size, first, spot)) in enumerate(zip(refs, pieces))
     ]
 
 
@@ -286,6 +286,58 @@
     )(numbers, spots, gains, bias, *[p[0] for p in weight], *x, *dy, down, *after)
 
 
+def packed(qkv_weight, up_weight, vectors, lengths, place, head, tokens, cotangent):
+    wide, up_wide = qkv_weight.shape[1], up_weight.shape[1]
+    part, up_part = 3 * head, up_wide // 8
+    cols = part + up_part
+
+    def body(place_ref, len_ref, q_ref, u_ref, x_ref, dy_ref, *refs):
+        v_refs, out_ref, pair_ref = refs[: len(vectors)], refs[-2], refs[-1]
+        pair_ref[0] = x_ref[...]
+        pair_ref[1] = dy_ref[...]
+        lane = lax.broadcasted_iota(jnp.int32, (8, cols), 1)
+        row = lax.broadcasted_iota(jnp.int32, (8, cols), 0)
+        sizes = jnp.zeros((8, cols), f32)
+        for at in range(3):
+            sizes = jnp.where(lane == at, len_ref[0, at].astype(f32), sizes)
+        vector = jnp.concatenate([ref[...].astype(f32) for ref in v_refs], 1)
+        vector = jnp.broadcast_to(vector, (8, cols))
+        tail = jnp.where(row == 0, vector, jnp.where(row == 1, sizes, 0.0)).astype(bf16)
+        for owner in range(8):
+            pieces = [
+                q_ref[:, (third * 8 + owner) * head : (third * 8 + owner + 1) * head]
+                for third in range(3)
+            ]
+            pieces.append(u_ref[:, owner * up_part : (owner + 1) * up_part])
+            out_ref[owner] = jnp.concatenate([jnp.concatenate(pieces, 1), tail], 0)
+
+    return pl.pallas_call(
+        body,
+        out_shape=(
+            jax.ShapeDtypeStruct((8, 40, cols), bf16),
+            jax.ShapeDtypeStruct((2,) + tokens.shape, bf16),
+        ),
+        grid_spec=pltpu.PrefetchScalarGridSpec(
+            num_scalar_prefetch=2,
+            grid=(1,),
+            in_specs=[
+                pl.BlockSpec((32, wide), lambda i, place, lens: (place[0], 0)),
+                pl.BlockSpec((32, up_wide), lambda i, place, lens: (place[0], 0)),
+                pl.BlockSpec(tokens.shape, lambda i, place, lens: (0, 0)),
+                pl.BlockSpec(tokens.shape, lambda i, place, lens: (0, 0)),
+            ]
+            + [pl.BlockSpec(v.shape, lambda i, place, lens: (0, 0)) for v in vectors],
+            out_specs=(
+                pl.BlockSpec((8, 40, cols), lambda i, place, lens: (0, 0, 0)),
+                pl.BlockSpec((2,) + tokens.shape, lambda i, place, lens: (0, 0, 0)),
+            ),
+        ),
+        compiler_params=kernel_params(),
+        cost_estimate=cost(3),
+        name="packed",
+    )(place, lengths, qkv_weight, up_weight, tokens, cotangent, *vectors)
+
+
 def attend(h1, dy, weight, spots, out, bias, cosine, sine, lengths, numbers, after, rows=128):
     total, width = h1.shape
     count = len(dy)
@@ -364,26 +416,27 @@
         dq_copy = pltpu.make_async_copy(dq_v, dq_hbm, sems.at[1])
         dq_copy.start()
 
-        def split(part, high, wide):
-            at = (slice(None), high, wide)
-
-            @pl.when(own)
-            def _():
-                keep_v[at] = part[:, 0]
-                send_v[at] = part[:, 1]
-
-            @pl.when(jnp.logical_not(own))
-            def _():
-                keep_v[at] = part[:, 1]
-                send_v[at] = part[:, 0]
-
-        part = dot_rows(ol_v[...], dy_v[...]).astype(bf16).reshape(8, 2, 16, width)
+        def split(part, high, lanes):
+            for z_hi in range(2):
+                at = (pl.ds(4 * z_hi, 4), high, lanes)
+
+                @pl.when(own)
+                def _(z_hi=z_hi, at=at):
+                    keep_v[at] = part[:, z_hi, 0]
+                    send_v[at] = part[:, z_hi, 1]
+
+                @pl.when(jnp.logical_not(own))
+                def _(z_hi=z_hi, at=at):
+                    keep_v[at] = part[:, z_hi, 1]
+                    send_v[at] = part[:, z_hi, 0]
+
+        part = dot_rows(ol_v[...], dy_v[...]).astype(bf16).reshape(4, 2, 2, 16, width)
         split(part, pl.ds(48, 16), slice(None))
 
         @pl.loop(0, 8)
         def _(n):
             lanes = pl.ds(pl.multiple_of(n * 256, 256), 256)
-            part = dot_rows(h1_v[:, lanes], dq_v[...]).astype(bf16).reshape(8, 2, 16, 3 * head)
+            part = dot_rows(h1_v[:, lanes], dq_v[...]).astype(bf16).reshape(4, 2, 2, 16, 3 * head)
             for third in range(3):
                 split(
                     part[..., third * head : (third + 1) * head],
@@ -447,122 +500,45 @@
     )
 
 
-def mixed_part(active, attended, down, out, bias, sources, after):
-    rows, ff = active.shape
+def outer(d_qkv, d_hidden, weight, spots, x, mean, inverse, gains, active, attended, down, out, bias, after):
+    total, n1 = d_qkv.shape
+    n2 = d_hidden.shape[1]
+    count = len(x)
+    parts = len(weight)
     head, width = out.shape
     step = 512
 
-    def body(source_ref, act_ref, ol_ref, wd_ref, wo_ref, b_ref, mix_ref):
-        total = dot(act_ref[...], wd_ref[...]) + dot(ol_ref[...], wo_ref[...]) + b_ref[...]
-        total = total.astype(bf16)
-        for at in range(rows // 128):
-            to = pl.ds(pl.multiple_of(source_ref[at] * 128, 128), 128)
-            mix_ref[to, :] = total[at * 128 : (at + 1) * 128]
-
-    return pl.pallas_call(
-        after_inputs(body, 6, len(after)),
-        out_shape=jax.ShapeDtypeStruct((rows, width), bf16),
-        grid_spec=pltpu.PrefetchScalarGridSpec(
-            num_scalar_prefetch=1,
-            grid=(width // step,),
-            in_specs=[
-                pl.BlockSpec((rows, ff), lambda i, n: (0, 0)),
-                pl.BlockSpec((rows, head), lambda i, n: (0, 0)),
-                pl.BlockSpec((ff, step), lambda i, n: (0, i)),
-                pl.BlockSpec((head, step), lambda i, n: (0, i)),
-                pl.BlockSpec((1, step), lambda i, n: (0, i)),
-            ]
-            + anywhere(len(after)),
-            out_specs=pl.BlockSpec((rows, step), lambda i, n: (0, i)),
-        ),
-        compiler_params=kernel_params(),
-        cost_estimate=cost(10),
-        name="mixed_part",
-    )(sources, active, attended, down, out, bias, *after)
-
-
-def packed(qkv_weight, up_weight, vectors, lengths, place, head, tokens, cotangent):
-    wide, up_wide = qkv_weight.shape[1], up_weight.shape[1]
-    part, up_part = 3 * head, up_wide // 8
-    cols = part + up_part
-
-    def body(place_ref, len_ref, q_ref, u_ref, x_ref, dy_ref, *refs):
-        v_refs, out_ref, pair_ref = refs[: len(vectors)], refs[-2], refs[-1]
-        pair_ref[0] = x_ref[...]
-        pair_ref[1] = dy_ref[...]
-        lane = lax.broadcasted_iota(jnp.int32, (8, cols), 1)
-        row = lax.broadcasted_iota(jnp.int32, (8, cols), 0)
-        sizes = jnp.zeros((8, cols), f32)
-        for at in range(3):
-            sizes = jnp.where(lane == at, len_ref[0, at].astype(f32), sizes)
-        vector = jnp.concatenate([ref[...].astype(f32) for ref in v_refs], 1)
-        vector = jnp.broadcast_to(vector, (8, cols))
-        tail = jnp.where(row == 0, vector, jnp.where(row == 1, sizes, 0.0)).astype(bf16)
-        for owner in range(8):
-            pieces = [
-                q_ref[:, (third * 8 + owner) * head : (third * 8 + owner + 1) * head]
-                for third in range(3)
-            ]
-            pieces.append(u_ref[:, owner * up_part : (owner + 1) * up_part])
-            out_ref[owner] = jnp.concatenate([jnp.concatenate(pieces, 1), tail], 0)
-
-    return pl.pallas_call(
-        body,
-        out_shape=(
-            jax.ShapeDtypeStruct((8, 40, cols), bf16),
-            jax.ShapeDtypeStruct((2,) + tokens.shape, bf16),
-        ),
-        grid_spec=pltpu.PrefetchScalarGridSpec(
-            num_scalar_prefetch=2,
-            grid=(1,),
-            in_specs=[
-                pl.BlockSpec((32, wide), lambda i, place, lens: (place[0], 0)),
-                pl.BlockSpec((32, up_wide), lambda i, place, lens: (place[0], 0)),
-                pl.BlockSpec(tokens.shape, lambda i, place, lens: (0, 0)),
-                pl.BlockSpec(tokens.shape, lambda i, place, lens: (0, 0)),
-            ]
-            + [pl.BlockSpec(v.shape, lambda i, place, lens: (0, 0)) for v in vectors],
-            out_specs=(
-                pl.BlockSpec((8, 40, cols), lambda i, place, lens: (0, 0, 0)),
-                pl.BlockSpec((2,) + tokens.shape, lambda i, place, lens: (0, 0, 0)),
-            ),
-        ),
-        compiler_params=kernel_params(),
-        cost_estimate=cost(3),
-        name="packed",
-    )(place, lengths, qkv_weight, up_weight, tokens, cotangent, *vectors)
-
-
-def back_norms(d_qkv, d_hidden, weight, spots, tokens, mean, inverse, gains, after):
-    total, n1 = d_qkv.shape
-    n2 = d_hidden.shape[1]
-    count = len(tokens)
-    parts = len(weight)
-    width = tokens[0].shape[-1]
-    step = 512
-
-    def body(spot_ref, m_ref, i_ref, g_ref, *refs):
-        w_refs, x_refs = refs[:parts], refs[parts : parts + count]
-        dq_hbm, du_hbm = refs[parts + count : parts + count + 2]
-        sums_ref = refs[parts + count + 2]
-        outs = refs[parts + count + 3 : parts + 2 * count + 3]
-        dq_v, du_v, w_v, x_v, s_v, w_sem, x_sem, sems = refs[parts + 2 * count + 3 :]
+    def body(spot_ref, m_ref, i_ref, g_ref, b_ref, *refs):
+        w_refs, refs = refs[:parts], refs[parts:]
+        x_refs, refs = refs[:count], refs[count:]
+        plain, sums_ref, outs = refs[:6], refs[6], refs[7 : 7 + count]
+        dq_v, du_v, act_v, ol_v, wd_v, wo_v, w_v, x_v, pair_v, w_sem, x_sem, sems, out_sem = refs[
+            7 + count :
+        ]
+        plain_v = (dq_v, du_v, act_v, ol_v, wd_v, wo_v)
         copies = loads(
             [
-                pltpu.make_async_copy(dq_hbm, dq_v, sems.at[0]),
-                pltpu.make_async_copy(du_hbm, du_v, sems.at[1]),
+                pltpu.make_async_copy(source, target, sems.at[n])
+                for n, (source, target) in enumerate(zip(plain[:2], plain_v[:2]))
             ]
             + weight_copies(weight, w_refs, spot_ref, w_v, slice(None), w_sem)
             + piece_copies(x_refs, 0, x_v, x_sem, 128)
         )
+        later = loads(
+            [
+                pltpu.make_async_copy(plain[n], plain_v[n], sems.at[n]) for n in range(2, 6)
+            ]
+        )
         for copy in copies:
             copy.wait()
 
-        def leaving(n):
+        def leaving(n, half):
             lanes = pl.ds(pl.multiple_of(n * step, step), step)
             return [
                 pltpu.make_async_copy(
-                    s_v.at[pl.ds(at * 128, 128), lanes], outs[at].at[:, lanes], x_sem.at[at]
+                    pair_v.at[half, pl.ds(at * 128, 128), lanes],
+                    outs[at].at[half, :, lanes],
+                    out_sem.at[half, at],
                 )
                 for at in range(count)
             ]
@@ -573,8 +549,8 @@
             sources = pl.ds(n * (step // 256), step // 256)
             d1 = dot(dq_v[...], w_v[sources, :, :, 0:n1].reshape(step, n1), 1, 1)
             d2 = dot(du_v[...], w_v[sources, :, :, n1:].reshape(step, n2), 1, 1)
-            s_v[:, lanes] = (d1 * g_ref[0:1, lanes] + d2 * g_ref[1:2, lanes]).astype(bf16)
-            for copy in leaving(n):
+            pair_v[1, :, lanes] = (d1 * g_ref[0:1, lanes] + d2 * g_ref[1:2, lanes]).astype(bf16)
+            for copy in leaving(n, 1):
                 copy.start()
             normed = (x_v[:, lanes].astype(f32) - m_ref[...]) * i_ref[...]
             sums_ref[0:1, lanes] = jnp.sum(d1 * normed, 0, keepdims=True)
@@ -582,32 +558,65 @@
             sums_ref[2:3, lanes] = jnp.sum(d2 * normed, 0, keepdims=True)
             sums_ref[3:4, lanes] = jnp.sum(d2, 0, keepdims=True)
 
+        for copy in later:
+            copy.wait()
+
+        @pl.loop(0, width // step)
+        def _(n):
+            lanes = pl.ds(pl.multiple_of(n * step, step), step)
+            mix = dot(act_v[...], wd_v[:, lanes]) + dot(ol_v[...], wo_v[:, lanes])
+            pair_v[0, :, lanes] = (mix + b_ref[:, lanes]).astype(bf16)
+            for copy in leaving(n, 0):
+                copy.start()
+
         for n in range(width // step):
-            for copy in leaving(n):
-                copy.wait()
+            for half in range(2):
+                for copy in leaving(n, half):
+                    copy.wait()
 
     vmem = pl.BlockSpec(memory_space=pltpu.VMEM)
     return pl.pallas_call(
-        after_inputs(body, 6 + parts + count, len(after)),
+        after_inputs(body, 11 + parts + count, len(after)),
         out_shape=(jax.ShapeDtypeStruct((4, width), f32),)
-        + (jax.ShapeDtypeStruct((128, width), bf16),) * count,
-        in_specs=[pl.BlockSpec(memory_space=pltpu.SMEM), vmem, vmem, vmem]
-        + anywhere(parts + count + 2 + len(after)),
+        + (jax.ShapeDtypeStruct((2, 128, width), bf16),) * count,
+        in_specs=[pl.BlockSpec(memory_space=pltpu.SMEM)]
+        + [vmem] * 4
+        + anywhere(parts + count + 6 + len(after)),
         out_specs=(vmem,) + tuple(anywhere(count)),
         scratch_shapes=[
             pltpu.VMEM((total, n1), bf16),
             pltpu.VMEM((total, n2), bf16),
+            pltpu.VMEM((total, n2), bf16),
+            pltpu.VMEM((total, head), bf16),
+            pltpu.VMEM((n2, width), bf16),
+            pltpu.VMEM((head, width), bf16),
             pltpu.VMEM((8, 8, width // 64, n1 + n2), bf16),
             pltpu.VMEM((total, width), bf16),
-            pltpu.VMEM((total, width), bf16),
+            pltpu.VMEM((2, total, width), bf16),
             pltpu.SemaphoreType.DMA((parts,)),
             pltpu.SemaphoreType.DMA((count,)),
-            pltpu.SemaphoreType.DMA((2,)),
+            pltpu.SemaphoreType.DMA((6,)),
+            pltpu.SemaphoreType.DMA((2, count)),
         ],
         compiler_params=kernel_params(),
-        cost_estimate=cost(14),
-        name="back_norms",
-    )(spots, mean, inverse, gains, *[p[0] for p in weight], *tokens, d_qkv, d_hidden, *after)
+        cost_estimate=cost(20),
+        name="outer",
+    )(
+        spots,
+        mean,
+        inverse,
+        gains,
+        bias,
+        *[p[0] for p in weight],
+        *x,
+        d_qkv,
+        d_hidden,
+        active,
+        attended,
+        down,
+        out,
+        *after,
+    )
 
 
 def unpacked(part, after):
@@ -632,92 +641,146 @@
     )(part, *after)
 
 
-def halves(below, above, after):
-    count, rows, cols = below.shape
-    half = (count // 2, rows, cols) if count > 1 else (1, rows // 2, cols)
-    at = (1, 0, 0) if count > 1 else (0, 1, 0)
-
-    def body(below_ref, above_ref, low_ref, high_ref):
-        low_ref[...] = below_ref[...]
-        high_ref[...] = above_ref[...]
-
-    out = jax.ShapeDtypeStruct(half, bf16)
-    return pl.pallas_call(
-        after_inputs(body, 2, len(after)),
-        out_shape=(out, out),
-        grid=(1,),
-        in_specs=[
-            pl.BlockSpec(half, lambda i: (0, 0, 0)),
-            pl.BlockSpec(half, lambda i: at),
-        ]
-        + anywhere(len(after)),
-        out_specs=(pl.BlockSpec(half, lambda i: (0, 0, 0)),) * 2,
-        compiler_params=kernel_params(),
-        cost_estimate=cost(3),
-        name="halves",
-    )(below, above, *after)
-
-
-def packed_sums(inner, own, below, above, ff, head, after):
-    width = inner.shape[1]
-
-    def body(inner_ref, own_ref, below_ref, above_ref, out_ref, down_ref, stay_ref):
-        total = own_ref[...].astype(f32) + below_ref[...].astype(f32) + above_ref[...].astype(f32)
-        total = total.astype(bf16)
+def packed_sums(stays, crossed, own, below, above, ff, head, after):
+    width = own.shape[1]
+
+    def body(stay_ref, cross_ref, own_ref, below_ref, above_ref, out_ref, keep_ref):
+        inner = (stay_ref[0].astype(f32) + cross_ref[0].astype(f32)).astype(bf16)
+        total = wide(own_ref, below_ref, above_ref).astype(bf16)
         for owner in range(8):
             pieces = [
                 total[16 * third : 16 * third + 16, owner * head : (owner + 1) * head]
                 for third in range(3)
             ]
             row, col = 64 + 16 * (owner % 4), owner // 4 * ff
-            pieces.append(inner_ref[row : row + 16, col : col + ff])
+            pieces.append(inner[row : row + 16, col : col + ff])
             out_ref[owner] = jnp.concatenate(pieces, 1)
-        down_ref[...] = inner_ref[0:64, :]
-        stay_ref[...] = total[48:64]
+        keep_ref[0:64] = inner[0:64]
+        keep_ref[64:80] = total[48:64]
 
     vmem = pl.BlockSpec(memory_space=pltpu.VMEM)
     return pl.pallas_call(
-        after_inputs(body, 4, len(after)),
+        after_inputs(body, 5, len(after)),
         out_shape=(
             jax.ShapeDtypeStruct((8, 16, 3 * head + ff), bf16),
-            jax.ShapeDtypeStruct((64, width), bf16),
-            jax.ShapeDtypeStruct((16, width), bf16),
+            jax.ShapeDtypeStruct((80, width), bf16),
         ),
-        in_specs=[vmem] * 4 + anywhere(len(after)),
-        out_specs=(vmem,) * 3,
+        in_specs=[vmem] * 5 + anywhere(len(after)),
+        out_specs=(vmem,) * 2,
         compiler_params=kernel_params(),
         cost_estimate=cost(3),
         name="packed_sums",
-    )(inner, own, below, above, *after)
-
-
-def unpacked_sums(part, down, stay, ff, head, after):
-    width = down.shape[1]
-
-    def body(part_ref, down_ref, stay_ref, inner_ref, out_ref):
-        inner_ref[0:64] = down_ref[...]
-        out_ref[48:64] = stay_ref[...]
-        for source in range(8):
-            for third in range(3):
-                out_ref[16 * third : 16 * third + 16, source * head : (source + 1) * head] = part_ref[
-                    source, :, third * head : (third + 1) * head
-                ]
-            row, col = 64 + 16 * (source % 4), source // 4 * ff
-            inner_ref[row : row + 16, col : col + ff] = part_ref[source, :, 3 * head :]
-
-    vmem = pl.BlockSpec(memory_space=pltpu.VMEM)
+    )(stays, crossed, own, below, above, *after)
+
+
+def stayed(parts, after):
+    count, _, width = parts.shape
+    step = 4
+
+    def body(part_ref, down_ref, out_ref):
+        for at in range(step):
+            down_ref[at * 64 : (at + 1) * 64] = part_ref[at, 0:64].astype(f32)
+            out_ref[at * 16 : (at + 1) * 16] = part_ref[at, 64:80].astype(f32)
+
     return pl.pallas_call(
-        after_inputs(body, 3, len(after)),
+        after_inputs(body, 1, len(after)),
         out_shape=(
-            jax.ShapeDtypeStruct((128, width), bf16),
-            jax.ShapeDtypeStruct((64, width), bf16),
+            jax.ShapeDtypeStruct((count * 64, width), f32),
+            jax.ShapeDtypeStruct((count * 16, width), f32),
         ),
-        in_specs=[vmem] * 3 + anywhere(len(after)),
-        out_specs=(vmem,) * 2,
+        grid=(count // step,),
+        in_specs=[pl.BlockSpec((step, 80, width), lambda i: (i, 0, 0))] + anywhere(len(after)),
+        out_specs=(
+            pl.BlockSpec((step * 64, width), lambda i: (i, 0)),
+            pl.BlockSpec((step * 16, width), lambda i: (i, 0)),
+        ),
+        compiler_params=kernel_params(),
+        cost_estimate=cost(6),
+        name="stayed",
+    )(parts, *after)
+
+
+def halves(below, above, x_pair, dy_pair, after):
+    count, rows, cols = below.shape
+    _, tokens, width = x_pair.shape
+    half = (count // 2, rows, cols)
+
+    def body(below_ref, above_ref, x_ref, dy_ref, low_ref, high_ref, x_out, dy_out):
+        low_ref[...] = below_ref[...]
+        high_ref[...] = above_ref[...]
+        x_out[...] = x_ref[0]
+        dy_out[...] = dy_ref[0]
+
+    def at(block, first):
+        return pl.BlockSpec(block, lambda i: (first,) + (0,) * (len(block) - 1))
+
+    return pl.pallas_call(
+        after_inputs(body, 4, len(after)),
+        out_shape=(jax.ShapeDtypeStruct(half, bf16),) * 2
+        + (jax.ShapeDtypeStruct((tokens, width), bf16),) * 2,
+        grid=(1,),
+        in_specs=[
+            at(half, 0),
+            at(half, 1),
+            at((1, tokens, width), 0),
+            at((1, tokens, width), 1),
+        ]
+        + anywhere(len(after)),
+        out_specs=(at(half, 0), at(half, 0), at((tokens, width), 0), at((tokens, width), 0)),
         compiler_params=kernel_params(),
         cost_estimate=cost(3),
-        name="unpacked_sums",
-    )(part, down, stay, *after)
+        name="halves",
+    )(below, above, x_pair, dy_pair, *after)
+
+
+def joined(arrays, after):
+    size, rows, cols = arrays[0].shape
+    count = len(arrays)
+
+    def body(*refs):
+        for at in range(count):
+
+            @pl.when(pl.program_id(0) == at)
+            def _(at=at):
+                refs[count][...] = refs[at][...]
+
+    block = pl.BlockSpec((size, rows, cols), lambda i: (0, 0, 0))
+    return pl.pallas_call(
+        after_inputs(body, count, len(after)),
+        out_shape=jax.ShapeDtypeStruct((size * count, rows, cols), bf16),
+        grid=(count,),
+        in_specs=[block] * count + anywhere(len(after)),
+        out_specs=pl.BlockSpec((size, rows, cols), lambda i: (i, 0, 0)),
+        compiler_params=kernel_params(),
+        cost_estimate=cost(3),
+        name="joined",
+    )(*arrays, *after)
+
+
+def blocks_call(name, body, numbers, terms, outs, after):
+    def came(block, index):
+        rest = (0,) * (len(block) - 1)
+        return pl.BlockSpec(block, lambda i, n: (index(n),) + rest)
+
+    return pl.pallas_call(
+        after_inputs(body, 1 + len(terms), len(after)),
+        out_shape=tuple(jax.ShapeDtypeStruct(out, bf16) for out in outs),
+        grid_spec=pltpu.PrefetchScalarGridSpec(
+            num_scalar_prefetch=1,
+            grid=(1,),
+            in_specs=[came(block, index) for _, block, index in terms] + anywhere(len(after)),
+            out_specs=tuple(
+                pl.BlockSpec(out, lambda i, n, size=len(out): (0,) * size) for out in outs
+            ),
+        ),
+        compiler_params=kernel_params(),
+        cost_estimate=cost(3),
+        name=name,
+    )(numbers, *[array for array, _, _ in terms], *after)
+
+
+def wide(*refs):
+    return functools.reduce(jnp.add, [ref[...].astype(f32) for ref in refs])
 
 
 def spread(pieces, places, core, targets, count, before, after):
@@ -821,47 +884,6 @@
     )(numbers, norm_sums, qkv_sums, up_sums, dy_sums)
 
 
-def added(terms, groups, numbers, after):
-    rows, cols = terms[0][0].shape[1:]
-    firsts = [sum(groups[:n]) for n in range(len(groups))]
-
-    def body(number_ref, *refs):
-        step = pl.program_id(0)
-        total = None
-        for ref, (_, _, steps) in zip(refs, terms):
-            value = ref[0].astype(f32)
-            if steps is not None:
-                counts = functools.reduce(jnp.logical_or, [step == at for at in steps])
-                value = jnp.where(counts, value, 0.0)
-            total = value if total is None else total + value
-        total = total.astype(bf16)
-        for ref, first, size in zip(refs[len(terms) :], firsts, groups):
-
-            @pl.when((step >= first) & (step < first + size))
-            def _(ref=ref):
-                ref[0] = total
-
-    def came(place):
-        return pl.BlockSpec((1, rows, cols), lambda i, n: (place(i, n), 0, 0))
-
-    def goes(first, size):
-        return pl.BlockSpec((1, rows, cols), lambda i, n: (jnp.clip(i - first, 0, size - 1), 0, 0))
-
-    return pl.pallas_call(
-        after_inputs(body, 1 + len(terms), len(after)),
-        out_shape=tuple(jax.ShapeDtypeStruct((size, rows, cols), bf16) for size in groups),
-        grid_spec=pltpu.PrefetchScalarGridSpec(
-            num_scalar_prefetch=1,
-            grid=(sum(groups),),
-            in_specs=[came(place) for _, place, _ in terms] + anywhere(len(after)),
-            out_specs=tuple(goes(first, size) for first, size in zip(firsts, groups)),
-        ),
-        compiler_params=kernel_params(),
-        cost_estimate=cost(4),
-        name="added",
-    )(numbers, *[term[0] for term in terms], *after)
-
-
 def local(
     tokens,
     doc_lengths,
@@ -896,21 +918,32 @@
     )
     below, above, other = move(pair, x=1), move(pair, x=-1), move(pair, l=1)
     far, other_above, other_below = move(below, x=1), move(other, x=-1), move(below, l=1)
-    x_other_far, dy_other_far = move(other_below[0], x=1), move(other_above[1], x=-1)
     pairs = (pair, above, far, below, other, other_above, None, other_below)
-    x_all = tuple(x_other_far if p is None else p for p in pairs)
-    dy_all = tuple(dy_other_far if p is None else p for p in pairs)
 
     part = lax.all_to_all(part, "shard", 0, 0)
     own, infos = unpacked(part, (pairs[1], pairs[3], pairs[4]))
     below, above = move(own, y=1), move(own, y=-1)
-    low, high = halves(below, above, (pairs[2], pairs[5], pairs[7]))
+    low, high, x_half, dy_half = halves(below, above, other_below, other_above, (far,))
     far_low, far_high = move(low, y=1), move(high, y=-1)
-    mine = ((own, 0, 0), (above, 0, 1), (far_low, 0, 2), (far_high, 4, 2), (below, 0, 3))
-    yours = tuple((move(array, c=1), first, spot + 4) for array, first, spot in mine)
+    x_other_far, dy_other_far = move(x_half, x=1), move(dy_half, x=-1)
+    x_all = tuple(x_other_far if p is None else p for p in pairs)
+    dy_all = tuple(dy_other_far if p is None else p for p in pairs)
+    yours = move(joined((own, above, below), (low,)), c=1)
+    far_low_c, far_high_c = move(far_low, c=1), move(far_high, c=1)
+    weight = (
+        (own, 0, 8, 0, 0),
+        (above, 0, 8, 0, 1),
+        (far_low, 0, 4, 0, 2),
+        (far_high, 0, 4, 4, 2),
+        (below, 0, 8, 0, 3),
+        (yours, 0, 8, 0, 4),
+        (yours, 8, 8, 0, 5),
+        (far_low_c, 0, 4, 0, 6),
+        (far_high_c, 0, 4, 4, 6),
+        (yours, 16, 8, 0, 7),
+    )
     steps4 = (y + jnp.arange(4)) % 4
     spots = jnp.concatenate([steps4 * 2 + c, steps4 * 2 + 1 - c]).astype(jnp.int32)
-    weight = mine + yours
 
     gains = infos[:, 0, :1024].reshape(8, 4, 256).transpose(1, 0, 2).reshape(4, width)
     qkv_b = infos[:, 0, 1024:].reshape(8 * 3, 1, head)
@@ -961,13 +994,27 @@
         h1, dy_all, weight, spots, out_weight, qkv_b, cosine, sine, lengths, numbers, (send,)
     )
 
+    pair_shape, one = (2, 128, width), (1, 128, width)
+
     def turn(k):
-        return lambda i, n: (n[2] + k) % 4 * 2 + i % 2
-
-    low, high = added([(keep, turn(2), None), (got, turn(2), None)], (1, 1), numbers, (attended,))
+        return lambda n: (n[2] + k) % 4
+
+    def far_body(n_ref, keep_ref, got_ref, low_ref, high_ref):
+        total = wide(keep_ref, got_ref).astype(bf16)
+        low_ref[0] = total[0]
+        high_ref[0] = total[1]
+
+    low, high = blocks_call(
+        "far_sums",
+        far_body,
+        numbers,
+        [(keep, pair_shape, turn(2)), (got, pair_shape, turn(2))],
+        (one, one),
+        (attended,),
+    )
     from_low, from_high = move(low, y=1), move(high, y=-1)
     a_got = move(a_send, c=1)
-    norm_sums, *sums = back_norms(
+    norm_sums, *pairs_out = outer(
         d_qkv,
         d_hidden,
         weight,
@@ -976,108 +1023,70 @@
         mean,
         inverse,
         jnp.stack([gains[0], gains[2]]),
+        active,
+        attended,
+        down_weight,
+        out_weight,
+        wide_bias,
         (low, high),
     )
 
-    def sides(i, n):
-        return (n[2] + 1 + i // 2 * 2) % 4 * 2 + i % 2
-
-    above, below = added(
-        [
-            (keep, sides, None),
-            (got, sides, None),
-            (from_low, lambda i, n: 0, (0,)),
-            (from_high, lambda i, n: 0, (3,)),
-        ],
-        (2, 2),
+    def near_body(n_ref, k1_ref, g1_ref, k3_ref, g3_ref, low_ref, high_ref, above_ref, below_ref):
+        above, below = wide(k1_ref, g1_ref), wide(k3_ref, g3_ref)
+        above_ref[0] = (above[0] + low_ref[0].astype(f32)).astype(bf16)
+        above_ref[1] = above[1].astype(bf16)
+        below_ref[0] = below[0].astype(bf16)
+        below_ref[1] = (below[1] + high_ref[0].astype(f32)).astype(bf16)
+
+    above, below = blocks_call(
+        "near_sums",
+        near_body,
         numbers,
-        (sums[0],),
+        [(v, pair_shape, turn(k)) for k in (1, 3) for v in (keep, got)]
+        + [(v, one, lambda n: 0) for v in (from_low, from_high)],
+        (pair_shape, pair_shape),
+        (pairs_out[0],),
     )
     from_below, from_above = move(above, y=1), move(below, y=-1)
-    def away(i, n):
-        return i * 2 + 1 - n[3]
-
-    (a_away,) = added([(a_keep, away, None), (a_got, away, None)], (4,), numbers, (above,))
+
+    four, part_shape = (4, 64, width), (1, 64, width)
+
+    def away_body(n_ref, keep_ref, got_ref, out_ref):
+        out_ref[...] = wide(keep_ref, got_ref).astype(bf16)
+
+    (a_away,) = blocks_call(
+        "away_sums",
+        away_body,
+        numbers,
+        [(v, four, lambda n: 1 - n[3]) for v in (a_keep, a_got)],
+        (four,),
+        (above,),
+    )
     a_crossed = move(a_away, h=1)
-    mix = mixed_part(
-        active, attended, down_weight, out_weight, wide_bias, sources, (above, below, a_away)
-    )
 
     smalls = small_sums(norm_sums, qkv_sums, up_sums, dy_sums, numbers)
     smalls = jnp.broadcast_to(smalls[None], (16, 8, 24, 128)).reshape(128, 24, 128)
     smalls = lax.all_to_all(smalls, BOTH, 0, 0)
     smalls = jnp.sum(smalls.astype(f32), 0)
 
-    def ends_at(i, n):
-        return n[2] * 2 + jnp.where(i == 0, 1 - n[3], n[3])
-
-    def crosses(i, n):
-        return jnp.where(i == 0, 1 - n[3], n[3])
-
-    leaves, inner = added(
-        [
-            (keep, ends_at, None),
-            (got, ends_at, None),
-            (from_below, crosses, None),
-            (from_above, crosses, None),
-        ],
-        (1, 1),
-        numbers,
-        (mix,),
-    )
-    crossed = move(leaves, h=1)
-
-    def around(i, n):
-        return (n[2] + 2 - i) % 4
-
-    def around_here(i, n):
-        return around(i, n) * 2 + n[3]
-
-    a_far, a_above, a_own, a_below = added(
-        [
-            (a_keep, around_here, None),
-            (a_got, around_here, None),
-            (a_crossed, around, None),
-        ],
-        (1, 1, 1, 1),
-        numbers,
-        (),
-    )
-    a_low, a_high = move(a_far[0, :32], y=1), move(a_far[0, 32:], y=-1)
-    ((inner,),) = added(
-        [(inner, lambda i, n: 0, None), (crossed, lambda i, n: 0, None)],
-        (1,),
-        numbers,
-        (a_low, a_high),
-    )
-    a_above = jnp.concatenate(
-        [a_above[0, :32].astype(f32) + a_low.astype(f32), a_above[0, 32:].astype(f32)], 0
-    )
-    a_below = jnp.concatenate(
-        [a_below[0, :32].astype(f32), a_below[0, 32:].astype(f32) + a_high.astype(f32)], 0
-    )
-    a_from_below, a_from_above = move(a_above.astype(bf16), y=1), move(a_below.astype(bf16), y=-1)
-
-    part, down_stays, out_stays = packed_sums(
-        inner, a_own[0], a_from_below, a_from_above, ff, head, (smalls,)
-    )
-    part = lax.all_to_all(part, "shard", 0, 0)
-    inner, a_sum = unpacked_sums(part, down_stays, out_stays, ff, head, ())
-    inner_other = move(inner, h=1)
-    inner = jnp.stack([inner, inner_other])
-
-    def ring(pieces, way):
-        own, above, far, below = pieces if way == 1 else (pieces[n] for n in (0, 3, 2, 1))
-        passed = move(far, x=way)
+    def ring_start(pieces, way):
+        return move(pieces[2], x=way)
+
+    def ring_middle(pieces, passed, way):
+        above, below = (pieces[1], pieces[3]) if way == 1 else (pieces[3], pieces[1])
         above = (above.astype(f32) + passed.astype(f32)).astype(bf16)
-        return (
-            own.astype(f32) + move(above, x=way).astype(f32) + move(below, x=-way).astype(f32)
-        )
-
-    sum_other = move(ring(sums[4:], 1).astype(bf16), l=1)
-    own_sum = ring(sums[:4], -1) + sum_other.astype(f32)
-    mixed = lax.psum_scatter(mix, "shard", scatter_dimension=0, tiled=True)
-    mixed = (tokens.astype(f32) + mixed.astype(f32)).astype(bf16)
+        return move(above, x=way), move(below, x=-way)
+
+    def ring_end(pieces, arrived):
+        return functools.reduce(jnp.add, [v.astype(f32) for v in (pieces[0],) + arrived])
+
+    passed_other, passed_own = ring_start(pairs_out[4:], 1), ring_start(pairs_out[:4], -1)
+    arrived_other = ring_middle(pairs_out[4:], passed_other, 1)
+    arrived_own = ring_middle(pairs_out[:4], passed_own, -1)
+    total_other = move(ring_end(pairs_out[4:], arrived_other).astype(bf16), l=1)
+    totals = ring_end(pairs_out[:4], arrived_own) + total_other.astype(f32)
+    mixed = (tokens.astype(f32) + totals[0]).astype(bf16)
+    own_sum = totals[1]
     own_normed, own_inverse = normalize(tokens)
     tokens_grad = cotangent.astype(f32) + own_inverse * (
         own_sum
@@ -1085,43 +1094,92 @@
         - own_normed * jnp.mean(own_sum * own_normed, -1, keepdims=True)
     )
 
+    def ends_body(n_ref, keep_ref, got_ref, below_ref, above_ref, leave_ref, stay_ref):
+        total = wide(keep_ref, got_ref, below_ref, above_ref).astype(bf16)
+        first = n_ref[3] == 0
+        leave_ref[0] = jnp.where(first, total[1], total[0])
+        stay_ref[0] = jnp.where(first, total[0], total[1])
+
+    leaves, stays = blocks_call(
+        "end_sums",
+        ends_body,
+        numbers,
+        [(v, pair_shape, turn(0)) for v in (keep, got)]
+        + [(v, pair_shape, lambda n: 0) for v in (from_below, from_above)],
+        (one, one),
+        (a_away, passed_other, passed_own),
+    )
+    crossed = move(leaves, h=1)
+
+    def around_body(n_ref, keep_ref, got_ref, crossed_ref, low_ref, high_ref, above_ref, own_ref, below_ref):
+        def part(k):
+            at = (n_ref[2] + k) % 4
+            return wide(keep_ref.at[at], got_ref.at[at], crossed_ref.at[at]).astype(bf16)
+
+        far = part(2)
+        low_ref[...] = far[:32]
+        high_ref[...] = far[32:]
+        above_ref[...] = part(1)
+        own_ref[...] = part(0)
+        below_ref[...] = part(3)
+
+    a_low, a_high, a_above, a_own, a_below = blocks_call(
+        "around_sums",
+        around_body,
+        numbers,
+        [(v, four, lambda n: n[3]) for v in (a_keep, a_got)] + [(a_crossed, four, lambda n: 0)],
+        ((32, width), (32, width), (64, width), (64, width), (64, width)),
+        (leaves,),
+    )
+    a_low, a_high = move(a_low, y=1), move(a_high, y=-1)
+
+    def beside_body(n_ref, above_ref, below_ref, low_ref, high_ref, up_ref, down_ref):
+        up_ref[0:32] = (above_ref[0:32].astype(f32) + low_ref[...].astype(f32)).astype(bf16)
+        up_ref[32:64] = above_ref[32:64]
+        down_ref[0:32] = below_ref[0:32]
+        down_ref[32:64] = (below_ref[32:64].astype(f32) + high_ref[...].astype(f32)).astype(bf16)
+
+    a_above, a_below = blocks_call(
+        "beside_sums",
+        beside_body,
+        numbers,
+        [(v, v.shape, lambda n: 0) for v in (a_above, a_below, a_low, a_high)],
+        ((64, width), (64, width)),
+        (),
+    )
+    a_from_below, a_from_above = move(a_above, y=1), move(a_below, y=-1)
+
+    part, stays = packed_sums(
+        stays, crossed, a_own, a_from_below, a_from_above, ff, head, (smalls, *arrived_other)
+    )
+    stays = lax.all_gather(stays, "rep", axis=0)
+    part = lax.all_to_all(part, "shard", 0, 0).reshape(1, 128, cols)
+
+    part = jnp.concatenate([part, move(part, h=1)])
+    below, above = move(part, y=1), move(part, y=-1)
+    far_low, far_high = move(below[:1], y=1), move(above[1:], y=-1)
+    pieces = [(v, move(v, c=1)) for v in (part, above, below, far_low, far_high)]
+    order = ((0, h), (0, 1 - h), (1, h), (1, 1 - h), (3, h), (3, 1 - h), (2, h), (2, 1 - h))
+    places = jnp.stack([(y + k) % 4 * 2 + high for k, high in order]).astype(jnp.int32)
+    targets = [
+        (
+            3 * width,
+            16,
+            [
+                ((third * 8 + source) * head, 16 * source, third * head, head)
+                for source in range(8)
+                for third in range(3)
+            ],
+        ),
+        (8 * ff, 16, [(source * ff, 16 * source, 3 * head, ff) for source in range(8)]),
+    ]
+    down_grad, out_grad = stayed(stays, ())
+    grads = spread(pieces[:3], places[:6], numbers[:1], targets, 8, (), ())
+    qkv_grad, up_grad = spread(
+        pieces[3:], places[6:], numbers[:1], targets, 8, grads, (tokens_grad, mixed, down_grad)
+    )
     norm_grads = smalls[:8].reshape(4, 256)
     dy_total = smalls[22:].reshape(256)
-
-    below, above = move(inner, y=1), move(inner, y=-1)
-    far_low, far_high = move(below[:1], y=1), move(above[1:], y=-1)
-    pieces = [(v, move(v, c=1)) for v in (inner, above, far_low, far_high, below)]
-    order = ((0, h), (0, 1 - h), (1, h), (1, 1 - h), (2, h), (2, 1 - h), (3, h), (3, 1 - h))
-    places = jnp.stack([(y + k) % 4 * 2 + high for k, high in order]).astype(jnp.int32)
-    up_parts = [
-        (source * ff, 64 + 16 * (source % 4), source // 4 * ff, ff) for source in range(8)
-    ]
-    targets = [(width, 64, [(0, 0, 0, width)]), (8 * ff, 16, up_parts)]
-    near = pieces[:2] + pieces[4:]
-    near_places = jnp.concatenate([places[:4], places[6:]])
-    grads = spread(near, near_places, numbers[:1], targets, 8, (), ())
-    down_grad, up_grad = spread(
-        pieces[2:4], places[4:6], numbers[:1], targets, 8, grads, (tokens_grad, mixed)
-    )
-
-    a_below, a_above = move(a_sum, y=1), move(a_sum, y=-1)
-    a_low, a_high = halves(a_below[None], a_above[None], (inner_other,))
-    a_far = jnp.concatenate([move(a_low, y=1), move(a_high, y=-1)], 1)
-    a_sum = jnp.concatenate([a_sum[None], a_above[None], a_far, a_below[None]])
-    a_other = move(a_sum, h=1)
-    places = jnp.concatenate([steps4 * 2 + h, steps4 * 2 + 1 - h]).astype(jnp.int32)
-    out_grad, qkv_grad = spread(
-        [(a_sum, move(a_sum, c=1)), (a_other, move(a_other, c=1))],
-        places,
-        numbers[:1],
-        [
-            (width, 16, [(0, 48, 0, width)]),
-            (3 * width, 16, [(n * width, 16 * n, 0, width) for n in range(3)]),
-        ],
-        8,
-        (),
-        (),
-    )
     return (
         mixed,
         tokens_grad,

time: 473 us -> 432 us (0.913)
  starting transfers between devices: 116 us -> 90.2 us
  local copies, waits for them, and re-layouts: 35 us -> 26.3 us
  Pallas kernels: 150 us -> 143 us
  waiting for transfers between devices: 135 us -> 130 us
  other arithmetic: 15.9 us -> 20.7 us
    ppermute x53 -> x44, starting transfers between devices: 101 us -> 77.3 us  [move(): return lax.ppermute(value, BOTH, pairs)]
    all_to_all x2 -> x1, waiting for transfers between devices: 31.5 us -> 9.32 us  [local(): part = lax.all_to_all(part, 'shard', 0, 0)]
    all_to_all x0 -> x1, waiting for transfers between devices: none -> 11.6 us  [local(): part = lax.all_to_all(part, 'shard', 0, 0).reshape(1, 128, cols)]
    pallas_call x3 -> x2, Pallas kernels: 22.2 us -> 12.9 us  [spread(): pl.pallas_call(after_inputs(body, 2 + 2 * len(pieces) + len(before), len(...]
    convert_element_type x3, other arithmetic: 1.28 us -> 7.45 us  [the longest x2 3.95 us: ring_middle(): above = (above.astype(f32) + passed.astype(f32)).astype(bf16)]
    ppermute x53 -> x44, waiting for transfers between devices: 103 us -> 109 us  [move(): return lax.ppermute(value, BOTH, pairs)]
    pallas_call x12 -> x11, Pallas kernels: 62.2 us -> 65 us  [the longest x1 26.5 us: outer(): pl.pallas_call(after_inputs(body, 11 + parts + count, len(after)), out_sh...]
    unnamed x101 -> x93, local copies, waits for them, and re-layouts: 14.5 us -> 12.8 us
  transfers between devices with their start and end apart: 57 -> 48, of which waited for: 15 -> 14; matrix products, arithmetic and copies ran while one was open for 7% -> 7% of each run, Pallas kernels for 23% -> 22%
where the time goes in v5:
time: 432 us; the launch traced here: 425 us
  Pallas kernels  143 us (33%)
  waiting for transfers between devices  130 us (30%)
  starting transfers between devices  90.2 us (21%)
  local copies, waits for them, and re-layouts  26.3 us (6%)
  other arithmetic  20.7 us (5%)
  between operations  15 us (3%)
    ppermute x44, waiting for transfers between devices, move(): return lax.ppermute(value, BOTH, pairs)  109 us
    ppermute x44, starting transfers between devices, move(): return lax.ppermute(value, BOTH, pairs)  77.3 us
    pallas_call x1, Pallas kernels, feed_forward(): pl.pallas_call(after_inputs(body, 5 + parts + 2 * count, len(after)), out...  32.2 us
    pallas_call x1, Pallas kernels, outer(): pl.pallas_call(after_inputs(body, 11 + parts + count, len(after)), out_sh...  26.5 us
    pallas_call x1, Pallas kernels, attend(): pl.pallas_call(after_inputs(body, 8 + parts + count, len(after)), out_sha...  25.7 us
    pallas_call x6, Pallas kernels, blocks_call(): pl.pallas_call(after_inputs(body, 1 + len(terms), len(after)), out_shape=...  22.4 us
    pallas_call x2, Pallas kernels, spread(): pl.pallas_call(after_inputs(body, 2 + 2 * len(pieces) + len(before), len(...  12.9 us
    unnamed x93, local copies, waits for them, and re-layouts  12.8 us
  transfers between devices with their start and end apart: 48, of which 14 were waited for; matrix products, arithmetic and copies ran while one was open for 7% of the time, Pallas kernels for 22%

profile of v5, /device:TPU:1, one launch (start us, length us, event | category | flops | bytes accessed | tf_op | source)
XLA Modules:
  0.0 425.2 jit_solution(5571716881940293011)
XLA Ops:
  13.3 3.6 packed.1
  22.1 3.6 all-to-all-start
  25.7 17.2 %collective-permute-done.1.refs_2_.refs_17_.refs_25_.refs_18_ = bf16[2,128,2048]{2,1,0:T(8,128)(2,1)S(1)} collective-permute-done((bf16[2,128,2048]{2,1,0:T(8,128)(2,1)}, bf16[2,128,2048]{2,1,0:T(8,128)(2,1)S(1)}, u32[]{:S(2)}, u32[]{:S(2)}) %collective-permute-start.1) | collective-permute-done | bytes 1048608 | tf_op jit(solution)/shard_map/ppermute | solution.py:45
  47.5 9.3 %all-to-all-done.refs_0_ = bf16[8,40,1792]{2,1,0:T(8,128)(2,1)S(1)} async-done(((bf16[8,40,1792]{2,1,0:T(8,128)(2,1)}), bf16[8,40,1792]{2,1,0:T(8,128)(2,1)S(1)}, u32[]{:S(2)}, u32[]{:S(2)}) %all-to-all-start) | async-done | bytes 1146912 | tf_op jit(solution)/shard_map/all_to_all | solution.py:923
  63.0 17.3 %collective-permute-done.3.refs_1_.refs_5_.refs_6_ = bf16[8,32,1792]{2,1,0:T(8,128)(2,1)S(1)} collective-permute-done((bf16[8,32,1792]{2,1,0:T(8,128)(2,1)}, bf16[8,32,1792]{2,1,0:T(8,128)(2,1)S(1)}, u32[]{:S(2)}, u32[]{:S(2)}) %collective-permute-start.3) | collective-permute-done | bytes 917536 | tf_op jit(solution)/shard_map/ppermute | solution.py:45
  87.1 3.7 joined.1
  90.8 3.9 collective-permute-start.10
  105.1 6.3 %collective-permute-done.8.refs_6_.refs_7_ = bf16[4,32,1792]{2,1,0:T(8,128)(2,1)} collective-permute-done((bf16[4,32,1792]{2,1,0:T(8,128)(2,1)}, bf16[4,32,1792]{2,1,0:T(8,128)(2,1)}, u32[]{:S(2)}, u32[]{:S(2)}) %collective-permute-start.8) | collective-permute-done | bytes 458784 | tf_op jit(solution)/shard_map/ppermute | solution.py:45
  118.3 32.2 %feed_forward.1 = (bf16[1024,2048]{1,0:T(8,128)(2,1)}, bf16[1024,1024]{1,0:T(8,128)(2,1)}, bf16[1024,1024]{1,0:T(8,128)(2,1)}, bf16[8,128,2048]{2,1,0:T(8,128)(2...) custom-call(s32[4]{0:T(128)} %get-tuple-element.132.refs_0_.number_r, ...), custom_call_target="tpu_custom_call" | custom-call | flops 36800000000 | bytes 1000 | tf_op jit(solution)/shard_map/feed_forward/pallas_call | solution.py:250
  154.3 25.7 %attend.1 = (bf16[1024,256]{1,0:T(8,128)(2,1)}, bf16[1024,768]{1,0:T(8,128)(2,1)}, bf16[8,64,2048]{2,1,0:T(8,128)(2,1)}, bf16[8,64,2048]{2,1,0:T(8,128)(2,1)}, f32[1,768]{1,0:T(1,128)}) custom-call(s32[4]{0:T(128)} %get-tuple-element.132.refs_0_.number_ref, s32[8,3]{1,0:T(8,128)} %copy-done.18, s32[8]{0:T(128)} %pad_add_fusion.refs_1_.refs_2_.refs_0_, ...), custom_call_target="tpu_custom_call" | custom-call | flops 25300000768 | bytes 1000 | tf_op jit(solution)/shard_map/attend/pallas_call | solution.py:457
  180.1 3.3 far_sums.1
  186.3 26.5 %outer.1 = (f32[4,2048]{1,0:T(4,128)}, bf16[2,128,2048]{2,1,0:T(8,128)(2,1)}, bf16[2,128,2048]{2,1,0:T(8,128)(2,1)}, bf16[2,128,2048]{2,1,0:T(8,128)(2,1)}, bf16...) custom-call(s32[8]{0:T(128)} %pad_add_fusion.refs_1_.refs_2_.refs_0_, ...), custom_call_target="tpu_custom_call" | custom-call | flops 23000000512 | bytes 1000 | tf_op jit(solution)/shard_map/outer/pallas_call | solution.py:578
  216.6 4.8 %near_sums.1 = (bf16[2,128,2048]{2,1,0:T(8,128)(2,1)}, bf16[2,128,2048]{2,1,0:T(8,128)(2,1)}) custom-call(s32[4]{0:T(128)} %get-tuple-element.132.refs_0_.number_ref, bf16[8,128,2048]{2,1,0:T(8,128)(2,1)} %get-tuple-element.82.refs_1_.refs_3_, bf16[8,128,2048]{2,1,0:T(8,128)(2,1)} %collective-permute-done.15.refs_2_.refs_4_, ...), custom_call_target="tpu_custom_call" | custom-call | flops 3449999872 | bytes 1000 | tf_op jit(solution)/shard_map/near_sums/pallas_call | solution.py:765
  225.3 3.4 away_sums.1.refs_5_
  228.7 3.3 collective-permute-start.29
  235.4 5.9 %all-to-all-start.1 = ((bf16[128,24,128]{2,1,0:T(8,128)(2,1)}), bf16[128,24,128]{2,1,0:T(8,128)(2,1)S(1)}, u32[]{:S(2)}, u32[]{:S(2)}) async-start(bf16[128,24,128]{2,1,0:T(8,128)(2,1)} %bitcast.56), calls=%async_computation.1 | async-start | bytes 1572864 | tf_op jit(solution)/shard_map/all_to_all | solution.py:1069
  248.9 4.3 %end_sums.1 = (bf16[1,128,2048]{2,1,0:T(8,128)(2,1)}, bf16[1,128,2048]{2,1,0:T(8,128)(2,1)}) custom-call(s32[4]{0:T(128)} %get-tuple-element.132.refs_0_.number_ref, bf16[8,128,2048]{2,1,0:T(8,128)(2,1)} %get-tuple-element.82.refs_1_.refs_3_, bf16[8,128,2048]{2,1,0:T(8,128)(2,1)} %collective-permute-done.15.refs_2_.refs_4_, ...), custom_call_target="tpu_custom_call" | custom-call | flops 3449999872 | bytes 1000 | tf_op jit(solution)/shard_map/end_sums/pallas_call | solution.py:765
  253.3 8.5 %collective-permute-done.29.refs_3_ = bf16[4,64,2048]{2,1,0:T(8,128)(2,1)} collective-permute-done((bf16[4,64,2048]{2,1,0:T(8,128)(2,1)}, bf16[4,64,2048]{2,1,0:T(8,128)(2,1)}, u32[]{:S(2)}, u32[]{:S(2)}) %collective-permute-start.29) | collective-permute-done | bytes 1048608 | tf_op jit(solution)/shard_map/ppermute | solution.py:45
  261.7 3.9 around_sums.1
  278.1 3.5 collective-permute-done.32.refs_3_
  290.0 3.5 all-to-all-start.2
  293.5 3.5 add_convert_fusion
  298.8 11.6 %all-to-all-done.2 = bf16[8,16,1792]{2,1,0:T(8,128)(2,1)S(1)} async-done(((bf16[8,16,1792]{2,1,0:T(8,128)(2,1)}), bf16[8,16,1792]{2,1,0:T(8,128)(2,1)S(1)}, u32[]{:S(2)}, u32[]{:S(2)}) %all-to-all-start.2) | async-done | bytes 458784 | tf_op jit(solution)/shard_map/all_to_all | solution.py:1156
  310.4 3.7 collective-permute-start.34
  316.5 32.6 %collective-permute-done.34 = bf16[1,128,1792]{2,1,0:T(8,128)(2,1)S(1)} collective-permute-done((bf16[1,128,1792]{2,1,0:T(8,128)(2,1)S(1)}, bf16[1,128,1792]{2,1,0:T(8,128)(2,1)S(1)}, u32[]{:S(2)}, u32[]{:S(2)}) %collective-permute-start.34) | collective-permute-done | bytes 458784 | tf_op jit(solution)/shard_map/ppermute | solution.py:45
  351.5 8.8 %collective-permute-start.41 = (bf16[2,128,1792]{2,1,0:T(8,128)(2,1)S(1)}, bf16[2,128,1792]{2,1,0:T(8,128)(2,1)S(1)}, u32[]{:S(2)}, u32[]{:S(2)}) collective-permute-start(bf16[2,128,1792]{2,1,0:T(8,128)(2,1)S(1)} %pad_maximum_fusion.refs_2_), channel_id=1, source_target_pairs={{0,8},{1,9},{2,10},{3,11},{4,12},{5,13},{6,14},{7,15},{8,0},{9,1},... | collective-permute-start | bytes 2752520 | tf_op jit(solution)/shard_map/ppermute | solution.py:45
  362.9 8.0 %collective-permute-done.38.refs_4_ = bf16[2,128,1792]{2,1,0:T(8,128)(2,1)S(1)} collective-permute-done((bf16[2,128,1792]{2,1,0:T(8,128)(2,1)S(1)}, bf16[2,128,1792]{2,1,0:T(8,128)(2,1)S(1)}, u32[]{:S(2)}, u32[]{:S(2)}) %collective-permute-start.38) | collective-permute-done | bytes 917536 | tf_op jit(solution)/shard_map/ppermute | solution.py:45
  370.9 6.4 %collective-permute-start.42 = (bf16[2,128,1792]{2,1,0:T(8,128)(2,1)S(1)}, bf16[2,128,1792]{2,1,0:T(8,128)(2,1)S(1)}, u32[]{:S(2)}, u32[]{:S(2)}) collective-permute-start(bf16[2,128,1792]{2,1,0:T(8,128)(2,1)S(1)} %collective-permute-done.38.refs_4_), channel_id=1, source_target_pairs={{0,8},{1,9},{2,10},{3,11},{4,12},{5,13},{6,14},{7,15},{8,0},{9,1},... | collective-permute-start | bytes 2752520 | tf_op jit(solution)/shard_map/ppermute | solution.py:45
  384.4 8.9 %collective-permute-done.36.refs_2_ = bf16[1,128,1792]{2,1,0:T(8,128)(2,1)S(1)} collective-permute-done((bf16[1,128,1792]{2,1,0:T(8,128)(2,1)S(1)}, bf16[1,128,1792]{2,1,0:T(8,128)(2,1)S(1)}, u32[]{:S(2)}, u32[]{:S(2)}) %collective-permute-start.36) | collective-permute-done | bytes 458784 | tf_op jit(solution)/shard_map/ppermute | solution.py:45
  396.5 8.7 %spread.2 = (f32[256,6144]{1,0:T(8,128)}, f32[256,8192]{1,0:T(8,128)}) custom-call(s32[6]{0:T(128)} %stack.69.refs_0_, s32[1]{0:T(128)} %bitcast.refs_1_, bf16[2,128,1792]{2,1,0:T(8,128)(2,1)} %copy-done.7, bf16[2,128,1792]{2,1,0:T(8,128)(2,1)} %copy-done.31, bf16[2,128,1792]{2,1,0:T(8,128)(2,1)} %copy-done.15, bf16[2,128,1792]{2,1,0:T(8,128)(2,1)} %copy-done.32, ...), custom_call_target="tpu_custom_call" | custom-call | flops 8280000000 | bytes 1000 | tf_op jit(solution)/shard_map/spread/pallas_call | solution.py:827
  405.2 7.0 %stayed.1 = (f32[1024,2048]{1,0:T(8,128)}, f32[256,2048]{1,0:T(8,128)}) custom-call(bf16[16,80,2048]{2,1,0:T(8,128)(2,1)} %bitcast.68), custom_call_target="tpu_custom_call" | custom-call | flops 6899999744 | bytes 1000 | tf_op jit(solution)/shard_map/stayed/pallas_call | solution.py:685
  413.1 4.2 spread.3
  (233 shorter events, 113.1 us)
Async XLA Ops:
  16.9 26.0 %collective-permute-start.1 = (bf16[2,128,2048]{2,1,0:T(8,128)(2,1)}, bf16[2,128,2048]{2,1,0:T(8,128)(2,1)S(1)}, u32[]{:S(2)}, u32[]{:S(2)}) collective-permute-start(bf16[2,128,2048]{2,1,0:T(8,128)(2,1)} %get-tuple-element.67.refs_14_.refs_22_.refs_15_), channel_id=1, source_target_pairs={{0,1},{1,2},{2,3},{3,0},{4,5},{5,6},{6,7},{7,4},{8,9},{9,10},{10,1... | collective-permute-start | bytes 3145736 | tf_op jit(solution)/shard_map/ppermute | solution.py:45
  19.0 26.0 %collective-permute-start.2 = (bf16[2,128,2048]{2,1,0:T(8,128)(2,1)}, bf16[2,128,2048]{2,1,0:T(8,128)(2,1)S(1)}, u32[]{:S(2)}, u32[]{:S(2)}) collective-permute-start(bf16[2,128,2048]{2,1,0:T(8,128)(2,1)} %get-tuple-element.67.refs_14_.refs_22_.refs_15_), channel_id=1, source_target_pairs={{0,4},{1,5},{2,6},{3,7},{4,0},{5,1},{6,2},{7,3},{8,12},{9,13},{10,... | collective-permute-start | bytes 3145736 | tf_op jit(solution)/shard_map/ppermute | solution.py:45
  20.6 36.2 %collective-permute-start = (bf16[2,128,2048]{2,1,0:T(8,128)(2,1)}, bf16[2,128,2048]{2,1,0:T(8,128)(2,1)}, u32[]{:S(2)}, u32[]{:S(2)}) collective-permute-start(bf16[2,128,2048]{2,1,0:T(8,128)(2,1)} %get-tuple-element.67.refs_14_.refs_22_.refs_15_), channel_id=1, source_target_pairs={{0,3},{1,0},{2,1},{3,2},{4,7},{5,4},{6,5},{7,6},{8,11},{9,8},{10,9... | collective-permute-start | bytes 3145736 | tf_op jit(solution)/shard_map/ppermute | solution.py:45
  22.1 34.8 %all-to-all-start = ((bf16[8,40,1792]{2,1,0:T(8,128)(2,1)}), bf16[8,40,1792]{2,1,0:T(8,128)(2,1)S(1)}, u32[]{:S(2)}, u32[]{:S(2)}) async-start(bf16[8,40,1792]{2,1,0:T(8,128)(2,1)} %get-tuple-element.66), calls=%async_computation | async-start | bytes 2293760 | tf_op jit(solution)/shard_map/all_to_all | solution.py:923
  42.9 40.4 %collective-permute-start.5 = (bf16[2,128,2048]{2,1,0:T(8,128)(2,1)S(1)}, bf16[2,128,2048]{2,1,0:T(8,128)(2,1)}, u32[]{:S(2)}, u32[]{:S(2)}) collective-permute-start(bf16[2,128,2048]{2,1,0:T(8,128)(2,1)S(1)} %collective-permute-done.1.refs_2_.refs_17_.refs_25_.refs_18_), channel_id=1, source_target_pairs={{0,4},{1,5},{2,6},{3,7},{4,0},{5,1},{6,2},{7,3},{8,12},{9,13},{10,... | collective-permute-start | bytes 3145736 | tf_op jit(solution)/shard_map/ppermute | solution.py:45
  44.9 38.5 %collective-permute-start.7 = (bf16[2,128,2048]{2,1,0:T(8,128)(2,1)S(1)}, bf16[2,128,2048]{2,1,0:T(8,128)(2,1)}, u32[]{:S(2)}, u32[]{:S(2)}) collective-permute-start(bf16[2,128,2048]{2,1,0:T(8,128)(2,1)S(1)} %collective-permute-done.1.refs_2_.refs_17_.refs_25_.refs_18_), channel_id=1, source_target_pairs={{0,1},{1,2},{2,3},{3,0},{4,5},{5,6},{6,7},{7,4},{8,9},{9,10},{10,1... | collective-permute-start | bytes 3145736 | tf_op jit(solution)/shard_map/ppermute | solution.py:45
  45.0 38.4 %collective-permute-start.6 = (bf16[2,128,2048]{2,1,0:T(8,128)(2,1)S(1)}, bf16[2,128,2048]{2,1,0:T(8,128)(2,1)}, u32[]{:S(2)}, u32[]{:S(2)}) collective-permute-start(bf16[2,128,2048]{2,1,0:T(8,128)(2,1)S(1)} %collective-permute-done.2.refs_3_.refs_18_.refs_26_.refs_19_), channel_id=1, source_target_pairs={{0,3},{1,0},{2,1},{3,2},{4,7},{5,4},{6,5},{7,6},{8,11},{9,8},{10,9... | collective-permute-start | bytes 3145736 | tf_op jit(solution)/shard_map/ppermute | solution.py:45
  60.3 20.0 %collective-permute-start.3 = (bf16[8,32,1792]{2,1,0:T(8,128)(2,1)}, bf16[8,32,1792]{2,1,0:T(8,128)(2,1)S(1)}, u32[]{:S(2)}, u32[]{:S(2)}) collective-permute-start(bf16[8,32,1792]{2,1,0:T(8,128)(2,1)} %get-tuple-element.69.refs_0_.refs_4_.refs_5_), channel_id=1, source_target_pairs={{0,96},{1,97},{2,98},{3,99},{4,100},{5,101},{6,102},{7,103},{8,104... | collective-permute-start | bytes 2752520 | tf_op jit(solution)/shard_map/ppermute | solution.py:45
  63.0 20.3 %collective-permute-start.4 = (bf16[8,32,1792]{2,1,0:T(8,128)(2,1)}, bf16[8,32,1792]{2,1,0:T(8,128)(2,1)S(1)}, u32[]{:S(2)}, u32[]{:S(2)}) collective-permute-start(bf16[8,32,1792]{2,1,0:T(8,128)(2,1)} %get-tuple-element.69.refs_0_.refs_4_.refs_5_), channel_id=1, source_target_pairs={{0,32},{1,33},{2,34},{3,35},{4,36},{5,37},{6,38},{7,39},{8,40},{9,... | collective-permute-start | bytes 2752520 | tf_op jit(solution)/shard_map/ppermute | solution.py:45
  90.8 25.4 %collective-permute-start.10 = (bf16[24,32,1792]{2,1,0:T(8,128)(2,1)}, bf16[24,32,1792]{2,1,0:T(8,128)(2,1)S(1)}, u32[]{:S(2)}, u32[]{:S(2)}) collective-permute-start(bf16[24,32,1792]{2,1,0:T(8,128)(2,1)} %joined.1), channel_id=1, source_target_pairs={{0,8},{1,9},{2,10},{3,11},{4,12},{5,13},{6,14},{7,15},{8,0},{9,1},... | collective-permute-start | bytes 8257544 | tf_op jit(solution)/shard_map/ppermute | solution.py:45
  150.6 29.5 %collective-permute-start.15 = (bf16[8,128,2048]{2,1,0:T(8,128)(2,1)}, bf16[8,128,2048]{2,1,0:T(8,128)(2,1)}, u32[]{:S(2)}, u32[]{:S(2)}) collective-permute-start(bf16[8,128,2048]{2,1,0:T(8,128)(2,1)} %get-tuple-element.77.refs_26_), channel_id=1, source_target_pairs={{0,8},{1,9},{2,10},{3,11},{4,12},{5,13},{6,14},{7,15},{8,0},{9,1},... | collective-permute-start | bytes 12582920 | tf_op jit(solution)/shard_map/ppermute | solution.py:45
  180.0 44.0 %collective-permute-start.27 = (bf16[8,64,2048]{2,1,0:T(8,128)(2,1)}, bf16[8,64,2048]{2,1,0:T(8,128)(2,1)S(1)}, u32[]{:S(2)}, u32[]{:S(2)}) collective-permute-start(bf16[8,64,2048]{2,1,0:T(8,128)(2,1)} %get-tuple-element.100), channel_id=1, source_target_pairs={{0,8},{1,9},{2,10},{3,11},{4,12},{5,13},{6,14},{7,15},{8,0},{9,1},... | collective-permute-start | bytes 6291464 | tf_op jit(solution)/shard_map/ppermute | solution.py:45
  183.4 32.1 %collective-permute-start.23 = (bf16[1,128,2048]{2,1,0:T(8,128)(2,1)}, bf16[1,128,2048]{2,1,0:T(8,128)(2,1)S(1)}, u32[]{:S(2)}, u32[]{:S(2)}) collective-permute-start(bf16[1,128,2048]{2,1,0:T(8,128)(2,1)} %get-tuple-element.83.refs_29_), channel_id=1, source_target_pairs={{0,32},{1,33},{2,34},{3,35},{4,36},{5,37},{6,38},{7,39},{8,40},{9,... | collective-permute-start | bytes 1572872 | tf_op jit(solution)/shard_map/ppermute | solution.py:45
  183.4 32.1 %collective-permute-start.24 = (bf16[1,128,2048]{2,1,0:T(8,128)(2,1)}, bf16[1,128,2048]{2,1,0:T(8,128)(2,1)S(1)}, u32[]{:S(2)}, u32[]{:S(2)}) collective-permute-start(bf16[1,128,2048]{2,1,0:T(8,128)(2,1)} %get-tuple-element.84.refs_30_), channel_id=1, source_target_pairs={{0,96},{1,97},{2,98},{3,99},{4,100},{5,101},{6,102},{7,103},{8,104... | collective-permute-start | bytes 1572872 | tf_op jit(solution)/shard_map/ppermute | solution.py:45
  212.8 28.5 %collective-permute-start.19 = (bf16[2,128,2048]{2,1,0:T(8,128)(2,1)}, bf16[2,128,2048]{2,1,0:T(8,128)(2,1)S(1)}, u32[]{:S(2)}, u32[]{:S(2)}) collective-permute-start(bf16[2,128,2048]{2,1,0:T(8,128)(2,1)} %get-tuple-element.91), channel_id=1, source_target_pairs={{0,1},{1,2},{2,3},{3,0},{4,5},{5,6},{6,7},{7,4},{8,9},{9,10},{10,1... | collective-permute-start | bytes 3145736 | tf_op jit(solution)/shard_map/ppermute | solution.py:45
  213.0 33.6 %collective-permute-start.16 = (bf16[2,128,2048]{2,1,0:T(8,128)(2,1)}, bf16[2,128,2048]{2,1,0:T(8,128)(2,1)S(1)}, u32[]{:S(2)}, u32[]{:S(2)}) collective-permute-start(bf16[2,128,2048]{2,1,0:T(8,128)(2,1)} %get-tuple-element.87), channel_id=1, source_target_pairs={{0,3},{1,0},{2,1},{3,2},{4,7},{5,4},{6,5},{7,6},{8,11},{9,8},{10,9... | collective-permute-start | bytes 3145736 | tf_op jit(solution)/shard_map/ppermute | solution.py:45
  221.3 25.3 %collective-permute-start.25 = (bf16[2,128,2048]{2,1,0:T(8,128)(2,1)}, bf16[2,128,2048]{2,1,0:T(8,128)(2,1)}, u32[]{:S(2)}, u32[]{:S(2)}) collective-permute-start(bf16[2,128,2048]{2,1,0:T(8,128)(2,1)} %get-tuple-element.97.refs_3_), channel_id=1, source_target_pairs={{0,32},{1,33},{2,34},{3,35},{4,36},{5,37},{6,38},{7,39},{8,40},{9,... | collective-permute-start | bytes 3145736 | tf_op jit(solution)/shard_map/ppermute | solution.py:45
  221.3 27.6 %collective-permute-start.26 = (bf16[2,128,2048]{2,1,0:T(8,128)(2,1)}, bf16[2,128,2048]{2,1,0:T(8,128)(2,1)}, u32[]{:S(2)}, u32[]{:S(2)}) collective-permute-start(bf16[2,128,2048]{2,1,0:T(8,128)(2,1)} %get-tuple-element.98), channel_id=1, source_target_pairs={{0,96},{1,97},{2,98},{3,99},{4,100},{5,101},{6,102},{7,103},{8,104... | collective-permute-start | bytes 3145736 | tf_op jit(solution)/shard_map/ppermute | solution.py:45
  228.7 33.0 %collective-permute-start.29 = (bf16[4,64,2048]{2,1,0:T(8,128)(2,1)}, bf16[4,64,2048]{2,1,0:T(8,128)(2,1)}, u32[]{:S(2)}, u32[]{:S(2)}) collective-permute-start(bf16[4,64,2048]{2,1,0:T(8,128)(2,1)} %away_sums.1.refs_5_), channel_id=1, source_target_pairs={{0,16},{1,17},{2,18},{3,19},{4,20},{5,21},{6,22},{7,23},{8,24},{9,... | collective-permute-start | bytes 3145736 | tf_op jit(solution)/shard_map/ppermute | solution.py:45
  235.4 41.9 %all-to-all-start.1 = ((bf16[128,24,128]{2,1,0:T(8,128)(2,1)}), bf16[128,24,128]{2,1,0:T(8,128)(2,1)S(1)}, u32[]{:S(2)}, u32[]{:S(2)}) async-start(bf16[128,24,128]{2,1,0:T(8,128)(2,1)} %bitcast.56), calls=%async_computation.1 | async-start | bytes 1572864 | tf_op jit(solution)/shard_map/all_to_all | solution.py:1069
  241.3 163.9 %all-gather.3.cloned.1.call-start = ((), (), s32[]{:S(2)}) async-start(), calls=%async_computation.3 | async-start | bytes 5570560 | tf_op jit(solution)/shard_map/all_gather | solution.py:1155
  241.3 36.7 %collective-permute-start.21 = (bf16[2,128,2048]{2,1,0:T(8,128)(2,1)}, bf16[2,128,2048]{2,1,0:T(8,128)(2,1)}, u32[]{:S(2)}, u32[]{:S(2)}) collective-permute-start(bf16[2,128,2048]{2,1,0:T(8,128)(2,1)} %get-tuple-element.92), channel_id=1, source_target_pairs={{0,3},{1,0},{2,1},{3,2},{4,7},{5,4},{6,5},{7,6},{8,11},{9,8},{10,9... | collective-permute-start | bytes 3145736 | tf_op jit(solution)/shard_map/ppermute | solution.py:45
  246.6 34.9 %collective-permute-start.20 = (bf16[2,128,2048]{2,1,0:T(8,128)(2,1)}, bf16[2,128,2048]{2,1,0:T(8,128)(2,1)}, u32[]{:S(2)}, u32[]{:S(2)}) collective-permute-start(bf16[2,128,2048]{2,1,0:T(8,128)(2,1)} %add_convert_fusion.1), channel_id=1, source_target_pairs={{0,1},{1,2},{2,3},{3,0},{4,5},{5,6},{6,7},{7,4},{8,9},{9,10},{10,1... | collective-permute-start | bytes 3145736 | tf_op jit(solution)/shard_map/ppermute | solution.py:45
  285.6 66.0 %collective-permute-start.18 = (bf16[2,128,2048]{2,1,0:T(8,128)(2,1)}, bf16[2,128,2048]{2,1,0:T(8,128)(2,1)}, u32[]{:S(2)}, u32[]{:S(2)}) collective-permute-start(bf16[2,128,2048]{2,1,0:T(8,128)(2,1)} %get-tuple-element.88), channel_id=1, source_target_pairs={{0,1},{1,2},{2,3},{3,0},{4,5},{5,6},{6,7},{7,4},{8,9},{9,10},{10,1... | collective-permute-start | bytes 3145736 | tf_op jit(solution)/shard_map/ppermute | solution.py:45
  287.7 72.6 %collective-permute-start.17 = (bf16[2,128,2048]{2,1,0:T(8,128)(2,1)}, bf16[2,128,2048]{2,1,0:T(8,128)(2,1)S(1)}, u32[]{:S(2)}, u32[]{:S(2)}) collective-permute-start(bf16[2,128,2048]{2,1,0:T(8,128)(2,1)} %add_convert_fusion.2), channel_id=1, source_target_pairs={{0,3},{1,0},{2,1},{3,2},{4,7},{5,4},{6,5},{7,6},{8,11},{9,8},{10,9... | collective-permute-start | bytes 3145736 | tf_op jit(solution)/shard_map/ppermute | solution.py:45
  290.0 20.5 %all-to-all-start.2 = ((bf16[8,16,1792]{2,1,0:T(8,128)(2,1)}), bf16[8,16,1792]{2,1,0:T(8,128)(2,1)S(1)}, u32[]{:S(2)}, u32[]{:S(2)}) async-start(bf16[8,16,1792]{2,1,0:T(8,128)(2,1)} %get-tuple-element.110), calls=%async_computation.2 | async-start | bytes 917504 | tf_op jit(solution)/shard_map/all_to_all | solution.py:1156
  297.0 63.4 %collective-permute-start.22 = (bf16[2,128,2048]{2,1,0:T(8,128)(2,1)}, bf16[2,128,2048]{2,1,0:T(8,128)(2,1)}, u32[]{:S(2)}, u32[]{:S(2)}) collective-permute-start(bf16[2,128,2048]{2,1,0:T(8,128)(2,1)} %add_convert_fusion), channel_id=1, source_target_pairs={{0,4},{1,5},{2,6},{3,7},{4,0},{5,1},{6,2},{7,3},{8,12},{9,13},{10,... | collective-permute-start | bytes 3145736 | tf_op jit(solution)/shard_map/ppermute | solution.py:45
  310.4 38.7 %collective-permute-start.34 = (bf16[1,128,1792]{2,1,0:T(8,128)(2,1)S(1)}, bf16[1,128,1792]{2,1,0:T(8,128)(2,1)S(1)}, u32[]{:S(2)}, u32[]{:S(2)}) collective-permute-start(bf16[1,128,1792]{2,1,0:T(8,128)(2,1)S(1)} %bitcast.57), channel_id=1, source_target_pairs={{0,16},{1,17},{2,18},{3,19},{4,20},{5,21},{6,22},{7,23},{8,24},{9,... | collective-permute-start | bytes 1376264 | tf_op jit(solution)/shard_map/ppermute | solution.py:45
  349.2 21.7 %collective-permute-start.38 = (bf16[2,128,1792]{2,1,0:T(8,128)(2,1)S(1)}, bf16[2,128,1792]{2,1,0:T(8,128)(2,1)S(1)}, u32[]{:S(2)}, u32[]{:S(2)}) collective-permute-start(bf16[2,128,1792]{2,1,0:T(8,128)(2,1)S(1)} %pad_maximum_fusion.refs_2_), channel_id=1, source_target_pairs={{0,96},{1,97},{2,98},{3,99},{4,100},{5,101},{6,102},{7,103},{8,104... | collective-permute-start | bytes 2752520 | tf_op jit(solution)/shard_map/ppermute | solution.py:45
  350.9 26.4 %collective-permute-start.35 = (bf16[2,128,1792]{2,1,0:T(8,128)(2,1)S(1)}, bf16[2,128,1792]{2,1,0:T(8,128)(2,1)S(1)}, u32[]{:S(2)}, u32[]{:S(2)}) collective-permute-start(bf16[2,128,1792]{2,1,0:T(8,128)(2,1)S(1)} %pad_maximum_fusion.refs_2_), channel_id=1, source_target_pairs={{0,32},{1,33},{2,34},{3,35},{4,36},{5,37},{6,38},{7,39},{8,40},{9,... | collective-permute-start | bytes 2752520 | tf_op jit(solution)/shard_map/ppermute | solution.py:45
  351.5 42.7 %collective-permute-start.41 = (bf16[2,128,1792]{2,1,0:T(8,128)(2,1)S(1)}, bf16[2,128,1792]{2,1,0:T(8,128)(2,1)S(1)}, u32[]{:S(2)}, u32[]{:S(2)}) collective-permute-start(bf16[2,128,1792]{2,1,0:T(8,128)(2,1)S(1)} %pad_maximum_fusion.refs_2_), channel_id=1, source_target_pairs={{0,8},{1,9},{2,10},{3,11},{4,12},{5,13},{6,14},{7,15},{8,0},{9,1},... | collective-permute-start | bytes 2752520 | tf_op jit(solution)/shard_map/ppermute | solution.py:45
  370.9 23.3 %collective-permute-start.42 = (bf16[2,128,1792]{2,1,0:T(8,128)(2,1)S(1)}, bf16[2,128,1792]{2,1,0:T(8,128)(2,1)S(1)}, u32[]{:S(2)}, u32[]{:S(2)}) collective-permute-start(bf16[2,128,1792]{2,1,0:T(8,128)(2,1)S(1)} %collective-permute-done.38.refs_4_), channel_id=1, source_target_pairs={{0,8},{1,9},{2,10},{3,11},{4,12},{5,13},{6,14},{7,15},{8,0},{9,1},... | collective-permute-start | bytes 2752520 | tf_op jit(solution)/shard_map/ppermute | solution.py:45
  (60 other events, 593.7 us)
Sparse Core Ops, SparseCore 0:
  285.2 83.4 all-gather.2

commit v6 on v5

--- a/solution.py
+++ b/solution.py
@@ -300,7 +300,7 @@
         sizes = jnp.zeros((8, cols), f32)
         for at in range(3):
             sizes = jnp.where(lane == at, len_ref[0, at].astype(f32), sizes)
-        vector = jnp.concatenate([ref[...].astype(f32) for ref in v_refs], 1)
+        vector = jnp.concatenate([ref[...].astype(f32) for ref in v_refs])[None, :]
         vector = jnp.broadcast_to(vector, (8, cols))
         tail = jnp.where(row == 0, vector, jnp.where(row == 1, sizes, 0.0)).astype(bf16)
         for owner in range(8):
@@ -326,7 +326,7 @@
                 pl.BlockSpec(tokens.shape, lambda i, place, lens: (0, 0)),
                 pl.BlockSpec(tokens.shape, lambda i, place, lens: (0, 0)),
             ]
-            + [pl.BlockSpec(v.shape, lambda i, place, lens: (0, 0)) for v in vectors],
+            + [pl.BlockSpec(v.shape, lambda i, place, lens: (0,)) for v in vectors],
             out_specs=(
                 pl.BlockSpec((8, 40, cols), lambda i, place, lens: (0, 0, 0)),
                 pl.BlockSpec((2,) + tokens.shape, lambda i, place, lens: (0, 0, 0)),
@@ -673,33 +673,6 @@
     )(stays, crossed, own, below, above, *after)
 
 
-def stayed(parts, after):
-    count, _, width = parts.shape
-    step = 4
-
-    def body(part_ref, down_ref, out_ref):
-        for at in range(step):
-            down_ref[at * 64 : (at + 1) * 64] = part_ref[at, 0:64].astype(f32)
-            out_ref[at * 16 : (at + 1) * 16] = part_ref[at, 64:80].astype(f32)
-
-    return pl.pallas_call(
-        after_inputs(body, 1, len(after)),
-        out_shape=(
-            jax.ShapeDtypeStruct((count * 64, width), f32),
-            jax.ShapeDtypeStruct((count * 16, width), f32),
-        ),
-        grid=(count // step,),
-        in_specs=[pl.BlockSpec((step, 80, width), lambda i: (i, 0, 0))] + anywhere(len(after)),
-        out_specs=(
-            pl.BlockSpec((step * 64, width), lambda i: (i, 0)),
-            pl.BlockSpec((step * 16, width), lambda i: (i, 0)),
-        ),
-        compiler_params=kernel_params(),
-        cost_estimate=cost(6),
-        name="stayed",
-    )(parts, *after)
-
-
 def halves(below, above, x_pair, dy_pair, after):
     count, rows, cols = below.shape
     _, tokens, width = x_pair.shape
@@ -734,23 +707,29 @@
 
 
 def joined(arrays, after):
-    size, rows, cols = arrays[0].shape
+    sizes = [array.shape[0] for array in arrays]
+    unit = math.gcd(*sizes)
+    block = (unit,) + arrays[0].shape[1:]
     count = len(arrays)
+    firsts = [sum(sizes[:n]) // unit for n in range(count)]
 
     def body(*refs):
-        for at in range(count):
-
-            @pl.when(pl.program_id(0) == at)
-            def _(at=at):
-                refs[count][...] = refs[at][...]
-
-    block = pl.BlockSpec((size, rows, cols), lambda i: (0, 0, 0))
+        step = pl.program_id(0)
+        for ref, first, size in zip(refs, firsts, sizes):
+
+            @pl.when((step >= first) & (step < first + size // unit))
+            def _(ref=ref):
+                refs[count][...] = ref[...]
+
+    def came(first, size):
+        return pl.BlockSpec(block, lambda i: (jnp.clip(i - first, 0, size // unit - 1), 0, 0))
+
     return pl.pallas_call(
         after_inputs(body, count, len(after)),
-        out_shape=jax.ShapeDtypeStruct((size * count, rows, cols), bf16),
-        grid=(count,),
-        in_specs=[block] * count + anywhere(len(after)),
-        out_specs=pl.BlockSpec((size, rows, cols), lambda i: (i, 0, 0)),
+        out_shape=jax.ShapeDtypeStruct((sum(sizes),) + block[1:], bf16),
+        grid=(sum(sizes) // unit,),
+        in_specs=[came(first, size) for first, size in zip(firsts, sizes)] + anywhere(len(after)),
+        out_specs=pl.BlockSpec(block, lambda i: (i, 0, 0)),
         compiler_params=kernel_params(),
         cost_estimate=cost(3),
         name="joined",
@@ -911,7 +890,7 @@
     ff = up_bias.shape[0]
 
     cols = 3 * head + ff
-    vectors = [v[None] for v in (ln1_gain, ln1_bias, ln2_gain, ln2_bias, qkv_bias)]
+    vectors = [ln1_gain, ln1_bias, ln2_gain, ln2_bias, qkv_bias]
     place = (y * 2 + c).astype(jnp.int32).reshape(1)
     part, pair = packed(
         qkv_weight, up_weight, vectors, doc_lengths, place, head, tokens, cotangent
@@ -1069,22 +1048,105 @@
     smalls = lax.all_to_all(smalls, BOTH, 0, 0)
     smalls = jnp.sum(smalls.astype(f32), 0)
 
-    def ring_start(pieces, way):
-        return move(pieces[2], x=way)
-
-    def ring_middle(pieces, passed, way):
-        above, below = (pieces[1], pieces[3]) if way == 1 else (pieces[3], pieces[1])
-        above = (above.astype(f32) + passed.astype(f32)).astype(bf16)
-        return move(above, x=way), move(below, x=-way)
-
-    def ring_end(pieces, arrived):
-        return functools.reduce(jnp.add, [v.astype(f32) for v in (pieces[0],) + arrived])
-
-    passed_other, passed_own = ring_start(pairs_out[4:], 1), ring_start(pairs_out[:4], -1)
-    arrived_other = ring_middle(pairs_out[4:], passed_other, 1)
-    arrived_own = ring_middle(pairs_out[:4], passed_own, -1)
-    total_other = move(ring_end(pairs_out[4:], arrived_other).astype(bf16), l=1)
-    totals = ring_end(pairs_out[:4], arrived_own) + total_other.astype(f32)
+    passed_below, passed_above = move(pairs_out[6], x=1), move(pairs_out[2], x=-1)
+
+    def passed_body(n_ref, up_ref, from_below, here_ref, down_ref, from_above, there_ref, up_out, down_out):
+        up_out[0:2] = wide(up_ref, from_below).astype(bf16)
+        up_out[2:4] = here_ref[...]
+        down_out[0:2] = wide(down_ref, from_above).astype(bf16)
+        down_out[2:4] = there_ref[...]
+
+    ups, downs = blocks_call(
+        "passed_sums",
+        passed_body,
+        numbers,
+        [
+            (v, pair_shape, lambda n: 0)
+            for v in (
+                pairs_out[5],
+                passed_below,
+                pairs_out[1],
+                pairs_out[3],
+                passed_above,
+                pairs_out[7],
+            )
+        ],
+        ((4, 128, width),) * 2,
+        (a_away,),
+    )
+    from_device_below, from_device_above = move(ups, x=1), move(downs, x=-1)
+
+    def ends_body(n_ref, keep_ref, got_ref, below_ref, above_ref, leave_ref, stay_ref):
+        total = wide(keep_ref, got_ref, below_ref, above_ref).astype(bf16)
+        first = n_ref[3] == 0
+        leave_ref[0] = jnp.where(first, total[1], total[0])
+        stay_ref[0] = jnp.where(first, total[0], total[1])
+
+    leaves, stays = blocks_call(
+        "end_sums",
+        ends_body,
+        numbers,
+        [(v, pair_shape, turn(0)) for v in (keep, got)]
+        + [(v, pair_shape, lambda n: 0) for v in (from_below, from_above)],
+        (one, one),
+        (a_away,),
+    )
+    crossed = move(leaves, h=1)
+
+    def around_body(n_ref, keep_ref, got_ref, crossed_ref, low_ref, high_ref, above_ref, own_ref, below_ref):
+        def part(k):
+            at = (n_ref[2] + k) % 4
+            return wide(keep_ref.at[at], got_ref.at[at], crossed_ref.at[at]).astype(bf16)
+
+        far = part(2)
+        low_ref[...] = far[:32]
+        high_ref[...] = far[32:]
+        above_ref[...] = part(1)
+        own_ref[...] = part(0)
+        below_ref[...] = part(3)
+
+    a_low, a_high, a_above, a_own, a_below = blocks_call(
+        "around_sums",
+        around_body,
+        numbers,
+        [(v, four, lambda n: n[3]) for v in (a_keep, a_got)] + [(a_crossed, four, lambda n: 0)],
+        ((32, width), (32, width), (64, width), (64, width), (64, width)),
+        (leaves,),
+    )
+    a_low, a_high = move(a_low, y=1), move(a_high, y=-1)
+
+    def beside_body(n_ref, above_ref, below_ref, low_ref, high_ref, up_ref, down_ref):
+        up_ref[0:32] = (above_ref[0:32].astype(f32) + low_ref[...].astype(f32)).astype(bf16)
+        up_ref[32:64] = above_ref[32:64]
+        down_ref[0:32] = below_ref[0:32]
+        down_ref[32:64] = (below_ref[32:64].astype(f32) + high_ref[...].astype(f32)).astype(bf16)
+
+    a_above, a_below = blocks_call(
+        "beside_sums",
+        beside_body,
+        numbers,
+        [(v, v.shape, lambda n: 0) for v in (a_above, a_below, a_low, a_high)],
+        ((64, width), (64, width)),
+        (crossed,),
+    )
+    a_from_below, a_from_above = move(a_above, y=1), move(a_below, y=-1)
+
+    part, stays = packed_sums(
+        stays,
+        crossed,
+        a_own,
+        a_from_below,
+        a_from_above,
+        ff,
+        head,
+        (smalls,),
+    )
+    part = lax.all_to_all(part, "shard", 0, 0).reshape(1, 128, cols)
+
+    total = pairs_out[4].astype(f32) + from_device_below[:2].astype(f32)
+    total = (total + from_device_above[2:].astype(f32)).astype(bf16)
+    totals = pairs_out[0].astype(f32) + from_device_below[2:].astype(f32)
+    totals = totals + from_device_above[:2].astype(f32) + move(total, l=1).astype(f32)
     mixed = (tokens.astype(f32) + totals[0]).astype(bf16)
     own_sum = totals[1]
     own_normed, own_inverse = normalize(tokens)
@@ -1094,73 +1156,16 @@
         - own_normed * jnp.mean(own_sum * own_normed, -1, keepdims=True)
     )
 
-    def ends_body(n_ref, keep_ref, got_ref, below_ref, above_ref, leave_ref, stay_ref):
-        total = wide(keep_ref, got_ref, below_ref, above_ref).astype(bf16)
-        first = n_ref[3] == 0
-        leave_ref[0] = jnp.where(first, total[1], total[0])
-        stay_ref[0] = jnp.where(first, total[0], total[1])
-
-    leaves, stays = blocks_call(
-        "end_sums",
-        ends_body,
-        numbers,
-        [(v, pair_shape, turn(0)) for v in (keep, got)]
-        + [(v, pair_shape, lambda n: 0) for v in (from_below, from_above)],
-        (one, one),
-        (a_away, passed_other, passed_own),
-    )
-    crossed = move(leaves, h=1)
-
-    def around_body(n_ref, keep_ref, got_ref, crossed_ref, low_ref, high_ref, above_ref, own_ref, below_ref):
-        def part(k):
-            at = (n_ref[2] + k) % 4
-            return wide(keep_ref.at[at], got_ref.at[at], crossed_ref.at[at]).astype(bf16)
-
-        far = part(2)
-        low_ref[...] = far[:32]
-        high_ref[...] = far[32:]
-        above_ref[...] = part(1)
-        own_ref[...] = part(0)
-        below_ref[...] = part(3)
-
-    a_low, a_high, a_above, a_own, a_below = blocks_call(
-        "around_sums",
-        around_body,
-        numbers,
-        [(v, four, lambda n: n[3]) for v in (a_keep, a_got)] + [(a_crossed, four, lambda n: 0)],
-        ((32, width), (32, width), (64, width), (64, width), (64, width)),
-        (leaves,),
-    )
-    a_low, a_high = move(a_low, y=1), move(a_high, y=-1)
-
-    def beside_body(n_ref, above_ref, below_ref, low_ref, high_ref, up_ref, down_ref):
-        up_ref[0:32] = (above_ref[0:32].astype(f32) + low_ref[...].astype(f32)).astype(bf16)
-        up_ref[32:64] = above_ref[32:64]
-        down_ref[0:32] = below_ref[0:32]
-        down_ref[32:64] = (below_ref[32:64].astype(f32) + high_ref[...].astype(f32)).astype(bf16)
-
-    a_above, a_below = blocks_call(
-        "beside_sums",
-        beside_body,
-        numbers,
-        [(v, v.shape, lambda n: 0) for v in (a_above, a_below, a_low, a_high)],
-        ((64, width), (64, width)),
-        (),
-    )
-    a_from_below, a_from_above = move(a_above, y=1), move(a_below, y=-1)
-
-    part, stays = packed_sums(
-        stays, crossed, a_own, a_from_below, a_from_above, ff, head, (smalls, *arrived_other)
-    )
-    stays = lax.all_gather(stays, "rep", axis=0)
-    part = lax.all_to_all(part, "shard", 0, 0).reshape(1, 128, cols)
-
-    part = jnp.concatenate([part, move(part, h=1)])
-    below, above = move(part, y=1), move(part, y=-1)
-    far_low, far_high = move(below[:1], y=1), move(above[1:], y=-1)
-    pieces = [(v, move(v, c=1)) for v in (part, above, below, far_low, far_high)]
     order = ((0, h), (0, 1 - h), (1, h), (1, 1 - h), (3, h), (3, 1 - h), (2, h), (2, 1 - h))
     places = jnp.stack([(y + k) % 4 * 2 + high for k, high in order]).astype(jnp.int32)
+
+    def rep_gather(own):
+        own = jnp.concatenate([own, move(own, h=1)])
+        below, above = move(own, y=1), move(own, y=-1)
+        return (own, above, below), (move(below[:1], y=1), move(above[1:], y=-1))
+
+    near, far = rep_gather(part)
+    near = [(v, move(v, c=1)) for v in near]
     targets = [
         (
             3 * width,
@@ -1173,10 +1178,28 @@
         ),
         (8 * ff, 16, [(source * ff, 16 * source, 3 * head, ff) for source in range(8)]),
     ]
-    down_grad, out_grad = stayed(stays, ())
-    grads = spread(pieces[:3], places[:6], numbers[:1], targets, 8, (), ())
+    grads = spread(near, places[:6], numbers[:1], targets, 8, (), ())
+    far = joined(far, (grads[0],))
+
+    near_stays, far_stays = rep_gather(stays[None])
+    stays = joined(near_stays + far_stays, ())
+    down_grad, out_grad = spread(
+        [(stays, move(stays, c=1))],
+        places,
+        numbers[:1],
+        [(width, 64, [(0, 0, 0, width)]), (width, 16, [(0, 64, 0, width)])],
+        8,
+        (),
+        (),
+    )
     qkv_grad, up_grad = spread(
-        pieces[3:], places[6:], numbers[:1], targets, 8, grads, (tokens_grad, mixed, down_grad)
+        [(far, move(far, c=1))],
+        places[6:],
+        numbers[:1],
+        targets,
+        8,
+        grads,
+        (tokens_grad, mixed, down_grad),
     )
     norm_grads = smalls[:8].reshape(4, 256)
     dy_total = smalls[22:].reshape(256)

time: 432 us -> 386 us (0.89)
  waiting for transfers between devices: 130 us -> 85.8 us
  Pallas kernels: 143 us -> 158 us
  between operations: 15 us -> 1.66 us
    ppermute x44 -> x47, waiting for transfers between devices: 109 us -> 74.2 us  [move(): return lax.ppermute(value, BOTH, pairs)]
    all_to_all x1, waiting for transfers between devices: 11.6 us -> 2.21 us  [local(): part = lax.all_to_all(part, 'shard', 0, 0).reshape(1, 128, cols)]
    pallas_call x2 -> x3, Pallas kernels: 12.9 us -> 21.1 us  [spread(): pl.pallas_call(after_inputs(body, 2 + 2 * len(pieces) + len(before), len(...]
    pallas_call x1 -> x3, Pallas kernels: 3.71 us -> 11.9 us  [joined(): pl.pallas_call(after_inputs(body, count, len(after)), out_shape=jax.Shape...]
    pallas_call x1 -> x0, Pallas kernels: 7.01 us -> none  [stayed(): pl.pallas_call(after_inputs(body, 1, len(after)), out_shape=(jax.ShapeDty...]
    broadcast_in_dim x5 -> x0, local copies, waits for them, and re-layouts: 6.14 us -> none  [local(): v[None]]
    pallas_call x6 -> x7, Pallas kernels: 22.4 us -> 28.1 us  [blocks_call(): pl.pallas_call(after_inputs(body, 1 + len(terms), len(after)), out_shape=...]
    convert_element_type x3 -> x1, other arithmetic: 7.45 us -> 2.09 us  [local(): total = (total + from_device_above[2:].astype(f32)).astype(bf16)]
  transfers between devices with their start and end apart: 48 -> 50, of which waited for: 14 -> 14; matrix products, arithmetic and copies ran while one was open for 7% -> 7% of each run, Pallas kernels for 22% -> 30%
where the time goes in v6:
time: 386 us; the launch traced here: 378 us
  Pallas kernels  158 us (41%)
  starting transfers between devices  91 us (24%)
  waiting for transfers between devices  85.8 us (22%)
  local copies, waits for them, and re-layouts  25.4 us (7%)
  other arithmetic  16.5 us (4%)
    ppermute x47, starting transfers between devices, move(): return lax.ppermute(value, BOTH, pairs)  78.2 us
    ppermute x47, waiting for transfers between devices, move(): return lax.ppermute(value, BOTH, pairs)  74.2 us
    pallas_call x1, Pallas kernels, feed_forward(): pl.pallas_call(after_inputs(body, 5 + parts + 2 * count, len(after)), out...  32.2 us
    pallas_call x7, Pallas kernels, blocks_call(): pl.pallas_call(after_inputs(body, 1 + len(terms), len(after)), out_shape=...  28.1 us
    pallas_call x1, Pallas kernels, outer(): pl.pallas_call(after_inputs(body, 11 + parts + count, len(after)), out_sh...  26.2 us
    pallas_call x1, Pallas kernels, attend(): pl.pallas_call(after_inputs(body, 8 + parts + count, len(after)), out_sha...  25.8 us
    pallas_call x3, Pallas kernels, spread(): pl.pallas_call(after_inputs(body, 2 + 2 * len(pieces) + len(before), len(...  21.1 us
    unnamed x75, local copies, waits for them, and re-layouts  14.4 us
  transfers between devices with their start and end apart: 50, of which 14 were waited for; matrix products, arithmetic and copies ran while one was open for 7% of the time, Pallas kernels for 30%

profile of v6, /device:TPU:1, one launch (start us, length us, event | category | flops | bytes accessed | tf_op | source)
XLA Modules:
  0.0 378.5 jit_solution(9391326150341474421)
XLA Ops:
  0.7 3.6 packed.1
  9.4 3.6 all-to-all-start
  13.0 17.2 %collective-permute-done.1.refs_2_.refs_17_.refs_25_.refs_18_ = bf16[2,128,2048]{2,1,0:T(8,128)(2,1)S(1)} collective-permute-done((bf16[2,128,2048]{2,1,0:T(8,128)(2,1)}, bf16[2,128,2048]{2,1,0:T(8,128)(2,1)S(1)}, u32[]{:S(2)}, u32[]{:S(2)}) %collective-permute-start.1) | collective-permute-done | bytes 1048608 | tf_op jit(solution)/shard_map/ppermute | solution.py:45
  34.9 9.3 %all-to-all-done.refs_0_ = bf16[8,40,1792]{2,1,0:T(8,128)(2,1)S(1)} async-done(((bf16[8,40,1792]{2,1,0:T(8,128)(2,1)}), bf16[8,40,1792]{2,1,0:T(8,128)(2,1)S(1)}, u32[]{:S(2)}, u32[]{:S(2)}) %all-to-all-start) | async-done | bytes 1146912 | tf_op jit(solution)/shard_map/all_to_all | solution.py:902
  50.4 17.3 %collective-permute-done.3.refs_1_.refs_5_.refs_6_ = bf16[8,32,1792]{2,1,0:T(8,128)(2,1)S(1)} collective-permute-done((bf16[8,32,1792]{2,1,0:T(8,128)(2,1)}, bf16[8,32,1792]{2,1,0:T(8,128)(2,1)S(1)}, u32[]{:S(2)}, u32[]{:S(2)}) %collective-permute-start.3) | collective-permute-done | bytes 917536 | tf_op jit(solution)/shard_map/ppermute | solution.py:45
  67.6 3.0 collective-permute-done.4.refs_0_.refs_2_.refs_8_.refs_9_
  74.4 3.7 joined.3
  78.1 3.9 %collective-permute-start.10 = (bf16[24,32,1792]{2,1,0:T(8,128)(2,1)}, bf16[24,32,1792]{2,1,0:T(8,128)(2,1)S(1)}, u32[]{:S(2)}, u32[]{:S(2)}) collective-permute-start(bf16[24,32,1792]{2,1,0:T(8,128)(2,1)} %joined.3), channel_id=1, source_target_pairs={{0,8},{1,9},{2,10},{3,11},{4,12},{5,13},{6,14},{7,15},{8,0},{9,1},... | collective-permute-start | bytes 8257544 | tf_op jit(solution)/shard_map/ppermute | solution.py:45
  92.5 6.3 %collective-permute-done.8.refs_6_.refs_7_ = bf16[4,32,1792]{2,1,0:T(8,128)(2,1)} collective-permute-done((bf16[4,32,1792]{2,1,0:T(8,128)(2,1)}, bf16[4,32,1792]{2,1,0:T(8,128)(2,1)}, u32[]{:S(2)}, u32[]{:S(2)}) %collective-permute-start.8) | collective-permute-done | bytes 458784 | tf_op jit(solution)/shard_map/ppermute | solution.py:45
  99.7 3.1 fusion.12
  105.6 32.2 %feed_forward.1 = (bf16[1024,2048]{1,0:T(8,128)(2,1)}, bf16[1024,1024]{1,0:T(8,128)(2,1)}, bf16[1024,1024]{1,0:T(8,128)(2,1)}, bf16[8,128,2048]{2,1,0:T(8,128)(2...) custom-call(s32[4]{0:T(128)} %get-tuple-element.136.refs_0_.number_r, ...), custom_call_target="tpu_custom_call" | custom-call | flops 36800000000 | bytes 1000 | tf_op jit(solution)/shard_map/feed_forward/pallas_call | solution.py:250
  141.6 25.8 %attend.1 = (bf16[1024,256]{1,0:T(8,128)(2,1)}, bf16[1024,768]{1,0:T(8,128)(2,1)}, bf16[8,64,2048]{2,1,0:T(8,128)(2,1)}, bf16[8,64,2048]{2,1,0:T(8,128)(2,1)}, f32[1,768]{1,0:T(1,128)}) custom-call(s32[4]{0:T(128)} %get-tuple-element.136.refs_0_.number_ref, s32[8,3]{1,0:T(8,128)} %copy-done.10, s32[8]{0:T(128)} %pad_add_fusion.refs_1_.refs_2_.refs_0_, ...), custom_call_target="tpu_custom_call" | custom-call | flops 25300000768 | bytes 1000 | tf_op jit(solution)/shard_map/attend/pallas_call | solution.py:457
  167.6 3.3 far_sums.1
  173.8 26.2 %outer.1 = (f32[4,2048]{1,0:T(4,128)}, bf16[2,128,2048]{2,1,0:T(8,128)(2,1)}, bf16[2,128,2048]{2,1,0:T(8,128)(2,1)}, bf16[2,128,2048]{2,1,0:T(8,128)(2,1)}, bf16...) custom-call(s32[8]{0:T(128)} %pad_add_fusion.refs_1_.refs_2_.refs_0_, ...), custom_call_target="tpu_custom_call" | custom-call | flops 23000000512 | bytes 1000 | tf_op jit(solution)/shard_map/outer/pallas_call | solution.py:578
  203.7 4.7 %near_sums.1 = (bf16[2,128,2048]{2,1,0:T(8,128)(2,1)}, bf16[2,128,2048]{2,1,0:T(8,128)(2,1)}) custom-call(s32[4]{0:T(128)} %get-tuple-element.136.refs_0_.number_ref, bf16[8,128,2048]{2,1,0:T(8,128)(2,1)} %get-tuple-element.84.refs_1_.refs_3_, bf16[8,128,2048]{2,1,0:T(8,128)(2,1)} %collective-permute-done.15.refs_2_.refs_4_, ...), custom_call_target="tpu_custom_call" | custom-call | flops 3449999872 | bytes 1000 | tf_op jit(solution)/shard_map/near_sums/pallas_call | solution.py:744
  212.5 3.5 away_sums.1.refs_7_.refs_5_
  216.0 3.3 collective-permute-start.27
  222.9 5.8 %all-to-all-start.1 = ((bf16[128,24,128]{2,1,0:T(8,128)(2,1)}), bf16[128,24,128]{2,1,0:T(8,128)(2,1)S(1)}, u32[]{:S(2)}, u32[]{:S(2)}) async-start(bf16[128,24,128]{2,1,0:T(8,128)(2,1)} %bitcast.13), calls=%async_computation.1 | async-start | bytes 1572864 | tf_op jit(solution)/shard_map/all_to_all | solution.py:1048
  230.0 5.7 %passed_sums.1 = (bf16[4,128,2048]{2,1,0:T(8,128)(2,1)}, bf16[4,128,2048]{2,1,0:T(8,128)(2,1)}) custom-call(s32[4]{0:T(128)} %get-tuple-element.136.refs_0_.number_ref, bf16[2,128,2048]{2,1,0:T(8,128)(2,1)} %get-tuple-element.88.refs_1_, bf16[2,128,2048]{2,1,0:T(8,128)(2,1)} %copy-done.20, bf16[2,128,2048]{2,1,0:T(8,128)(2,1)} %get-tuple-element.90.refs_3_, ...), custom_call_target="tpu_custom_call" | custom-call | flops 3449999872 | bytes 1000 | tf_op jit(solution)/shard_map/passed_sums/pallas_call | solution.py:744
  238.5 4.3 %end_sums.1 = (bf16[1,128,2048]{2,1,0:T(8,128)(2,1)}, bf16[1,128,2048]{2,1,0:T(8,128)(2,1)}) custom-call(s32[4]{0:T(128)} %get-tuple-element.136.refs_0_.number_ref, bf16[8,128,2048]{2,1,0:T(8,128)(2,1)} %get-tuple-element.84.refs_1_.refs_3_, bf16[8,128,2048]{2,1,0:T(8,128)(2,1)} %collective-permute-done.15.refs_2_.refs_4_, ...), custom_call_target="tpu_custom_call" | custom-call | flops 3449999872 | bytes 1000 | tf_op jit(solution)/shard_map/end_sums/pallas_call | solution.py:744
  242.8 3.4 collective-permute-start.26
  249.0 3.8 around_sums.1
  267.8 3.2 collective-permute-done.30.refs_3_
  276.4 3.5 all-to-all-start.2
  288.6 4.8 %collective-permute-start.32 = (bf16[1,128,1792]{2,1,0:T(8,128)(2,1)S(1)}, bf16[1,128,1792]{2,1,0:T(8,128)(2,1)S(1)}, u32[]{:S(2)}, u32[]{:S(2)}) collective-permute-start(bf16[1,128,1792]{2,1,0:T(8,128)(2,1)S(1)} %bitcast.56), channel_id=1, source_target_pairs={{0,16},{1,17},{2,18},{3,19},{4,20},{5,21},{6,22},{7,23},{8,24},{9,... | collective-permute-start | bytes 1376264 | tf_op jit(solution)/shard_map/ppermute | solution.py:45
  295.7 4.6 %collective-permute-done.32 = bf16[1,128,1792]{2,1,0:T(8,128)(2,1)S(1)} collective-permute-done((bf16[1,128,1792]{2,1,0:T(8,128)(2,1)S(1)}, bf16[1,128,1792]{2,1,0:T(8,128)(2,1)S(1)}, u32[]{:S(2)}, u32[]{:S(2)}) %collective-permute-start.32) | collective-permute-done | bytes 458784 | tf_op jit(solution)/shard_map/ppermute | solution.py:45
  309.6 13.3 %collective-permute-done.44.refs_3_ = bf16[1,80,2048]{2,1,0:T(8,128)(2,1)S(1)} collective-permute-done((bf16[1,80,2048]{2,1,0:T(8,128)(2,1)S(1)}, bf16[1,80,2048]{2,1,0:T(8,128)(2,1)S(1)}, u32[]{:S(2)}, u32[]{:S(2)}) %collective-permute-start.44) | collective-permute-done | bytes 327712 | tf_op jit(solution)/shard_map/ppermute | solution.py:45
  322.9 10.6 %collective-permute-start.37 = (bf16[2,128,1792]{2,1,0:T(8,128)(2,1)S(1)}, bf16[2,128,1792]{2,1,0:T(8,128)(2,1)}, u32[]{:S(2)}, u32[]{:S(2)}) collective-permute-start(bf16[2,128,1792]{2,1,0:T(8,128)(2,1)S(1)} %pad_maximum_fusion.refs_2_), channel_id=1, source_target_pairs={{0,8},{1,9},{2,10},{3,11},{4,12},{5,13},{6,14},{7,15},{8,0},{9,1},... | collective-permute-start | bytes 2752520 | tf_op jit(solution)/shard_map/ppermute | solution.py:45
  334.2 6.0 %joined.5.refs_2_ = bf16[8,80,2048]{2,1,0:T(8,128)(2,1)} custom-call(bf16[2,80,2048]{2,1,0:T(8,128)(2,1)} %pad_maximum_fusion.1.refs_0_, bf16[2,80,2048]{2,1,0:T(8,128)(2,1)} %collective-permute-done.42.refs_1_, bf16[2,80,2048]{2,1,0:T(8,128)(2,1)} %collective-permute-done.43.refs_2_, bf16[1,80,2048]{2,1,0:T(8,128)(2,1)} %copy-done.31, ...), custom_call_target="tpu_custom_call" | custom-call | flops 3449999872 | bytes 1000 | tf_op jit(solution)/shard_map/joined/pallas_call | solution.py:727
  351.0 8.7 %spread.3 = (f32[256,6144]{1,0:T(8,128)}, f32[256,8192]{1,0:T(8,128)}) custom-call(s32[6]{0:T(128)} %stack.71.refs_0_, s32[1]{0:T(128)} %bitcast.refs_1_, bf16[2,128,1792]{2,1,0:T(8,128)(2,1)} %copy-done.3, bf16[2,128,1792]{2,1,0:T(8,128)(2,1)} %collective-permute-done.37.refs_3_, bf16[2,128,1792]{2,1,0:T(8,128)(2,1)} %collective-permute-done.35.refs_4_, ...), custom_call_target="tpu_custom_call" | custom-call | flops 8280000000 | bytes 1000 | tf_op jit(solution)/shard_map/spread/pallas_call | solution.py:806
  364.0 8.7 %spread.4 = (f32[1024,2048]{1,0:T(8,128)}, f32[256,2048]{1,0:T(8,128)}) custom-call(s32[8]{0:T(128)} %stack.72.refs_0_, s32[1]{0:T(128)} %bitcast.refs_1_, bf16[8,80,2048]{2,1,0:T(8,128)(2,1)} %joined.5.refs_2_, bf16[8,80,2048]{2,1,0:T(8,128)(2,1)} %collective-permute-done.46.refs_3_), custom_call_target="tpu_custom_call" | custom-call | flops 11040000000 | bytes 1000 | tf_op jit(solution)/shard_map/spread/pallas_call | solution.py:806
  373.7 3.8 %spread.5 = (f32[256,6144]{1,0:T(8,128)}, f32[256,8192]{1,0:T(8,128)}) custom-call(s32[2]{0:T(128)} %pad_add_fusion.2.refs_0_, s32[1]{0:T(128)} %bitcast.refs_1_, bf16[2,128,1792]{2,1,0:T(8,128)(2,1)} %joined.4.refs_2_, bf16[2,128,1792]{2,1,0:T(8,128)(2,1)} %copy-done.4, ...), custom_call_target="tpu_custom_call", output_to_operand_aliasing={{0}: (4, {}), {1}: (5, {})} | custom-call | flops 2760000000 | bytes 1000 | tf_op jit(solution)/shard_map/spread/pallas_call | solution.py:806
  (218 shorter events, 116.3 us)
Async XLA Ops:
  4.3 26.0 %collective-permute-start.1 = (bf16[2,128,2048]{2,1,0:T(8,128)(2,1)}, bf16[2,128,2048]{2,1,0:T(8,128)(2,1)S(1)}, u32[]{:S(2)}, u32[]{:S(2)}) collective-permute-start(bf16[2,128,2048]{2,1,0:T(8,128)(2,1)} %get-tuple-element.69.refs_14_.refs_22_.refs_15_), channel_id=1, source_target_pairs={{0,1},{1,2},{2,3},{3,0},{4,5},{5,6},{6,7},{7,4},{8,9},{9,10},{10,1... | collective-permute-start | bytes 3145736 | tf_op jit(solution)/shard_map/ppermute | solution.py:45
  6.3 26.0 %collective-permute-start.2 = (bf16[2,128,2048]{2,1,0:T(8,128)(2,1)}, bf16[2,128,2048]{2,1,0:T(8,128)(2,1)S(1)}, u32[]{:S(2)}, u32[]{:S(2)}) collective-permute-start(bf16[2,128,2048]{2,1,0:T(8,128)(2,1)} %get-tuple-element.69.refs_14_.refs_22_.refs_15_), channel_id=1, source_target_pairs={{0,4},{1,5},{2,6},{3,7},{4,0},{5,1},{6,2},{7,3},{8,12},{9,13},{10,... | collective-permute-start | bytes 3145736 | tf_op jit(solution)/shard_map/ppermute | solution.py:45
  8.0 36.2 %collective-permute-start = (bf16[2,128,2048]{2,1,0:T(8,128)(2,1)}, bf16[2,128,2048]{2,1,0:T(8,128)(2,1)}, u32[]{:S(2)}, u32[]{:S(2)}) collective-permute-start(bf16[2,128,2048]{2,1,0:T(8,128)(2,1)} %get-tuple-element.69.refs_14_.refs_22_.refs_15_), channel_id=1, source_target_pairs={{0,3},{1,0},{2,1},{3,2},{4,7},{5,4},{6,5},{7,6},{8,11},{9,8},{10,9... | collective-permute-start | bytes 3145736 | tf_op jit(solution)/shard_map/ppermute | solution.py:45
  9.4 34.8 %all-to-all-start = ((bf16[8,40,1792]{2,1,0:T(8,128)(2,1)}), bf16[8,40,1792]{2,1,0:T(8,128)(2,1)S(1)}, u32[]{:S(2)}, u32[]{:S(2)}) async-start(bf16[8,40,1792]{2,1,0:T(8,128)(2,1)} %get-tuple-element.68), calls=%async_computation | async-start | bytes 2293760 | tf_op jit(solution)/shard_map/all_to_all | solution.py:902
  30.2 40.4 %collective-permute-start.5 = (bf16[2,128,2048]{2,1,0:T(8,128)(2,1)S(1)}, bf16[2,128,2048]{2,1,0:T(8,128)(2,1)}, u32[]{:S(2)}, u32[]{:S(2)}) collective-permute-start(bf16[2,128,2048]{2,1,0:T(8,128)(2,1)S(1)} %collective-permute-done.1.refs_2_.refs_17_.refs_25_.refs_18_), channel_id=1, source_target_pairs={{0,4},{1,5},{2,6},{3,7},{4,0},{5,1},{6,2},{7,3},{8,12},{9,13},{10,... | collective-permute-start | bytes 3145736 | tf_op jit(solution)/shard_map/ppermute | solution.py:45
  32.2 38.5 %collective-permute-start.7 = (bf16[2,128,2048]{2,1,0:T(8,128)(2,1)S(1)}, bf16[2,128,2048]{2,1,0:T(8,128)(2,1)}, u32[]{:S(2)}, u32[]{:S(2)}) collective-permute-start(bf16[2,128,2048]{2,1,0:T(8,128)(2,1)S(1)} %collective-permute-done.1.refs_2_.refs_17_.refs_25_.refs_18_), channel_id=1, source_target_pairs={{0,1},{1,2},{2,3},{3,0},{4,5},{5,6},{6,7},{7,4},{8,9},{9,10},{10,1... | collective-permute-start | bytes 3145736 | tf_op jit(solution)/shard_map/ppermute | solution.py:45
  32.3 38.4 %collective-permute-start.6 = (bf16[2,128,2048]{2,1,0:T(8,128)(2,1)S(1)}, bf16[2,128,2048]{2,1,0:T(8,128)(2,1)}, u32[]{:S(2)}, u32[]{:S(2)}) collective-permute-start(bf16[2,128,2048]{2,1,0:T(8,128)(2,1)S(1)} %collective-permute-done.2.refs_3_.refs_18_.refs_26_.refs_19_), channel_id=1, source_target_pairs={{0,3},{1,0},{2,1},{3,2},{4,7},{5,4},{6,5},{7,6},{8,11},{9,8},{10,9... | collective-permute-start | bytes 3145736 | tf_op jit(solution)/shard_map/ppermute | solution.py:45
  47.6 20.0 %collective-permute-start.3 = (bf16[8,32,1792]{2,1,0:T(8,128)(2,1)}, bf16[8,32,1792]{2,1,0:T(8,128)(2,1)S(1)}, u32[]{:S(2)}, u32[]{:S(2)}) collective-permute-start(bf16[8,32,1792]{2,1,0:T(8,128)(2,1)} %get-tuple-element.71.refs_0_.refs_4_.refs_5_), channel_id=1, source_target_pairs={{0,96},{1,97},{2,98},{3,99},{4,100},{5,101},{6,102},{7,103},{8,104... | collective-permute-start | bytes 2752520 | tf_op jit(solution)/shard_map/ppermute | solution.py:45
  50.4 20.3 %collective-permute-start.4 = (bf16[8,32,1792]{2,1,0:T(8,128)(2,1)}, bf16[8,32,1792]{2,1,0:T(8,128)(2,1)S(1)}, u32[]{:S(2)}, u32[]{:S(2)}) collective-permute-start(bf16[8,32,1792]{2,1,0:T(8,128)(2,1)} %get-tuple-element.71.refs_0_.refs_4_.refs_5_), channel_id=1, source_target_pairs={{0,32},{1,33},{2,34},{3,35},{4,36},{5,37},{6,38},{7,39},{8,40},{9,... | collective-permute-start | bytes 2752520 | tf_op jit(solution)/shard_map/ppermute | solution.py:45
  78.1 25.4 %collective-permute-start.10 = (bf16[24,32,1792]{2,1,0:T(8,128)(2,1)}, bf16[24,32,1792]{2,1,0:T(8,128)(2,1)S(1)}, u32[]{:S(2)}, u32[]{:S(2)}) collective-permute-start(bf16[24,32,1792]{2,1,0:T(8,128)(2,1)} %joined.3), channel_id=1, source_target_pairs={{0,8},{1,9},{2,10},{3,11},{4,12},{5,13},{6,14},{7,15},{8,0},{9,1},... | collective-permute-start | bytes 8257544 | tf_op jit(solution)/shard_map/ppermute | solution.py:45
  137.9 29.7 %collective-permute-start.15 = (bf16[8,128,2048]{2,1,0:T(8,128)(2,1)}, bf16[8,128,2048]{2,1,0:T(8,128)(2,1)}, u32[]{:S(2)}, u32[]{:S(2)}) collective-permute-start(bf16[8,128,2048]{2,1,0:T(8,128)(2,1)} %get-tuple-element.79.refs_26_), channel_id=1, source_target_pairs={{0,8},{1,9},{2,10},{3,11},{4,12},{5,13},{6,14},{7,15},{8,0},{9,1},... | collective-permute-start | bytes 12582920 | tf_op jit(solution)/shard_map/ppermute | solution.py:45
  167.5 43.7 %collective-permute-start.18 = (bf16[8,64,2048]{2,1,0:T(8,128)(2,1)}, bf16[8,64,2048]{2,1,0:T(8,128)(2,1)S(1)}, u32[]{:S(2)}, u32[]{:S(2)}) collective-permute-start(bf16[8,64,2048]{2,1,0:T(8,128)(2,1)} %get-tuple-element.95), channel_id=1, source_target_pairs={{0,8},{1,9},{2,10},{3,11},{4,12},{5,13},{6,14},{7,15},{8,0},{9,1},... | collective-permute-start | bytes 6291464 | tf_op jit(solution)/shard_map/ppermute | solution.py:45
  170.9 31.9 %collective-permute-start.19 = (bf16[1,128,2048]{2,1,0:T(8,128)(2,1)}, bf16[1,128,2048]{2,1,0:T(8,128)(2,1)S(1)}, u32[]{:S(2)}, u32[]{:S(2)}) collective-permute-start(bf16[1,128,2048]{2,1,0:T(8,128)(2,1)} %get-tuple-element.85.refs_29_), channel_id=1, source_target_pairs={{0,32},{1,33},{2,34},{3,35},{4,36},{5,37},{6,38},{7,39},{8,40},{9,... | collective-permute-start | bytes 1572872 | tf_op jit(solution)/shard_map/ppermute | solution.py:45
  170.9 31.9 %collective-permute-start.20 = (bf16[1,128,2048]{2,1,0:T(8,128)(2,1)}, bf16[1,128,2048]{2,1,0:T(8,128)(2,1)S(1)}, u32[]{:S(2)}, u32[]{:S(2)}) collective-permute-start(bf16[1,128,2048]{2,1,0:T(8,128)(2,1)} %get-tuple-element.86.refs_30_), channel_id=1, source_target_pairs={{0,96},{1,97},{2,98},{3,99},{4,100},{5,101},{6,102},{7,103},{8,104... | collective-permute-start | bytes 1572872 | tf_op jit(solution)/shard_map/ppermute | solution.py:45
  200.0 28.7 %collective-permute-start.16 = (bf16[2,128,2048]{2,1,0:T(8,128)(2,1)}, bf16[2,128,2048]{2,1,0:T(8,128)(2,1)S(1)}, u32[]{:S(2)}, u32[]{:S(2)}) collective-permute-start(bf16[2,128,2048]{2,1,0:T(8,128)(2,1)} %get-tuple-element.89), channel_id=1, source_target_pairs={{0,1},{1,2},{2,3},{3,0},{4,5},{5,6},{6,7},{7,4},{8,9},{9,10},{10,1... | collective-permute-start | bytes 3145736 | tf_op jit(solution)/shard_map/ppermute | solution.py:45
  200.2 28.5 %collective-permute-start.17 = (bf16[2,128,2048]{2,1,0:T(8,128)(2,1)}, bf16[2,128,2048]{2,1,0:T(8,128)(2,1)S(1)}, u32[]{:S(2)}, u32[]{:S(2)}) collective-permute-start(bf16[2,128,2048]{2,1,0:T(8,128)(2,1)} %get-tuple-element.92), channel_id=1, source_target_pairs={{0,3},{1,0},{2,1},{3,2},{4,7},{5,4},{6,5},{7,6},{8,11},{9,8},{10,9... | collective-permute-start | bytes 3145736 | tf_op jit(solution)/shard_map/ppermute | solution.py:45
  208.5 30.0 %collective-permute-start.24 = (bf16[2,128,2048]{2,1,0:T(8,128)(2,1)}, bf16[2,128,2048]{2,1,0:T(8,128)(2,1)}, u32[]{:S(2)}, u32[]{:S(2)}) collective-permute-start(bf16[2,128,2048]{2,1,0:T(8,128)(2,1)} %get-tuple-element.96.refs_3_), channel_id=1, source_target_pairs={{0,32},{1,33},{2,34},{3,35},{4,36},{5,37},{6,38},{7,39},{8,40},{9,... | collective-permute-start | bytes 3145736 | tf_op jit(solution)/shard_map/ppermute | solution.py:45
  208.5 30.0 %collective-permute-start.25 = (bf16[2,128,2048]{2,1,0:T(8,128)(2,1)}, bf16[2,128,2048]{2,1,0:T(8,128)(2,1)}, u32[]{:S(2)}, u32[]{:S(2)}) collective-permute-start(bf16[2,128,2048]{2,1,0:T(8,128)(2,1)} %get-tuple-element.104), channel_id=1, source_target_pairs={{0,96},{1,97},{2,98},{3,99},{4,100},{5,101},{6,102},{7,103},{8,104... | collective-permute-start | bytes 3145736 | tf_op jit(solution)/shard_map/ppermute | solution.py:45
  216.0 33.0 %collective-permute-start.27 = (bf16[4,64,2048]{2,1,0:T(8,128)(2,1)}, bf16[4,64,2048]{2,1,0:T(8,128)(2,1)}, u32[]{:S(2)}, u32[]{:S(2)}) collective-permute-start(bf16[4,64,2048]{2,1,0:T(8,128)(2,1)} %away_sums.1.refs_7_.refs_5_), channel_id=1, source_target_pairs={{0,16},{1,17},{2,18},{3,19},{4,20},{5,21},{6,22},{7,23},{8,24},{9,... | collective-permute-start | bytes 3145736 | tf_op jit(solution)/shard_map/ppermute | solution.py:45
  222.9 44.2 %all-to-all-start.1 = ((bf16[128,24,128]{2,1,0:T(8,128)(2,1)}), bf16[128,24,128]{2,1,0:T(8,128)(2,1)S(1)}, u32[]{:S(2)}, u32[]{:S(2)}) async-start(bf16[128,24,128]{2,1,0:T(8,128)(2,1)} %bitcast.13), calls=%async_computation.1 | async-start | bytes 1572864 | tf_op jit(solution)/shard_map/all_to_all | solution.py:1048
  235.8 57.7 %collective-permute-start.21 = (bf16[4,128,2048]{2,1,0:T(8,128)(2,1)}, bf16[4,128,2048]{2,1,0:T(8,128)(2,1)S(1)}, u32[]{:S(2)}, u32[]{:S(2)}) collective-permute-start(bf16[4,128,2048]{2,1,0:T(8,128)(2,1)} %get-tuple-element.97), channel_id=1, source_target_pairs={{0,1},{1,2},{2,3},{3,0},{4,5},{5,6},{6,7},{7,4},{8,9},{9,10},{10,1... | collective-permute-start | bytes 6291464 | tf_op jit(solution)/shard_map/ppermute | solution.py:45
  237.2 56.3 %collective-permute-start.22 = (bf16[4,128,2048]{2,1,0:T(8,128)(2,1)}, bf16[4,128,2048]{2,1,0:T(8,128)(2,1)}, u32[]{:S(2)}, u32[]{:S(2)}) collective-permute-start(bf16[4,128,2048]{2,1,0:T(8,128)(2,1)} %get-tuple-element.98), channel_id=1, source_target_pairs={{0,3},{1,0},{2,1},{3,2},{4,7},{5,4},{6,5},{7,6},{8,11},{9,8},{10,9... | collective-permute-start | bytes 6291464 | tf_op jit(solution)/shard_map/ppermute | solution.py:45
  283.7 19.9 %collective-permute-start.43 = (bf16[2,80,2048]{2,1,0:T(8,128)(2,1)}, bf16[2,80,2048]{2,1,0:T(8,128)(2,1)}, u32[]{:S(2)}, u32[]{:S(2)}) collective-permute-start(bf16[2,80,2048]{2,1,0:T(8,128)(2,1)} %pad_maximum_fusion.1.refs_0_), channel_id=1, source_target_pairs={{0,32},{1,33},{2,34},{3,35},{4,36},{5,37},{6,38},{7,39},{8,40},{9,... | collective-permute-start | bytes 1966088 | tf_op jit(solution)/shard_map/ppermute | solution.py:45
  283.7 22.4 %collective-permute-start.42 = (bf16[2,80,2048]{2,1,0:T(8,128)(2,1)}, bf16[2,80,2048]{2,1,0:T(8,128)(2,1)}, u32[]{:S(2)}, u32[]{:S(2)}) collective-permute-start(bf16[2,80,2048]{2,1,0:T(8,128)(2,1)} %pad_maximum_fusion.1.refs_0_), channel_id=1, source_target_pairs={{0,96},{1,97},{2,98},{3,99},{4,100},{5,101},{6,102},{7,103},{8,104... | collective-permute-start | bytes 1966088 | tf_op jit(solution)/shard_map/ppermute | solution.py:45
  295.6 47.5 %collective-permute-start.23 = (bf16[2,128,2048]{2,1,0:T(8,128)(2,1)S(1)}, bf16[2,128,2048]{2,1,0:T(8,128)(2,1)S(1)}, u32[]{:S(2)}, u32[]{:S(2)}) collective-permute-start(bf16[2,128,2048]{2,1,0:T(8,128)(2,1)S(1)} %add_convert_fusion), channel_id=1, source_target_pairs={{0,4},{1,5},{2,6},{3,7},{4,0},{5,1},{6,2},{7,3},{8,12},{9,13},{10,... | collective-permute-start | bytes 3145736 | tf_op jit(solution)/shard_map/ppermute | solution.py:45
  300.4 40.8 %collective-permute-start.35 = (bf16[2,128,1792]{2,1,0:T(8,128)(2,1)S(1)}, bf16[2,128,1792]{2,1,0:T(8,128)(2,1)}, u32[]{:S(2)}, u32[]{:S(2)}) collective-permute-start(bf16[2,128,1792]{2,1,0:T(8,128)(2,1)S(1)} %pad_maximum_fusion.refs_2_), channel_id=1, source_target_pairs={{0,96},{1,97},{2,98},{3,99},{4,100},{5,101},{6,102},{7,103},{8,104... | collective-permute-start | bytes 2752520 | tf_op jit(solution)/shard_map/ppermute | solution.py:45
  302.5 38.5 %collective-permute-start.33 = (bf16[2,128,1792]{2,1,0:T(8,128)(2,1)S(1)}, bf16[2,128,1792]{2,1,0:T(8,128)(2,1)S(1)}, u32[]{:S(2)}, u32[]{:S(2)}) collective-permute-start(bf16[2,128,1792]{2,1,0:T(8,128)(2,1)S(1)} %pad_maximum_fusion.refs_2_), channel_id=1, source_target_pairs={{0,32},{1,33},{2,34},{3,35},{4,36},{5,37},{6,38},{7,39},{8,40},{9,... | collective-permute-start | bytes 2752520 | tf_op jit(solution)/shard_map/ppermute | solution.py:45
  304.6 18.3 %collective-permute-start.44 = (bf16[1,80,2048]{2,1,0:T(8,128)(2,1)S(1)}, bf16[1,80,2048]{2,1,0:T(8,128)(2,1)S(1)}, u32[]{:S(2)}, u32[]{:S(2)}) collective-permute-start(bf16[1,80,2048]{2,1,0:T(8,128)(2,1)S(1)} %slice.123), channel_id=1, source_target_pairs={{0,32},{1,33},{2,34},{3,35},{4,36},{5,37},{6,38},{7,39},{8,40},{9,... | collective-permute-start | bytes 983048 | tf_op jit(solution)/shard_map/ppermute | solution.py:45
  307.1 26.4 %collective-permute-start.45 = (bf16[1,80,2048]{2,1,0:T(8,128)(2,1)S(1)}, bf16[1,80,2048]{2,1,0:T(8,128)(2,1)S(1)}, u32[]{:S(2)}, u32[]{:S(2)}) collective-permute-start(bf16[1,80,2048]{2,1,0:T(8,128)(2,1)S(1)} %slice.124), channel_id=1, source_target_pairs={{0,96},{1,97},{2,98},{3,99},{4,100},{5,101},{6,102},{7,103},{8,104... | collective-permute-start | bytes 983048 | tf_op jit(solution)/shard_map/ppermute | solution.py:45
  322.9 25.2 %collective-permute-start.37 = (bf16[2,128,1792]{2,1,0:T(8,128)(2,1)S(1)}, bf16[2,128,1792]{2,1,0:T(8,128)(2,1)}, u32[]{:S(2)}, u32[]{:S(2)}) collective-permute-start(bf16[2,128,1792]{2,1,0:T(8,128)(2,1)S(1)} %pad_maximum_fusion.refs_2_), channel_id=1, source_target_pairs={{0,8},{1,9},{2,10},{3,11},{4,12},{5,13},{6,14},{7,15},{8,0},{9,1},... | collective-permute-start | bytes 2752520 | tf_op jit(solution)/shard_map/ppermute | solution.py:45
  340.2 23.8 %collective-permute-start.46 = (bf16[8,80,2048]{2,1,0:T(8,128)(2,1)}, bf16[8,80,2048]{2,1,0:T(8,128)(2,1)}, u32[]{:S(2)}, u32[]{:S(2)}) collective-permute-start(bf16[8,80,2048]{2,1,0:T(8,128)(2,1)} %joined.5.refs_2_), channel_id=1, source_target_pairs={{0,8},{1,9},{2,10},{3,11},{4,12},{5,13},{6,14},{7,15},{8,0},{9,1},... | collective-permute-start | bytes 7864328 | tf_op jit(solution)/shard_map/ppermute | solution.py:45
  341.1 18.6 %collective-permute-start.34 = (bf16[1,128,1792]{2,1,0:T(8,128)(2,1)S(1)}, bf16[1,128,1792]{2,1,0:T(8,128)(2,1)}, u32[]{:S(2)}, u32[]{:S(2)}) collective-permute-start(bf16[1,128,1792]{2,1,0:T(8,128)(2,1)S(1)} %slice.121), channel_id=1, source_target_pairs={{0,32},{1,33},{2,34},{3,35},{4,36},{5,37},{6,38},{7,39},{8,40},{9,... | collective-permute-start | bytes 1376264 | tf_op jit(solution)/shard_map/ppermute | solution.py:45
  (53 other events, 529.7 us)

commit v7 on v6

--- a/solution.py
+++ b/solution.py
@@ -47,13 +47,6 @@
 
 def pick(value, index, axis):
     return lax.dynamic_index_in_dim(value, index, axis, keepdims=False)
-
-
-def normalize(value):
-    xf = value.astype(f32)
-    centre = xf - jnp.mean(xf, -1, keepdims=True)
-    inverse = lax.rsqrt(jnp.mean(centre * centre, -1, keepdims=True) + EPS)
-    return centre * inverse, inverse
 
 
 def kernel_params():
@@ -338,7 +331,7 @@
     )(place, lengths, qkv_weight, up_weight, tokens, cotangent, *vectors)
 
 
-def attend(h1, dy, weight, spots, out, bias, cosine, sine, lengths, numbers, after, rows=128):
+def attend(h1, dy, weight, spots, out, bias, cosine, sine, lengths, after, rows=128):
     total, width = h1.shape
     count = len(dy)
     head = out.shape[0]
@@ -346,15 +339,14 @@
 
     parts = len(weight)
 
-    def body(number_ref, len_ref, spot_ref, b_ref, *refs):
+    def body(len_ref, spot_ref, b_ref, *refs):
         w_refs, refs = refs[:parts], refs[parts:]
         dy_refs = refs[:count]
         h1_hbm, out_hbm, cos_hbm, sin_hbm = refs[count : count + 4]
-        ol_hbm, dq_hbm, keep_hbm, send_hbm, sum_ref = refs[count + 4 : count + 9]
-        (dy_v, h1_v, w_v, wo_v, cos_v, sin_v, qkv_v, do_v, ol_v, dq_v, keep_v, send_v, dy_sem, w_sem, sems) = (
-            refs[count + 9 :]
+        ol_hbm, dq_hbm, sum_ref = refs[count + 4 : count + 7]
+        (dy_v, h1_v, w_v, wo_v, cos_v, sin_v, qkv_v, do_v, ol_v, dq_v, dy_sem, w_sem, sems) = (
+            refs[count + 7 :]
         )
-        own = number_ref[0] == 0
         pairs = (
             (h1_hbm, h1_v),
             (out_hbm, wo_v),
@@ -381,7 +373,7 @@
         do_v[...] = dot(dy_v[...], wo_v[...], 1, 1).astype(bf16)
         sum_ref[...] = jnp.zeros_like(sum_ref)
 
-        @pl.loop(0, total // rows)
+        @pl.loop(0, total // rows, unroll=2)
         def _(block):
             at = pl.ds(pl.multiple_of(block * rows, rows), rows)
             cos, sin = cos_v[at, :], sin_v[at, :]
@@ -416,55 +408,20 @@
         dq_copy = pltpu.make_async_copy(dq_v, dq_hbm, sems.at[1])
         dq_copy.start()
 
-        def split(part, high, lanes):
-            for z_hi in range(2):
-                at = (pl.ds(4 * z_hi, 4), high, lanes)
-
-                @pl.when(own)
-                def _(z_hi=z_hi, at=at):
-                    keep_v[at] = part[:, z_hi, 0]
-                    send_v[at] = part[:, z_hi, 1]
-
-                @pl.when(jnp.logical_not(own))
-                def _(z_hi=z_hi, at=at):
-                    keep_v[at] = part[:, z_hi, 1]
-                    send_v[at] = part[:, z_hi, 0]
-
-        part = dot_rows(ol_v[...], dy_v[...]).astype(bf16).reshape(4, 2, 2, 16, width)
-        split(part, pl.ds(48, 16), slice(None))
-
-        @pl.loop(0, 8)
-        def _(n):
-            lanes = pl.ds(pl.multiple_of(n * 256, 256), 256)
-            part = dot_rows(h1_v[:, lanes], dq_v[...]).astype(bf16).reshape(4, 2, 2, 16, 3 * head)
-            for third in range(3):
-                split(
-                    part[..., third * head : (third + 1) * head],
-                    pl.ds(16 * third, 16),
-                    pl.ds(pl.multiple_of(n * head, head), head),
-                )
-
-        keep_copy = pltpu.make_async_copy(keep_v, keep_hbm, sems.at[2])
-        keep_copy.start()
-        send_copy = pltpu.make_async_copy(send_v, send_hbm, sems.at[3])
-        send_copy.start()
-        for copy in (ol_copy, dq_copy, keep_copy, send_copy):
+        for copy in (ol_copy, dq_copy):
             copy.wait()
 
-    grads = jax.ShapeDtypeStruct((8, 64, width), bf16)
     vmem = pl.BlockSpec(memory_space=pltpu.VMEM)
     smem = pl.BlockSpec(memory_space=pltpu.SMEM)
     return pl.pallas_call(
-        after_inputs(body, 8 + parts + count, len(after)),
+        after_inputs(body, 7 + parts + count, len(after)),
         out_shape=(
             jax.ShapeDtypeStruct((total, head), bf16),
             jax.ShapeDtypeStruct((total, 3 * head), bf16),
-            grads,
-            grads,
             jax.ShapeDtypeStruct((1, 3 * head), f32),
         ),
-        in_specs=[smem, smem, smem, vmem] + anywhere(parts + count + 4 + len(after)),
-        out_specs=tuple(anywhere(4)) + (vmem,),
+        in_specs=[smem, smem, vmem] + anywhere(parts + count + 4 + len(after)),
+        out_specs=tuple(anywhere(2)) + (vmem,),
         scratch_shapes=[
             pltpu.VMEM((total, width), bf16),
             pltpu.VMEM((total, width), bf16),
@@ -476,17 +433,14 @@
             pltpu.VMEM((total, head), bf16),
             pltpu.VMEM((total, head), bf16),
             pltpu.VMEM((total, 3 * head), bf16),
-            pltpu.VMEM((8, 64, width), bf16),
-            pltpu.VMEM((8, 64, width), bf16),
             pltpu.SemaphoreType.DMA((count,)),
             pltpu.SemaphoreType.DMA((parts,)),
             pltpu.SemaphoreType.DMA((4,)),
         ],
         compiler_params=kernel_params(),
-        cost_estimate=cost(22),
+        cost_estimate=cost(17),
         name="attend",
     )(
-        numbers,
         lengths,
         spots,
         bias,
@@ -500,6 +454,83 @@
     )
 
 
+def attention_grads(h1, dy, d_qkv, attended, numbers, after):
+    total, width = h1.shape
+    count = len(dy)
+    rows = total // count
+    head = attended.shape[1]
+
+    def body(number_ref, *refs):
+        dy_refs = refs[:count]
+        h1_hbm, dq_hbm, ol_hbm, keep_hbm, send_hbm = refs[count : count + 5]
+        dy_v, h1_v, dq_v, ol_v, keep_v, send_v, dy_sem, sems = refs[count + 5 :]
+        own = number_ref[0] == 0
+        pairs = ((h1_hbm, h1_v), (dq_hbm, dq_v), (ol_hbm, ol_v))
+        copies = loads(
+            [pltpu.make_async_copy(*pair, sems.at[n]) for n, pair in enumerate(pairs)]
+        )
+        dy_copies = loads(piece_copies(dy_refs, 1, dy_v, dy_sem, rows))
+        for copy in copies:
+            copy.wait()
+
+        def split(part, high, lanes):
+            for z_hi in range(2):
+                at = (pl.ds(4 * z_hi, 4), high, lanes)
+
+                @pl.when(own)
+                def _(z_hi=z_hi, at=at):
+                    keep_v[at] = part[:, z_hi, 0]
+                    send_v[at] = part[:, z_hi, 1]
+
+                @pl.when(jnp.logical_not(own))
+                def _(z_hi=z_hi, at=at):
+                    keep_v[at] = part[:, z_hi, 1]
+                    send_v[at] = part[:, z_hi, 0]
+
+        @pl.loop(0, 8)
+        def _(n):
+            lanes = pl.ds(pl.multiple_of(n * 256, 256), 256)
+            part = dot_rows(h1_v[:, lanes], dq_v[...]).astype(bf16).reshape(4, 2, 2, 16, 3 * head)
+            for third in range(3):
+                split(
+                    part[..., third * head : (third + 1) * head],
+                    pl.ds(16 * third, 16),
+                    pl.ds(pl.multiple_of(n * head, head), head),
+                )
+
+        for copy in dy_copies:
+            copy.wait()
+        part = dot_rows(ol_v[...], dy_v[...]).astype(bf16).reshape(4, 2, 2, 16, width)
+        split(part, pl.ds(48, 16), slice(None))
+        keep_copy = pltpu.make_async_copy(keep_v, keep_hbm, sems.at[0])
+        keep_copy.start()
+        send_copy = pltpu.make_async_copy(send_v, send_hbm, sems.at[1])
+        send_copy.start()
+        keep_copy.wait()
+        send_copy.wait()
+
+    grads = jax.ShapeDtypeStruct((8, 64, width), bf16)
+    return pl.pallas_call(
+        after_inputs(body, 4 + count, len(after)),
+        out_shape=(grads, grads),
+        in_specs=[pl.BlockSpec(memory_space=pltpu.SMEM)] + anywhere(count + 3 + len(after)),
+        out_specs=tuple(anywhere(2)),
+        scratch_shapes=[
+            pltpu.VMEM((total, width), bf16),
+            pltpu.VMEM((total, width), bf16),
+            pltpu.VMEM((total, 3 * head), bf16),
+            pltpu.VMEM((total, head), bf16),
+            pltpu.VMEM((8, 64, width), bf16),
+            pltpu.VMEM((8, 64, width), bf16),
+            pltpu.SemaphoreType.DMA((count,)),
+            pltpu.SemaphoreType.DMA((3,)),
+        ],
+        compiler_params=kernel_params(),
+        cost_estimate=cost(12),
+        name="attention_grads",
+    )(numbers, *dy, h1, d_qkv, attended, *after)
+
+
 def outer(d_qkv, d_hidden, weight, spots, x, mean, inverse, gains, active, attended, down, out, bias, after):
     total, n1 = d_qkv.shape
     n2 = d_hidden.shape[1]
@@ -516,20 +547,19 @@
             7 + count :
         ]
         plain_v = (dq_v, du_v, act_v, ol_v, wd_v, wo_v)
+        first = loads(
+            [
+                pltpu.make_async_copy(plain[n], plain_v[n], sems.at[n]) for n in range(2, 6)
+            ]
+        )
         copies = loads(
             [
-                pltpu.make_async_copy(source, target, sems.at[n])
-                for n, (source, target) in enumerate(zip(plain[:2], plain_v[:2]))
+                pltpu.make_async_copy(plain[n], plain_v[n], sems.at[n]) for n in range(2)
             ]
             + weight_copies(weight, w_refs, spot_ref, w_v, slice(None), w_sem)
             + piece_copies(x_refs, 0, x_v, x_sem, 128)
         )
-        later = loads(
-            [
-                pltpu.make_async_copy(plain[n], plain_v[n], sems.at[n]) for n in range(2, 6)
-            ]
-        )
-        for copy in copies:
+        for copy in first:
             copy.wait()
 
         def leaving(n, half):
@@ -542,6 +572,17 @@
                 )
                 for at in range(count)
             ]
+
+        @pl.loop(0, width // step)
+        def _(n):
+            lanes = pl.ds(pl.multiple_of(n * step, step), step)
+            mix = dot(act_v[...], wd_v[:, lanes]) + dot(ol_v[...], wo_v[:, lanes])
+            pair_v[0, :, lanes] = (mix + b_ref[:, lanes]).astype(bf16)
+            for copy in leaving(n, 0):
+                copy.start()
+
+        for copy in copies:
+            copy.wait()
 
         @pl.loop(0, width // step)
         def _(n):
@@ -557,17 +598,6 @@
             sums_ref[1:2, lanes] = jnp.sum(d1, 0, keepdims=True)
             sums_ref[2:3, lanes] = jnp.sum(d2 * normed, 0, keepdims=True)
             sums_ref[3:4, lanes] = jnp.sum(d2, 0, keepdims=True)
-
-        for copy in later:
-            copy.wait()
-
-        @pl.loop(0, width // step)
-        def _(n):
-            lanes = pl.ds(pl.multiple_of(n * step, step), step)
-            mix = dot(act_v[...], wd_v[:, lanes]) + dot(ol_v[...], wo_v[:, lanes])
-            pair_v[0, :, lanes] = (mix + b_ref[:, lanes]).astype(bf16)
-            for copy in leaving(n, 0):
-                copy.start()
 
         for n in range(width // step):
             for half in range(2):
@@ -644,7 +674,7 @@
 def packed_sums(stays, crossed, own, below, above, ff, head, after):
     width = own.shape[1]
 
-    def body(stay_ref, cross_ref, own_ref, below_ref, above_ref, out_ref, keep_ref):
+    def body(stay_ref, cross_ref, own_ref, below_ref, above_ref, out_ref, lanes_ref, keep_ref):
         inner = (stay_ref[0].astype(f32) + cross_ref[0].astype(f32)).astype(bf16)
         total = wide(own_ref, below_ref, above_ref).astype(bf16)
         for owner in range(8):
@@ -655,55 +685,23 @@
             row, col = 64 + 16 * (owner % 4), owner // 4 * ff
             pieces.append(inner[row : row + 16, col : col + ff])
             out_ref[owner] = jnp.concatenate(pieces, 1)
-        keep_ref[0:64] = inner[0:64]
-        keep_ref[64:80] = total[48:64]
+            lanes_ref[owner] = total[48:64, owner * head : (owner + 1) * head]
+        keep_ref[...] = inner[0:64]
 
     vmem = pl.BlockSpec(memory_space=pltpu.VMEM)
     return pl.pallas_call(
         after_inputs(body, 5, len(after)),
         out_shape=(
             jax.ShapeDtypeStruct((8, 16, 3 * head + ff), bf16),
-            jax.ShapeDtypeStruct((80, width), bf16),
+            jax.ShapeDtypeStruct((8, 16, width // 8), bf16),
+            jax.ShapeDtypeStruct((64, width), bf16),
         ),
         in_specs=[vmem] * 5 + anywhere(len(after)),
-        out_specs=(vmem,) * 2,
+        out_specs=(vmem,) * 3,
         compiler_params=kernel_params(),
         cost_estimate=cost(3),
         name="packed_sums",
     )(stays, crossed, own, below, above, *after)
-
-
-def halves(below, above, x_pair, dy_pair, after):
-    count, rows, cols = below.shape
-    _, tokens, width = x_pair.shape
-    half = (count // 2, rows, cols)
-
-    def body(below_ref, above_ref, x_ref, dy_ref, low_ref, high_ref, x_out, dy_out):
-        low_ref[...] = below_ref[...]
-        high_ref[...] = above_ref[...]
-        x_out[...] = x_ref[0]
-        dy_out[...] = dy_ref[0]
-
-    def at(block, first):
-        return pl.BlockSpec(block, lambda i: (first,) + (0,) * (len(block) - 1))
-
-    return pl.pallas_call(
-        after_inputs(body, 4, len(after)),
-        out_shape=(jax.ShapeDtypeStruct(half, bf16),) * 2
-        + (jax.ShapeDtypeStruct((tokens, width), bf16),) * 2,
-        grid=(1,),
-        in_specs=[
-            at(half, 0),
-            at(half, 1),
-            at((1, tokens, width), 0),
-            at((1, tokens, width), 1),
-        ]
-        + anywhere(len(after)),
-        out_specs=(at(half, 0), at(half, 0), at((tokens, width), 0), at((tokens, width), 0)),
-        compiler_params=kernel_params(),
-        cost_estimate=cost(3),
-        name="halves",
-    )(below, above, x_pair, dy_pair, *after)
 
 
 def joined(arrays, after):
@@ -736,95 +734,45 @@
     )(*arrays, *after)
 
 
-def blocks_call(name, body, numbers, terms, outs, after):
-    def came(block, index):
-        rest = (0,) * (len(block) - 1)
-        return pl.BlockSpec(block, lambda i, n: (index(n),) + rest)
-
-    return pl.pallas_call(
-        after_inputs(body, 1 + len(terms), len(after)),
-        out_shape=tuple(jax.ShapeDtypeStruct(out, bf16) for out in outs),
-        grid_spec=pltpu.PrefetchScalarGridSpec(
-            num_scalar_prefetch=1,
-            grid=(1,),
-            in_specs=[came(block, index) for _, block, index in terms] + anywhere(len(after)),
-            out_specs=tuple(
-                pl.BlockSpec(out, lambda i, n, size=len(out): (0,) * size) for out in outs
-            ),
+def halves(own, below, above, after):
+    count, rows, cols = own.shape
+    half = count // 2
+
+    def body(own_ref, below_ref, above_ref, low_ref, high_ref, all_ref):
+        step = pl.program_id(0)
+        all_ref[0] = own_ref[...]
+        all_ref[1] = above_ref[...]
+        all_ref[2] = below_ref[...]
+
+        @pl.when(step == 0)
+        def _():
+            low_ref[...] = below_ref[...]
+
+        @pl.when(step == 1)
+        def _():
+            high_ref[...] = above_ref[...]
+
+    block = pl.BlockSpec((half, rows, cols), lambda i: (i, 0, 0))
+    whole = pl.BlockSpec((half, rows, cols), lambda i: (0, 0, 0))
+    low, high, together = pl.pallas_call(
+        after_inputs(body, 3, len(after)),
+        out_shape=(jax.ShapeDtypeStruct((half, rows, cols), bf16),) * 2
+        + (jax.ShapeDtypeStruct((3, count, rows, cols), bf16),),
+        grid=(2,),
+        in_specs=[block] * 3 + anywhere(len(after)),
+        out_specs=(
+            whole,
+            whole,
+            pl.BlockSpec((3, half, rows, cols), lambda i: (0, i, 0, 0)),
         ),
         compiler_params=kernel_params(),
-        cost_estimate=cost(3),
-        name=name,
-    )(numbers, *[array for array, _, _ in terms], *after)
-
-
-def wide(*refs):
-    return functools.reduce(jnp.add, [ref[...].astype(f32) for ref in refs])
-
-
-def spread(pieces, places, core, targets, count, before, after):
-    rows, cols = pieces[0][0].shape[1:]
-    firsts, total = [], 0
-    for mine, _ in pieces:
-        firsts.append(total)
-        total += mine.shape[0]
-
-    def body(place_ref, core_ref, *refs):
-        step = pl.program_id(0)
-        outs = refs[2 * len(pieces) + len(before) :]
-        first_core = core_ref[0] == 0
-
-        def fill(ref, low):
-            for out_ref, (_, high, parts) in zip(outs, targets):
-                for to, row, col, size in parts:
-                    out_ref[low * high : (low + 1) * high, to : to + size] = ref[
-                        0, row : row + high, col : col + size
-                    ].astype(f32)
-
-        for n, (first, (mine, _)) in enumerate(zip(firsts, pieces)):
-            here = (step >= first) & (step < first + mine.shape[0])
-
-            @pl.when(here & first_core)
-            def _(n=n):
-                fill(refs[2 * n], 0)
-                fill(refs[2 * n + 1], 1)
-
-            @pl.when(here & jnp.logical_not(first_core))
-            def _(n=n):
-                fill(refs[2 * n], 1)
-                fill(refs[2 * n + 1], 0)
-
-    def chosen(first, size):
-        return pl.BlockSpec(
-            (1, rows, cols), lambda i, place, core: (jnp.clip(i - first, 0, size - 1), 0, 0)
-        )
-
-    specs, arrays = [], []
-    for first, (mine, yours) in zip(firsts, pieces):
-        specs += [chosen(first, mine.shape[0])] * 2
-        arrays += [mine, yours]
-    return pl.pallas_call(
-        after_inputs(body, 2 + 2 * len(pieces) + len(before), len(after)),
-        out_shape=tuple(
-            jax.ShapeDtypeStruct((2 * count * high, wide), f32) for wide, high, _ in targets
-        ),
-        grid_spec=pltpu.PrefetchScalarGridSpec(
-            num_scalar_prefetch=2,
-            grid=(total,),
-            in_specs=specs + anywhere(len(before) + len(after)),
-            out_specs=tuple(
-                pl.BlockSpec((2 * high, wide), lambda i, place, core: (place[i], 0))
-                for wide, high, _ in targets
-            ),
-        ),
-        input_output_aliases={2 + len(arrays) + n: n for n in range(len(before))},
-        compiler_params=kernel_params(),
-        cost_estimate=cost(1.2 * total),
-        name="spread",
-    )(places, core, *arrays, *before, *after)
-
-
-def small_sums(norm_sums, qkv_sums, up_sums, dy_sums, numbers):
+        cost_estimate=cost(4),
+        name="halves",
+    )(own, below, above, *after)
+    return low, high, together.reshape(3 * count, rows, cols)
+
+
+def small_sums(norm_sums, qkv_sums, up_sums, dy_sums, numbers, after):
     def body(number_ref, norm_ref, q_ref, u_ref, y_ref, out_ref, work):
         shard = number_ref[1]
         for owner in range(8):
@@ -852,15 +800,140 @@
 
     vmem = pl.BlockSpec(memory_space=pltpu.VMEM)
     return pl.pallas_call(
-        body,
+        after_inputs(body, 5, len(after)),
         out_shape=jax.ShapeDtypeStruct((8, 24, 128), bf16),
-        in_specs=[pl.BlockSpec(memory_space=pltpu.SMEM)] + [vmem] * 4,
+        in_specs=[pl.BlockSpec(memory_space=pltpu.SMEM)] + [vmem] * 4 + anywhere(len(after)),
         out_specs=vmem,
         scratch_shapes=[pltpu.VMEM((8, 24, 128), f32)],
         compiler_params=kernel_params(),
         cost_estimate=cost(3),
         name="small_sums",
-    )(numbers, norm_sums, qkv_sums, up_sums, dy_sums)
+    )(numbers, norm_sums, qkv_sums, up_sums, dy_sums, *after)
+
+
+def finished(own, below, above, other, tokens, cotangent, after):
+    rows, width = tokens.shape
+    step = rows // 2
+
+    def body(own_ref, below_ref, above_ref, other_ref, x_ref, dy_ref, mixed_ref, grad_ref):
+        total = wide(own_ref, below_ref, above_ref, other_ref)
+        x = x_ref[...].astype(f32)
+        mixed_ref[...] = (x + total[0]).astype(bf16)
+        centre = x - jnp.mean(x, 1, keepdims=True)
+        inverse = lax.rsqrt(jnp.mean(centre * centre, 1, keepdims=True) + EPS)
+        normed = centre * inverse
+        gain = total[1]
+        grad_ref[...] = dy_ref[...].astype(f32) + inverse * (
+            gain
+            - jnp.mean(gain, 1, keepdims=True)
+            - normed * jnp.mean(gain * normed, 1, keepdims=True)
+        )
+
+    def pair(first):
+        return pl.BlockSpec((2, step, width), lambda i: (first, i, 0))
+
+    block = pl.BlockSpec((step, width), lambda i: (i, 0))
+    return pl.pallas_call(
+        after_inputs(body, 6, len(after)),
+        out_shape=(
+            jax.ShapeDtypeStruct((rows, width), bf16),
+            jax.ShapeDtypeStruct((rows, width), f32),
+        ),
+        grid=(2,),
+        in_specs=[pair(0), pair(1), pair(0), pair(0), block, block] + anywhere(len(after)),
+        out_specs=(block, block),
+        compiler_params=kernel_params(),
+        cost_estimate=cost(3),
+        name="finished",
+    )(own, below, above, other, tokens, cotangent, *after)
+
+
+def blocks_call(name, body, numbers, terms, outs, after, time=3):
+    def came(block, index):
+        rest = (0,) * (len(block) - 1)
+        return pl.BlockSpec(block, lambda i, n: (index(n),) + rest)
+
+    return pl.pallas_call(
+        after_inputs(body, 1 + len(terms), len(after)),
+        out_shape=tuple(jax.ShapeDtypeStruct(out, bf16) for out in outs),
+        grid_spec=pltpu.PrefetchScalarGridSpec(
+            num_scalar_prefetch=1,
+            grid=(1,),
+            in_specs=[came(block, index) for _, block, index in terms] + anywhere(len(after)),
+            out_specs=tuple(
+                pl.BlockSpec(out, lambda i, n, size=len(out): (0,) * size) for out in outs
+            ),
+        ),
+        compiler_params=kernel_params(),
+        cost_estimate=cost(time),
+        name=name,
+    )(numbers, *[array for array, _, _ in terms], *after)
+
+
+def wide(*refs):
+    return functools.reduce(jnp.add, [ref[...].astype(f32) for ref in refs])
+
+
+def spread(pieces, places, core, targets, count, before, after):
+    rows, cols = pieces[0][0].shape[1:]
+    firsts, total = [], 0
+    for mine, _ in pieces:
+        firsts.append(total)
+        total += mine.shape[0]
+
+    def body(place_ref, core_ref, *refs):
+        step = pl.program_id(0)
+        outs = refs[2 * len(pieces) + len(before) :]
+        first_core = core_ref[0] == 0
+
+        def fill(ref, low):
+            for out_ref, (_, high, parts) in zip(outs, targets):
+                for to, row, col, size in parts:
+                    out_ref[low * high : (low + 1) * high, to : to + size] = ref[
+                        0, row : row + high, col : col + size
+                    ].astype(f32)
+
+        for n, (first, (mine, _)) in enumerate(zip(firsts, pieces)):
+            here = (step >= first) & (step < first + mine.shape[0])
+
+            @pl.when(here & first_core)
+            def _(n=n):
+                fill(refs[2 * n], 0)
+                fill(refs[2 * n + 1], 1)
+
+            @pl.when(here & jnp.logical_not(first_core))
+            def _(n=n):
+                fill(refs[2 * n], 1)
+                fill(refs[2 * n + 1], 0)
+
+    def chosen(first, size):
+        return pl.BlockSpec(
+            (1, rows, cols), lambda i, place, core: (jnp.clip(i - first, 0, size - 1), 0, 0)
+        )
+
+    specs, arrays = [], []
+    for first, (mine, yours) in zip(firsts, pieces):
+        specs += [chosen(first, mine.shape[0])] * 2
+        arrays += [mine, yours]
+    return pl.pallas_call(
+        after_inputs(body, 2 + 2 * len(pieces) + len(before), len(after)),
+        out_shape=tuple(
+            jax.ShapeDtypeStruct((2 * count * high, wide), f32) for wide, high, _ in targets
+        ),
+        grid_spec=pltpu.PrefetchScalarGridSpec(
+            num_scalar_prefetch=2,
+            grid=(total,),
+            in_specs=specs + anywhere(len(before) + len(after)),
+            out_specs=tuple(
+                pl.BlockSpec((2 * high, wide), lambda i, place, core: (place[i], 0))
+                for wide, high, _ in targets
+            ),
+        ),
+        input_output_aliases={2 + len(arrays) + n: n for n in range(len(before))},
+        compiler_params=kernel_params(),
+        cost_estimate=cost(0.3 * total),
+        name="spread",
+    )(places, core, *arrays, *before, *after)
 
 
 def local(
@@ -902,12 +975,12 @@
     part = lax.all_to_all(part, "shard", 0, 0)
     own, infos = unpacked(part, (pairs[1], pairs[3], pairs[4]))
     below, above = move(own, y=1), move(own, y=-1)
-    low, high, x_half, dy_half = halves(below, above, other_below, other_above, (far,))
+    x_other_far, dy_other_far = move(other_below[0], x=1), move(other_above[1], x=-1)
+    low, high, yours = halves(own, below, above, (far, other_above, other_below))
     far_low, far_high = move(low, y=1), move(high, y=-1)
-    x_other_far, dy_other_far = move(x_half, x=1), move(dy_half, x=-1)
     x_all = tuple(x_other_far if p is None else p for p in pairs)
     dy_all = tuple(dy_other_far if p is None else p for p in pairs)
-    yours = move(joined((own, above, below), (low,)), c=1)
+    yours = move(yours, c=1)
     far_low_c, far_high_c = move(far_low, c=1), move(far_high, c=1)
     weight = (
         (own, 0, 8, 0, 0),
@@ -969,8 +1042,8 @@
         (cosine, sine),
     )
     got = move(send, c=1)
-    attended, d_qkv, a_keep, a_send, qkv_sums = attend(
-        h1, dy_all, weight, spots, out_weight, qkv_b, cosine, sine, lengths, numbers, (send,)
+    attended, d_qkv, qkv_sums = attend(
+        h1, dy_all, weight, spots, out_weight, qkv_b, cosine, sine, lengths, (send,)
     )
 
     pair_shape, one = (2, 128, width), (1, 128, width)
@@ -992,7 +1065,41 @@
         (attended,),
     )
     from_low, from_high = move(low, y=1), move(high, y=-1)
+    a_keep, a_send = attention_grads(h1, dy_all, d_qkv, attended, numbers, (low, high))
     a_got = move(a_send, c=1)
+    def near_body(n_ref, k1_ref, g1_ref, k3_ref, g3_ref, low_ref, high_ref, above_ref, below_ref):
+        above, below = wide(k1_ref, g1_ref), wide(k3_ref, g3_ref)
+        above_ref[0] = (above[0] + low_ref[0].astype(f32)).astype(bf16)
+        above_ref[1] = above[1].astype(bf16)
+        below_ref[0] = below[0].astype(bf16)
+        below_ref[1] = (below[1] + high_ref[0].astype(f32)).astype(bf16)
+
+    above, below = blocks_call(
+        "near_sums",
+        near_body,
+        numbers,
+        [(v, pair_shape, turn(k)) for k in (1, 3) for v in (keep, got)]
+        + [(v, one, lambda n: 0) for v in (from_low, from_high)],
+        (pair_shape, pair_shape),
+        (a_send,),
+        20,
+    )
+    from_below, from_above = move(above, y=1), move(below, y=-1)
+
+    four, part_shape = (4, 64, width), (1, 64, width)
+
+    def away_body(n_ref, keep_ref, got_ref, out_ref):
+        out_ref[...] = wide(keep_ref, got_ref).astype(bf16)
+
+    (a_away,) = blocks_call(
+        "away_sums",
+        away_body,
+        numbers,
+        [(v, four, lambda n: 1 - n[3]) for v in (a_keep, a_got)],
+        (four,),
+        (above,),
+    )
+    a_crossed = move(a_away, h=1)
     norm_sums, *pairs_out = outer(
         d_qkv,
         d_hidden,
@@ -1007,48 +1114,69 @@
         down_weight,
         out_weight,
         wide_bias,
-        (low, high),
-    )
-
-    def near_body(n_ref, k1_ref, g1_ref, k3_ref, g3_ref, low_ref, high_ref, above_ref, below_ref):
-        above, below = wide(k1_ref, g1_ref), wide(k3_ref, g3_ref)
-        above_ref[0] = (above[0] + low_ref[0].astype(f32)).astype(bf16)
-        above_ref[1] = above[1].astype(bf16)
-        below_ref[0] = below[0].astype(bf16)
-        below_ref[1] = (below[1] + high_ref[0].astype(f32)).astype(bf16)
-
-    above, below = blocks_call(
-        "near_sums",
-        near_body,
+        (a_away, above, below),
+    )
+
+    smalls = small_sums(norm_sums, qkv_sums, up_sums, dy_sums, numbers, ())
+    smalls = jnp.sum(lax.all_to_all(smalls, "shard", 0, 0).astype(f32), 0)
+    smalls = jnp.pad(smalls.astype(bf16).reshape(-1), (0, 16 * width - 3072)).reshape(16, width)
+
+    def ends_body(n_ref, keep_ref, got_ref, below_ref, above_ref, leave_ref, stay_ref):
+        total = wide(keep_ref, got_ref, below_ref, above_ref).astype(bf16)
+        first = n_ref[3] == 0
+        leave_ref[0] = jnp.where(first, total[1], total[0])
+        stay_ref[0] = jnp.where(first, total[0], total[1])
+
+    leaves, stays = blocks_call(
+        "end_sums",
+        ends_body,
         numbers,
-        [(v, pair_shape, turn(k)) for k in (1, 3) for v in (keep, got)]
-        + [(v, one, lambda n: 0) for v in (from_low, from_high)],
-        (pair_shape, pair_shape),
-        (pairs_out[0],),
-    )
-    from_below, from_above = move(above, y=1), move(below, y=-1)
-
-    four, part_shape = (4, 64, width), (1, 64, width)
-
-    def away_body(n_ref, keep_ref, got_ref, out_ref):
-        out_ref[...] = wide(keep_ref, got_ref).astype(bf16)
-
-    (a_away,) = blocks_call(
-        "away_sums",
-        away_body,
+        [(v, pair_shape, turn(0)) for v in (keep, got)]
+        + [(v, pair_shape, lambda n: 0) for v in (from_below, from_above)],
+        (one, one),
+        (norm_sums,),
+    )
+    crossed = move(leaves, h=1)
+
+    passed_below, passed_above = move(pairs_out[6], x=1), move(pairs_out[2], x=-1)
+
+    def around_body(n_ref, keep_ref, got_ref, crossed_ref, low_ref, high_ref, above_ref, own_ref, below_ref):
+        def part(k):
+            at = (n_ref[2] + k) % 4
+            return wide(keep_ref.at[at], got_ref.at[at], crossed_ref.at[at]).astype(bf16)
+
+        far = part(2)
+        low_ref[...] = far[:32]
+        high_ref[...] = far[32:]
+        above_ref[...] = part(1)
+        own_ref[...] = part(0)
+        below_ref[...] = part(3)
+
+    a_low, a_high, a_above, a_own, a_below = blocks_call(
+        "around_sums",
+        around_body,
         numbers,
-        [(v, four, lambda n: 1 - n[3]) for v in (a_keep, a_got)],
-        (four,),
-        (above,),
-    )
-    a_crossed = move(a_away, h=1)
-
-    smalls = small_sums(norm_sums, qkv_sums, up_sums, dy_sums, numbers)
-    smalls = jnp.broadcast_to(smalls[None], (16, 8, 24, 128)).reshape(128, 24, 128)
-    smalls = lax.all_to_all(smalls, BOTH, 0, 0)
-    smalls = jnp.sum(smalls.astype(f32), 0)
-
-    passed_below, passed_above = move(pairs_out[6], x=1), move(pairs_out[2], x=-1)
+        [(v, four, lambda n: n[3]) for v in (a_keep, a_got)] + [(a_crossed, four, lambda n: 0)],
+        ((32, width), (32, width), (64, width), (64, width), (64, width)),
+        (leaves,),
+    )
+    a_low, a_high = move(a_low, y=1), move(a_high, y=-1)
+
+    def beside_body(n_ref, above_ref, below_ref, low_ref, high_ref, up_ref, down_ref):
+        up_ref[0:32] = (above_ref[0:32].astype(f32) + low_ref[...].astype(f32)).astype(bf16)
+        up_ref[32:64] = above_ref[32:64]
+        down_ref[0:32] = below_ref[0:32]
+        down_ref[32:64] = (below_ref[32:64].astype(f32) + high_ref[...].astype(f32)).astype(bf16)
+
+    a_above, a_below = blocks_call(
+        "beside_sums",
+        beside_body,
+        numbers,
+        [(v, v.shape, lambda n: 0) for v in (a_above, a_below, a_low, a_high)],
+        ((64, width), (64, width)),
+        (crossed, smalls),
+    )
+    a_from_below, a_from_above = move(a_above, y=1), move(a_below, y=-1)
 
     def passed_body(n_ref, up_ref, from_below, here_ref, down_ref, from_above, there_ref, up_out, down_out):
         up_out[0:2] = wide(up_ref, from_below).astype(bf16)
@@ -1072,100 +1200,54 @@
             )
         ],
         ((4, 128, width),) * 2,
-        (a_away,),
+        (a_low,),
     )
     from_device_below, from_device_above = move(ups, x=1), move(downs, x=-1)
 
-    def ends_body(n_ref, keep_ref, got_ref, below_ref, above_ref, leave_ref, stay_ref):
-        total = wide(keep_ref, got_ref, below_ref, above_ref).astype(bf16)
-        first = n_ref[3] == 0
-        leave_ref[0] = jnp.where(first, total[1], total[0])
-        stay_ref[0] = jnp.where(first, total[0], total[1])
-
-    leaves, stays = blocks_call(
-        "end_sums",
-        ends_body,
+    part, outs, downs_sum = packed_sums(
+        stays, crossed, a_own, a_from_below, a_from_above, ff, head, (ups,)
+    )
+    received = lax.all_to_all(part, "shard", 0, 0)
+    part = jnp.concatenate([received, outs], 2).reshape(1, 128, width)
+    def other_body(n_ref, own_ref, below_ref, above_ref, out_ref):
+        out_ref[...] = wide(own_ref, below_ref, above_ref).astype(bf16)
+
+    (total_other,) = blocks_call(
+        "other_sums",
+        other_body,
         numbers,
-        [(v, pair_shape, turn(0)) for v in (keep, got)]
-        + [(v, pair_shape, lambda n: 0) for v in (from_below, from_above)],
-        (one, one),
-        (a_away,),
-    )
-    crossed = move(leaves, h=1)
-
-    def around_body(n_ref, keep_ref, got_ref, crossed_ref, low_ref, high_ref, above_ref, own_ref, below_ref):
-        def part(k):
-            at = (n_ref[2] + k) % 4
-            return wide(keep_ref.at[at], got_ref.at[at], crossed_ref.at[at]).astype(bf16)
-
-        far = part(2)
-        low_ref[...] = far[:32]
-        high_ref[...] = far[32:]
-        above_ref[...] = part(1)
-        own_ref[...] = part(0)
-        below_ref[...] = part(3)
-
-    a_low, a_high, a_above, a_own, a_below = blocks_call(
-        "around_sums",
-        around_body,
-        numbers,
-        [(v, four, lambda n: n[3]) for v in (a_keep, a_got)] + [(a_crossed, four, lambda n: 0)],
-        ((32, width), (32, width), (64, width), (64, width), (64, width)),
-        (leaves,),
-    )
-    a_low, a_high = move(a_low, y=1), move(a_high, y=-1)
-
-    def beside_body(n_ref, above_ref, below_ref, low_ref, high_ref, up_ref, down_ref):
-        up_ref[0:32] = (above_ref[0:32].astype(f32) + low_ref[...].astype(f32)).astype(bf16)
-        up_ref[32:64] = above_ref[32:64]
-        down_ref[0:32] = below_ref[0:32]
-        down_ref[32:64] = (below_ref[32:64].astype(f32) + high_ref[...].astype(f32)).astype(bf16)
-
-    a_above, a_below = blocks_call(
-        "beside_sums",
-        beside_body,
-        numbers,
-        [(v, v.shape, lambda n: 0) for v in (a_above, a_below, a_low, a_high)],
-        ((64, width), (64, width)),
-        (crossed,),
-    )
-    a_from_below, a_from_above = move(a_above, y=1), move(a_below, y=-1)
-
-    part, stays = packed_sums(
-        stays,
-        crossed,
-        a_own,
-        a_from_below,
-        a_from_above,
-        ff,
-        head,
-        (smalls,),
-    )
-    part = lax.all_to_all(part, "shard", 0, 0).reshape(1, 128, cols)
-
-    total = pairs_out[4].astype(f32) + from_device_below[:2].astype(f32)
-    total = (total + from_device_above[2:].astype(f32)).astype(bf16)
-    totals = pairs_out[0].astype(f32) + from_device_below[2:].astype(f32)
-    totals = totals + from_device_above[:2].astype(f32) + move(total, l=1).astype(f32)
-    mixed = (tokens.astype(f32) + totals[0]).astype(bf16)
-    own_sum = totals[1]
-    own_normed, own_inverse = normalize(tokens)
-    tokens_grad = cotangent.astype(f32) + own_inverse * (
-        own_sum
-        - jnp.mean(own_sum, -1, keepdims=True)
-        - own_normed * jnp.mean(own_sum * own_normed, -1, keepdims=True)
-    )
+        [
+            (pairs_out[4], pair_shape, lambda n: 0),
+            (from_device_below, pair_shape, lambda n: 0),
+            (from_device_above, pair_shape, lambda n: 1),
+        ],
+        (pair_shape,),
+        (),
+    )
+    total_other, sent_other = move(total_other, l=1), total_other
 
     order = ((0, h), (0, 1 - h), (1, h), (1, 1 - h), (3, h), (3, 1 - h), (2, h), (2, 1 - h))
     places = jnp.stack([(y + k) % 4 * 2 + high for k, high in order]).astype(jnp.int32)
 
-    def rep_gather(own):
+    def rep_gather(own, after):
         own = jnp.concatenate([own, move(own, h=1)])
         below, above = move(own, y=1), move(own, y=-1)
-        return (own, above, below), (move(below[:1], y=1), move(above[1:], y=-1))
-
-    near, far = rep_gather(part)
-    near = [(v, move(v, c=1)) for v in near]
+        low, high, near = halves(own, below, above, after)
+        return near, (move(low, y=1), move(high, y=-1))
+
+    near, far = rep_gather(jnp.concatenate([downs_sum, smalls])[None], ())
+    downs_all = joined((near, *far), ())
+    downs_yours = move(downs_all, c=1)
+    (down_grad,) = spread(
+        [(downs_all, downs_yours)],
+        places,
+        numbers[:1],
+        [(width, 64, [(0, 0, 0, width)])],
+        8,
+        (),
+        (),
+    )
+    near, far = rep_gather(part, (sent_other, downs_all))
     targets = [
         (
             3 * width,
@@ -1177,32 +1259,26 @@
             ],
         ),
         (8 * ff, 16, [(source * ff, 16 * source, 3 * head, ff) for source in range(8)]),
+        (width, 16, [(source * head, 16 * source, cols, head) for source in range(8)]),
     ]
-    grads = spread(near, places[:6], numbers[:1], targets, 8, (), ())
+    grads = spread([(near, move(near, c=1))], places[:6], numbers[:1], targets, 8, (), (down_grad,))
     far = joined(far, (grads[0],))
-
-    near_stays, far_stays = rep_gather(stays[None])
-    stays = joined(near_stays + far_stays, ())
-    down_grad, out_grad = spread(
-        [(stays, move(stays, c=1))],
-        places,
-        numbers[:1],
-        [(width, 64, [(0, 0, 0, width)]), (width, 16, [(0, 64, 0, width)])],
-        8,
-        (),
-        (),
-    )
-    qkv_grad, up_grad = spread(
+    mixed, tokens_grad = finished(
+        pairs_out[0], from_device_below, from_device_above, total_other, tokens, cotangent, (far,)
+    )
+    qkv_grad, up_grad, out_grad = spread(
         [(far, move(far, c=1))],
         places[6:],
         numbers[:1],
         targets,
         8,
         grads,
-        (tokens_grad, mixed, down_grad),
-    )
-    norm_grads = smalls[:8].reshape(4, 256)
-    dy_total = smalls[22:].reshape(256)
+        (tokens_grad,),
+    )
+    smalls = jnp.concatenate([downs_all[:, 64:66], downs_yours[:, 64:66]]).astype(f32)
+    smalls = jnp.sum(smalls, 0).reshape(-1)
+    norm_grads = smalls[:1024].reshape(4, 256)
+    dy_total = smalls[2816:3072]
     return (
         mixed,
         tokens_grad,
@@ -1211,11 +1287,11 @@
         norm_grads[2],
         norm_grads[3],
         qkv_grad,
-        smalls[8:14].reshape(768),
+        smalls[1024:1792],
         out_grad,
         dy_total,
         up_grad,
-        smalls[14:22].reshape(ff),
+        smalls[1792:2816],
         down_grad,
         dy_total,
     )

time: 386 us -> 429 us (1.11)
  waiting for transfers between devices: 85.8 us -> 123 us
  starting transfers between devices: 91 us -> 74.8 us
  Pallas kernels: 158 us -> 172 us
  blocking collectives: 0 us -> 8.87 us
  other arithmetic: 16.5 us -> 8.58 us
  local copies, waits for them, and re-layouts: 25.4 us -> 33.1 us
    all_to_all x2 -> x1, waiting for transfers between devices: 2.22 us -> 37.9 us  [local(): received = lax.all_to_all(part, 'shard', 0, 0)]
    pallas_call x3 -> x7, Pallas kernels: 30.1 us -> 46 us  [the longest x1 17.1 us: attend(): pl.pallas_call(after_inputs(body, 7 + parts + count, len(after)), out_sha...]
    ppermute x47 -> x45, starting transfers between devices: 78.2 us -> 67.7 us  [move(): return lax.ppermute(value, BOTH, pairs)]
    all_to_all x0 -> x1, blocking collectives: none -> 8.87 us  [local(): smalls = jnp.sum(lax.all_to_all(smalls, 'shard', 0, 0).astype(f32), 0)]
    unnamed x75 -> x92, local copies, waits for them, and re-layouts: 14.4 us -> 22.2 us
    all_to_all x2 -> x1, starting transfers between devices: 9.31 us -> 3.47 us  [local(): received = lax.all_to_all(part, 'shard', 0, 0)]
    pallas_call x3 -> x2, Pallas kernels: 11.9 us -> 7.95 us  [joined(): pl.pallas_call(after_inputs(body, count, len(after)), out_shape=jax.Shape...]
    pallas_call x7 -> x8, Pallas kernels: 28.1 us -> 31.9 us  [blocks_call(): pl.pallas_call(after_inputs(body, 1 + len(terms), len(after)), out_shape=...]
  transfers between devices with their start and end apart: 50 -> 47, of which waited for: 14 -> 11; matrix products, arithmetic and copies ran while one was open for 7% -> 5% of each run, Pallas kernels for 30% -> 28%
where the time goes in v7:
time: 429 us; the launch traced here: 422 us
  Pallas kernels  172 us (40%)
  waiting for transfers between devices  123 us (29%)
  starting transfers between devices  74.8 us (17%)
  local copies, waits for them, and re-layouts  33.1 us (8%)
  blocking collectives  8.87 us (2%)
  other arithmetic  8.58 us (2%)
    ppermute x45, waiting for transfers between devices, move(): return lax.ppermute(value, BOTH, pairs)  76.3 us
    ppermute x45, starting transfers between devices, move(): return lax.ppermute(value, BOTH, pairs)  67.7 us
    all_to_all x1, waiting for transfers between devices, local(): received = lax.all_to_all(part, 'shard', 0, 0)  37.9 us
    pallas_call x1, Pallas kernels, feed_forward(): pl.pallas_call(after_inputs(body, 5 + parts + 2 * count, len(after)), out...  32.2 us
    pallas_call x8, Pallas kernels, blocks_call(): pl.pallas_call(after_inputs(body, 1 + len(terms), len(after)), out_shape=...  31.9 us
    pallas_call x1, Pallas kernels, outer(): pl.pallas_call(after_inputs(body, 11 + parts + count, len(after)), out_sh...  24.3 us
    unnamed x92, local copies, waits for them, and re-layouts  22.2 us
    pallas_call x3, Pallas kernels, spread(): pl.pallas_call(after_inputs(body, 2 + 2 * len(pieces) + len(before), len(...  21.1 us
  transfers between devices with their start and end apart: 47, of which 11 were waited for; matrix products, arithmetic and copies ran while one was open for 5% of the time, Pallas kernels for 28%

profile of v7, /device:TPU:1, one launch (start us, length us, event | category | flops | bytes accessed | tf_op | source)
XLA Modules:
  0.0 422.3 jit_solution(1689917728013948906)
XLA Ops:
  0.7 3.6 packed.1
  9.4 3.6 all-to-all-start
  13.0 17.3 %collective-permute-done.1.refs_2_.refs_17_.refs_25_.refs_16_.refs_4_.refs_18_ = bf16[2,128,2048]{2,1,0:T(8,128)(2,1)} collective-permute-done((bf16[2,128,2048]{2,1,0:T(8,128)(2,1)}, bf16[2,128,2048]{2,1,0:T(8,128)(2,1)}, u32[]{:S(2)}, u32[]{:S(2)}) %collective-permute-start.1) | collective-permute-done | bytes 1048608 | tf_op jit(solution)/shard_map/ppermute | solution.py:45
  35.0 9.2 %all-to-all-done.refs_0_ = bf16[8,40,1792]{2,1,0:T(8,128)(2,1)S(1)} async-done(((bf16[8,40,1792]{2,1,0:T(8,128)(2,1)}), bf16[8,40,1792]{2,1,0:T(8,128)(2,1)S(1)}, u32[]{:S(2)}, u32[]{:S(2)}) %all-to-all-start) | async-done | bytes 1146912 | tf_op jit(solution)/shard_map/all_to_all | solution.py:975
  51.6 16.1 %collective-permute-done.3.refs_2_.refs_5_.refs_4_.refs_6_ = bf16[8,32,1792]{2,1,0:T(8,128)(2,1)S(1)} collective-permute-done((bf16[8,32,1792]{2,1,0:T(8,128)(2,1)}, bf16[8,32,1792]{2,1,0:T(8,128)(2,1)S(1)}, u32[]{:S(2)}, u32[]{:S(2)}) %collective-permute-start.3) | collective-permute-done | bytes 917536 | tf_op jit(solution)/shard_map/ppermute | solution.py:45
  76.0 3.9 collective-permute-start.10
  91.5 5.2 %collective-permute-done.8.refs_6_.refs_5_.refs_7_ = bf16[4,32,1792]{2,1,0:T(8,128)(2,1)S(1)} collective-permute-done((bf16[4,32,1792]{2,1,0:T(8,128)(2,1)}, bf16[4,32,1792]{2,1,0:T(8,128)(2,1)S(1)}, u32[]{:S(2)}, u32[]{:S(2)}) %collective-permute-start.8) | collective-permute-done | bytes 458784 | tf_op jit(solution)/shard_map/ppermute | solution.py:45
  103.9 32.2 %feed_forward.1 = (bf16[1024,2048]{1,0:T(8,128)(2,1)}, bf16[1024,1024]{1,0:T(8,128)(2,1)}, bf16[1024,1024]{1,0:T(8,128)(2,1)}, bf16[8,128,2048]{2,1,0:T(8,128)(2...) custom-call(s32[4]{0:T(128)} %get-tuple-element.150.refs_0_, ...), custom_call_target="tpu_custom_call" | custom-call | flops 36800000000 | bytes 1000 | tf_op jit(solution)/shard_map/feed_forward/pallas_call | solution.py:243
  140.3 17.1 %attend.1 = (bf16[1024,256]{1,0:T(8,128)(2,1)}, bf16[1024,768]{1,0:T(8,128)(2,1)}, f32[1,768]{1,0:T(1,128)}) custom-call(s32[8,3]{1,0:T(8,128)} %copy-done.9, s32[8]{0:T(128)} %pad_add_fusion.refs_1_.refs_0_, f32[3,1,256]{2,1,0:T(1,128)} %pad_maximum_fusion.4.refs_2_, bf16[8,32,1792]{2,1,0:T(8,128)(2,1)} %get-tuple-element.79.refs_0_.refs_4_.refs_3_.refs_5_, ...), custom_call_target="tpu_custom_call" | custom-call | flops 19549999104 | bytes 1000 | tf_op jit(solution)/shard_map/attend/pallas_call | solution.py:416
  157.4 3.3 far_sums.1
  163.4 13.7 %attention_grads.1 = (bf16[8,64,2048]{2,1,0:T(8,128)(2,1)}, bf16[8,64,2048]{2,1,0:T(8,128)(2,1)}) custom-call(s32[4]{0:T(128)} %get-tuple-element.150.refs_0_, bf16[2,128,2048]{2,1,0:T(8,128)(2,1)} %get-tuple-element.77.refs_14_.refs_22_.refs_13_.refs_1_.refs_15_, ...), custom_call_target="tpu_custom_call" | custom-call | flops 13799999488 | bytes 1000 | tf_op jit(solution)/shard_map/attention_grads/pallas_call | solution.py:513
  179.6 4.8 %near_sums.1 = (bf16[2,128,2048]{2,1,0:T(8,128)(2,1)}, bf16[2,128,2048]{2,1,0:T(8,128)(2,1)}) custom-call(s32[4]{0:T(128)} %get-tuple-element.150.refs_0_, bf16[8,128,2048]{2,1,0:T(8,128)(2,1)} %get-tuple-element.91.refs_1_.refs_3_, bf16[8,128,2048]{2,1,0:T(8,128)(2,1)} %collective-permute-done.15.refs_2_.refs_4_, ...), custom_call_target="tpu_custom_call" | custom-call | flops 23000000512 | bytes 1000 | tf_op jit(solution)/shard_map/near_sums/pallas_call | solution.py:856
  188.4 3.4 away_sums.1.refs_29_
  195.2 24.3 %outer.1 = (f32[4,2048]{1,0:T(4,128)}, bf16[2,128,2048]{2,1,0:T(8,128)(2,1)}, bf16[2,128,2048]{2,1,0:T(8,128)(2,1)}, bf16[2,128,2048]{2,1,0:T(8,128)(2,1)}, bf16...) custom-call(s32[8]{0:T(128)} %pad_add_fusion.refs_1_.refs_0_, ...), custom_call_target="tpu_custom_call" | custom-call | flops 23000000512 | bytes 1000 | tf_op jit(solution)/shard_map/outer/pallas_call | solution.py:608
  223.7 4.4 %end_sums.1 = (bf16[1,128,2048]{2,1,0:T(8,128)(2,1)}, bf16[1,128,2048]{2,1,0:T(8,128)(2,1)}) custom-call(s32[4]{0:T(128)} %get-tuple-element.150.refs_0_, bf16[8,128,2048]{2,1,0:T(8,128)(2,1)} %get-tuple-element.91.refs_1_.refs_3_, bf16[8,128,2048]{2,1,0:T(8,128)(2,1)} %collective-permute-done.15.refs_2_.refs_4_, bf16[2,128,2048]{2,1,0:T(8,128)(2,1)} %copy-done.20, ...), custom_call_target="tpu_custom_call" | custom-call | flops 3449999872 | bytes 1000 | tf_op jit(solution)/shard_map/end_sums/pallas_call | solution.py:856
  229.0 3.8 around_sums.1
  237.0 8.9 %all_to_all.15 = bf16[8,24,128]{2,1,0:T(8,128)(2,1)S(1)} all-to-all(bf16[8,24,128]{2,1,0:T(8,128)(2,1)} %small_sums.1), channel_id=1, replica_groups=mesh['rep'=16,'shard'=8] {'shard'}, dimensions={0} | all-to-all | bytes 98304 | tf_op jit(solution)/shard_map/all_to_all | solution.py:1121
  254.0 5.7 %passed_sums.1 = (bf16[4,128,2048]{2,1,0:T(8,128)(2,1)}, bf16[4,128,2048]{2,1,0:T(8,128)(2,1)}) custom-call(s32[4]{0:T(128)} %get-tuple-element.150.refs_0_, bf16[2,128,2048]{2,1,0:T(8,128)(2,1)} %get-tuple-element.99.refs_1_, bf16[2,128,2048]{2,1,0:T(8,128)(2,1)} %copy-done.17, bf16[2,128,2048]{2,1,0:T(8,128)(2,1)} %get-tuple-element.101.refs_3_, ...), custom_call_target="tpu_custom_call" | custom-call | flops 3449999872 | bytes 1000 | tf_op jit(solution)/shard_map/passed_sums/pallas_call | solution.py:856
  269.3 3.5 all-to-all-start.2
  275.8 37.9 %all-to-all-done.2 = bf16[8,16,1792]{2,1,0:T(8,128)(2,1)S(1)} async-done(((bf16[8,16,1792]{2,1,0:T(8,128)(2,1)}), bf16[8,16,1792]{2,1,0:T(8,128)(2,1)S(1)}, u32[]{:S(2)}, u32[]{:S(2)}) %all-to-all-start.2) | async-done | bytes 458784 | tf_op jit(solution)/shard_map/all_to_all | solution.py:1210
  313.8 3.9 collective-permute-start.32
  322.2 4.9 %collective-permute-done.32 = bf16[1,128,2048]{2,1,0:T(8,128)(2,1)S(1)} collective-permute-done((bf16[1,128,2048]{2,1,0:T(8,128)(2,1)S(1)}, bf16[1,128,2048]{2,1,0:T(8,128)(2,1)S(1)}, u32[]{:S(2)}, u32[]{:S(2)}) %collective-permute-start.32) | collective-permute-done | bytes 524320 | tf_op jit(solution)/shard_map/ppermute | solution.py:45
  330.0 24.1 %collective-permute-done.39.refs_2_ = bf16[1,80,2048]{2,1,0:T(8,128)(2,1)S(1)} collective-permute-done((bf16[1,80,2048]{2,1,0:T(8,128)(2,1)}, bf16[1,80,2048]{2,1,0:T(8,128)(2,1)S(1)}, u32[]{:S(2)}, u32[]{:S(2)}) %collective-permute-start.39) | collective-permute-done | bytes 327712 | tf_op jit(solution)/shard_map/ppermute | solution.py:45
  354.9 5.7 %joined.2.refs_4_.refs_2_ = bf16[8,80,2048]{2,1,0:T(8,128)(2,1)} custom-call(bf16[6,80,2048]{2,1,0:T(8,128)(2,1)} %bitcast.62, bf16[1,80,2048]{2,1,0:T(8,128)(2,1)} %copy-done.37, bf16[1,80,2048]{2,1,0:T(8,128)(2,1)} %copy-done.38), custom_call_target="tpu_custom_call" | custom-call | flops 3449999872 | bytes 1000 | tf_op jit(solution)/shard_map/joined/pallas_call | solution.py:725
  360.7 3.9 other_sums.1.refs_3_
  366.5 3.6 halves.5
  370.0 6.3 %collective-permute-start.42 = (bf16[6,128,2048]{2,1,0:T(8,128)(2,1)}, bf16[6,128,2048]{2,1,0:T(8,128)(2,1)S(1)}, u32[]{:S(2)}, u32[]{:S(2)}) collective-permute-start(bf16[6,128,2048]{2,1,0:T(8,128)(2,1)} %bitcast.43), channel_id=1, source_target_pairs={{0,8},{1,9},{2,10},{3,11},{4,12},{5,13},{6,14},{7,15},{8,0},{9,1},... | collective-permute-start | bytes 9437192 | tf_op jit(solution)/shard_map/ppermute | solution.py:45
  381.2 4.3 %collective-permute-done.43.refs_3_ = bf16[8,80,2048]{2,1,0:T(8,128)(2,1)} collective-permute-done((bf16[8,80,2048]{2,1,0:T(8,128)(2,1)}, bf16[8,80,2048]{2,1,0:T(8,128)(2,1)}, u32[]{:S(2)}, u32[]{:S(2)}) %collective-permute-start.43) | collective-permute-done | bytes 2621472 | tf_op jit(solution)/shard_map/ppermute | solution.py:45
  385.6 8.3 %spread.3.refs_4_ = f32[1024,2048]{1,0:T(8,128)} custom-call(s32[8]{0:T(128)} %stack.71.refs_0_, s32[1]{0:T(128)} %bitcast.refs_1_, bf16[8,80,2048]{2,1,0:T(8,128)(2,1)} %joined.2.refs_4_.refs_2_, bf16[8,80,2048]{2,1,0:T(8,128)(2,1)} %collective-permute-done.43.refs_3_), custom_call_target="tpu_custom_call" | custom-call | flops 2760000000 | bytes 1000 | tf_op jit(solution)/shard_map/spread/pallas_call | solution.py:918
  395.6 8.8 %spread.4 = (f32[256,6144]{1,0:T(8,128)}, f32[256,8192]{1,0:T(8,128)}, f32[256,2048]{1,0:T(8,128)}) custom-call(s32[6]{0:T(128)} %stack.68.refs_0_, s32[1]{0:T(128)} %bitcast.refs_1_, bf16[6,128,2048]{2,1,0:T(8,128)(2,1)} %bitcast.44, bf16[6,128,2048]{2,1,0:T(8,128)(2,1)} %copy-done, f32[1024,2048]{1,0:T(8,128)} %spread.3.refs_4_), custom_call_target="tpu_custom_call" | custom-call | flops 2070000000 | bytes 1000 | tf_op jit(solution)/shard_map/spread/pallas_call | solution.py:918
  412.2 4.1 finished.1
  417.3 4.0 spread.5
  (227 shorter events, 116.8 us)
Async XLA Ops:
  4.3 26.1 %collective-permute-start.1 = (bf16[2,128,2048]{2,1,0:T(8,128)(2,1)}, bf16[2,128,2048]{2,1,0:T(8,128)(2,1)}, u32[]{:S(2)}, u32[]{:S(2)}) collective-permute-start(bf16[2,128,2048]{2,1,0:T(8,128)(2,1)} %get-tuple-element.77.refs_14_.refs_22_.refs_13_.refs_1_.refs_15_), channel_id=1, source_target_pairs={{0,1},{1,2},{2,3},{3,0},{4,5},{5,6},{6,7},{7,4},{8,9},{9,10},{10,1... | collective-permute-start | bytes 3145736 | tf_op jit(solution)/shard_map/ppermute | solution.py:45
  6.3 26.0 %collective-permute-start.2 = (bf16[2,128,2048]{2,1,0:T(8,128)(2,1)}, bf16[2,128,2048]{2,1,0:T(8,128)(2,1)}, u32[]{:S(2)}, u32[]{:S(2)}) collective-permute-start(bf16[2,128,2048]{2,1,0:T(8,128)(2,1)} %get-tuple-element.77.refs_14_.refs_22_.refs_13_.refs_1_.refs_15_), channel_id=1, source_target_pairs={{0,4},{1,5},{2,6},{3,7},{4,0},{5,1},{6,2},{7,3},{8,12},{9,13},{10,... | collective-permute-start | bytes 3145736 | tf_op jit(solution)/shard_map/ppermute | solution.py:45
  8.0 36.2 %collective-permute-start = (bf16[2,128,2048]{2,1,0:T(8,128)(2,1)}, bf16[2,128,2048]{2,1,0:T(8,128)(2,1)}, u32[]{:S(2)}, u32[]{:S(2)}) collective-permute-start(bf16[2,128,2048]{2,1,0:T(8,128)(2,1)} %get-tuple-element.77.refs_14_.refs_22_.refs_13_.refs_1_.refs_15_), channel_id=1, source_target_pairs={{0,3},{1,0},{2,1},{3,2},{4,7},{5,4},{6,5},{7,6},{8,11},{9,8},{10,9... | collective-permute-start | bytes 3145736 | tf_op jit(solution)/shard_map/ppermute | solution.py:45
  9.4 34.8 %all-to-all-start = ((bf16[8,40,1792]{2,1,0:T(8,128)(2,1)}), bf16[8,40,1792]{2,1,0:T(8,128)(2,1)S(1)}, u32[]{:S(2)}, u32[]{:S(2)}) async-start(bf16[8,40,1792]{2,1,0:T(8,128)(2,1)} %get-tuple-element.76), calls=%async_computation | async-start | bytes 2293760 | tf_op jit(solution)/shard_map/all_to_all | solution.py:975
  30.3 40.4 %collective-permute-start.5 = (bf16[2,128,2048]{2,1,0:T(8,128)(2,1)}, bf16[2,128,2048]{2,1,0:T(8,128)(2,1)}, u32[]{:S(2)}, u32[]{:S(2)}) collective-permute-start(bf16[2,128,2048]{2,1,0:T(8,128)(2,1)} %collective-permute-done.1.refs_2_.refs_17_.refs_25_.refs_16_.refs_4_.refs_18_), channel_id=1, source_target_pairs={{0,1},{1,2},{2,3},{3,0},{4,5},{5,6},{6,7},{7,4},{8,9},{9,10},{10,1... | collective-permute-start | bytes 3145736 | tf_op jit(solution)/shard_map/ppermute | solution.py:45
  30.7 40.1 %collective-permute-start.7 = (bf16[2,128,2048]{2,1,0:T(8,128)(2,1)}, bf16[2,128,2048]{2,1,0:T(8,128)(2,1)S(1)}, u32[]{:S(2)}, u32[]{:S(2)}) collective-permute-start(bf16[2,128,2048]{2,1,0:T(8,128)(2,1)} %collective-permute-done.1.refs_2_.refs_17_.refs_25_.refs_16_.refs_4_.refs_18_), channel_id=1, source_target_pairs={{0,4},{1,5},{2,6},{3,7},{4,0},{5,1},{6,2},{7,3},{8,12},{9,13},{10,... | collective-permute-start | bytes 3145736 | tf_op jit(solution)/shard_map/ppermute | solution.py:45
  32.3 38.5 %collective-permute-start.6 = (bf16[2,128,2048]{2,1,0:T(8,128)(2,1)}, bf16[2,128,2048]{2,1,0:T(8,128)(2,1)S(1)}, u32[]{:S(2)}, u32[]{:S(2)}) collective-permute-start(bf16[2,128,2048]{2,1,0:T(8,128)(2,1)} %collective-permute-done.2.refs_3_.refs_18_.refs_26_.refs_17_.refs_5_.refs_19_), channel_id=1, source_target_pairs={{0,3},{1,0},{2,1},{3,2},{4,7},{5,4},{6,5},{7,6},{8,11},{9,8},{10,9... | collective-permute-start | bytes 3145736 | tf_op jit(solution)/shard_map/ppermute | solution.py:45
  47.6 20.0 %collective-permute-start.3 = (bf16[8,32,1792]{2,1,0:T(8,128)(2,1)}, bf16[8,32,1792]{2,1,0:T(8,128)(2,1)S(1)}, u32[]{:S(2)}, u32[]{:S(2)}) collective-permute-start(bf16[8,32,1792]{2,1,0:T(8,128)(2,1)} %get-tuple-element.79.refs_0_.refs_4_.refs_3_.refs_5_), channel_id=1, source_target_pairs={{0,96},{1,97},{2,98},{3,99},{4,100},{5,101},{6,102},{7,103},{8,104... | collective-permute-start | bytes 2752520 | tf_op jit(solution)/shard_map/ppermute | solution.py:45
  50.4 20.4 %collective-permute-start.4 = (bf16[8,32,1792]{2,1,0:T(8,128)(2,1)}, bf16[8,32,1792]{2,1,0:T(8,128)(2,1)}, u32[]{:S(2)}, u32[]{:S(2)}) collective-permute-start(bf16[8,32,1792]{2,1,0:T(8,128)(2,1)} %get-tuple-element.79.refs_0_.refs_4_.refs_3_.refs_5_), channel_id=1, source_target_pairs={{0,32},{1,33},{2,34},{3,35},{4,36},{5,37},{6,38},{7,39},{8,40},{9,... | collective-permute-start | bytes 2752520 | tf_op jit(solution)/shard_map/ppermute | solution.py:45
  76.0 26.0 %collective-permute-start.10 = (bf16[24,32,1792]{2,1,0:T(8,128)(2,1)}, bf16[24,32,1792]{2,1,0:T(8,128)(2,1)S(1)}, u32[]{:S(2)}, u32[]{:S(2)}) collective-permute-start(bf16[24,32,1792]{2,1,0:T(8,128)(2,1)} %bitcast.61), channel_id=1, source_target_pairs={{0,8},{1,9},{2,10},{3,11},{4,12},{5,13},{6,14},{7,15},{8,0},{9,1},... | collective-permute-start | bytes 8257544 | tf_op jit(solution)/shard_map/ppermute | solution.py:45
  83.2 14.3 %collective-permute-start.9 = (bf16[4,32,1792]{2,1,0:T(8,128)(2,1)}, bf16[4,32,1792]{2,1,0:T(8,128)(2,1)S(1)}, u32[]{:S(2)}, u32[]{:S(2)}) collective-permute-start(bf16[4,32,1792]{2,1,0:T(8,128)(2,1)} %get-tuple-element.81), channel_id=1, source_target_pairs={{0,96},{1,97},{2,98},{3,99},{4,100},{5,101},{6,102},{7,103},{8,104... | collective-permute-start | bytes 1376264 | tf_op jit(solution)/shard_map/ppermute | solution.py:45
  136.2 21.2 %collective-permute-start.15 = (bf16[8,128,2048]{2,1,0:T(8,128)(2,1)}, bf16[8,128,2048]{2,1,0:T(8,128)(2,1)}, u32[]{:S(2)}, u32[]{:S(2)}) collective-permute-start(bf16[8,128,2048]{2,1,0:T(8,128)(2,1)} %get-tuple-element.86.refs_25_), channel_id=1, source_target_pairs={{0,8},{1,9},{2,10},{3,11},{4,12},{5,13},{6,14},{7,15},{8,0},{9,1},... | collective-permute-start | bytes 12582920 | tf_op jit(solution)/shard_map/ppermute | solution.py:45
  160.7 17.3 %collective-permute-start.17 = (bf16[1,128,2048]{2,1,0:T(8,128)(2,1)}, bf16[1,128,2048]{2,1,0:T(8,128)(2,1)S(1)}, u32[]{:S(2)}, u32[]{:S(2)}) collective-permute-start(bf16[1,128,2048]{2,1,0:T(8,128)(2,1)} %get-tuple-element.92.refs_12_), channel_id=1, source_target_pairs={{0,32},{1,33},{2,34},{3,35},{4,36},{5,37},{6,38},{7,39},{8,40},{9,... | collective-permute-start | bytes 1572872 | tf_op jit(solution)/shard_map/ppermute | solution.py:45
  160.7 17.3 %collective-permute-start.18 = (bf16[1,128,2048]{2,1,0:T(8,128)(2,1)}, bf16[1,128,2048]{2,1,0:T(8,128)(2,1)S(1)}, u32[]{:S(2)}, u32[]{:S(2)}) collective-permute-start(bf16[1,128,2048]{2,1,0:T(8,128)(2,1)} %get-tuple-element.93.refs_13_), channel_id=1, source_target_pairs={{0,96},{1,97},{2,98},{3,99},{4,100},{5,101},{6,102},{7,103},{8,104... | collective-permute-start | bytes 1572872 | tf_op jit(solution)/shard_map/ppermute | solution.py:45
  184.4 37.9 %collective-permute-start.22 = (bf16[2,128,2048]{2,1,0:T(8,128)(2,1)}, bf16[2,128,2048]{2,1,0:T(8,128)(2,1)S(1)}, u32[]{:S(2)}, u32[]{:S(2)}) collective-permute-start(bf16[2,128,2048]{2,1,0:T(8,128)(2,1)} %get-tuple-element.96.refs_3_.refs_30_), channel_id=1, source_target_pairs={{0,32},{1,33},{2,34},{3,35},{4,36},{5,37},{6,38},{7,39},{8,40},{9,... | collective-permute-start | bytes 3145736 | tf_op jit(solution)/shard_map/ppermute | solution.py:45
  184.4 37.9 %collective-permute-start.23 = (bf16[2,128,2048]{2,1,0:T(8,128)(2,1)}, bf16[2,128,2048]{2,1,0:T(8,128)(2,1)S(1)}, u32[]{:S(2)}, u32[]{:S(2)}) collective-permute-start(bf16[2,128,2048]{2,1,0:T(8,128)(2,1)} %get-tuple-element.97.refs_31_), channel_id=1, source_target_pairs={{0,96},{1,97},{2,98},{3,99},{4,100},{5,101},{6,102},{7,103},{8,104... | collective-permute-start | bytes 3145736 | tf_op jit(solution)/shard_map/ppermute | solution.py:45
  191.9 36.2 %collective-permute-start.21 = (bf16[4,64,2048]{2,1,0:T(8,128)(2,1)}, bf16[4,64,2048]{2,1,0:T(8,128)(2,1)S(1)}, u32[]{:S(2)}, u32[]{:S(2)}) collective-permute-start(bf16[4,64,2048]{2,1,0:T(8,128)(2,1)} %away_sums.1.refs_29_), channel_id=1, source_target_pairs={{0,16},{1,17},{2,18},{3,19},{4,20},{5,21},{6,22},{7,23},{8,24},{9,... | collective-permute-start | bytes 3145736 | tf_op jit(solution)/shard_map/ppermute | solution.py:45
  219.5 33.2 %collective-permute-start.19 = (bf16[2,128,2048]{2,1,0:T(8,128)(2,1)}, bf16[2,128,2048]{2,1,0:T(8,128)(2,1)S(1)}, u32[]{:S(2)}, u32[]{:S(2)}) collective-permute-start(bf16[2,128,2048]{2,1,0:T(8,128)(2,1)} %get-tuple-element.100), channel_id=1, source_target_pairs={{0,1},{1,2},{2,3},{3,0},{4,5},{5,6},{6,7},{7,4},{8,9},{9,10},{10,1... | collective-permute-start | bytes 3145736 | tf_op jit(solution)/shard_map/ppermute | solution.py:45
  219.9 32.8 %collective-permute-start.20 = (bf16[2,128,2048]{2,1,0:T(8,128)(2,1)}, bf16[2,128,2048]{2,1,0:T(8,128)(2,1)S(1)}, u32[]{:S(2)}, u32[]{:S(2)}) collective-permute-start(bf16[2,128,2048]{2,1,0:T(8,128)(2,1)} %get-tuple-element.103), channel_id=1, source_target_pairs={{0,3},{1,0},{2,1},{3,2},{4,7},{5,4},{6,5},{7,6},{8,11},{9,8},{10,9... | collective-permute-start | bytes 3145736 | tf_op jit(solution)/shard_map/ppermute | solution.py:45
  228.0 18.5 %collective-permute-start.28 = (bf16[1,128,2048]{2,1,0:T(8,128)(2,1)}, bf16[1,128,2048]{2,1,0:T(8,128)(2,1)S(1)}, u32[]{:S(2)}, u32[]{:S(2)}) collective-permute-start(bf16[1,128,2048]{2,1,0:T(8,128)(2,1)} %get-tuple-element.106.refs_4_), channel_id=1, source_target_pairs={{0,16},{1,17},{2,18},{3,19},{4,20},{5,21},{6,22},{7,23},{8,24},{9,... | collective-permute-start | bytes 1572872 | tf_op jit(solution)/shard_map/ppermute | solution.py:45
  266.6 94.0 %collective-permute-start.25 = (bf16[4,128,2048]{2,1,0:T(8,128)(2,1)}, bf16[4,128,2048]{2,1,0:T(8,128)(2,1)}, u32[]{:S(2)}, u32[]{:S(2)}) collective-permute-start(bf16[4,128,2048]{2,1,0:T(8,128)(2,1)} %get-tuple-element.108.refs_5_), channel_id=1, source_target_pairs={{0,1},{1,2},{2,3},{3,0},{4,5},{5,6},{6,7},{7,4},{8,9},{9,10},{10,1... | collective-permute-start | bytes 6291464 | tf_op jit(solution)/shard_map/ppermute | solution.py:45
  267.0 93.6 %collective-permute-start.26 = (bf16[4,128,2048]{2,1,0:T(8,128)(2,1)}, bf16[4,128,2048]{2,1,0:T(8,128)(2,1)}, u32[]{:S(2)}, u32[]{:S(2)}) collective-permute-start(bf16[4,128,2048]{2,1,0:T(8,128)(2,1)} %get-tuple-element.109), channel_id=1, source_target_pairs={{0,3},{1,0},{2,1},{3,2},{4,7},{5,4},{6,5},{7,6},{8,11},{9,8},{10,9... | collective-permute-start | bytes 6291464 | tf_op jit(solution)/shard_map/ppermute | solution.py:45
  269.3 44.5 %all-to-all-start.2 = ((bf16[8,16,1792]{2,1,0:T(8,128)(2,1)}), bf16[8,16,1792]{2,1,0:T(8,128)(2,1)S(1)}, u32[]{:S(2)}, u32[]{:S(2)}) async-start(bf16[8,16,1792]{2,1,0:T(8,128)(2,1)} %get-tuple-element.121), calls=%async_computation.2 | async-start | bytes 917504 | tf_op jit(solution)/shard_map/all_to_all | solution.py:1210
  272.8 44.9 %collective-permute-start.36 = (bf16[2,80,2048]{2,1,0:T(8,128)(2,1)S(1)}, bf16[2,80,2048]{2,1,0:T(8,128)(2,1)S(1)}, u32[]{:S(2)}, u32[]{:S(2)}) collective-permute-start(bf16[2,80,2048]{2,1,0:T(8,128)(2,1)S(1)} %pad_maximum_fusion.1.refs_0_), channel_id=1, source_target_pairs={{0,32},{1,33},{2,34},{3,35},{4,36},{5,37},{6,38},{7,39},{8,40},{9,... | collective-permute-start | bytes 1966088 | tf_op jit(solution)/shard_map/ppermute | solution.py:45
  272.9 44.8 %collective-permute-start.37 = (bf16[2,80,2048]{2,1,0:T(8,128)(2,1)S(1)}, bf16[2,80,2048]{2,1,0:T(8,128)(2,1)S(1)}, u32[]{:S(2)}, u32[]{:S(2)}) collective-permute-start(bf16[2,80,2048]{2,1,0:T(8,128)(2,1)S(1)} %pad_maximum_fusion.1.refs_0_), channel_id=1, source_target_pairs={{0,96},{1,97},{2,98},{3,99},{4,100},{5,101},{6,102},{7,103},{8,104... | collective-permute-start | bytes 1966088 | tf_op jit(solution)/shard_map/ppermute | solution.py:45
  327.2 37.3 %collective-permute-start.33 = (bf16[2,128,2048]{2,1,0:T(8,128)(2,1)S(1)}, bf16[2,128,2048]{2,1,0:T(8,128)(2,1)S(1)}, u32[]{:S(2)}, u32[]{:S(2)}) collective-permute-start(bf16[2,128,2048]{2,1,0:T(8,128)(2,1)S(1)} %pad_maximum_fusion.refs_0_), channel_id=1, source_target_pairs={{0,32},{1,33},{2,34},{3,35},{4,36},{5,37},{6,38},{7,39},{8,40},{9,... | collective-permute-start | bytes 3145736 | tf_op jit(solution)/shard_map/ppermute | solution.py:45
  327.3 37.2 %collective-permute-start.34 = (bf16[2,128,2048]{2,1,0:T(8,128)(2,1)S(1)}, bf16[2,128,2048]{2,1,0:T(8,128)(2,1)S(1)}, u32[]{:S(2)}, u32[]{:S(2)}) collective-permute-start(bf16[2,128,2048]{2,1,0:T(8,128)(2,1)S(1)} %pad_maximum_fusion.refs_0_), channel_id=1, source_target_pairs={{0,96},{1,97},{2,98},{3,99},{4,100},{5,101},{6,102},{7,103},{8,104... | collective-permute-start | bytes 3145736 | tf_op jit(solution)/shard_map/ppermute | solution.py:45
  330.0 24.2 %collective-permute-start.39 = (bf16[1,80,2048]{2,1,0:T(8,128)(2,1)}, bf16[1,80,2048]{2,1,0:T(8,128)(2,1)S(1)}, u32[]{:S(2)}, u32[]{:S(2)}) collective-permute-start(bf16[1,80,2048]{2,1,0:T(8,128)(2,1)} %get-tuple-element.126), channel_id=1, source_target_pairs={{0,96},{1,97},{2,98},{3,99},{4,100},{5,101},{6,102},{7,103},{8,104... | collective-permute-start | bytes 983048 | tf_op jit(solution)/shard_map/ppermute | solution.py:45
  370.0 23.9 %collective-permute-start.42 = (bf16[6,128,2048]{2,1,0:T(8,128)(2,1)}, bf16[6,128,2048]{2,1,0:T(8,128)(2,1)S(1)}, u32[]{:S(2)}, u32[]{:S(2)}) collective-permute-start(bf16[6,128,2048]{2,1,0:T(8,128)(2,1)} %bitcast.43), channel_id=1, source_target_pairs={{0,8},{1,9},{2,10},{3,11},{4,12},{5,13},{6,14},{7,15},{8,0},{9,1},... | collective-permute-start | bytes 9437192 | tf_op jit(solution)/shard_map/ppermute | solution.py:45
  376.3 28.0 %collective-permute-start.40 = (bf16[1,128,2048]{2,1,0:T(8,128)(2,1)}, bf16[1,128,2048]{2,1,0:T(8,128)(2,1)}, u32[]{:S(2)}, u32[]{:S(2)}) collective-permute-start(bf16[1,128,2048]{2,1,0:T(8,128)(2,1)} %get-tuple-element.127), channel_id=1, source_target_pairs={{0,32},{1,33},{2,34},{3,35},{4,36},{5,37},{6,38},{7,39},{8,40},{9,... | collective-permute-start | bytes 1572872 | tf_op jit(solution)/shard_map/ppermute | solution.py:45
  376.3 28.0 %collective-permute-start.41 = (bf16[1,128,2048]{2,1,0:T(8,128)(2,1)}, bf16[1,128,2048]{2,1,0:T(8,128)(2,1)}, u32[]{:S(2)}, u32[]{:S(2)}) collective-permute-start(bf16[1,128,2048]{2,1,0:T(8,128)(2,1)} %get-tuple-element.128), channel_id=1, source_target_pairs={{0,96},{1,97},{2,98},{3,99},{4,100},{5,101},{6,102},{7,103},{8,104... | collective-permute-start | bytes 1572872 | tf_op jit(solution)/shard_map/ppermute | solution.py:45
  380.8 30.4 %collective-permute-start.27 = (bf16[2,128,2048]{2,1,0:T(8,128)(2,1)}, bf16[2,128,2048]{2,1,0:T(8,128)(2,1)S(1)}, u32[]{:S(2)}, u32[]{:S(2)}) collective-permute-start(bf16[2,128,2048]{2,1,0:T(8,128)(2,1)} %other_sums.1.refs_3_), channel_id=1, source_target_pairs={{0,4},{1,5},{2,6},{3,7},{4,0},{5,1},{6,2},{7,3},{8,12},{9,13},{10,... | collective-permute-start | bytes 3145736 | tf_op jit(solution)/shard_map/ppermute | solution.py:45
  (58 other events, 543.2 us)

commit v8 on v7

--- a/solution.py
+++ b/solution.py
@@ -531,27 +531,50 @@
     )(numbers, *dy, h1, d_qkv, attended, *after)
 
 
-def outer(d_qkv, d_hidden, weight, spots, x, mean, inverse, gains, active, attended, down, out, bias, after):
+def mixed_part(active, attended, down, out, bias, after):
+    rows, ff = active.shape
+    head, width = out.shape
+    step = 512
+    count = rows // 128
+
+    def body(act_ref, ol_ref, wd_ref, wo_ref, b_ref, *refs):
+        total = dot(act_ref[...], wd_ref[...]) + dot(ol_ref[...], wo_ref[...]) + b_ref[...]
+        for at in range(count):
+            refs[at][...] = total[at * 128 : (at + 1) * 128].astype(bf16)
+
+    return pl.pallas_call(
+        after_inputs(body, 5, len(after)),
+        out_shape=(jax.ShapeDtypeStruct((128, width), bf16),) * count,
+        grid=(width // step,),
+        in_specs=[
+            pl.BlockSpec((rows, ff), lambda i: (0, 0)),
+            pl.BlockSpec((rows, head), lambda i: (0, 0)),
+            pl.BlockSpec((ff, step), lambda i: (0, i)),
+            pl.BlockSpec((head, step), lambda i: (0, i)),
+            pl.BlockSpec((1, step), lambda i: (0, i)),
+        ]
+        + anywhere(len(after)),
+        out_specs=(pl.BlockSpec((128, step), lambda i: (0, i)),) * count,
+        compiler_params=kernel_params(),
+        cost_estimate=cost(10),
+        name="mixed_part",
+    )(active, attended, down, out, bias, *after)
+
+
+def back_norms(d_qkv, d_hidden, weight, spots, x, mean, inverse, gains, after):
     total, n1 = d_qkv.shape
     n2 = d_hidden.shape[1]
     count = len(x)
     parts = len(weight)
-    head, width = out.shape
+    width = x[0].shape[-1]
     step = 512
 
-    def body(spot_ref, m_ref, i_ref, g_ref, b_ref, *refs):
+    def body(spot_ref, m_ref, i_ref, g_ref, *refs):
         w_refs, refs = refs[:parts], refs[parts:]
         x_refs, refs = refs[:count], refs[count:]
-        plain, sums_ref, outs = refs[:6], refs[6], refs[7 : 7 + count]
-        dq_v, du_v, act_v, ol_v, wd_v, wo_v, w_v, x_v, pair_v, w_sem, x_sem, sems, out_sem = refs[
-            7 + count :
-        ]
-        plain_v = (dq_v, du_v, act_v, ol_v, wd_v, wo_v)
-        first = loads(
-            [
-                pltpu.make_async_copy(plain[n], plain_v[n], sems.at[n]) for n in range(2, 6)
-            ]
-        )
+        plain, sums_ref, outs = refs[:2], refs[2], refs[3 : 3 + count]
+        dq_v, du_v, w_v, x_v, s_v, w_sem, x_sem, sems, out_sem = refs[3 + count :]
+        plain_v = (dq_v, du_v)
         copies = loads(
             [
                 pltpu.make_async_copy(plain[n], plain_v[n], sems.at[n]) for n in range(2)
@@ -559,27 +582,14 @@
             + weight_copies(weight, w_refs, spot_ref, w_v, slice(None), w_sem)
             + piece_copies(x_refs, 0, x_v, x_sem, 128)
         )
-        for copy in first:
-            copy.wait()
-
-        def leaving(n, half):
+        def leaving(n):
             lanes = pl.ds(pl.multiple_of(n * step, step), step)
             return [
                 pltpu.make_async_copy(
-                    pair_v.at[half, pl.ds(at * 128, 128), lanes],
-                    outs[at].at[half, :, lanes],
-                    out_sem.at[half, at],
+                    s_v.at[pl.ds(at * 128, 128), lanes], outs[at].at[:, lanes], out_sem.at[at]
                 )
                 for at in range(count)
             ]
-
-        @pl.loop(0, width // step)
-        def _(n):
-            lanes = pl.ds(pl.multiple_of(n * step, step), step)
-            mix = dot(act_v[...], wd_v[:, lanes]) + dot(ol_v[...], wo_v[:, lanes])
-            pair_v[0, :, lanes] = (mix + b_ref[:, lanes]).astype(bf16)
-            for copy in leaving(n, 0):
-                copy.start()
 
         for copy in copies:
             copy.wait()
@@ -590,8 +600,8 @@
             sources = pl.ds(n * (step // 256), step // 256)
             d1 = dot(dq_v[...], w_v[sources, :, :, 0:n1].reshape(step, n1), 1, 1)
             d2 = dot(du_v[...], w_v[sources, :, :, n1:].reshape(step, n2), 1, 1)
-            pair_v[1, :, lanes] = (d1 * g_ref[0:1, lanes] + d2 * g_ref[1:2, lanes]).astype(bf16)
-            for copy in leaving(n, 1):
+            s_v[:, lanes] = (d1 * g_ref[0:1, lanes] + d2 * g_ref[1:2, lanes]).astype(bf16)
+            for copy in leaving(n):
                 copy.start()
             normed = (x_v[:, lanes].astype(f32) - m_ref[...]) * i_ref[...]
             sums_ref[0:1, lanes] = jnp.sum(d1 * normed, 0, keepdims=True)
@@ -600,51 +610,41 @@
             sums_ref[3:4, lanes] = jnp.sum(d2, 0, keepdims=True)
 
         for n in range(width // step):
-            for half in range(2):
-                for copy in leaving(n, half):
-                    copy.wait()
+            for copy in leaving(n):
+                copy.wait()
 
     vmem = pl.BlockSpec(memory_space=pltpu.VMEM)
     return pl.pallas_call(
-        after_inputs(body, 11 + parts + count, len(after)),
+        after_inputs(body, 6 + parts + count, len(after)),
         out_shape=(jax.ShapeDtypeStruct((4, width), f32),)
-        + (jax.ShapeDtypeStruct((2, 128, width), bf16),) * count,
+        + (jax.ShapeDtypeStruct((128, width), bf16),) * count,
         in_specs=[pl.BlockSpec(memory_space=pltpu.SMEM)]
-        + [vmem] * 4
-        + anywhere(parts + count + 6 + len(after)),
+        + [vmem] * 3
+        + anywhere(parts + count + 2 + len(after)),
         out_specs=(vmem,) + tuple(anywhere(count)),
         scratch_shapes=[
             pltpu.VMEM((total, n1), bf16),
             pltpu.VMEM((total, n2), bf16),
-            pltpu.VMEM((total, n2), bf16),
-            pltpu.VMEM((total, head), bf16),
-            pltpu.VMEM((n2, width), bf16),
-            pltpu.VMEM((head, width), bf16),
             pltpu.VMEM((8, 8, width // 64, n1 + n2), bf16),
             pltpu.VMEM((total, width), bf16),
-            pltpu.VMEM((2, total, width), bf16),
+            pltpu.VMEM((total, width), bf16),
             pltpu.SemaphoreType.DMA((parts,)),
             pltpu.SemaphoreType.DMA((count,)),
-            pltpu.SemaphoreType.DMA((6,)),
-            pltpu.SemaphoreType.DMA((2, count)),
+            pltpu.SemaphoreType.DMA((2,)),
+            pltpu.SemaphoreType.DMA((count,)),
         ],
         compiler_params=kernel_params(),
-        cost_estimate=cost(20),
-        name="outer",
+        cost_estimate=cost(15),
+        name="back_norms",
     )(
         spots,
         mean,
         inverse,
         gains,
-        bias,
         *[p[0] for p in weight],
         *x,
         d_qkv,
         d_hidden,
-        active,
-        attended,
-        down,
-        out,
         *after,
     )
 
@@ -669,39 +669,6 @@
         cost_estimate=cost(3),
         name="unpacked",
     )(part, *after)
-
-
-def packed_sums(stays, crossed, own, below, above, ff, head, after):
-    width = own.shape[1]
-
-    def body(stay_ref, cross_ref, own_ref, below_ref, above_ref, out_ref, lanes_ref, keep_ref):
-        inner = (stay_ref[0].astype(f32) + cross_ref[0].astype(f32)).astype(bf16)
-        total = wide(own_ref, below_ref, above_ref).astype(bf16)
-        for owner in range(8):
-            pieces = [
-                total[16 * third : 16 * third + 16, owner * head : (owner + 1) * head]
-                for third in range(3)
-            ]
-            row, col = 64 + 16 * (owner % 4), owner // 4 * ff
-            pieces.append(inner[row : row + 16, col : col + ff])
-            out_ref[owner] = jnp.concatenate(pieces, 1)
-            lanes_ref[owner] = total[48:64, owner * head : (owner + 1) * head]
-        keep_ref[...] = inner[0:64]
-
-    vmem = pl.BlockSpec(memory_space=pltpu.VMEM)
-    return pl.pallas_call(
-        after_inputs(body, 5, len(after)),
-        out_shape=(
-            jax.ShapeDtypeStruct((8, 16, 3 * head + ff), bf16),
-            jax.ShapeDtypeStruct((8, 16, width // 8), bf16),
-            jax.ShapeDtypeStruct((64, width), bf16),
-        ),
-        in_specs=[vmem] * 5 + anywhere(len(after)),
-        out_specs=(vmem,) * 3,
-        compiler_params=kernel_params(),
-        cost_estimate=cost(3),
-        name="packed_sums",
-    )(stays, crossed, own, below, above, *after)
 
 
 def joined(arrays, after):
@@ -772,80 +739,121 @@
     return low, high, together.reshape(3 * count, rows, cols)
 
 
-def small_sums(norm_sums, qkv_sums, up_sums, dy_sums, numbers, after):
-    def body(number_ref, norm_ref, q_ref, u_ref, y_ref, out_ref, work):
-        shard = number_ref[1]
-        for owner in range(8):
-            mine = shard == owner
-            for n in range(4):
-                for half in range(2):
-                    at = owner * 256 + half * 128
-                    work[owner, n * 2 + half : n * 2 + half + 1] = norm_ref[n : n + 1, at : at + 128]
-            for n in range(3):
-                third, source = divmod(owner * 3 + n, 8)
-                for half in range(2):
-                    at = third * 256 + half * 128
-                    work[owner, 8 + n * 2 + half : 9 + n * 2 + half] = jnp.where(
-                        shard == source, q_ref[:, at : at + 128], 0.0
-                    )
-            for n in range(8):
-                work[owner, 14 + n : 15 + n] = jnp.where(
-                    mine, u_ref[:, n * 128 : (n + 1) * 128], 0.0
-                )
-            for n in range(2):
-                work[owner, 22 + n : 23 + n] = jnp.where(
-                    mine, y_ref[:, n * 128 : (n + 1) * 128], 0.0
-                )
-        out_ref[...] = work[...].astype(bf16)
-
-    vmem = pl.BlockSpec(memory_space=pltpu.VMEM)
-    return pl.pallas_call(
-        after_inputs(body, 5, len(after)),
-        out_shape=jax.ShapeDtypeStruct((8, 24, 128), bf16),
-        in_specs=[pl.BlockSpec(memory_space=pltpu.SMEM)] + [vmem] * 4 + anywhere(len(after)),
-        out_specs=vmem,
-        scratch_shapes=[pltpu.VMEM((8, 24, 128), f32)],
-        compiler_params=kernel_params(),
-        cost_estimate=cost(3),
-        name="small_sums",
-    )(numbers, norm_sums, qkv_sums, up_sums, dy_sums, *after)
-
-
-def finished(own, below, above, other, tokens, cotangent, after):
+def finished(mix, sums, tokens, cotangent, after):
     rows, width = tokens.shape
     step = rows // 2
 
-    def body(own_ref, below_ref, above_ref, other_ref, x_ref, dy_ref, mixed_ref, grad_ref):
-        total = wide(own_ref, below_ref, above_ref, other_ref)
+    def body(*refs):
+        x_ref, dy_ref, mixed_ref, grad_ref = refs[8:]
         x = x_ref[...].astype(f32)
-        mixed_ref[...] = (x + total[0]).astype(bf16)
+        mixed_ref[...] = (x + wide(*refs[:4])).astype(bf16)
+        gain = wide(*refs[4:8])
         centre = x - jnp.mean(x, 1, keepdims=True)
         inverse = lax.rsqrt(jnp.mean(centre * centre, 1, keepdims=True) + EPS)
         normed = centre * inverse
-        gain = total[1]
         grad_ref[...] = dy_ref[...].astype(f32) + inverse * (
             gain
             - jnp.mean(gain, 1, keepdims=True)
             - normed * jnp.mean(gain * normed, 1, keepdims=True)
         )
 
-    def pair(first):
-        return pl.BlockSpec((2, step, width), lambda i: (first, i, 0))
-
     block = pl.BlockSpec((step, width), lambda i: (i, 0))
+    later = pl.BlockSpec((step, width), lambda i: (i + 2, 0))
     return pl.pallas_call(
-        after_inputs(body, 6, len(after)),
+        after_inputs(body, 10, len(after)),
         out_shape=(
             jax.ShapeDtypeStruct((rows, width), bf16),
             jax.ShapeDtypeStruct((rows, width), f32),
         ),
         grid=(2,),
-        in_specs=[pair(0), pair(1), pair(0), pair(0), block, block] + anywhere(len(after)),
+        in_specs=[block, later, block, block] * 2 + [block, block] + anywhere(len(after)),
         out_specs=(block, block),
         compiler_params=kernel_params(),
         cost_estimate=cost(3),
         name="finished",
-    )(own, below, above, other, tokens, cotangent, *after)
+    )(*mix, *sums, tokens, cotangent, *after)
+
+
+def packed_sums(stays, crossed, own, below, above, norm_sums, qkv_sums, up_sums, dy_sums, numbers, ff, head, after):
+    width = own.shape[1]
+
+    def body(*refs):
+        stay_ref, cross_ref, own_ref, below_ref, above_ref = refs[:5]
+        norm_ref, q_ref, u_ref, y_ref, number_ref, out_ref, lanes_ref, keep_ref, small = refs[5:]
+        shard = number_ref[1]
+        inner = (stay_ref[0].astype(f32) + cross_ref[0].astype(f32)).astype(bf16)
+        total = wide(own_ref, below_ref, above_ref).astype(bf16)
+        for owner in range(8):
+            mine = shard == owner
+            small[...] = jnp.zeros_like(small)
+            small[0:4] = norm_ref[:, owner * head : (owner + 1) * head]
+            for n in range(3):
+                third, source = divmod(owner * 3 + n, 8)
+                lanes = slice(third * head, (third + 1) * head)
+                small[4 + n : 5 + n] = jnp.where(shard == source, q_ref[:, lanes], 0.0)
+            for n in range(4):
+                lanes = slice(n * head, (n + 1) * head)
+                small[7 + n : 8 + n] = jnp.where(mine, u_ref[:, lanes], 0.0)
+            small[11:12] = jnp.where(mine, y_ref[...], 0.0)
+            pieces = [
+                total[16 * third : 16 * third + 16, owner * head : (owner + 1) * head]
+                for third in range(3)
+            ]
+            row, col = 64 + 16 * (owner % 4), owner // 4 * ff
+            pieces.append(inner[row : row + 16, col : col + ff])
+            pieces.append(small[...].astype(bf16))
+            out_ref[owner] = jnp.concatenate(pieces, 1)
+            lanes_ref[owner] = total[48:64, owner * head : (owner + 1) * head]
+        keep_ref[...] = inner[0:64]
+
+    vmem = pl.BlockSpec(memory_space=pltpu.VMEM)
+    return pl.pallas_call(
+        after_inputs(body, 10, len(after)),
+        out_shape=(
+            jax.ShapeDtypeStruct((8, 16, 4 * head + ff), bf16),
+            jax.ShapeDtypeStruct((8, 16, width // 8), bf16),
+            jax.ShapeDtypeStruct((64, width), bf16),
+        ),
+        in_specs=[vmem] * 9 + [pl.BlockSpec(memory_space=pltpu.SMEM)] + anywhere(len(after)),
+        out_specs=(vmem,) * 3,
+        scratch_shapes=[pltpu.VMEM((16, head), f32)],
+        compiler_params=kernel_params(),
+        cost_estimate=cost(3),
+        name="packed_sums",
+    )(stays, crossed, own, below, above, norm_sums, qkv_sums, up_sums, dy_sums, numbers, *after)
+
+
+def unpacked_sums(received, outs, downs, after):
+    sources, rows, width = received.shape
+    cols = width - outs.shape[2]
+
+    def body(part_ref, outs_ref, down_ref, part_out, down_out):
+        part_out[0] = jnp.concatenate(
+            [
+                jnp.concatenate([part_ref[n, :, 0:cols], outs_ref[n]], 1)
+                for n in range(sources)
+            ],
+            0,
+        )
+        small = jnp.sum(part_ref[:, :, cols:].astype(f32), 0).astype(bf16)
+        down_out[0, 0:64] = down_ref[...]
+        down_out[0, 64 : 64 + rows] = jnp.concatenate(
+            [small, jnp.zeros((rows, cols), bf16)], 1
+        )
+
+    vmem = pl.BlockSpec(memory_space=pltpu.VMEM)
+    return pl.pallas_call(
+        after_inputs(body, 3, len(after)),
+        out_shape=(
+            jax.ShapeDtypeStruct((1, sources * rows, width), bf16),
+            jax.ShapeDtypeStruct((1, 64 + rows, width), bf16),
+        ),
+        in_specs=[vmem] * 3 + anywhere(len(after)),
+        out_specs=(vmem,) * 2,
+        compiler_params=kernel_params(),
+        cost_estimate=cost(3),
+        name="unpacked_sums",
+    )(received, outs, downs, *after)
 
 
 def blocks_call(name, body, numbers, terms, outs, after, time=3):
@@ -1100,7 +1108,8 @@
         (above,),
     )
     a_crossed = move(a_away, h=1)
-    norm_sums, *pairs_out = outer(
+    mix = mixed_part(active, attended, down_weight, out_weight, wide_bias, (a_away, above, below))
+    norm_sums, *sums = back_norms(
         d_qkv,
         d_hidden,
         weight,
@@ -1109,17 +1118,55 @@
         mean,
         inverse,
         jnp.stack([gains[0], gains[2]]),
-        active,
-        attended,
-        down_weight,
-        out_weight,
-        wide_bias,
-        (a_away, above, below),
-    )
-
-    smalls = small_sums(norm_sums, qkv_sums, up_sums, dy_sums, numbers, ())
-    smalls = jnp.sum(lax.all_to_all(smalls, "shard", 0, 0).astype(f32), 0)
-    smalls = jnp.pad(smalls.astype(bf16).reshape(-1), (0, 16 * width - 3072)).reshape(16, width)
+        (mix[0],),
+    )
+
+    flat, both = (128, width), (256, width)
+
+    def passed_body(n_ref, up_ref, from_below, here_ref, down_ref, from_above, there_ref, up_out, down_out):
+        up_out[0:128] = wide(up_ref, from_below).astype(bf16)
+        up_out[128:256] = here_ref[...]
+        down_out[0:128] = wide(down_ref, from_above).astype(bf16)
+        down_out[128:256] = there_ref[...]
+
+    def other_body(n_ref, own_ref, below_ref, above_ref, out_ref):
+        out_ref[...] = wide(own_ref, below_ref, above_ref).astype(bf16)
+
+    def first(n):
+        return 0
+
+    def ring_start(pieces):
+        return move(pieces[6], x=1), move(pieces[2], x=-1)
+
+    def ring_middle(pieces, passed, after):
+        operands = (pieces[5], passed[0], pieces[1], pieces[3], passed[1], pieces[7])
+        ups, downs = blocks_call(
+            "passed_sums",
+            passed_body,
+            numbers,
+            [(v, flat, first) for v in operands],
+            (both, both),
+            after,
+        )
+        return (move(ups, x=1), move(downs, x=-1)), ups
+
+    def ring_end(pieces, arrived, after):
+        (other,) = blocks_call(
+            "other_sums",
+            other_body,
+            numbers,
+            [
+                (pieces[4], flat, first),
+                (arrived[0], flat, first),
+                (arrived[1], flat, lambda n: 1),
+            ],
+            (flat,),
+            after,
+        )
+        return (pieces[0], *arrived, move(other, l=1)), other
+
+    mix_passed = ring_start(mix)
+    mix_arrived, mix_ups = ring_middle(mix, mix_passed, (norm_sums,))
 
     def ends_body(n_ref, keep_ref, got_ref, below_ref, above_ref, leave_ref, stay_ref):
         total = wide(keep_ref, got_ref, below_ref, above_ref).astype(bf16)
@@ -1134,11 +1181,9 @@
         [(v, pair_shape, turn(0)) for v in (keep, got)]
         + [(v, pair_shape, lambda n: 0) for v in (from_below, from_above)],
         (one, one),
-        (norm_sums,),
+        (mix_ups,),
     )
     crossed = move(leaves, h=1)
-
-    passed_below, passed_above = move(pairs_out[6], x=1), move(pairs_out[2], x=-1)
 
     def around_body(n_ref, keep_ref, got_ref, crossed_ref, low_ref, high_ref, above_ref, own_ref, below_ref):
         def part(k):
@@ -1174,57 +1219,30 @@
         numbers,
         [(v, v.shape, lambda n: 0) for v in (a_above, a_below, a_low, a_high)],
         ((64, width), (64, width)),
-        (crossed, smalls),
+        (crossed,),
     )
     a_from_below, a_from_above = move(a_above, y=1), move(a_below, y=-1)
 
-    def passed_body(n_ref, up_ref, from_below, here_ref, down_ref, from_above, there_ref, up_out, down_out):
-        up_out[0:2] = wide(up_ref, from_below).astype(bf16)
-        up_out[2:4] = here_ref[...]
-        down_out[0:2] = wide(down_ref, from_above).astype(bf16)
-        down_out[2:4] = there_ref[...]
-
-    ups, downs = blocks_call(
-        "passed_sums",
-        passed_body,
+    part, outs, downs = packed_sums(
+        stays,
+        crossed,
+        a_own,
+        a_from_below,
+        a_from_above,
+        norm_sums,
+        qkv_sums,
+        up_sums,
+        dy_sums,
         numbers,
-        [
-            (v, pair_shape, lambda n: 0)
-            for v in (
-                pairs_out[5],
-                passed_below,
-                pairs_out[1],
-                pairs_out[3],
-                passed_above,
-                pairs_out[7],
-            )
-        ],
-        ((4, 128, width),) * 2,
-        (a_low,),
-    )
-    from_device_below, from_device_above = move(ups, x=1), move(downs, x=-1)
-
-    part, outs, downs_sum = packed_sums(
-        stays, crossed, a_own, a_from_below, a_from_above, ff, head, (ups,)
+        ff,
+        head,
+        (),
     )
     received = lax.all_to_all(part, "shard", 0, 0)
-    part = jnp.concatenate([received, outs], 2).reshape(1, 128, width)
-    def other_body(n_ref, own_ref, below_ref, above_ref, out_ref):
-        out_ref[...] = wide(own_ref, below_ref, above_ref).astype(bf16)
-
-    (total_other,) = blocks_call(
-        "other_sums",
-        other_body,
-        numbers,
-        [
-            (pairs_out[4], pair_shape, lambda n: 0),
-            (from_device_below, pair_shape, lambda n: 0),
-            (from_device_above, pair_shape, lambda n: 1),
-        ],
-        (pair_shape,),
-        (),
-    )
-    total_other, sent_other = move(total_other, l=1), total_other
+    mix_left, mix_other = ring_end(mix, mix_arrived, ())
+    part, downs = unpacked_sums(received, outs, downs, (mix_other,))
+    sums_arrived, sums_ups = ring_middle(sums, ring_start(sums), (received,))
+    sums_left, sums_other = ring_end(sums, sums_arrived, ())
 
     order = ((0, h), (0, 1 - h), (1, h), (1, 1 - h), (3, h), (3, 1 - h), (2, h), (2, 1 - h))
     places = jnp.stack([(y + k) % 4 * 2 + high for k, high in order]).astype(jnp.int32)
@@ -1235,7 +1253,7 @@
         low, high, near = halves(own, below, above, after)
         return near, (move(low, y=1), move(high, y=-1))
 
-    near, far = rep_gather(jnp.concatenate([downs_sum, smalls])[None], ())
+    near, far = rep_gather(downs, (sums_ups,))
     downs_all = joined((near, *far), ())
     downs_yours = move(downs_all, c=1)
     (down_grad,) = spread(
@@ -1247,7 +1265,7 @@
         (),
         (),
     )
-    near, far = rep_gather(part, (sent_other, downs_all))
+    near, far = rep_gather(part, (downs_all, sums_other))
     targets = [
         (
             3 * width,
@@ -1263,9 +1281,7 @@
     ]
     grads = spread([(near, move(near, c=1))], places[:6], numbers[:1], targets, 8, (), (down_grad,))
     far = joined(far, (grads[0],))
-    mixed, tokens_grad = finished(
-        pairs_out[0], from_device_below, from_device_above, total_other, tokens, cotangent, (far,)
-    )
+    mixed, tokens_grad = finished(mix_left, sums_left, tokens, cotangent, (far,))
     qkv_grad, up_grad, out_grad = spread(
         [(far, move(far, c=1))],
         places[6:],
@@ -1275,10 +1291,10 @@
         grads,
         (tokens_grad,),
     )
-    smalls = jnp.concatenate([downs_all[:, 64:66], downs_yours[:, 64:66]]).astype(f32)
-    smalls = jnp.sum(smalls, 0).reshape(-1)
-    norm_grads = smalls[:1024].reshape(4, 256)
-    dy_total = smalls[2816:3072]
+    smalls = jnp.concatenate([downs_all[:, 64:80, 0:head], downs_yours[:, 64:80, 0:head]])
+    smalls = jnp.sum(smalls.astype(f32), 0)
+    norm_grads = smalls[:4]
+    dy_total = smalls[11]
     return (
         mixed,
         tokens_grad,
@@ -1287,11 +1303,11 @@
         norm_grads[2],
         norm_grads[3],
         qkv_grad,
-        smalls[1024:1792],
+        smalls[4:7].reshape(3 * head),
         out_grad,
         dy_total,
         up_grad,
-        smalls[1792:2816],
+        smalls[7:11].reshape(ff),
         down_grad,
         dy_total,
     )

time: 429 us -> 421 us (0.981)
  waiting for transfers between devices: 123 us -> 114 us
  blocking collectives: 8.87 us -> 0 us
  Pallas kernels: 172 us -> 180 us
    all_to_all x1, waiting for transfers between devices: 37.9 us -> 3.03 us  [local(): received = lax.all_to_all(part, 'shard', 0, 0)]
    ppermute x45 -> x50, waiting for transfers between devices: 76.3 us -> 102 us  [move(): return lax.ppermute(value, BOTH, pairs)]
    all_to_all x1 -> x0, blocking collectives: 8.87 us -> none  [local(): smalls = jnp.sum(lax.all_to_all(smalls, 'shard', 0, 0).astype(f32), 0)]
    pallas_call x8 -> x10, Pallas kernels: 31.9 us -> 36.4 us  [blocks_call(): pl.pallas_call(after_inputs(body, 1 + len(terms), len(after)), out_shape=...]
    pallas_call x4 -> x5, Pallas kernels: 32.4 us -> 36.2 us  [the longest x1 17.8 us: back_norms(): pl.pallas_call(after_inputs(body, 6 + parts + count, len(after)), out_sha...]
    unnamed x92 -> x115, local copies, waits for them, and re-layouts: 22.2 us -> 25.9 us
    ppermute x45 -> x50, starting transfers between devices: 67.7 us -> 68.6 us  [move(): return lax.ppermute(value, BOTH, pairs)]
  transfers between devices with their start and end apart: 47 -> 52, of which waited for: 11 -> 18; matrix products, arithmetic and copies ran while one was open for 5% -> 5% of each run, Pallas kernels for 28% -> 30%
where the time goes in v8:
time: 421 us; the launch traced here: 414 us
  Pallas kernels  180 us (43%)
  waiting for transfers between devices  114 us (27%)
  starting transfers between devices  75.7 us (18%)
  local copies, waits for them, and re-layouts  35.3 us (8%)
  other arithmetic  7.19 us (2%)
    ppermute x50, waiting for transfers between devices, move(): return lax.ppermute(value, BOTH, pairs)  102 us
    ppermute x50, starting transfers between devices, move(): return lax.ppermute(value, BOTH, pairs)  68.6 us
    pallas_call x10, Pallas kernels, blocks_call(): pl.pallas_call(after_inputs(body, 1 + len(terms), len(after)), out_shape=...  36.4 us
    pallas_call x1, Pallas kernels, feed_forward(): pl.pallas_call(after_inputs(body, 5 + parts + 2 * count, len(after)), out...  32.2 us
    unnamed x115, local copies, waits for them, and re-layouts  25.9 us
    pallas_call x3, Pallas kernels, spread(): pl.pallas_call(after_inputs(body, 2 + 2 * len(pieces) + len(before), len(...  21.1 us
    pallas_call x1, Pallas kernels, back_norms(): pl.pallas_call(after_inputs(body, 6 + parts + count, len(after)), out_sha...  17.8 us
    pallas_call x1, Pallas kernels, attend(): pl.pallas_call(after_inputs(body, 7 + parts + count, len(after)), out_sha...  17.1 us
  transfers between devices with their start and end apart: 52, of which 18 were waited for; matrix products, arithmetic and copies ran while one was open for 5% of the time, Pallas kernels for 30%

profile of v8, /device:TPU:1, one launch (start us, length us, event | category | flops | bytes accessed | tf_op | source)
XLA Modules:
  0.0 414.5 jit_solution(1073316657571174326)
XLA Ops:
  0.7 3.6 packed.1
  9.4 3.6 all-to-all-start
  13.0 17.3 %collective-permute-done.1.refs_2_.refs_17_.refs_25_.refs_16_.refs_4_ = bf16[2,128,2048]{2,1,0:T(8,128)(2,1)} collective-permute-done((bf16[2,128,2048]{2,1,0:T(8,128)(2,1)}, bf16[2,128,2048]{2,1,0:T(8,128)(2,1)}, u32[]{:S(2)}, u32[]{:S(2)}) %collective-permute-start.1) | collective-permute-done | bytes 1048608 | tf_op jit(solution)/shard_map/ppermute | solution.py:45
  35.0 9.2 %all-to-all-done.refs_0_ = bf16[8,40,1792]{2,1,0:T(8,128)(2,1)S(1)} async-done(((bf16[8,40,1792]{2,1,0:T(8,128)(2,1)}), bf16[8,40,1792]{2,1,0:T(8,128)(2,1)S(1)}, u32[]{:S(2)}, u32[]{:S(2)}) %all-to-all-start) | async-done | bytes 1146912 | tf_op jit(solution)/shard_map/all_to_all | solution.py:983
  50.9 17.4 %collective-permute-done.4.refs_1_.refs_8_.refs_7_ = bf16[8,32,1792]{2,1,0:T(8,128)(2,1)} collective-permute-done((bf16[8,32,1792]{2,1,0:T(8,128)(2,1)}, bf16[8,32,1792]{2,1,0:T(8,128)(2,1)}, u32[]{:S(2)}, u32[]{:S(2)}) %collective-permute-start.4) | collective-permute-done | bytes 917536 | tf_op jit(solution)/shard_map/ppermute | solution.py:45
  72.9 3.6 collective-permute-start.10
  88.0 8.7 %collective-permute-done.8.refs_6_.refs_5_ = bf16[4,32,1792]{2,1,0:T(8,128)(2,1)S(1)} collective-permute-done((bf16[4,32,1792]{2,1,0:T(8,128)(2,1)}, bf16[4,32,1792]{2,1,0:T(8,128)(2,1)S(1)}, u32[]{:S(2)}, u32[]{:S(2)}) %collective-permute-start.8) | collective-permute-done | bytes 458784 | tf_op jit(solution)/shard_map/ppermute | solution.py:45
  103.5 32.2 %feed_forward.1 = (bf16[1024,2048]{1,0:T(8,128)(2,1)}, bf16[1024,1024]{1,0:T(8,128)(2,1)}, bf16[1024,1024]{1,0:T(8,128)(2,1)}, bf16[8,128,2048]{2,1,0:T(8,128)(2...) custom-call(s32[4]{0:T(128)} %get-tuple-element.174.refs_0_.refs_9_,, ...), custom_call_target="tpu_custom_call" | custom-call | flops 36800000000 | bytes 1000 | tf_op jit(solution)/shard_map/feed_forward/pallas_call | solution.py:243
  139.6 17.1 %attend.1 = (bf16[1024,256]{1,0:T(8,128)(2,1)}, bf16[1024,768]{1,0:T(8,128)(2,1)}, f32[1,768]{1,0:T(1,128)}) custom-call(s32[8,3]{1,0:T(8,128)} %copy-done.9, s32[8]{0:T(128)} %pad_add_fusion.1.refs_1_.refs_0_, f32[3,1,256]{2,1,0:T(1,128)} %pad_maximum_fusion.1.refs_2_, bf16[8,32,1792]{2,1,0:T(8,128)(2,1)} %get-tuple-element.91.refs_0_.refs_4_.refs_3_, ...), custom_call_target="tpu_custom_call" | custom-call | flops 19549999104 | bytes 1000 | tf_op jit(solution)/shard_map/attend/pallas_call | solution.py:416
  162.7 13.6 %attention_grads.1 = (bf16[8,64,2048]{2,1,0:T(8,128)(2,1)}, bf16[8,64,2048]{2,1,0:T(8,128)(2,1)}) custom-call(s32[4]{0:T(128)} %get-tuple-element.174.refs_0_.refs_9_, bf16[2,128,2048]{2,1,0:T(8,128)(2,1)} %get-tuple-element.89.refs_14_.refs_22_.refs_13_.refs_1_, bf16[2,128,2048]{2,1,0:T(8,128)(2,1)} %collective-permute-done.refs_1_.refs_15_.refs_23_.refs_14_.refs_2_, ...), custom_call_target="tpu_custom_call" | custom-call | flops 13799999488 | bytes 1000 | tf_op jit(solution)/shard_map/attention_grads/pallas_call | solution.py:513
  178.8 4.8 %near_sums.1 = (bf16[2,128,2048]{2,1,0:T(8,128)(2,1)}, bf16[2,128,2048]{2,1,0:T(8,128)(2,1)}) custom-call(s32[4]{0:T(128)} %get-tuple-element.174.refs_0_.refs_9_, bf16[8,128,2048]{2,1,0:T(8,128)(2,1)} %get-tuple-element.100.refs_1_.refs_3_, bf16[8,128,2048]{2,1,0:T(8,128)(2,1)} %collective-permute-done.15.refs_2_.refs_4_, ...), custom_call_target="tpu_custom_call" | custom-call | flops 23000000512 | bytes 1000 | tf_op jit(solution)/shard_map/near_sums/pallas_call | solution.py:864
  193.1 9.3 %mixed_part.1 = (bf16[128,2048]{1,0:T(8,128)(2,1)}, bf16[128,2048]{1,0:T(8,128)(2,1)}, bf16[128,2048]{1,0:T(8,128)(2,1)}, bf16[128,2048]{1,0:T(8,128)(2,1)}, bf1...) custom-call(bf16[1024,1024]{1,0:T(8,128)(2,1)} %get-tuple-element.95., ...), custom_call_target="tpu_custom_call" | custom-call | flops 11500000256 | bytes 1000 | tf_op jit(solution)/shard_map/mixed_part/pallas_call | solution.py:545
  205.2 17.8 %back_norms.1 = (f32[4,2048]{1,0:T(4,128)}, bf16[128,2048]{1,0:T(8,128)(2,1)}, bf16[128,2048]{1,0:T(8,128)(2,1)}, bf16[128,2048]{1,0:T(8,128)(2,1)}, bf16[128,20...) custom-call(s32[8]{0:T(128)} %pad_add_fusion.1.refs_1_.refs_0_, ...), custom_call_target="tpu_custom_call" | custom-call | flops 17250000896 | bytes 1000 | tf_op jit(solution)/shard_map/back_norms/pallas_call | solution.py:617
  224.0 3.9 passed_sums.2
  229.2 4.4 %end_sums.1 = (bf16[1,128,2048]{2,1,0:T(8,128)(2,1)}, bf16[1,128,2048]{2,1,0:T(8,128)(2,1)}) custom-call(s32[4]{0:T(128)} %get-tuple-element.174.refs_0_.refs_9_, bf16[8,128,2048]{2,1,0:T(8,128)(2,1)} %get-tuple-element.100.refs_1_.refs_3_, bf16[8,128,2048]{2,1,0:T(8,128)(2,1)} %collective-permute-done.15.refs_2_.refs_4_, bf16[2,128,2048]{2,1,0:T(8,128)(2,1)} %copy-done.23, ...), custom_call_target="tpu_custom_call" | custom-call | flops 3449999872 | bytes 1000 | tf_op jit(solution)/shard_map/end_sums/pallas_call | solution.py:864
  234.6 3.9 around_sums.1
  242.7 4.6 %collective-permute-done.28.refs_5_.refs_1_ = bf16[1,128,2048]{2,1,0:T(8,128)(2,1)S(1)} collective-permute-done((bf16[1,128,2048]{2,1,0:T(8,128)(2,1)}, bf16[1,128,2048]{2,1,0:T(8,128)(2,1)S(1)}, u32[]{:S(2)}, u32[]{:S(2)}) %collective-permute-start.28) | collective-permute-done | bytes 524320 | tf_op jit(solution)/shard_map/ppermute | solution.py:45
  253.5 4.3 %collective-permute-done.32.refs_3_ = bf16[64,2048]{1,0:T(8,128)(2,1)S(1)} collective-permute-done((bf16[64,2048]{1,0:T(8,128)(2,1)}, bf16[64,2048]{1,0:T(8,128)(2,1)S(1)}, u32[]{:S(2)}, u32[]{:S(2)}) %collective-permute-start.32) | collective-permute-done | bytes 262176 | tf_op jit(solution)/shard_map/ppermute | solution.py:45
  261.3 3.5 all-to-all-start.1
  286.9 4.1 passed_sums.3
  300.4 8.6 %collective-permute-done.35.refs_3_.refs_6_ = bf16[256,2048]{1,0:T(8,128)(2,1)S(1)} collective-permute-done((bf16[256,2048]{1,0:T(8,128)(2,1)}, bf16[256,2048]{1,0:T(8,128)(2,1)S(1)}, u32[]{:S(2)}, u32[]{:S(2)}) %collective-permute-start.35) | collective-permute-done | bytes 1048608 | tf_op jit(solution)/shard_map/ppermute | solution.py:45
  316.0 11.8 %collective-permute-done.43.refs_1_ = bf16[1,80,2048]{2,1,0:T(8,128)(2,1)S(1)} collective-permute-done((bf16[1,80,2048]{2,1,0:T(8,128)(2,1)}, bf16[1,80,2048]{2,1,0:T(8,128)(2,1)S(1)}, u32[]{:S(2)}, u32[]{:S(2)}) %collective-permute-start.43) | collective-permute-done | bytes 327712 | tf_op jit(solution)/shard_map/ppermute | solution.py:45
  328.6 5.8 %joined.2.refs_3_.refs_2_ = bf16[8,80,2048]{2,1,0:T(8,128)(2,1)} custom-call(bf16[6,80,2048]{2,1,0:T(8,128)(2,1)} %bitcast.64, bf16[1,80,2048]{2,1,0:T(8,128)(2,1)} %copy-done.47, bf16[1,80,2048]{2,1,0:T(8,128)(2,1)} %copy-done.48), custom_call_target="tpu_custom_call" | custom-call | flops 3449999872 | bytes 1000 | tf_op jit(solution)/shard_map/joined/pallas_call | solution.py:692
  336.3 3.6 halves.5
  339.9 8.7 %collective-permute-start.47 = (bf16[6,128,2048]{2,1,0:T(8,128)(2,1)}, bf16[6,128,2048]{2,1,0:T(8,128)(2,1)S(1)}, u32[]{:S(2)}, u32[]{:S(2)}) collective-permute-start(bf16[6,128,2048]{2,1,0:T(8,128)(2,1)} %bitcast.45), channel_id=1, source_target_pairs={{0,8},{1,9},{2,10},{3,11},{4,12},{5,13},{6,14},{7,15},{8,0},{9,1},... | collective-permute-start | bytes 9437192 | tf_op jit(solution)/shard_map/ppermute | solution.py:45
  352.5 5.4 %collective-permute-done.48.refs_3_ = bf16[8,80,2048]{2,1,0:T(8,128)(2,1)} collective-permute-done((bf16[8,80,2048]{2,1,0:T(8,128)(2,1)}, bf16[8,80,2048]{2,1,0:T(8,128)(2,1)}, u32[]{:S(2)}, u32[]{:S(2)}) %collective-permute-start.48) | collective-permute-done | bytes 2621472 | tf_op jit(solution)/shard_map/ppermute | solution.py:45
  357.8 8.3 %spread.3.refs_4_ = f32[1024,2048]{1,0:T(8,128)} custom-call(s32[8]{0:T(128)} %stack.71.refs_0_, s32[1]{0:T(128)} %bitcast.refs_1_, bf16[8,80,2048]{2,1,0:T(8,128)(2,1)} %joined.2.refs_3_.refs_2_, bf16[8,80,2048]{2,1,0:T(8,128)(2,1)} %collective-permute-done.48.refs_3_), custom_call_target="tpu_custom_call" | custom-call | flops 2760000000 | bytes 1000 | tf_op jit(solution)/shard_map/spread/pallas_call | solution.py:926
  367.8 8.8 %spread.4 = (f32[256,6144]{1,0:T(8,128)}, f32[256,8192]{1,0:T(8,128)}, f32[256,2048]{1,0:T(8,128)}) custom-call(s32[6]{0:T(128)} %stack.68.refs_0_, s32[1]{0:T(128)} %bitcast.refs_1_, bf16[6,128,2048]{2,1,0:T(8,128)(2,1)} %bitcast.46, bf16[6,128,2048]{2,1,0:T(8,128)(2,1)} %copy-done, f32[1024,2048]{1,0:T(8,128)} %spread.3.refs_4_), custom_call_target="tpu_custom_call" | custom-call | flops 2070000000 | bytes 1000 | tf_op jit(solution)/shard_map/spread/pallas_call | solution.py:926
  384.7 7.6 %collective-permute-done.23.refs_3_ = bf16[128,2048]{1,0:T(8,128)(2,1)S(1)} collective-permute-done((bf16[128,2048]{1,0:T(8,128)(2,1)S(1)}, bf16[128,2048]{1,0:T(8,128)(2,1)S(1)}, u32[]{:S(2)}, u32[]{:S(2)}) %collective-permute-start.23) | collective-permute-done | bytes 524320 | tf_op jit(solution)/shard_map/ppermute | solution.py:45
  392.3 11.2 %collective-permute-done.36.refs_7_ = bf16[128,2048]{1,0:T(8,128)(2,1)S(1)} collective-permute-done((bf16[128,2048]{1,0:T(8,128)(2,1)S(1)}, bf16[128,2048]{1,0:T(8,128)(2,1)S(1)}, u32[]{:S(2)}, u32[]{:S(2)}) %collective-permute-start.36) | collective-permute-done | bytes 524320 | tf_op jit(solution)/shard_map/ppermute | solution.py:45
  404.3 4.1 %finished.1 = (bf16[128,2048]{1,0:T(8,128)(2,1)}, f32[128,2048]{1,0:T(8,128)}) custom-call(bf16[128,2048]{1,0:T(8,128)(2,1)} %get-tuple-element.107.refs_24_.refs_0_, bf16[256,2048]{1,0:T(8,128)(2,1)} %copy-done.18, bf16[256,2048]{1,0:T(8,128)(2,1)} %copy-done.17, bf16[128,2048]{1,0:T(8,128)(2,1)} %copy-done.37, ...), custom_call_target="tpu_custom_call" | custom-call | flops 3449999872 | bytes 1000 | tf_op jit(solution)/shard_map/finished/pallas_call | solution.py:762
  409.4 4.0 spread.5
  (257 shorter events, 137.8 us)
Async XLA Ops:
  4.3 26.1 %collective-permute-start.1 = (bf16[2,128,2048]{2,1,0:T(8,128)(2,1)}, bf16[2,128,2048]{2,1,0:T(8,128)(2,1)}, u32[]{:S(2)}, u32[]{:S(2)}) collective-permute-start(bf16[2,128,2048]{2,1,0:T(8,128)(2,1)} %get-tuple-element.89.refs_14_.refs_22_.refs_13_.refs_1_), channel_id=1, source_target_pairs={{0,1},{1,2},{2,3},{3,0},{4,5},{5,6},{6,7},{7,4},{8,9},{9,10},{10,1... | collective-permute-start | bytes 3145736 | tf_op jit(solution)/shard_map/ppermute | solution.py:45
  6.3 26.0 %collective-permute-start.2 = (bf16[2,128,2048]{2,1,0:T(8,128)(2,1)}, bf16[2,128,2048]{2,1,0:T(8,128)(2,1)}, u32[]{:S(2)}, u32[]{:S(2)}) collective-permute-start(bf16[2,128,2048]{2,1,0:T(8,128)(2,1)} %get-tuple-element.89.refs_14_.refs_22_.refs_13_.refs_1_), channel_id=1, source_target_pairs={{0,4},{1,5},{2,6},{3,7},{4,0},{5,1},{6,2},{7,3},{8,12},{9,13},{10,... | collective-permute-start | bytes 3145736 | tf_op jit(solution)/shard_map/ppermute | solution.py:45
  8.0 36.2 %collective-permute-start = (bf16[2,128,2048]{2,1,0:T(8,128)(2,1)}, bf16[2,128,2048]{2,1,0:T(8,128)(2,1)}, u32[]{:S(2)}, u32[]{:S(2)}) collective-permute-start(bf16[2,128,2048]{2,1,0:T(8,128)(2,1)} %get-tuple-element.89.refs_14_.refs_22_.refs_13_.refs_1_), channel_id=1, source_target_pairs={{0,3},{1,0},{2,1},{3,2},{4,7},{5,4},{6,5},{7,6},{8,11},{9,8},{10,9... | collective-permute-start | bytes 3145736 | tf_op jit(solution)/shard_map/ppermute | solution.py:45
  9.4 34.8 %all-to-all-start = ((bf16[8,40,1792]{2,1,0:T(8,128)(2,1)}), bf16[8,40,1792]{2,1,0:T(8,128)(2,1)S(1)}, u32[]{:S(2)}, u32[]{:S(2)}) async-start(bf16[8,40,1792]{2,1,0:T(8,128)(2,1)} %get-tuple-element.88), calls=%async_computation | async-start | bytes 2293760 | tf_op jit(solution)/shard_map/all_to_all | solution.py:983
  30.3 38.1 %collective-permute-start.7 = (bf16[2,128,2048]{2,1,0:T(8,128)(2,1)}, bf16[2,128,2048]{2,1,0:T(8,128)(2,1)S(1)}, u32[]{:S(2)}, u32[]{:S(2)}) collective-permute-start(bf16[2,128,2048]{2,1,0:T(8,128)(2,1)} %collective-permute-done.1.refs_2_.refs_17_.refs_25_.refs_16_.refs_4_), channel_id=1, source_target_pairs={{0,4},{1,5},{2,6},{3,7},{4,0},{5,1},{6,2},{7,3},{8,12},{9,13},{10,... | collective-permute-start | bytes 3145736 | tf_op jit(solution)/shard_map/ppermute | solution.py:45
  32.3 36.1 %collective-permute-start.5 = (bf16[2,128,2048]{2,1,0:T(8,128)(2,1)}, bf16[2,128,2048]{2,1,0:T(8,128)(2,1)}, u32[]{:S(2)}, u32[]{:S(2)}) collective-permute-start(bf16[2,128,2048]{2,1,0:T(8,128)(2,1)} %collective-permute-done.1.refs_2_.refs_17_.refs_25_.refs_16_.refs_4_), channel_id=1, source_target_pairs={{0,1},{1,2},{2,3},{3,0},{4,5},{5,6},{6,7},{7,4},{8,9},{9,10},{10,1... | collective-permute-start | bytes 3145736 | tf_op jit(solution)/shard_map/ppermute | solution.py:45
  32.3 36.1 %collective-permute-start.6 = (bf16[2,128,2048]{2,1,0:T(8,128)(2,1)}, bf16[2,128,2048]{2,1,0:T(8,128)(2,1)S(1)}, u32[]{:S(2)}, u32[]{:S(2)}) collective-permute-start(bf16[2,128,2048]{2,1,0:T(8,128)(2,1)} %collective-permute-done.2.refs_3_.refs_18_.refs_26_.refs_17_.refs_5_), channel_id=1, source_target_pairs={{0,3},{1,0},{2,1},{3,2},{4,7},{5,4},{6,5},{7,6},{8,11},{9,8},{10,9... | collective-permute-start | bytes 3145736 | tf_op jit(solution)/shard_map/ppermute | solution.py:45
  47.6 20.8 %collective-permute-start.4 = (bf16[8,32,1792]{2,1,0:T(8,128)(2,1)}, bf16[8,32,1792]{2,1,0:T(8,128)(2,1)}, u32[]{:S(2)}, u32[]{:S(2)}) collective-permute-start(bf16[8,32,1792]{2,1,0:T(8,128)(2,1)} %get-tuple-element.91.refs_0_.refs_4_.refs_3_), channel_id=1, source_target_pairs={{0,32},{1,33},{2,34},{3,35},{4,36},{5,37},{6,38},{7,39},{8,40},{9,... | collective-permute-start | bytes 2752520 | tf_op jit(solution)/shard_map/ppermute | solution.py:45
  48.9 19.5 %collective-permute-start.3 = (bf16[8,32,1792]{2,1,0:T(8,128)(2,1)}, bf16[8,32,1792]{2,1,0:T(8,128)(2,1)}, u32[]{:S(2)}, u32[]{:S(2)}) collective-permute-start(bf16[8,32,1792]{2,1,0:T(8,128)(2,1)} %get-tuple-element.91.refs_0_.refs_4_.refs_3_), channel_id=1, source_target_pairs={{0,96},{1,97},{2,98},{3,99},{4,100},{5,101},{6,102},{7,103},{8,104... | collective-permute-start | bytes 2752520 | tf_op jit(solution)/shard_map/ppermute | solution.py:45
  72.9 28.4 %collective-permute-start.10 = (bf16[24,32,1792]{2,1,0:T(8,128)(2,1)}, bf16[24,32,1792]{2,1,0:T(8,128)(2,1)S(1)}, u32[]{:S(2)}, u32[]{:S(2)}) collective-permute-start(bf16[24,32,1792]{2,1,0:T(8,128)(2,1)} %bitcast.63), channel_id=1, source_target_pairs={{0,8},{1,9},{2,10},{3,11},{4,12},{5,13},{6,14},{7,15},{8,0},{9,1},... | collective-permute-start | bytes 8257544 | tf_op jit(solution)/shard_map/ppermute | solution.py:45
  81.3 19.9 %collective-permute-start.14 = (bf16[128,2048]{1,0:T(8,128)(2,1)S(1)}, bf16[128,2048]{1,0:T(8,128)(2,1)S(1)}, u32[]{:S(2)}, u32[]{:S(2)}) collective-permute-start(bf16[128,2048]{1,0:T(8,128)(2,1)S(1)} %slice_bitcast_fusion), channel_id=1, source_target_pairs={{0,3},{1,0},{2,1},{3,2},{4,7},{5,4},{6,5},{7,6},{8,11},{9,8},{10,9... | collective-permute-start | bytes 1572872 | tf_op jit(solution)/shard_map/ppermute | solution.py:45
  135.7 21.0 %collective-permute-start.15 = (bf16[8,128,2048]{2,1,0:T(8,128)(2,1)}, bf16[8,128,2048]{2,1,0:T(8,128)(2,1)}, u32[]{:S(2)}, u32[]{:S(2)}) collective-permute-start(bf16[8,128,2048]{2,1,0:T(8,128)(2,1)} %get-tuple-element.97.refs_25_), channel_id=1, source_target_pairs={{0,8},{1,9},{2,10},{3,11},{4,12},{5,13},{6,14},{7,15},{8,0},{9,1},... | collective-permute-start | bytes 12582920 | tf_op jit(solution)/shard_map/ppermute | solution.py:45
  160.0 17.2 %collective-permute-start.17 = (bf16[1,128,2048]{2,1,0:T(8,128)(2,1)}, bf16[1,128,2048]{2,1,0:T(8,128)(2,1)S(1)}, u32[]{:S(2)}, u32[]{:S(2)}) collective-permute-start(bf16[1,128,2048]{2,1,0:T(8,128)(2,1)} %get-tuple-element.101.refs_12_), channel_id=1, source_target_pairs={{0,32},{1,33},{2,34},{3,35},{4,36},{5,37},{6,38},{7,39},{8,40},{9,... | collective-permute-start | bytes 1572872 | tf_op jit(solution)/shard_map/ppermute | solution.py:45
  160.1 17.2 %collective-permute-start.18 = (bf16[1,128,2048]{2,1,0:T(8,128)(2,1)}, bf16[1,128,2048]{2,1,0:T(8,128)(2,1)S(1)}, u32[]{:S(2)}, u32[]{:S(2)}) collective-permute-start(bf16[1,128,2048]{2,1,0:T(8,128)(2,1)} %get-tuple-element.102.refs_13_), channel_id=1, source_target_pairs={{0,96},{1,97},{2,98},{3,99},{4,100},{5,101},{6,102},{7,103},{8,104... | collective-permute-start | bytes 1572872 | tf_op jit(solution)/shard_map/ppermute | solution.py:45
  183.6 44.3 %collective-permute-start.27 = (bf16[2,128,2048]{2,1,0:T(8,128)(2,1)}, bf16[2,128,2048]{2,1,0:T(8,128)(2,1)S(1)}, u32[]{:S(2)}, u32[]{:S(2)}) collective-permute-start(bf16[2,128,2048]{2,1,0:T(8,128)(2,1)} %get-tuple-element.106.refs_7_), channel_id=1, source_target_pairs={{0,96},{1,97},{2,98},{3,99},{4,100},{5,101},{6,102},{7,103},{8,104... | collective-permute-start | bytes 3145736 | tf_op jit(solution)/shard_map/ppermute | solution.py:45
  184.0 43.9 %collective-permute-start.26 = (bf16[2,128,2048]{2,1,0:T(8,128)(2,1)}, bf16[2,128,2048]{2,1,0:T(8,128)(2,1)S(1)}, u32[]{:S(2)}, u32[]{:S(2)}) collective-permute-start(bf16[2,128,2048]{2,1,0:T(8,128)(2,1)} %get-tuple-element.105.refs_3_.refs_6_), channel_id=1, source_target_pairs={{0,32},{1,33},{2,34},{3,35},{4,36},{5,37},{6,38},{7,39},{8,40},{9,... | collective-permute-start | bytes 3145736 | tf_op jit(solution)/shard_map/ppermute | solution.py:45
  189.8 43.8 %collective-permute-start.29 = (bf16[4,64,2048]{2,1,0:T(8,128)(2,1)}, bf16[4,64,2048]{2,1,0:T(8,128)(2,1)S(1)}, u32[]{:S(2)}, u32[]{:S(2)}) collective-permute-start(bf16[4,64,2048]{2,1,0:T(8,128)(2,1)} %away_sums.1.refs_5_), channel_id=1, source_target_pairs={{0,16},{1,17},{2,18},{3,19},{4,20},{5,21},{6,22},{7,23},{8,24},{9,... | collective-permute-start | bytes 3145736 | tf_op jit(solution)/shard_map/ppermute | solution.py:45
  202.4 20.5 %collective-permute-start.19 = (bf16[128,2048]{1,0:T(8,128)(2,1)}, bf16[128,2048]{1,0:T(8,128)(2,1)S(1)}, u32[]{:S(2)}, u32[]{:S(2)}) collective-permute-start(bf16[128,2048]{1,0:T(8,128)(2,1)} %get-tuple-element.109), channel_id=1, source_target_pairs={{0,1},{1,2},{2,3},{3,0},{4,5},{5,6},{6,7},{7,4},{8,9},{9,10},{10,1... | collective-permute-start | bytes 1572872 | tf_op jit(solution)/shard_map/ppermute | solution.py:45
  202.5 20.5 %collective-permute-start.20 = (bf16[128,2048]{1,0:T(8,128)(2,1)}, bf16[128,2048]{1,0:T(8,128)(2,1)S(1)}, u32[]{:S(2)}, u32[]{:S(2)}) collective-permute-start(bf16[128,2048]{1,0:T(8,128)(2,1)} %get-tuple-element.112), channel_id=1, source_target_pairs={{0,3},{1,0},{2,1},{3,2},{4,7},{5,4},{6,5},{7,6},{8,11},{9,8},{10,9... | collective-permute-start | bytes 1572872 | tf_op jit(solution)/shard_map/ppermute | solution.py:45
  241.2 23.6 %collective-permute-start.22 = (bf16[256,2048]{1,0:T(8,128)(2,1)}, bf16[256,2048]{1,0:T(8,128)(2,1)S(1)}, u32[]{:S(2)}, u32[]{:S(2)}) collective-permute-start(bf16[256,2048]{1,0:T(8,128)(2,1)} %get-tuple-element.119), channel_id=1, source_target_pairs={{0,3},{1,0},{2,1},{3,2},{4,7},{5,4},{6,5},{7,6},{8,11},{9,8},{10,9... | collective-permute-start | bytes 3145736 | tf_op jit(solution)/shard_map/ppermute | solution.py:45
  241.2 24.1 %collective-permute-start.21 = (bf16[256,2048]{1,0:T(8,128)(2,1)}, bf16[256,2048]{1,0:T(8,128)(2,1)S(1)}, u32[]{:S(2)}, u32[]{:S(2)}) collective-permute-start(bf16[256,2048]{1,0:T(8,128)(2,1)} %get-tuple-element.118.refs_5_), channel_id=1, source_target_pairs={{0,1},{1,2},{2,3},{3,0},{4,5},{5,6},{6,7},{7,4},{8,9},{9,10},{10,1... | collective-permute-start | bytes 3145736 | tf_op jit(solution)/shard_map/ppermute | solution.py:45
  291.0 17.9 %collective-permute-start.35 = (bf16[256,2048]{1,0:T(8,128)(2,1)}, bf16[256,2048]{1,0:T(8,128)(2,1)S(1)}, u32[]{:S(2)}, u32[]{:S(2)}) collective-permute-start(bf16[256,2048]{1,0:T(8,128)(2,1)} %get-tuple-element.142), channel_id=1, source_target_pairs={{0,3},{1,0},{2,1},{3,2},{4,7},{5,4},{6,5},{7,6},{8,11},{9,8},{10,9... | collective-permute-start | bytes 3145736 | tf_op jit(solution)/shard_map/ppermute | solution.py:45
  293.5 18.4 %collective-permute-start.34 = (bf16[256,2048]{1,0:T(8,128)(2,1)}, bf16[256,2048]{1,0:T(8,128)(2,1)S(1)}, u32[]{:S(2)}, u32[]{:S(2)}) collective-permute-start(bf16[256,2048]{1,0:T(8,128)(2,1)} %get-tuple-element.141.refs_3_), channel_id=1, source_target_pairs={{0,1},{1,2},{2,3},{3,0},{4,5},{5,6},{6,7},{7,4},{8,9},{9,10},{10,1... | collective-permute-start | bytes 3145736 | tf_op jit(solution)/shard_map/ppermute | solution.py:45
  294.4 40.0 %collective-permute-start.39 = (bf16[2,128,2048]{2,1,0:T(8,128)(2,1)S(1)}, bf16[2,128,2048]{2,1,0:T(8,128)(2,1)S(1)}, u32[]{:S(2)}, u32[]{:S(2)}) collective-permute-start(bf16[2,128,2048]{2,1,0:T(8,128)(2,1)S(1)} %constant_dynamic-update-slice_fusion.refs_0_), channel_id=1, source_target_pairs={{0,96},{1,97},{2,98},{3,99},{4,100},{5,101},{6,102},{7,103},{8,104... | collective-permute-start | bytes 3145736 | tf_op jit(solution)/shard_map/ppermute | solution.py:45
  295.7 38.7 %collective-permute-start.38 = (bf16[2,128,2048]{2,1,0:T(8,128)(2,1)S(1)}, bf16[2,128,2048]{2,1,0:T(8,128)(2,1)S(1)}, u32[]{:S(2)}, u32[]{:S(2)}) collective-permute-start(bf16[2,128,2048]{2,1,0:T(8,128)(2,1)S(1)} %constant_dynamic-update-slice_fusion.refs_0_), channel_id=1, source_target_pairs={{0,32},{1,33},{2,34},{3,35},{4,36},{5,37},{6,38},{7,39},{8,40},{9,... | collective-permute-start | bytes 3145736 | tf_op jit(solution)/shard_map/ppermute | solution.py:45
  300.2 27.6 %collective-permute-start.43 = (bf16[1,80,2048]{2,1,0:T(8,128)(2,1)}, bf16[1,80,2048]{2,1,0:T(8,128)(2,1)S(1)}, u32[]{:S(2)}, u32[]{:S(2)}) collective-permute-start(bf16[1,80,2048]{2,1,0:T(8,128)(2,1)} %get-tuple-element.149), channel_id=1, source_target_pairs={{0,32},{1,33},{2,34},{3,35},{4,36},{5,37},{6,38},{7,39},{8,40},{9,... | collective-permute-start | bytes 983048 | tf_op jit(solution)/shard_map/ppermute | solution.py:45
  308.9 18.9 %collective-permute-start.44 = (bf16[1,80,2048]{2,1,0:T(8,128)(2,1)}, bf16[1,80,2048]{2,1,0:T(8,128)(2,1)S(1)}, u32[]{:S(2)}, u32[]{:S(2)}) collective-permute-start(bf16[1,80,2048]{2,1,0:T(8,128)(2,1)} %get-tuple-element.150), channel_id=1, source_target_pairs={{0,96},{1,97},{2,98},{3,99},{4,100},{5,101},{6,102},{7,103},{8,104... | collective-permute-start | bytes 983048 | tf_op jit(solution)/shard_map/ppermute | solution.py:45
  339.9 26.3 %collective-permute-start.47 = (bf16[6,128,2048]{2,1,0:T(8,128)(2,1)}, bf16[6,128,2048]{2,1,0:T(8,128)(2,1)S(1)}, u32[]{:S(2)}, u32[]{:S(2)}) collective-permute-start(bf16[6,128,2048]{2,1,0:T(8,128)(2,1)} %bitcast.45), channel_id=1, source_target_pairs={{0,8},{1,9},{2,10},{3,11},{4,12},{5,13},{6,14},{7,15},{8,0},{9,1},... | collective-permute-start | bytes 9437192 | tf_op jit(solution)/shard_map/ppermute | solution.py:45
  348.6 28.0 %collective-permute-start.45 = (bf16[1,128,2048]{2,1,0:T(8,128)(2,1)}, bf16[1,128,2048]{2,1,0:T(8,128)(2,1)}, u32[]{:S(2)}, u32[]{:S(2)}) collective-permute-start(bf16[1,128,2048]{2,1,0:T(8,128)(2,1)} %get-tuple-element.151), channel_id=1, source_target_pairs={{0,32},{1,33},{2,34},{3,35},{4,36},{5,37},{6,38},{7,39},{8,40},{9,... | collective-permute-start | bytes 1572872 | tf_op jit(solution)/shard_map/ppermute | solution.py:45
  348.6 28.0 %collective-permute-start.46 = (bf16[1,128,2048]{2,1,0:T(8,128)(2,1)}, bf16[1,128,2048]{2,1,0:T(8,128)(2,1)}, u32[]{:S(2)}, u32[]{:S(2)}) collective-permute-start(bf16[1,128,2048]{2,1,0:T(8,128)(2,1)} %get-tuple-element.152), channel_id=1, source_target_pairs={{0,96},{1,97},{2,98},{3,99},{4,100},{5,101},{6,102},{7,103},{8,104... | collective-permute-start | bytes 1572872 | tf_op jit(solution)/shard_map/ppermute | solution.py:45
  378.9 29.5 %collective-permute-start.49 = (bf16[2,128,2048]{2,1,0:T(8,128)(2,1)}, bf16[2,128,2048]{2,1,0:T(8,128)(2,1)S(1)}, u32[]{:S(2)}, u32[]{:S(2)}) collective-permute-start(bf16[2,128,2048]{2,1,0:T(8,128)(2,1)} %joined.3.refs_10_.refs_2_), channel_id=1, source_target_pairs={{0,8},{1,9},{2,10},{3,11},{4,12},{5,13},{6,14},{7,15},{8,0},{9,1},... | collective-permute-start | bytes 3145736 | tf_op jit(solution)/shard_map/ppermute | solution.py:45
  379.4 24.2 %collective-permute-start.36 = (bf16[128,2048]{1,0:T(8,128)(2,1)S(1)}, bf16[128,2048]{1,0:T(8,128)(2,1)S(1)}, u32[]{:S(2)}, u32[]{:S(2)}) collective-permute-start(bf16[128,2048]{1,0:T(8,128)(2,1)S(1)} %copy-done.30), channel_id=1, source_target_pairs={{0,4},{1,5},{2,6},{3,7},{4,0},{5,1},{6,2},{7,3},{8,12},{9,13},{10,... | collective-permute-start | bytes 1572872 | tf_op jit(solution)/shard_map/ppermute | solution.py:45
  (73 other events, 501.2 us)

commit v9 on v8

--- a/solution.py
+++ b/solution.py
@@ -779,7 +779,7 @@
 
     def body(*refs):
         stay_ref, cross_ref, own_ref, below_ref, above_ref = refs[:5]
-        norm_ref, q_ref, u_ref, y_ref, number_ref, out_ref, lanes_ref, keep_ref, small = refs[5:]
+        norm_ref, q_ref, u_ref, y_ref, number_ref, out_ref, keep_ref, small = refs[5:]
         shard = number_ref[1]
         inner = (stay_ref[0].astype(f32) + cross_ref[0].astype(f32)).astype(bf16)
         total = wide(own_ref, below_ref, above_ref).astype(bf16)
@@ -803,19 +803,18 @@
             pieces.append(inner[row : row + 16, col : col + ff])
             pieces.append(small[...].astype(bf16))
             out_ref[owner] = jnp.concatenate(pieces, 1)
-            lanes_ref[owner] = total[48:64, owner * head : (owner + 1) * head]
-        keep_ref[...] = inner[0:64]
+        keep_ref[0:64] = inner[0:64]
+        keep_ref[64:80] = total[48:64]
 
     vmem = pl.BlockSpec(memory_space=pltpu.VMEM)
     return pl.pallas_call(
         after_inputs(body, 10, len(after)),
         out_shape=(
             jax.ShapeDtypeStruct((8, 16, 4 * head + ff), bf16),
-            jax.ShapeDtypeStruct((8, 16, width // 8), bf16),
-            jax.ShapeDtypeStruct((64, width), bf16),
+            jax.ShapeDtypeStruct((80, width), bf16),
         ),
         in_specs=[vmem] * 9 + [pl.BlockSpec(memory_space=pltpu.SMEM)] + anywhere(len(after)),
-        out_specs=(vmem,) * 3,
+        out_specs=(vmem,) * 2,
         scratch_shapes=[pltpu.VMEM((16, head), f32)],
         compiler_params=kernel_params(),
         cost_estimate=cost(3),
@@ -823,37 +822,27 @@
     )(stays, crossed, own, below, above, norm_sums, qkv_sums, up_sums, dy_sums, numbers, *after)
 
 
-def unpacked_sums(received, outs, downs, after):
+def unpacked_sums(received, cols, after):
     sources, rows, width = received.shape
-    cols = width - outs.shape[2]
-
-    def body(part_ref, outs_ref, down_ref, part_out, down_out):
-        part_out[0] = jnp.concatenate(
-            [
-                jnp.concatenate([part_ref[n, :, 0:cols], outs_ref[n]], 1)
-                for n in range(sources)
-            ],
+
+    def body(part_ref, out_ref):
+        small = jnp.sum(part_ref[:, :, cols:].astype(f32), 0).astype(bf16)
+        out_ref[0] = jnp.concatenate(
+            [jnp.concatenate([part_ref[0, :, 0:cols], small], 1)]
+            + [part_ref[n] for n in range(1, sources)],
             0,
         )
-        small = jnp.sum(part_ref[:, :, cols:].astype(f32), 0).astype(bf16)
-        down_out[0, 0:64] = down_ref[...]
-        down_out[0, 64 : 64 + rows] = jnp.concatenate(
-            [small, jnp.zeros((rows, cols), bf16)], 1
-        )
 
     vmem = pl.BlockSpec(memory_space=pltpu.VMEM)
     return pl.pallas_call(
-        after_inputs(body, 3, len(after)),
-        out_shape=(
-            jax.ShapeDtypeStruct((1, sources * rows, width), bf16),
-            jax.ShapeDtypeStruct((1, 64 + rows, width), bf16),
-        ),
-        in_specs=[vmem] * 3 + anywhere(len(after)),
-        out_specs=(vmem,) * 2,
+        after_inputs(body, 1, len(after)),
+        out_shape=jax.ShapeDtypeStruct((1, sources * rows, width), bf16),
+        in_specs=[vmem] + anywhere(len(after)),
+        out_specs=vmem,
         compiler_params=kernel_params(),
         cost_estimate=cost(3),
         name="unpacked_sums",
-    )(received, outs, downs, *after)
+    )(received, *after)
 
 
 def blocks_call(name, body, numbers, terms, outs, after, time=3):
@@ -1129,14 +1118,17 @@
         down_out[0:128] = wide(down_ref, from_above).astype(bf16)
         down_out[128:256] = there_ref[...]
 
-    def other_body(n_ref, own_ref, below_ref, above_ref, out_ref):
-        out_ref[...] = wide(own_ref, below_ref, above_ref).astype(bf16)
+    def other_body(n_ref, own_ref, below_ref, above_ref, *refs):
+        passing = len(refs) // 2
+        refs[passing][...] = wide(own_ref, below_ref, above_ref).astype(bf16)
+        for at in range(passing):
+            refs[passing + 1 + at][...] = refs[at][...]
 
     def first(n):
         return 0
 
-    def ring_start(pieces):
-        return move(pieces[6], x=1), move(pieces[2], x=-1)
+    def ring_start(high, low):
+        return move(high, x=1), move(low, x=-1)
 
     def ring_middle(pieces, passed, after):
         operands = (pieces[5], passed[0], pieces[1], pieces[3], passed[1], pieces[7])
@@ -1150,8 +1142,8 @@
         )
         return (move(ups, x=1), move(downs, x=-1)), ups
 
-    def ring_end(pieces, arrived, after):
-        (other,) = blocks_call(
+    def ring_end(pieces, arrived, passing):
+        other, *copies = blocks_call(
             "other_sums",
             other_body,
             numbers,
@@ -1159,13 +1151,14 @@
                 (pieces[4], flat, first),
                 (arrived[0], flat, first),
                 (arrived[1], flat, lambda n: 1),
-            ],
-            (flat,),
-            after,
+            ]
+            + [(v, flat, first) for v in passing],
+            (flat,) * (1 + len(passing)),
+            (),
         )
-        return (pieces[0], *arrived, move(other, l=1)), other
-
-    mix_passed = ring_start(mix)
+        return (pieces[0], *arrived, move(other, l=1)), other, *copies
+
+    mix_passed = ring_start(mix[6], mix[2])
     mix_arrived, mix_ups = ring_middle(mix, mix_passed, (norm_sums,))
 
     def ends_body(n_ref, keep_ref, got_ref, below_ref, above_ref, leave_ref, stay_ref):
@@ -1223,7 +1216,7 @@
     )
     a_from_below, a_from_above = move(a_above, y=1), move(a_below, y=-1)
 
-    part, outs, downs = packed_sums(
+    part, stays = packed_sums(
         stays,
         crossed,
         a_own,
@@ -1239,9 +1232,9 @@
         (),
     )
     received = lax.all_to_all(part, "shard", 0, 0)
-    mix_left, mix_other = ring_end(mix, mix_arrived, ())
-    part, downs = unpacked_sums(received, outs, downs, (mix_other,))
-    sums_arrived, sums_ups = ring_middle(sums, ring_start(sums), (received,))
+    mix_left, mix_other, high, low = ring_end(mix, mix_arrived, (sums[6], sums[2]))
+    part = unpacked_sums(received, cols, (mix_other,))
+    sums_arrived, sums_ups = ring_middle(sums, ring_start(high, low), (received,))
     sums_left, sums_other = ring_end(sums, sums_arrived, ())
 
     order = ((0, h), (0, 1 - h), (1, h), (1, 1 - h), (3, h), (3, 1 - h), (2, h), (2, 1 - h))
@@ -1253,19 +1246,18 @@
         low, high, near = halves(own, below, above, after)
         return near, (move(low, y=1), move(high, y=-1))
 
-    near, far = rep_gather(downs, (sums_ups,))
-    downs_all = joined((near, *far), ())
-    downs_yours = move(downs_all, c=1)
-    (down_grad,) = spread(
-        [(downs_all, downs_yours)],
+    near, far = rep_gather(stays[None], ())
+    stays = joined((near, *far), ())
+    down_grad, out_grad = spread(
+        [(stays, move(stays, c=1))],
         places,
         numbers[:1],
-        [(width, 64, [(0, 0, 0, width)])],
+        [(width, 64, [(0, 0, 0, width)]), (width, 16, [(0, 64, 0, width)])],
         8,
         (),
-        (),
-    )
-    near, far = rep_gather(part, (downs_all, sums_other))
+        (mix_left[3],),
+    )
+    near, far = rep_gather(part, (stays, sums_other, mix_left[3]))
     targets = [
         (
             3 * width,
@@ -1277,13 +1269,16 @@
             ],
         ),
         (8 * ff, 16, [(source * ff, 16 * source, 3 * head, ff) for source in range(8)]),
-        (width, 16, [(source * head, 16 * source, cols, head) for source in range(8)]),
     ]
-    grads = spread([(near, move(near, c=1))], places[:6], numbers[:1], targets, 8, (), (down_grad,))
+    near_yours = move(near, c=1)
+    grads = spread(
+        [(near, near_yours)], places[:6], numbers[:1], targets, 8, (), (down_grad, sums_left[3])
+    )
     far = joined(far, (grads[0],))
     mixed, tokens_grad = finished(mix_left, sums_left, tokens, cotangent, (far,))
-    qkv_grad, up_grad, out_grad = spread(
-        [(far, move(far, c=1))],
+    far_yours = move(far, c=1)
+    qkv_grad, up_grad = spread(
+        [(far, far_yours)],
         places[6:],
         numbers[:1],
         targets,
@@ -1291,8 +1286,8 @@
         grads,
         (tokens_grad,),
     )
-    smalls = jnp.concatenate([downs_all[:, 64:80, 0:head], downs_yours[:, 64:80, 0:head]])
-    smalls = jnp.sum(smalls.astype(f32), 0)
+    smalls = [v[:, 0:16, cols:] for v in (near, near_yours, far, far_yours)]
+    smalls = jnp.sum(jnp.concatenate(smalls).astype(f32), 0)
     norm_grads = smalls[:4]
     dy_total = smalls[11]
     return (

time: 421 us -> 404 us (0.960)
  waiting for transfers between devices: 114 us -> 96.4 us
    ppermute x50, waiting for transfers between devices: 102 us -> 87.2 us  [move(): return lax.ppermute(value, BOTH, pairs)]
    unnamed x115 -> x107, local copies, waits for them, and re-layouts: 25.9 us -> 24 us
  transfers between devices with their start and end apart: 52 -> 52, of which waited for: 18 -> 13; matrix products, arithmetic and copies ran while one was open for 5% -> 4% of each run, Pallas kernels for 30% -> 32%
where the time goes in v9:
time: 404 us; the launch traced here: 398 us
  Pallas kernels  180 us (45%)
  waiting for transfers between devices  96.4 us (24%)
  starting transfers between devices  78 us (19%)
  local copies, waits for them, and re-layouts  34.1 us (8%)
  other arithmetic  7.35 us (2%)
    ppermute x50, waiting for transfers between devices, move(): return lax.ppermute(value, BOTH, pairs)  87.2 us
    ppermute x50, starting transfers between devices, move(): return lax.ppermute(value, BOTH, pairs)  71 us
    pallas_call x10, Pallas kernels, blocks_call(): pl.pallas_call(after_inputs(body, 1 + len(terms), len(after)), out_shape=...  36.7 us
    pallas_call x1, Pallas kernels, feed_forward(): pl.pallas_call(after_inputs(body, 5 + parts + 2 * count, len(after)), out...  32.2 us
    unnamed x107, local copies, waits for them, and re-layouts  24 us
    pallas_call x3, Pallas kernels, spread(): pl.pallas_call(after_inputs(body, 2 + 2 * len(pieces) + len(before), len(...  21 us
    pallas_call x1, Pallas kernels, back_norms(): pl.pallas_call(after_inputs(body, 6 + parts + count, len(after)), out_sha...  17.8 us
    pallas_call x1, Pallas kernels, attend(): pl.pallas_call(after_inputs(body, 7 + parts + count, len(after)), out_sha...  17.2 us
  transfers between devices with their start and end apart: 52, of which 13 were waited for; matrix products, arithmetic and copies ran while one was open for 4% of the time, Pallas kernels for 32%

profile of v9, /device:TPU:1, one launch (start us, length us, event | category | flops | bytes accessed | tf_op | source)
XLA Modules:
  0.0 397.9 jit_solution(13910108921716528882)
XLA Ops:
  0.7 3.6 packed.1
  9.4 3.6 all-to-all-start
  13.0 17.3 %collective-permute-done.1.refs_2_.refs_17_.refs_25_.refs_16_.refs_4_ = bf16[2,128,2048]{2,1,0:T(8,128)(2,1)} collective-permute-done((bf16[2,128,2048]{2,1,0:T(8,128)(2,1)}, bf16[2,128,2048]{2,1,0:T(8,128)(2,1)}, u32[]{:S(2)}, u32[]{:S(2)}) %collective-permute-start.1) | collective-permute-done | bytes 1048608 | tf_op jit(solution)/shard_map/ppermute | solution.py:45
  35.0 9.2 %all-to-all-done.refs_0_ = bf16[8,40,1792]{2,1,0:T(8,128)(2,1)S(1)} async-done(((bf16[8,40,1792]{2,1,0:T(8,128)(2,1)}), bf16[8,40,1792]{2,1,0:T(8,128)(2,1)S(1)}, u32[]{:S(2)}, u32[]{:S(2)}) %all-to-all-start) | async-done | bytes 1146912 | tf_op jit(solution)/shard_map/all_to_all | solution.py:972
  51.6 16.1 %collective-permute-done.3.refs_2_.refs_5_.refs_4_ = bf16[8,32,1792]{2,1,0:T(8,128)(2,1)S(1)} collective-permute-done((bf16[8,32,1792]{2,1,0:T(8,128)(2,1)}, bf16[8,32,1792]{2,1,0:T(8,128)(2,1)S(1)}, u32[]{:S(2)}, u32[]{:S(2)}) %collective-permute-start.3) | collective-permute-done | bytes 917536 | tf_op jit(solution)/shard_map/ppermute | solution.py:45
  76.0 3.9 collective-permute-start.10
  91.4 5.2 %collective-permute-done.8.refs_6_.refs_5_ = bf16[4,32,1792]{2,1,0:T(8,128)(2,1)S(1)} collective-permute-done((bf16[4,32,1792]{2,1,0:T(8,128)(2,1)}, bf16[4,32,1792]{2,1,0:T(8,128)(2,1)S(1)}, u32[]{:S(2)}, u32[]{:S(2)}) %collective-permute-start.8) | collective-permute-done | bytes 458784 | tf_op jit(solution)/shard_map/ppermute | solution.py:45
  103.9 32.2 %feed_forward.1 = (bf16[1024,2048]{1,0:T(8,128)(2,1)}, bf16[1024,1024]{1,0:T(8,128)(2,1)}, bf16[1024,1024]{1,0:T(8,128)(2,1)}, bf16[8,128,2048]{2,1,0:T(8,128)(2...) custom-call(s32[4]{0:T(128)} %get-tuple-element.174.refs_0_.refs_9_,, ...), custom_call_target="tpu_custom_call" | custom-call | flops 36800000000 | bytes 1000 | tf_op jit(solution)/shard_map/feed_forward/pallas_call | solution.py:243
  140.2 17.2 %attend.1 = (bf16[1024,256]{1,0:T(8,128)(2,1)}, bf16[1024,768]{1,0:T(8,128)(2,1)}, f32[1,768]{1,0:T(1,128)}) custom-call(s32[8,3]{1,0:T(8,128)} %copy-done.10, s32[8]{0:T(128)} %pad_add_fusion.1.refs_1_.refs_0_, f32[3,1,256]{2,1,0:T(1,128)} %pad_maximum_fusion.3.refs_2_, bf16[8,32,1792]{2,1,0:T(8,128)(2,1)} %get-tuple-element.91.refs_0_.refs_4_.refs_3_, ...), custom_call_target="tpu_custom_call" | custom-call | flops 19549999104 | bytes 1000 | tf_op jit(solution)/shard_map/attend/pallas_call | solution.py:416
  163.4 13.8 %attention_grads.1 = (bf16[8,64,2048]{2,1,0:T(8,128)(2,1)}, bf16[8,64,2048]{2,1,0:T(8,128)(2,1)}) custom-call(s32[4]{0:T(128)} %get-tuple-element.174.refs_0_.refs_9_, bf16[2,128,2048]{2,1,0:T(8,128)(2,1)} %get-tuple-element.89.refs_14_.refs_22_.refs_13_.refs_1_, bf16[2,128,2048]{2,1,0:T(8,128)(2,1)} %collective-permute-done.refs_1_.refs_15_.refs_23_.refs_14_.refs_2_, ...), custom_call_target="tpu_custom_call" | custom-call | flops 13799999488 | bytes 1000 | tf_op jit(solution)/shard_map/attention_grads/pallas_call | solution.py:513
  179.7 4.7 %near_sums.1 = (bf16[2,128,2048]{2,1,0:T(8,128)(2,1)}, bf16[2,128,2048]{2,1,0:T(8,128)(2,1)}) custom-call(s32[4]{0:T(128)} %get-tuple-element.174.refs_0_.refs_9_, bf16[8,128,2048]{2,1,0:T(8,128)(2,1)} %get-tuple-element.100.refs_1_.refs_3_, bf16[8,128,2048]{2,1,0:T(8,128)(2,1)} %collective-permute-done.15.refs_2_.refs_4_, ...), custom_call_target="tpu_custom_call" | custom-call | flops 23000000512 | bytes 1000 | tf_op jit(solution)/shard_map/near_sums/pallas_call | solution.py:853
  195.1 9.3 %mixed_part.1 = (bf16[128,2048]{1,0:T(8,128)(2,1)}, bf16[128,2048]{1,0:T(8,128)(2,1)}, bf16[128,2048]{1,0:T(8,128)(2,1)}, bf16[128,2048]{1,0:T(8,128)(2,1)}, bf1...) custom-call(bf16[1024,1024]{1,0:T(8,128)(2,1)} %get-tuple-element.95., ...), custom_call_target="tpu_custom_call" | custom-call | flops 11500000256 | bytes 1000 | tf_op jit(solution)/shard_map/mixed_part/pallas_call | solution.py:545
  207.3 17.8 %back_norms.1 = (f32[4,2048]{1,0:T(4,128)}, bf16[128,2048]{1,0:T(8,128)(2,1)}, bf16[128,2048]{1,0:T(8,128)(2,1)}, bf16[128,2048]{1,0:T(8,128)(2,1)}, bf16[128,20...) custom-call(s32[8]{0:T(128)} %pad_add_fusion.1.refs_1_.refs_0_, ...), custom_call_target="tpu_custom_call" | custom-call | flops 17250000896 | bytes 1000 | tf_op jit(solution)/shard_map/back_norms/pallas_call | solution.py:617
  226.1 3.9 passed_sums.2
  231.3 4.4 %end_sums.1 = (bf16[1,128,2048]{2,1,0:T(8,128)(2,1)}, bf16[1,128,2048]{2,1,0:T(8,128)(2,1)}) custom-call(s32[4]{0:T(128)} %get-tuple-element.174.refs_0_.refs_9_, bf16[8,128,2048]{2,1,0:T(8,128)(2,1)} %get-tuple-element.100.refs_1_.refs_3_, bf16[8,128,2048]{2,1,0:T(8,128)(2,1)} %collective-permute-done.15.refs_2_.refs_4_, bf16[2,128,2048]{2,1,0:T(8,128)(2,1)} %copy-done.22, ...), custom_call_target="tpu_custom_call" | custom-call | flops 3449999872 | bytes 1000 | tf_op jit(solution)/shard_map/end_sums/pallas_call | solution.py:853
  239.3 3.8 around_sums.1
  245.8 3.7 collective-permute-done.28.refs_5_.refs_1_
  255.6 4.3 %collective-permute-done.32.refs_3_ = bf16[64,2048]{1,0:T(8,128)(2,1)S(1)} collective-permute-done((bf16[64,2048]{1,0:T(8,128)(2,1)}, bf16[64,2048]{1,0:T(8,128)(2,1)S(1)}, u32[]{:S(2)}, u32[]{:S(2)}) %collective-permute-start.32) | collective-permute-done | bytes 262176 | tf_op jit(solution)/shard_map/ppermute | solution.py:45
  265.5 3.5 all-to-all-start.1
  269.9 3.6 other_sums.2
  283.1 6.6 %collective-permute-done.24.refs_2_ = bf16[128,2048]{1,0:T(8,128)(2,1)S(1)} collective-permute-done((bf16[128,2048]{1,0:T(8,128)(2,1)}, bf16[128,2048]{1,0:T(8,128)(2,1)S(1)}, u32[]{:S(2)}, u32[]{:S(2)}) %collective-permute-start.24) | collective-permute-done | bytes 524320 | tf_op jit(solution)/shard_map/ppermute | solution.py:45
  290.6 3.9 passed_sums.3
  305.5 4.0 collective-permute-done.43.refs_1_
  310.7 20.9 %collective-permute-done.44.refs_2_ = bf16[1,80,2048]{2,1,0:T(8,128)(2,1)S(1)} collective-permute-done((bf16[1,80,2048]{2,1,0:T(8,128)(2,1)}, bf16[1,80,2048]{2,1,0:T(8,128)(2,1)S(1)}, u32[]{:S(2)}, u32[]{:S(2)}) %collective-permute-start.44) | collective-permute-done | bytes 327712 | tf_op jit(solution)/shard_map/ppermute | solution.py:45
  332.4 5.7 %joined.2.refs_3_.refs_2_ = bf16[8,80,2048]{2,1,0:T(8,128)(2,1)} custom-call(bf16[6,80,2048]{2,1,0:T(8,128)(2,1)} %bitcast.68, bf16[1,80,2048]{2,1,0:T(8,128)(2,1)} %copy-done.44, bf16[1,80,2048]{2,1,0:T(8,128)(2,1)} %copy-done.45), custom_call_target="tpu_custom_call" | custom-call | flops 3449999872 | bytes 1000 | tf_op jit(solution)/shard_map/joined/pallas_call | solution.py:692
  344.6 3.5 halves.5
  348.1 5.4 %collective-permute-start.47 = (bf16[6,128,2048]{2,1,0:T(8,128)(2,1)}, bf16[6,128,2048]{2,1,0:T(8,128)(2,1)S(1)}, u32[]{:S(2)}, u32[]{:S(2)}) collective-permute-start(bf16[6,128,2048]{2,1,0:T(8,128)(2,1)} %bitcast.46), channel_id=1, source_target_pairs={{0,8},{1,9},{2,10},{3,11},{4,12},{5,13},{6,14},{7,15},{8,0},{9,1},... | collective-permute-start | bytes 9437192 | tf_op jit(solution)/shard_map/ppermute | solution.py:45
  357.9 4.8 %collective-permute-done.48.refs_3_ = bf16[8,80,2048]{2,1,0:T(8,128)(2,1)} collective-permute-done((bf16[8,80,2048]{2,1,0:T(8,128)(2,1)}, bf16[8,80,2048]{2,1,0:T(8,128)(2,1)}, u32[]{:S(2)}, u32[]{:S(2)}) %collective-permute-start.48) | collective-permute-done | bytes 2621472 | tf_op jit(solution)/shard_map/ppermute | solution.py:45
  362.7 8.7 %spread.3 = (f32[1024,2048]{1,0:T(8,128)}, f32[256,2048]{1,0:T(8,128)}) custom-call(s32[8]{0:T(128)} %stack.71.refs_0_, s32[1]{0:T(128)} %bitcast.refs_1_, bf16[8,80,2048]{2,1,0:T(8,128)(2,1)} %joined.2.refs_3_.refs_2_, bf16[8,80,2048]{2,1,0:T(8,128)(2,1)} %collective-permute-done.48.refs_3_, bf16[128,2048]{1,0:T(8,128)(2,1)} %copy-done.30), custom_call_target="tpu_custom_call" | custom-call | flops 2760000000 | bytes 1000 | tf_op jit(solution)/shard_map/spread/pallas_call | solution.py:915
  373.1 8.5 %spread.4 = (f32[256,6144]{1,0:T(8,128)}, f32[256,8192]{1,0:T(8,128)}) custom-call(s32[6]{0:T(128)} %stack.68.refs_0_, s32[1]{0:T(128)} %bitcast.refs_1_, bf16[6,128,2048]{2,1,0:T(8,128)(2,1)} %bitcast.47, bf16[6,128,2048]{2,1,0:T(8,128)(2,1)} %copy-done, f32[1024,2048]{1,0:T(8,128)} %get-tuple-element.204.refs_4_, ...), custom_call_target="tpu_custom_call" | custom-call | flops 2070000000 | bytes 1000 | tf_op jit(solution)/shard_map/spread/pallas_call | solution.py:915
  386.9 4.1 %finished.1 = (bf16[128,2048]{1,0:T(8,128)(2,1)}, f32[128,2048]{1,0:T(8,128)}) custom-call(bf16[128,2048]{1,0:T(8,128)(2,1)} %get-tuple-element.107.refs_24_.refs_0_, bf16[256,2048]{1,0:T(8,128)(2,1)} %copy-done.18, bf16[256,2048]{1,0:T(8,128)(2,1)} %collective-permute-done.22.refs_3_.refs_2_, bf16[128,2048]{1,0:T(8,128)(2,1)} %copy-done.30, ...), custom_call_target="tpu_custom_call" | custom-call | flops 3449999872 | bytes 1000 | tf_op jit(solution)/shard_map/finished/pallas_call | solution.py:762
  393.0 3.8 spread.5
  (251 shorter events, 135.1 us)
Async XLA Ops:
  4.3 26.1 %collective-permute-start.1 = (bf16[2,128,2048]{2,1,0:T(8,128)(2,1)}, bf16[2,128,2048]{2,1,0:T(8,128)(2,1)}, u32[]{:S(2)}, u32[]{:S(2)}) collective-permute-start(bf16[2,128,2048]{2,1,0:T(8,128)(2,1)} %get-tuple-element.89.refs_14_.refs_22_.refs_13_.refs_1_), channel_id=1, source_target_pairs={{0,1},{1,2},{2,3},{3,0},{4,5},{5,6},{6,7},{7,4},{8,9},{9,10},{10,1... | collective-permute-start | bytes 3145736 | tf_op jit(solution)/shard_map/ppermute | solution.py:45
  6.3 26.0 %collective-permute-start.2 = (bf16[2,128,2048]{2,1,0:T(8,128)(2,1)}, bf16[2,128,2048]{2,1,0:T(8,128)(2,1)}, u32[]{:S(2)}, u32[]{:S(2)}) collective-permute-start(bf16[2,128,2048]{2,1,0:T(8,128)(2,1)} %get-tuple-element.89.refs_14_.refs_22_.refs_13_.refs_1_), channel_id=1, source_target_pairs={{0,4},{1,5},{2,6},{3,7},{4,0},{5,1},{6,2},{7,3},{8,12},{9,13},{10,... | collective-permute-start | bytes 3145736 | tf_op jit(solution)/shard_map/ppermute | solution.py:45
  8.0 36.2 %collective-permute-start = (bf16[2,128,2048]{2,1,0:T(8,128)(2,1)}, bf16[2,128,2048]{2,1,0:T(8,128)(2,1)}, u32[]{:S(2)}, u32[]{:S(2)}) collective-permute-start(bf16[2,128,2048]{2,1,0:T(8,128)(2,1)} %get-tuple-element.89.refs_14_.refs_22_.refs_13_.refs_1_), channel_id=1, source_target_pairs={{0,3},{1,0},{2,1},{3,2},{4,7},{5,4},{6,5},{7,6},{8,11},{9,8},{10,9... | collective-permute-start | bytes 3145736 | tf_op jit(solution)/shard_map/ppermute | solution.py:45
  9.4 34.8 %all-to-all-start = ((bf16[8,40,1792]{2,1,0:T(8,128)(2,1)}), bf16[8,40,1792]{2,1,0:T(8,128)(2,1)S(1)}, u32[]{:S(2)}, u32[]{:S(2)}) async-start(bf16[8,40,1792]{2,1,0:T(8,128)(2,1)} %get-tuple-element.88), calls=%async_computation | async-start | bytes 2293760 | tf_op jit(solution)/shard_map/all_to_all | solution.py:972
  30.3 40.4 %collective-permute-start.5 = (bf16[2,128,2048]{2,1,0:T(8,128)(2,1)}, bf16[2,128,2048]{2,1,0:T(8,128)(2,1)}, u32[]{:S(2)}, u32[]{:S(2)}) collective-permute-start(bf16[2,128,2048]{2,1,0:T(8,128)(2,1)} %collective-permute-done.1.refs_2_.refs_17_.refs_25_.refs_16_.refs_4_), channel_id=1, source_target_pairs={{0,1},{1,2},{2,3},{3,0},{4,5},{5,6},{6,7},{7,4},{8,9},{9,10},{10,1... | collective-permute-start | bytes 3145736 | tf_op jit(solution)/shard_map/ppermute | solution.py:45
  30.7 40.1 %collective-permute-start.7 = (bf16[2,128,2048]{2,1,0:T(8,128)(2,1)}, bf16[2,128,2048]{2,1,0:T(8,128)(2,1)S(1)}, u32[]{:S(2)}, u32[]{:S(2)}) collective-permute-start(bf16[2,128,2048]{2,1,0:T(8,128)(2,1)} %collective-permute-done.1.refs_2_.refs_17_.refs_25_.refs_16_.refs_4_), channel_id=1, source_target_pairs={{0,4},{1,5},{2,6},{3,7},{4,0},{5,1},{6,2},{7,3},{8,12},{9,13},{10,... | collective-permute-start | bytes 3145736 | tf_op jit(solution)/shard_map/ppermute | solution.py:45
  32.3 38.5 %collective-permute-start.6 = (bf16[2,128,2048]{2,1,0:T(8,128)(2,1)}, bf16[2,128,2048]{2,1,0:T(8,128)(2,1)S(1)}, u32[]{:S(2)}, u32[]{:S(2)}) collective-permute-start(bf16[2,128,2048]{2,1,0:T(8,128)(2,1)} %collective-permute-done.2.refs_3_.refs_18_.refs_26_.refs_17_.refs_5_), channel_id=1, source_target_pairs={{0,3},{1,0},{2,1},{3,2},{4,7},{5,4},{6,5},{7,6},{8,11},{9,8},{10,9... | collective-permute-start | bytes 3145736 | tf_op jit(solution)/shard_map/ppermute | solution.py:45
  47.6 20.0 %collective-permute-start.3 = (bf16[8,32,1792]{2,1,0:T(8,128)(2,1)}, bf16[8,32,1792]{2,1,0:T(8,128)(2,1)S(1)}, u32[]{:S(2)}, u32[]{:S(2)}) collective-permute-start(bf16[8,32,1792]{2,1,0:T(8,128)(2,1)} %get-tuple-element.91.refs_0_.refs_4_.refs_3_), channel_id=1, source_target_pairs={{0,96},{1,97},{2,98},{3,99},{4,100},{5,101},{6,102},{7,103},{8,104... | collective-permute-start | bytes 2752520 | tf_op jit(solution)/shard_map/ppermute | solution.py:45
  50.4 20.4 %collective-permute-start.4 = (bf16[8,32,1792]{2,1,0:T(8,128)(2,1)}, bf16[8,32,1792]{2,1,0:T(8,128)(2,1)}, u32[]{:S(2)}, u32[]{:S(2)}) collective-permute-start(bf16[8,32,1792]{2,1,0:T(8,128)(2,1)} %get-tuple-element.91.refs_0_.refs_4_.refs_3_), channel_id=1, source_target_pairs={{0,32},{1,33},{2,34},{3,35},{4,36},{5,37},{6,38},{7,39},{8,40},{9,... | collective-permute-start | bytes 2752520 | tf_op jit(solution)/shard_map/ppermute | solution.py:45
  76.0 26.0 %collective-permute-start.10 = (bf16[24,32,1792]{2,1,0:T(8,128)(2,1)}, bf16[24,32,1792]{2,1,0:T(8,128)(2,1)S(1)}, u32[]{:S(2)}, u32[]{:S(2)}) collective-permute-start(bf16[24,32,1792]{2,1,0:T(8,128)(2,1)} %bitcast.67), channel_id=1, source_target_pairs={{0,8},{1,9},{2,10},{3,11},{4,12},{5,13},{6,14},{7,15},{8,0},{9,1},... | collective-permute-start | bytes 8257544 | tf_op jit(solution)/shard_map/ppermute | solution.py:45
  136.1 21.3 %collective-permute-start.15 = (bf16[8,128,2048]{2,1,0:T(8,128)(2,1)}, bf16[8,128,2048]{2,1,0:T(8,128)(2,1)}, u32[]{:S(2)}, u32[]{:S(2)}) collective-permute-start(bf16[8,128,2048]{2,1,0:T(8,128)(2,1)} %get-tuple-element.97.refs_25_), channel_id=1, source_target_pairs={{0,8},{1,9},{2,10},{3,11},{4,12},{5,13},{6,14},{7,15},{8,0},{9,1},... | collective-permute-start | bytes 12582920 | tf_op jit(solution)/shard_map/ppermute | solution.py:45
  160.8 17.3 %collective-permute-start.17 = (bf16[1,128,2048]{2,1,0:T(8,128)(2,1)}, bf16[1,128,2048]{2,1,0:T(8,128)(2,1)S(1)}, u32[]{:S(2)}, u32[]{:S(2)}) collective-permute-start(bf16[1,128,2048]{2,1,0:T(8,128)(2,1)} %get-tuple-element.101.refs_12_), channel_id=1, source_target_pairs={{0,32},{1,33},{2,34},{3,35},{4,36},{5,37},{6,38},{7,39},{8,40},{9,... | collective-permute-start | bytes 1572872 | tf_op jit(solution)/shard_map/ppermute | solution.py:45
  160.8 17.3 %collective-permute-start.18 = (bf16[1,128,2048]{2,1,0:T(8,128)(2,1)}, bf16[1,128,2048]{2,1,0:T(8,128)(2,1)S(1)}, u32[]{:S(2)}, u32[]{:S(2)}) collective-permute-start(bf16[1,128,2048]{2,1,0:T(8,128)(2,1)} %get-tuple-element.102.refs_13_), channel_id=1, source_target_pairs={{0,96},{1,97},{2,98},{3,99},{4,100},{5,101},{6,102},{7,103},{8,104... | collective-permute-start | bytes 1572872 | tf_op jit(solution)/shard_map/ppermute | solution.py:45
  184.4 45.6 %collective-permute-start.26 = (bf16[2,128,2048]{2,1,0:T(8,128)(2,1)}, bf16[2,128,2048]{2,1,0:T(8,128)(2,1)S(1)}, u32[]{:S(2)}, u32[]{:S(2)}) collective-permute-start(bf16[2,128,2048]{2,1,0:T(8,128)(2,1)} %get-tuple-element.105.refs_3_.refs_6_), channel_id=1, source_target_pairs={{0,32},{1,33},{2,34},{3,35},{4,36},{5,37},{6,38},{7,39},{8,40},{9,... | collective-permute-start | bytes 3145736 | tf_op jit(solution)/shard_map/ppermute | solution.py:45
  184.4 45.6 %collective-permute-start.27 = (bf16[2,128,2048]{2,1,0:T(8,128)(2,1)}, bf16[2,128,2048]{2,1,0:T(8,128)(2,1)S(1)}, u32[]{:S(2)}, u32[]{:S(2)}) collective-permute-start(bf16[2,128,2048]{2,1,0:T(8,128)(2,1)} %get-tuple-element.106.refs_7_), channel_id=1, source_target_pairs={{0,96},{1,97},{2,98},{3,99},{4,100},{5,101},{6,102},{7,103},{8,104... | collective-permute-start | bytes 3145736 | tf_op jit(solution)/shard_map/ppermute | solution.py:45
  191.8 46.5 %collective-permute-start.29 = (bf16[4,64,2048]{2,1,0:T(8,128)(2,1)}, bf16[4,64,2048]{2,1,0:T(8,128)(2,1)S(1)}, u32[]{:S(2)}, u32[]{:S(2)}) collective-permute-start(bf16[4,64,2048]{2,1,0:T(8,128)(2,1)} %away_sums.1.refs_5_), channel_id=1, source_target_pairs={{0,16},{1,17},{2,18},{3,19},{4,20},{5,21},{6,22},{7,23},{8,24},{9,... | collective-permute-start | bytes 3145736 | tf_op jit(solution)/shard_map/ppermute | solution.py:45
  204.4 20.7 %collective-permute-start.19 = (bf16[128,2048]{1,0:T(8,128)(2,1)}, bf16[128,2048]{1,0:T(8,128)(2,1)S(1)}, u32[]{:S(2)}, u32[]{:S(2)}) collective-permute-start(bf16[128,2048]{1,0:T(8,128)(2,1)} %get-tuple-element.109), channel_id=1, source_target_pairs={{0,1},{1,2},{2,3},{3,0},{4,5},{5,6},{6,7},{7,4},{8,9},{9,10},{10,1... | collective-permute-start | bytes 1572872 | tf_op jit(solution)/shard_map/ppermute | solution.py:45
  204.8 20.3 %collective-permute-start.20 = (bf16[128,2048]{1,0:T(8,128)(2,1)}, bf16[128,2048]{1,0:T(8,128)(2,1)S(1)}, u32[]{:S(2)}, u32[]{:S(2)}) collective-permute-start(bf16[128,2048]{1,0:T(8,128)(2,1)} %get-tuple-element.112), channel_id=1, source_target_pairs={{0,3},{1,0},{2,1},{3,2},{4,7},{5,4},{6,5},{7,6},{8,11},{9,8},{10,9... | collective-permute-start | bytes 1572872 | tf_op jit(solution)/shard_map/ppermute | solution.py:45
  235.7 33.3 %collective-permute-start.21 = (bf16[256,2048]{1,0:T(8,128)(2,1)}, bf16[256,2048]{1,0:T(8,128)(2,1)S(1)}, u32[]{:S(2)}, u32[]{:S(2)}) collective-permute-start(bf16[256,2048]{1,0:T(8,128)(2,1)} %get-tuple-element.118.refs_5_), channel_id=1, source_target_pairs={{0,1},{1,2},{2,3},{3,0},{4,5},{5,6},{6,7},{7,4},{8,9},{9,10},{10,1... | collective-permute-start | bytes 3145736 | tf_op jit(solution)/shard_map/ppermute | solution.py:45
  235.7 33.3 %collective-permute-start.22 = (bf16[256,2048]{1,0:T(8,128)(2,1)}, bf16[256,2048]{1,0:T(8,128)(2,1)}, u32[]{:S(2)}, u32[]{:S(2)}) collective-permute-start(bf16[256,2048]{1,0:T(8,128)(2,1)} %get-tuple-element.119), channel_id=1, source_target_pairs={{0,3},{1,0},{2,1},{3,2},{4,7},{5,4},{6,5},{7,6},{8,11},{9,8},{10,9... | collective-permute-start | bytes 3145736 | tf_op jit(solution)/shard_map/ppermute | solution.py:45
  276.4 20.9 %collective-permute-start.41 = (bf16[2,80,2048]{2,1,0:T(8,128)(2,1)S(1)}, bf16[2,80,2048]{2,1,0:T(8,128)(2,1)S(1)}, u32[]{:S(2)}, u32[]{:S(2)}) collective-permute-start(bf16[2,80,2048]{2,1,0:T(8,128)(2,1)S(1)} %pad_maximum_fusion.1.refs_0_), channel_id=1, source_target_pairs={{0,32},{1,33},{2,34},{3,35},{4,36},{5,37},{6,38},{7,39},{8,40},{9,... | collective-permute-start | bytes 1966088 | tf_op jit(solution)/shard_map/ppermute | solution.py:45
  277.5 19.8 %collective-permute-start.42 = (bf16[2,80,2048]{2,1,0:T(8,128)(2,1)S(1)}, bf16[2,80,2048]{2,1,0:T(8,128)(2,1)S(1)}, u32[]{:S(2)}, u32[]{:S(2)}) collective-permute-start(bf16[2,80,2048]{2,1,0:T(8,128)(2,1)S(1)} %pad_maximum_fusion.1.refs_0_), channel_id=1, source_target_pairs={{0,96},{1,97},{2,98},{3,99},{4,100},{5,101},{6,102},{7,103},{8,104... | collective-permute-start | bytes 1966088 | tf_op jit(solution)/shard_map/ppermute | solution.py:45
  282.1 20.5 %collective-permute-start.37 = (bf16[1,128,2048]{2,1,0:T(8,128)(2,1)}, bf16[1,128,2048]{2,1,0:T(8,128)(2,1)S(1)}, u32[]{:S(2)}, u32[]{:S(2)}) collective-permute-start(bf16[1,128,2048]{2,1,0:T(8,128)(2,1)} %unpacked_sums.1), channel_id=1, source_target_pairs={{0,16},{1,17},{2,18},{3,19},{4,20},{5,21},{6,22},{7,23},{8,24},{9,... | collective-permute-start | bytes 1572872 | tf_op jit(solution)/shard_map/ppermute | solution.py:45
  294.6 43.5 %collective-permute-start.34 = (bf16[256,2048]{1,0:T(8,128)(2,1)}, bf16[256,2048]{1,0:T(8,128)(2,1)S(1)}, u32[]{:S(2)}, u32[]{:S(2)}) collective-permute-start(bf16[256,2048]{1,0:T(8,128)(2,1)} %get-tuple-element.144), channel_id=1, source_target_pairs={{0,1},{1,2},{2,3},{3,0},{4,5},{5,6},{6,7},{7,4},{8,9},{9,10},{10,1... | collective-permute-start | bytes 3145736 | tf_op jit(solution)/shard_map/ppermute | solution.py:45
  294.6 43.5 %collective-permute-start.35 = (bf16[256,2048]{1,0:T(8,128)(2,1)}, bf16[256,2048]{1,0:T(8,128)(2,1)S(1)}, u32[]{:S(2)}, u32[]{:S(2)}) collective-permute-start(bf16[256,2048]{1,0:T(8,128)(2,1)} %get-tuple-element.145), channel_id=1, source_target_pairs={{0,3},{1,0},{2,1},{3,2},{4,7},{5,4},{6,5},{7,6},{8,11},{9,8},{10,9... | collective-permute-start | bytes 3145736 | tf_op jit(solution)/shard_map/ppermute | solution.py:45
  302.7 39.8 %collective-permute-start.38 = (bf16[2,128,2048]{2,1,0:T(8,128)(2,1)S(1)}, bf16[2,128,2048]{2,1,0:T(8,128)(2,1)S(1)}, u32[]{:S(2)}, u32[]{:S(2)}) collective-permute-start(bf16[2,128,2048]{2,1,0:T(8,128)(2,1)S(1)} %pad_maximum_fusion.refs_0_), channel_id=1, source_target_pairs={{0,32},{1,33},{2,34},{3,35},{4,36},{5,37},{6,38},{7,39},{8,40},{9,... | collective-permute-start | bytes 3145736 | tf_op jit(solution)/shard_map/ppermute | solution.py:45
  303.7 38.8 %collective-permute-start.39 = (bf16[2,128,2048]{2,1,0:T(8,128)(2,1)S(1)}, bf16[2,128,2048]{2,1,0:T(8,128)(2,1)S(1)}, u32[]{:S(2)}, u32[]{:S(2)}) collective-permute-start(bf16[2,128,2048]{2,1,0:T(8,128)(2,1)S(1)} %pad_maximum_fusion.refs_0_), channel_id=1, source_target_pairs={{0,96},{1,97},{2,98},{3,99},{4,100},{5,101},{6,102},{7,103},{8,104... | collective-permute-start | bytes 3145736 | tf_op jit(solution)/shard_map/ppermute | solution.py:45
  309.4 22.2 %collective-permute-start.44 = (bf16[1,80,2048]{2,1,0:T(8,128)(2,1)}, bf16[1,80,2048]{2,1,0:T(8,128)(2,1)S(1)}, u32[]{:S(2)}, u32[]{:S(2)}) collective-permute-start(bf16[1,80,2048]{2,1,0:T(8,128)(2,1)} %get-tuple-element.150), channel_id=1, source_target_pairs={{0,96},{1,97},{2,98},{3,99},{4,100},{5,101},{6,102},{7,103},{8,104... | collective-permute-start | bytes 983048 | tf_op jit(solution)/shard_map/ppermute | solution.py:45
  348.1 23.3 %collective-permute-start.47 = (bf16[6,128,2048]{2,1,0:T(8,128)(2,1)}, bf16[6,128,2048]{2,1,0:T(8,128)(2,1)S(1)}, u32[]{:S(2)}, u32[]{:S(2)}) collective-permute-start(bf16[6,128,2048]{2,1,0:T(8,128)(2,1)} %bitcast.46), channel_id=1, source_target_pairs={{0,8},{1,9},{2,10},{3,11},{4,12},{5,13},{6,14},{7,15},{8,0},{9,1},... | collective-permute-start | bytes 9437192 | tf_op jit(solution)/shard_map/ppermute | solution.py:45
  353.5 17.9 %collective-permute-start.36 = (bf16[128,2048]{1,0:T(8,128)(2,1)}, bf16[128,2048]{1,0:T(8,128)(2,1)}, u32[]{:S(2)}, u32[]{:S(2)}) collective-permute-start(bf16[128,2048]{1,0:T(8,128)(2,1)} %other_sums.3.refs_4_), channel_id=1, source_target_pairs={{0,4},{1,5},{2,6},{3,7},{4,0},{5,1},{6,2},{7,3},{8,12},{9,13},{10,... | collective-permute-start | bytes 1572872 | tf_op jit(solution)/shard_map/ppermute | solution.py:45
  353.9 27.7 %collective-permute-start.45 = (bf16[1,128,2048]{2,1,0:T(8,128)(2,1)}, bf16[1,128,2048]{2,1,0:T(8,128)(2,1)}, u32[]{:S(2)}, u32[]{:S(2)}) collective-permute-start(bf16[1,128,2048]{2,1,0:T(8,128)(2,1)} %get-tuple-element.151), channel_id=1, source_target_pairs={{0,32},{1,33},{2,34},{3,35},{4,36},{5,37},{6,38},{7,39},{8,40},{9,... | collective-permute-start | bytes 1572872 | tf_op jit(solution)/shard_map/ppermute | solution.py:45
  355.4 26.2 %collective-permute-start.46 = (bf16[1,128,2048]{2,1,0:T(8,128)(2,1)}, bf16[1,128,2048]{2,1,0:T(8,128)(2,1)}, u32[]{:S(2)}, u32[]{:S(2)}) collective-permute-start(bf16[1,128,2048]{2,1,0:T(8,128)(2,1)} %get-tuple-element.152), channel_id=1, source_target_pairs={{0,96},{1,97},{2,98},{3,99},{4,100},{5,101},{6,102},{7,103},{8,104... | collective-permute-start | bytes 1572872 | tf_op jit(solution)/shard_map/ppermute | solution.py:45
  (70 other events, 555.7 us)

commit v10 on v9

--- a/solution.py
+++ b/solution.py
@@ -90,10 +90,10 @@
     return copies
 
 
-def piece_copies(pieces, half, target, sems, rows):
+def piece_copies(pieces, half, target, sems, rows, lanes=slice(None)):
     return [
         pltpu.make_async_copy(
-            piece.at[half] if len(piece.shape) == 3 else piece,
+            piece.at[half, :, lanes] if len(piece.shape) == 3 else piece.at[:, lanes],
             target.at[pl.ds(at * rows, rows)],
             sems.at[at],
         )
@@ -101,14 +101,29 @@
     ]
 
 
-def weight_copies(pieces, refs, spot_ref, target, lanes, sems):
+def weight_copies(pieces, refs, spot_ref, target, lanes, sems, source=None):
+    if source is not None:
+        pieces = [
+            (
+                array,
+                begin + max(source - first, 0),
+                min(size, 4),
+                max(first, source) - source,
+                spot,
+                ref,
+            )
+            for (array, begin, size, first, spot), ref in zip(pieces, refs)
+            if first <= source < first + size
+        ]
+    else:
+        pieces = [(*piece, ref) for piece, ref in zip(pieces, refs)]
     return [
         pltpu.make_async_copy(
             ref.at[pl.ds(begin, size), :, lanes],
             target.at[pl.ds(first, size), spot_ref[spot]],
             sems.at[at],
         )
-        for at, (ref, (_, begin, size, first, spot)) in enumerate(zip(refs, pieces))
+        for at, (_, begin, size, first, spot, ref) in enumerate(pieces)
     ]
 
 
@@ -561,32 +576,35 @@
     )(active, attended, down, out, bias, *after)
 
 
-def back_norms(d_qkv, d_hidden, weight, spots, x, mean, inverse, gains, after):
+def back_norms(d_qkv, d_hidden, weight, spots, x, mean, inverse, gains, part, before, after):
     total, n1 = d_qkv.shape
     n2 = d_hidden.shape[1]
     count = len(x)
     parts = len(weight)
     width = x[0].shape[-1]
     step = 512
+    half = width // 2
 
     def body(spot_ref, m_ref, i_ref, g_ref, *refs):
         w_refs, refs = refs[:parts], refs[parts:]
         x_refs, refs = refs[:count], refs[count:]
-        plain, sums_ref, outs = refs[:2], refs[2], refs[3 : 3 + count]
-        dq_v, du_v, w_v, x_v, s_v, w_sem, x_sem, sems, out_sem = refs[3 + count :]
+        plain, refs = refs[:2], refs[2 + len(before) :]
+        sums_ref, outs = refs[0], refs[1 : 1 + count]
+        dq_v, du_v, w_v, x_v, s_v, w_sem, x_sem, sems, out_sem = refs[1 + count :]
         plain_v = (dq_v, du_v)
         copies = loads(
             [
                 pltpu.make_async_copy(plain[n], plain_v[n], sems.at[n]) for n in range(2)
             ]
-            + weight_copies(weight, w_refs, spot_ref, w_v, slice(None), w_sem)
-            + piece_copies(x_refs, 0, x_v, x_sem, 128)
+            + weight_copies(weight, w_refs, spot_ref, w_v, slice(None), w_sem, part * 4)
+            + piece_copies(x_refs, 0, x_v, x_sem, 128, pl.ds(part * half, half))
         )
         def leaving(n):
             lanes = pl.ds(pl.multiple_of(n * step, step), step)
+            there = pl.ds(pl.multiple_of(part * half + n * step, step), step)
             return [
                 pltpu.make_async_copy(
-                    s_v.at[pl.ds(at * 128, 128), lanes], outs[at].at[:, lanes], out_sem.at[at]
+                    s_v.at[pl.ds(at * 128, 128), lanes], outs[at].at[:, there], out_sem.at[at]
                 )
                 for at in range(count)
             ]
@@ -594,13 +612,14 @@
         for copy in copies:
             copy.wait()
 
-        @pl.loop(0, width // step)
+        @pl.loop(0, half // step)
         def _(n):
             lanes = pl.ds(pl.multiple_of(n * step, step), step)
+            gain = pl.ds(pl.multiple_of(part * half + n * step, step), step)
             sources = pl.ds(n * (step // 256), step // 256)
             d1 = dot(dq_v[...], w_v[sources, :, :, 0:n1].reshape(step, n1), 1, 1)
             d2 = dot(du_v[...], w_v[sources, :, :, n1:].reshape(step, n2), 1, 1)
-            s_v[:, lanes] = (d1 * g_ref[0:1, lanes] + d2 * g_ref[1:2, lanes]).astype(bf16)
+            s_v[:, lanes] = (d1 * g_ref[0:1, gain] + d2 * g_ref[1:2, gain]).astype(bf16)
             for copy in leaving(n):
                 copy.start()
             normed = (x_v[:, lanes].astype(f32) - m_ref[...]) * i_ref[...]
@@ -609,32 +628,33 @@
             sums_ref[2:3, lanes] = jnp.sum(d2 * normed, 0, keepdims=True)
             sums_ref[3:4, lanes] = jnp.sum(d2, 0, keepdims=True)
 
-        for n in range(width // step):
+        for n in range(half // step):
             for copy in leaving(n):
                 copy.wait()
 
     vmem = pl.BlockSpec(memory_space=pltpu.VMEM)
     return pl.pallas_call(
-        after_inputs(body, 6 + parts + count, len(after)),
-        out_shape=(jax.ShapeDtypeStruct((4, width), f32),)
+        after_inputs(body, 6 + parts + count + len(before), len(after)),
+        out_shape=(jax.ShapeDtypeStruct((4, half), f32),)
         + (jax.ShapeDtypeStruct((128, width), bf16),) * count,
         in_specs=[pl.BlockSpec(memory_space=pltpu.SMEM)]
         + [vmem] * 3
-        + anywhere(parts + count + 2 + len(after)),
+        + anywhere(parts + count + 2 + len(before) + len(after)),
         out_specs=(vmem,) + tuple(anywhere(count)),
         scratch_shapes=[
             pltpu.VMEM((total, n1), bf16),
             pltpu.VMEM((total, n2), bf16),
-            pltpu.VMEM((8, 8, width // 64, n1 + n2), bf16),
-            pltpu.VMEM((total, width), bf16),
-            pltpu.VMEM((total, width), bf16),
+            pltpu.VMEM((4, 8, width // 64, n1 + n2), bf16),
+            pltpu.VMEM((total, half), bf16),
+            pltpu.VMEM((total, half), bf16),
             pltpu.SemaphoreType.DMA((parts,)),
             pltpu.SemaphoreType.DMA((count,)),
             pltpu.SemaphoreType.DMA((2,)),
             pltpu.SemaphoreType.DMA((count,)),
         ],
+        input_output_aliases={6 + parts + count + n: 1 + n for n in range(len(before))},
         compiler_params=kernel_params(),
-        cost_estimate=cost(15),
+        cost_estimate=cost(9),
         name="back_norms",
     )(
         spots,
@@ -645,6 +665,7 @@
         *x,
         d_qkv,
         d_hidden,
+        *before,
         *after,
     )
 
@@ -1098,17 +1119,20 @@
     )
     a_crossed = move(a_away, h=1)
     mix = mixed_part(active, attended, down_weight, out_weight, wide_bias, (a_away, above, below))
-    norm_sums, *sums = back_norms(
-        d_qkv,
-        d_hidden,
-        weight,
-        spots,
-        x_all,
-        mean,
-        inverse,
-        jnp.stack([gains[0], gains[2]]),
-        (mix[0],),
-    )
+    def norms_back(part, before, after):
+        return back_norms(
+            d_qkv,
+            d_hidden,
+            weight,
+            spots,
+            x_all,
+            mean,
+            inverse,
+            jnp.stack([gains[0], gains[2]]),
+            part,
+            before,
+            after,
+        )
 
     flat, both = (128, width), (256, width)
 
@@ -1159,7 +1183,6 @@
         return (pieces[0], *arrived, move(other, l=1)), other, *copies
 
     mix_passed = ring_start(mix[6], mix[2])
-    mix_arrived, mix_ups = ring_middle(mix, mix_passed, (norm_sums,))
 
     def ends_body(n_ref, keep_ref, got_ref, below_ref, above_ref, leave_ref, stay_ref):
         total = wide(keep_ref, got_ref, below_ref, above_ref).astype(bf16)
@@ -1174,7 +1197,7 @@
         [(v, pair_shape, turn(0)) for v in (keep, got)]
         + [(v, pair_shape, lambda n: 0) for v in (from_below, from_above)],
         (one, one),
-        (mix_ups,),
+        (mix[0],),
     )
     crossed = move(leaves, h=1)
 
@@ -1198,6 +1221,8 @@
         ((32, width), (32, width), (64, width), (64, width), (64, width)),
         (leaves,),
     )
+    low_sums, *sums = norms_back(0, (), (a_low,))
+    mix_arrived, mix_ups = ring_middle(mix, mix_passed, (low_sums,))
     a_low, a_high = move(a_low, y=1), move(a_high, y=-1)
 
     def beside_body(n_ref, above_ref, below_ref, low_ref, high_ref, up_ref, down_ref):
@@ -1212,9 +1237,10 @@
         numbers,
         [(v, v.shape, lambda n: 0) for v in (a_above, a_below, a_low, a_high)],
         ((64, width), (64, width)),
-        (crossed,),
+        (crossed, low_sums),
     )
     a_from_below, a_from_above = move(a_above, y=1), move(a_below, y=-1)
+    high_sums, *sums = norms_back(1, tuple(sums), (a_above, mix_ups))
 
     part, stays = packed_sums(
         stays,
@@ -1222,7 +1248,7 @@
         a_own,
         a_from_below,
         a_from_above,
-        norm_sums,
+        jnp.concatenate([low_sums, high_sums], 1),
         qkv_sums,
         up_sums,
         dy_sums,
@@ -1234,20 +1260,15 @@
     received = lax.all_to_all(part, "shard", 0, 0)
     mix_left, mix_other, high, low = ring_end(mix, mix_arrived, (sums[6], sums[2]))
     part = unpacked_sums(received, cols, (mix_other,))
+    order = ((0, h), (0, 1 - h), (1, h), (1, 1 - h), (3, h), (3, 1 - h), (2, h), (2, 1 - h))
+    places = jnp.stack([(y + k) % 4 * 2 + high for k, high in order]).astype(jnp.int32)
+
     sums_arrived, sums_ups = ring_middle(sums, ring_start(high, low), (received,))
     sums_left, sums_other = ring_end(sums, sums_arrived, ())
-
-    order = ((0, h), (0, 1 - h), (1, h), (1, 1 - h), (3, h), (3, 1 - h), (2, h), (2, 1 - h))
-    places = jnp.stack([(y + k) % 4 * 2 + high for k, high in order]).astype(jnp.int32)
-
-    def rep_gather(own, after):
-        own = jnp.concatenate([own, move(own, h=1)])
-        below, above = move(own, y=1), move(own, y=-1)
-        low, high, near = halves(own, below, above, after)
-        return near, (move(low, y=1), move(high, y=-1))
-
-    near, far = rep_gather(stays[None], ())
-    stays = joined((near, *far), ())
+    stays = stays[None]
+    stays = jnp.concatenate([stays, move(stays, h=1)])
+    below, above = move(stays, y=1), move(stays, y=-1)
+    stays = joined((stays, above, below, move(below, y=1)), ())
     down_grad, out_grad = spread(
         [(stays, move(stays, c=1))],
         places,
@@ -1257,7 +1278,10 @@
         (),
         (mix_left[3],),
     )
-    near, far = rep_gather(part, (stays, sums_other, mix_left[3]))
+    part = joined((part, move(part, h=1)), (sums_ups,))
+    below, above = move(part, y=1), move(part, y=-1)
+    low, high, near = halves(part, below, above, (stays, mix_left[3], sums_other))
+    far = move(low, y=1), move(high, y=-1)
     targets = [
         (
             3 * width,

time: 404 us -> 398 us (0.985)
  waiting for transfers between devices: 96.4 us -> 87.8 us
    ppermute x50 -> x49, waiting for transfers between devices: 87.2 us -> 78.3 us  [move(): return lax.ppermute(value, BOTH, pairs)]
    pallas_call x1 -> x2, Pallas kernels: 17.8 us -> 22.8 us  [back_norms(): pl.pallas_call(after_inputs(body, 6 + parts + count + len(before), len(af...]
    pallas_call x3 -> x2, Pallas kernels: 9.52 us -> 6.87 us  [halves(): pl.pallas_call(after_inputs(body, 3, len(after)), out_shape=(jax.ShapeDty...]
    ppermute x50 -> x49, starting transfers between devices: 71 us -> 70.1 us  [move(): return lax.ppermute(value, BOTH, pairs)]
    unnamed x107 -> x103, local copies, waits for them, and re-layouts: 24 us -> 23.7 us
    pallas_call x2 -> x3, Pallas kernels: 7.97 us -> 8.16 us  [joined(): pl.pallas_call(after_inputs(body, count, len(after)), out_shape=jax.Shape...]
  transfers between devices with their start and end apart: 52 -> 51, of which waited for: 13 -> 14; matrix products, arithmetic and copies ran while one was open for 4% -> 5% of each run, Pallas kernels for 32% -> 33%
where the time goes in v10:
time: 398 us; the launch traced here: 392 us
  Pallas kernels  183 us (46%)
  waiting for transfers between devices  87.8 us (22%)
  starting transfers between devices  77.2 us (19%)
  local copies, waits for them, and re-layouts  33.7 us (8%)
  other arithmetic  8.62 us (2%)
    ppermute x49, waiting for transfers between devices, move(): return lax.ppermute(value, BOTH, pairs)  78.3 us
    ppermute x49, starting transfers between devices, move(): return lax.ppermute(value, BOTH, pairs)  70.1 us
    pallas_call x10, Pallas kernels, blocks_call(): pl.pallas_call(after_inputs(body, 1 + len(terms), len(after)), out_shape=...  36.8 us
    pallas_call x1, Pallas kernels, feed_forward(): pl.pallas_call(after_inputs(body, 5 + parts + 2 * count, len(after)), out...  32.2 us
    unnamed x103, local copies, waits for them, and re-layouts  23.7 us
    pallas_call x2, Pallas kernels, back_norms(): pl.pallas_call(after_inputs(body, 6 + parts + count + len(before), len(af...  22.8 us
    pallas_call x3, Pallas kernels, spread(): pl.pallas_call(after_inputs(body, 2 + 2 * len(pieces) + len(before), len(...  21 us
    pallas_call x1, Pallas kernels, attend(): pl.pallas_call(after_inputs(body, 7 + parts + count, len(after)), out_sha...  17.1 us
  transfers between devices with their start and end apart: 51, of which 14 were waited for; matrix products, arithmetic and copies ran while one was open for 5% of the time, Pallas kernels for 33%

profile of v10, /device:TPU:1, one launch (start us, length us, event | category | flops | bytes accessed | tf_op | source)
XLA Modules:
  0.0 391.8 jit_solution(7804665451426520664)
XLA Ops:
  0.7 3.6 packed.1
  9.4 3.6 all-to-all-start
  13.0 17.3 %collective-permute-done.1.refs_2_.refs_17_.refs_25_.refs_16_.refs_4_ = bf16[2,128,2048]{2,1,0:T(8,128)(2,1)} collective-permute-done((bf16[2,128,2048]{2,1,0:T(8,128)(2,1)}, bf16[2,128,2048]{2,1,0:T(8,128)(2,1)}, u32[]{:S(2)}, u32[]{:S(2)}) %collective-permute-start.1) | collective-permute-done | bytes 1048608 | tf_op jit(solution)/shard_map/ppermute | solution.py:45
  35.0 9.2 %all-to-all-done.refs_0_ = bf16[8,40,1792]{2,1,0:T(8,128)(2,1)S(1)} async-done(((bf16[8,40,1792]{2,1,0:T(8,128)(2,1)}), bf16[8,40,1792]{2,1,0:T(8,128)(2,1)S(1)}, u32[]{:S(2)}, u32[]{:S(2)}) %all-to-all-start) | async-done | bytes 1146912 | tf_op jit(solution)/shard_map/all_to_all | solution.py:993
  51.6 16.1 %collective-permute-done.3.refs_2_.refs_5_.refs_4_ = bf16[8,32,1792]{2,1,0:T(8,128)(2,1)} collective-permute-done((bf16[8,32,1792]{2,1,0:T(8,128)(2,1)}, bf16[8,32,1792]{2,1,0:T(8,128)(2,1)}, u32[]{:S(2)}, u32[]{:S(2)}) %collective-permute-start.3) | collective-permute-done | bytes 917536 | tf_op jit(solution)/shard_map/ppermute | solution.py:45
  76.0 3.9 collective-permute-start.10
  91.5 5.2 %collective-permute-done.8.refs_6_.refs_5_ = bf16[4,32,1792]{2,1,0:T(8,128)(2,1)S(1)} collective-permute-done((bf16[4,32,1792]{2,1,0:T(8,128)(2,1)}, bf16[4,32,1792]{2,1,0:T(8,128)(2,1)S(1)}, u32[]{:S(2)}, u32[]{:S(2)}) %collective-permute-start.8) | collective-permute-done | bytes 458784 | tf_op jit(solution)/shard_map/ppermute | solution.py:45
  103.9 32.2 %feed_forward.1 = (bf16[1024,2048]{1,0:T(8,128)(2,1)}, bf16[1024,1024]{1,0:T(8,128)(2,1)}, bf16[1024,1024]{1,0:T(8,128)(2,1)}, bf16[8,128,2048]{2,1,0:T(8,128)(2...) custom-call(s32[4]{0:T(128)} %get-tuple-element.186.refs_0_.refs_9_,, ...), custom_call_target="tpu_custom_call" | custom-call | flops 36800000000 | bytes 1000 | tf_op jit(solution)/shard_map/feed_forward/pallas_call | solution.py:258
  140.2 17.1 %attend.1 = (bf16[1024,256]{1,0:T(8,128)(2,1)}, bf16[1024,768]{1,0:T(8,128)(2,1)}, f32[1,768]{1,0:T(1,128)}) custom-call(s32[8,3]{1,0:T(8,128)} %copy-done.8, s32[8]{0:T(128)} %pad_add_fusion.1.refs_1_.refs_0_, f32[3,1,256]{2,1,0:T(1,128)} %pad_maximum_fusion.3.refs_2_, bf16[8,32,1792]{2,1,0:T(8,128)(2,1)} %get-tuple-element.97.refs_0_.refs_4_.refs_3_, ...), custom_call_target="tpu_custom_call" | custom-call | flops 19549999104 | bytes 1000 | tf_op jit(solution)/shard_map/attend/pallas_call | solution.py:431
  163.4 13.7 %attention_grads.1 = (bf16[8,64,2048]{2,1,0:T(8,128)(2,1)}, bf16[8,64,2048]{2,1,0:T(8,128)(2,1)}) custom-call(s32[4]{0:T(128)} %get-tuple-element.186.refs_0_.refs_9_, bf16[2,128,2048]{2,1,0:T(8,128)(2,1)} %get-tuple-element.95.refs_14_.refs_22_.refs_13_.refs_1_, bf16[2,128,2048]{2,1,0:T(8,128)(2,1)} %collective-permute-done.refs_1_.refs_15_.refs_23_.refs_14_.refs_2_, ...), custom_call_target="tpu_custom_call" | custom-call | flops 13799999488 | bytes 1000 | tf_op jit(solution)/shard_map/attention_grads/pallas_call | solution.py:528
  179.6 4.8 %near_sums.1 = (bf16[2,128,2048]{2,1,0:T(8,128)(2,1)}, bf16[2,128,2048]{2,1,0:T(8,128)(2,1)}) custom-call(s32[4]{0:T(128)} %get-tuple-element.186.refs_0_.refs_9_, bf16[8,128,2048]{2,1,0:T(8,128)(2,1)} %get-tuple-element.106.refs_1_.refs_3_, bf16[8,128,2048]{2,1,0:T(8,128)(2,1)} %collective-permute-done.15.refs_2_.refs_4_, ...), custom_call_target="tpu_custom_call" | custom-call | flops 23000000512 | bytes 1000 | tf_op jit(solution)/shard_map/near_sums/pallas_call | solution.py:874
  188.4 3.4 away_sums.1.refs_5_
  195.0 9.3 %mixed_part.1 = (bf16[128,2048]{1,0:T(8,128)(2,1)}, bf16[128,2048]{1,0:T(8,128)(2,1)}, bf16[128,2048]{1,0:T(8,128)(2,1)}, bf16[128,2048]{1,0:T(8,128)(2,1)}, bf1...) custom-call(bf16[1024,1024]{1,0:T(8,128)(2,1)} %get-tuple-element.101, ...), custom_call_target="tpu_custom_call" | custom-call | flops 11500000256 | bytes 1000 | tf_op jit(solution)/shard_map/mixed_part/pallas_call | solution.py:560
  211.9 4.4 %end_sums.1 = (bf16[1,128,2048]{2,1,0:T(8,128)(2,1)}, bf16[1,128,2048]{2,1,0:T(8,128)(2,1)}) custom-call(s32[4]{0:T(128)} %get-tuple-element.186.refs_0_.refs_9_, bf16[8,128,2048]{2,1,0:T(8,128)(2,1)} %get-tuple-element.106.refs_1_.refs_3_, bf16[8,128,2048]{2,1,0:T(8,128)(2,1)} %collective-permute-done.15.refs_2_.refs_4_, bf16[2,128,2048]{2,1,0:T(8,128)(2,1)} %copy-done.21, ...), custom_call_target="tpu_custom_call" | custom-call | flops 3449999872 | bytes 1000 | tf_op jit(solution)/shard_map/end_sums/pallas_call | solution.py:874
  220.5 3.8 around_sums.1
  227.0 11.4 %back_norms.2 = (f32[4,1024]{1,0:T(4,128)}, bf16[128,2048]{1,0:T(8,128)(2,1)}, bf16[128,2048]{1,0:T(8,128)(2,1)}, bf16[128,2048]{1,0:T(8,128)(2,1)}, bf16[128,20...) custom-call(s32[8]{0:T(128)} %pad_add_fusion.1.refs_1_.refs_0_, ...), custom_call_target="tpu_custom_call" | custom-call | flops 10350000128 | bytes 1000 | tf_op jit(solution)/shard_map/back_norms/pallas_call | solution.py:636
  239.4 3.9 %passed_sums.2 = (bf16[256,2048]{1,0:T(8,128)(2,1)}, bf16[256,2048]{1,0:T(8,128)(2,1)}) custom-call(s32[4]{0:T(128)} %get-tuple-element.186.refs_0_.refs_9_, bf16[128,2048]{1,0:T(8,128)(2,1)} %get-tuple-element.114.refs_1_, bf16[128,2048]{1,0:T(8,128)(2,1)} %copy-done.33, bf16[128,2048]{1,0:T(8,128)(2,1)} %get-tuple-element.116.refs_3_, ...), custom_call_target="tpu_custom_call" | custom-call | flops 3449999872 | bytes 1000 | tf_op jit(solution)/shard_map/passed_sums/pallas_call | solution.py:874
  252.4 11.4 %back_norms.3 = (f32[4,1024]{1,0:T(4,128)}, bf16[128,2048]{1,0:T(8,128)(2,1)}, bf16[128,2048]{1,0:T(8,128)(2,1)}, bf16[128,2048]{1,0:T(8,128)(2,1)}, bf16[128,20...) custom-call(s32[8]{0:T(128)} %pad_add_fusion.1.refs_1_.refs_0_, ...), custom_call_target="tpu_custom_call", output_to_operand_aliasing={{1}: (24, {}), {2}: (25, {}), {3}: (26, {}), {4}: (27, {}),... | custom-call | flops 10350000128 | bytes 1000 | tf_op jit(solution)/shard_map/back_norms/pallas_call | solution.py:636
  270.2 3.5 all-to-all-start.1
  274.7 3.6 other_sums.2
  288.2 5.3 %collective-permute-done.30.refs_2_ = bf16[128,2048]{1,0:T(8,128)(2,1)S(1)} collective-permute-done((bf16[128,2048]{1,0:T(8,128)(2,1)}, bf16[128,2048]{1,0:T(8,128)(2,1)S(1)}, u32[]{:S(2)}, u32[]{:S(2)}) %collective-permute-start.30) | collective-permute-done | bytes 524320 | tf_op jit(solution)/shard_map/ppermute | solution.py:45
  294.5 3.9 %passed_sums.3 = (bf16[256,2048]{1,0:T(8,128)(2,1)}, bf16[256,2048]{1,0:T(8,128)(2,1)}) custom-call(s32[4]{0:T(128)} %get-tuple-element.186.refs_0_.refs_9_, bf16[128,2048]{1,0:T(8,128)(2,1)} %get-tuple-element.145.refs_1_, bf16[128,2048]{1,0:T(8,128)(2,1)} %copy-done.35, bf16[128,2048]{1,0:T(8,128)(2,1)} %get-tuple-element.147.refs_3_, ...), custom_call_target="tpu_custom_call" | custom-call | flops 3449999872 | bytes 1000 | tf_op jit(solution)/shard_map/passed_sums/pallas_call | solution.py:874
  306.9 8.7 %collective-permute-done.43.refs_3_ = bf16[2,80,2048]{2,1,0:T(8,128)(2,1)S(1)} collective-permute-done((bf16[2,80,2048]{2,1,0:T(8,128)(2,1)S(1)}, bf16[2,80,2048]{2,1,0:T(8,128)(2,1)S(1)}, u32[]{:S(2)}, u32[]{:S(2)}) %collective-permute-start.43) | collective-permute-done | bytes 655392 | tf_op jit(solution)/shard_map/ppermute | solution.py:45
  316.4 3.7 joined.4.refs_3_.refs_2_
  326.4 11.6 %collective-permute-done.38.refs_1_ = bf16[2,128,2048]{2,1,0:T(8,128)(2,1)S(1)} collective-permute-done((bf16[2,128,2048]{2,1,0:T(8,128)(2,1)}, bf16[2,128,2048]{2,1,0:T(8,128)(2,1)S(1)}, u32[]{:S(2)}, u32[]{:S(2)}) %collective-permute-start.38) | collective-permute-done | bytes 1048608 | tf_op jit(solution)/shard_map/ppermute | solution.py:45
  339.9 3.6 halves.3
  343.6 3.9 %collective-permute-start.46 = (bf16[6,128,2048]{2,1,0:T(8,128)(2,1)}, bf16[6,128,2048]{2,1,0:T(8,128)(2,1)S(1)}, u32[]{:S(2)}, u32[]{:S(2)}) collective-permute-start(bf16[6,128,2048]{2,1,0:T(8,128)(2,1)} %bitcast.45), channel_id=1, source_target_pairs={{0,8},{1,9},{2,10},{3,11},{4,12},{5,13},{6,14},{7,15},{8,0},{9,1},... | collective-permute-start | bytes 9437192 | tf_op jit(solution)/shard_map/ppermute | solution.py:45
  352.1 4.6 %collective-permute-done.47.refs_3_ = bf16[8,80,2048]{2,1,0:T(8,128)(2,1)} collective-permute-done((bf16[8,80,2048]{2,1,0:T(8,128)(2,1)}, bf16[8,80,2048]{2,1,0:T(8,128)(2,1)}, u32[]{:S(2)}, u32[]{:S(2)}) %collective-permute-start.47) | collective-permute-done | bytes 2621472 | tf_op jit(solution)/shard_map/ppermute | solution.py:45
  356.7 8.7 %spread.3 = (f32[1024,2048]{1,0:T(8,128)}, f32[256,2048]{1,0:T(8,128)}) custom-call(s32[8]{0:T(128)} %stack.72.refs_0_, s32[1]{0:T(128)} %bitcast.refs_1_, bf16[8,80,2048]{2,1,0:T(8,128)(2,1)} %joined.4.refs_3_.refs_2_, bf16[8,80,2048]{2,1,0:T(8,128)(2,1)} %collective-permute-done.47.refs_3_, bf16[128,2048]{1,0:T(8,128)(2,1)} %copy-done.29), custom_call_target="tpu_custom_call" | custom-call | flops 2760000000 | bytes 1000 | tf_op jit(solution)/shard_map/spread/pallas_call | solution.py:936
  367.0 8.5 %spread.4 = (f32[256,6144]{1,0:T(8,128)}, f32[256,8192]{1,0:T(8,128)}) custom-call(s32[6]{0:T(128)} %stack.69.refs_0_, s32[1]{0:T(128)} %bitcast.refs_1_, bf16[6,128,2048]{2,1,0:T(8,128)(2,1)} %bitcast.46, bf16[6,128,2048]{2,1,0:T(8,128)(2,1)} %copy-done, f32[1024,2048]{1,0:T(8,128)} %get-tuple-element.216.refs_4_, ...), custom_call_target="tpu_custom_call" | custom-call | flops 2070000000 | bytes 1000 | tf_op jit(solution)/shard_map/spread/pallas_call | solution.py:936
  380.9 4.1 %finished.1 = (bf16[128,2048]{1,0:T(8,128)(2,1)}, f32[128,2048]{1,0:T(8,128)}) custom-call(bf16[128,2048]{1,0:T(8,128)(2,1)} %get-tuple-element.113.refs_5_.refs_0_, bf16[256,2048]{1,0:T(8,128)(2,1)} %copy-done.17, bf16[256,2048]{1,0:T(8,128)(2,1)} %collective-permute-done.25.refs_3_.refs_2_, bf16[128,2048]{1,0:T(8,128)(2,1)} %copy-done.29, ...), custom_call_target="tpu_custom_call" | custom-call | flops 3449999872 | bytes 1000 | tf_op jit(solution)/shard_map/finished/pallas_call | solution.py:783
  387.0 3.8 spread.5
  (246 shorter events, 138.2 us)
Async XLA Ops:
  4.3 26.1 %collective-permute-start.1 = (bf16[2,128,2048]{2,1,0:T(8,128)(2,1)}, bf16[2,128,2048]{2,1,0:T(8,128)(2,1)}, u32[]{:S(2)}, u32[]{:S(2)}) collective-permute-start(bf16[2,128,2048]{2,1,0:T(8,128)(2,1)} %get-tuple-element.95.refs_14_.refs_22_.refs_13_.refs_1_), channel_id=1, source_target_pairs={{0,1},{1,2},{2,3},{3,0},{4,5},{5,6},{6,7},{7,4},{8,9},{9,10},{10,1... | collective-permute-start | bytes 3145736 | tf_op jit(solution)/shard_map/ppermute | solution.py:45
  6.3 26.0 %collective-permute-start.2 = (bf16[2,128,2048]{2,1,0:T(8,128)(2,1)}, bf16[2,128,2048]{2,1,0:T(8,128)(2,1)}, u32[]{:S(2)}, u32[]{:S(2)}) collective-permute-start(bf16[2,128,2048]{2,1,0:T(8,128)(2,1)} %get-tuple-element.95.refs_14_.refs_22_.refs_13_.refs_1_), channel_id=1, source_target_pairs={{0,4},{1,5},{2,6},{3,7},{4,0},{5,1},{6,2},{7,3},{8,12},{9,13},{10,... | collective-permute-start | bytes 3145736 | tf_op jit(solution)/shard_map/ppermute | solution.py:45
  8.0 36.2 %collective-permute-start = (bf16[2,128,2048]{2,1,0:T(8,128)(2,1)}, bf16[2,128,2048]{2,1,0:T(8,128)(2,1)}, u32[]{:S(2)}, u32[]{:S(2)}) collective-permute-start(bf16[2,128,2048]{2,1,0:T(8,128)(2,1)} %get-tuple-element.95.refs_14_.refs_22_.refs_13_.refs_1_), channel_id=1, source_target_pairs={{0,3},{1,0},{2,1},{3,2},{4,7},{5,4},{6,5},{7,6},{8,11},{9,8},{10,9... | collective-permute-start | bytes 3145736 | tf_op jit(solution)/shard_map/ppermute | solution.py:45
  9.4 34.8 %all-to-all-start = ((bf16[8,40,1792]{2,1,0:T(8,128)(2,1)}), bf16[8,40,1792]{2,1,0:T(8,128)(2,1)S(1)}, u32[]{:S(2)}, u32[]{:S(2)}) async-start(bf16[8,40,1792]{2,1,0:T(8,128)(2,1)} %get-tuple-element.94), calls=%async_computation | async-start | bytes 2293760 | tf_op jit(solution)/shard_map/all_to_all | solution.py:993
  30.3 40.4 %collective-permute-start.5 = (bf16[2,128,2048]{2,1,0:T(8,128)(2,1)}, bf16[2,128,2048]{2,1,0:T(8,128)(2,1)}, u32[]{:S(2)}, u32[]{:S(2)}) collective-permute-start(bf16[2,128,2048]{2,1,0:T(8,128)(2,1)} %collective-permute-done.1.refs_2_.refs_17_.refs_25_.refs_16_.refs_4_), channel_id=1, source_target_pairs={{0,1},{1,2},{2,3},{3,0},{4,5},{5,6},{6,7},{7,4},{8,9},{9,10},{10,1... | collective-permute-start | bytes 3145736 | tf_op jit(solution)/shard_map/ppermute | solution.py:45
  30.7 40.1 %collective-permute-start.7 = (bf16[2,128,2048]{2,1,0:T(8,128)(2,1)}, bf16[2,128,2048]{2,1,0:T(8,128)(2,1)S(1)}, u32[]{:S(2)}, u32[]{:S(2)}) collective-permute-start(bf16[2,128,2048]{2,1,0:T(8,128)(2,1)} %collective-permute-done.1.refs_2_.refs_17_.refs_25_.refs_16_.refs_4_), channel_id=1, source_target_pairs={{0,4},{1,5},{2,6},{3,7},{4,0},{5,1},{6,2},{7,3},{8,12},{9,13},{10,... | collective-permute-start | bytes 3145736 | tf_op jit(solution)/shard_map/ppermute | solution.py:45
  32.3 38.5 %collective-permute-start.6 = (bf16[2,128,2048]{2,1,0:T(8,128)(2,1)}, bf16[2,128,2048]{2,1,0:T(8,128)(2,1)S(1)}, u32[]{:S(2)}, u32[]{:S(2)}) collective-permute-start(bf16[2,128,2048]{2,1,0:T(8,128)(2,1)} %collective-permute-done.2.refs_3_.refs_18_.refs_26_.refs_17_.refs_5_), channel_id=1, source_target_pairs={{0,3},{1,0},{2,1},{3,2},{4,7},{5,4},{6,5},{7,6},{8,11},{9,8},{10,9... | collective-permute-start | bytes 3145736 | tf_op jit(solution)/shard_map/ppermute | solution.py:45
  47.6 20.0 %collective-permute-start.3 = (bf16[8,32,1792]{2,1,0:T(8,128)(2,1)}, bf16[8,32,1792]{2,1,0:T(8,128)(2,1)}, u32[]{:S(2)}, u32[]{:S(2)}) collective-permute-start(bf16[8,32,1792]{2,1,0:T(8,128)(2,1)} %get-tuple-element.97.refs_0_.refs_4_.refs_3_), channel_id=1, source_target_pairs={{0,96},{1,97},{2,98},{3,99},{4,100},{5,101},{6,102},{7,103},{8,104... | collective-permute-start | bytes 2752520 | tf_op jit(solution)/shard_map/ppermute | solution.py:45
  50.4 20.4 %collective-permute-start.4 = (bf16[8,32,1792]{2,1,0:T(8,128)(2,1)}, bf16[8,32,1792]{2,1,0:T(8,128)(2,1)}, u32[]{:S(2)}, u32[]{:S(2)}) collective-permute-start(bf16[8,32,1792]{2,1,0:T(8,128)(2,1)} %get-tuple-element.97.refs_0_.refs_4_.refs_3_), channel_id=1, source_target_pairs={{0,32},{1,33},{2,34},{3,35},{4,36},{5,37},{6,38},{7,39},{8,40},{9,... | collective-permute-start | bytes 2752520 | tf_op jit(solution)/shard_map/ppermute | solution.py:45
  76.0 26.0 %collective-permute-start.10 = (bf16[24,32,1792]{2,1,0:T(8,128)(2,1)}, bf16[24,32,1792]{2,1,0:T(8,128)(2,1)S(1)}, u32[]{:S(2)}, u32[]{:S(2)}) collective-permute-start(bf16[24,32,1792]{2,1,0:T(8,128)(2,1)} %bitcast.66), channel_id=1, source_target_pairs={{0,8},{1,9},{2,10},{3,11},{4,12},{5,13},{6,14},{7,15},{8,0},{9,1},... | collective-permute-start | bytes 8257544 | tf_op jit(solution)/shard_map/ppermute | solution.py:45
  136.1 21.2 %collective-permute-start.15 = (bf16[8,128,2048]{2,1,0:T(8,128)(2,1)}, bf16[8,128,2048]{2,1,0:T(8,128)(2,1)}, u32[]{:S(2)}, u32[]{:S(2)}) collective-permute-start(bf16[8,128,2048]{2,1,0:T(8,128)(2,1)} %get-tuple-element.103.refs_25_), channel_id=1, source_target_pairs={{0,8},{1,9},{2,10},{3,11},{4,12},{5,13},{6,14},{7,15},{8,0},{9,1},... | collective-permute-start | bytes 12582920 | tf_op jit(solution)/shard_map/ppermute | solution.py:45
  160.7 17.2 %collective-permute-start.18 = (bf16[1,128,2048]{2,1,0:T(8,128)(2,1)}, bf16[1,128,2048]{2,1,0:T(8,128)(2,1)S(1)}, u32[]{:S(2)}, u32[]{:S(2)}) collective-permute-start(bf16[1,128,2048]{2,1,0:T(8,128)(2,1)} %get-tuple-element.108.refs_13_), channel_id=1, source_target_pairs={{0,96},{1,97},{2,98},{3,99},{4,100},{5,101},{6,102},{7,103},{8,104... | collective-permute-start | bytes 1572872 | tf_op jit(solution)/shard_map/ppermute | solution.py:45
  184.4 26.2 %collective-permute-start.22 = (bf16[2,128,2048]{2,1,0:T(8,128)(2,1)}, bf16[2,128,2048]{2,1,0:T(8,128)(2,1)S(1)}, u32[]{:S(2)}, u32[]{:S(2)}) collective-permute-start(bf16[2,128,2048]{2,1,0:T(8,128)(2,1)} %get-tuple-element.111.refs_3_.refs_6_), channel_id=1, source_target_pairs={{0,32},{1,33},{2,34},{3,35},{4,36},{5,37},{6,38},{7,39},{8,40},{9,... | collective-permute-start | bytes 3145736 | tf_op jit(solution)/shard_map/ppermute | solution.py:45
  184.4 26.2 %collective-permute-start.23 = (bf16[2,128,2048]{2,1,0:T(8,128)(2,1)}, bf16[2,128,2048]{2,1,0:T(8,128)(2,1)S(1)}, u32[]{:S(2)}, u32[]{:S(2)}) collective-permute-start(bf16[2,128,2048]{2,1,0:T(8,128)(2,1)} %get-tuple-element.112.refs_7_), channel_id=1, source_target_pairs={{0,96},{1,97},{2,98},{3,99},{4,100},{5,101},{6,102},{7,103},{8,104... | collective-permute-start | bytes 3145736 | tf_op jit(solution)/shard_map/ppermute | solution.py:45
  191.8 27.7 %collective-permute-start.21 = (bf16[4,64,2048]{2,1,0:T(8,128)(2,1)}, bf16[4,64,2048]{2,1,0:T(8,128)(2,1)S(1)}, u32[]{:S(2)}, u32[]{:S(2)}) collective-permute-start(bf16[4,64,2048]{2,1,0:T(8,128)(2,1)} %away_sums.1.refs_5_), channel_id=1, source_target_pairs={{0,16},{1,17},{2,18},{3,19},{4,20},{5,21},{6,22},{7,23},{8,24},{9,... | collective-permute-start | bytes 3145736 | tf_op jit(solution)/shard_map/ppermute | solution.py:45
  204.4 34.1 %collective-permute-start.19 = (bf16[128,2048]{1,0:T(8,128)(2,1)}, bf16[128,2048]{1,0:T(8,128)(2,1)S(1)}, u32[]{:S(2)}, u32[]{:S(2)}) collective-permute-start(bf16[128,2048]{1,0:T(8,128)(2,1)} %get-tuple-element.115), channel_id=1, source_target_pairs={{0,1},{1,2},{2,3},{3,0},{4,5},{5,6},{6,7},{7,4},{8,9},{9,10},{10,1... | collective-permute-start | bytes 1572872 | tf_op jit(solution)/shard_map/ppermute | solution.py:45
  204.8 33.6 %collective-permute-start.20 = (bf16[128,2048]{1,0:T(8,128)(2,1)}, bf16[128,2048]{1,0:T(8,128)(2,1)S(1)}, u32[]{:S(2)}, u32[]{:S(2)}) collective-permute-start(bf16[128,2048]{1,0:T(8,128)(2,1)} %get-tuple-element.118), channel_id=1, source_target_pairs={{0,3},{1,0},{2,1},{3,2},{4,7},{5,4},{6,5},{7,6},{8,11},{9,8},{10,9... | collective-permute-start | bytes 1572872 | tf_op jit(solution)/shard_map/ppermute | solution.py:45
  216.3 29.8 %collective-permute-start.28 = (bf16[1,128,2048]{2,1,0:T(8,128)(2,1)}, bf16[1,128,2048]{2,1,0:T(8,128)(2,1)S(1)}, u32[]{:S(2)}, u32[]{:S(2)}) collective-permute-start(bf16[1,128,2048]{2,1,0:T(8,128)(2,1)} %get-tuple-element.123.refs_4_), channel_id=1, source_target_pairs={{0,16},{1,17},{2,18},{3,19},{4,20},{5,21},{6,22},{7,23},{8,24},{9,... | collective-permute-start | bytes 1572872 | tf_op jit(solution)/shard_map/ppermute | solution.py:45
  224.3 21.7 %collective-permute-start.26 = (bf16[32,2048]{1,0:T(8,128)(2,1)}, bf16[32,2048]{1,0:T(8,128)(2,1)S(1)}, u32[]{:S(2)}, u32[]{:S(2)}) collective-permute-start(bf16[32,2048]{1,0:T(8,128)(2,1)} %get-tuple-element.124.refs_24_), channel_id=1, source_target_pairs={{0,32},{1,33},{2,34},{3,35},{4,36},{5,37},{6,38},{7,39},{8,40},{9,... | collective-permute-start | bytes 393224 | tf_op jit(solution)/shard_map/ppermute | solution.py:45
  224.3 21.8 %collective-permute-start.27 = (bf16[32,2048]{1,0:T(8,128)(2,1)}, bf16[32,2048]{1,0:T(8,128)(2,1)S(1)}, u32[]{:S(2)}, u32[]{:S(2)}) collective-permute-start(bf16[32,2048]{1,0:T(8,128)(2,1)} %get-tuple-element.139), channel_id=1, source_target_pairs={{0,96},{1,97},{2,98},{3,99},{4,100},{5,101},{6,102},{7,103},{8,104... | collective-permute-start | bytes 393224 | tf_op jit(solution)/shard_map/ppermute | solution.py:45
  243.3 30.3 %collective-permute-start.24 = (bf16[256,2048]{1,0:T(8,128)(2,1)}, bf16[256,2048]{1,0:T(8,128)(2,1)S(1)}, u32[]{:S(2)}, u32[]{:S(2)}) collective-permute-start(bf16[256,2048]{1,0:T(8,128)(2,1)} %get-tuple-element.126.refs_33_), channel_id=1, source_target_pairs={{0,1},{1,2},{2,3},{3,0},{4,5},{5,6},{6,7},{7,4},{8,9},{9,10},{10,1... | collective-permute-start | bytes 3145736 | tf_op jit(solution)/shard_map/ppermute | solution.py:45
  243.7 30.0 %collective-permute-start.25 = (bf16[256,2048]{1,0:T(8,128)(2,1)}, bf16[256,2048]{1,0:T(8,128)(2,1)}, u32[]{:S(2)}, u32[]{:S(2)}) collective-permute-start(bf16[256,2048]{1,0:T(8,128)(2,1)} %get-tuple-element.127), channel_id=1, source_target_pairs={{0,3},{1,0},{2,1},{3,2},{4,7},{5,4},{6,5},{7,6},{8,11},{9,8},{10,9... | collective-permute-start | bytes 3145736 | tf_op jit(solution)/shard_map/ppermute | solution.py:45
  281.1 20.0 %collective-permute-start.42 = (bf16[2,80,2048]{2,1,0:T(8,128)(2,1)S(1)}, bf16[2,80,2048]{2,1,0:T(8,128)(2,1)S(1)}, u32[]{:S(2)}, u32[]{:S(2)}) collective-permute-start(bf16[2,80,2048]{2,1,0:T(8,128)(2,1)S(1)} %pad_maximum_fusion.refs_0_), channel_id=1, source_target_pairs={{0,32},{1,33},{2,34},{3,35},{4,36},{5,37},{6,38},{7,39},{8,40},{9,... | collective-permute-start | bytes 1966088 | tf_op jit(solution)/shard_map/ppermute | solution.py:45
  285.8 18.4 %collective-permute-start.41 = (bf16[2,80,2048]{2,1,0:T(8,128)(2,1)S(1)}, bf16[2,80,2048]{2,1,0:T(8,128)(2,1)S(1)}, u32[]{:S(2)}, u32[]{:S(2)}) collective-permute-start(bf16[2,80,2048]{2,1,0:T(8,128)(2,1)S(1)} %pad_maximum_fusion.refs_0_), channel_id=1, source_target_pairs={{0,96},{1,97},{2,98},{3,99},{4,100},{5,101},{6,102},{7,103},{8,104... | collective-permute-start | bytes 1966088 | tf_op jit(solution)/shard_map/ppermute | solution.py:45
  298.4 23.6 %collective-permute-start.34 = (bf16[256,2048]{1,0:T(8,128)(2,1)}, bf16[256,2048]{1,0:T(8,128)(2,1)S(1)}, u32[]{:S(2)}, u32[]{:S(2)}) collective-permute-start(bf16[256,2048]{1,0:T(8,128)(2,1)} %get-tuple-element.159.refs_2_), channel_id=1, source_target_pairs={{0,1},{1,2},{2,3},{3,0},{4,5},{5,6},{6,7},{7,4},{8,9},{9,10},{10,1... | collective-permute-start | bytes 3145736 | tf_op jit(solution)/shard_map/ppermute | solution.py:45
  298.4 23.6 %collective-permute-start.35 = (bf16[256,2048]{1,0:T(8,128)(2,1)}, bf16[256,2048]{1,0:T(8,128)(2,1)S(1)}, u32[]{:S(2)}, u32[]{:S(2)}) collective-permute-start(bf16[256,2048]{1,0:T(8,128)(2,1)} %get-tuple-element.160), channel_id=1, source_target_pairs={{0,3},{1,0},{2,1},{3,2},{4,7},{5,4},{6,5},{7,6},{8,11},{9,8},{10,9... | collective-permute-start | bytes 3145736 | tf_op jit(solution)/shard_map/ppermute | solution.py:45
  304.2 33.8 %collective-permute-start.38 = (bf16[2,128,2048]{2,1,0:T(8,128)(2,1)}, bf16[2,128,2048]{2,1,0:T(8,128)(2,1)S(1)}, u32[]{:S(2)}, u32[]{:S(2)}) collective-permute-start(bf16[2,128,2048]{2,1,0:T(8,128)(2,1)} %joined.3.refs_0_), channel_id=1, source_target_pairs={{0,32},{1,33},{2,34},{3,35},{4,36},{5,37},{6,38},{7,39},{8,40},{9,... | collective-permute-start | bytes 3145736 | tf_op jit(solution)/shard_map/ppermute | solution.py:45
  304.2 33.8 %collective-permute-start.39 = (bf16[2,128,2048]{2,1,0:T(8,128)(2,1)}, bf16[2,128,2048]{2,1,0:T(8,128)(2,1)S(1)}, u32[]{:S(2)}, u32[]{:S(2)}) collective-permute-start(bf16[2,128,2048]{2,1,0:T(8,128)(2,1)} %joined.3.refs_0_), channel_id=1, source_target_pairs={{0,96},{1,97},{2,98},{3,99},{4,100},{5,101},{6,102},{7,103},{8,104... | collective-permute-start | bytes 3145736 | tf_op jit(solution)/shard_map/ppermute | solution.py:45
  343.6 21.8 %collective-permute-start.46 = (bf16[6,128,2048]{2,1,0:T(8,128)(2,1)}, bf16[6,128,2048]{2,1,0:T(8,128)(2,1)S(1)}, u32[]{:S(2)}, u32[]{:S(2)}) collective-permute-start(bf16[6,128,2048]{2,1,0:T(8,128)(2,1)} %bitcast.45), channel_id=1, source_target_pairs={{0,8},{1,9},{2,10},{3,11},{4,12},{5,13},{6,14},{7,15},{8,0},{9,1},... | collective-permute-start | bytes 9437192 | tf_op jit(solution)/shard_map/ppermute | solution.py:45
  347.5 17.9 %collective-permute-start.36 = (bf16[128,2048]{1,0:T(8,128)(2,1)}, bf16[128,2048]{1,0:T(8,128)(2,1)}, u32[]{:S(2)}, u32[]{:S(2)}) collective-permute-start(bf16[128,2048]{1,0:T(8,128)(2,1)} %other_sums.3.refs_5_), channel_id=1, source_target_pairs={{0,4},{1,5},{2,6},{3,7},{4,0},{5,1},{6,2},{7,3},{8,12},{9,13},{10,... | collective-permute-start | bytes 1572872 | tf_op jit(solution)/shard_map/ppermute | solution.py:45
  348.3 27.3 %collective-permute-start.44 = (bf16[1,128,2048]{2,1,0:T(8,128)(2,1)}, bf16[1,128,2048]{2,1,0:T(8,128)(2,1)}, u32[]{:S(2)}, u32[]{:S(2)}) collective-permute-start(bf16[1,128,2048]{2,1,0:T(8,128)(2,1)} %get-tuple-element.163), channel_id=1, source_target_pairs={{0,32},{1,33},{2,34},{3,35},{4,36},{5,37},{6,38},{7,39},{8,40},{9,... | collective-permute-start | bytes 1572872 | tf_op jit(solution)/shard_map/ppermute | solution.py:45
  348.3 27.3 %collective-permute-start.45 = (bf16[1,128,2048]{2,1,0:T(8,128)(2,1)}, bf16[1,128,2048]{2,1,0:T(8,128)(2,1)}, u32[]{:S(2)}, u32[]{:S(2)}) collective-permute-start(bf16[1,128,2048]{2,1,0:T(8,128)(2,1)} %get-tuple-element.164), channel_id=1, source_target_pairs={{0,96},{1,97},{2,98},{3,99},{4,100},{5,101},{6,102},{7,103},{8,104... | collective-permute-start | bytes 1572872 | tf_op jit(solution)/shard_map/ppermute | solution.py:45
  (67 other events, 528.4 us)

commit v11 on v10

--- a/solution.py
+++ b/solution.py
@@ -489,23 +489,22 @@
             copy.wait()
 
         def split(part, high, lanes):
-            for z_hi in range(2):
-                at = (pl.ds(4 * z_hi, 4), high, lanes)
-
-                @pl.when(own)
-                def _(z_hi=z_hi, at=at):
-                    keep_v[at] = part[:, z_hi, 0]
-                    send_v[at] = part[:, z_hi, 1]
-
-                @pl.when(jnp.logical_not(own))
-                def _(z_hi=z_hi, at=at):
-                    keep_v[at] = part[:, z_hi, 1]
-                    send_v[at] = part[:, z_hi, 0]
+            at = (slice(None), high, lanes)
+
+            @pl.when(own)
+            def _():
+                keep_v[at] = part[:, 0]
+                send_v[at] = part[:, 1]
+
+            @pl.when(jnp.logical_not(own))
+            def _():
+                keep_v[at] = part[:, 1]
+                send_v[at] = part[:, 0]
 
         @pl.loop(0, 8)
         def _(n):
             lanes = pl.ds(pl.multiple_of(n * 256, 256), 256)
-            part = dot_rows(h1_v[:, lanes], dq_v[...]).astype(bf16).reshape(4, 2, 2, 16, 3 * head)
+            part = dot_rows(h1_v[:, lanes], dq_v[...]).astype(bf16).reshape(8, 2, 16, 3 * head)
             for third in range(3):
                 split(
                     part[..., third * head : (third + 1) * head],
@@ -515,7 +514,7 @@
 
         for copy in dy_copies:
             copy.wait()
-        part = dot_rows(ol_v[...], dy_v[...]).astype(bf16).reshape(4, 2, 2, 16, width)
+        part = dot_rows(ol_v[...], dy_v[...]).astype(bf16).reshape(8, 2, 16, width)
         split(part, pl.ds(48, 16), slice(None))
         keep_copy = pltpu.make_async_copy(keep_v, keep_hbm, sems.at[0])
         keep_copy.start()
@@ -795,15 +794,15 @@
     )(*mix, *sums, tokens, cotangent, *after)
 
 
-def packed_sums(stays, crossed, own, below, above, norm_sums, qkv_sums, up_sums, dy_sums, numbers, ff, head, after):
-    width = own.shape[1]
+def packed_sums(stays, crossed, parts, norm_sums, qkv_sums, up_sums, dy_sums, numbers, ff, head, after):
+    width = parts.shape[2]
 
     def body(*refs):
-        stay_ref, cross_ref, own_ref, below_ref, above_ref = refs[:5]
-        norm_ref, q_ref, u_ref, y_ref, number_ref, out_ref, keep_ref, small = refs[5:]
+        stay_ref, cross_ref, parts_ref = refs[:3]
+        norm_ref, q_ref, u_ref, y_ref, number_ref, out_ref, keep_ref, small = refs[3:]
         shard = number_ref[1]
         inner = (stay_ref[0].astype(f32) + cross_ref[0].astype(f32)).astype(bf16)
-        total = wide(own_ref, below_ref, above_ref).astype(bf16)
+        total = jnp.sum(parts_ref[...].astype(f32), 0).astype(bf16)
         for owner in range(8):
             mine = shard == owner
             small[...] = jnp.zeros_like(small)
@@ -829,41 +828,69 @@
 
     vmem = pl.BlockSpec(memory_space=pltpu.VMEM)
     return pl.pallas_call(
-        after_inputs(body, 10, len(after)),
+        after_inputs(body, 8, len(after)),
         out_shape=(
             jax.ShapeDtypeStruct((8, 16, 4 * head + ff), bf16),
             jax.ShapeDtypeStruct((80, width), bf16),
         ),
-        in_specs=[vmem] * 9 + [pl.BlockSpec(memory_space=pltpu.SMEM)] + anywhere(len(after)),
+        in_specs=[vmem] * 7 + [pl.BlockSpec(memory_space=pltpu.SMEM)] + anywhere(len(after)),
         out_specs=(vmem,) * 2,
         scratch_shapes=[pltpu.VMEM((16, head), f32)],
         compiler_params=kernel_params(),
         cost_estimate=cost(3),
         name="packed_sums",
-    )(stays, crossed, own, below, above, norm_sums, qkv_sums, up_sums, dy_sums, numbers, *after)
-
-
-def unpacked_sums(received, cols, after):
+    )(stays, crossed, parts, norm_sums, qkv_sums, up_sums, dy_sums, numbers, *after)
+
+
+def unpacked_sums(received, n1, n2, after):
     sources, rows, width = received.shape
-
-    def body(part_ref, out_ref):
+    cols = n1 + n2
+    total = sources * rows
+
+    def body(part_ref, up_ref, rest_ref):
         small = jnp.sum(part_ref[:, :, cols:].astype(f32), 0).astype(bf16)
-        out_ref[0] = jnp.concatenate(
-            [jnp.concatenate([part_ref[0, :, 0:cols], small], 1)]
-            + [part_ref[n] for n in range(1, sources)],
+        up_ref[0] = part_ref[:, :, n1:cols].reshape(total, n2)
+        rest_ref[0] = jnp.concatenate(
+            [jnp.concatenate([part_ref[0, :, 0:n1], small], 1)]
+            + [
+                jnp.concatenate([part_ref[n, :, 0:n1], part_ref[n, :, cols:]], 1)
+                for n in range(1, sources)
+            ],
             0,
         )
 
-    vmem = pl.BlockSpec(memory_space=pltpu.VMEM)
+    def block(size):
+        return pl.BlockSpec((1, total, size), lambda i: (i, 0, 0))
+
     return pl.pallas_call(
         after_inputs(body, 1, len(after)),
-        out_shape=jax.ShapeDtypeStruct((1, sources * rows, width), bf16),
-        in_specs=[vmem] + anywhere(len(after)),
-        out_specs=vmem,
+        out_shape=(
+            jax.ShapeDtypeStruct((8, total, n2), bf16),
+            jax.ShapeDtypeStruct((8, total, width - n2), bf16),
+        ),
+        grid=(8,),
+        in_specs=[pl.BlockSpec(received.shape, lambda i: (0, 0, 0))] + anywhere(len(after)),
+        out_specs=(block(n2), block(width - n2)),
         compiler_params=kernel_params(),
         cost_estimate=cost(3),
         name="unpacked_sums",
     )(received, *after)
+
+
+def held(array, after):
+    def body(*refs):
+        pass
+
+    return pl.pallas_call(
+        body,
+        out_shape=jax.ShapeDtypeStruct(array.shape, array.dtype),
+        in_specs=anywhere(1 + len(after)),
+        out_specs=pl.BlockSpec(memory_space=pl.ANY),
+        input_output_aliases={0: 0},
+        compiler_params=kernel_params(),
+        cost_estimate=cost(1),
+        name="held",
+    )(array, *after)
 
 
 def blocks_call(name, body, numbers, terms, outs, after, time=3):
@@ -1104,21 +1131,22 @@
     )
     from_below, from_above = move(above, y=1), move(below, y=-1)
 
-    four, part_shape = (4, 64, width), (1, 64, width)
-
-    def away_body(n_ref, keep_ref, got_ref, out_ref):
-        out_ref[...] = wide(keep_ref, got_ref).astype(bf16)
-
-    (a_away,) = blocks_call(
-        "away_sums",
-        away_body,
+    four = (4, 64, width)
+
+    def both_body(n_ref, low_keep, low_got, high_keep, high_got, out_ref):
+        out_ref[0:4] = wide(low_keep, low_got).astype(bf16)
+        out_ref[4:8] = wide(high_keep, high_got).astype(bf16)
+
+    (a_sent,) = blocks_call(
+        "both_sums",
+        both_body,
         numbers,
-        [(v, four, lambda n: 1 - n[3]) for v in (a_keep, a_got)],
-        (four,),
+        [(v, four, lambda n, half=half: half) for half in range(2) for v in (a_keep, a_got)],
+        ((8, 64, width),),
         (above,),
     )
-    a_crossed = move(a_away, h=1)
-    mix = mixed_part(active, attended, down_weight, out_weight, wide_bias, (a_away, above, below))
+    a_parts = lax.all_to_all(a_sent, "rep", 0, 0, axis_index_groups=SAME_CORE)
+    mix = mixed_part(active, attended, down_weight, out_weight, wide_bias, (a_sent, above, below))
     def norms_back(part, before, after):
         return back_norms(
             d_qkv,
@@ -1134,6 +1162,8 @@
             after,
         )
 
+    low_sums, *sums = norms_back(0, (), (mix[0],))
+
     flat, both = (128, width), (256, width)
 
     def passed_body(n_ref, up_ref, from_below, here_ref, down_ref, from_above, there_ref, up_out, down_out):
@@ -1197,57 +1227,17 @@
         [(v, pair_shape, turn(0)) for v in (keep, got)]
         + [(v, pair_shape, lambda n: 0) for v in (from_below, from_above)],
         (one, one),
-        (mix[0],),
+        (low_sums,),
     )
     crossed = move(leaves, h=1)
 
-    def around_body(n_ref, keep_ref, got_ref, crossed_ref, low_ref, high_ref, above_ref, own_ref, below_ref):
-        def part(k):
-            at = (n_ref[2] + k) % 4
-            return wide(keep_ref.at[at], got_ref.at[at], crossed_ref.at[at]).astype(bf16)
-
-        far = part(2)
-        low_ref[...] = far[:32]
-        high_ref[...] = far[32:]
-        above_ref[...] = part(1)
-        own_ref[...] = part(0)
-        below_ref[...] = part(3)
-
-    a_low, a_high, a_above, a_own, a_below = blocks_call(
-        "around_sums",
-        around_body,
-        numbers,
-        [(v, four, lambda n: n[3]) for v in (a_keep, a_got)] + [(a_crossed, four, lambda n: 0)],
-        ((32, width), (32, width), (64, width), (64, width), (64, width)),
-        (leaves,),
-    )
-    low_sums, *sums = norms_back(0, (), (a_low,))
-    mix_arrived, mix_ups = ring_middle(mix, mix_passed, (low_sums,))
-    a_low, a_high = move(a_low, y=1), move(a_high, y=-1)
-
-    def beside_body(n_ref, above_ref, below_ref, low_ref, high_ref, up_ref, down_ref):
-        up_ref[0:32] = (above_ref[0:32].astype(f32) + low_ref[...].astype(f32)).astype(bf16)
-        up_ref[32:64] = above_ref[32:64]
-        down_ref[0:32] = below_ref[0:32]
-        down_ref[32:64] = (below_ref[32:64].astype(f32) + high_ref[...].astype(f32)).astype(bf16)
-
-    a_above, a_below = blocks_call(
-        "beside_sums",
-        beside_body,
-        numbers,
-        [(v, v.shape, lambda n: 0) for v in (a_above, a_below, a_low, a_high)],
-        ((64, width), (64, width)),
-        (crossed, low_sums),
-    )
-    a_from_below, a_from_above = move(a_above, y=1), move(a_below, y=-1)
-    high_sums, *sums = norms_back(1, tuple(sums), (a_above, mix_ups))
+    mix_arrived, mix_ups = ring_middle(mix, mix_passed, (leaves,))
+    high_sums, *sums = norms_back(1, tuple(sums), (mix_ups,))
 
     part, stays = packed_sums(
         stays,
         crossed,
-        a_own,
-        a_from_below,
-        a_from_above,
+        a_parts,
         jnp.concatenate([low_sums, high_sums], 1),
         qkv_sums,
         up_sums,
@@ -1259,14 +1249,14 @@
     )
     received = lax.all_to_all(part, "shard", 0, 0)
     mix_left, mix_other, high, low = ring_end(mix, mix_arrived, (sums[6], sums[2]))
-    part = unpacked_sums(received, cols, (mix_other,))
+    stays_pair = jnp.concatenate([stays[None], move(stays[None], h=1)])
+    up, rest = unpacked_sums(received, 3 * head, ff, (mix_other, stays_pair))
     order = ((0, h), (0, 1 - h), (1, h), (1, 1 - h), (3, h), (3, 1 - h), (2, h), (2, 1 - h))
     places = jnp.stack([(y + k) % 4 * 2 + high for k, high in order]).astype(jnp.int32)
 
     sums_arrived, sums_ups = ring_middle(sums, ring_start(high, low), (received,))
     sums_left, sums_other = ring_end(sums, sums_arrived, ())
-    stays = stays[None]
-    stays = jnp.concatenate([stays, move(stays, h=1)])
+    stays = stays_pair
     below, above = move(stays, y=1), move(stays, y=-1)
     stays = joined((stays, above, below, move(below, y=1)), ())
     down_grad, out_grad = spread(
@@ -1278,39 +1268,42 @@
         (),
         (mix_left[3],),
     )
-    part = joined((part, move(part, h=1)), (sums_ups,))
-    below, above = move(part, y=1), move(part, y=-1)
-    low, high, near = halves(part, below, above, (stays, mix_left[3], sums_other))
-    far = move(low, y=1), move(high, y=-1)
-    targets = [
-        (
-            3 * width,
-            16,
-            [
-                ((third * 8 + source) * head, 16 * source, third * head, head)
-                for source in range(8)
-                for third in range(3)
-            ],
-        ),
-        (8 * ff, 16, [(source * ff, 16 * source, 3 * head, ff) for source in range(8)]),
-    ]
-    near_yours = move(near, c=1)
-    grads = spread(
-        [(near, near_yours)], places[:6], numbers[:1], targets, 8, (), (down_grad, sums_left[3])
-    )
-    far = joined(far, (grads[0],))
-    mixed, tokens_grad = finished(mix_left, sums_left, tokens, cotangent, (far,))
-    far_yours = move(far, c=1)
-    qkv_grad, up_grad = spread(
-        [(far, far_yours)],
-        places[6:],
+    mixed, tokens_grad = finished(mix_left, sums_left, tokens, cotangent, ())
+    order = jnp.arange(8, dtype=jnp.int32)
+    up = lax.all_to_all(up, "rep", 0, 0, axis_index_groups=SAME_CORE)
+    up = held(up, (stays,))
+    rest = lax.all_to_all(rest, "rep", 0, 0, axis_index_groups=SAME_CORE)
+    (up_grad,) = spread(
+        [(up, move(up, c=1))],
+        order,
         numbers[:1],
-        targets,
+        [(8 * ff, 16, [(source * ff, 16 * source, 0, ff) for source in range(8)])],
         8,
-        grads,
-        (tokens_grad,),
-    )
-    smalls = [v[:, 0:16, cols:] for v in (near, near_yours, far, far_yours)]
+        (),
+        (),
+    )
+    rest = held(rest, (down_grad, up_grad, tokens_grad))
+    rest_yours = move(rest, c=1)
+    (qkv_grad,) = spread(
+        [(rest, rest_yours)],
+        order,
+        numbers[:1],
+        [
+            (
+                3 * width,
+                16,
+                [
+                    ((third * 8 + source) * head, 16 * source, third * head, head)
+                    for source in range(8)
+                    for third in range(3)
+                ],
+            )
+        ],
+        8,
+        (),
+        (),
+    )
+    smalls = [v[:, 0:16, 3 * head :] for v in (rest, rest_yours)]
     smalls = jnp.sum(jnp.concatenate(smalls).astype(f32), 0)
     norm_grads = smalls[:4]
     dy_total = smalls[11]

time: 398 us -> 434 us (1.090)
  waiting for transfers between devices: 87.8 us -> 130 us
  Pallas kernels: 183 us -> 176 us
  local copies, waits for them, and re-layouts: 33.7 us -> 29.2 us
    ppermute x49 -> x39, waiting for transfers between devices: 78.3 us -> 121 us  [move(): return lax.ppermute(value, BOTH, pairs)]
    all_to_all x0 -> x3, starting transfers between devices: none -> 13.9 us  [the longest x1 5.4 us: local(): rest = lax.all_to_all(rest, 'rep', 0, 0, axis_index_groups=SAME_CORE)]
    ppermute x49 -> x39, starting transfers between devices: 70.1 us -> 59.2 us  [move(): return lax.ppermute(value, BOTH, pairs)]
    pallas_call x10 -> x8, Pallas kernels: 36.8 us -> 31.5 us  [blocks_call(): pl.pallas_call(after_inputs(body, 1 + len(terms), len(after)), out_shape=...]
    pallas_call x3 -> x1, Pallas kernels: 8.16 us -> 3.67 us  [joined(): pl.pallas_call(after_inputs(body, count, len(after)), out_shape=jax.Shape...]
    unnamed x103 -> x83, local copies, waits for them, and re-layouts: 23.7 us -> 20.2 us
  transfers between devices with their start and end apart: 51 -> 44, of which waited for: 14 -> 14; matrix products, arithmetic and copies ran while one was open for 5% -> 4% of each run, Pallas kernels for 33% -> 29%
where the time goes in v11:
time: 434 us; the launch traced here: 427 us
  Pallas kernels  176 us (41%)
  waiting for transfers between devices  130 us (30%)
  starting transfers between devices  80.2 us (18%)
  local copies, waits for them, and re-layouts  29.2 us (7%)
  other arithmetic  9.85 us (2%)
    ppermute x39, waiting for transfers between devices, move(): return lax.ppermute(value, BOTH, pairs)  121 us
    ppermute x39, starting transfers between devices, move(): return lax.ppermute(value, BOTH, pairs)  59.2 us
    pallas_call x1, Pallas kernels, feed_forward(): pl.pallas_call(after_inputs(body, 5 + parts + 2 * count, len(after)), out...  32.2 us
    pallas_call x8, Pallas kernels, blocks_call(): pl.pallas_call(after_inputs(body, 1 + len(terms), len(after)), out_shape=...  31.5 us
    pallas_call x3, Pallas kernels, spread(): pl.pallas_call(after_inputs(body, 2 + 2 * len(pieces) + len(before), len(...  24.2 us
    pallas_call x2, Pallas kernels, back_norms(): pl.pallas_call(after_inputs(body, 6 + parts + count + len(before), len(af...  22.8 us
    unnamed x83, local copies, waits for them, and re-layouts  20.2 us
    pallas_call x1, Pallas kernels, attend(): pl.pallas_call(after_inputs(body, 7 + parts + count, len(after)), out_sha...  17.2 us
  transfers between devices with their start and end apart: 44, of which 14 were waited for; matrix products, arithmetic and copies ran while one was open for 4% of the time, Pallas kernels for 29%

profile of v11, /device:TPU:1, one launch (start us, length us, event | category | flops | bytes accessed | tf_op | source)
XLA Modules:
  0.0 427.1 jit_solution(11621475657168128057)
XLA Ops:
  13.0 17.3 %collective-permute-done.1.refs_2_.refs_17_.refs_25_.refs_16_.refs_4_ = bf16[2,128,2048]{2,1,0:T(8,128)(2,1)} collective-permute-done((bf16[2,128,2048]{2,1,0:T(8,128)(2,1)}, bf16[2,128,2048]{2,1,0:T(8,128)(2,1)}, u32[]{:S(2)}, u32[]{:S(2)}) %collective-permute-start.1) | collective-permute-done | bytes 1048608 | tf_op jit(solution)/shard_map/ppermute | solution.py:45
  35.0 9.2 %all-to-all-done.refs_0_ = bf16[8,40,1792]{2,1,0:T(8,128)(2,1)S(1)} async-done(((bf16[8,40,1792]{2,1,0:T(8,128)(2,1)}), bf16[8,40,1792]{2,1,0:T(8,128)(2,1)S(1)}, u32[]{:S(2)}, u32[]{:S(2)}) %all-to-all-start) | async-done | bytes 1146912 | tf_op jit(solution)/shard_map/all_to_all | solution.py:1020
  51.6 16.1 %collective-permute-done.3.refs_2_.refs_5_.refs_4_ = bf16[8,32,1792]{2,1,0:T(8,128)(2,1)S(1)} collective-permute-done((bf16[8,32,1792]{2,1,0:T(8,128)(2,1)}, bf16[8,32,1792]{2,1,0:T(8,128)(2,1)S(1)}, u32[]{:S(2)}, u32[]{:S(2)}) %collective-permute-start.3) | collective-permute-done | bytes 917536 | tf_op jit(solution)/shard_map/ppermute | solution.py:45
  75.9 3.9 collective-permute-start.10
  91.4 5.2 %collective-permute-done.8.refs_6_.refs_5_ = bf16[4,32,1792]{2,1,0:T(8,128)(2,1)S(1)} collective-permute-done((bf16[4,32,1792]{2,1,0:T(8,128)(2,1)}, bf16[4,32,1792]{2,1,0:T(8,128)(2,1)S(1)}, u32[]{:S(2)}, u32[]{:S(2)}) %collective-permute-start.8) | collective-permute-done | bytes 458784 | tf_op jit(solution)/shard_map/ppermute | solution.py:45
  103.8 32.2 %feed_forward.1 = (bf16[1024,2048]{1,0:T(8,128)(2,1)}, bf16[1024,1024]{1,0:T(8,128)(2,1)}, bf16[1024,1024]{1,0:T(8,128)(2,1)}, bf16[8,128,2048]{2,1,0:T(8,128)(2...) custom-call(s32[4]{0:T(128)} %get-tuple-element.162.refs_0_.refs_7_,, ...), custom_call_target="tpu_custom_call" | custom-call | flops 36800000000 | bytes 1000 | tf_op jit(solution)/shard_map/feed_forward/pallas_call | solution.py:258
  140.1 17.2 %attend.1 = (bf16[1024,256]{1,0:T(8,128)(2,1)}, bf16[1024,768]{1,0:T(8,128)(2,1)}, f32[1,768]{1,0:T(1,128)}) custom-call(s32[8,3]{1,0:T(8,128)} %copy-done.7, s32[8]{0:T(128)} %pad_add_fusion.1.refs_1_.refs_0_, f32[3,1,256]{2,1,0:T(1,128)} %pad_maximum_fusion.3.refs_2_, bf16[8,32,1792]{2,1,0:T(8,128)(2,1)} %get-tuple-element.85.refs_0_.refs_4_.refs_3_, ...), custom_call_target="tpu_custom_call" | custom-call | flops 19549999104 | bytes 1000 | tf_op jit(solution)/shard_map/attend/pallas_call | solution.py:431
  163.3 13.6 %attention_grads.1 = (bf16[8,64,2048]{2,1,0:T(8,128)(2,1)}, bf16[8,64,2048]{2,1,0:T(8,128)(2,1)}) custom-call(s32[4]{0:T(128)} %get-tuple-element.162.refs_0_.refs_7_, bf16[2,128,2048]{2,1,0:T(8,128)(2,1)} %get-tuple-element.83.refs_14_.refs_22_.refs_13_.refs_1_, bf16[2,128,2048]{2,1,0:T(8,128)(2,1)} %collective-permute-done.refs_1_.refs_15_.refs_23_.refs_14_.refs_2_, ...), custom_call_target="tpu_custom_call" | custom-call | flops 13799999488 | bytes 1000 | tf_op jit(solution)/shard_map/attention_grads/pallas_call | solution.py:527
  179.4 4.8 %near_sums.1 = (bf16[2,128,2048]{2,1,0:T(8,128)(2,1)}, bf16[2,128,2048]{2,1,0:T(8,128)(2,1)}) custom-call(s32[4]{0:T(128)} %get-tuple-element.162.refs_0_.refs_7_, bf16[8,128,2048]{2,1,0:T(8,128)(2,1)} %get-tuple-element.94.refs_1_.refs_3_, bf16[8,128,2048]{2,1,0:T(8,128)(2,1)} %collective-permute-done.15.refs_2_.refs_4_, ...), custom_call_target="tpu_custom_call" | custom-call | flops 23000000512 | bytes 1000 | tf_op jit(solution)/shard_map/near_sums/pallas_call | solution.py:901
  188.2 4.6 %both_sums.1.refs_5_ = bf16[8,64,2048]{2,1,0:T(8,128)(2,1)} custom-call(s32[4]{0:T(128)} %get-tuple-element.162.refs_0_.refs_7_, bf16[8,64,2048]{2,1,0:T(8,128)(2,1)} %get-tuple-element.97.refs_1_.refs_3_, bf16[8,64,2048]{2,1,0:T(8,128)(2,1)} %copy-done.15, bf16[8,64,2048]{2,1,0:T(8,128)(2,1)} %get-tuple-element.97.refs_1_.refs_3_, ...), custom_call_target="tpu_custom_call" | custom-call | flops 3449999872 | bytes 1000 | tf_op jit(solution)/shard_map/both_sums/pallas_call | solution.py:901
  192.8 4.5 %all-to-all-start.1 = ((bf16[8,64,2048]{2,1,0:T(8,128)(2,1)}), bf16[8,64,2048]{2,1,0:T(8,128)(2,1)S(1)}, u32[]{:S(2)}, u32[]{:S(2)}) async-start(bf16[8,64,2048]{2,1,0:T(8,128)(2,1)} %both_sums.1.refs_5_), calls=%async_computation.1 | async-start | bytes 4194304 | tf_op jit(solution)/shard_map/all_to_all | solution.py:1148
  197.3 9.3 %mixed_part.1 = (bf16[128,2048]{1,0:T(8,128)(2,1)}, bf16[128,2048]{1,0:T(8,128)(2,1)}, bf16[128,2048]{1,0:T(8,128)(2,1)}, bf16[128,2048]{1,0:T(8,128)(2,1)}, bf1...) custom-call(bf16[1024,1024]{1,0:T(8,128)(2,1)} %get-tuple-element.89., ...), custom_call_target="tpu_custom_call" | custom-call | flops 11500000256 | bytes 1000 | tf_op jit(solution)/shard_map/mixed_part/pallas_call | solution.py:559
  209.5 11.4 %back_norms.2 = (f32[4,1024]{1,0:T(4,128)}, bf16[128,2048]{1,0:T(8,128)(2,1)}, bf16[128,2048]{1,0:T(8,128)(2,1)}, bf16[128,2048]{1,0:T(8,128)(2,1)}, bf16[128,20...) custom-call(s32[8]{0:T(128)} %pad_add_fusion.1.refs_1_.refs_0_, ...), custom_call_target="tpu_custom_call" | custom-call | flops 10350000128 | bytes 1000 | tf_op jit(solution)/shard_map/back_norms/pallas_call | solution.py:635
  221.9 4.4 %end_sums.1 = (bf16[1,128,2048]{2,1,0:T(8,128)(2,1)}, bf16[1,128,2048]{2,1,0:T(8,128)(2,1)}) custom-call(s32[4]{0:T(128)} %get-tuple-element.162.refs_0_.refs_7_, bf16[8,128,2048]{2,1,0:T(8,128)(2,1)} %get-tuple-element.94.refs_1_.refs_3_, bf16[8,128,2048]{2,1,0:T(8,128)(2,1)} %collective-permute-done.15.refs_2_.refs_4_, bf16[2,128,2048]{2,1,0:T(8,128)(2,1)} %copy-done.17, ...), custom_call_target="tpu_custom_call" | custom-call | flops 3449999872 | bytes 1000 | tf_op jit(solution)/shard_map/end_sums/pallas_call | solution.py:901
  230.1 3.9 passed_sums.2
  236.8 11.4 %back_norms.3 = (f32[4,1024]{1,0:T(4,128)}, bf16[128,2048]{1,0:T(8,128)(2,1)}, bf16[128,2048]{1,0:T(8,128)(2,1)}, bf16[128,2048]{1,0:T(8,128)(2,1)}, bf16[128,20...) custom-call(s32[8]{0:T(128)} %pad_add_fusion.1.refs_1_.refs_0_, ...), custom_call_target="tpu_custom_call", output_to_operand_aliasing={{1}: (24, {}), {2}: (25, {}), {3}: (26, {}), {4}: (27, {}),... | custom-call | flops 10350000128 | bytes 1000 | tf_op jit(solution)/shard_map/back_norms/pallas_call | solution.py:635
  258.1 5.0 %collective-permute-done.32 = bf16[1,80,2048]{2,1,0:T(8,128)(2,1)S(1)} collective-permute-done((bf16[1,80,2048]{2,1,0:T(8,128)(2,1)}, bf16[1,80,2048]{2,1,0:T(8,128)(2,1)S(1)}, u32[]{:S(2)}, u32[]{:S(2)}) %collective-permute-start.32) | collective-permute-done | bytes 327712 | tf_op jit(solution)/shard_map/ppermute | solution.py:45
  270.5 4.5 %unpacked_sums.1 = (bf16[8,128,1024]{2,1,0:T(8,128)(2,1)}, bf16[8,128,1024]{2,1,0:T(8,128)(2,1)}) custom-call(bf16[8,16,2048]{2,1,0:T(8,128)(2,1)} %copy-done.5, bf16[128,2048]{1,0:T(8,128)(2,1)} %get-tuple-element.126.refs_1_, bf16[2,80,2048]{2,1,0:T(8,128)(2,1)} %pad_maximum_fusion.refs_2_.refs_0_), custom_call_target="tpu_custom_call" | custom-call | flops 3449999872 | bytes 1000 | tf_op jit(solution)/shard_map/unpacked_sums/pallas_call | solution.py:865
  275.0 4.0 all-to-all-start.4
  284.4 25.6 %collective-permute-done.33.refs_1_ = bf16[2,80,2048]{2,1,0:T(8,128)(2,1)S(1)} collective-permute-done((bf16[2,80,2048]{2,1,0:T(8,128)(2,1)}, bf16[2,80,2048]{2,1,0:T(8,128)(2,1)S(1)}, u32[]{:S(2)}, u32[]{:S(2)}) %collective-permute-start.33) | collective-permute-done | bytes 655392 | tf_op jit(solution)/shard_map/ppermute | solution.py:45
  309.9 3.9 collective-permute-done.35.refs_3_
  314.7 3.7 joined.1.refs_2_.refs_1_
  318.4 7.9 %collective-permute-start.36 = (bf16[8,80,2048]{2,1,0:T(8,128)(2,1)}, bf16[8,80,2048]{2,1,0:T(8,128)(2,1)}, u32[]{:S(2)}, u32[]{:S(2)}) collective-permute-start(bf16[8,80,2048]{2,1,0:T(8,128)(2,1)} %joined.1.refs_2_.refs_1_), channel_id=1, source_target_pairs={{0,8},{1,9},{2,10},{3,11},{4,12},{5,13},{6,14},{7,15},{8,0},{9,1},... | collective-permute-start | bytes 7864328 | tf_op jit(solution)/shard_map/ppermute | solution.py:45
  327.2 3.9 passed_sums.3
  335.9 5.4 %all-to-all-start.3 = ((bf16[8,128,1024]{2,1,0:T(8,128)(2,1)}), bf16[8,128,1024]{2,1,0:T(8,128)(2,1)S(1)}, u32[]{:S(2)}, u32[]{:S(2)}) async-start(bf16[8,128,1024]{2,1,0:T(8,128)(2,1)} %get-tuple-element.146), calls=%async_computation.3 | async-start | bytes 4194304 | tf_op jit(solution)/shard_map/all_to_all | solution.py:1275
  341.8 15.6 %collective-permute-done.29.refs_2_.refs_5_ = bf16[256,2048]{1,0:T(8,128)(2,1)S(1)} collective-permute-done((bf16[256,2048]{1,0:T(8,128)(2,1)}, bf16[256,2048]{1,0:T(8,128)(2,1)S(1)}, u32[]{:S(2)}, u32[]{:S(2)}) %collective-permute-start.29) | collective-permute-done | bytes 1048608 | tf_op jit(solution)/shard_map/ppermute | solution.py:45
  362.6 14.1 %collective-permute-done.25.refs_3_.refs_4_ = bf16[128,2048]{1,0:T(8,128)(2,1)} collective-permute-done((bf16[128,2048]{1,0:T(8,128)(2,1)}, bf16[128,2048]{1,0:T(8,128)(2,1)}, u32[]{:S(2)}, u32[]{:S(2)}) %collective-permute-start.25) | collective-permute-done | bytes 524320 | tf_op jit(solution)/shard_map/ppermute | solution.py:45
  376.7 11.1 %collective-permute-done.31.refs_7_ = bf16[128,2048]{1,0:T(8,128)(2,1)S(1)} collective-permute-done((bf16[128,2048]{1,0:T(8,128)(2,1)}, bf16[128,2048]{1,0:T(8,128)(2,1)S(1)}, u32[]{:S(2)}, u32[]{:S(2)}) %collective-permute-start.31) | collective-permute-done | bytes 524320 | tf_op jit(solution)/shard_map/ppermute | solution.py:45
  388.6 4.1 finished.1
  392.8 8.7 %spread.3 = (f32[1024,2048]{1,0:T(8,128)}, f32[256,2048]{1,0:T(8,128)}) custom-call(s32[8]{0:T(128)} %stack.67.refs_0_, s32[1]{0:T(128)} %bitcast.refs_1_, bf16[8,80,2048]{2,1,0:T(8,128)(2,1)} %joined.1.refs_2_.refs_1_, bf16[8,80,2048]{2,1,0:T(8,128)(2,1)} %collective-permute-done.36.refs_3_, bf16[128,2048]{1,0:T(8,128)(2,1)} %collective-permute-done.25.refs_3_.refs_4_), custom_call_target="tpu_custom_call" | custom-call | flops 2760000000 | bytes 1000 | tf_op jit(solution)/shard_map/spread/pallas_call | solution.py:963
  402.0 7.9 %spread.4.refs_2_ = f32[256,8192]{1,0:T(8,128)} custom-call(s32[8]{0:T(128)} %iota.49.refs_0_, s32[1]{0:T(128)} %bitcast.refs_1_, bf16[8,128,1024]{2,1,0:T(8,128)(2,1)} %held.2.refs_2_, bf16[8,128,1024]{2,1,0:T(8,128)(2,1)} %collective-permute-done.37.refs_3_), custom_call_target="tpu_custom_call" | custom-call | flops 2760000000 | bytes 1000 | tf_op jit(solution)/shard_map/spread/pallas_call | solution.py:963
  418.5 7.6 %spread.5 = f32[256,6144]{1,0:T(8,128)} custom-call(s32[8]{0:T(128)} %iota.50.refs_0_, s32[1]{0:T(128)} %bitcast.refs_1_, bf16[8,128,1024]{2,1,0:T(8,128)(2,1)} %held.3.refs_2_, bf16[8,128,1024]{2,1,0:T(8,128)(2,1)} %copy-done.2), custom_call_target="tpu_custom_call" | custom-call | flops 2760000000 | bytes 1000 | tf_op jit(solution)/shard_map/spread/pallas_call | solution.py:963
  (207 shorter events, 123.5 us)
Async XLA Ops:
  4.3 26.1 %collective-permute-start.1 = (bf16[2,128,2048]{2,1,0:T(8,128)(2,1)}, bf16[2,128,2048]{2,1,0:T(8,128)(2,1)}, u32[]{:S(2)}, u32[]{:S(2)}) collective-permute-start(bf16[2,128,2048]{2,1,0:T(8,128)(2,1)} %get-tuple-element.83.refs_14_.refs_22_.refs_13_.refs_1_), channel_id=1, source_target_pairs={{0,1},{1,2},{2,3},{3,0},{4,5},{5,6},{6,7},{7,4},{8,9},{9,10},{10,1... | collective-permute-start | bytes 3145736 | tf_op jit(solution)/shard_map/ppermute | solution.py:45
  6.3 26.0 %collective-permute-start.2 = (bf16[2,128,2048]{2,1,0:T(8,128)(2,1)}, bf16[2,128,2048]{2,1,0:T(8,128)(2,1)}, u32[]{:S(2)}, u32[]{:S(2)}) collective-permute-start(bf16[2,128,2048]{2,1,0:T(8,128)(2,1)} %get-tuple-element.83.refs_14_.refs_22_.refs_13_.refs_1_), channel_id=1, source_target_pairs={{0,4},{1,5},{2,6},{3,7},{4,0},{5,1},{6,2},{7,3},{8,12},{9,13},{10,... | collective-permute-start | bytes 3145736 | tf_op jit(solution)/shard_map/ppermute | solution.py:45
  8.0 36.2 %collective-permute-start = (bf16[2,128,2048]{2,1,0:T(8,128)(2,1)}, bf16[2,128,2048]{2,1,0:T(8,128)(2,1)}, u32[]{:S(2)}, u32[]{:S(2)}) collective-permute-start(bf16[2,128,2048]{2,1,0:T(8,128)(2,1)} %get-tuple-element.83.refs_14_.refs_22_.refs_13_.refs_1_), channel_id=1, source_target_pairs={{0,3},{1,0},{2,1},{3,2},{4,7},{5,4},{6,5},{7,6},{8,11},{9,8},{10,9... | collective-permute-start | bytes 3145736 | tf_op jit(solution)/shard_map/ppermute | solution.py:45
  9.4 34.8 %all-to-all-start = ((bf16[8,40,1792]{2,1,0:T(8,128)(2,1)}), bf16[8,40,1792]{2,1,0:T(8,128)(2,1)S(1)}, u32[]{:S(2)}, u32[]{:S(2)}) async-start(bf16[8,40,1792]{2,1,0:T(8,128)(2,1)} %get-tuple-element.82), calls=%async_computation | async-start | bytes 2293760 | tf_op jit(solution)/shard_map/all_to_all | solution.py:1020
  30.3 40.3 %collective-permute-start.5 = (bf16[2,128,2048]{2,1,0:T(8,128)(2,1)}, bf16[2,128,2048]{2,1,0:T(8,128)(2,1)}, u32[]{:S(2)}, u32[]{:S(2)}) collective-permute-start(bf16[2,128,2048]{2,1,0:T(8,128)(2,1)} %collective-permute-done.1.refs_2_.refs_17_.refs_25_.refs_16_.refs_4_), channel_id=1, source_target_pairs={{0,1},{1,2},{2,3},{3,0},{4,5},{5,6},{6,7},{7,4},{8,9},{9,10},{10,1... | collective-permute-start | bytes 3145736 | tf_op jit(solution)/shard_map/ppermute | solution.py:45
  30.7 40.0 %collective-permute-start.7 = (bf16[2,128,2048]{2,1,0:T(8,128)(2,1)}, bf16[2,128,2048]{2,1,0:T(8,128)(2,1)S(1)}, u32[]{:S(2)}, u32[]{:S(2)}) collective-permute-start(bf16[2,128,2048]{2,1,0:T(8,128)(2,1)} %collective-permute-done.1.refs_2_.refs_17_.refs_25_.refs_16_.refs_4_), channel_id=1, source_target_pairs={{0,4},{1,5},{2,6},{3,7},{4,0},{5,1},{6,2},{7,3},{8,12},{9,13},{10,... | collective-permute-start | bytes 3145736 | tf_op jit(solution)/shard_map/ppermute | solution.py:45
  32.3 38.4 %collective-permute-start.6 = (bf16[2,128,2048]{2,1,0:T(8,128)(2,1)}, bf16[2,128,2048]{2,1,0:T(8,128)(2,1)}, u32[]{:S(2)}, u32[]{:S(2)}) collective-permute-start(bf16[2,128,2048]{2,1,0:T(8,128)(2,1)} %collective-permute-done.2.refs_3_.refs_18_.refs_26_.refs_17_.refs_5_), channel_id=1, source_target_pairs={{0,3},{1,0},{2,1},{3,2},{4,7},{5,4},{6,5},{7,6},{8,11},{9,8},{10,9... | collective-permute-start | bytes 3145736 | tf_op jit(solution)/shard_map/ppermute | solution.py:45
  47.6 20.0 %collective-permute-start.3 = (bf16[8,32,1792]{2,1,0:T(8,128)(2,1)}, bf16[8,32,1792]{2,1,0:T(8,128)(2,1)S(1)}, u32[]{:S(2)}, u32[]{:S(2)}) collective-permute-start(bf16[8,32,1792]{2,1,0:T(8,128)(2,1)} %get-tuple-element.85.refs_0_.refs_4_.refs_3_), channel_id=1, source_target_pairs={{0,96},{1,97},{2,98},{3,99},{4,100},{5,101},{6,102},{7,103},{8,104... | collective-permute-start | bytes 2752520 | tf_op jit(solution)/shard_map/ppermute | solution.py:45
  50.4 20.3 %collective-permute-start.4 = (bf16[8,32,1792]{2,1,0:T(8,128)(2,1)}, bf16[8,32,1792]{2,1,0:T(8,128)(2,1)S(1)}, u32[]{:S(2)}, u32[]{:S(2)}) collective-permute-start(bf16[8,32,1792]{2,1,0:T(8,128)(2,1)} %get-tuple-element.85.refs_0_.refs_4_.refs_3_), channel_id=1, source_target_pairs={{0,32},{1,33},{2,34},{3,35},{4,36},{5,37},{6,38},{7,39},{8,40},{9,... | collective-permute-start | bytes 2752520 | tf_op jit(solution)/shard_map/ppermute | solution.py:45
  75.9 26.0 %collective-permute-start.10 = (bf16[24,32,1792]{2,1,0:T(8,128)(2,1)}, bf16[24,32,1792]{2,1,0:T(8,128)(2,1)S(1)}, u32[]{:S(2)}, u32[]{:S(2)}) collective-permute-start(bf16[24,32,1792]{2,1,0:T(8,128)(2,1)} %bitcast.62), channel_id=1, source_target_pairs={{0,8},{1,9},{2,10},{3,11},{4,12},{5,13},{6,14},{7,15},{8,0},{9,1},... | collective-permute-start | bytes 8257544 | tf_op jit(solution)/shard_map/ppermute | solution.py:45
  136.0 21.3 %collective-permute-start.15 = (bf16[8,128,2048]{2,1,0:T(8,128)(2,1)}, bf16[8,128,2048]{2,1,0:T(8,128)(2,1)}, u32[]{:S(2)}, u32[]{:S(2)}) collective-permute-start(bf16[8,128,2048]{2,1,0:T(8,128)(2,1)} %get-tuple-element.91.refs_25_), channel_id=1, source_target_pairs={{0,8},{1,9},{2,10},{3,11},{4,12},{5,13},{6,14},{7,15},{8,0},{9,1},... | collective-permute-start | bytes 12582920 | tf_op jit(solution)/shard_map/ppermute | solution.py:45
  160.7 17.1 %collective-permute-start.18 = (bf16[1,128,2048]{2,1,0:T(8,128)(2,1)}, bf16[1,128,2048]{2,1,0:T(8,128)(2,1)S(1)}, u32[]{:S(2)}, u32[]{:S(2)}) collective-permute-start(bf16[1,128,2048]{2,1,0:T(8,128)(2,1)} %get-tuple-element.96.refs_13_), channel_id=1, source_target_pairs={{0,96},{1,97},{2,98},{3,99},{4,100},{5,101},{6,102},{7,103},{8,104... | collective-permute-start | bytes 1572872 | tf_op jit(solution)/shard_map/ppermute | solution.py:45
  184.2 36.7 %collective-permute-start.21 = (bf16[2,128,2048]{2,1,0:T(8,128)(2,1)}, bf16[2,128,2048]{2,1,0:T(8,128)(2,1)S(1)}, u32[]{:S(2)}, u32[]{:S(2)}) collective-permute-start(bf16[2,128,2048]{2,1,0:T(8,128)(2,1)} %get-tuple-element.99.refs_5_.refs_6_), channel_id=1, source_target_pairs={{0,32},{1,33},{2,34},{3,35},{4,36},{5,37},{6,38},{7,39},{8,40},{9,... | collective-permute-start | bytes 3145736 | tf_op jit(solution)/shard_map/ppermute | solution.py:45
  184.2 36.7 %collective-permute-start.22 = (bf16[2,128,2048]{2,1,0:T(8,128)(2,1)}, bf16[2,128,2048]{2,1,0:T(8,128)(2,1)}, u32[]{:S(2)}, u32[]{:S(2)}) collective-permute-start(bf16[2,128,2048]{2,1,0:T(8,128)(2,1)} %get-tuple-element.100.refs_7_), channel_id=1, source_target_pairs={{0,96},{1,97},{2,98},{3,99},{4,100},{5,101},{6,102},{7,103},{8,104... | collective-permute-start | bytes 3145736 | tf_op jit(solution)/shard_map/ppermute | solution.py:45
  192.8 56.7 %all-to-all-start.1 = ((bf16[8,64,2048]{2,1,0:T(8,128)(2,1)}), bf16[8,64,2048]{2,1,0:T(8,128)(2,1)S(1)}, u32[]{:S(2)}, u32[]{:S(2)}) async-start(bf16[8,64,2048]{2,1,0:T(8,128)(2,1)} %both_sums.1.refs_5_), calls=%async_computation.1 | async-start | bytes 4194304 | tf_op jit(solution)/shard_map/all_to_all | solution.py:1148
  206.6 22.6 %collective-permute-start.19 = (bf16[128,2048]{1,0:T(8,128)(2,1)}, bf16[128,2048]{1,0:T(8,128)(2,1)S(1)}, u32[]{:S(2)}, u32[]{:S(2)}) collective-permute-start(bf16[128,2048]{1,0:T(8,128)(2,1)} %get-tuple-element.103), channel_id=1, source_target_pairs={{0,1},{1,2},{2,3},{3,0},{4,5},{5,6},{6,7},{7,4},{8,9},{9,10},{10,1... | collective-permute-start | bytes 1572872 | tf_op jit(solution)/shard_map/ppermute | solution.py:45
  207.1 22.1 %collective-permute-start.20 = (bf16[128,2048]{1,0:T(8,128)(2,1)}, bf16[128,2048]{1,0:T(8,128)(2,1)S(1)}, u32[]{:S(2)}, u32[]{:S(2)}) collective-permute-start(bf16[128,2048]{1,0:T(8,128)(2,1)} %get-tuple-element.106), channel_id=1, source_target_pairs={{0,3},{1,0},{2,1},{3,2},{4,7},{5,4},{6,5},{7,6},{8,11},{9,8},{10,9... | collective-permute-start | bytes 1572872 | tf_op jit(solution)/shard_map/ppermute | solution.py:45
  226.2 23.3 %collective-permute-start.28 = (bf16[1,128,2048]{2,1,0:T(8,128)(2,1)}, bf16[1,128,2048]{2,1,0:T(8,128)(2,1)S(1)}, u32[]{:S(2)}, u32[]{:S(2)}) collective-permute-start(bf16[1,128,2048]{2,1,0:T(8,128)(2,1)} %get-tuple-element.112.refs_7_), channel_id=1, source_target_pairs={{0,16},{1,17},{2,18},{3,19},{4,20},{5,21},{6,22},{7,23},{8,24},{9,... | collective-permute-start | bytes 1572872 | tf_op jit(solution)/shard_map/ppermute | solution.py:45
  234.1 32.1 %collective-permute-start.23 = (bf16[256,2048]{1,0:T(8,128)(2,1)}, bf16[256,2048]{1,0:T(8,128)(2,1)}, u32[]{:S(2)}, u32[]{:S(2)}) collective-permute-start(bf16[256,2048]{1,0:T(8,128)(2,1)} %get-tuple-element.113.refs_32_), channel_id=1, source_target_pairs={{0,1},{1,2},{2,3},{3,0},{4,5},{5,6},{6,7},{7,4},{8,9},{9,10},{10,1... | collective-permute-start | bytes 3145736 | tf_op jit(solution)/shard_map/ppermute | solution.py:45
  234.1 32.1 %collective-permute-start.24 = (bf16[256,2048]{1,0:T(8,128)(2,1)}, bf16[256,2048]{1,0:T(8,128)(2,1)}, u32[]{:S(2)}, u32[]{:S(2)}) collective-permute-start(bf16[256,2048]{1,0:T(8,128)(2,1)} %get-tuple-element.114), channel_id=1, source_target_pairs={{0,3},{1,0},{2,1},{3,2},{4,7},{5,4},{6,5},{7,6},{8,11},{9,8},{10,9... | collective-permute-start | bytes 3145736 | tf_op jit(solution)/shard_map/ppermute | solution.py:45
  275.0 58.9 %all-to-all-start.4 = ((bf16[8,128,1024]{2,1,0:T(8,128)(2,1)}), bf16[8,128,1024]{2,1,0:T(8,128)(2,1)S(1)}, u32[]{:S(2)}, u32[]{:S(2)}) async-start(bf16[8,128,1024]{2,1,0:T(8,128)(2,1)} %get-tuple-element.148), calls=%async_computation.4 | async-start | bytes 4194304 | tf_op jit(solution)/shard_map/all_to_all | solution.py:1273
  279.0 30.9 %collective-permute-start.33 = (bf16[2,80,2048]{2,1,0:T(8,128)(2,1)}, bf16[2,80,2048]{2,1,0:T(8,128)(2,1)S(1)}, u32[]{:S(2)}, u32[]{:S(2)}) collective-permute-start(bf16[2,80,2048]{2,1,0:T(8,128)(2,1)} %pad_maximum_fusion.refs_2_.refs_0_), channel_id=1, source_target_pairs={{0,96},{1,97},{2,98},{3,99},{4,100},{5,101},{6,102},{7,103},{8,104... | collective-permute-start | bytes 1966088 | tf_op jit(solution)/shard_map/ppermute | solution.py:45
  281.6 32.2 %collective-permute-start.35 = (bf16[2,80,2048]{2,1,0:T(8,128)(2,1)S(1)}, bf16[2,80,2048]{2,1,0:T(8,128)(2,1)S(1)}, u32[]{:S(2)}, u32[]{:S(2)}) collective-permute-start(bf16[2,80,2048]{2,1,0:T(8,128)(2,1)S(1)} %collective-permute-done.34.refs_2_), channel_id=1, source_target_pairs={{0,32},{1,33},{2,34},{3,35},{4,36},{5,37},{6,38},{7,39},{8,40},{9,... | collective-permute-start | bytes 1966088 | tf_op jit(solution)/shard_map/ppermute | solution.py:45
  281.6 44.7 %collective-permute-start.26 = (bf16[128,2048]{1,0:T(8,128)(2,1)}, bf16[128,2048]{1,0:T(8,128)(2,1)S(1)}, u32[]{:S(2)}, u32[]{:S(2)}) collective-permute-start(bf16[128,2048]{1,0:T(8,128)(2,1)} %get-tuple-element.129), channel_id=1, source_target_pairs={{0,1},{1,2},{2,3},{3,0},{4,5},{5,6},{6,7},{7,4},{8,9},{9,10},{10,1... | collective-permute-start | bytes 1572872 | tf_op jit(solution)/shard_map/ppermute | solution.py:45
  281.7 44.6 %collective-permute-start.27 = (bf16[128,2048]{1,0:T(8,128)(2,1)S(1)}, bf16[128,2048]{1,0:T(8,128)(2,1)S(1)}, u32[]{:S(2)}, u32[]{:S(2)}) collective-permute-start(bf16[128,2048]{1,0:T(8,128)(2,1)S(1)} %copy-done.27), channel_id=1, source_target_pairs={{0,3},{1,0},{2,1},{3,2},{4,7},{5,4},{6,5},{7,6},{8,11},{9,8},{10,9... | collective-permute-start | bytes 1572872 | tf_op jit(solution)/shard_map/ppermute | solution.py:45
  318.4 74.4 %collective-permute-start.36 = (bf16[8,80,2048]{2,1,0:T(8,128)(2,1)}, bf16[8,80,2048]{2,1,0:T(8,128)(2,1)}, u32[]{:S(2)}, u32[]{:S(2)}) collective-permute-start(bf16[8,80,2048]{2,1,0:T(8,128)(2,1)} %joined.1.refs_2_.refs_1_), channel_id=1, source_target_pairs={{0,8},{1,9},{2,10},{3,11},{4,12},{5,13},{6,14},{7,15},{8,0},{9,1},... | collective-permute-start | bytes 7864328 | tf_op jit(solution)/shard_map/ppermute | solution.py:45
  331.2 26.2 %collective-permute-start.29 = (bf16[256,2048]{1,0:T(8,128)(2,1)}, bf16[256,2048]{1,0:T(8,128)(2,1)S(1)}, u32[]{:S(2)}, u32[]{:S(2)}) collective-permute-start(bf16[256,2048]{1,0:T(8,128)(2,1)} %get-tuple-element.140), channel_id=1, source_target_pairs={{0,1},{1,2},{2,3},{3,0},{4,5},{5,6},{6,7},{7,4},{8,9},{9,10},{10,1... | collective-permute-start | bytes 3145736 | tf_op jit(solution)/shard_map/ppermute | solution.py:45
  331.2 26.2 %collective-permute-start.30 = (bf16[256,2048]{1,0:T(8,128)(2,1)}, bf16[256,2048]{1,0:T(8,128)(2,1)}, u32[]{:S(2)}, u32[]{:S(2)}) collective-permute-start(bf16[256,2048]{1,0:T(8,128)(2,1)} %get-tuple-element.141), channel_id=1, source_target_pairs={{0,3},{1,0},{2,1},{3,2},{4,7},{5,4},{6,5},{7,6},{8,11},{9,8},{10,9... | collective-permute-start | bytes 3145736 | tf_op jit(solution)/shard_map/ppermute | solution.py:45
  335.3 66.2 %collective-permute-start.37 = (bf16[8,128,1024]{2,1,0:T(8,128)(2,1)}, bf16[8,128,1024]{2,1,0:T(8,128)(2,1)}, u32[]{:S(2)}, u32[]{:S(2)}) collective-permute-start(bf16[8,128,1024]{2,1,0:T(8,128)(2,1)} %held.2.refs_2_), channel_id=1, source_target_pairs={{0,8},{1,9},{2,10},{3,11},{4,12},{5,13},{6,14},{7,15},{8,0},{9,1},... | collective-permute-start | bytes 6291464 | tf_op jit(solution)/shard_map/ppermute | solution.py:45
  335.9 74.0 %all-to-all-start.3 = ((bf16[8,128,1024]{2,1,0:T(8,128)(2,1)}), bf16[8,128,1024]{2,1,0:T(8,128)(2,1)S(1)}, u32[]{:S(2)}, u32[]{:S(2)}) async-start(bf16[8,128,1024]{2,1,0:T(8,128)(2,1)} %get-tuple-element.146), calls=%async_computation.3 | async-start | bytes 4194304 | tf_op jit(solution)/shard_map/all_to_all | solution.py:1275
  341.3 35.4 %collective-permute-start.25 = (bf16[128,2048]{1,0:T(8,128)(2,1)}, bf16[128,2048]{1,0:T(8,128)(2,1)}, u32[]{:S(2)}, u32[]{:S(2)}) collective-permute-start(bf16[128,2048]{1,0:T(8,128)(2,1)} %get-tuple-element.126.refs_1_), channel_id=1, source_target_pairs={{0,4},{1,5},{2,6},{3,7},{4,0},{5,1},{6,2},{7,3},{8,12},{9,13},{10,... | collective-permute-start | bytes 1572872 | tf_op jit(solution)/shard_map/ppermute | solution.py:45
  361.4 26.4 %collective-permute-start.31 = (bf16[128,2048]{1,0:T(8,128)(2,1)}, bf16[128,2048]{1,0:T(8,128)(2,1)S(1)}, u32[]{:S(2)}, u32[]{:S(2)}) collective-permute-start(bf16[128,2048]{1,0:T(8,128)(2,1)} %other_sums.3), channel_id=1, source_target_pairs={{0,4},{1,5},{2,6},{3,7},{4,0},{5,1},{6,2},{7,3},{8,12},{9,13},{10,... | collective-permute-start | bytes 1572872 | tf_op jit(solution)/shard_map/ppermute | solution.py:45
  (50 other events, 419.5 us)

commit v12 on v7

--- a/solution.py
+++ b/solution.py
@@ -90,10 +90,10 @@
     return copies
 
 
-def piece_copies(pieces, half, target, sems, rows):
+def piece_copies(pieces, half, target, sems, rows, lanes=slice(None)):
     return [
         pltpu.make_async_copy(
-            piece.at[half] if len(piece.shape) == 3 else piece,
+            piece.at[half, :, lanes] if len(piece.shape) == 3 else piece.at[:, lanes],
             target.at[pl.ds(at * rows, rows)],
             sems.at[at],
         )
@@ -101,14 +101,29 @@
     ]
 
 
-def weight_copies(pieces, refs, spot_ref, target, lanes, sems):
+def weight_copies(pieces, refs, spot_ref, target, lanes, sems, source=None):
+    if source is not None:
+        pieces = [
+            (
+                array,
+                begin + max(source - first, 0),
+                min(size, 4),
+                max(first, source) - source,
+                spot,
+                ref,
+            )
+            for (array, begin, size, first, spot), ref in zip(pieces, refs)
+            if first <= source < first + size
+        ]
+    else:
+        pieces = [(*piece, ref) for piece, ref in zip(pieces, refs)]
     return [
         pltpu.make_async_copy(
             ref.at[pl.ds(begin, size), :, lanes],
             target.at[pl.ds(first, size), spot_ref[spot]],
             sems.at[at],
         )
-        for at, (ref, (_, begin, size, first, spot)) in enumerate(zip(refs, pieces))
+        for at, (_, begin, size, first, spot, ref) in enumerate(pieces)
     ]
 
 
@@ -474,23 +489,22 @@
             copy.wait()
 
         def split(part, high, lanes):
-            for z_hi in range(2):
-                at = (pl.ds(4 * z_hi, 4), high, lanes)
-
-                @pl.when(own)
-                def _(z_hi=z_hi, at=at):
-                    keep_v[at] = part[:, z_hi, 0]
-                    send_v[at] = part[:, z_hi, 1]
-
-                @pl.when(jnp.logical_not(own))
-                def _(z_hi=z_hi, at=at):
-                    keep_v[at] = part[:, z_hi, 1]
-                    send_v[at] = part[:, z_hi, 0]
+            at = (slice(None), high, lanes)
+
+            @pl.when(own)
+            def _():
+                keep_v[at] = part[:, 0]
+                send_v[at] = part[:, 1]
+
+            @pl.when(jnp.logical_not(own))
+            def _():
+                keep_v[at] = part[:, 1]
+                send_v[at] = part[:, 0]
 
         @pl.loop(0, 8)
         def _(n):
             lanes = pl.ds(pl.multiple_of(n * 256, 256), 256)
-            part = dot_rows(h1_v[:, lanes], dq_v[...]).astype(bf16).reshape(4, 2, 2, 16, 3 * head)
+            part = dot_rows(h1_v[:, lanes], dq_v[...]).astype(bf16).reshape(8, 2, 16, 3 * head)
             for third in range(3):
                 split(
                     part[..., third * head : (third + 1) * head],
@@ -500,7 +514,7 @@
 
         for copy in dy_copies:
             copy.wait()
-        part = dot_rows(ol_v[...], dy_v[...]).astype(bf16).reshape(4, 2, 2, 16, width)
+        part = dot_rows(ol_v[...], dy_v[...]).astype(bf16).reshape(8, 2, 16, width)
         split(part, pl.ds(48, 16), slice(None))
         keep_copy = pltpu.make_async_copy(keep_v, keep_hbm, sems.at[0])
         keep_copy.start()
@@ -671,39 +685,6 @@
     )(part, *after)
 
 
-def packed_sums(stays, crossed, own, below, above, ff, head, after):
-    width = own.shape[1]
-
-    def body(stay_ref, cross_ref, own_ref, below_ref, above_ref, out_ref, lanes_ref, keep_ref):
-        inner = (stay_ref[0].astype(f32) + cross_ref[0].astype(f32)).astype(bf16)
-        total = wide(own_ref, below_ref, above_ref).astype(bf16)
-        for owner in range(8):
-            pieces = [
-                total[16 * third : 16 * third + 16, owner * head : (owner + 1) * head]
-                for third in range(3)
-            ]
-            row, col = 64 + 16 * (owner % 4), owner // 4 * ff
-            pieces.append(inner[row : row + 16, col : col + ff])
-            out_ref[owner] = jnp.concatenate(pieces, 1)
-            lanes_ref[owner] = total[48:64, owner * head : (owner + 1) * head]
-        keep_ref[...] = inner[0:64]
-
-    vmem = pl.BlockSpec(memory_space=pltpu.VMEM)
-    return pl.pallas_call(
-        after_inputs(body, 5, len(after)),
-        out_shape=(
-            jax.ShapeDtypeStruct((8, 16, 3 * head + ff), bf16),
-            jax.ShapeDtypeStruct((8, 16, width // 8), bf16),
-            jax.ShapeDtypeStruct((64, width), bf16),
-        ),
-        in_specs=[vmem] * 5 + anywhere(len(after)),
-        out_specs=(vmem,) * 3,
-        compiler_params=kernel_params(),
-        cost_estimate=cost(3),
-        name="packed_sums",
-    )(stays, crossed, own, below, above, *after)
-
-
 def joined(arrays, after):
     sizes = [array.shape[0] for array in arrays]
     unit = math.gcd(*sizes)
@@ -772,43 +753,75 @@
     return low, high, together.reshape(3 * count, rows, cols)
 
 
-def small_sums(norm_sums, qkv_sums, up_sums, dy_sums, numbers, after):
-    def body(number_ref, norm_ref, q_ref, u_ref, y_ref, out_ref, work):
+def unpacked_sums(received, cols, after):
+    sources, rows, width = received.shape
+
+    def body(part_ref, out_ref):
+        small = jnp.sum(part_ref[:, :, cols:].astype(f32), 0).astype(bf16)
+        out_ref[0] = jnp.concatenate(
+            [jnp.concatenate([part_ref[0, :, 0:cols], small], 1)]
+            + [part_ref[n] for n in range(1, sources)],
+            0,
+        )
+
+    vmem = pl.BlockSpec(memory_space=pltpu.VMEM)
+    return pl.pallas_call(
+        after_inputs(body, 1, len(after)),
+        out_shape=jax.ShapeDtypeStruct((1, sources * rows, width), bf16),
+        in_specs=[vmem] + anywhere(len(after)),
+        out_specs=vmem,
+        compiler_params=kernel_params(),
+        cost_estimate=cost(3),
+        name="unpacked_sums",
+    )(received, *after)
+
+
+def packed_sums(stays, crossed, parts, norm_sums, qkv_sums, up_sums, dy_sums, numbers, ff, head, after):
+    width = parts.shape[2]
+
+    def body(*refs):
+        stay_ref, cross_ref, parts_ref = refs[:3]
+        norm_ref, q_ref, u_ref, y_ref, number_ref, out_ref, keep_ref, small = refs[3:]
         shard = number_ref[1]
+        inner = (stay_ref[0].astype(f32) + cross_ref[0].astype(f32)).astype(bf16)
+        total = jnp.sum(parts_ref[...].astype(f32), 0).astype(bf16)
         for owner in range(8):
             mine = shard == owner
-            for n in range(4):
-                for half in range(2):
-                    at = owner * 256 + half * 128
-                    work[owner, n * 2 + half : n * 2 + half + 1] = norm_ref[n : n + 1, at : at + 128]
+            small[...] = jnp.zeros_like(small)
+            small[0:4] = norm_ref[:, owner * head : (owner + 1) * head]
             for n in range(3):
                 third, source = divmod(owner * 3 + n, 8)
-                for half in range(2):
-                    at = third * 256 + half * 128
-                    work[owner, 8 + n * 2 + half : 9 + n * 2 + half] = jnp.where(
-                        shard == source, q_ref[:, at : at + 128], 0.0
-                    )
-            for n in range(8):
-                work[owner, 14 + n : 15 + n] = jnp.where(
-                    mine, u_ref[:, n * 128 : (n + 1) * 128], 0.0
-                )
-            for n in range(2):
-                work[owner, 22 + n : 23 + n] = jnp.where(
-                    mine, y_ref[:, n * 128 : (n + 1) * 128], 0.0
-                )
-        out_ref[...] = work[...].astype(bf16)
+                lanes = slice(third * head, (third + 1) * head)
+                small[4 + n : 5 + n] = jnp.where(shard == source, q_ref[:, lanes], 0.0)
+            for n in range(4):
+                lanes = slice(n * head, (n + 1) * head)
+                small[7 + n : 8 + n] = jnp.where(mine, u_ref[:, lanes], 0.0)
+            small[11:12] = jnp.where(mine, y_ref[...], 0.0)
+            pieces = [
+                total[16 * third : 16 * third + 16, owner * head : (owner + 1) * head]
+                for third in range(3)
+            ]
+            row, col = 64 + 16 * (owner % 4), owner // 4 * ff
+            pieces.append(inner[row : row + 16, col : col + ff])
+            pieces.append(small[...].astype(bf16))
+            out_ref[owner] = jnp.concatenate(pieces, 1)
+        keep_ref[0:64] = inner[0:64]
+        keep_ref[64:80] = total[48:64]
 
     vmem = pl.BlockSpec(memory_space=pltpu.VMEM)
     return pl.pallas_call(
-        after_inputs(body, 5, len(after)),
-        out_shape=jax.ShapeDtypeStruct((8, 24, 128), bf16),
-        in_specs=[pl.BlockSpec(memory_space=pltpu.SMEM)] + [vmem] * 4 + anywhere(len(after)),
-        out_specs=vmem,
-        scratch_shapes=[pltpu.VMEM((8, 24, 128), f32)],
+        after_inputs(body, 8, len(after)),
+        out_shape=(
+            jax.ShapeDtypeStruct((8, 16, 4 * head + ff), bf16),
+            jax.ShapeDtypeStruct((80, width), bf16),
+        ),
+        in_specs=[vmem] * 7 + [pl.BlockSpec(memory_space=pltpu.SMEM)] + anywhere(len(after)),
+        out_specs=(vmem,) * 2,
+        scratch_shapes=[pltpu.VMEM((16, head), f32)],
         compiler_params=kernel_params(),
         cost_estimate=cost(3),
-        name="small_sums",
-    )(numbers, norm_sums, qkv_sums, up_sums, dy_sums, *after)
+        name="packed_sums",
+    )(stays, crossed, parts, norm_sums, qkv_sums, up_sums, dy_sums, numbers, *after)
 
 
 def finished(own, below, above, other, tokens, cotangent, after):
@@ -1086,20 +1099,21 @@
     )
     from_below, from_above = move(above, y=1), move(below, y=-1)
 
-    four, part_shape = (4, 64, width), (1, 64, width)
-
-    def away_body(n_ref, keep_ref, got_ref, out_ref):
-        out_ref[...] = wide(keep_ref, got_ref).astype(bf16)
-
-    (a_away,) = blocks_call(
-        "away_sums",
-        away_body,
+    four = (4, 64, width)
+
+    def both_body(n_ref, low_keep, low_got, high_keep, high_got, out_ref):
+        out_ref[0:4] = wide(low_keep, low_got).astype(bf16)
+        out_ref[4:8] = wide(high_keep, high_got).astype(bf16)
+
+    (a_sent,) = blocks_call(
+        "both_sums",
+        both_body,
         numbers,
-        [(v, four, lambda n: 1 - n[3]) for v in (a_keep, a_got)],
-        (four,),
+        [(v, four, lambda n, half=half: half) for half in range(2) for v in (a_keep, a_got)],
+        ((8, 64, width),),
         (above,),
     )
-    a_crossed = move(a_away, h=1)
+    a_parts = lax.all_to_all(a_sent, "rep", 0, 0, axis_index_groups=SAME_CORE)
     norm_sums, *pairs_out = outer(
         d_qkv,
         d_hidden,
@@ -1114,12 +1128,22 @@
         down_weight,
         out_weight,
         wide_bias,
-        (a_away, above, below),
-    )
-
-    smalls = small_sums(norm_sums, qkv_sums, up_sums, dy_sums, numbers, ())
-    smalls = jnp.sum(lax.all_to_all(smalls, "shard", 0, 0).astype(f32), 0)
-    smalls = jnp.pad(smalls.astype(bf16).reshape(-1), (0, 16 * width - 3072)).reshape(16, width)
+        (a_sent, above, below),
+    )
+
+    passed_below, passed_above = move(pairs_out[6], x=1), move(pairs_out[2], x=-1)
+
+    def passed_body(n_ref, up_ref, from_below, here_ref, down_ref, from_above, there_ref, up_out, down_out):
+        up_out[0:2] = wide(up_ref, from_below).astype(bf16)
+        up_out[2:4] = here_ref[...]
+        down_out[0:2] = wide(down_ref, from_above).astype(bf16)
+        down_out[2:4] = there_ref[...]
+
+    def other_body(n_ref, own_ref, below_ref, above_ref, out_ref):
+        out_ref[...] = wide(own_ref, below_ref, above_ref).astype(bf16)
+
+    def first(n):
+        return 0
 
     def ends_body(n_ref, keep_ref, got_ref, below_ref, above_ref, leave_ref, stay_ref):
         total = wide(keep_ref, got_ref, below_ref, above_ref).astype(bf16)
@@ -1138,58 +1162,26 @@
     )
     crossed = move(leaves, h=1)
 
-    passed_below, passed_above = move(pairs_out[6], x=1), move(pairs_out[2], x=-1)
-
-    def around_body(n_ref, keep_ref, got_ref, crossed_ref, low_ref, high_ref, above_ref, own_ref, below_ref):
-        def part(k):
-            at = (n_ref[2] + k) % 4
-            return wide(keep_ref.at[at], got_ref.at[at], crossed_ref.at[at]).astype(bf16)
-
-        far = part(2)
-        low_ref[...] = far[:32]
-        high_ref[...] = far[32:]
-        above_ref[...] = part(1)
-        own_ref[...] = part(0)
-        below_ref[...] = part(3)
-
-    a_low, a_high, a_above, a_own, a_below = blocks_call(
-        "around_sums",
-        around_body,
+    part, stays = packed_sums(
+        stays,
+        crossed,
+        a_parts,
+        norm_sums,
+        qkv_sums,
+        up_sums,
+        dy_sums,
         numbers,
-        [(v, four, lambda n: n[3]) for v in (a_keep, a_got)] + [(a_crossed, four, lambda n: 0)],
-        ((32, width), (32, width), (64, width), (64, width), (64, width)),
-        (leaves,),
-    )
-    a_low, a_high = move(a_low, y=1), move(a_high, y=-1)
-
-    def beside_body(n_ref, above_ref, below_ref, low_ref, high_ref, up_ref, down_ref):
-        up_ref[0:32] = (above_ref[0:32].astype(f32) + low_ref[...].astype(f32)).astype(bf16)
-        up_ref[32:64] = above_ref[32:64]
-        down_ref[0:32] = below_ref[0:32]
-        down_ref[32:64] = (below_ref[32:64].astype(f32) + high_ref[...].astype(f32)).astype(bf16)
-
-    a_above, a_below = blocks_call(
-        "beside_sums",
-        beside_body,
-        numbers,
-        [(v, v.shape, lambda n: 0) for v in (a_above, a_below, a_low, a_high)],
-        ((64, width), (64, width)),
-        (crossed, smalls),
-    )
-    a_from_below, a_from_above = move(a_above, y=1), move(a_below, y=-1)
-
-    def passed_body(n_ref, up_ref, from_below, here_ref, down_ref, from_above, there_ref, up_out, down_out):
-        up_out[0:2] = wide(up_ref, from_below).astype(bf16)
-        up_out[2:4] = here_ref[...]
-        down_out[0:2] = wide(down_ref, from_above).astype(bf16)
-        down_out[2:4] = there_ref[...]
-
+        ff,
+        head,
+        (),
+    )
+    received = lax.all_to_all(part, "shard", 0, 0)
     ups, downs = blocks_call(
         "passed_sums",
         passed_body,
         numbers,
         [
-            (v, pair_shape, lambda n: 0)
+            (v, pair_shape, first)
             for v in (
                 pairs_out[5],
                 passed_below,
@@ -1200,54 +1192,44 @@
             )
         ],
         ((4, 128, width),) * 2,
-        (a_low,),
-    )
+        (part,),
+    )
+    stays = stays[None]
+    stays = jnp.concatenate([stays, move(stays, h=1)])
+    part = unpacked_sums(received, cols, (ups, stays))
+    beside = move(stays, y=1), move(stays, y=-1)
+    stays = joined((stays, beside[1], beside[0], move(beside[0], y=1)), ())
     from_device_below, from_device_above = move(ups, x=1), move(downs, x=-1)
-
-    part, outs, downs_sum = packed_sums(
-        stays, crossed, a_own, a_from_below, a_from_above, ff, head, (ups,)
-    )
-    received = lax.all_to_all(part, "shard", 0, 0)
-    part = jnp.concatenate([received, outs], 2).reshape(1, 128, width)
-    def other_body(n_ref, own_ref, below_ref, above_ref, out_ref):
-        out_ref[...] = wide(own_ref, below_ref, above_ref).astype(bf16)
-
-    (total_other,) = blocks_call(
+    (sent_other,) = blocks_call(
         "other_sums",
         other_body,
         numbers,
         [
-            (pairs_out[4], pair_shape, lambda n: 0),
-            (from_device_below, pair_shape, lambda n: 0),
+            (pairs_out[4], pair_shape, first),
+            (from_device_below, pair_shape, first),
             (from_device_above, pair_shape, lambda n: 1),
         ],
         (pair_shape,),
         (),
     )
-    total_other, sent_other = move(total_other, l=1), total_other
+    total_other = move(sent_other, l=1)
 
     order = ((0, h), (0, 1 - h), (1, h), (1, 1 - h), (3, h), (3, 1 - h), (2, h), (2, 1 - h))
     places = jnp.stack([(y + k) % 4 * 2 + high for k, high in order]).astype(jnp.int32)
 
-    def rep_gather(own, after):
-        own = jnp.concatenate([own, move(own, h=1)])
-        below, above = move(own, y=1), move(own, y=-1)
-        low, high, near = halves(own, below, above, after)
-        return near, (move(low, y=1), move(high, y=-1))
-
-    near, far = rep_gather(jnp.concatenate([downs_sum, smalls])[None], ())
-    downs_all = joined((near, *far), ())
-    downs_yours = move(downs_all, c=1)
-    (down_grad,) = spread(
-        [(downs_all, downs_yours)],
+    down_grad, out_grad = spread(
+        [(stays, move(stays, c=1))],
         places,
         numbers[:1],
-        [(width, 64, [(0, 0, 0, width)])],
+        [(width, 64, [(0, 0, 0, width)]), (width, 16, [(0, 64, 0, width)])],
         8,
         (),
         (),
     )
-    near, far = rep_gather(part, (sent_other, downs_all))
+    part = joined((part, move(part, h=1)), beside)
+    below, above = move(part, y=1), move(part, y=-1)
+    low, high, near = halves(part, below, above, (stays, sent_other))
+    far = move(low, y=1), move(high, y=-1)
     targets = [
         (
             3 * width,
@@ -1259,15 +1241,18 @@
             ],
         ),
         (8 * ff, 16, [(source * ff, 16 * source, 3 * head, ff) for source in range(8)]),
-        (width, 16, [(source * head, 16 * source, cols, head) for source in range(8)]),
     ]
-    grads = spread([(near, move(near, c=1))], places[:6], numbers[:1], targets, 8, (), (down_grad,))
+    near_yours = move(near, c=1)
+    grads = spread(
+        [(near, near_yours)], places[:6], numbers[:1], targets, 8, (), (down_grad, sent_other)
+    )
     far = joined(far, (grads[0],))
     mixed, tokens_grad = finished(
         pairs_out[0], from_device_below, from_device_above, total_other, tokens, cotangent, (far,)
     )
-    qkv_grad, up_grad, out_grad = spread(
-        [(far, move(far, c=1))],
+    far_yours = move(far, c=1)
+    qkv_grad, up_grad = spread(
+        [(far, far_yours)],
         places[6:],
         numbers[:1],
         targets,
@@ -1275,10 +1260,10 @@
         grads,
         (tokens_grad,),
     )
-    smalls = jnp.concatenate([downs_all[:, 64:66], downs_yours[:, 64:66]]).astype(f32)
-    smalls = jnp.sum(smalls, 0).reshape(-1)
-    norm_grads = smalls[:1024].reshape(4, 256)
-    dy_total = smalls[2816:3072]
+    smalls = [v[:, 0:16, cols:] for v in (near, near_yours, far, far_yours)]
+    smalls = jnp.sum(jnp.concatenate(smalls).astype(f32), 0)
+    norm_grads = smalls[:4]
+    dy_total = smalls[11]
     return (
         mixed,
         tokens_grad,
@@ -1287,11 +1272,11 @@
         norm_grads[2],
         norm_grads[3],
         qkv_grad,
-        smalls[1024:1792],
+        smalls[4:7].reshape(3 * head),
         out_grad,
         dy_total,
         up_grad,
-        smalls[1792:2816],
+        smalls[7:11].reshape(ff),
         down_grad,
         dy_total,
     )

time: 429 us -> 371 us (0.86); the launches traced: 422 us -> 369 us
  waiting for transfers between devices: 123 us -> 94.7 us
  blocking collectives: 8.87 us -> 0 us
  Pallas kernels: 172 us -> 165 us
    all_to_all x1, waiting for transfers between devices: 37.9 us -> 0.01 us  [local(): received = lax.all_to_all(part, 'shard', 0, 0)]
    ppermute x45 -> x39, waiting for transfers between devices: 76.3 us -> 85.5 us  [move(): return lax.ppermute(value, BOTH, pairs)]
    all_to_all x1 -> x0, blocking collectives: 8.87 us -> none  [local(): smalls = jnp.sum(lax.all_to_all(smalls, 'shard', 0, 0).astype(f32), 0)]
    ppermute x45 -> x39, starting transfers between devices: 67.7 us -> 59.1 us  [move(): return lax.ppermute(value, BOTH, pairs)]
    pallas_call x8 -> x6, Pallas kernels: 31.9 us -> 26.8 us  [blocks_call(): pl.pallas_call(after_inputs(body, 1 + len(terms), len(after)), out_shape=...]
    all_to_all x0 -> x1, starting transfers between devices: none -> 4.49 us  [local(): a_parts = lax.all_to_all(a_sent, 'rep', 0, 0, axis_index_groups=SAME_CORE)]
    pallas_call x3 -> x2, Pallas kernels: 9.57 us -> 6.75 us  [halves(): pl.pallas_call(after_inputs(body, 3, len(after)), out_shape=(jax.ShapeDty...]
    unnamed x92 -> x77, local copies, waits for them, and re-layouts: 22.2 us -> 20 us
  transfers between devices with their start and end apart: 47 -> 42, of which waited for: 11 -> 14; matrix products, arithmetic and copies ran while one was open for 5% -> 5% of each run, Pallas kernels for 28% -> 31%
where the time goes in v12:
time: 371 us; the launch traced here: 369 us
  Pallas kernels  165 us (44%)
  waiting for transfers between devices  94.7 us (26%)
  starting transfers between devices  70.7 us (19%)
  local copies, waits for them, and re-layouts  30.1 us (8%)
  other arithmetic  7.24 us (2%)
    ppermute x39, waiting for transfers between devices, move(): return lax.ppermute(value, BOTH, pairs)  85.5 us
    ppermute x39, starting transfers between devices, move(): return lax.ppermute(value, BOTH, pairs)  59.1 us
    pallas_call x1, Pallas kernels, feed_forward(): pl.pallas_call(after_inputs(body, 5 + parts + 2 * count, len(after)), out...  32.2 us
    pallas_call x6, Pallas kernels, blocks_call(): pl.pallas_call(after_inputs(body, 1 + len(terms), len(after)), out_shape=...  26.8 us
    pallas_call x1, Pallas kernels, outer(): pl.pallas_call(after_inputs(body, 11 + parts + count, len(after)), out_sh...  24.2 us
    pallas_call x3, Pallas kernels, spread(): pl.pallas_call(after_inputs(body, 2 + 2 * len(pieces) + len(before), len(...  21 us
    unnamed x77, local copies, waits for them, and re-layouts  20 us
    pallas_call x1, Pallas kernels, attend(): pl.pallas_call(after_inputs(body, 7 + parts + count, len(after)), out_sha...  17.2 us
  transfers between devices with their start and end apart: 42, of which 14 were waited for; matrix products, arithmetic and copies ran while one was open for 5% of the time, Pallas kernels for 31%

profile of v12, /device:TPU:1, one launch (start us, length us, event | category | flops | bytes accessed | tf_op | source)
XLA Modules:
  0.0 369.2 jit_solution(13206674738645457503)
XLA Ops:
  0.7 3.6 packed.1
  9.4 3.6 all-to-all-start
  13.0 17.3 %collective-permute-done.1.refs_2_.refs_17_.refs_25_.refs_16_.refs_4_.refs_18_ = bf16[2,128,2048]{2,1,0:T(8,128)(2,1)} collective-permute-done((bf16[2,128,2048]{2,1,0:T(8,128)(2,1)}, bf16[2,128,2048]{2,1,0:T(8,128)(2,1)}, u32[]{:S(2)}, u32[]{:S(2)}) %collective-permute-start.1) | collective-permute-done | bytes 1048608 | tf_op jit(solution)/shard_map/ppermute | solution.py:45
  35.0 9.2 %all-to-all-done.refs_0_ = bf16[8,40,1792]{2,1,0:T(8,128)(2,1)S(1)} async-done(((bf16[8,40,1792]{2,1,0:T(8,128)(2,1)}), bf16[8,40,1792]{2,1,0:T(8,128)(2,1)S(1)}, u32[]{:S(2)}, u32[]{:S(2)}) %all-to-all-start) | async-done | bytes 1146912 | tf_op jit(solution)/shard_map/all_to_all | solution.py:988
  51.6 16.1 %collective-permute-done.3.refs_2_.refs_5_.refs_4_.refs_6_ = bf16[8,32,1792]{2,1,0:T(8,128)(2,1)S(1)} collective-permute-done((bf16[8,32,1792]{2,1,0:T(8,128)(2,1)}, bf16[8,32,1792]{2,1,0:T(8,128)(2,1)S(1)}, u32[]{:S(2)}, u32[]{:S(2)}) %collective-permute-start.3) | collective-permute-done | bytes 917536 | tf_op jit(solution)/shard_map/ppermute | solution.py:45
  75.9 3.9 %collective-permute-start.10 = (bf16[24,32,1792]{2,1,0:T(8,128)(2,1)}, bf16[24,32,1792]{2,1,0:T(8,128)(2,1)S(1)}, u32[]{:S(2)}, u32[]{:S(2)}) collective-permute-start(bf16[24,32,1792]{2,1,0:T(8,128)(2,1)} %bitcast.66), channel_id=1, source_target_pairs={{0,8},{1,9},{2,10},{3,11},{4,12},{5,13},{6,14},{7,15},{8,0},{9,1},... | collective-permute-start | bytes 8257544 | tf_op jit(solution)/shard_map/ppermute | solution.py:45
  91.4 5.2 %collective-permute-done.8.refs_6_.refs_5_.refs_7_ = bf16[4,32,1792]{2,1,0:T(8,128)(2,1)S(1)} collective-permute-done((bf16[4,32,1792]{2,1,0:T(8,128)(2,1)}, bf16[4,32,1792]{2,1,0:T(8,128)(2,1)S(1)}, u32[]{:S(2)}, u32[]{:S(2)}) %collective-permute-start.8) | collective-permute-done | bytes 458784 | tf_op jit(solution)/shard_map/ppermute | solution.py:45
  103.8 32.2 %feed_forward.1 = (bf16[1024,2048]{1,0:T(8,128)(2,1)}, bf16[1024,1024]{1,0:T(8,128)(2,1)}, bf16[1024,1024]{1,0:T(8,128)(2,1)}, bf16[8,128,2048]{2,1,0:T(8,128)(2...) custom-call(s32[4]{0:T(128)} %get-tuple-element.128.refs_0_.refs_7_,, ...), custom_call_target="tpu_custom_call" | custom-call | flops 36800000000 | bytes 1000 | tf_op jit(solution)/shard_map/feed_forward/pallas_call | solution.py:258
  140.1 17.2 %attend.1 = (bf16[1024,256]{1,0:T(8,128)(2,1)}, bf16[1024,768]{1,0:T(8,128)(2,1)}, f32[1,768]{1,0:T(1,128)}) custom-call(s32[8,3]{1,0:T(8,128)} %copy-done.8, s32[8]{0:T(128)} %pad_add_fusion.refs_1_.refs_0_, f32[3,1,256]{2,1,0:T(1,128)} %pad_maximum_fusion.2.refs_2_, bf16[8,32,1792]{2,1,0:T(8,128)(2,1)} %get-tuple-element.68.refs_0_.refs_4_.refs_3_.refs_5_, ...), custom_call_target="tpu_custom_call" | custom-call | flops 19549999104 | bytes 1000 | tf_op jit(solution)/shard_map/attend/pallas_call | solution.py:431
  157.3 3.3 far_sums.1
  163.3 13.6 %attention_grads.1 = (bf16[8,64,2048]{2,1,0:T(8,128)(2,1)}, bf16[8,64,2048]{2,1,0:T(8,128)(2,1)}) custom-call(s32[4]{0:T(128)} %get-tuple-element.128.refs_0_.refs_7_, bf16[2,128,2048]{2,1,0:T(8,128)(2,1)} %get-tuple-element.66.refs_14_.refs_22_.refs_13_.refs_1_.refs_15_, ...), custom_call_target="tpu_custom_call" | custom-call | flops 13799999488 | bytes 1000 | tf_op jit(solution)/shard_map/attention_grads/pallas_call | solution.py:527
  179.3 4.8 %near_sums.1 = (bf16[2,128,2048]{2,1,0:T(8,128)(2,1)}, bf16[2,128,2048]{2,1,0:T(8,128)(2,1)}) custom-call(s32[4]{0:T(128)} %get-tuple-element.128.refs_0_.refs_7_, bf16[8,128,2048]{2,1,0:T(8,128)(2,1)} %get-tuple-element.80.refs_1_.refs_3_, bf16[8,128,2048]{2,1,0:T(8,128)(2,1)} %collective-permute-done.15.refs_2_.refs_4_, ...), custom_call_target="tpu_custom_call" | custom-call | flops 23000000512 | bytes 1000 | tf_op jit(solution)/shard_map/near_sums/pallas_call | solution.py:869
  188.1 4.6 %both_sums.1.refs_29_ = bf16[8,64,2048]{2,1,0:T(8,128)(2,1)} custom-call(s32[4]{0:T(128)} %get-tuple-element.128.refs_0_.refs_7_, bf16[8,64,2048]{2,1,0:T(8,128)(2,1)} %get-tuple-element.83.refs_1_.refs_3_, bf16[8,64,2048]{2,1,0:T(8,128)(2,1)} %copy-done.15, bf16[8,64,2048]{2,1,0:T(8,128)(2,1)} %get-tuple-element.83.refs_1_.refs_3_, ...), custom_call_target="tpu_custom_call" | custom-call | flops 3449999872 | bytes 1000 | tf_op jit(solution)/shard_map/both_sums/pallas_call | solution.py:869
  192.7 4.5 %all-to-all-start.1 = ((bf16[8,64,2048]{2,1,0:T(8,128)(2,1)}), bf16[8,64,2048]{2,1,0:T(8,128)(2,1)S(1)}, u32[]{:S(2)}, u32[]{:S(2)}) async-start(bf16[8,64,2048]{2,1,0:T(8,128)(2,1)} %both_sums.1.refs_29_), calls=%async_computation.1 | async-start | bytes 4194304 | tf_op jit(solution)/shard_map/all_to_all | solution.py:1116
  197.2 24.2 %outer.1 = (f32[4,2048]{1,0:T(4,128)}, bf16[2,128,2048]{2,1,0:T(8,128)(2,1)}, bf16[2,128,2048]{2,1,0:T(8,128)(2,1)}, bf16[2,128,2048]{2,1,0:T(8,128)(2,1)}, bf16...) custom-call(s32[8]{0:T(128)} %pad_add_fusion.refs_1_.refs_0_, ...), custom_call_target="tpu_custom_call" | custom-call | flops 23000000512 | bytes 1000 | tf_op jit(solution)/shard_map/outer/pallas_call | solution.py:622
  225.3 4.3 %end_sums.1 = (bf16[1,128,2048]{2,1,0:T(8,128)(2,1)}, bf16[1,128,2048]{2,1,0:T(8,128)(2,1)}) custom-call(s32[4]{0:T(128)} %get-tuple-element.128.refs_0_.refs_7_, bf16[8,128,2048]{2,1,0:T(8,128)(2,1)} %get-tuple-element.80.refs_1_.refs_3_, bf16[8,128,2048]{2,1,0:T(8,128)(2,1)} %collective-permute-done.15.refs_2_.refs_4_, bf16[2,128,2048]{2,1,0:T(8,128)(2,1)} %copy-done.16, ...), custom_call_target="tpu_custom_call" | custom-call | flops 3449999872 | bytes 1000 | tf_op jit(solution)/shard_map/end_sums/pallas_call | solution.py:869
  232.6 14.1 %collective-permute-done.23.refs_1_ = bf16[1,128,2048]{2,1,0:T(8,128)(2,1)S(1)} collective-permute-done((bf16[1,128,2048]{2,1,0:T(8,128)(2,1)}, bf16[1,128,2048]{2,1,0:T(8,128)(2,1)S(1)}, u32[]{:S(2)}, u32[]{:S(2)}) %collective-permute-start.23) | collective-permute-done | bytes 524320 | tf_op jit(solution)/shard_map/ppermute | solution.py:45
  248.2 3.5 packed_sums.1
  251.7 3.5 all-to-all-start.2
  255.2 5.9 %passed_sums.1 = (bf16[4,128,2048]{2,1,0:T(8,128)(2,1)}, bf16[4,128,2048]{2,1,0:T(8,128)(2,1)}) custom-call(s32[4]{0:T(128)} %get-tuple-element.128.refs_0_.refs_7_, bf16[2,128,2048]{2,1,0:T(8,128)(2,1)} %get-tuple-element.88.refs_1_, bf16[2,128,2048]{2,1,0:T(8,128)(2,1)} %collective-permute-done.19.refs_2_, ...), custom_call_target="tpu_custom_call" | custom-call | flops 3449999872 | bytes 1000 | tf_op jit(solution)/shard_map/passed_sums/pallas_call | solution.py:869
  272.3 4.6 %collective-permute-done.29.refs_2_ = bf16[2,80,2048]{2,1,0:T(8,128)(2,1)S(1)} collective-permute-done((bf16[2,80,2048]{2,1,0:T(8,128)(2,1)S(1)}, bf16[2,80,2048]{2,1,0:T(8,128)(2,1)S(1)}, u32[]{:S(2)}, u32[]{:S(2)}) %collective-permute-start.29) | collective-permute-done | bytes 655392 | tf_op jit(solution)/shard_map/ppermute | solution.py:45
  277.4 4.1 %collective-permute-done.28.refs_1_ = bf16[1,128,2048]{2,1,0:T(8,128)(2,1)S(1)} collective-permute-done((bf16[1,128,2048]{2,1,0:T(8,128)(2,1)}, bf16[1,128,2048]{2,1,0:T(8,128)(2,1)S(1)}, u32[]{:S(2)}, u32[]{:S(2)}) %collective-permute-start.28) | collective-permute-done | bytes 524320 | tf_op jit(solution)/shard_map/ppermute | solution.py:45
  291.0 3.7 joined.4.refs_3_.refs_2_
  294.7 12.8 %collective-permute-done.24.refs_2_.refs_1_ = bf16[4,128,2048]{2,1,0:T(8,128)(2,1)} collective-permute-done((bf16[4,128,2048]{2,1,0:T(8,128)(2,1)}, bf16[4,128,2048]{2,1,0:T(8,128)(2,1)}, u32[]{:S(2)}, u32[]{:S(2)}) %collective-permute-start.24) | collective-permute-done | bytes 2097184 | tf_op jit(solution)/shard_map/ppermute | solution.py:45
  307.5 3.9 %other_sums.1.refs_4_.refs_5_ = bf16[2,128,2048]{2,1,0:T(8,128)(2,1)} custom-call(s32[4]{0:T(128)} %get-tuple-element.128.refs_0_.refs_7_, bf16[2,128,2048]{2,1,0:T(8,128)(2,1)} %get-tuple-element.103.refs_1_, bf16[4,128,2048]{2,1,0:T(8,128)(2,1)} %collective-permute-done.24.refs_2_.refs_1_, bf16[4,128,2048]{2,1,0:T(8,128)(2,1)} %collective-permute-done.25.refs_3_.refs_2_), custom_call_target="tpu_custom_call" | custom-call | flops 3449999872 | bytes 1000 | tf_op jit(solution)/shard_map/other_sums/pallas_call | solution.py:869
  314.4 3.5 halves.3
  317.9 6.3 %collective-permute-start.36 = (bf16[6,128,2048]{2,1,0:T(8,128)(2,1)}, bf16[6,128,2048]{2,1,0:T(8,128)(2,1)S(1)}, u32[]{:S(2)}, u32[]{:S(2)}) collective-permute-start(bf16[6,128,2048]{2,1,0:T(8,128)(2,1)} %bitcast.45), channel_id=1, source_target_pairs={{0,8},{1,9},{2,10},{3,11},{4,12},{5,13},{6,14},{7,15},{8,0},{9,1},... | collective-permute-start | bytes 9437192 | tf_op jit(solution)/shard_map/ppermute | solution.py:45
  329.5 4.0 %collective-permute-done.37.refs_3_ = bf16[8,80,2048]{2,1,0:T(8,128)(2,1)} collective-permute-done((bf16[8,80,2048]{2,1,0:T(8,128)(2,1)}, bf16[8,80,2048]{2,1,0:T(8,128)(2,1)}, u32[]{:S(2)}, u32[]{:S(2)}) %collective-permute-start.37) | collective-permute-done | bytes 2621472 | tf_op jit(solution)/shard_map/ppermute | solution.py:45
  333.5 8.7 %spread.3 = (f32[1024,2048]{1,0:T(8,128)}, f32[256,2048]{1,0:T(8,128)}) custom-call(s32[8]{0:T(128)} %stack.71.refs_0_, s32[1]{0:T(128)} %bitcast.refs_1_, bf16[8,80,2048]{2,1,0:T(8,128)(2,1)} %joined.4.refs_3_.refs_2_, bf16[8,80,2048]{2,1,0:T(8,128)(2,1)} %collective-permute-done.37.refs_3_), custom_call_target="tpu_custom_call" | custom-call | flops 2760000000 | bytes 1000 | tf_op jit(solution)/shard_map/spread/pallas_call | solution.py:931
  343.9 8.5 %spread.4 = (f32[256,6144]{1,0:T(8,128)}, f32[256,8192]{1,0:T(8,128)}) custom-call(s32[6]{0:T(128)} %stack.68.refs_0_, s32[1]{0:T(128)} %bitcast.refs_1_, bf16[6,128,2048]{2,1,0:T(8,128)(2,1)} %bitcast.46, bf16[6,128,2048]{2,1,0:T(8,128)(2,1)} %copy-done, f32[1024,2048]{1,0:T(8,128)} %get-tuple-element.158.refs_4_, ...), custom_call_target="tpu_custom_call" | custom-call | flops 2070000000 | bytes 1000 | tf_op jit(solution)/shard_map/spread/pallas_call | solution.py:931
  358.7 4.1 %finished.1 = (bf16[128,2048]{1,0:T(8,128)(2,1)}, f32[128,2048]{1,0:T(8,128)}) custom-call(bf16[2,128,2048]{2,1,0:T(8,128)(2,1)} %get-tuple-element.87.refs_0_, bf16[4,128,2048]{2,1,0:T(8,128)(2,1)} %collective-permute-done.24.refs_2_.refs_1_, bf16[4,128,2048]{2,1,0:T(8,128)(2,1)} %collective-permute-done.25.refs_3_.refs_2_, ...), custom_call_target="tpu_custom_call" | custom-call | flops 3449999872 | bytes 1000 | tf_op jit(solution)/shard_map/finished/pallas_call | solution.py:849
  364.8 3.8 %spread.5 = (f32[256,6144]{1,0:T(8,128)}, f32[256,8192]{1,0:T(8,128)}) custom-call(s32[2]{0:T(128)} %pad_add_fusion.2.refs_0_, s32[1]{0:T(128)} %bitcast.refs_1_, bf16[2,128,2048]{2,1,0:T(8,128)(2,1)} %joined.5.refs_6_.refs_2_, bf16[2,128,2048]{2,1,0:T(8,128)(2,1)} %copy-done.3, ...), custom_call_target="tpu_custom_call", output_to_operand_aliasing={{0}: (4, {}), {1}: (5, {})} | custom-call | flops 690000000 | bytes 1000 | tf_op jit(solution)/shard_map/spread/pallas_call | solution.py:931
  (195 shorter events, 105.7 us)
Async XLA Ops:
  4.3 26.1 %collective-permute-start.1 = (bf16[2,128,2048]{2,1,0:T(8,128)(2,1)}, bf16[2,128,2048]{2,1,0:T(8,128)(2,1)}, u32[]{:S(2)}, u32[]{:S(2)}) collective-permute-start(bf16[2,128,2048]{2,1,0:T(8,128)(2,1)} %get-tuple-element.66.refs_14_.refs_22_.refs_13_.refs_1_.refs_15_), channel_id=1, source_target_pairs={{0,1},{1,2},{2,3},{3,0},{4,5},{5,6},{6,7},{7,4},{8,9},{9,10},{10,1... | collective-permute-start | bytes 3145736 | tf_op jit(solution)/shard_map/ppermute | solution.py:45
  6.3 26.0 %collective-permute-start.2 = (bf16[2,128,2048]{2,1,0:T(8,128)(2,1)}, bf16[2,128,2048]{2,1,0:T(8,128)(2,1)}, u32[]{:S(2)}, u32[]{:S(2)}) collective-permute-start(bf16[2,128,2048]{2,1,0:T(8,128)(2,1)} %get-tuple-element.66.refs_14_.refs_22_.refs_13_.refs_1_.refs_15_), channel_id=1, source_target_pairs={{0,4},{1,5},{2,6},{3,7},{4,0},{5,1},{6,2},{7,3},{8,12},{9,13},{10,... | collective-permute-start | bytes 3145736 | tf_op jit(solution)/shard_map/ppermute | solution.py:45
  8.0 36.2 %collective-permute-start = (bf16[2,128,2048]{2,1,0:T(8,128)(2,1)}, bf16[2,128,2048]{2,1,0:T(8,128)(2,1)}, u32[]{:S(2)}, u32[]{:S(2)}) collective-permute-start(bf16[2,128,2048]{2,1,0:T(8,128)(2,1)} %get-tuple-element.66.refs_14_.refs_22_.refs_13_.refs_1_.refs_15_), channel_id=1, source_target_pairs={{0,3},{1,0},{2,1},{3,2},{4,7},{5,4},{6,5},{7,6},{8,11},{9,8},{10,9... | collective-permute-start | bytes 3145736 | tf_op jit(solution)/shard_map/ppermute | solution.py:45
  9.4 34.8 %all-to-all-start = ((bf16[8,40,1792]{2,1,0:T(8,128)(2,1)}), bf16[8,40,1792]{2,1,0:T(8,128)(2,1)S(1)}, u32[]{:S(2)}, u32[]{:S(2)}) async-start(bf16[8,40,1792]{2,1,0:T(8,128)(2,1)} %get-tuple-element.65), calls=%async_computation | async-start | bytes 2293760 | tf_op jit(solution)/shard_map/all_to_all | solution.py:988
  30.3 40.4 %collective-permute-start.5 = (bf16[2,128,2048]{2,1,0:T(8,128)(2,1)}, bf16[2,128,2048]{2,1,0:T(8,128)(2,1)}, u32[]{:S(2)}, u32[]{:S(2)}) collective-permute-start(bf16[2,128,2048]{2,1,0:T(8,128)(2,1)} %collective-permute-done.1.refs_2_.refs_17_.refs_25_.refs_16_.refs_4_.refs_18_), channel_id=1, source_target_pairs={{0,1},{1,2},{2,3},{3,0},{4,5},{5,6},{6,7},{7,4},{8,9},{9,10},{10,1... | collective-permute-start | bytes 3145736 | tf_op jit(solution)/shard_map/ppermute | solution.py:45
  30.7 40.0 %collective-permute-start.7 = (bf16[2,128,2048]{2,1,0:T(8,128)(2,1)}, bf16[2,128,2048]{2,1,0:T(8,128)(2,1)S(1)}, u32[]{:S(2)}, u32[]{:S(2)}) collective-permute-start(bf16[2,128,2048]{2,1,0:T(8,128)(2,1)} %collective-permute-done.1.refs_2_.refs_17_.refs_25_.refs_16_.refs_4_.refs_18_), channel_id=1, source_target_pairs={{0,4},{1,5},{2,6},{3,7},{4,0},{5,1},{6,2},{7,3},{8,12},{9,13},{10,... | collective-permute-start | bytes 3145736 | tf_op jit(solution)/shard_map/ppermute | solution.py:45
  32.3 38.4 %collective-permute-start.6 = (bf16[2,128,2048]{2,1,0:T(8,128)(2,1)}, bf16[2,128,2048]{2,1,0:T(8,128)(2,1)}, u32[]{:S(2)}, u32[]{:S(2)}) collective-permute-start(bf16[2,128,2048]{2,1,0:T(8,128)(2,1)} %collective-permute-done.2.refs_3_.refs_18_.refs_26_.refs_17_.refs_5_.refs_19_), channel_id=1, source_target_pairs={{0,3},{1,0},{2,1},{3,2},{4,7},{5,4},{6,5},{7,6},{8,11},{9,8},{10,9... | collective-permute-start | bytes 3145736 | tf_op jit(solution)/shard_map/ppermute | solution.py:45
  47.7 20.0 %collective-permute-start.3 = (bf16[8,32,1792]{2,1,0:T(8,128)(2,1)}, bf16[8,32,1792]{2,1,0:T(8,128)(2,1)S(1)}, u32[]{:S(2)}, u32[]{:S(2)}) collective-permute-start(bf16[8,32,1792]{2,1,0:T(8,128)(2,1)} %get-tuple-element.68.refs_0_.refs_4_.refs_3_.refs_5_), channel_id=1, source_target_pairs={{0,96},{1,97},{2,98},{3,99},{4,100},{5,101},{6,102},{7,103},{8,104... | collective-permute-start | bytes 2752520 | tf_op jit(solution)/shard_map/ppermute | solution.py:45
  50.4 20.3 %collective-permute-start.4 = (bf16[8,32,1792]{2,1,0:T(8,128)(2,1)}, bf16[8,32,1792]{2,1,0:T(8,128)(2,1)S(1)}, u32[]{:S(2)}, u32[]{:S(2)}) collective-permute-start(bf16[8,32,1792]{2,1,0:T(8,128)(2,1)} %get-tuple-element.68.refs_0_.refs_4_.refs_3_.refs_5_), channel_id=1, source_target_pairs={{0,32},{1,33},{2,34},{3,35},{4,36},{5,37},{6,38},{7,39},{8,40},{9,... | collective-permute-start | bytes 2752520 | tf_op jit(solution)/shard_map/ppermute | solution.py:45
  75.9 26.0 %collective-permute-start.10 = (bf16[24,32,1792]{2,1,0:T(8,128)(2,1)}, bf16[24,32,1792]{2,1,0:T(8,128)(2,1)S(1)}, u32[]{:S(2)}, u32[]{:S(2)}) collective-permute-start(bf16[24,32,1792]{2,1,0:T(8,128)(2,1)} %bitcast.66), channel_id=1, source_target_pairs={{0,8},{1,9},{2,10},{3,11},{4,12},{5,13},{6,14},{7,15},{8,0},{9,1},... | collective-permute-start | bytes 8257544 | tf_op jit(solution)/shard_map/ppermute | solution.py:45
  82.9 13.6 %collective-permute-start.8 = (bf16[4,32,1792]{2,1,0:T(8,128)(2,1)}, bf16[4,32,1792]{2,1,0:T(8,128)(2,1)S(1)}, u32[]{:S(2)}, u32[]{:S(2)}) collective-permute-start(bf16[4,32,1792]{2,1,0:T(8,128)(2,1)} %get-tuple-element.69), channel_id=1, source_target_pairs={{0,32},{1,33},{2,34},{3,35},{4,36},{5,37},{6,38},{7,39},{8,40},{9,... | collective-permute-start | bytes 1376264 | tf_op jit(solution)/shard_map/ppermute | solution.py:45
  83.0 14.3 %collective-permute-start.9 = (bf16[4,32,1792]{2,1,0:T(8,128)(2,1)}, bf16[4,32,1792]{2,1,0:T(8,128)(2,1)S(1)}, u32[]{:S(2)}, u32[]{:S(2)}) collective-permute-start(bf16[4,32,1792]{2,1,0:T(8,128)(2,1)} %get-tuple-element.70), channel_id=1, source_target_pairs={{0,96},{1,97},{2,98},{3,99},{4,100},{5,101},{6,102},{7,103},{8,104... | collective-permute-start | bytes 1376264 | tf_op jit(solution)/shard_map/ppermute | solution.py:45
  86.8 14.2 %collective-permute-start.13 = (bf16[128,2048]{1,0:T(8,128)(2,1)S(1)}, bf16[128,2048]{1,0:T(8,128)(2,1)S(1)}, u32[]{:S(2)}, u32[]{:S(2)}) collective-permute-start(bf16[128,2048]{1,0:T(8,128)(2,1)S(1)} %slice_bitcast_fusion.1), channel_id=1, source_target_pairs={{0,1},{1,2},{2,3},{3,0},{4,5},{5,6},{6,7},{7,4},{8,9},{9,10},{10,1... | collective-permute-start | bytes 1572872 | tf_op jit(solution)/shard_map/ppermute | solution.py:45
  136.0 21.3 %collective-permute-start.15 = (bf16[8,128,2048]{2,1,0:T(8,128)(2,1)}, bf16[8,128,2048]{2,1,0:T(8,128)(2,1)}, u32[]{:S(2)}, u32[]{:S(2)}) collective-permute-start(bf16[8,128,2048]{2,1,0:T(8,128)(2,1)} %get-tuple-element.75.refs_25_), channel_id=1, source_target_pairs={{0,8},{1,9},{2,10},{3,11},{4,12},{5,13},{6,14},{7,15},{8,0},{9,1},... | collective-permute-start | bytes 12582920 | tf_op jit(solution)/shard_map/ppermute | solution.py:45
  160.6 17.1 %collective-permute-start.17 = (bf16[1,128,2048]{2,1,0:T(8,128)(2,1)}, bf16[1,128,2048]{2,1,0:T(8,128)(2,1)S(1)}, u32[]{:S(2)}, u32[]{:S(2)}) collective-permute-start(bf16[1,128,2048]{2,1,0:T(8,128)(2,1)} %get-tuple-element.81.refs_12_), channel_id=1, source_target_pairs={{0,32},{1,33},{2,34},{3,35},{4,36},{5,37},{6,38},{7,39},{8,40},{9,... | collective-permute-start | bytes 1572872 | tf_op jit(solution)/shard_map/ppermute | solution.py:45
  160.6 17.1 %collective-permute-start.18 = (bf16[1,128,2048]{2,1,0:T(8,128)(2,1)}, bf16[1,128,2048]{2,1,0:T(8,128)(2,1)S(1)}, u32[]{:S(2)}, u32[]{:S(2)}) collective-permute-start(bf16[1,128,2048]{2,1,0:T(8,128)(2,1)} %get-tuple-element.82.refs_13_), channel_id=1, source_target_pairs={{0,96},{1,97},{2,98},{3,99},{4,100},{5,101},{6,102},{7,103},{8,104... | collective-permute-start | bytes 1572872 | tf_op jit(solution)/shard_map/ppermute | solution.py:45
  184.1 40.2 %collective-permute-start.21 = (bf16[2,128,2048]{2,1,0:T(8,128)(2,1)}, bf16[2,128,2048]{2,1,0:T(8,128)(2,1)S(1)}, u32[]{:S(2)}, u32[]{:S(2)}) collective-permute-start(bf16[2,128,2048]{2,1,0:T(8,128)(2,1)} %get-tuple-element.85.refs_5_.refs_30_), channel_id=1, source_target_pairs={{0,32},{1,33},{2,34},{3,35},{4,36},{5,37},{6,38},{7,39},{8,40},{9,... | collective-permute-start | bytes 3145736 | tf_op jit(solution)/shard_map/ppermute | solution.py:45
  184.1 40.2 %collective-permute-start.22 = (bf16[2,128,2048]{2,1,0:T(8,128)(2,1)}, bf16[2,128,2048]{2,1,0:T(8,128)(2,1)}, u32[]{:S(2)}, u32[]{:S(2)}) collective-permute-start(bf16[2,128,2048]{2,1,0:T(8,128)(2,1)} %get-tuple-element.86.refs_31_), channel_id=1, source_target_pairs={{0,96},{1,97},{2,98},{3,99},{4,100},{5,101},{6,102},{7,103},{8,104... | collective-permute-start | bytes 3145736 | tf_op jit(solution)/shard_map/ppermute | solution.py:45
  192.7 54.0 %all-to-all-start.1 = ((bf16[8,64,2048]{2,1,0:T(8,128)(2,1)}), bf16[8,64,2048]{2,1,0:T(8,128)(2,1)S(1)}, u32[]{:S(2)}, u32[]{:S(2)}) async-start(bf16[8,64,2048]{2,1,0:T(8,128)(2,1)} %both_sums.1.refs_29_), calls=%async_computation.1 | async-start | bytes 4194304 | tf_op jit(solution)/shard_map/all_to_all | solution.py:1116
  221.4 33.8 %collective-permute-start.19 = (bf16[2,128,2048]{2,1,0:T(8,128)(2,1)}, bf16[2,128,2048]{2,1,0:T(8,128)(2,1)}, u32[]{:S(2)}, u32[]{:S(2)}) collective-permute-start(bf16[2,128,2048]{2,1,0:T(8,128)(2,1)} %get-tuple-element.89), channel_id=1, source_target_pairs={{0,1},{1,2},{2,3},{3,0},{4,5},{5,6},{6,7},{7,4},{8,9},{9,10},{10,1... | collective-permute-start | bytes 3145736 | tf_op jit(solution)/shard_map/ppermute | solution.py:45
  221.9 33.3 %collective-permute-start.20 = (bf16[2,128,2048]{2,1,0:T(8,128)(2,1)}, bf16[2,128,2048]{2,1,0:T(8,128)(2,1)}, u32[]{:S(2)}, u32[]{:S(2)}) collective-permute-start(bf16[2,128,2048]{2,1,0:T(8,128)(2,1)} %get-tuple-element.92), channel_id=1, source_target_pairs={{0,3},{1,0},{2,1},{3,2},{4,7},{5,4},{6,5},{7,6},{8,11},{9,8},{10,9... | collective-permute-start | bytes 3145736 | tf_op jit(solution)/shard_map/ppermute | solution.py:45
  229.6 17.1 %collective-permute-start.23 = (bf16[1,128,2048]{2,1,0:T(8,128)(2,1)}, bf16[1,128,2048]{2,1,0:T(8,128)(2,1)S(1)}, u32[]{:S(2)}, u32[]{:S(2)}) collective-permute-start(bf16[1,128,2048]{2,1,0:T(8,128)(2,1)} %get-tuple-element.96), channel_id=1, source_target_pairs={{0,16},{1,17},{2,18},{3,19},{4,20},{5,21},{6,22},{7,23},{8,24},{9,... | collective-permute-start | bytes 1572872 | tf_op jit(solution)/shard_map/ppermute | solution.py:45
  251.7 14.9 %all-to-all-start.2 = ((bf16[8,16,2048]{2,1,0:T(8,128)(2,1)}), bf16[8,16,2048]{2,1,0:T(8,128)(2,1)S(1)}, u32[]{:S(2)}, u32[]{:S(2)}) async-start(bf16[8,16,2048]{2,1,0:T(8,128)(2,1)} %get-tuple-element.100.refs_7_), calls=%async_computation.2 | async-start | bytes 1048576 | tf_op jit(solution)/shard_map/all_to_all | solution.py:1178
  261.1 46.4 %collective-permute-start.24 = (bf16[4,128,2048]{2,1,0:T(8,128)(2,1)}, bf16[4,128,2048]{2,1,0:T(8,128)(2,1)}, u32[]{:S(2)}, u32[]{:S(2)}) collective-permute-start(bf16[4,128,2048]{2,1,0:T(8,128)(2,1)} %get-tuple-element.101.refs_1_), channel_id=1, source_target_pairs={{0,1},{1,2},{2,3},{3,0},{4,5},{5,6},{6,7},{7,4},{8,9},{9,10},{10,1... | collective-permute-start | bytes 6291464 | tf_op jit(solution)/shard_map/ppermute | solution.py:45
  262.5 45.1 %collective-permute-start.25 = (bf16[4,128,2048]{2,1,0:T(8,128)(2,1)}, bf16[4,128,2048]{2,1,0:T(8,128)(2,1)}, u32[]{:S(2)}, u32[]{:S(2)}) collective-permute-start(bf16[4,128,2048]{2,1,0:T(8,128)(2,1)} %get-tuple-element.102), channel_id=1, source_target_pairs={{0,3},{1,0},{2,1},{3,2},{4,7},{5,4},{6,5},{7,6},{8,11},{9,8},{10,9... | collective-permute-start | bytes 6291464 | tf_op jit(solution)/shard_map/ppermute | solution.py:45
  264.7 16.8 %collective-permute-start.30 = (bf16[2,80,2048]{2,1,0:T(8,128)(2,1)S(1)}, bf16[2,80,2048]{2,1,0:T(8,128)(2,1)S(1)}, u32[]{:S(2)}, u32[]{:S(2)}) collective-permute-start(bf16[2,80,2048]{2,1,0:T(8,128)(2,1)S(1)} %pad_maximum_fusion.refs_2_.refs_0_), channel_id=1, source_target_pairs={{0,96},{1,97},{2,98},{3,99},{4,100},{5,101},{6,102},{7,103},{8,104... | collective-permute-start | bytes 1966088 | tf_op jit(solution)/shard_map/ppermute | solution.py:45
  285.4 27.1 %collective-permute-start.31 = (bf16[2,128,2048]{2,1,0:T(8,128)(2,1)}, bf16[2,128,2048]{2,1,0:T(8,128)(2,1)S(1)}, u32[]{:S(2)}, u32[]{:S(2)}) collective-permute-start(bf16[2,128,2048]{2,1,0:T(8,128)(2,1)} %joined.3.refs_0_), channel_id=1, source_target_pairs={{0,32},{1,33},{2,34},{3,35},{4,36},{5,37},{6,38},{7,39},{8,40},{9,... | collective-permute-start | bytes 3145736 | tf_op jit(solution)/shard_map/ppermute | solution.py:45
  285.4 27.1 %collective-permute-start.32 = (bf16[2,128,2048]{2,1,0:T(8,128)(2,1)}, bf16[2,128,2048]{2,1,0:T(8,128)(2,1)S(1)}, u32[]{:S(2)}, u32[]{:S(2)}) collective-permute-start(bf16[2,128,2048]{2,1,0:T(8,128)(2,1)} %joined.3.refs_0_), channel_id=1, source_target_pairs={{0,96},{1,97},{2,98},{3,99},{4,100},{5,101},{6,102},{7,103},{8,104... | collective-permute-start | bytes 3145736 | tf_op jit(solution)/shard_map/ppermute | solution.py:45
  317.9 24.2 %collective-permute-start.36 = (bf16[6,128,2048]{2,1,0:T(8,128)(2,1)}, bf16[6,128,2048]{2,1,0:T(8,128)(2,1)S(1)}, u32[]{:S(2)}, u32[]{:S(2)}) collective-permute-start(bf16[6,128,2048]{2,1,0:T(8,128)(2,1)} %bitcast.45), channel_id=1, source_target_pairs={{0,8},{1,9},{2,10},{3,11},{4,12},{5,13},{6,14},{7,15},{8,0},{9,1},... | collective-permute-start | bytes 9437192 | tf_op jit(solution)/shard_map/ppermute | solution.py:45
  324.3 28.1 %collective-permute-start.34 = (bf16[1,128,2048]{2,1,0:T(8,128)(2,1)}, bf16[1,128,2048]{2,1,0:T(8,128)(2,1)}, u32[]{:S(2)}, u32[]{:S(2)}) collective-permute-start(bf16[1,128,2048]{2,1,0:T(8,128)(2,1)} %get-tuple-element.105), channel_id=1, source_target_pairs={{0,32},{1,33},{2,34},{3,35},{4,36},{5,37},{6,38},{7,39},{8,40},{9,... | collective-permute-start | bytes 1572872 | tf_op jit(solution)/shard_map/ppermute | solution.py:45
  324.3 28.1 %collective-permute-start.35 = (bf16[1,128,2048]{2,1,0:T(8,128)(2,1)}, bf16[1,128,2048]{2,1,0:T(8,128)(2,1)}, u32[]{:S(2)}, u32[]{:S(2)}) collective-permute-start(bf16[1,128,2048]{2,1,0:T(8,128)(2,1)} %get-tuple-element.106), channel_id=1, source_target_pairs={{0,96},{1,97},{2,98},{3,99},{4,100},{5,101},{6,102},{7,103},{8,104... | collective-permute-start | bytes 1572872 | tf_op jit(solution)/shard_map/ppermute | solution.py:45
  328.1 29.5 %collective-permute-start.26 = (bf16[2,128,2048]{2,1,0:T(8,128)(2,1)}, bf16[2,128,2048]{2,1,0:T(8,128)(2,1)S(1)}, u32[]{:S(2)}, u32[]{:S(2)}) collective-permute-start(bf16[2,128,2048]{2,1,0:T(8,128)(2,1)} %other_sums.1.refs_4_.refs_5_), channel_id=1, source_target_pairs={{0,4},{1,5},{2,6},{3,7},{4,0},{5,1},{6,2},{7,3},{8,12},{9,13},{10,... | collective-permute-start | bytes 3145736 | tf_op jit(solution)/shard_map/ppermute | solution.py:45
  (45 other events, 338.3 us)

commit v13 on v12

--- a/solution.py
+++ b/solution.py
@@ -856,7 +856,7 @@
         in_specs=[pair(0), pair(1), pair(0), pair(0), block, block] + anywhere(len(after)),
         out_specs=(block, block),
         compiler_params=kernel_params(),
-        cost_estimate=cost(3),
+        cost_estimate=cost(14),
         name="finished",
     )(own, below, above, other, tokens, cotangent, *after)
 
@@ -887,7 +887,7 @@
     return functools.reduce(jnp.add, [ref[...].astype(f32) for ref in refs])
 
 
-def spread(pieces, places, core, targets, count, before, after):
+def spread(pieces, places, core, targets, count, before, after, time=2):
     rows, cols = pieces[0][0].shape[1:]
     firsts, total = [], 0
     for mine, _ in pieces:
@@ -944,7 +944,7 @@
         ),
         input_output_aliases={2 + len(arrays) + n: n for n in range(len(before))},
         compiler_params=kernel_params(),
-        cost_estimate=cost(0.3 * total),
+        cost_estimate=cost(time),
         name="spread",
     )(places, core, *arrays, *before, *after)
 
@@ -1225,6 +1225,7 @@
         8,
         (),
         (),
+        14,
     )
     part = joined((part, move(part, h=1)), beside)
     below, above = move(part, y=1), move(part, y=-1)

time: 371 us -> 369 us (level)
  waiting for transfers between devices: 94.7 us -> 78.8 us
  starting transfers between devices: 70.7 us -> 83.5 us
    ppermute x39, waiting for transfers between devices: 85.5 us -> 69.5 us  [move(): return lax.ppermute(value, BOTH, pairs)]
    ppermute x39, starting transfers between devices: 59.1 us -> 71.9 us  [move(): return lax.ppermute(value, BOTH, pairs)]
    unnamed x77 -> x81, local copies, waits for them, and re-layouts: 20 us -> 20.9 us
  transfers between devices with their start and end apart: 42 -> 42, of which waited for: 14 -> 13; matrix products, arithmetic and copies ran while one was open for 5% -> 5% of each run, Pallas kernels for 31% -> 32%
where the time goes in v13:
time: 369 us; the launch traced here: 367 us
  Pallas kernels  165 us (45%)
  starting transfers between devices  83.5 us (23%)
  waiting for transfers between devices  78.8 us (21%)
  local copies, waits for them, and re-layouts  30.9 us (8%)
  other arithmetic  7.24 us (2%)
    ppermute x39, starting transfers between devices, move(): return lax.ppermute(value, BOTH, pairs)  71.9 us
    ppermute x39, waiting for transfers between devices, move(): return lax.ppermute(value, BOTH, pairs)  69.5 us
    pallas_call x1, Pallas kernels, feed_forward(): pl.pallas_call(after_inputs(body, 5 + parts + 2 * count, len(after)), out...  32.2 us
    pallas_call x6, Pallas kernels, blocks_call(): pl.pallas_call(after_inputs(body, 1 + len(terms), len(after)), out_shape=...  26.8 us
    pallas_call x1, Pallas kernels, outer(): pl.pallas_call(after_inputs(body, 11 + parts + count, len(after)), out_sh...  24.2 us
    pallas_call x3, Pallas kernels, spread(): pl.pallas_call(after_inputs(body, 2 + 2 * len(pieces) + len(before), len(...  21 us
    unnamed x81, local copies, waits for them, and re-layouts  20.9 us
    pallas_call x1, Pallas kernels, attend(): pl.pallas_call(after_inputs(body, 7 + parts + count, len(after)), out_sha...  17.1 us
  transfers between devices with their start and end apart: 42, of which 13 were waited for; matrix products, arithmetic and copies ran while one was open for 5% of the time, Pallas kernels for 32%

profile of v13, /device:TPU:1, one launch (start us, length us, event | category | flops | bytes accessed | tf_op | source)
XLA Modules:
  0.0 366.9 jit_solution(7013410045107691314)
XLA Ops:
  0.7 3.6 packed.1
  9.4 3.6 all-to-all-start
  13.0 17.3 %collective-permute-done.1.refs_2_.refs_17_.refs_25_.refs_16_.refs_4_.refs_18_ = bf16[2,128,2048]{2,1,0:T(8,128)(2,1)} collective-permute-done((bf16[2,128,2048]{2,1,0:T(8,128)(2,1)}, bf16[2,128,2048]{2,1,0:T(8,128)(2,1)}, u32[]{:S(2)}, u32[]{:S(2)}) %collective-permute-start.1) | collective-permute-done | bytes 1048608 | tf_op jit(solution)/shard_map/ppermute | solution.py:45
  35.0 9.2 %all-to-all-done.refs_0_ = bf16[8,40,1792]{2,1,0:T(8,128)(2,1)S(1)} async-done(((bf16[8,40,1792]{2,1,0:T(8,128)(2,1)}), bf16[8,40,1792]{2,1,0:T(8,128)(2,1)S(1)}, u32[]{:S(2)}, u32[]{:S(2)}) %all-to-all-start) | async-done | bytes 1146912 | tf_op jit(solution)/shard_map/all_to_all | solution.py:988
  51.6 16.1 %collective-permute-done.3.refs_2_.refs_5_.refs_4_.refs_6_ = bf16[8,32,1792]{2,1,0:T(8,128)(2,1)S(1)} collective-permute-done((bf16[8,32,1792]{2,1,0:T(8,128)(2,1)}, bf16[8,32,1792]{2,1,0:T(8,128)(2,1)S(1)}, u32[]{:S(2)}, u32[]{:S(2)}) %collective-permute-start.3) | collective-permute-done | bytes 917536 | tf_op jit(solution)/shard_map/ppermute | solution.py:45
  72.6 3.3 halves.2
  75.8 3.9 %collective-permute-start.10 = (bf16[24,32,1792]{2,1,0:T(8,128)(2,1)}, bf16[24,32,1792]{2,1,0:T(8,128)(2,1)S(1)}, u32[]{:S(2)}, u32[]{:S(2)}) collective-permute-start(bf16[24,32,1792]{2,1,0:T(8,128)(2,1)} %bitcast.66), channel_id=1, source_target_pairs={{0,8},{1,9},{2,10},{3,11},{4,12},{5,13},{6,14},{7,15},{8,0},{9,1},... | collective-permute-start | bytes 8257544 | tf_op jit(solution)/shard_map/ppermute | solution.py:45
  91.3 5.2 %collective-permute-done.8.refs_6_.refs_5_.refs_7_ = bf16[4,32,1792]{2,1,0:T(8,128)(2,1)S(1)} collective-permute-done((bf16[4,32,1792]{2,1,0:T(8,128)(2,1)}, bf16[4,32,1792]{2,1,0:T(8,128)(2,1)S(1)}, u32[]{:S(2)}, u32[]{:S(2)}) %collective-permute-start.8) | collective-permute-done | bytes 458784 | tf_op jit(solution)/shard_map/ppermute | solution.py:45
  103.7 32.2 %feed_forward.1 = (bf16[1024,2048]{1,0:T(8,128)(2,1)}, bf16[1024,1024]{1,0:T(8,128)(2,1)}, bf16[1024,1024]{1,0:T(8,128)(2,1)}, bf16[8,128,2048]{2,1,0:T(8,128)(2...) custom-call(s32[4]{0:T(128)} %get-tuple-element.128.refs_0_.refs_7_,, ...), custom_call_target="tpu_custom_call" | custom-call | flops 36800000000 | bytes 1000 | tf_op jit(solution)/shard_map/feed_forward/pallas_call | solution.py:258
  140.0 17.1 %attend.1 = (bf16[1024,256]{1,0:T(8,128)(2,1)}, bf16[1024,768]{1,0:T(8,128)(2,1)}, f32[1,768]{1,0:T(1,128)}) custom-call(s32[8,3]{1,0:T(8,128)} %copy-done.8, s32[8]{0:T(128)} %pad_add_fusion.refs_1_.refs_0_, f32[3,1,256]{2,1,0:T(1,128)} %pad_maximum_fusion.2.refs_2_, bf16[8,32,1792]{2,1,0:T(8,128)(2,1)} %get-tuple-element.68.refs_0_.refs_4_.refs_3_.refs_5_, ...), custom_call_target="tpu_custom_call" | custom-call | flops 19549999104 | bytes 1000 | tf_op jit(solution)/shard_map/attend/pallas_call | solution.py:431
  157.2 3.4 far_sums.1
  163.2 13.5 %attention_grads.1 = (bf16[8,64,2048]{2,1,0:T(8,128)(2,1)}, bf16[8,64,2048]{2,1,0:T(8,128)(2,1)}) custom-call(s32[4]{0:T(128)} %get-tuple-element.128.refs_0_.refs_7_, bf16[2,128,2048]{2,1,0:T(8,128)(2,1)} %get-tuple-element.66.refs_14_.refs_22_.refs_13_.refs_1_.refs_15_, ...), custom_call_target="tpu_custom_call" | custom-call | flops 13799999488 | bytes 1000 | tf_op jit(solution)/shard_map/attention_grads/pallas_call | solution.py:527
  179.2 4.8 %near_sums.1 = (bf16[2,128,2048]{2,1,0:T(8,128)(2,1)}, bf16[2,128,2048]{2,1,0:T(8,128)(2,1)}) custom-call(s32[4]{0:T(128)} %get-tuple-element.128.refs_0_.refs_7_, bf16[8,128,2048]{2,1,0:T(8,128)(2,1)} %get-tuple-element.80.refs_1_.refs_3_, bf16[8,128,2048]{2,1,0:T(8,128)(2,1)} %collective-permute-done.15.refs_2_.refs_4_, ...), custom_call_target="tpu_custom_call" | custom-call | flops 23000000512 | bytes 1000 | tf_op jit(solution)/shard_map/near_sums/pallas_call | solution.py:869
  188.0 4.6 %both_sums.1.refs_29_ = bf16[8,64,2048]{2,1,0:T(8,128)(2,1)} custom-call(s32[4]{0:T(128)} %get-tuple-element.128.refs_0_.refs_7_, bf16[8,64,2048]{2,1,0:T(8,128)(2,1)} %get-tuple-element.83.refs_1_.refs_3_, bf16[8,64,2048]{2,1,0:T(8,128)(2,1)} %copy-done.15, bf16[8,64,2048]{2,1,0:T(8,128)(2,1)} %get-tuple-element.83.refs_1_.refs_3_, ...), custom_call_target="tpu_custom_call" | custom-call | flops 3449999872 | bytes 1000 | tf_op jit(solution)/shard_map/both_sums/pallas_call | solution.py:869
  192.6 4.6 %all-to-all-start.1 = ((bf16[8,64,2048]{2,1,0:T(8,128)(2,1)}), bf16[8,64,2048]{2,1,0:T(8,128)(2,1)S(1)}, u32[]{:S(2)}, u32[]{:S(2)}) async-start(bf16[8,64,2048]{2,1,0:T(8,128)(2,1)} %both_sums.1.refs_29_), calls=%async_computation.1 | async-start | bytes 4194304 | tf_op jit(solution)/shard_map/all_to_all | solution.py:1116
  197.2 24.2 %outer.1 = (f32[4,2048]{1,0:T(4,128)}, bf16[2,128,2048]{2,1,0:T(8,128)(2,1)}, bf16[2,128,2048]{2,1,0:T(8,128)(2,1)}, bf16[2,128,2048]{2,1,0:T(8,128)(2,1)}, bf16...) custom-call(s32[8]{0:T(128)} %pad_add_fusion.refs_1_.refs_0_, ...), custom_call_target="tpu_custom_call" | custom-call | flops 23000000512 | bytes 1000 | tf_op jit(solution)/shard_map/outer/pallas_call | solution.py:622
  225.3 4.3 %end_sums.1 = (bf16[1,128,2048]{2,1,0:T(8,128)(2,1)}, bf16[1,128,2048]{2,1,0:T(8,128)(2,1)}) custom-call(s32[4]{0:T(128)} %get-tuple-element.128.refs_0_.refs_7_, bf16[8,128,2048]{2,1,0:T(8,128)(2,1)} %get-tuple-element.80.refs_1_.refs_3_, bf16[8,128,2048]{2,1,0:T(8,128)(2,1)} %collective-permute-done.15.refs_2_.refs_4_, bf16[2,128,2048]{2,1,0:T(8,128)(2,1)} %copy-done.16, ...), custom_call_target="tpu_custom_call" | custom-call | flops 3449999872 | bytes 1000 | tf_op jit(solution)/shard_map/end_sums/pallas_call | solution.py:869
  232.6 14.1 %collective-permute-done.23.refs_1_ = bf16[1,128,2048]{2,1,0:T(8,128)(2,1)S(1)} collective-permute-done((bf16[1,128,2048]{2,1,0:T(8,128)(2,1)}, bf16[1,128,2048]{2,1,0:T(8,128)(2,1)S(1)}, u32[]{:S(2)}, u32[]{:S(2)}) %collective-permute-start.23) | collective-permute-done | bytes 524320 | tf_op jit(solution)/shard_map/ppermute | solution.py:45
  248.2 3.5 packed_sums.1
  251.7 3.5 all-to-all-start.2
  255.3 5.9 %passed_sums.1 = (bf16[4,128,2048]{2,1,0:T(8,128)(2,1)}, bf16[4,128,2048]{2,1,0:T(8,128)(2,1)}) custom-call(s32[4]{0:T(128)} %get-tuple-element.128.refs_0_.refs_7_, bf16[2,128,2048]{2,1,0:T(8,128)(2,1)} %get-tuple-element.88.refs_1_, bf16[2,128,2048]{2,1,0:T(8,128)(2,1)} %collective-permute-done.19.refs_2_, ...), custom_call_target="tpu_custom_call" | custom-call | flops 3449999872 | bytes 1000 | tf_op jit(solution)/shard_map/passed_sums/pallas_call | solution.py:869
  272.3 4.6 %collective-permute-done.29.refs_2_ = bf16[2,80,2048]{2,1,0:T(8,128)(2,1)S(1)} collective-permute-done((bf16[2,80,2048]{2,1,0:T(8,128)(2,1)S(1)}, bf16[2,80,2048]{2,1,0:T(8,128)(2,1)S(1)}, u32[]{:S(2)}, u32[]{:S(2)}) %collective-permute-start.29) | collective-permute-done | bytes 655392 | tf_op jit(solution)/shard_map/ppermute | solution.py:45
  277.4 4.2 %collective-permute-done.28.refs_1_ = bf16[1,128,2048]{2,1,0:T(8,128)(2,1)S(1)} collective-permute-done((bf16[1,128,2048]{2,1,0:T(8,128)(2,1)}, bf16[1,128,2048]{2,1,0:T(8,128)(2,1)S(1)}, u32[]{:S(2)}, u32[]{:S(2)}) %collective-permute-start.28) | collective-permute-done | bytes 524320 | tf_op jit(solution)/shard_map/ppermute | solution.py:45
  291.0 3.7 %joined.4.refs_3_.refs_2_ = bf16[8,80,2048]{2,1,0:T(8,128)(2,1)} custom-call(bf16[2,80,2048]{2,1,0:T(8,128)(2,1)} %copy-done.4, bf16[2,80,2048]{2,1,0:T(8,128)(2,1)} %copy-done.23, bf16[2,80,2048]{2,1,0:T(8,128)(2,1)} %copy-done.22, bf16[2,80,2048]{2,1,0:T(8,128)(2,1)} %copy-done.24), custom_call_target="tpu_custom_call" | custom-call | flops 3449999872 | bytes 1000 | tf_op jit(solution)/shard_map/joined/pallas_call | solution.py:706
  294.7 12.1 %collective-permute-start.37 = (bf16[8,80,2048]{2,1,0:T(8,128)(2,1)}, bf16[8,80,2048]{2,1,0:T(8,128)(2,1)}, u32[]{:S(2)}, u32[]{:S(2)}) collective-permute-start(bf16[8,80,2048]{2,1,0:T(8,128)(2,1)} %joined.4.refs_3_.refs_2_), channel_id=1, source_target_pairs={{0,8},{1,9},{2,10},{3,11},{4,12},{5,13},{6,14},{7,15},{8,0},{9,1},... | collective-permute-start | bytes 7864328 | tf_op jit(solution)/shard_map/ppermute | solution.py:45
  307.6 3.9 %other_sums.1.refs_4_.refs_5_ = bf16[2,128,2048]{2,1,0:T(8,128)(2,1)} custom-call(s32[4]{0:T(128)} %get-tuple-element.128.refs_0_.refs_7_, bf16[2,128,2048]{2,1,0:T(8,128)(2,1)} %get-tuple-element.103.refs_1_, bf16[4,128,2048]{2,1,0:T(8,128)(2,1)} %collective-permute-done.24.refs_2_.refs_1_, bf16[4,128,2048]{2,1,0:T(8,128)(2,1)} %collective-permute-done.25.refs_3_.refs_2_), custom_call_target="tpu_custom_call" | custom-call | flops 3449999872 | bytes 1000 | tf_op jit(solution)/shard_map/other_sums/pallas_call | solution.py:869
  314.5 3.5 halves.3
  318.0 6.3 %collective-permute-start.36 = (bf16[6,128,2048]{2,1,0:T(8,128)(2,1)}, bf16[6,128,2048]{2,1,0:T(8,128)(2,1)S(1)}, u32[]{:S(2)}, u32[]{:S(2)}) collective-permute-start(bf16[6,128,2048]{2,1,0:T(8,128)(2,1)} %bitcast.45), channel_id=1, source_target_pairs={{0,8},{1,9},{2,10},{3,11},{4,12},{5,13},{6,14},{7,15},{8,0},{9,1},... | collective-permute-start | bytes 9437192 | tf_op jit(solution)/shard_map/ppermute | solution.py:45
  331.0 8.7 %spread.3 = (f32[1024,2048]{1,0:T(8,128)}, f32[256,2048]{1,0:T(8,128)}) custom-call(s32[8]{0:T(128)} %stack.71.refs_0_, s32[1]{0:T(128)} %bitcast.refs_1_, bf16[8,80,2048]{2,1,0:T(8,128)(2,1)} %joined.4.refs_3_.refs_2_, bf16[8,80,2048]{2,1,0:T(8,128)(2,1)} %collective-permute-done.37.refs_3_), custom_call_target="tpu_custom_call" | custom-call | flops 16099999744 | bytes 1000 | tf_op jit(solution)/shard_map/spread/pallas_call | solution.py:931
  341.3 8.5 %spread.4 = (f32[256,6144]{1,0:T(8,128)}, f32[256,8192]{1,0:T(8,128)}) custom-call(s32[6]{0:T(128)} %stack.68.refs_0_, s32[1]{0:T(128)} %bitcast.refs_1_, bf16[6,128,2048]{2,1,0:T(8,128)(2,1)} %bitcast.47, bf16[6,128,2048]{2,1,0:T(8,128)(2,1)} %copy-done, f32[1024,2048]{1,0:T(8,128)} %get-tuple-element.158.refs_4_, ...), custom_call_target="tpu_custom_call" | custom-call | flops 2300000000 | bytes 1000 | tf_op jit(solution)/shard_map/spread/pallas_call | solution.py:931
  356.4 4.1 %finished.1 = (bf16[128,2048]{1,0:T(8,128)(2,1)}, f32[128,2048]{1,0:T(8,128)}) custom-call(bf16[2,128,2048]{2,1,0:T(8,128)(2,1)} %get-tuple-element.87.refs_0_, bf16[4,128,2048]{2,1,0:T(8,128)(2,1)} %collective-permute-done.24.refs_2_.refs_1_, bf16[4,128,2048]{2,1,0:T(8,128)(2,1)} %collective-permute-done.25.refs_3_.refs_2_, ...), custom_call_target="tpu_custom_call" | custom-call | flops 16099999744 | bytes 1000 | tf_op jit(solution)/shard_map/finished/pallas_call | solution.py:849
  362.5 3.8 %spread.5 = (f32[256,6144]{1,0:T(8,128)}, f32[256,8192]{1,0:T(8,128)}) custom-call(s32[2]{0:T(128)} %pad_add_fusion.2.refs_0_, s32[1]{0:T(128)} %bitcast.refs_1_, bf16[2,128,2048]{2,1,0:T(8,128)(2,1)} %joined.5.refs_6_.refs_2_, bf16[2,128,2048]{2,1,0:T(8,128)(2,1)} %copy-done.3, ...), custom_call_target="tpu_custom_call", output_to_operand_aliasing={{0}: (4, {}), {1}: (5, {})} | custom-call | flops 2300000000 | bytes 1000 | tf_op jit(solution)/shard_map/spread/pallas_call | solution.py:931
  (199 shorter events, 104.5 us)
Async XLA Ops:
  4.3 26.1 %collective-permute-start.1 = (bf16[2,128,2048]{2,1,0:T(8,128)(2,1)}, bf16[2,128,2048]{2,1,0:T(8,128)(2,1)}, u32[]{:S(2)}, u32[]{:S(2)}) collective-permute-start(bf16[2,128,2048]{2,1,0:T(8,128)(2,1)} %get-tuple-element.66.refs_14_.refs_22_.refs_13_.refs_1_.refs_15_), channel_id=1, source_target_pairs={{0,1},{1,2},{2,3},{3,0},{4,5},{5,6},{6,7},{7,4},{8,9},{9,10},{10,1... | collective-permute-start | bytes 3145736 | tf_op jit(solution)/shard_map/ppermute | solution.py:45
  6.3 26.0 %collective-permute-start.2 = (bf16[2,128,2048]{2,1,0:T(8,128)(2,1)}, bf16[2,128,2048]{2,1,0:T(8,128)(2,1)}, u32[]{:S(2)}, u32[]{:S(2)}) collective-permute-start(bf16[2,128,2048]{2,1,0:T(8,128)(2,1)} %get-tuple-element.66.refs_14_.refs_22_.refs_13_.refs_1_.refs_15_), channel_id=1, source_target_pairs={{0,4},{1,5},{2,6},{3,7},{4,0},{5,1},{6,2},{7,3},{8,12},{9,13},{10,... | collective-permute-start | bytes 3145736 | tf_op jit(solution)/shard_map/ppermute | solution.py:45
  8.0 36.2 %collective-permute-start = (bf16[2,128,2048]{2,1,0:T(8,128)(2,1)}, bf16[2,128,2048]{2,1,0:T(8,128)(2,1)}, u32[]{:S(2)}, u32[]{:S(2)}) collective-permute-start(bf16[2,128,2048]{2,1,0:T(8,128)(2,1)} %get-tuple-element.66.refs_14_.refs_22_.refs_13_.refs_1_.refs_15_), channel_id=1, source_target_pairs={{0,3},{1,0},{2,1},{3,2},{4,7},{5,4},{6,5},{7,6},{8,11},{9,8},{10,9... | collective-permute-start | bytes 3145736 | tf_op jit(solution)/shard_map/ppermute | solution.py:45
  9.4 34.8 %all-to-all-start = ((bf16[8,40,1792]{2,1,0:T(8,128)(2,1)}), bf16[8,40,1792]{2,1,0:T(8,128)(2,1)S(1)}, u32[]{:S(2)}, u32[]{:S(2)}) async-start(bf16[8,40,1792]{2,1,0:T(8,128)(2,1)} %get-tuple-element.65), calls=%async_computation | async-start | bytes 2293760 | tf_op jit(solution)/shard_map/all_to_all | solution.py:988
  30.3 40.3 %collective-permute-start.5 = (bf16[2,128,2048]{2,1,0:T(8,128)(2,1)}, bf16[2,128,2048]{2,1,0:T(8,128)(2,1)}, u32[]{:S(2)}, u32[]{:S(2)}) collective-permute-start(bf16[2,128,2048]{2,1,0:T(8,128)(2,1)} %collective-permute-done.1.refs_2_.refs_17_.refs_25_.refs_16_.refs_4_.refs_18_), channel_id=1, source_target_pairs={{0,1},{1,2},{2,3},{3,0},{4,5},{5,6},{6,7},{7,4},{8,9},{9,10},{10,1... | collective-permute-start | bytes 3145736 | tf_op jit(solution)/shard_map/ppermute | solution.py:45
  30.7 40.0 %collective-permute-start.7 = (bf16[2,128,2048]{2,1,0:T(8,128)(2,1)}, bf16[2,128,2048]{2,1,0:T(8,128)(2,1)S(1)}, u32[]{:S(2)}, u32[]{:S(2)}) collective-permute-start(bf16[2,128,2048]{2,1,0:T(8,128)(2,1)} %collective-permute-done.1.refs_2_.refs_17_.refs_25_.refs_16_.refs_4_.refs_18_), channel_id=1, source_target_pairs={{0,4},{1,5},{2,6},{3,7},{4,0},{5,1},{6,2},{7,3},{8,12},{9,13},{10,... | collective-permute-start | bytes 3145736 | tf_op jit(solution)/shard_map/ppermute | solution.py:45
  32.3 38.4 %collective-permute-start.6 = (bf16[2,128,2048]{2,1,0:T(8,128)(2,1)}, bf16[2,128,2048]{2,1,0:T(8,128)(2,1)}, u32[]{:S(2)}, u32[]{:S(2)}) collective-permute-start(bf16[2,128,2048]{2,1,0:T(8,128)(2,1)} %collective-permute-done.2.refs_3_.refs_18_.refs_26_.refs_17_.refs_5_.refs_19_), channel_id=1, source_target_pairs={{0,3},{1,0},{2,1},{3,2},{4,7},{5,4},{6,5},{7,6},{8,11},{9,8},{10,9... | collective-permute-start | bytes 3145736 | tf_op jit(solution)/shard_map/ppermute | solution.py:45
  47.6 20.0 %collective-permute-start.3 = (bf16[8,32,1792]{2,1,0:T(8,128)(2,1)}, bf16[8,32,1792]{2,1,0:T(8,128)(2,1)S(1)}, u32[]{:S(2)}, u32[]{:S(2)}) collective-permute-start(bf16[8,32,1792]{2,1,0:T(8,128)(2,1)} %get-tuple-element.68.refs_0_.refs_4_.refs_3_.refs_5_), channel_id=1, source_target_pairs={{0,96},{1,97},{2,98},{3,99},{4,100},{5,101},{6,102},{7,103},{8,104... | collective-permute-start | bytes 2752520 | tf_op jit(solution)/shard_map/ppermute | solution.py:45
  50.4 20.3 %collective-permute-start.4 = (bf16[8,32,1792]{2,1,0:T(8,128)(2,1)}, bf16[8,32,1792]{2,1,0:T(8,128)(2,1)S(1)}, u32[]{:S(2)}, u32[]{:S(2)}) collective-permute-start(bf16[8,32,1792]{2,1,0:T(8,128)(2,1)} %get-tuple-element.68.refs_0_.refs_4_.refs_3_.refs_5_), channel_id=1, source_target_pairs={{0,32},{1,33},{2,34},{3,35},{4,36},{5,37},{6,38},{7,39},{8,40},{9,... | collective-permute-start | bytes 2752520 | tf_op jit(solution)/shard_map/ppermute | solution.py:45
  75.8 26.0 %collective-permute-start.10 = (bf16[24,32,1792]{2,1,0:T(8,128)(2,1)}, bf16[24,32,1792]{2,1,0:T(8,128)(2,1)S(1)}, u32[]{:S(2)}, u32[]{:S(2)}) collective-permute-start(bf16[24,32,1792]{2,1,0:T(8,128)(2,1)} %bitcast.66), channel_id=1, source_target_pairs={{0,8},{1,9},{2,10},{3,11},{4,12},{5,13},{6,14},{7,15},{8,0},{9,1},... | collective-permute-start | bytes 8257544 | tf_op jit(solution)/shard_map/ppermute | solution.py:45
  83.0 14.3 %collective-permute-start.9 = (bf16[4,32,1792]{2,1,0:T(8,128)(2,1)}, bf16[4,32,1792]{2,1,0:T(8,128)(2,1)S(1)}, u32[]{:S(2)}, u32[]{:S(2)}) collective-permute-start(bf16[4,32,1792]{2,1,0:T(8,128)(2,1)} %get-tuple-element.70), channel_id=1, source_target_pairs={{0,96},{1,97},{2,98},{3,99},{4,100},{5,101},{6,102},{7,103},{8,104... | collective-permute-start | bytes 1376264 | tf_op jit(solution)/shard_map/ppermute | solution.py:45
  86.7 14.2 %collective-permute-start.13 = (bf16[128,2048]{1,0:T(8,128)(2,1)S(1)}, bf16[128,2048]{1,0:T(8,128)(2,1)S(1)}, u32[]{:S(2)}, u32[]{:S(2)}) collective-permute-start(bf16[128,2048]{1,0:T(8,128)(2,1)S(1)} %slice_bitcast_fusion.1), channel_id=1, source_target_pairs={{0,1},{1,2},{2,3},{3,0},{4,5},{5,6},{6,7},{7,4},{8,9},{9,10},{10,1... | collective-permute-start | bytes 1572872 | tf_op jit(solution)/shard_map/ppermute | solution.py:45
  135.9 21.2 %collective-permute-start.15 = (bf16[8,128,2048]{2,1,0:T(8,128)(2,1)}, bf16[8,128,2048]{2,1,0:T(8,128)(2,1)}, u32[]{:S(2)}, u32[]{:S(2)}) collective-permute-start(bf16[8,128,2048]{2,1,0:T(8,128)(2,1)} %get-tuple-element.75.refs_25_), channel_id=1, source_target_pairs={{0,8},{1,9},{2,10},{3,11},{4,12},{5,13},{6,14},{7,15},{8,0},{9,1},... | collective-permute-start | bytes 12582920 | tf_op jit(solution)/shard_map/ppermute | solution.py:45
  160.5 17.1 %collective-permute-start.17 = (bf16[1,128,2048]{2,1,0:T(8,128)(2,1)}, bf16[1,128,2048]{2,1,0:T(8,128)(2,1)S(1)}, u32[]{:S(2)}, u32[]{:S(2)}) collective-permute-start(bf16[1,128,2048]{2,1,0:T(8,128)(2,1)} %get-tuple-element.81.refs_12_), channel_id=1, source_target_pairs={{0,32},{1,33},{2,34},{3,35},{4,36},{5,37},{6,38},{7,39},{8,40},{9,... | collective-permute-start | bytes 1572872 | tf_op jit(solution)/shard_map/ppermute | solution.py:45
  160.6 17.1 %collective-permute-start.18 = (bf16[1,128,2048]{2,1,0:T(8,128)(2,1)}, bf16[1,128,2048]{2,1,0:T(8,128)(2,1)S(1)}, u32[]{:S(2)}, u32[]{:S(2)}) collective-permute-start(bf16[1,128,2048]{2,1,0:T(8,128)(2,1)} %get-tuple-element.82.refs_13_), channel_id=1, source_target_pairs={{0,96},{1,97},{2,98},{3,99},{4,100},{5,101},{6,102},{7,103},{8,104... | collective-permute-start | bytes 1572872 | tf_op jit(solution)/shard_map/ppermute | solution.py:45
  184.0 40.3 %collective-permute-start.21 = (bf16[2,128,2048]{2,1,0:T(8,128)(2,1)}, bf16[2,128,2048]{2,1,0:T(8,128)(2,1)S(1)}, u32[]{:S(2)}, u32[]{:S(2)}) collective-permute-start(bf16[2,128,2048]{2,1,0:T(8,128)(2,1)} %get-tuple-element.85.refs_5_.refs_30_), channel_id=1, source_target_pairs={{0,32},{1,33},{2,34},{3,35},{4,36},{5,37},{6,38},{7,39},{8,40},{9,... | collective-permute-start | bytes 3145736 | tf_op jit(solution)/shard_map/ppermute | solution.py:45
  184.0 40.3 %collective-permute-start.22 = (bf16[2,128,2048]{2,1,0:T(8,128)(2,1)}, bf16[2,128,2048]{2,1,0:T(8,128)(2,1)}, u32[]{:S(2)}, u32[]{:S(2)}) collective-permute-start(bf16[2,128,2048]{2,1,0:T(8,128)(2,1)} %get-tuple-element.86.refs_31_), channel_id=1, source_target_pairs={{0,96},{1,97},{2,98},{3,99},{4,100},{5,101},{6,102},{7,103},{8,104... | collective-permute-start | bytes 3145736 | tf_op jit(solution)/shard_map/ppermute | solution.py:45
  192.6 54.1 %all-to-all-start.1 = ((bf16[8,64,2048]{2,1,0:T(8,128)(2,1)}), bf16[8,64,2048]{2,1,0:T(8,128)(2,1)S(1)}, u32[]{:S(2)}, u32[]{:S(2)}) async-start(bf16[8,64,2048]{2,1,0:T(8,128)(2,1)} %both_sums.1.refs_29_), calls=%async_computation.1 | async-start | bytes 4194304 | tf_op jit(solution)/shard_map/all_to_all | solution.py:1116
  221.4 33.8 %collective-permute-start.19 = (bf16[2,128,2048]{2,1,0:T(8,128)(2,1)}, bf16[2,128,2048]{2,1,0:T(8,128)(2,1)}, u32[]{:S(2)}, u32[]{:S(2)}) collective-permute-start(bf16[2,128,2048]{2,1,0:T(8,128)(2,1)} %get-tuple-element.89), channel_id=1, source_target_pairs={{0,1},{1,2},{2,3},{3,0},{4,5},{5,6},{6,7},{7,4},{8,9},{9,10},{10,1... | collective-permute-start | bytes 3145736 | tf_op jit(solution)/shard_map/ppermute | solution.py:45
  221.8 33.4 %collective-permute-start.20 = (bf16[2,128,2048]{2,1,0:T(8,128)(2,1)}, bf16[2,128,2048]{2,1,0:T(8,128)(2,1)}, u32[]{:S(2)}, u32[]{:S(2)}) collective-permute-start(bf16[2,128,2048]{2,1,0:T(8,128)(2,1)} %get-tuple-element.92), channel_id=1, source_target_pairs={{0,3},{1,0},{2,1},{3,2},{4,7},{5,4},{6,5},{7,6},{8,11},{9,8},{10,9... | collective-permute-start | bytes 3145736 | tf_op jit(solution)/shard_map/ppermute | solution.py:45
  229.6 17.1 %collective-permute-start.23 = (bf16[1,128,2048]{2,1,0:T(8,128)(2,1)}, bf16[1,128,2048]{2,1,0:T(8,128)(2,1)S(1)}, u32[]{:S(2)}, u32[]{:S(2)}) collective-permute-start(bf16[1,128,2048]{2,1,0:T(8,128)(2,1)} %get-tuple-element.96), channel_id=1, source_target_pairs={{0,16},{1,17},{2,18},{3,19},{4,20},{5,21},{6,22},{7,23},{8,24},{9,... | collective-permute-start | bytes 1572872 | tf_op jit(solution)/shard_map/ppermute | solution.py:45
  251.7 14.9 %all-to-all-start.2 = ((bf16[8,16,2048]{2,1,0:T(8,128)(2,1)}), bf16[8,16,2048]{2,1,0:T(8,128)(2,1)S(1)}, u32[]{:S(2)}, u32[]{:S(2)}) async-start(bf16[8,16,2048]{2,1,0:T(8,128)(2,1)} %get-tuple-element.100.refs_7_), calls=%async_computation.2 | async-start | bytes 1048576 | tf_op jit(solution)/shard_map/all_to_all | solution.py:1178
  261.2 46.5 %collective-permute-start.24 = (bf16[4,128,2048]{2,1,0:T(8,128)(2,1)}, bf16[4,128,2048]{2,1,0:T(8,128)(2,1)}, u32[]{:S(2)}, u32[]{:S(2)}) collective-permute-start(bf16[4,128,2048]{2,1,0:T(8,128)(2,1)} %get-tuple-element.101.refs_1_), channel_id=1, source_target_pairs={{0,1},{1,2},{2,3},{3,0},{4,5},{5,6},{6,7},{7,4},{8,9},{9,10},{10,1... | collective-permute-start | bytes 6291464 | tf_op jit(solution)/shard_map/ppermute | solution.py:45
  262.5 45.1 %collective-permute-start.25 = (bf16[4,128,2048]{2,1,0:T(8,128)(2,1)}, bf16[4,128,2048]{2,1,0:T(8,128)(2,1)}, u32[]{:S(2)}, u32[]{:S(2)}) collective-permute-start(bf16[4,128,2048]{2,1,0:T(8,128)(2,1)} %get-tuple-element.102), channel_id=1, source_target_pairs={{0,3},{1,0},{2,1},{3,2},{4,7},{5,4},{6,5},{7,6},{8,11},{9,8},{10,9... | collective-permute-start | bytes 6291464 | tf_op jit(solution)/shard_map/ppermute | solution.py:45
  264.7 16.9 %collective-permute-start.30 = (bf16[2,80,2048]{2,1,0:T(8,128)(2,1)S(1)}, bf16[2,80,2048]{2,1,0:T(8,128)(2,1)S(1)}, u32[]{:S(2)}, u32[]{:S(2)}) collective-permute-start(bf16[2,80,2048]{2,1,0:T(8,128)(2,1)S(1)} %pad_maximum_fusion.refs_2_.refs_0_), channel_id=1, source_target_pairs={{0,96},{1,97},{2,98},{3,99},{4,100},{5,101},{6,102},{7,103},{8,104... | collective-permute-start | bytes 1966088 | tf_op jit(solution)/shard_map/ppermute | solution.py:45
  285.4 27.1 %collective-permute-start.31 = (bf16[2,128,2048]{2,1,0:T(8,128)(2,1)}, bf16[2,128,2048]{2,1,0:T(8,128)(2,1)S(1)}, u32[]{:S(2)}, u32[]{:S(2)}) collective-permute-start(bf16[2,128,2048]{2,1,0:T(8,128)(2,1)} %joined.3.refs_0_), channel_id=1, source_target_pairs={{0,32},{1,33},{2,34},{3,35},{4,36},{5,37},{6,38},{7,39},{8,40},{9,... | collective-permute-start | bytes 3145736 | tf_op jit(solution)/shard_map/ppermute | solution.py:45
  285.4 27.1 %collective-permute-start.32 = (bf16[2,128,2048]{2,1,0:T(8,128)(2,1)}, bf16[2,128,2048]{2,1,0:T(8,128)(2,1)S(1)}, u32[]{:S(2)}, u32[]{:S(2)}) collective-permute-start(bf16[2,128,2048]{2,1,0:T(8,128)(2,1)} %joined.3.refs_0_), channel_id=1, source_target_pairs={{0,96},{1,97},{2,98},{3,99},{4,100},{5,101},{6,102},{7,103},{8,104... | collective-permute-start | bytes 3145736 | tf_op jit(solution)/shard_map/ppermute | solution.py:45
  294.7 36.2 %collective-permute-start.37 = (bf16[8,80,2048]{2,1,0:T(8,128)(2,1)}, bf16[8,80,2048]{2,1,0:T(8,128)(2,1)}, u32[]{:S(2)}, u32[]{:S(2)}) collective-permute-start(bf16[8,80,2048]{2,1,0:T(8,128)(2,1)} %joined.4.refs_3_.refs_2_), channel_id=1, source_target_pairs={{0,8},{1,9},{2,10},{3,11},{4,12},{5,13},{6,14},{7,15},{8,0},{9,1},... | collective-permute-start | bytes 7864328 | tf_op jit(solution)/shard_map/ppermute | solution.py:45
  318.0 21.6 %collective-permute-start.36 = (bf16[6,128,2048]{2,1,0:T(8,128)(2,1)}, bf16[6,128,2048]{2,1,0:T(8,128)(2,1)S(1)}, u32[]{:S(2)}, u32[]{:S(2)}) collective-permute-start(bf16[6,128,2048]{2,1,0:T(8,128)(2,1)} %bitcast.45), channel_id=1, source_target_pairs={{0,8},{1,9},{2,10},{3,11},{4,12},{5,13},{6,14},{7,15},{8,0},{9,1},... | collective-permute-start | bytes 9437192 | tf_op jit(solution)/shard_map/ppermute | solution.py:45
  326.1 29.3 %collective-permute-start.26 = (bf16[2,128,2048]{2,1,0:T(8,128)(2,1)}, bf16[2,128,2048]{2,1,0:T(8,128)(2,1)S(1)}, u32[]{:S(2)}, u32[]{:S(2)}) collective-permute-start(bf16[2,128,2048]{2,1,0:T(8,128)(2,1)} %other_sums.1.refs_4_.refs_5_), channel_id=1, source_target_pairs={{0,4},{1,5},{2,6},{3,7},{4,0},{5,1},{6,2},{7,3},{8,12},{9,13},{10,... | collective-permute-start | bytes 3145736 | tf_op jit(solution)/shard_map/ppermute | solution.py:45
  328.3 21.5 %collective-permute-start.34 = (bf16[1,128,2048]{2,1,0:T(8,128)(2,1)}, bf16[1,128,2048]{2,1,0:T(8,128)(2,1)S(1)}, u32[]{:S(2)}, u32[]{:S(2)}) collective-permute-start(bf16[1,128,2048]{2,1,0:T(8,128)(2,1)} %get-tuple-element.105), channel_id=1, source_target_pairs={{0,32},{1,33},{2,34},{3,35},{4,36},{5,37},{6,38},{7,39},{8,40},{9,... | collective-permute-start | bytes 1572872 | tf_op jit(solution)/shard_map/ppermute | solution.py:45
  328.3 21.5 %collective-permute-start.35 = (bf16[1,128,2048]{2,1,0:T(8,128)(2,1)}, bf16[1,128,2048]{2,1,0:T(8,128)(2,1)S(1)}, u32[]{:S(2)}, u32[]{:S(2)}) collective-permute-start(bf16[1,128,2048]{2,1,0:T(8,128)(2,1)} %get-tuple-element.106), channel_id=1, source_target_pairs={{0,96},{1,97},{2,98},{3,99},{4,100},{5,101},{6,102},{7,103},{8,104... | collective-permute-start | bytes 1572872 | tf_op jit(solution)/shard_map/ppermute | solution.py:45
  (47 other events, 343.6 us)

commit v14 on v13

--- a/solution.py
+++ b/solution.py
@@ -776,6 +776,63 @@
     )(received, *after)
 
 
+def spread(pieces, places, numbers, targets, count, before, after, time=2):
+    rows, cols = pieces[0][0].shape[1:]
+    firsts, total = [], 0
+    for mine, _ in pieces:
+        firsts.append(total)
+        total += mine.shape[0] // 2
+
+    def body(place_ref, number_ref, *refs):
+        step = pl.program_id(0)
+        outs = refs[2 * len(pieces) + len(before) :]
+        core, z_hi = number_ref[0], number_ref[3]
+        for n, (first, (mine, _)) in enumerate(zip(firsts, pieces)):
+
+            @pl.when((step >= first) & (step < first + mine.shape[0] // 2))
+            def _(n=n):
+                for other_core in range(2):
+                    ref = refs[2 * n + other_core]
+                    low = 1 - core if other_core else core
+                    for other_z in range(2):
+                        at = (1 - z_hi if other_z else z_hi) * 2 + low
+                        for out_ref, (_, high, parts) in zip(outs, targets):
+                            to_rows = pl.ds(pl.multiple_of(at * high, high), high)
+                            for to, row, col, size in parts:
+                                out_ref[to_rows, to : to + size] = ref[
+                                    other_z, row : row + high, col : col + size
+                                ].astype(f32)
+
+    def chosen(first, size):
+        return pl.BlockSpec(
+            (2, rows, cols), lambda i, place, n: (jnp.clip(i - first, 0, size - 1), 0, 0)
+        )
+
+    specs, arrays = [], []
+    for first, (mine, yours) in zip(firsts, pieces):
+        specs += [chosen(first, mine.shape[0] // 2)] * 2
+        arrays += [mine, yours]
+    return pl.pallas_call(
+        after_inputs(body, 2 + 2 * len(pieces) + len(before), len(after)),
+        out_shape=tuple(
+            jax.ShapeDtypeStruct((4 * count * high, wide), f32) for wide, high, _ in targets
+        ),
+        grid_spec=pltpu.PrefetchScalarGridSpec(
+            num_scalar_prefetch=2,
+            grid=(total,),
+            in_specs=specs + anywhere(len(before) + len(after)),
+            out_specs=tuple(
+                pl.BlockSpec((4 * high, wide), lambda i, place, n: (place[i], 0))
+                for wide, high, _ in targets
+            ),
+        ),
+        input_output_aliases={2 + len(arrays) + n: n for n in range(len(before))},
+        compiler_params=kernel_params(),
+        cost_estimate=cost(time),
+        name="spread",
+    )(places, numbers, *arrays, *before, *after)
+
+
 def packed_sums(stays, crossed, parts, norm_sums, qkv_sums, up_sums, dy_sums, numbers, ff, head, after):
     width = parts.shape[2]
 
@@ -887,68 +944,6 @@
     return functools.reduce(jnp.add, [ref[...].astype(f32) for ref in refs])
 
 
-def spread(pieces, places, core, targets, count, before, after, time=2):
-    rows, cols = pieces[0][0].shape[1:]
-    firsts, total = [], 0
-    for mine, _ in pieces:
-        firsts.append(total)
-        total += mine.shape[0]
-
-    def body(place_ref, core_ref, *refs):
-        step = pl.program_id(0)
-        outs = refs[2 * len(pieces) + len(before) :]
-        first_core = core_ref[0] == 0
-
-        def fill(ref, low):
-            for out_ref, (_, high, parts) in zip(outs, targets):
-                for to, row, col, size in parts:
-                    out_ref[low * high : (low + 1) * high, to : to + size] = ref[
-                        0, row : row + high, col : col + size
-                    ].astype(f32)
-
-        for n, (first, (mine, _)) in enumerate(zip(firsts, pieces)):
-            here = (step >= first) & (step < first + mine.shape[0])
-
-            @pl.when(here & first_core)
-            def _(n=n):
-                fill(refs[2 * n], 0)
-                fill(refs[2 * n + 1], 1)
-
-            @pl.when(here & jnp.logical_not(first_core))
-            def _(n=n):
-                fill(refs[2 * n], 1)
-                fill(refs[2 * n + 1], 0)
-
-    def chosen(first, size):
-        return pl.BlockSpec(
-            (1, rows, cols), lambda i, place, core: (jnp.clip(i - first, 0, size - 1), 0, 0)
-        )
-
-    specs, arrays = [], []
-    for first, (mine, yours) in zip(firsts, pieces):
-        specs += [chosen(first, mine.shape[0])] * 2
-        arrays += [mine, yours]
-    return pl.pallas_call(
-        after_inputs(body, 2 + 2 * len(pieces) + len(before), len(after)),
-        out_shape=tuple(
-            jax.ShapeDtypeStruct((2 * count * high, wide), f32) for wide, high, _ in targets
-        ),
-        grid_spec=pltpu.PrefetchScalarGridSpec(
-            num_scalar_prefetch=2,
-            grid=(total,),
-            in_specs=specs + anywhere(len(before) + len(after)),
-            out_specs=tuple(
-                pl.BlockSpec((2 * high, wide), lambda i, place, core: (place[i], 0))
-                for wide, high, _ in targets
-            ),
-        ),
-        input_output_aliases={2 + len(arrays) + n: n for n in range(len(before))},
-        compiler_params=kernel_params(),
-        cost_estimate=cost(time),
-        name="spread",
-    )(places, core, *arrays, *before, *after)
-
-
 def local(
     tokens,
     doc_lengths,
@@ -1214,15 +1209,14 @@
     )
     total_other = move(sent_other, l=1)
 
-    order = ((0, h), (0, 1 - h), (1, h), (1, 1 - h), (3, h), (3, 1 - h), (2, h), (2, 1 - h))
-    places = jnp.stack([(y + k) % 4 * 2 + high for k, high in order]).astype(jnp.int32)
+    places = jnp.stack([(y + k) % 4 for k in (0, 1, 3, 2)]).astype(jnp.int32)
 
     down_grad, out_grad = spread(
         [(stays, move(stays, c=1))],
         places,
-        numbers[:1],
+        numbers,
         [(width, 64, [(0, 0, 0, width)]), (width, 16, [(0, 64, 0, width)])],
-        8,
+        4,
         (),
         (),
         14,
@@ -1245,7 +1239,7 @@
     ]
     near_yours = move(near, c=1)
     grads = spread(
-        [(near, near_yours)], places[:6], numbers[:1], targets, 8, (), (down_grad, sent_other)
+        [(near, near_yours)], places[:3], numbers, targets, 4, (), (down_grad, sent_other)
     )
     far = joined(far, (grads[0],))
     mixed, tokens_grad = finished(
@@ -1254,10 +1248,10 @@
     far_yours = move(far, c=1)
     qkv_grad, up_grad = spread(
         [(far, far_yours)],
-        places[6:],
-        numbers[:1],
+        places[3:],
+        numbers,
         targets,
-        8,
+        4,
         grads,
         (tokens_grad,),
     )

time: 369 us -> 366 us (level)
  transfers between devices with their start and end apart: 42 -> 42, of which waited for: 13 -> 13; matrix products, arithmetic and copies ran while one was open for 5% -> 4% of each run, Pallas kernels for 32% -> 32%
where the time goes in v14:
time: 366 us; the launch traced here: 365 us
  Pallas kernels  164 us (45%)
  starting transfers between devices  83.5 us (23%)
  waiting for transfers between devices  78.6 us (21%)
  local copies, waits for them, and re-layouts  29.7 us (8%)
  other arithmetic  7.91 us (2%)
    ppermute x39, starting transfers between devices, move(): return lax.ppermute(value, BOTH, pairs)  71.8 us
    ppermute x39, waiting for transfers between devices, move(): return lax.ppermute(value, BOTH, pairs)  69.4 us
    pallas_call x1, Pallas kernels, feed_forward(): pl.pallas_call(after_inputs(body, 5 + parts + 2 * count, len(after)), out...  32.2 us
    pallas_call x6, Pallas kernels, blocks_call(): pl.pallas_call(after_inputs(body, 1 + len(terms), len(after)), out_shape=...  26.8 us
    pallas_call x1, Pallas kernels, outer(): pl.pallas_call(after_inputs(body, 11 + parts + count, len(after)), out_sh...  24.2 us
    unnamed x81, local copies, waits for them, and re-layouts  20.9 us
    pallas_call x3, Pallas kernels, spread(): pl.pallas_call(after_inputs(body, 2 + 2 * len(pieces) + len(before), len(...  19.7 us
    pallas_call x1, Pallas kernels, attend(): pl.pallas_call(after_inputs(body, 7 + parts + count, len(after)), out_sha...  17.1 us
  transfers between devices with their start and end apart: 42, of which 13 were waited for; matrix products, arithmetic and copies ran while one was open for 4% of the time, Pallas kernels for 32%

profile of v14, /device:TPU:1, one launch (start us, length us, event | category | flops | bytes accessed | tf_op | source)
XLA Modules:
  0.0 364.9 jit_solution(4586500026684204627)
XLA Ops:
  0.7 3.6 packed.1
  9.4 3.6 all-to-all-start
  13.0 17.3 %collective-permute-done.1.refs_2_.refs_17_.refs_25_.refs_16_.refs_4_.refs_18_ = bf16[2,128,2048]{2,1,0:T(8,128)(2,1)} collective-permute-done((bf16[2,128,2048]{2,1,0:T(8,128)(2,1)}, bf16[2,128,2048]{2,1,0:T(8,128)(2,1)}, u32[]{:S(2)}, u32[]{:S(2)}) %collective-permute-start.1) | collective-permute-done | bytes 1048608 | tf_op jit(solution)/shard_map/ppermute | solution.py:45
  35.0 9.2 %all-to-all-done.refs_0_ = bf16[8,40,1792]{2,1,0:T(8,128)(2,1)S(1)} async-done(((bf16[8,40,1792]{2,1,0:T(8,128)(2,1)}), bf16[8,40,1792]{2,1,0:T(8,128)(2,1)S(1)}, u32[]{:S(2)}, u32[]{:S(2)}) %all-to-all-start) | async-done | bytes 1146912 | tf_op jit(solution)/shard_map/all_to_all | solution.py:983
  51.7 16.0 %collective-permute-done.3.refs_2_.refs_5_.refs_4_.refs_6_ = bf16[8,32,1792]{2,1,0:T(8,128)(2,1)S(1)} collective-permute-done((bf16[8,32,1792]{2,1,0:T(8,128)(2,1)}, bf16[8,32,1792]{2,1,0:T(8,128)(2,1)S(1)}, u32[]{:S(2)}, u32[]{:S(2)}) %collective-permute-start.3) | collective-permute-done | bytes 917536 | tf_op jit(solution)/shard_map/ppermute | solution.py:45
  72.6 3.3 halves.2
  75.8 3.9 %collective-permute-start.10 = (bf16[24,32,1792]{2,1,0:T(8,128)(2,1)}, bf16[24,32,1792]{2,1,0:T(8,128)(2,1)S(1)}, u32[]{:S(2)}, u32[]{:S(2)}) collective-permute-start(bf16[24,32,1792]{2,1,0:T(8,128)(2,1)} %bitcast.62), channel_id=1, source_target_pairs={{0,8},{1,9},{2,10},{3,11},{4,12},{5,13},{6,14},{7,15},{8,0},{9,1},... | collective-permute-start | bytes 8257544 | tf_op jit(solution)/shard_map/ppermute | solution.py:45
  91.3 5.2 %collective-permute-done.8.refs_6_.refs_5_.refs_7_ = bf16[4,32,1792]{2,1,0:T(8,128)(2,1)S(1)} collective-permute-done((bf16[4,32,1792]{2,1,0:T(8,128)(2,1)}, bf16[4,32,1792]{2,1,0:T(8,128)(2,1)S(1)}, u32[]{:S(2)}, u32[]{:S(2)}) %collective-permute-start.8) | collective-permute-done | bytes 458784 | tf_op jit(solution)/shard_map/ppermute | solution.py:45
  103.7 32.2 %feed_forward.1 = (bf16[1024,2048]{1,0:T(8,128)(2,1)}, bf16[1024,1024]{1,0:T(8,128)(2,1)}, bf16[1024,1024]{1,0:T(8,128)(2,1)}, bf16[8,128,2048]{2,1,0:T(8,128)(2...) custom-call(s32[4]{0:T(128)} %get-tuple-element.128.refs_0_.refs_7_., ...), custom_call_target="tpu_custom_call" | custom-call | flops 36800000000 | bytes 1000 | tf_op jit(solution)/shard_map/feed_forward/pallas_call | solution.py:258
  140.0 17.1 %attend.1 = (bf16[1024,256]{1,0:T(8,128)(2,1)}, bf16[1024,768]{1,0:T(8,128)(2,1)}, f32[1,768]{1,0:T(1,128)}) custom-call(s32[8,3]{1,0:T(8,128)} %copy-done.8, s32[8]{0:T(128)} %pad_add_fusion.refs_1_.refs_0_, f32[3,1,256]{2,1,0:T(1,128)} %pad_maximum_fusion.2.refs_2_, bf16[8,32,1792]{2,1,0:T(8,128)(2,1)} %get-tuple-element.68.refs_0_.refs_4_.refs_3_.refs_5_, ...), custom_call_target="tpu_custom_call" | custom-call | flops 19549999104 | bytes 1000 | tf_op jit(solution)/shard_map/attend/pallas_call | solution.py:431
  157.2 3.4 far_sums.1
  163.2 13.6 %attention_grads.1 = (bf16[8,64,2048]{2,1,0:T(8,128)(2,1)}, bf16[8,64,2048]{2,1,0:T(8,128)(2,1)}) custom-call(s32[4]{0:T(128)} %get-tuple-element.128.refs_0_.refs_7_.refs_1_, bf16[2,128,2048]{2,1,0:T(8,128)(2,1)} %get-tuple-element.66.refs_14_.refs_22_.refs_13_.refs_1_.refs_15_, ...), custom_call_target="tpu_custom_call" | custom-call | flops 13799999488 | bytes 1000 | tf_op jit(solution)/shard_map/attention_grads/pallas_call | solution.py:527
  179.2 4.8 %near_sums.1 = (bf16[2,128,2048]{2,1,0:T(8,128)(2,1)}, bf16[2,128,2048]{2,1,0:T(8,128)(2,1)}) custom-call(s32[4]{0:T(128)} %get-tuple-element.128.refs_0_.refs_7_.refs_1_, bf16[8,128,2048]{2,1,0:T(8,128)(2,1)} %get-tuple-element.80.refs_1_.refs_3_, bf16[8,128,2048]{2,1,0:T(8,128)(2,1)} %collective-permute-done.15.refs_2_.refs_4_, ...), custom_call_target="tpu_custom_call" | custom-call | flops 23000000512 | bytes 1000 | tf_op jit(solution)/shard_map/near_sums/pallas_call | solution.py:926
  188.0 4.6 %both_sums.1.refs_29_ = bf16[8,64,2048]{2,1,0:T(8,128)(2,1)} custom-call(s32[4]{0:T(128)} %get-tuple-element.128.refs_0_.refs_7_.refs_1_, bf16[8,64,2048]{2,1,0:T(8,128)(2,1)} %get-tuple-element.83.refs_1_.refs_3_, bf16[8,64,2048]{2,1,0:T(8,128)(2,1)} %copy-done.15, bf16[8,64,2048]{2,1,0:T(8,128)(2,1)} %get-tuple-element.83.refs_1_.refs_3_, ...), custom_call_target="tpu_custom_call" | custom-call | flops 3449999872 | bytes 1000 | tf_op jit(solution)/shard_map/both_sums/pallas_call | solution.py:926
  192.6 4.6 %all-to-all-start.1 = ((bf16[8,64,2048]{2,1,0:T(8,128)(2,1)}), bf16[8,64,2048]{2,1,0:T(8,128)(2,1)S(1)}, u32[]{:S(2)}, u32[]{:S(2)}) async-start(bf16[8,64,2048]{2,1,0:T(8,128)(2,1)} %both_sums.1.refs_29_), calls=%async_computation.1 | async-start | bytes 4194304 | tf_op jit(solution)/shard_map/all_to_all | solution.py:1111
  197.2 24.2 %outer.1 = (f32[4,2048]{1,0:T(4,128)}, bf16[2,128,2048]{2,1,0:T(8,128)(2,1)}, bf16[2,128,2048]{2,1,0:T(8,128)(2,1)}, bf16[2,128,2048]{2,1,0:T(8,128)(2,1)}, bf16...) custom-call(s32[8]{0:T(128)} %pad_add_fusion.refs_1_.refs_0_, ...), custom_call_target="tpu_custom_call" | custom-call | flops 23000000512 | bytes 1000 | tf_op jit(solution)/shard_map/outer/pallas_call | solution.py:622
  225.3 4.3 %end_sums.1 = (bf16[1,128,2048]{2,1,0:T(8,128)(2,1)}, bf16[1,128,2048]{2,1,0:T(8,128)(2,1)}) custom-call(s32[4]{0:T(128)} %get-tuple-element.128.refs_0_.refs_7_.refs_1_, bf16[8,128,2048]{2,1,0:T(8,128)(2,1)} %get-tuple-element.80.refs_1_.refs_3_, bf16[8,128,2048]{2,1,0:T(8,128)(2,1)} %collective-permute-done.15.refs_2_.refs_4_, ...), custom_call_target="tpu_custom_call" | custom-call | flops 3449999872 | bytes 1000 | tf_op jit(solution)/shard_map/end_sums/pallas_call | solution.py:926
  232.6 14.1 %collective-permute-done.23.refs_1_ = bf16[1,128,2048]{2,1,0:T(8,128)(2,1)S(1)} collective-permute-done((bf16[1,128,2048]{2,1,0:T(8,128)(2,1)}, bf16[1,128,2048]{2,1,0:T(8,128)(2,1)S(1)}, u32[]{:S(2)}, u32[]{:S(2)}) %collective-permute-start.23) | collective-permute-done | bytes 524320 | tf_op jit(solution)/shard_map/ppermute | solution.py:45
  248.2 3.5 packed_sums.1
  251.7 3.5 all-to-all-start.2
  255.3 5.9 %passed_sums.1 = (bf16[4,128,2048]{2,1,0:T(8,128)(2,1)}, bf16[4,128,2048]{2,1,0:T(8,128)(2,1)}) custom-call(s32[4]{0:T(128)} %get-tuple-element.128.refs_0_.refs_7_.refs_1_, bf16[2,128,2048]{2,1,0:T(8,128)(2,1)} %get-tuple-element.88.refs_1_, bf16[2,128,2048]{2,1,0:T(8,128)(2,1)} %collective-permute-done.19.refs_2_, ...), custom_call_target="tpu_custom_call" | custom-call | flops 3449999872 | bytes 1000 | tf_op jit(solution)/shard_map/passed_sums/pallas_call | solution.py:926
  272.3 4.6 %collective-permute-done.29.refs_2_ = bf16[2,80,2048]{2,1,0:T(8,128)(2,1)S(1)} collective-permute-done((bf16[2,80,2048]{2,1,0:T(8,128)(2,1)S(1)}, bf16[2,80,2048]{2,1,0:T(8,128)(2,1)S(1)}, u32[]{:S(2)}, u32[]{:S(2)}) %collective-permute-start.29) | collective-permute-done | bytes 655392 | tf_op jit(solution)/shard_map/ppermute | solution.py:45
  277.4 4.1 %collective-permute-done.28.refs_1_ = bf16[1,128,2048]{2,1,0:T(8,128)(2,1)S(1)} collective-permute-done((bf16[1,128,2048]{2,1,0:T(8,128)(2,1)}, bf16[1,128,2048]{2,1,0:T(8,128)(2,1)S(1)}, u32[]{:S(2)}, u32[]{:S(2)}) %collective-permute-start.28) | collective-permute-done | bytes 524320 | tf_op jit(solution)/shard_map/ppermute | solution.py:45
  291.0 3.7 %joined.4.refs_3_.refs_2_ = bf16[8,80,2048]{2,1,0:T(8,128)(2,1)} custom-call(bf16[2,80,2048]{2,1,0:T(8,128)(2,1)} %copy-done.4, bf16[2,80,2048]{2,1,0:T(8,128)(2,1)} %copy-done.23, bf16[2,80,2048]{2,1,0:T(8,128)(2,1)} %copy-done.22, bf16[2,80,2048]{2,1,0:T(8,128)(2,1)} %copy-done.24), custom_call_target="tpu_custom_call" | custom-call | flops 3449999872 | bytes 1000 | tf_op jit(solution)/shard_map/joined/pallas_call | solution.py:706
  294.7 12.1 %collective-permute-start.37 = (bf16[8,80,2048]{2,1,0:T(8,128)(2,1)}, bf16[8,80,2048]{2,1,0:T(8,128)(2,1)}, u32[]{:S(2)}, u32[]{:S(2)}) collective-permute-start(bf16[8,80,2048]{2,1,0:T(8,128)(2,1)} %joined.4.refs_3_.refs_2_), channel_id=1, source_target_pairs={{0,8},{1,9},{2,10},{3,11},{4,12},{5,13},{6,14},{7,15},{8,0},{9,1},... | collective-permute-start | bytes 7864328 | tf_op jit(solution)/shard_map/ppermute | solution.py:45
  307.6 3.9 %other_sums.1.refs_4_.refs_5_ = bf16[2,128,2048]{2,1,0:T(8,128)(2,1)} custom-call(s32[4]{0:T(128)} %get-tuple-element.128.refs_0_.refs_7_.refs_1_, bf16[2,128,2048]{2,1,0:T(8,128)(2,1)} %get-tuple-element.103.refs_1_, bf16[4,128,2048]{2,1,0:T(8,128)(2,1)} %collective-permute-done.24.refs_2_.refs_1_, bf16[4,128,2048]{2,1,0:T(8,128)(2,1)} %collective-permute-done.25.refs_3_.refs_2_), custom_call_target="tpu_custom_call" | custom-call | flops 3449999872 | bytes 1000 | tf_op jit(solution)/shard_map/other_sums/pallas_call | solution.py:926
  314.5 3.5 halves.3
  318.0 6.3 %collective-permute-start.36 = (bf16[6,128,2048]{2,1,0:T(8,128)(2,1)}, bf16[6,128,2048]{2,1,0:T(8,128)(2,1)S(1)}, u32[]{:S(2)}, u32[]{:S(2)}) collective-permute-start(bf16[6,128,2048]{2,1,0:T(8,128)(2,1)} %bitcast.41), channel_id=1, source_target_pairs={{0,8},{1,9},{2,10},{3,11},{4,12},{5,13},{6,14},{7,15},{8,0},{9,1},... | collective-permute-start | bytes 9437192 | tf_op jit(solution)/shard_map/ppermute | solution.py:45
  330.3 7.6 %spread.3 = (f32[1024,2048]{1,0:T(8,128)}, f32[256,2048]{1,0:T(8,128)}) custom-call(s32[4]{0:T(128)} %pad_add_fusion.3.refs_0_, s32[4]{0:T(128)} %get-tuple-element.128.refs_0_.refs_7_.refs_1_, bf16[8,80,2048]{2,1,0:T(8,128)(2,1)} %joined.4.refs_3_.refs_2_, bf16[8,80,2048]{2,1,0:T(8,128)(2,1)} %collective-permute-done.37.refs_3_), custom_call_target="tpu_custom_call" | custom-call | flops 16099999744 | bytes 1000 | tf_op jit(solution)/shard_map/spread/pallas_call | solution.py:815
  339.6 7.8 %spread.4 = (f32[256,6144]{1,0:T(8,128)}, f32[256,8192]{1,0:T(8,128)}) custom-call(s32[3]{0:T(128)} %pad_add_fusion.2.refs_0_, s32[4]{0:T(128)} %get-tuple-element.128.refs_0_.refs_7_.refs_1_, bf16[6,128,2048]{2,1,0:T(8,128)(2,1)} %bitcast.43, bf16[6,128,2048]{2,1,0:T(8,128)(2,1)} %copy-done, f32[1024,2048]{1,0:T(8,128)} %get-tuple-element.158.refs_4_, ...), custom_call_target="tpu_custom_call" | custom-call | flops 2300000000 | bytes 1000 | tf_op jit(solution)/shard_map/spread/pallas_call | solution.py:815
  354.0 4.1 %finished.1 = (bf16[128,2048]{1,0:T(8,128)(2,1)}, f32[128,2048]{1,0:T(8,128)}) custom-call(bf16[2,128,2048]{2,1,0:T(8,128)(2,1)} %get-tuple-element.87.refs_0_, bf16[4,128,2048]{2,1,0:T(8,128)(2,1)} %collective-permute-done.24.refs_2_.refs_1_, bf16[4,128,2048]{2,1,0:T(8,128)(2,1)} %collective-permute-done.25.refs_3_.refs_2_, ...), custom_call_target="tpu_custom_call" | custom-call | flops 16099999744 | bytes 1000 | tf_op jit(solution)/shard_map/finished/pallas_call | solution.py:906
  360.1 4.2 %spread.5 = (f32[256,6144]{1,0:T(8,128)}, f32[256,8192]{1,0:T(8,128)}) custom-call(s32[1]{0:T(128)} %bitcast.19.refs_0_, s32[4]{0:T(128)} %get-tuple-element.128.refs_0_.refs_7_.refs_1_, bf16[2,128,2048]{2,1,0:T(8,128)(2,1)} %joined.5.refs_6_.refs_2_, bf16[2,128,2048]{2,1,0:T(8,128)(2,1)} %copy-done.3, ...), custom_call_target="tpu_custom_call", output_to_operand_aliasing={{0}: (4, {}), {1}: (5, {})} | custom-call | flops 2300000000 | bytes 1000 | tf_op jit(solution)/shard_map/spread/pallas_call | solution.py:815
  (198 shorter events, 103.9 us)
Async XLA Ops:
  4.3 26.1 %collective-permute-start.1 = (bf16[2,128,2048]{2,1,0:T(8,128)(2,1)}, bf16[2,128,2048]{2,1,0:T(8,128)(2,1)}, u32[]{:S(2)}, u32[]{:S(2)}) collective-permute-start(bf16[2,128,2048]{2,1,0:T(8,128)(2,1)} %get-tuple-element.66.refs_14_.refs_22_.refs_13_.refs_1_.refs_15_), channel_id=1, source_target_pairs={{0,1},{1,2},{2,3},{3,0},{4,5},{5,6},{6,7},{7,4},{8,9},{9,10},{10,1... | collective-permute-start | bytes 3145736 | tf_op jit(solution)/shard_map/ppermute | solution.py:45
  6.3 26.0 %collective-permute-start.2 = (bf16[2,128,2048]{2,1,0:T(8,128)(2,1)}, bf16[2,128,2048]{2,1,0:T(8,128)(2,1)}, u32[]{:S(2)}, u32[]{:S(2)}) collective-permute-start(bf16[2,128,2048]{2,1,0:T(8,128)(2,1)} %get-tuple-element.66.refs_14_.refs_22_.refs_13_.refs_1_.refs_15_), channel_id=1, source_target_pairs={{0,4},{1,5},{2,6},{3,7},{4,0},{5,1},{6,2},{7,3},{8,12},{9,13},{10,... | collective-permute-start | bytes 3145736 | tf_op jit(solution)/shard_map/ppermute | solution.py:45
  8.0 36.2 %collective-permute-start = (bf16[2,128,2048]{2,1,0:T(8,128)(2,1)}, bf16[2,128,2048]{2,1,0:T(8,128)(2,1)}, u32[]{:S(2)}, u32[]{:S(2)}) collective-permute-start(bf16[2,128,2048]{2,1,0:T(8,128)(2,1)} %get-tuple-element.66.refs_14_.refs_22_.refs_13_.refs_1_.refs_15_), channel_id=1, source_target_pairs={{0,3},{1,0},{2,1},{3,2},{4,7},{5,4},{6,5},{7,6},{8,11},{9,8},{10,9... | collective-permute-start | bytes 3145736 | tf_op jit(solution)/shard_map/ppermute | solution.py:45
  9.4 34.8 %all-to-all-start = ((bf16[8,40,1792]{2,1,0:T(8,128)(2,1)}), bf16[8,40,1792]{2,1,0:T(8,128)(2,1)S(1)}, u32[]{:S(2)}, u32[]{:S(2)}) async-start(bf16[8,40,1792]{2,1,0:T(8,128)(2,1)} %get-tuple-element.65), calls=%async_computation | async-start | bytes 2293760 | tf_op jit(solution)/shard_map/all_to_all | solution.py:983
  30.3 40.3 %collective-permute-start.5 = (bf16[2,128,2048]{2,1,0:T(8,128)(2,1)}, bf16[2,128,2048]{2,1,0:T(8,128)(2,1)}, u32[]{:S(2)}, u32[]{:S(2)}) collective-permute-start(bf16[2,128,2048]{2,1,0:T(8,128)(2,1)} %collective-permute-done.1.refs_2_.refs_17_.refs_25_.refs_16_.refs_4_.refs_18_), channel_id=1, source_target_pairs={{0,1},{1,2},{2,3},{3,0},{4,5},{5,6},{6,7},{7,4},{8,9},{9,10},{10,1... | collective-permute-start | bytes 3145736 | tf_op jit(solution)/shard_map/ppermute | solution.py:45
  30.7 40.0 %collective-permute-start.7 = (bf16[2,128,2048]{2,1,0:T(8,128)(2,1)}, bf16[2,128,2048]{2,1,0:T(8,128)(2,1)S(1)}, u32[]{:S(2)}, u32[]{:S(2)}) collective-permute-start(bf16[2,128,2048]{2,1,0:T(8,128)(2,1)} %collective-permute-done.1.refs_2_.refs_17_.refs_25_.refs_16_.refs_4_.refs_18_), channel_id=1, source_target_pairs={{0,4},{1,5},{2,6},{3,7},{4,0},{5,1},{6,2},{7,3},{8,12},{9,13},{10,... | collective-permute-start | bytes 3145736 | tf_op jit(solution)/shard_map/ppermute | solution.py:45
  32.3 38.4 %collective-permute-start.6 = (bf16[2,128,2048]{2,1,0:T(8,128)(2,1)}, bf16[2,128,2048]{2,1,0:T(8,128)(2,1)}, u32[]{:S(2)}, u32[]{:S(2)}) collective-permute-start(bf16[2,128,2048]{2,1,0:T(8,128)(2,1)} %collective-permute-done.2.refs_3_.refs_18_.refs_26_.refs_17_.refs_5_.refs_19_), channel_id=1, source_target_pairs={{0,3},{1,0},{2,1},{3,2},{4,7},{5,4},{6,5},{7,6},{8,11},{9,8},{10,9... | collective-permute-start | bytes 3145736 | tf_op jit(solution)/shard_map/ppermute | solution.py:45
  47.6 20.0 %collective-permute-start.3 = (bf16[8,32,1792]{2,1,0:T(8,128)(2,1)}, bf16[8,32,1792]{2,1,0:T(8,128)(2,1)S(1)}, u32[]{:S(2)}, u32[]{:S(2)}) collective-permute-start(bf16[8,32,1792]{2,1,0:T(8,128)(2,1)} %get-tuple-element.68.refs_0_.refs_4_.refs_3_.refs_5_), channel_id=1, source_target_pairs={{0,96},{1,97},{2,98},{3,99},{4,100},{5,101},{6,102},{7,103},{8,104... | collective-permute-start | bytes 2752520 | tf_op jit(solution)/shard_map/ppermute | solution.py:45
  50.4 20.3 %collective-permute-start.4 = (bf16[8,32,1792]{2,1,0:T(8,128)(2,1)}, bf16[8,32,1792]{2,1,0:T(8,128)(2,1)S(1)}, u32[]{:S(2)}, u32[]{:S(2)}) collective-permute-start(bf16[8,32,1792]{2,1,0:T(8,128)(2,1)} %get-tuple-element.68.refs_0_.refs_4_.refs_3_.refs_5_), channel_id=1, source_target_pairs={{0,32},{1,33},{2,34},{3,35},{4,36},{5,37},{6,38},{7,39},{8,40},{9,... | collective-permute-start | bytes 2752520 | tf_op jit(solution)/shard_map/ppermute | solution.py:45
  75.8 26.0 %collective-permute-start.10 = (bf16[24,32,1792]{2,1,0:T(8,128)(2,1)}, bf16[24,32,1792]{2,1,0:T(8,128)(2,1)S(1)}, u32[]{:S(2)}, u32[]{:S(2)}) collective-permute-start(bf16[24,32,1792]{2,1,0:T(8,128)(2,1)} %bitcast.62), channel_id=1, source_target_pairs={{0,8},{1,9},{2,10},{3,11},{4,12},{5,13},{6,14},{7,15},{8,0},{9,1},... | collective-permute-start | bytes 8257544 | tf_op jit(solution)/shard_map/ppermute | solution.py:45
  83.0 14.3 %collective-permute-start.9 = (bf16[4,32,1792]{2,1,0:T(8,128)(2,1)}, bf16[4,32,1792]{2,1,0:T(8,128)(2,1)S(1)}, u32[]{:S(2)}, u32[]{:S(2)}) collective-permute-start(bf16[4,32,1792]{2,1,0:T(8,128)(2,1)} %get-tuple-element.70), channel_id=1, source_target_pairs={{0,96},{1,97},{2,98},{3,99},{4,100},{5,101},{6,102},{7,103},{8,104... | collective-permute-start | bytes 1376264 | tf_op jit(solution)/shard_map/ppermute | solution.py:45
  86.7 14.2 %collective-permute-start.13 = (bf16[128,2048]{1,0:T(8,128)(2,1)S(1)}, bf16[128,2048]{1,0:T(8,128)(2,1)S(1)}, u32[]{:S(2)}, u32[]{:S(2)}) collective-permute-start(bf16[128,2048]{1,0:T(8,128)(2,1)S(1)} %slice_bitcast_fusion.1), channel_id=1, source_target_pairs={{0,1},{1,2},{2,3},{3,0},{4,5},{5,6},{6,7},{7,4},{8,9},{9,10},{10,1... | collective-permute-start | bytes 1572872 | tf_op jit(solution)/shard_map/ppermute | solution.py:45
  135.9 21.2 %collective-permute-start.15 = (bf16[8,128,2048]{2,1,0:T(8,128)(2,1)}, bf16[8,128,2048]{2,1,0:T(8,128)(2,1)}, u32[]{:S(2)}, u32[]{:S(2)}) collective-permute-start(bf16[8,128,2048]{2,1,0:T(8,128)(2,1)} %get-tuple-element.75.refs_25_), channel_id=1, source_target_pairs={{0,8},{1,9},{2,10},{3,11},{4,12},{5,13},{6,14},{7,15},{8,0},{9,1},... | collective-permute-start | bytes 12582920 | tf_op jit(solution)/shard_map/ppermute | solution.py:45
  160.5 17.1 %collective-permute-start.17 = (bf16[1,128,2048]{2,1,0:T(8,128)(2,1)}, bf16[1,128,2048]{2,1,0:T(8,128)(2,1)S(1)}, u32[]{:S(2)}, u32[]{:S(2)}) collective-permute-start(bf16[1,128,2048]{2,1,0:T(8,128)(2,1)} %get-tuple-element.81.refs_12_), channel_id=1, source_target_pairs={{0,32},{1,33},{2,34},{3,35},{4,36},{5,37},{6,38},{7,39},{8,40},{9,... | collective-permute-start | bytes 1572872 | tf_op jit(solution)/shard_map/ppermute | solution.py:45
  160.5 17.1 %collective-permute-start.18 = (bf16[1,128,2048]{2,1,0:T(8,128)(2,1)}, bf16[1,128,2048]{2,1,0:T(8,128)(2,1)S(1)}, u32[]{:S(2)}, u32[]{:S(2)}) collective-permute-start(bf16[1,128,2048]{2,1,0:T(8,128)(2,1)} %get-tuple-element.82.refs_13_), channel_id=1, source_target_pairs={{0,96},{1,97},{2,98},{3,99},{4,100},{5,101},{6,102},{7,103},{8,104... | collective-permute-start | bytes 1572872 | tf_op jit(solution)/shard_map/ppermute | solution.py:45
  184.0 40.3 %collective-permute-start.21 = (bf16[2,128,2048]{2,1,0:T(8,128)(2,1)}, bf16[2,128,2048]{2,1,0:T(8,128)(2,1)S(1)}, u32[]{:S(2)}, u32[]{:S(2)}) collective-permute-start(bf16[2,128,2048]{2,1,0:T(8,128)(2,1)} %get-tuple-element.85.refs_5_.refs_30_), channel_id=1, source_target_pairs={{0,32},{1,33},{2,34},{3,35},{4,36},{5,37},{6,38},{7,39},{8,40},{9,... | collective-permute-start | bytes 3145736 | tf_op jit(solution)/shard_map/ppermute | solution.py:45
  184.0 40.3 %collective-permute-start.22 = (bf16[2,128,2048]{2,1,0:T(8,128)(2,1)}, bf16[2,128,2048]{2,1,0:T(8,128)(2,1)}, u32[]{:S(2)}, u32[]{:S(2)}) collective-permute-start(bf16[2,128,2048]{2,1,0:T(8,128)(2,1)} %get-tuple-element.86.refs_31_), channel_id=1, source_target_pairs={{0,96},{1,97},{2,98},{3,99},{4,100},{5,101},{6,102},{7,103},{8,104... | collective-permute-start | bytes 3145736 | tf_op jit(solution)/shard_map/ppermute | solution.py:45
  192.6 54.1 %all-to-all-start.1 = ((bf16[8,64,2048]{2,1,0:T(8,128)(2,1)}), bf16[8,64,2048]{2,1,0:T(8,128)(2,1)S(1)}, u32[]{:S(2)}, u32[]{:S(2)}) async-start(bf16[8,64,2048]{2,1,0:T(8,128)(2,1)} %both_sums.1.refs_29_), calls=%async_computation.1 | async-start | bytes 4194304 | tf_op jit(solution)/shard_map/all_to_all | solution.py:1111
  221.4 33.8 %collective-permute-start.19 = (bf16[2,128,2048]{2,1,0:T(8,128)(2,1)}, bf16[2,128,2048]{2,1,0:T(8,128)(2,1)}, u32[]{:S(2)}, u32[]{:S(2)}) collective-permute-start(bf16[2,128,2048]{2,1,0:T(8,128)(2,1)} %get-tuple-element.89), channel_id=1, source_target_pairs={{0,1},{1,2},{2,3},{3,0},{4,5},{5,6},{6,7},{7,4},{8,9},{9,10},{10,1... | collective-permute-start | bytes 3145736 | tf_op jit(solution)/shard_map/ppermute | solution.py:45
  221.8 33.4 %collective-permute-start.20 = (bf16[2,128,2048]{2,1,0:T(8,128)(2,1)}, bf16[2,128,2048]{2,1,0:T(8,128)(2,1)}, u32[]{:S(2)}, u32[]{:S(2)}) collective-permute-start(bf16[2,128,2048]{2,1,0:T(8,128)(2,1)} %get-tuple-element.92), channel_id=1, source_target_pairs={{0,3},{1,0},{2,1},{3,2},{4,7},{5,4},{6,5},{7,6},{8,11},{9,8},{10,9... | collective-permute-start | bytes 3145736 | tf_op jit(solution)/shard_map/ppermute | solution.py:45
  229.6 17.1 %collective-permute-start.23 = (bf16[1,128,2048]{2,1,0:T(8,128)(2,1)}, bf16[1,128,2048]{2,1,0:T(8,128)(2,1)S(1)}, u32[]{:S(2)}, u32[]{:S(2)}) collective-permute-start(bf16[1,128,2048]{2,1,0:T(8,128)(2,1)} %get-tuple-element.96), channel_id=1, source_target_pairs={{0,16},{1,17},{2,18},{3,19},{4,20},{5,21},{6,22},{7,23},{8,24},{9,... | collective-permute-start | bytes 1572872 | tf_op jit(solution)/shard_map/ppermute | solution.py:45
  251.7 14.9 %all-to-all-start.2 = ((bf16[8,16,2048]{2,1,0:T(8,128)(2,1)}), bf16[8,16,2048]{2,1,0:T(8,128)(2,1)S(1)}, u32[]{:S(2)}, u32[]{:S(2)}) async-start(bf16[8,16,2048]{2,1,0:T(8,128)(2,1)} %get-tuple-element.100.refs_7_), calls=%async_computation.2 | async-start | bytes 1048576 | tf_op jit(solution)/shard_map/all_to_all | solution.py:1173
  261.1 46.4 %collective-permute-start.24 = (bf16[4,128,2048]{2,1,0:T(8,128)(2,1)}, bf16[4,128,2048]{2,1,0:T(8,128)(2,1)}, u32[]{:S(2)}, u32[]{:S(2)}) collective-permute-start(bf16[4,128,2048]{2,1,0:T(8,128)(2,1)} %get-tuple-element.101.refs_1_), channel_id=1, source_target_pairs={{0,1},{1,2},{2,3},{3,0},{4,5},{5,6},{6,7},{7,4},{8,9},{9,10},{10,1... | collective-permute-start | bytes 6291464 | tf_op jit(solution)/shard_map/ppermute | solution.py:45
  262.5 45.1 %collective-permute-start.25 = (bf16[4,128,2048]{2,1,0:T(8,128)(2,1)}, bf16[4,128,2048]{2,1,0:T(8,128)(2,1)}, u32[]{:S(2)}, u32[]{:S(2)}) collective-permute-start(bf16[4,128,2048]{2,1,0:T(8,128)(2,1)} %get-tuple-element.102), channel_id=1, source_target_pairs={{0,3},{1,0},{2,1},{3,2},{4,7},{5,4},{6,5},{7,6},{8,11},{9,8},{10,9... | collective-permute-start | bytes 6291464 | tf_op jit(solution)/shard_map/ppermute | solution.py:45
  264.7 16.8 %collective-permute-start.30 = (bf16[2,80,2048]{2,1,0:T(8,128)(2,1)S(1)}, bf16[2,80,2048]{2,1,0:T(8,128)(2,1)S(1)}, u32[]{:S(2)}, u32[]{:S(2)}) collective-permute-start(bf16[2,80,2048]{2,1,0:T(8,128)(2,1)S(1)} %pad_maximum_fusion.refs_2_.refs_0_), channel_id=1, source_target_pairs={{0,96},{1,97},{2,98},{3,99},{4,100},{5,101},{6,102},{7,103},{8,104... | collective-permute-start | bytes 1966088 | tf_op jit(solution)/shard_map/ppermute | solution.py:45
  285.4 27.1 %collective-permute-start.31 = (bf16[2,128,2048]{2,1,0:T(8,128)(2,1)}, bf16[2,128,2048]{2,1,0:T(8,128)(2,1)S(1)}, u32[]{:S(2)}, u32[]{:S(2)}) collective-permute-start(bf16[2,128,2048]{2,1,0:T(8,128)(2,1)} %joined.3.refs_0_), channel_id=1, source_target_pairs={{0,32},{1,33},{2,34},{3,35},{4,36},{5,37},{6,38},{7,39},{8,40},{9,... | collective-permute-start | bytes 3145736 | tf_op jit(solution)/shard_map/ppermute | solution.py:45
  285.4 27.1 %collective-permute-start.32 = (bf16[2,128,2048]{2,1,0:T(8,128)(2,1)}, bf16[2,128,2048]{2,1,0:T(8,128)(2,1)S(1)}, u32[]{:S(2)}, u32[]{:S(2)}) collective-permute-start(bf16[2,128,2048]{2,1,0:T(8,128)(2,1)} %joined.3.refs_0_), channel_id=1, source_target_pairs={{0,96},{1,97},{2,98},{3,99},{4,100},{5,101},{6,102},{7,103},{8,104... | collective-permute-start | bytes 3145736 | tf_op jit(solution)/shard_map/ppermute | solution.py:45
  294.7 35.6 %collective-permute-start.37 = (bf16[8,80,2048]{2,1,0:T(8,128)(2,1)}, bf16[8,80,2048]{2,1,0:T(8,128)(2,1)}, u32[]{:S(2)}, u32[]{:S(2)}) collective-permute-start(bf16[8,80,2048]{2,1,0:T(8,128)(2,1)} %joined.4.refs_3_.refs_2_), channel_id=1, source_target_pairs={{0,8},{1,9},{2,10},{3,11},{4,12},{5,13},{6,14},{7,15},{8,0},{9,1},... | collective-permute-start | bytes 7864328 | tf_op jit(solution)/shard_map/ppermute | solution.py:45
  318.0 20.0 %collective-permute-start.36 = (bf16[6,128,2048]{2,1,0:T(8,128)(2,1)}, bf16[6,128,2048]{2,1,0:T(8,128)(2,1)S(1)}, u32[]{:S(2)}, u32[]{:S(2)}) collective-permute-start(bf16[6,128,2048]{2,1,0:T(8,128)(2,1)} %bitcast.41), channel_id=1, source_target_pairs={{0,8},{1,9},{2,10},{3,11},{4,12},{5,13},{6,14},{7,15},{8,0},{9,1},... | collective-permute-start | bytes 9437192 | tf_op jit(solution)/shard_map/ppermute | solution.py:45
  325.5 27.5 %collective-permute-start.26 = (bf16[2,128,2048]{2,1,0:T(8,128)(2,1)}, bf16[2,128,2048]{2,1,0:T(8,128)(2,1)S(1)}, u32[]{:S(2)}, u32[]{:S(2)}) collective-permute-start(bf16[2,128,2048]{2,1,0:T(8,128)(2,1)} %other_sums.1.refs_4_.refs_5_), channel_id=1, source_target_pairs={{0,4},{1,5},{2,6},{3,7},{4,0},{5,1},{6,2},{7,3},{8,12},{9,13},{10,... | collective-permute-start | bytes 3145736 | tf_op jit(solution)/shard_map/ppermute | solution.py:45
  327.6 19.7 %collective-permute-start.34 = (bf16[1,128,2048]{2,1,0:T(8,128)(2,1)}, bf16[1,128,2048]{2,1,0:T(8,128)(2,1)S(1)}, u32[]{:S(2)}, u32[]{:S(2)}) collective-permute-start(bf16[1,128,2048]{2,1,0:T(8,128)(2,1)} %get-tuple-element.105), channel_id=1, source_target_pairs={{0,32},{1,33},{2,34},{3,35},{4,36},{5,37},{6,38},{7,39},{8,40},{9,... | collective-permute-start | bytes 1572872 | tf_op jit(solution)/shard_map/ppermute | solution.py:45
  327.6 19.7 %collective-permute-start.35 = (bf16[1,128,2048]{2,1,0:T(8,128)(2,1)}, bf16[1,128,2048]{2,1,0:T(8,128)(2,1)S(1)}, u32[]{:S(2)}, u32[]{:S(2)}) collective-permute-start(bf16[1,128,2048]{2,1,0:T(8,128)(2,1)} %get-tuple-element.106), channel_id=1, source_target_pairs={{0,96},{1,97},{2,98},{3,99},{4,100},{5,101},{6,102},{7,103},{8,104... | collective-permute-start | bytes 1572872 | tf_op jit(solution)/shard_map/ppermute | solution.py:45
  (47 other events, 343.9 us)

commit v15 on v14

--- a/solution.py
+++ b/solution.py
@@ -127,6 +127,58 @@
     ]
 
 
+def packed(qkv_weight, up_weight, vectors, lengths, place, head, tokens, cotangent):
+    wide, up_wide = qkv_weight.shape[1], up_weight.shape[1]
+    part, up_part = 3 * head, up_wide // 8
+    cols = part + up_part
+
+    def body(place_ref, len_ref, q_ref, u_ref, x_ref, dy_ref, *refs):
+        v_refs, out_ref, pair_ref = refs[: len(vectors)], refs[-2], refs[-1]
+        pair_ref[0] = x_ref[...]
+        pair_ref[1] = dy_ref[...]
+        lane = lax.broadcasted_iota(jnp.int32, (8, cols), 1)
+        row = lax.broadcasted_iota(jnp.int32, (8, cols), 0)
+        sizes = jnp.zeros((8, cols), f32)
+        for at in range(3):
+            sizes = jnp.where(lane == at, len_ref[0, at].astype(f32), sizes)
+        vector = jnp.concatenate([ref[...].astype(f32) for ref in v_refs])[None, :]
+        vector = jnp.broadcast_to(vector, (8, cols))
+        tail = jnp.where(row == 0, vector, jnp.where(row == 1, sizes, 0.0)).astype(bf16)
+        for owner in range(8):
+            pieces = [
+                q_ref[:, (third * 8 + owner) * head : (third * 8 + owner + 1) * head]
+                for third in range(3)
+            ]
+            pieces.append(u_ref[:, owner * up_part : (owner + 1) * up_part])
+            out_ref[owner] = jnp.concatenate([jnp.concatenate(pieces, 1), tail], 0)
+
+    return pl.pallas_call(
+        body,
+        out_shape=(
+            jax.ShapeDtypeStruct((8, 40, cols), bf16),
+            jax.ShapeDtypeStruct((2,) + tokens.shape, bf16),
+        ),
+        grid_spec=pltpu.PrefetchScalarGridSpec(
+            num_scalar_prefetch=2,
+            grid=(1,),
+            in_specs=[
+                pl.BlockSpec((32, wide), lambda i, place, lens: (place[0], 0)),
+                pl.BlockSpec((32, up_wide), lambda i, place, lens: (place[0], 0)),
+                pl.BlockSpec(tokens.shape, lambda i, place, lens: (0, 0)),
+                pl.BlockSpec(tokens.shape, lambda i, place, lens: (0, 0)),
+            ]
+            + [pl.BlockSpec(v.shape, lambda i, place, lens: (0,)) for v in vectors],
+            out_specs=(
+                pl.BlockSpec((8, 40, cols), lambda i, place, lens: (0, 0, 0)),
+                pl.BlockSpec((2,) + tokens.shape, lambda i, place, lens: (0, 0, 0)),
+            ),
+        ),
+        compiler_params=kernel_params(),
+        cost_estimate=cost(3),
+        name="packed",
+    )(place, lengths, qkv_weight, up_weight, tokens, cotangent, *vectors)
+
+
 def feed_forward(x, dy, gains, weight, spots, down, bias, numbers, first, after):
     rows, width = x[0].shape[1:]
     count = len(x)
@@ -190,16 +242,16 @@
                 send_v[at] = part[:, 0]
 
         def leaving(n):
-            at = (pl.ds(n * 2, 2), pl.ds(0, 64))
+            at = (pl.ds(n * 4, 4), pl.ds(0, 64))
             return (
                 pltpu.make_async_copy(keep_v.at[at], keep_hbm.at[at], sems.at[3]),
                 pltpu.make_async_copy(send_v.at[at], send_hbm.at[at], sems.at[4]),
             )
 
-        @pl.loop(0, ff // 256)
+        @pl.loop(0, ff // 512)
         def _(n):
-            at = pl.ds(pl.multiple_of(n * 256, 256), 256)
-            u = dot(h2_v[...], w_v[:, :, :, at].reshape(width, 256)) + b_ref[:, at]
+            at = pl.ds(pl.multiple_of(n * 512, 512), 512)
+            u = dot(h2_v[...], w_v[:, :, :, at].reshape(width, 512)) + b_ref[:, at]
             cdf = 0.5 * (1.0 + lax.erf(u * math.sqrt(0.5)))
             pdf = jnp.exp(-0.5 * u * u) * (1.0 / math.sqrt(2.0 * math.pi))
             act = (u * cdf).astype(bf16)
@@ -207,8 +259,8 @@
             du = (dot(dy_v[...], d_v[at, :], 1, 1) * (cdf + u * pdf)).astype(bf16)
             du_v[:, at] = du
             db_ref[:, at] = jnp.sum(du.astype(f32), 0, keepdims=True)
-            part = dot_rows(act, dy_v[...]).astype(bf16).reshape(2, 2, 64, width)
-            split(part, pl.ds(n * 2, 2), pl.ds(0, 64), slice(None))
+            part = dot_rows(act, dy_v[...]).astype(bf16).reshape(4, 2, 64, width)
+            split(part, pl.ds(n * 4, 4), pl.ds(0, 64), slice(None))
             for copy in leaving(n):
                 copy.start()
 
@@ -216,7 +268,7 @@
         act_copy.start()
         du_copy = pltpu.make_async_copy(du_v, du_hbm, sems.at[1])
         du_copy.start()
-        for n in range(ff // 256):
+        for n in range(ff // 512):
             for copy in leaving(n):
                 copy.wait()
 
@@ -294,58 +346,6 @@
     )(numbers, spots, gains, bias, *[p[0] for p in weight], *x, *dy, down, *after)
 
 
-def packed(qkv_weight, up_weight, vectors, lengths, place, head, tokens, cotangent):
-    wide, up_wide = qkv_weight.shape[1], up_weight.shape[1]
-    part, up_part = 3 * head, up_wide // 8
-    cols = part + up_part
-
-    def body(place_ref, len_ref, q_ref, u_ref, x_ref, dy_ref, *refs):
-        v_refs, out_ref, pair_ref = refs[: len(vectors)], refs[-2], refs[-1]
-        pair_ref[0] = x_ref[...]
-        pair_ref[1] = dy_ref[...]
-        lane = lax.broadcasted_iota(jnp.int32, (8, cols), 1)
-        row = lax.broadcasted_iota(jnp.int32, (8, cols), 0)
-        sizes = jnp.zeros((8, cols), f32)
-        for at in range(3):
-            sizes = jnp.where(lane == at, len_ref[0, at].astype(f32), sizes)
-        vector = jnp.concatenate([ref[...].astype(f32) for ref in v_refs])[None, :]
-        vector = jnp.broadcast_to(vector, (8, cols))
-        tail = jnp.where(row == 0, vector, jnp.where(row == 1, sizes, 0.0)).astype(bf16)
-        for owner in range(8):
-            pieces = [
-                q_ref[:, (third * 8 + owner) * head : (third * 8 + owner + 1) * head]
-                for third in range(3)
-            ]
-            pieces.append(u_ref[:, owner * up_part : (owner + 1) * up_part])
-            out_ref[owner] = jnp.concatenate([jnp.concatenate(pieces, 1), tail], 0)
-
-    return pl.pallas_call(
-        body,
-        out_shape=(
-            jax.ShapeDtypeStruct((8, 40, cols), bf16),
-            jax.ShapeDtypeStruct((2,) + tokens.shape, bf16),
-        ),
-        grid_spec=pltpu.PrefetchScalarGridSpec(
-            num_scalar_prefetch=2,
-            grid=(1,),
-            in_specs=[
-                pl.BlockSpec((32, wide), lambda i, place, lens: (place[0], 0)),
-                pl.BlockSpec((32, up_wide), lambda i, place, lens: (place[0], 0)),
-                pl.BlockSpec(tokens.shape, lambda i, place, lens: (0, 0)),
-                pl.BlockSpec(tokens.shape, lambda i, place, lens: (0, 0)),
-            ]
-            + [pl.BlockSpec(v.shape, lambda i, place, lens: (0,)) for v in vectors],
-            out_specs=(
-                pl.BlockSpec((8, 40, cols), lambda i, place, lens: (0, 0, 0)),
-                pl.BlockSpec((2,) + tokens.shape, lambda i, place, lens: (0, 0, 0)),
-            ),
-        ),
-        compiler_params=kernel_params(),
-        cost_estimate=cost(3),
-        name="packed",
-    )(place, lengths, qkv_weight, up_weight, tokens, cotangent, *vectors)
-
-
 def attend(h1, dy, weight, spots, out, bias, cosine, sine, lengths, after, rows=128):
     total, width = h1.shape
     count = len(dy)

time: 366 us -> 371 us (1.014); the launches traced: 365 us -> 365 us
  no operation moved by 1% of the time
where the time goes in v15:
time: 371 us; the launch traced here: 365 us
  Pallas kernels  164 us (44%)
  starting transfers between devices  84 us (23%)
  waiting for transfers between devices  77.9 us (21%)
  local copies, waits for them, and re-layouts  29.7 us (8%)
  other arithmetic  7.91 us (2%)
    ppermute x39, starting transfers between devices, move(): return lax.ppermute(value, BOTH, pairs)  72.4 us
    ppermute x39, waiting for transfers between devices, move(): return lax.ppermute(value, BOTH, pairs)  68.7 us
    pallas_call x1, Pallas kernels, feed_forward(): pl.pallas_call(after_inputs(body, 5 + parts + 2 * count, len(after)), out...  32.1 us
    pallas_call x6, Pallas kernels, blocks_call(): pl.pallas_call(after_inputs(body, 1 + len(terms), len(after)), out_shape=...  26.8 us
    pallas_call x1, Pallas kernels, outer(): pl.pallas_call(after_inputs(body, 11 + parts + count, len(after)), out_sh...  24.2 us
    unnamed x81, local copies, waits for them, and re-layouts  20.9 us
    pallas_call x3, Pallas kernels, spread(): pl.pallas_call(after_inputs(body, 2 + 2 * len(pieces) + len(before), len(...  19.7 us
    pallas_call x1, Pallas kernels, attend(): pl.pallas_call(after_inputs(body, 7 + parts + count, len(after)), out_sha...  17.1 us
  transfers between devices with their start and end apart: 42, of which 13 were waited for; matrix products, arithmetic and copies ran while one was open for 4% of the time, Pallas kernels for 32%

profile of v15, /device:TPU:1, one launch (start us, length us, event | category | flops | bytes accessed | tf_op | source)
XLA Modules:
  0.0 365.1 jit_solution(1381194868617747117)
XLA Ops:
  0.7 3.6 packed.1
  9.4 3.6 all-to-all-start
  13.0 17.3 %collective-permute-done.1.refs_2_.refs_17_.refs_25_.refs_16_.refs_4_.refs_18_ = bf16[2,128,2048]{2,1,0:T(8,128)(2,1)} collective-permute-done((bf16[2,128,2048]{2,1,0:T(8,128)(2,1)}, bf16[2,128,2048]{2,1,0:T(8,128)(2,1)}, u32[]{:S(2)}, u32[]{:S(2)}) %collective-permute-start.1) | collective-permute-done | bytes 1048608 | tf_op jit(solution)/shard_map/ppermute | solution.py:45
  35.0 9.2 %all-to-all-done.refs_0_ = bf16[8,40,1792]{2,1,0:T(8,128)(2,1)S(1)} async-done(((bf16[8,40,1792]{2,1,0:T(8,128)(2,1)}), bf16[8,40,1792]{2,1,0:T(8,128)(2,1)S(1)}, u32[]{:S(2)}, u32[]{:S(2)}) %all-to-all-start) | async-done | bytes 1146912 | tf_op jit(solution)/shard_map/all_to_all | solution.py:983
  51.7 16.0 %collective-permute-done.3.refs_2_.refs_5_.refs_4_.refs_6_ = bf16[8,32,1792]{2,1,0:T(8,128)(2,1)S(1)} collective-permute-done((bf16[8,32,1792]{2,1,0:T(8,128)(2,1)}, bf16[8,32,1792]{2,1,0:T(8,128)(2,1)S(1)}, u32[]{:S(2)}, u32[]{:S(2)}) %collective-permute-start.3) | collective-permute-done | bytes 917536 | tf_op jit(solution)/shard_map/ppermute | solution.py:45
  72.6 3.3 halves.2
  75.8 3.9 %collective-permute-start.10 = (bf16[24,32,1792]{2,1,0:T(8,128)(2,1)}, bf16[24,32,1792]{2,1,0:T(8,128)(2,1)S(1)}, u32[]{:S(2)}, u32[]{:S(2)}) collective-permute-start(bf16[24,32,1792]{2,1,0:T(8,128)(2,1)} %bitcast.62), channel_id=1, source_target_pairs={{0,8},{1,9},{2,10},{3,11},{4,12},{5,13},{6,14},{7,15},{8,0},{9,1},... | collective-permute-start | bytes 8257544 | tf_op jit(solution)/shard_map/ppermute | solution.py:45
  91.3 5.2 %collective-permute-done.8.refs_6_.refs_5_.refs_7_ = bf16[4,32,1792]{2,1,0:T(8,128)(2,1)S(1)} collective-permute-done((bf16[4,32,1792]{2,1,0:T(8,128)(2,1)}, bf16[4,32,1792]{2,1,0:T(8,128)(2,1)S(1)}, u32[]{:S(2)}, u32[]{:S(2)}) %collective-permute-start.8) | collective-permute-done | bytes 458784 | tf_op jit(solution)/shard_map/ppermute | solution.py:45
  103.7 32.1 %feed_forward.1 = (bf16[1024,2048]{1,0:T(8,128)(2,1)}, bf16[1024,1024]{1,0:T(8,128)(2,1)}, bf16[1024,1024]{1,0:T(8,128)(2,1)}, bf16[8,128,2048]{2,1,0:T(8,128)(2...) custom-call(s32[4]{0:T(128)} %get-tuple-element.128.refs_0_.refs_7_., ...), custom_call_target="tpu_custom_call" | custom-call | flops 36800000000 | bytes 1000 | tf_op jit(solution)/shard_map/feed_forward/pallas_call | solution.py:310
  139.9 17.1 %attend.1 = (bf16[1024,256]{1,0:T(8,128)(2,1)}, bf16[1024,768]{1,0:T(8,128)(2,1)}, f32[1,768]{1,0:T(1,128)}) custom-call(s32[8,3]{1,0:T(8,128)} %copy-done.8, s32[8]{0:T(128)} %pad_add_fusion.refs_1_.refs_0_, f32[3,1,256]{2,1,0:T(1,128)} %pad_maximum_fusion.2.refs_2_, bf16[8,32,1792]{2,1,0:T(8,128)(2,1)} %get-tuple-element.68.refs_0_.refs_4_.refs_3_.refs_5_, ...), custom_call_target="tpu_custom_call" | custom-call | flops 19549999104 | bytes 1000 | tf_op jit(solution)/shard_map/attend/pallas_call | solution.py:431
  157.1 3.4 far_sums.1
  163.3 13.5 %attention_grads.1 = (bf16[8,64,2048]{2,1,0:T(8,128)(2,1)}, bf16[8,64,2048]{2,1,0:T(8,128)(2,1)}) custom-call(s32[4]{0:T(128)} %get-tuple-element.128.refs_0_.refs_7_.refs_1_, bf16[2,128,2048]{2,1,0:T(8,128)(2,1)} %get-tuple-element.66.refs_14_.refs_22_.refs_13_.refs_1_.refs_15_, ...), custom_call_target="tpu_custom_call" | custom-call | flops 13799999488 | bytes 1000 | tf_op jit(solution)/shard_map/attention_grads/pallas_call | solution.py:527
  179.1 4.8 %near_sums.1 = (bf16[2,128,2048]{2,1,0:T(8,128)(2,1)}, bf16[2,128,2048]{2,1,0:T(8,128)(2,1)}) custom-call(s32[4]{0:T(128)} %get-tuple-element.128.refs_0_.refs_7_.refs_1_, bf16[8,128,2048]{2,1,0:T(8,128)(2,1)} %get-tuple-element.80.refs_1_.refs_3_, bf16[8,128,2048]{2,1,0:T(8,128)(2,1)} %collective-permute-done.15.refs_2_.refs_4_, ...), custom_call_target="tpu_custom_call" | custom-call | flops 23000000512 | bytes 1000 | tf_op jit(solution)/shard_map/near_sums/pallas_call | solution.py:926
  187.9 4.6 %both_sums.1.refs_29_ = bf16[8,64,2048]{2,1,0:T(8,128)(2,1)} custom-call(s32[4]{0:T(128)} %get-tuple-element.128.refs_0_.refs_7_.refs_1_, bf16[8,64,2048]{2,1,0:T(8,128)(2,1)} %get-tuple-element.83.refs_1_.refs_3_, bf16[8,64,2048]{2,1,0:T(8,128)(2,1)} %copy-done.15, bf16[8,64,2048]{2,1,0:T(8,128)(2,1)} %get-tuple-element.83.refs_1_.refs_3_, ...), custom_call_target="tpu_custom_call" | custom-call | flops 3449999872 | bytes 1000 | tf_op jit(solution)/shard_map/both_sums/pallas_call | solution.py:926
  192.5 4.5 %all-to-all-start.1 = ((bf16[8,64,2048]{2,1,0:T(8,128)(2,1)}), bf16[8,64,2048]{2,1,0:T(8,128)(2,1)S(1)}, u32[]{:S(2)}, u32[]{:S(2)}) async-start(bf16[8,64,2048]{2,1,0:T(8,128)(2,1)} %both_sums.1.refs_29_), calls=%async_computation.1 | async-start | bytes 4194304 | tf_op jit(solution)/shard_map/all_to_all | solution.py:1111
  197.0 24.2 %outer.1 = (f32[4,2048]{1,0:T(4,128)}, bf16[2,128,2048]{2,1,0:T(8,128)(2,1)}, bf16[2,128,2048]{2,1,0:T(8,128)(2,1)}, bf16[2,128,2048]{2,1,0:T(8,128)(2,1)}, bf16...) custom-call(s32[8]{0:T(128)} %pad_add_fusion.refs_1_.refs_0_, ...), custom_call_target="tpu_custom_call" | custom-call | flops 23000000512 | bytes 1000 | tf_op jit(solution)/shard_map/outer/pallas_call | solution.py:622
  225.1 4.3 %end_sums.1 = (bf16[1,128,2048]{2,1,0:T(8,128)(2,1)}, bf16[1,128,2048]{2,1,0:T(8,128)(2,1)}) custom-call(s32[4]{0:T(128)} %get-tuple-element.128.refs_0_.refs_7_.refs_1_, bf16[8,128,2048]{2,1,0:T(8,128)(2,1)} %get-tuple-element.80.refs_1_.refs_3_, bf16[8,128,2048]{2,1,0:T(8,128)(2,1)} %collective-permute-done.15.refs_2_.refs_4_, ...), custom_call_target="tpu_custom_call" | custom-call | flops 3449999872 | bytes 1000 | tf_op jit(solution)/shard_map/end_sums/pallas_call | solution.py:926
  232.5 14.0 %collective-permute-done.23.refs_1_ = bf16[1,128,2048]{2,1,0:T(8,128)(2,1)S(1)} collective-permute-done((bf16[1,128,2048]{2,1,0:T(8,128)(2,1)}, bf16[1,128,2048]{2,1,0:T(8,128)(2,1)S(1)}, u32[]{:S(2)}, u32[]{:S(2)}) %collective-permute-start.23) | collective-permute-done | bytes 524320 | tf_op jit(solution)/shard_map/ppermute | solution.py:45
  247.9 3.5 packed_sums.1
  251.5 3.5 all-to-all-start.2
  255.0 5.9 %passed_sums.1 = (bf16[4,128,2048]{2,1,0:T(8,128)(2,1)}, bf16[4,128,2048]{2,1,0:T(8,128)(2,1)}) custom-call(s32[4]{0:T(128)} %get-tuple-element.128.refs_0_.refs_7_.refs_1_, bf16[2,128,2048]{2,1,0:T(8,128)(2,1)} %get-tuple-element.88.refs_1_, bf16[2,128,2048]{2,1,0:T(8,128)(2,1)} %collective-permute-done.19.refs_2_, ...), custom_call_target="tpu_custom_call" | custom-call | flops 3449999872 | bytes 1000 | tf_op jit(solution)/shard_map/passed_sums/pallas_call | solution.py:926
  272.3 4.3 %collective-permute-done.29.refs_2_ = bf16[2,80,2048]{2,1,0:T(8,128)(2,1)S(1)} collective-permute-done((bf16[2,80,2048]{2,1,0:T(8,128)(2,1)S(1)}, bf16[2,80,2048]{2,1,0:T(8,128)(2,1)S(1)}, u32[]{:S(2)}, u32[]{:S(2)}) %collective-permute-start.29) | collective-permute-done | bytes 655392 | tf_op jit(solution)/shard_map/ppermute | solution.py:45
  277.4 4.1 %collective-permute-done.28.refs_1_ = bf16[1,128,2048]{2,1,0:T(8,128)(2,1)S(1)} collective-permute-done((bf16[1,128,2048]{2,1,0:T(8,128)(2,1)}, bf16[1,128,2048]{2,1,0:T(8,128)(2,1)S(1)}, u32[]{:S(2)}, u32[]{:S(2)}) %collective-permute-start.28) | collective-permute-done | bytes 524320 | tf_op jit(solution)/shard_map/ppermute | solution.py:45
  290.8 3.7 %joined.4.refs_3_.refs_2_ = bf16[8,80,2048]{2,1,0:T(8,128)(2,1)} custom-call(bf16[2,80,2048]{2,1,0:T(8,128)(2,1)} %copy-done.4, bf16[2,80,2048]{2,1,0:T(8,128)(2,1)} %copy-done.23, bf16[2,80,2048]{2,1,0:T(8,128)(2,1)} %copy-done.22, bf16[2,80,2048]{2,1,0:T(8,128)(2,1)} %copy-done.24), custom_call_target="tpu_custom_call" | custom-call | flops 3449999872 | bytes 1000 | tf_op jit(solution)/shard_map/joined/pallas_call | solution.py:706
  294.4 12.1 %collective-permute-start.37 = (bf16[8,80,2048]{2,1,0:T(8,128)(2,1)}, bf16[8,80,2048]{2,1,0:T(8,128)(2,1)}, u32[]{:S(2)}, u32[]{:S(2)}) collective-permute-start(bf16[8,80,2048]{2,1,0:T(8,128)(2,1)} %joined.4.refs_3_.refs_2_), channel_id=1, source_target_pairs={{0,8},{1,9},{2,10},{3,11},{4,12},{5,13},{6,14},{7,15},{8,0},{9,1},... | collective-permute-start | bytes 7864328 | tf_op jit(solution)/shard_map/ppermute | solution.py:45
  307.2 3.9 %other_sums.1.refs_4_.refs_5_ = bf16[2,128,2048]{2,1,0:T(8,128)(2,1)} custom-call(s32[4]{0:T(128)} %get-tuple-element.128.refs_0_.refs_7_.refs_1_, bf16[2,128,2048]{2,1,0:T(8,128)(2,1)} %get-tuple-element.103.refs_1_, bf16[4,128,2048]{2,1,0:T(8,128)(2,1)} %collective-permute-done.24.refs_2_.refs_1_, bf16[4,128,2048]{2,1,0:T(8,128)(2,1)} %collective-permute-done.25.refs_3_.refs_2_), custom_call_target="tpu_custom_call" | custom-call | flops 3449999872 | bytes 1000 | tf_op jit(solution)/shard_map/other_sums/pallas_call | solution.py:926
  314.2 3.5 halves.3
  317.7 6.3 %collective-permute-start.36 = (bf16[6,128,2048]{2,1,0:T(8,128)(2,1)}, bf16[6,128,2048]{2,1,0:T(8,128)(2,1)S(1)}, u32[]{:S(2)}, u32[]{:S(2)}) collective-permute-start(bf16[6,128,2048]{2,1,0:T(8,128)(2,1)} %bitcast.41), channel_id=1, source_target_pairs={{0,8},{1,9},{2,10},{3,11},{4,12},{5,13},{6,14},{7,15},{8,0},{9,1},... | collective-permute-start | bytes 9437192 | tf_op jit(solution)/shard_map/ppermute | solution.py:45
  330.1 7.6 %spread.3 = (f32[1024,2048]{1,0:T(8,128)}, f32[256,2048]{1,0:T(8,128)}) custom-call(s32[4]{0:T(128)} %pad_add_fusion.3.refs_0_, s32[4]{0:T(128)} %get-tuple-element.128.refs_0_.refs_7_.refs_1_, bf16[8,80,2048]{2,1,0:T(8,128)(2,1)} %joined.4.refs_3_.refs_2_, bf16[8,80,2048]{2,1,0:T(8,128)(2,1)} %collective-permute-done.37.refs_3_), custom_call_target="tpu_custom_call" | custom-call | flops 16099999744 | bytes 1000 | tf_op jit(solution)/shard_map/spread/pallas_call | solution.py:815
  339.3 7.8 %spread.4 = (f32[256,6144]{1,0:T(8,128)}, f32[256,8192]{1,0:T(8,128)}) custom-call(s32[3]{0:T(128)} %pad_add_fusion.2.refs_0_, s32[4]{0:T(128)} %get-tuple-element.128.refs_0_.refs_7_.refs_1_, bf16[6,128,2048]{2,1,0:T(8,128)(2,1)} %bitcast.43, bf16[6,128,2048]{2,1,0:T(8,128)(2,1)} %copy-done, f32[1024,2048]{1,0:T(8,128)} %get-tuple-element.158.refs_4_, ...), custom_call_target="tpu_custom_call" | custom-call | flops 2300000000 | bytes 1000 | tf_op jit(solution)/shard_map/spread/pallas_call | solution.py:815
  353.8 4.1 %finished.1 = (bf16[128,2048]{1,0:T(8,128)(2,1)}, f32[128,2048]{1,0:T(8,128)}) custom-call(bf16[2,128,2048]{2,1,0:T(8,128)(2,1)} %get-tuple-element.87.refs_0_, bf16[4,128,2048]{2,1,0:T(8,128)(2,1)} %collective-permute-done.24.refs_2_.refs_1_, bf16[4,128,2048]{2,1,0:T(8,128)(2,1)} %collective-permute-done.25.refs_3_.refs_2_, ...), custom_call_target="tpu_custom_call" | custom-call | flops 16099999744 | bytes 1000 | tf_op jit(solution)/shard_map/finished/pallas_call | solution.py:906
  359.8 4.2 %spread.5 = (f32[256,6144]{1,0:T(8,128)}, f32[256,8192]{1,0:T(8,128)}) custom-call(s32[1]{0:T(128)} %bitcast.19.refs_0_, s32[4]{0:T(128)} %get-tuple-element.128.refs_0_.refs_7_.refs_1_, bf16[2,128,2048]{2,1,0:T(8,128)(2,1)} %joined.5.refs_6_.refs_2_, bf16[2,128,2048]{2,1,0:T(8,128)(2,1)} %copy-done.3, ...), custom_call_target="tpu_custom_call", output_to_operand_aliasing={{0}: (4, {}), {1}: (5, {})} | custom-call | flops 2300000000 | bytes 1000 | tf_op jit(solution)/shard_map/spread/pallas_call | solution.py:815
  (198 shorter events, 104.2 us)
Async XLA Ops:
  4.3 26.1 %collective-permute-start.1 = (bf16[2,128,2048]{2,1,0:T(8,128)(2,1)}, bf16[2,128,2048]{2,1,0:T(8,128)(2,1)}, u32[]{:S(2)}, u32[]{:S(2)}) collective-permute-start(bf16[2,128,2048]{2,1,0:T(8,128)(2,1)} %get-tuple-element.66.refs_14_.refs_22_.refs_13_.refs_1_.refs_15_), channel_id=1, source_target_pairs={{0,1},{1,2},{2,3},{3,0},{4,5},{5,6},{6,7},{7,4},{8,9},{9,10},{10,1... | collective-permute-start | bytes 3145736 | tf_op jit(solution)/shard_map/ppermute | solution.py:45
  6.3 26.0 %collective-permute-start.2 = (bf16[2,128,2048]{2,1,0:T(8,128)(2,1)}, bf16[2,128,2048]{2,1,0:T(8,128)(2,1)}, u32[]{:S(2)}, u32[]{:S(2)}) collective-permute-start(bf16[2,128,2048]{2,1,0:T(8,128)(2,1)} %get-tuple-element.66.refs_14_.refs_22_.refs_13_.refs_1_.refs_15_), channel_id=1, source_target_pairs={{0,4},{1,5},{2,6},{3,7},{4,0},{5,1},{6,2},{7,3},{8,12},{9,13},{10,... | collective-permute-start | bytes 3145736 | tf_op jit(solution)/shard_map/ppermute | solution.py:45
  8.0 36.2 %collective-permute-start = (bf16[2,128,2048]{2,1,0:T(8,128)(2,1)}, bf16[2,128,2048]{2,1,0:T(8,128)(2,1)}, u32[]{:S(2)}, u32[]{:S(2)}) collective-permute-start(bf16[2,128,2048]{2,1,0:T(8,128)(2,1)} %get-tuple-element.66.refs_14_.refs_22_.refs_13_.refs_1_.refs_15_), channel_id=1, source_target_pairs={{0,3},{1,0},{2,1},{3,2},{4,7},{5,4},{6,5},{7,6},{8,11},{9,8},{10,9... | collective-permute-start | bytes 3145736 | tf_op jit(solution)/shard_map/ppermute | solution.py:45
  9.4 34.8 %all-to-all-start = ((bf16[8,40,1792]{2,1,0:T(8,128)(2,1)}), bf16[8,40,1792]{2,1,0:T(8,128)(2,1)S(1)}, u32[]{:S(2)}, u32[]{:S(2)}) async-start(bf16[8,40,1792]{2,1,0:T(8,128)(2,1)} %get-tuple-element.65), calls=%async_computation | async-start | bytes 2293760 | tf_op jit(solution)/shard_map/all_to_all | solution.py:983
  30.3 40.3 %collective-permute-start.5 = (bf16[2,128,2048]{2,1,0:T(8,128)(2,1)}, bf16[2,128,2048]{2,1,0:T(8,128)(2,1)}, u32[]{:S(2)}, u32[]{:S(2)}) collective-permute-start(bf16[2,128,2048]{2,1,0:T(8,128)(2,1)} %collective-permute-done.1.refs_2_.refs_17_.refs_25_.refs_16_.refs_4_.refs_18_), channel_id=1, source_target_pairs={{0,1},{1,2},{2,3},{3,0},{4,5},{5,6},{6,7},{7,4},{8,9},{9,10},{10,1... | collective-permute-start | bytes 3145736 | tf_op jit(solution)/shard_map/ppermute | solution.py:45
  30.7 40.0 %collective-permute-start.7 = (bf16[2,128,2048]{2,1,0:T(8,128)(2,1)}, bf16[2,128,2048]{2,1,0:T(8,128)(2,1)S(1)}, u32[]{:S(2)}, u32[]{:S(2)}) collective-permute-start(bf16[2,128,2048]{2,1,0:T(8,128)(2,1)} %collective-permute-done.1.refs_2_.refs_17_.refs_25_.refs_16_.refs_4_.refs_18_), channel_id=1, source_target_pairs={{0,4},{1,5},{2,6},{3,7},{4,0},{5,1},{6,2},{7,3},{8,12},{9,13},{10,... | collective-permute-start | bytes 3145736 | tf_op jit(solution)/shard_map/ppermute | solution.py:45
  32.3 38.4 %collective-permute-start.6 = (bf16[2,128,2048]{2,1,0:T(8,128)(2,1)}, bf16[2,128,2048]{2,1,0:T(8,128)(2,1)}, u32[]{:S(2)}, u32[]{:S(2)}) collective-permute-start(bf16[2,128,2048]{2,1,0:T(8,128)(2,1)} %collective-permute-done.2.refs_3_.refs_18_.refs_26_.refs_17_.refs_5_.refs_19_), channel_id=1, source_target_pairs={{0,3},{1,0},{2,1},{3,2},{4,7},{5,4},{6,5},{7,6},{8,11},{9,8},{10,9... | collective-permute-start | bytes 3145736 | tf_op jit(solution)/shard_map/ppermute | solution.py:45
  47.6 20.0 %collective-permute-start.3 = (bf16[8,32,1792]{2,1,0:T(8,128)(2,1)}, bf16[8,32,1792]{2,1,0:T(8,128)(2,1)S(1)}, u32[]{:S(2)}, u32[]{:S(2)}) collective-permute-start(bf16[8,32,1792]{2,1,0:T(8,128)(2,1)} %get-tuple-element.68.refs_0_.refs_4_.refs_3_.refs_5_), channel_id=1, source_target_pairs={{0,96},{1,97},{2,98},{3,99},{4,100},{5,101},{6,102},{7,103},{8,104... | collective-permute-start | bytes 2752520 | tf_op jit(solution)/shard_map/ppermute | solution.py:45
  50.4 20.3 %collective-permute-start.4 = (bf16[8,32,1792]{2,1,0:T(8,128)(2,1)}, bf16[8,32,1792]{2,1,0:T(8,128)(2,1)S(1)}, u32[]{:S(2)}, u32[]{:S(2)}) collective-permute-start(bf16[8,32,1792]{2,1,0:T(8,128)(2,1)} %get-tuple-element.68.refs_0_.refs_4_.refs_3_.refs_5_), channel_id=1, source_target_pairs={{0,32},{1,33},{2,34},{3,35},{4,36},{5,37},{6,38},{7,39},{8,40},{9,... | collective-permute-start | bytes 2752520 | tf_op jit(solution)/shard_map/ppermute | solution.py:45
  75.8 26.0 %collective-permute-start.10 = (bf16[24,32,1792]{2,1,0:T(8,128)(2,1)}, bf16[24,32,1792]{2,1,0:T(8,128)(2,1)S(1)}, u32[]{:S(2)}, u32[]{:S(2)}) collective-permute-start(bf16[24,32,1792]{2,1,0:T(8,128)(2,1)} %bitcast.62), channel_id=1, source_target_pairs={{0,8},{1,9},{2,10},{3,11},{4,12},{5,13},{6,14},{7,15},{8,0},{9,1},... | collective-permute-start | bytes 8257544 | tf_op jit(solution)/shard_map/ppermute | solution.py:45
  83.0 14.3 %collective-permute-start.9 = (bf16[4,32,1792]{2,1,0:T(8,128)(2,1)}, bf16[4,32,1792]{2,1,0:T(8,128)(2,1)S(1)}, u32[]{:S(2)}, u32[]{:S(2)}) collective-permute-start(bf16[4,32,1792]{2,1,0:T(8,128)(2,1)} %get-tuple-element.70), channel_id=1, source_target_pairs={{0,96},{1,97},{2,98},{3,99},{4,100},{5,101},{6,102},{7,103},{8,104... | collective-permute-start | bytes 1376264 | tf_op jit(solution)/shard_map/ppermute | solution.py:45
  86.7 14.2 %collective-permute-start.13 = (bf16[128,2048]{1,0:T(8,128)(2,1)S(1)}, bf16[128,2048]{1,0:T(8,128)(2,1)S(1)}, u32[]{:S(2)}, u32[]{:S(2)}) collective-permute-start(bf16[128,2048]{1,0:T(8,128)(2,1)S(1)} %slice_bitcast_fusion.1), channel_id=1, source_target_pairs={{0,1},{1,2},{2,3},{3,0},{4,5},{5,6},{6,7},{7,4},{8,9},{9,10},{10,1... | collective-permute-start | bytes 1572872 | tf_op jit(solution)/shard_map/ppermute | solution.py:45
  135.8 21.2 %collective-permute-start.15 = (bf16[8,128,2048]{2,1,0:T(8,128)(2,1)}, bf16[8,128,2048]{2,1,0:T(8,128)(2,1)}, u32[]{:S(2)}, u32[]{:S(2)}) collective-permute-start(bf16[8,128,2048]{2,1,0:T(8,128)(2,1)} %get-tuple-element.75.refs_25_), channel_id=1, source_target_pairs={{0,8},{1,9},{2,10},{3,11},{4,12},{5,13},{6,14},{7,15},{8,0},{9,1},... | collective-permute-start | bytes 12582920 | tf_op jit(solution)/shard_map/ppermute | solution.py:45
  160.5 17.1 %collective-permute-start.17 = (bf16[1,128,2048]{2,1,0:T(8,128)(2,1)}, bf16[1,128,2048]{2,1,0:T(8,128)(2,1)S(1)}, u32[]{:S(2)}, u32[]{:S(2)}) collective-permute-start(bf16[1,128,2048]{2,1,0:T(8,128)(2,1)} %get-tuple-element.81.refs_12_), channel_id=1, source_target_pairs={{0,32},{1,33},{2,34},{3,35},{4,36},{5,37},{6,38},{7,39},{8,40},{9,... | collective-permute-start | bytes 1572872 | tf_op jit(solution)/shard_map/ppermute | solution.py:45
  160.5 17.1 %collective-permute-start.18 = (bf16[1,128,2048]{2,1,0:T(8,128)(2,1)}, bf16[1,128,2048]{2,1,0:T(8,128)(2,1)S(1)}, u32[]{:S(2)}, u32[]{:S(2)}) collective-permute-start(bf16[1,128,2048]{2,1,0:T(8,128)(2,1)} %get-tuple-element.82.refs_13_), channel_id=1, source_target_pairs={{0,96},{1,97},{2,98},{3,99},{4,100},{5,101},{6,102},{7,103},{8,104... | collective-permute-start | bytes 1572872 | tf_op jit(solution)/shard_map/ppermute | solution.py:45
  183.9 40.3 %collective-permute-start.21 = (bf16[2,128,2048]{2,1,0:T(8,128)(2,1)}, bf16[2,128,2048]{2,1,0:T(8,128)(2,1)S(1)}, u32[]{:S(2)}, u32[]{:S(2)}) collective-permute-start(bf16[2,128,2048]{2,1,0:T(8,128)(2,1)} %get-tuple-element.85.refs_5_.refs_30_), channel_id=1, source_target_pairs={{0,32},{1,33},{2,34},{3,35},{4,36},{5,37},{6,38},{7,39},{8,40},{9,... | collective-permute-start | bytes 3145736 | tf_op jit(solution)/shard_map/ppermute | solution.py:45
  183.9 40.3 %collective-permute-start.22 = (bf16[2,128,2048]{2,1,0:T(8,128)(2,1)}, bf16[2,128,2048]{2,1,0:T(8,128)(2,1)}, u32[]{:S(2)}, u32[]{:S(2)}) collective-permute-start(bf16[2,128,2048]{2,1,0:T(8,128)(2,1)} %get-tuple-element.86.refs_31_), channel_id=1, source_target_pairs={{0,96},{1,97},{2,98},{3,99},{4,100},{5,101},{6,102},{7,103},{8,104... | collective-permute-start | bytes 3145736 | tf_op jit(solution)/shard_map/ppermute | solution.py:45
  192.5 54.0 %all-to-all-start.1 = ((bf16[8,64,2048]{2,1,0:T(8,128)(2,1)}), bf16[8,64,2048]{2,1,0:T(8,128)(2,1)S(1)}, u32[]{:S(2)}, u32[]{:S(2)}) async-start(bf16[8,64,2048]{2,1,0:T(8,128)(2,1)} %both_sums.1.refs_29_), calls=%async_computation.1 | async-start | bytes 4194304 | tf_op jit(solution)/shard_map/all_to_all | solution.py:1111
  221.3 33.7 %collective-permute-start.19 = (bf16[2,128,2048]{2,1,0:T(8,128)(2,1)}, bf16[2,128,2048]{2,1,0:T(8,128)(2,1)}, u32[]{:S(2)}, u32[]{:S(2)}) collective-permute-start(bf16[2,128,2048]{2,1,0:T(8,128)(2,1)} %get-tuple-element.89), channel_id=1, source_target_pairs={{0,1},{1,2},{2,3},{3,0},{4,5},{5,6},{6,7},{7,4},{8,9},{9,10},{10,1... | collective-permute-start | bytes 3145736 | tf_op jit(solution)/shard_map/ppermute | solution.py:45
  221.7 33.3 %collective-permute-start.20 = (bf16[2,128,2048]{2,1,0:T(8,128)(2,1)}, bf16[2,128,2048]{2,1,0:T(8,128)(2,1)}, u32[]{:S(2)}, u32[]{:S(2)}) collective-permute-start(bf16[2,128,2048]{2,1,0:T(8,128)(2,1)} %get-tuple-element.92), channel_id=1, source_target_pairs={{0,3},{1,0},{2,1},{3,2},{4,7},{5,4},{6,5},{7,6},{8,11},{9,8},{10,9... | collective-permute-start | bytes 3145736 | tf_op jit(solution)/shard_map/ppermute | solution.py:45
  229.5 17.0 %collective-permute-start.23 = (bf16[1,128,2048]{2,1,0:T(8,128)(2,1)}, bf16[1,128,2048]{2,1,0:T(8,128)(2,1)S(1)}, u32[]{:S(2)}, u32[]{:S(2)}) collective-permute-start(bf16[1,128,2048]{2,1,0:T(8,128)(2,1)} %get-tuple-element.96), channel_id=1, source_target_pairs={{0,16},{1,17},{2,18},{3,19},{4,20},{5,21},{6,22},{7,23},{8,24},{9,... | collective-permute-start | bytes 1572872 | tf_op jit(solution)/shard_map/ppermute | solution.py:45
  251.5 15.2 %all-to-all-start.2 = ((bf16[8,16,2048]{2,1,0:T(8,128)(2,1)}), bf16[8,16,2048]{2,1,0:T(8,128)(2,1)S(1)}, u32[]{:S(2)}, u32[]{:S(2)}) async-start(bf16[8,16,2048]{2,1,0:T(8,128)(2,1)} %get-tuple-element.100.refs_7_), calls=%async_computation.2 | async-start | bytes 1048576 | tf_op jit(solution)/shard_map/all_to_all | solution.py:1173
  260.9 46.3 %collective-permute-start.24 = (bf16[4,128,2048]{2,1,0:T(8,128)(2,1)}, bf16[4,128,2048]{2,1,0:T(8,128)(2,1)}, u32[]{:S(2)}, u32[]{:S(2)}) collective-permute-start(bf16[4,128,2048]{2,1,0:T(8,128)(2,1)} %get-tuple-element.101.refs_1_), channel_id=1, source_target_pairs={{0,1},{1,2},{2,3},{3,0},{4,5},{5,6},{6,7},{7,4},{8,9},{9,10},{10,1... | collective-permute-start | bytes 6291464 | tf_op jit(solution)/shard_map/ppermute | solution.py:45
  262.2 45.0 %collective-permute-start.25 = (bf16[4,128,2048]{2,1,0:T(8,128)(2,1)}, bf16[4,128,2048]{2,1,0:T(8,128)(2,1)}, u32[]{:S(2)}, u32[]{:S(2)}) collective-permute-start(bf16[4,128,2048]{2,1,0:T(8,128)(2,1)} %get-tuple-element.102), channel_id=1, source_target_pairs={{0,3},{1,0},{2,1},{3,2},{4,7},{5,4},{6,5},{7,6},{8,11},{9,8},{10,9... | collective-permute-start | bytes 6291464 | tf_op jit(solution)/shard_map/ppermute | solution.py:45
  264.6 17.0 %collective-permute-start.30 = (bf16[2,80,2048]{2,1,0:T(8,128)(2,1)S(1)}, bf16[2,80,2048]{2,1,0:T(8,128)(2,1)S(1)}, u32[]{:S(2)}, u32[]{:S(2)}) collective-permute-start(bf16[2,80,2048]{2,1,0:T(8,128)(2,1)S(1)} %pad_maximum_fusion.refs_2_.refs_0_), channel_id=1, source_target_pairs={{0,96},{1,97},{2,98},{3,99},{4,100},{5,101},{6,102},{7,103},{8,104... | collective-permute-start | bytes 1966088 | tf_op jit(solution)/shard_map/ppermute | solution.py:45
  285.4 26.8 %collective-permute-start.31 = (bf16[2,128,2048]{2,1,0:T(8,128)(2,1)}, bf16[2,128,2048]{2,1,0:T(8,128)(2,1)S(1)}, u32[]{:S(2)}, u32[]{:S(2)}) collective-permute-start(bf16[2,128,2048]{2,1,0:T(8,128)(2,1)} %joined.3.refs_0_), channel_id=1, source_target_pairs={{0,32},{1,33},{2,34},{3,35},{4,36},{5,37},{6,38},{7,39},{8,40},{9,... | collective-permute-start | bytes 3145736 | tf_op jit(solution)/shard_map/ppermute | solution.py:45
  285.4 26.8 %collective-permute-start.32 = (bf16[2,128,2048]{2,1,0:T(8,128)(2,1)}, bf16[2,128,2048]{2,1,0:T(8,128)(2,1)S(1)}, u32[]{:S(2)}, u32[]{:S(2)}) collective-permute-start(bf16[2,128,2048]{2,1,0:T(8,128)(2,1)} %joined.3.refs_0_), channel_id=1, source_target_pairs={{0,96},{1,97},{2,98},{3,99},{4,100},{5,101},{6,102},{7,103},{8,104... | collective-permute-start | bytes 3145736 | tf_op jit(solution)/shard_map/ppermute | solution.py:45
  294.4 35.6 %collective-permute-start.37 = (bf16[8,80,2048]{2,1,0:T(8,128)(2,1)}, bf16[8,80,2048]{2,1,0:T(8,128)(2,1)}, u32[]{:S(2)}, u32[]{:S(2)}) collective-permute-start(bf16[8,80,2048]{2,1,0:T(8,128)(2,1)} %joined.4.refs_3_.refs_2_), channel_id=1, source_target_pairs={{0,8},{1,9},{2,10},{3,11},{4,12},{5,13},{6,14},{7,15},{8,0},{9,1},... | collective-permute-start | bytes 7864328 | tf_op jit(solution)/shard_map/ppermute | solution.py:45
  317.7 20.0 %collective-permute-start.36 = (bf16[6,128,2048]{2,1,0:T(8,128)(2,1)}, bf16[6,128,2048]{2,1,0:T(8,128)(2,1)S(1)}, u32[]{:S(2)}, u32[]{:S(2)}) collective-permute-start(bf16[6,128,2048]{2,1,0:T(8,128)(2,1)} %bitcast.41), channel_id=1, source_target_pairs={{0,8},{1,9},{2,10},{3,11},{4,12},{5,13},{6,14},{7,15},{8,0},{9,1},... | collective-permute-start | bytes 9437192 | tf_op jit(solution)/shard_map/ppermute | solution.py:45
  325.2 27.5 %collective-permute-start.26 = (bf16[2,128,2048]{2,1,0:T(8,128)(2,1)}, bf16[2,128,2048]{2,1,0:T(8,128)(2,1)S(1)}, u32[]{:S(2)}, u32[]{:S(2)}) collective-permute-start(bf16[2,128,2048]{2,1,0:T(8,128)(2,1)} %other_sums.1.refs_4_.refs_5_), channel_id=1, source_target_pairs={{0,4},{1,5},{2,6},{3,7},{4,0},{5,1},{6,2},{7,3},{8,12},{9,13},{10,... | collective-permute-start | bytes 3145736 | tf_op jit(solution)/shard_map/ppermute | solution.py:45
  327.4 19.7 %collective-permute-start.34 = (bf16[1,128,2048]{2,1,0:T(8,128)(2,1)}, bf16[1,128,2048]{2,1,0:T(8,128)(2,1)S(1)}, u32[]{:S(2)}, u32[]{:S(2)}) collective-permute-start(bf16[1,128,2048]{2,1,0:T(8,128)(2,1)} %get-tuple-element.105), channel_id=1, source_target_pairs={{0,32},{1,33},{2,34},{3,35},{4,36},{5,37},{6,38},{7,39},{8,40},{9,... | collective-permute-start | bytes 1572872 | tf_op jit(solution)/shard_map/ppermute | solution.py:45
  327.4 19.7 %collective-permute-start.35 = (bf16[1,128,2048]{2,1,0:T(8,128)(2,1)}, bf16[1,128,2048]{2,1,0:T(8,128)(2,1)S(1)}, u32[]{:S(2)}, u32[]{:S(2)}) collective-permute-start(bf16[1,128,2048]{2,1,0:T(8,128)(2,1)} %get-tuple-element.106), channel_id=1, source_target_pairs={{0,96},{1,97},{2,98},{3,99},{4,100},{5,101},{6,102},{7,103},{8,104... | collective-permute-start | bytes 1572872 | tf_op jit(solution)/shard_map/ppermute | solution.py:45
  (47 other events, 344.1 us)
